TPU v7x, 32 devices: a whole 2x2x4 slice. The times are simulated.
32 devices in a mesh: row: 8 (over y, x, core), col: 4 (over z).
Axes of the slice: x: 2, y: 2, z: 4, core: 2. Of those that a mesh axis runs over, the one named last changes fastest.
Arguments:
- grad_out: bfloat16 [65536, 256], P(('row', 'col')), may hold values from -6 to 6
- preact: bfloat16 [65536, 256], P(('row', 'col')), may hold values from -6 to 6
- features: bfloat16 [65536, 256], P(('col', 'row')), may hold values from -6 to 6
- weight: bfloat16 [256, 256], replicated, may hold values from -0.375 to 0.375
- tiles: bfloat16 [8, 4, 320, 128, 128], P('row', 'col'), may hold values from -0.099609375 to 0.099609375
- tile_rows: int32 [8, 4, 320], P('row', 'col'), may hold values from 0 to 63
- tile_cols: int32 [8, 4, 320], P('row', 'col'), may hold values from 0 to 127
- live_counts: int32 [8, 4], P('row', 'col'), may hold values from 80 to 320, as said below
Outputs:
- grad_features: bfloat16 [65536, 256], P(('col', 'row'))
- grad_weight: float32 [256, 256], replicated
Inputs may be any that keep to these rules, and one draw needn't show every extreme that they name: `live_counts`: some block holds exactly 320 live tiles in every draw.
All inputs are finite; a program needn't handle non-finite values.
Results may differ from a plain program's by a relative error of at most 0.02.
Values may be sent and summed in bfloat16 or wider, within the bound.
No kernel may reach another device: no remote copies, remote signals or barrier semaphores. Data moves between devices by JAX's collectives and lax.ppermute only.
A program may use at most 192 MiB of HBM per device.

v0:
```python
import math

import jax
import jax.numpy as jnp
from jax import lax
from jax.sharding import PartitionSpec as P


def body(grad_out, preact, features, weight, tiles, tile_rows, tile_cols, live_counts):
    width = grad_out.shape[1]
    masked = jnp.where(preact > 0, grad_out, jnp.zeros_like(grad_out))
    block = lax.all_gather(masked, "col", axis=0, tiled=True)
    row_count = block.shape[0] // 128
    row_flat = block.reshape(row_count, 128 * width)
    slots = tiles.shape[2]
    tile_stack = tiles.reshape(slots, 128, 128)
    row_index = tile_rows.reshape(slots)
    col_index = tile_cols.reshape(slots)
    count = live_counts.reshape(())
    col_tiles = lax.axis_size("row") * grad_out.shape[0] // 128
    group = math.gcd(slots, 32)
    offsets = jnp.arange(group, dtype=jnp.int32)
    row_ids = jnp.arange(row_count, dtype=jnp.int32)
    col_ids = jnp.arange(col_tiles, dtype=jnp.int32)

    def add_group(step, accum):
        start = step * group
        tile_blk = lax.dynamic_slice_in_dim(tile_stack, start, group, 0)
        rows_now = lax.dynamic_slice_in_dim(row_index, start, group, 0)
        cols_now = lax.dynamic_slice_in_dim(col_index, start, group, 0) - 0
        pick = (rows_now[:, None] == row_ids[None, :]).astype(jnp.bfloat16)
        gathered = jnp.dot(pick, row_flat, preferred_element_type=jnp.float32).astype(jnp.bfloat16)
        gathered = gathered.reshape(group, 128, width)
        prod = jnp.einsum("kab,kaf->kbf", tile_blk, gathered, preferred_element_type=jnp.float32)
        upper = prod.astype(jnp.bfloat16)
        lower = (prod - upper.astype(jnp.float32)).astype(jnp.bfloat16)
        keep = start + offsets < count
        place = ((cols_now[None, :] == col_ids[:, None]) & keep[None, :]).astype(jnp.bfloat16)
        both_place = jnp.concatenate([place, place], axis=1)
        both_vals = jnp.concatenate([upper, lower], axis=0).reshape(2 * group, 128 * width)
        return accum + jnp.dot(both_place, both_vals, preferred_element_type=jnp.float32)

    accum = jnp.zeros((col_tiles, 128 * width), jnp.float32)
    accum = lax.fori_loop(0, slots // group, add_group, accum)
    partial_value = accum.reshape(col_tiles * 128, width)
    summed = lax.psum_scatter(
        partial_value.astype(jnp.bfloat16), "row", scatter_dimension=0, tiled=True
    )
    grad_features = lax.dot_general(
        summed, weight, (((1,), (1,)), ((), ())), preferred_element_type=jnp.float32
    ).astype(jnp.bfloat16)
    weight_term = lax.dot_general(
        features, summed, (((0,), (0,)), ((), ())), preferred_element_type=jnp.float32
    )
    grad_weight = lax.psum(weight_term, ("row", "col"))
    return (grad_features, grad_weight)


def solution(mesh):
    in_specs = (
        P(("row", "col"), None),
        P(("row", "col"), None),
        P(("col", "row"), None),
        P(),
        P("row", "col", None, None, None),
        P("row", "col", None),
        P("row", "col", None),
        P("row", "col"),
    )
    out_specs = (P(("col", "row"), None), P())
    return jax.shard_map(body, mesh=mesh, in_specs=in_specs, out_specs=out_specs, check_vma=False)
```

profile of v0, /device:TPU:1, one launch (start us, length us, event | category | flops | bytes accessed | tf_op | source)
XLA Modules:
  0.0 590.0 jit_solution(11411385270567788028)
XLA Ops:
  10.1 14.6 %copy.12 = bf16[1,1,320,128,128]{3,4,2,1,0:T(8,128)(2,1)} copy(bf16[1,1,320,128,128]{4,3,2,1,0:T(8,128)(2,1)} %param.14) | data formatting | bytes 20971520 | tf_op args[4]
  24.7 68.4 %all-gather.2.cloned.1.call-done = bf16[8192,256]{1,0:T(8,128)(2,1)} async-done(((bf16[2048,256]{1,0:T(8,128)(2,1)}), bf16[8192,256]{1,0:T(8,128)(2,1)}) %all-gather.2.cloned.1.call-update) | async-done | bytes 4194320 | tf_op jit(solution)/shard_map/all_gather | solution.py:12
  93.1 7.4 %reshape.49 = bf16[64,32768]{1,0:T(8,128)(2,1)} reshape(bf16[8192,256]{1,0:T(8,128)(2,1)} %all-gather.2.cloned.1.call-done) | data formatting | bytes 8388608 | tf_op jit(solution)/shard_map/reshape | solution.py:14
  100.5 257.7 %while.14 = (s32[]{:T(128)}, f32[128,32768]{1,0:T(8,128)}, s32[320]{0:T(512)S(1)}, s32[]{:T(128)}, bf16[320,128,128]{1,2,0:T(8,128)(2,1)}, /*index=5*/s32[320]{0...) while((s32[]{:T(128)}, f32[128,32768]{1,0:T(8,128)}, ...), condition=%wide.region_1.2_spmd.clone, body=%wide.region_0.1_spmd.clone.sunk | while | flops 955271232 | bytes 189801616 | solution.py:44
  112.0 8.4 %convolution_add_fusion.2 = f32[128,32768]{1,0:T(8,128)S(1)} fusion(bf16[64,32768]{1,0:T(8,128)(2,1)} %bitcast.32, f32[128,32768]{1,0:T(8,128)S(1)} %bitcast.30, pred[]{:T(512)S(6)} %compare.3, pred[128,32]{0,1:T(32,128)(4,1)S(1)} %fusion.34), kind=kOutput, calls=%fused_computation.3.clone.1 | convolution fusion | flops 545267712 | bytes 37752832 | tf_op jit(solution)/shard_map/while/body/eval_jaxpr/dot_general | solution.py:41
  120.5 5.7 copy-done.1
  133.3 4.5 copy.19
  137.8 8.4 %convolution_add_fusion.2 = f32[128,32768]{1,0:T(8,128)S(1)} fusion(bf16[64,32768]{1,0:T(8,128)(2,1)} %bitcast.32, f32[128,32768]{1,0:T(8,128)S(1)} %bitcast.30, pred[]{:T(512)S(6)} %compare.3, pred[128,32]{0,1:T(32,128)(4,1)S(1)} %fusion.34), kind=kOutput, calls=%fused_computation.3.clone.1 | convolution fusion | flops 545267712 | bytes 37752832 | tf_op jit(solution)/shard_map/while/body/eval_jaxpr/dot_general | solution.py:41
  146.3 5.7 copy-done.1
  159.0 4.5 copy.19
  163.6 8.4 %convolution_add_fusion.2 = f32[128,32768]{1,0:T(8,128)S(1)} fusion(bf16[64,32768]{1,0:T(8,128)(2,1)} %bitcast.32, f32[128,32768]{1,0:T(8,128)S(1)} %bitcast.30, pred[]{:T(512)S(6)} %compare.3, pred[128,32]{0,1:T(32,128)(4,1)S(1)} %fusion.34), kind=kOutput, calls=%fused_computation.3.clone.1 | convolution fusion | flops 545267712 | bytes 37752832 | tf_op jit(solution)/shard_map/while/body/eval_jaxpr/dot_general | solution.py:41
  172.0 5.7 copy-done.1
  184.8 4.5 copy.19
  189.3 8.4 %convolution_add_fusion.2 = f32[128,32768]{1,0:T(8,128)S(1)} fusion(bf16[64,32768]{1,0:T(8,128)(2,1)} %bitcast.32, f32[128,32768]{1,0:T(8,128)S(1)} %bitcast.30, pred[]{:T(512)S(6)} %compare.3, pred[128,32]{0,1:T(32,128)(4,1)S(1)} %fusion.34), kind=kOutput, calls=%fused_computation.3.clone.1 | convolution fusion | flops 545267712 | bytes 37752832 | tf_op jit(solution)/shard_map/while/body/eval_jaxpr/dot_general | solution.py:41
  197.8 5.7 copy-done.1
  210.6 4.5 copy.19
  215.1 8.4 %convolution_add_fusion.2 = f32[128,32768]{1,0:T(8,128)S(1)} fusion(bf16[64,32768]{1,0:T(8,128)(2,1)} %bitcast.32, f32[128,32768]{1,0:T(8,128)S(1)} %bitcast.30, pred[]{:T(512)S(6)} %compare.3, pred[128,32]{0,1:T(32,128)(4,1)S(1)} %fusion.34), kind=kOutput, calls=%fused_computation.3.clone.1 | convolution fusion | flops 545267712 | bytes 37752832 | tf_op jit(solution)/shard_map/while/body/eval_jaxpr/dot_general | solution.py:41
  223.6 5.7 copy-done.1
  240.9 8.4 %convolution_add_fusion.2 = f32[128,32768]{1,0:T(8,128)S(1)} fusion(bf16[64,32768]{1,0:T(8,128)(2,1)} %bitcast.32, f32[128,32768]{1,0:T(8,128)S(1)} %bitcast.30, pred[]{:T(512)S(6)} %compare.3, pred[128,32]{0,1:T(32,128)(4,1)S(1)} %fusion.34), kind=kOutput, calls=%fused_computation.3.clone.1 | convolution fusion | flops 545267712 | bytes 37752832 | tf_op jit(solution)/shard_map/while/body/eval_jaxpr/dot_general | solution.py:41
  249.3 5.7 copy-done.1
  266.7 8.4 %convolution_add_fusion.2 = f32[128,32768]{1,0:T(8,128)S(1)} fusion(bf16[64,32768]{1,0:T(8,128)(2,1)} %bitcast.32, f32[128,32768]{1,0:T(8,128)S(1)} %bitcast.30, pred[]{:T(512)S(6)} %compare.3, pred[128,32]{0,1:T(32,128)(4,1)S(1)} %fusion.34), kind=kOutput, calls=%fused_computation.3.clone.1 | convolution fusion | flops 545267712 | bytes 37752832 | tf_op jit(solution)/shard_map/while/body/eval_jaxpr/dot_general | solution.py:41
  275.1 5.7 copy-done.1
  292.4 8.4 %convolution_add_fusion.2 = f32[128,32768]{1,0:T(8,128)S(1)} fusion(bf16[64,32768]{1,0:T(8,128)(2,1)} %bitcast.32, f32[128,32768]{1,0:T(8,128)S(1)} %bitcast.30, pred[]{:T(512)S(6)} %compare.3, pred[128,32]{0,1:T(32,128)(4,1)S(1)} %fusion.34), kind=kOutput, calls=%fused_computation.3.clone.1 | convolution fusion | flops 545267712 | bytes 37752832 | tf_op jit(solution)/shard_map/while/body/eval_jaxpr/dot_general | solution.py:41
  300.9 5.7 copy-done.1
  318.2 8.4 %convolution_add_fusion.2 = f32[128,32768]{1,0:T(8,128)S(1)} fusion(bf16[64,32768]{1,0:T(8,128)(2,1)} %bitcast.32, f32[128,32768]{1,0:T(8,128)S(1)} %bitcast.30, pred[]{:T(512)S(6)} %compare.3, pred[128,32]{0,1:T(32,128)(4,1)S(1)} %fusion.34), kind=kOutput, calls=%fused_computation.3.clone.1 | convolution fusion | flops 545267712 | bytes 37752832 | tf_op jit(solution)/shard_map/while/body/eval_jaxpr/dot_general | solution.py:41
  326.6 5.7 copy-done.1
  344.0 8.4 %convolution_add_fusion.2 = f32[128,32768]{1,0:T(8,128)S(1)} fusion(bf16[64,32768]{1,0:T(8,128)(2,1)} %bitcast.32, f32[128,32768]{1,0:T(8,128)S(1)} %bitcast.30, pred[]{:T(512)S(6)} %compare.3, pred[128,32]{0,1:T(32,128)(4,1)S(1)} %fusion.34), kind=kOutput, calls=%fused_computation.3.clone.1 | convolution fusion | flops 545267712 | bytes 37752832 | tf_op jit(solution)/shard_map/while/body/eval_jaxpr/dot_general | solution.py:41
  352.4 5.7 copy-done.1
  358.1 8.9 %convert_element_type.45 = bf16[128,32768]{1,0:T(8,128)(2,1)} convert(f32[128,32768]{1,0:T(8,128)} %get-tuple-element.171) | non-fusion elementwise | flops 4194304 | bytes 25165824 | tf_op jit(solution)/shard_map/convert_element_type | solution.py:47
  367.0 13.5 %convert_element_type.46 = bf16[16384,256]{1,0:T(8,128)(2,1)} reshape(bf16[128,32768]{1,0:T(8,128)(2,1)} %convert_element_type.45) | data formatting | bytes 16777216 | tf_op jit(solution)/shard_map/convert_element_type | solution.py:47
  380.6 69.9 %reduce-scatter.2.cloned.1.call-done = bf16[2048,256]{1,0:T(8,128)(2,1)} async-done(((bf16[16384,256]{1,0:T(8,128)(2,1)}), bf16[2048,256]{1,0:T(8,128)(2,1)}) %reduce-scatter.2.cloned.1.call-update) | async-done | bytes 1048592 | tf_op jit(solution)/shard_map/reduce_scatter | solution.py:46
  455.6 126.1 %all-reduce.2.cloned.1.call-done = f32[256,256]{0,1:T(8,128)} async-done(((f32[256,256]{0,1:T(8,128)}), f32[256,256]{0,1:T(8,128)}) %all-reduce.2.cloned.1.call-update) | async-done | bytes 262160 | tf_op jit(solution)/shard_map/psum | solution.py:55
  (207 shorter events, 106.8 us)
Async XLA Ops:
  7.2 443.4 %copy-start = (bf16[2048,256]{1,0:T(8,128)(2,1)S(1)}, bf16[2048,256]{1,0:T(8,128)(2,1)}, u32[]{:S(2)}) copy-start(bf16[2048,256]{1,0:T(8,128)(2,1)} %param.12) | copy-start | bytes 3145732
  7.2 85.9 %all-gather.2.cloned.1.call-start = ((), (), s32[]{:S(2)}) async-start(), calls=%async_computation.1 | async-start | bytes 5242880 | tf_op jit(solution)/shard_map/all_gather | solution.py:12
  10.0 440.6 %reduce-scatter.2.cloned.1.call-start = ((), (), s32[]{:S(2)}) async-start(), calls=%async_computation.2 | async-start | bytes 9437184 | tf_op jit(solution)/shard_map/reduce_scatter | solution.py:46
  101.3 10.7 %slice-start = ((s8[16777216]{0:T(1024)(128)(4,1)}), s8[4194304]{0:T(1024)(128)(4,1)S(1)}, s32[]{:S(2)}) async-start(s8[16777216]{0:T(1024)(128)(4,1)} %bitcast.29), calls=%async_computation.4 | async-start | bytes 8388608 | tf_op jit(solution)/shard_map/while
  104.5 7.6 %slice-start.1 = ((s8[16777216]{0:T(1024)(128)(4,1)}), s8[4194304]{0:T(1024)(128)(4,1)S(1)}, s32[]{:S(2)}) async-start(s8[16777216]{0:T(1024)(128)(4,1)} %bitcast.29), calls=%async_computation.5 | async-start | bytes 8388608 | tf_op jit(solution)/shard_map/while
  127.1 10.7 %slice-start = ((s8[16777216]{0:T(1024)(128)(4,1)}), s8[4194304]{0:T(1024)(128)(4,1)S(1)}, s32[]{:S(2)}) async-start(s8[16777216]{0:T(1024)(128)(4,1)} %bitcast.29), calls=%async_computation.4 | async-start | bytes 8388608 | tf_op jit(solution)/shard_map/while
  130.2 7.6 %slice-start.1 = ((s8[16777216]{0:T(1024)(128)(4,1)}), s8[4194304]{0:T(1024)(128)(4,1)S(1)}, s32[]{:S(2)}) async-start(s8[16777216]{0:T(1024)(128)(4,1)} %bitcast.29), calls=%async_computation.5 | async-start | bytes 8388608 | tf_op jit(solution)/shard_map/while
  130.7 7.1 %slice-start.2 = ((s8[16777216]{0:T(1024)(128)(4,1)}), s8[4194304]{0:T(1024)(128)(4,1)S(1)}, s32[]{:S(2)}) async-start(s8[16777216]{0:T(1024)(128)(4,1)} %bitcast.29), calls=%async_computation.6 | async-start | bytes 8388608 | tf_op jit(solution)/shard_map/while
  152.9 10.7 %slice-start = ((s8[16777216]{0:T(1024)(128)(4,1)}), s8[4194304]{0:T(1024)(128)(4,1)S(1)}, s32[]{:S(2)}) async-start(s8[16777216]{0:T(1024)(128)(4,1)} %bitcast.29), calls=%async_computation.4 | async-start | bytes 8388608 | tf_op jit(solution)/shard_map/while
  156.0 7.6 %slice-start.1 = ((s8[16777216]{0:T(1024)(128)(4,1)}), s8[4194304]{0:T(1024)(128)(4,1)S(1)}, s32[]{:S(2)}) async-start(s8[16777216]{0:T(1024)(128)(4,1)} %bitcast.29), calls=%async_computation.5 | async-start | bytes 8388608 | tf_op jit(solution)/shard_map/while
  156.5 7.1 %slice-start.2 = ((s8[16777216]{0:T(1024)(128)(4,1)}), s8[4194304]{0:T(1024)(128)(4,1)S(1)}, s32[]{:S(2)}) async-start(s8[16777216]{0:T(1024)(128)(4,1)} %bitcast.29), calls=%async_computation.6 | async-start | bytes 8388608 | tf_op jit(solution)/shard_map/while
  178.6 10.7 %slice-start = ((s8[16777216]{0:T(1024)(128)(4,1)}), s8[4194304]{0:T(1024)(128)(4,1)S(1)}, s32[]{:S(2)}) async-start(s8[16777216]{0:T(1024)(128)(4,1)} %bitcast.29), calls=%async_computation.4 | async-start | bytes 8388608 | tf_op jit(solution)/shard_map/while
  181.8 7.6 %slice-start.1 = ((s8[16777216]{0:T(1024)(128)(4,1)}), s8[4194304]{0:T(1024)(128)(4,1)S(1)}, s32[]{:S(2)}) async-start(s8[16777216]{0:T(1024)(128)(4,1)} %bitcast.29), calls=%async_computation.5 | async-start | bytes 8388608 | tf_op jit(solution)/shard_map/while
  182.3 7.1 %slice-start.2 = ((s8[16777216]{0:T(1024)(128)(4,1)}), s8[4194304]{0:T(1024)(128)(4,1)S(1)}, s32[]{:S(2)}) async-start(s8[16777216]{0:T(1024)(128)(4,1)} %bitcast.29), calls=%async_computation.6 | async-start | bytes 8388608 | tf_op jit(solution)/shard_map/while
  204.4 10.7 %slice-start = ((s8[16777216]{0:T(1024)(128)(4,1)}), s8[4194304]{0:T(1024)(128)(4,1)S(1)}, s32[]{:S(2)}) async-start(s8[16777216]{0:T(1024)(128)(4,1)} %bitcast.29), calls=%async_computation.4 | async-start | bytes 8388608 | tf_op jit(solution)/shard_map/while
  207.5 7.6 %slice-start.1 = ((s8[16777216]{0:T(1024)(128)(4,1)}), s8[4194304]{0:T(1024)(128)(4,1)S(1)}, s32[]{:S(2)}) async-start(s8[16777216]{0:T(1024)(128)(4,1)} %bitcast.29), calls=%async_computation.5 | async-start | bytes 8388608 | tf_op jit(solution)/shard_map/while
  208.0 7.1 %slice-start.2 = ((s8[16777216]{0:T(1024)(128)(4,1)}), s8[4194304]{0:T(1024)(128)(4,1)S(1)}, s32[]{:S(2)}) async-start(s8[16777216]{0:T(1024)(128)(4,1)} %bitcast.29), calls=%async_computation.6 | async-start | bytes 8388608 | tf_op jit(solution)/shard_map/while
  230.2 10.7 %slice-start = ((s8[16777216]{0:T(1024)(128)(4,1)}), s8[4194304]{0:T(1024)(128)(4,1)S(1)}, s32[]{:S(2)}) async-start(s8[16777216]{0:T(1024)(128)(4,1)} %bitcast.29), calls=%async_computation.4 | async-start | bytes 8388608 | tf_op jit(solution)/shard_map/while
  233.3 7.6 %slice-start.1 = ((s8[16777216]{0:T(1024)(128)(4,1)}), s8[4194304]{0:T(1024)(128)(4,1)S(1)}, s32[]{:S(2)}) async-start(s8[16777216]{0:T(1024)(128)(4,1)} %bitcast.29), calls=%async_computation.5 | async-start | bytes 8388608 | tf_op jit(solution)/shard_map/while
  233.8 7.1 %slice-start.2 = ((s8[16777216]{0:T(1024)(128)(4,1)}), s8[4194304]{0:T(1024)(128)(4,1)S(1)}, s32[]{:S(2)}) async-start(s8[16777216]{0:T(1024)(128)(4,1)} %bitcast.29), calls=%async_computation.6 | async-start | bytes 8388608 | tf_op jit(solution)/shard_map/while
  256.0 10.7 %slice-start = ((s8[16777216]{0:T(1024)(128)(4,1)}), s8[4194304]{0:T(1024)(128)(4,1)S(1)}, s32[]{:S(2)}) async-start(s8[16777216]{0:T(1024)(128)(4,1)} %bitcast.29), calls=%async_computation.4 | async-start | bytes 8388608 | tf_op jit(solution)/shard_map/while
  259.1 7.6 %slice-start.1 = ((s8[16777216]{0:T(1024)(128)(4,1)}), s8[4194304]{0:T(1024)(128)(4,1)S(1)}, s32[]{:S(2)}) async-start(s8[16777216]{0:T(1024)(128)(4,1)} %bitcast.29), calls=%async_computation.5 | async-start | bytes 8388608 | tf_op jit(solution)/shard_map/while
  259.6 7.1 %slice-start.2 = ((s8[16777216]{0:T(1024)(128)(4,1)}), s8[4194304]{0:T(1024)(128)(4,1)S(1)}, s32[]{:S(2)}) async-start(s8[16777216]{0:T(1024)(128)(4,1)} %bitcast.29), calls=%async_computation.6 | async-start | bytes 8388608 | tf_op jit(solution)/shard_map/while
  281.7 10.7 %slice-start = ((s8[16777216]{0:T(1024)(128)(4,1)}), s8[4194304]{0:T(1024)(128)(4,1)S(1)}, s32[]{:S(2)}) async-start(s8[16777216]{0:T(1024)(128)(4,1)} %bitcast.29), calls=%async_computation.4 | async-start | bytes 8388608 | tf_op jit(solution)/shard_map/while
  284.8 7.6 %slice-start.1 = ((s8[16777216]{0:T(1024)(128)(4,1)}), s8[4194304]{0:T(1024)(128)(4,1)S(1)}, s32[]{:S(2)}) async-start(s8[16777216]{0:T(1024)(128)(4,1)} %bitcast.29), calls=%async_computation.5 | async-start | bytes 8388608 | tf_op jit(solution)/shard_map/while
  285.3 7.1 %slice-start.2 = ((s8[16777216]{0:T(1024)(128)(4,1)}), s8[4194304]{0:T(1024)(128)(4,1)S(1)}, s32[]{:S(2)}) async-start(s8[16777216]{0:T(1024)(128)(4,1)} %bitcast.29), calls=%async_computation.6 | async-start | bytes 8388608 | tf_op jit(solution)/shard_map/while
  307.5 10.7 %slice-start = ((s8[16777216]{0:T(1024)(128)(4,1)}), s8[4194304]{0:T(1024)(128)(4,1)S(1)}, s32[]{:S(2)}) async-start(s8[16777216]{0:T(1024)(128)(4,1)} %bitcast.29), calls=%async_computation.4 | async-start | bytes 8388608 | tf_op jit(solution)/shard_map/while
  310.6 7.6 %slice-start.1 = ((s8[16777216]{0:T(1024)(128)(4,1)}), s8[4194304]{0:T(1024)(128)(4,1)S(1)}, s32[]{:S(2)}) async-start(s8[16777216]{0:T(1024)(128)(4,1)} %bitcast.29), calls=%async_computation.5 | async-start | bytes 8388608 | tf_op jit(solution)/shard_map/while
  333.3 10.7 %slice-start = ((s8[16777216]{0:T(1024)(128)(4,1)}), s8[4194304]{0:T(1024)(128)(4,1)S(1)}, s32[]{:S(2)}) async-start(s8[16777216]{0:T(1024)(128)(4,1)} %bitcast.29), calls=%async_computation.4 | async-start | bytes 8388608 | tf_op jit(solution)/shard_map/while
  336.4 7.6 %slice-start.1 = ((s8[16777216]{0:T(1024)(128)(4,1)}), s8[4194304]{0:T(1024)(128)(4,1)S(1)}, s32[]{:S(2)}) async-start(s8[16777216]{0:T(1024)(128)(4,1)} %bitcast.29), calls=%async_computation.5 | async-start | bytes 8388608 | tf_op jit(solution)/shard_map/while
  380.6 72.4 %copy-start.2 = (bf16[256,256]{1,0:T(8,128)(2,1)S(1)}, bf16[256,256]{1,0:T(8,128)(2,1)}, u32[]{:S(2)}) copy-start(bf16[256,256]{1,0:T(8,128)(2,1)} %param.13) | copy-start | bytes 393220
  380.6 201.1 %all-reduce.2.cloned.1.call-start = ((), (), s32[]{:S(2)}) async-start(), calls=%async_computation.3 | async-start | bytes 524288 | tf_op jit(solution)/shard_map/psum | solution.py:55
  (25 other events, 133.5 us)
Sparse Core Ops, SparseCore 0:
  10.2 82.8 all-gather.1
  380.7 69.7 reduce-scatter.1
  457.5 124.1 all-reduce.1
where the time goes:
time: 593 us; the launch traced here: 590 us
  waiting for transfers between devices  264 us (45%)
  local copies, waits for them, and re-layouts  146 us (25%)
  matrix products  142 us (24%)
  other arithmetic  22.5 us (4%)
  between operations  13.8 us (2%)
    psum x1, waiting for transfers between devices, body(): grad_weight = lax.psum(weight_term, ('row', 'col'))  126 us
    while x120, local copies, waits for them, and re-layouts  108 us
    dot_general x10, matrix products, add_group(): jnp.dot(both_place, both_vals, preferred_element_type=jnp.float32)  84.4 us
    reduce_scatter x1, waiting for transfers between devices, body(): lax.psum_scatter(partial_value.astype(jnp.bfloat16), 'row', scatter_dimen...  69.9 us
    all_gather x1, waiting for transfers between devices, body(): block = lax.all_gather(masked, 'col', axis=0, tiled=True)  68.4 us
    dot_general x10, matrix products, add_group(): jnp.dot(pick, row_flat, preferred_element_type=jnp.float32)  31 us
    dot_general x10, matrix products, add_group(): jnp.einsum('kab,kaf->kbf', tile_blk, gathered, preferred_element_type=jnp...  21.4 us
    unnamed x10, local copies, waits for them, and re-layouts  16.4 us
  transfers between devices with their start and end apart: 3, of which 3 were waited for; matrix products, arithmetic and copies ran while one was open for 3% of the time, Pallas kernels for 0%

commit v1 on v0

v1 whole, which is shorter than its diff:
```python
import functools

import jax
import jax.numpy as jnp
from jax import lax
from jax.experimental import pallas as pl
from jax.experimental.pallas import tpu as pltpu
from jax.sharding import PartitionSpec as P

SIDE = 128
UNROLL = 8
PREP_GROUP = 32
VMEM_BYTES = 60 * 1024 * 1024


def prep_kernel(order_ref, tiles_ref, out_ref, t_in, t_out, in_sem, out_sem):
    groups = t_in.shape[0] // PREP_GROUP
    loads = [
        pltpu.make_async_copy(
            tiles_ref.at[pl.ds(g * PREP_GROUP, PREP_GROUP)], t_in.at[pl.ds(g * PREP_GROUP, PREP_GROUP)], in_sem.at[g]
        )
        for g in range(groups)
    ]
    for load in loads:
        load.start()
    for load in loads:
        load.wait()
    stores = []
    for g in range(groups):

        def one(step, carry, g=g):
            for u in range(4):
                k = g * PREP_GROUP + step * 4 + u
                t_out[k] = t_in[order_ref[k]].T
            return carry

        lax.fori_loop(0, PREP_GROUP // 4, one, 0)
        store = pltpu.make_async_copy(
            t_out.at[pl.ds(g * PREP_GROUP, PREP_GROUP)], out_ref.at[pl.ds(g * PREP_GROUP, PREP_GROUP)], out_sem.at[g]
        )
        store.start()
        stores.append(store)
    for store in stores:
        store.wait()


def prep(order, tile_stack):
    slots = tile_stack.shape[0]
    groups = slots // PREP_GROUP
    return pl.pallas_call(
        prep_kernel,
        out_shape=jax.ShapeDtypeStruct(tile_stack.shape, tile_stack.dtype),
        grid_spec=pltpu.PrefetchScalarGridSpec(
            num_scalar_prefetch=1,
            grid=(),
            in_specs=[pl.BlockSpec(memory_space=pl.ANY)],
            out_specs=pl.BlockSpec(memory_space=pl.ANY),
            scratch_shapes=[
                pltpu.VMEM(tile_stack.shape, tile_stack.dtype),
                pltpu.VMEM(tile_stack.shape, tile_stack.dtype),
                pltpu.SemaphoreType.DMA((groups,)),
                pltpu.SemaphoreType.DMA((groups,)),
            ],
        ),
        compiler_params=pltpu.CompilerParams(vmem_limit_bytes=VMEM_BYTES),
        cost_estimate=pl.CostEstimate(flops=0, bytes_accessed=2 * tile_stack.size * 2, transcendentals=0),
        name="sort_tiles",
    )(order, tile_stack)


def spmm_kernel(n_pieces, rows_ref, cols_ref, same_ref, count_ref, *refs):
    pieces = refs[:n_pieces]
    tiles_ref, send_ref, keep_ref, m_vmem, t_vmem, o_vmem, total_ref, piece_sem, tile_sem, out_sem = refs[n_pieces:]
    nodes = pieces[0].shape[0]
    slots = t_vmem.shape[0]
    groups = slots // PREP_GROUP
    half = send_ref.shape[0]
    width = o_vmem.shape[1]
    piece_copies = [
        pltpu.make_async_copy(piece, m_vmem.at[pl.ds(p * nodes, nodes)], piece_sem.at[p]) for p, piece in enumerate(pieces)
    ]
    tile_copies = [
        pltpu.make_async_copy(
            tiles_ref.at[pl.ds(g * PREP_GROUP, PREP_GROUP)], t_vmem.at[pl.ds(g * PREP_GROUP, PREP_GROUP)], tile_sem.at[g]
        )
        for g in range(groups)
    ]
    for copy in piece_copies:
        copy.start()
    for copy in tile_copies:
        copy.start()

    def zero(step, carry):
        o_vmem[pl.ds(pl.multiple_of(step * 1024, 1024), 1024), :] = jnp.zeros((1024, width), o_vmem.dtype)
        return carry

    lax.fori_loop(0, 2 * half // 1024, zero, 0)
    for copy in piece_copies:
        copy.wait()
    count = count_ref[0]

    def add_slots(step, carry):
        prods = []
        total = total_ref[...]
        for u in range(UNROLL):
            k = step * UNROLL + u
            block = m_vmem[pl.ds(pl.multiple_of(rows_ref[k] * SIDE, SIDE), SIDE), :]
            prods.append(jnp.dot(t_vmem[k], block, preferred_element_type=jnp.float32))
        for u in range(UNROLL):
            k = step * UNROLL + u
            total = prods[u] + jnp.where(same_ref[k] == 1, total, jnp.zeros_like(total))
            o_vmem[pl.ds(pl.multiple_of(cols_ref[k] * SIDE, SIDE), SIDE), :] = total.astype(o_vmem.dtype)
        total_ref[...] = total
        return carry

    steps = (count + UNROLL - 1) // UNROLL
    per_group = PREP_GROUP // UNROLL
    total_ref[...] = jnp.zeros_like(total_ref)
    for g in range(groups):
        tile_copies[g].wait()
        low = jnp.minimum(steps, g * per_group)
        high = jnp.minimum(steps, (g + 1) * per_group)
        lax.fori_loop(low, high, add_slots, 0)
    out_copies = [
        pltpu.make_async_copy(o_vmem.at[pl.ds(0, half)], send_ref, out_sem.at[0]),
        pltpu.make_async_copy(o_vmem.at[pl.ds(half, half)], keep_ref, out_sem.at[1]),
    ]
    for copy in out_copies:
        copy.start()
    for copy in out_copies:
        copy.wait()


def spmm(rows, cols, same, count, pieces, tiles, n_row):
    nodes, width = pieces[0].shape
    slots = tiles.shape[0]
    groups = slots // PREP_GROUP
    half = n_row // 2 * nodes
    out = jax.ShapeDtypeStruct((half, width), jnp.bfloat16)
    return pl.pallas_call(
        functools.partial(spmm_kernel, len(pieces)),
        out_shape=(out, out),
        grid_spec=pltpu.PrefetchScalarGridSpec(
            num_scalar_prefetch=4,
            grid=(),
            in_specs=[pl.BlockSpec(memory_space=pl.ANY)] * (len(pieces) + 1),
            out_specs=[pl.BlockSpec(memory_space=pl.ANY)] * 2,
            scratch_shapes=[
                pltpu.VMEM((len(pieces) * nodes, width), jnp.bfloat16),
                pltpu.VMEM((slots, SIDE, SIDE), jnp.bfloat16),
                pltpu.VMEM((2 * half + SIDE, width), jnp.bfloat16),
                pltpu.VMEM((SIDE, width), jnp.float32),
                pltpu.SemaphoreType.DMA((len(pieces),)),
                pltpu.SemaphoreType.DMA((groups,)),
                pltpu.SemaphoreType.DMA((2,)),
            ],
        ),
        compiler_params=pltpu.CompilerParams(vmem_limit_bytes=VMEM_BYTES),
        cost_estimate=pl.CostEstimate(
            flops=2 * slots * SIDE * SIDE * width,
            bytes_accessed=2 * (slots * SIDE * SIDE + len(pieces) * nodes * width + 2 * half * width),
            transcendentals=0,
        ),
        name="spmm",
    )(rows, cols, same, count, *pieces, tiles)


def xor_permute(value, axis, mask):
    size = lax.axis_size(axis)
    return lax.ppermute(value, axis, [(i, i ^ mask) for i in range(size)])


def tree_sum(values):
    while len(values) > 1:
        values = [a + b for a, b in zip(values[::2], values[1::2])]
    return values[0]


def add_bf16(a, b):
    return (a.astype(jnp.float32) + b.astype(jnp.float32)).astype(jnp.bfloat16)


def reduce_scatter(keep, recv, bits, row):
    for pos in bits:
        axis = [b for b in sorted(bits, reverse=True) if b in reduce_scatter_left(bits, pos)].index(pos)
        mine = (row >> pos) & 1

        def pick(which, axis=axis):
            return add_bf16(
                lax.dynamic_index_in_dim(keep, which, axis, keepdims=False),
                lax.dynamic_index_in_dim(recv, which, axis, keepdims=False),
            )

        sent = pick(1 - mine)
        keep = pick(mine)
        recv = xor_permute(sent, "row", 1 << pos)
    return keep.astype(jnp.float32) + recv.astype(jnp.float32)


def reduce_scatter_left(bits, pos):
    return bits[bits.index(pos):]


def body(grad_out, preact, features, weight, tiles, tile_rows, tile_cols, live_counts):
    nodes, width = grad_out.shape
    n_row, n_col = lax.axis_size("row"), lax.axis_size("col")
    row, col = lax.axis_index("row"), lax.axis_index("col")
    slots = tiles.shape[2]
    per_dev = nodes // SIDE
    n_chunks = 2
    cw = width // n_chunks

    pieces = []
    for h in range(n_chunks):
        cols_h = slice(h * cw, (h + 1) * cw)
        masked = jnp.where(preact[:, cols_h] > 0, grad_out[:, cols_h], jnp.zeros_like(grad_out[:, cols_h]))
        pieces.append([masked] + [xor_permute(masked, "col", k) for k in range(1, n_col)])

    count = live_counts.reshape(1)
    row_index = tile_rows.reshape(slots)
    col_index = tile_cols.reshape(slots)
    row_pos = ((row_index // per_dev) ^ col) * per_dev + row_index % per_dev
    target = col_index // per_dev
    own_core = 1 - ((target & 1) ^ (row & 1))
    col_pos = (own_core * (n_row // 2) + target // 2) * per_dev + col_index % per_dev
    ids = jnp.arange(slots, dtype=jnp.int32)
    col_pos = jnp.where(ids < count, col_pos, n_row * per_dev)
    before = (col_pos[None, :] < col_pos[:, None]) | ((col_pos[None, :] == col_pos[:, None]) & (ids[None, :] < ids[:, None]))
    rank = jnp.sum(before.astype(jnp.int32), axis=1)
    hit = rank[None, :] == ids[:, None]

    def permuted(values):
        return jnp.sum(jnp.where(hit, values[None, :], 0), axis=1)

    order = permuted(ids)
    rows_sorted = permuted(row_pos)
    cols_sorted = permuted(col_pos)
    same = jnp.concatenate([jnp.zeros((1,), jnp.int32), (cols_sorted[1:] == cols_sorted[:-1]).astype(jnp.int32)])
    tiles_sorted = prep(order, tiles.reshape(slots, SIDE, SIDE))

    bits = list(range(1, n_row.bit_length() - 1))
    summed, terms = [], []
    for h in range(n_chunks):
        send, keep = spmm(rows_sorted, cols_sorted, same, count, pieces[h], tiles_sorted, n_row)
        recv = xor_permute(send, "row", 1)
        lead = (2,) * len(bits)
        keep = keep.reshape(lead + (nodes, cw))
        recv = recv.reshape(lead + (nodes, cw))
        first = reduce_scatter(keep[..., : nodes // 2, :], recv[..., : nodes // 2, :], bits, row)
        second = reduce_scatter(keep[..., nodes // 2 :, :], recv[..., nodes // 2 :, :], bits[::-1], row)
        colgrad = jnp.concatenate([first, second], axis=0).astype(jnp.bfloat16)
        summed.append(colgrad)
        term = lax.dot_general(features, colgrad, (((0,), (0,)), ((), ())), preferred_element_type=jnp.float32)
        term = term.astype(jnp.bfloat16)
        term = term.astype(jnp.float32) + xor_permute(term, "row", 1).astype(jnp.float32)
        for axis, masks in (("row", range(2, n_row, 2)), ("col", range(1, n_col))):
            term = term.astype(jnp.bfloat16)
            parts = [term] + [xor_permute(term, axis, m) for m in masks]
            term = tree_sum([p.astype(jnp.float32) for p in parts])
        terms.append(term)
    colgrad = jnp.concatenate(summed, axis=1)
    grad_features = lax.dot_general(
        colgrad, weight, (((1,), (1,)), ((), ())), preferred_element_type=jnp.float32
    ).astype(jnp.bfloat16)
    grad_weight = jnp.concatenate(terms, axis=1)
    return (grad_features, grad_weight)


def solution(mesh):
    in_specs = (
        P(("row", "col"), None),
        P(("row", "col"), None),
        P(("col", "row"), None),
        P(),
        P("row", "col", None, None, None),
        P("row", "col", None),
        P("row", "col", None),
        P("row", "col"),
    )
    out_specs = (P(("col", "row"), None), P())
    return jax.shard_map(body, mesh=mesh, in_specs=in_specs, out_specs=out_specs, check_vma=False)
```

time: 593 us -> 181 us (0.31)
  waiting for transfers between devices: 264 us -> 72.4 us
  local copies, waits for them, and re-layouts: 146 us -> 6.07 us
  matrix products: 142 us -> 2.24 us
  starting transfers between devices: 0.12 us -> 52.9 us
  Pallas kernels: 0 us -> 38 us
  other arithmetic: 22.5 us -> 5.7 us
  between operations: 13.8 us -> 1.61 us
    dot_general x32 -> x3, matrix products: 142 us -> 2.24 us  [the longest x1 1.46 us: body(): lax.dot_general(colgrad, weight, (((1,), (1,)), ((), ())), preferred_elem...]
    psum x1 -> x0, waiting for transfers between devices: 126 us -> none  [body(): grad_weight = lax.psum(weight_term, ('row', 'col'))]
    while x120 -> x0, local copies, waits for them, and re-layouts: 108 us -> none
    ppermute x0 -> x30, waiting for transfers between devices: none -> 72.4 us  [xor_permute(): return lax.ppermute(value, axis, [(i, i ^ mask) for i in range(size)])]
    reduce_scatter x1 -> x0, waiting for transfers between devices: 69.9 us -> none  [body(): lax.psum_scatter(partial_value.astype(jnp.bfloat16), 'row', scatter_dimen...]
    all_gather x1 -> x0, waiting for transfers between devices: 68.4 us -> none  [body(): block = lax.all_gather(masked, 'col', axis=0, tiled=True)]
    ppermute x0 -> x30, starting transfers between devices: none -> 52.9 us  [xor_permute(): return lax.ppermute(value, axis, [(i, i ^ mask) for i in range(size)])]
    pallas_call x0 -> x3, Pallas kernels: none -> 38 us  [the longest x2 25 us: spmm(): pl.pallas_call(functools.partial(spmm_kernel, len(pieces)), out_shape=(ou...]
  transfers between devices with their start and end apart: 3 -> 30, of which waited for: 3 -> 10; matrix products, arithmetic and copies ran while one was open for 3% -> 6% of each run, Pallas kernels for 0% -> 21%
where the time goes in v1:
time: 181 us; the launch traced here: 179 us
  waiting for transfers between devices  72.4 us (40%)
  starting transfers between devices  52.9 us (29%)
  Pallas kernels  38 us (21%)
  local copies, waits for them, and re-layouts  6.07 us (3%)
  other arithmetic  5.7 us (3%)
  matrix products  2.24 us (1%)
    ppermute x30, waiting for transfers between devices, xor_permute(): return lax.ppermute(value, axis, [(i, i ^ mask) for i in range(size)])  72.4 us
    ppermute x30, starting transfers between devices, xor_permute(): return lax.ppermute(value, axis, [(i, i ^ mask) for i in range(size)])  52.9 us
    pallas_call x2, Pallas kernels, spmm(): pl.pallas_call(functools.partial(spmm_kernel, len(pieces)), out_shape=(ou...  25 us
    pallas_call x1, Pallas kernels, prep(): pl.pallas_call(prep_kernel, out_shape=jax.ShapeDtypeStruct(tile_stack.sha...  13 us
  transfers between devices with their start and end apart: 30, of which 10 were waited for; matrix products, arithmetic and copies ran while one was open for 6% of the time, Pallas kernels for 21%

profile of v1, /device:TPU:1, one launch (start us, length us, event | category | flops | bytes accessed | tf_op | source)
XLA Modules:
  0.0 178.9 jit_solution(13390826268406147562)
XLA Ops:
  0.7 1.7 compare_select_fusion.1
  2.4 2.2 %collective-permute-start.8 = (bf16[2048,128]{1,0:T(8,128)(2,1)S(1)}, bf16[2048,128]{1,0:T(8,128)(2,1)}, u32[]{:S(2)}, u32[]{:S(2)}) collective-permute-start(bf16[2048,128]{1,0:T(8,128)(2,1)S(1)} %get-tuple-element.26.refs_0_), channel_id=1, source_target_pairs={{0,1},{1,0},{2,3},{3,2},{4,5},{5,4},{6,7},{7,6},{8,9},{9,8},{10,11... | collective-permute-start | bytes 1572872 | tf_op jit(solution)/shard_map/ppermute | solution.py:170
  4.6 2.3 %collective-permute-start.9 = (bf16[2048,128]{1,0:T(8,128)(2,1)S(1)}, bf16[2048,128]{1,0:T(8,128)(2,1)}, u32[]{:S(2)}, u32[]{:S(2)}) collective-permute-start(bf16[2048,128]{1,0:T(8,128)(2,1)S(1)} %get-tuple-element.26.refs_0_), channel_id=1, source_target_pairs={{0,2},{1,3},{2,0},{3,1},{4,6},{5,7},{6,4},{7,5},{8,10},{9,11},{10,... | collective-permute-start | bytes 1572872 | tf_op jit(solution)/shard_map/ppermute | solution.py:170
  7.2 3.2 %collective-permute-start.1 = (bf16[2048,128]{1,0:T(8,128)(2,1)S(1)}, bf16[2048,128]{1,0:T(8,128)(2,1)S(1)}, u32[]{:S(2)}, u32[]{:S(2)}) collective-permute-start(bf16[2048,128]{1,0:T(8,128)(2,1)S(1)} %get-tuple-element.25.refs_0_), channel_id=1, source_target_pairs={{0,2},{1,3},{2,0},{3,1},{4,6},{5,7},{6,4},{7,5},{8,10},{9,11},{10,... | collective-permute-start | bytes 1572872 | tf_op jit(solution)/shard_map/ppermute | solution.py:170
  12.4 13.0 %sort_tiles.1.refs_4_ = bf16[320,128,128]{2,1,0:T(8,128)(2,1)} custom-call(s32[320]{0:T(512)} %get-tuple-element.14.order_ref, bf16[320,128,128]{2,1,0:T(8,128)(2,1)} %bitcast.77), custom_call_target="tpu_custom_call" | custom-call | bytes 20971520 | tf_op jit(solution)/shard_map/sort_tiles/pallas_call | solution.py:50
  26.8 2.6 %collective-permute-start.2 = (bf16[2048,128]{1,0:T(8,128)(2,1)S(1)}, bf16[2048,128]{1,0:T(8,128)(2,1)S(1)}, u32[]{:S(2)}, u32[]{:S(2)}) collective-permute-start(bf16[2048,128]{1,0:T(8,128)(2,1)S(1)} %get-tuple-element.25.refs_0_), channel_id=1, source_target_pairs={{0,3},{1,2},{2,1},{3,0},{4,7},{5,6},{6,5},{7,4},{8,11},{9,10},{10,... | collective-permute-start | bytes 1572872 | tf_op jit(solution)/shard_map/ppermute | solution.py:170
  29.4 11.3 %collective-permute-done.10.refs_3_ = bf16[2048,128]{1,0:T(8,128)(2,1)} collective-permute-done((bf16[2048,128]{1,0:T(8,128)(2,1)S(1)}, bf16[2048,128]{1,0:T(8,128)(2,1)}, u32[]{:S(2)}, u32[]{:S(2)}) %collective-permute-start.10) | collective-permute-done | bytes 524320 | tf_op jit(solution)/shard_map/ppermute | solution.py:170
  40.8 12.5 %spmm.3 = (bf16[8192,128]{1,0:T(8,128)(2,1)}, bf16[8192,128]{1,0:T(8,128)(2,1)}) custom-call(s32[320]{0:T(512)} %get-tuple-element.16.rows_ref, s32[320]{0:T(512)} %copy-done.7, s32[320]{0:T(512)} %add_convert_fusion.12.same_ref, s32[1]{0:T(128)} %bitcast.76.count_ref, bf16[2048,128]{1,0:T(8,128)(2,1)} %copy-done.3, ...), custom_call_target="tpu_custom_call" | custom-call | flops 1342177280 | bytes 16777216 | tf_op jit(solution)/shard_map/spmm/pallas_call | solution.py:140
  53.3 3.2 %collective-permute-start.11 = (bf16[8192,128]{1,0:T(8,128)(2,1)}, bf16[8192,128]{1,0:T(8,128)(2,1)}, u32[]{:S(2)}, u32[]{:S(2)}) collective-permute-start(bf16[8192,128]{1,0:T(8,128)(2,1)} %get-tuple-element.9), channel_id=1, source_target_pairs={{0,4},{4,0},{8,12},{12,8},{16,20},{20,16},{24,28},{28,24},{1,5},{5... | collective-permute-start | bytes 6291464 | tf_op jit(solution)/shard_map/ppermute | solution.py:170
  56.5 29.0 %collective-permute-done.1.refs_2_ = bf16[2048,128]{1,0:T(8,128)(2,1)S(1)} collective-permute-done((bf16[2048,128]{1,0:T(8,128)(2,1)S(1)}, bf16[2048,128]{1,0:T(8,128)(2,1)S(1)}, u32[]{:S(2)}, u32[]{:S(2)}) %collective-permute-start.1) | collective-permute-done | bytes 524320 | tf_op jit(solution)/shard_map/ppermute | solution.py:170
  86.5 12.4 %spmm.2 = (bf16[8192,128]{1,0:T(8,128)(2,1)}, bf16[8192,128]{1,0:T(8,128)(2,1)}) custom-call(s32[320]{0:T(512)} %get-tuple-element.16.rows_ref, s32[320]{0:T(512)} %copy-done.7, s32[320]{0:T(512)} %add_convert_fusion.12.same_ref, s32[1]{0:T(128)} %bitcast.75.count_ref, bf16[2048,128]{1,0:T(8,128)(2,1)} %copy-done.2, bf16[2048,128]{1,0:T(8,128)(2,1)} %copy-done.4, ...), custom_call_target="tpu_custom_call" | custom-call | flops 1342177280 | bytes 16777216 | tf_op jit(solution)/shard_map/spmm/pallas_call | solution.py:140
  99.0 3.4 %collective-permute-start.3 = (bf16[8192,128]{1,0:T(8,128)(2,1)}, bf16[8192,128]{1,0:T(8,128)(2,1)S(1)}, u32[]{:S(2)}, u32[]{:S(2)}) collective-permute-start(bf16[8192,128]{1,0:T(8,128)(2,1)} %get-tuple-element.7), channel_id=1, source_target_pairs={{0,4},{4,0},{8,12},{12,8},{16,20},{20,16},{24,28},{28,24},{1,5},{5... | collective-permute-start | bytes 6291464 | tf_op jit(solution)/shard_map/ppermute | solution.py:170
  102.3 1.8 %fusion.58 = (bf16[2,2,1024,128]{3,2,1,0:T(8,128)(2,1)S(1)}, bf16[2,2,1024,128]{3,2,1,0:T(8,128)(2,1)S(1)}) fusion(bf16[2,2,2048,128]{3,2,1,0:T(8,128)(2,1)} %bitcast.79), kind=kLoop, calls=%fused_computation.116 | loop fusion | bytes 4194304 | tf_op jit(solution)/shard_map/slice | solution.py:249
  104.7 1.7 fusion.59
  108.0 2.2 %collective-permute-start.12 = (bf16[2,1024,128]{2,1,0:T(8,128)(2,1)S(1)}, bf16[2,1024,128]{2,1,0:T(8,128)(2,1)S(1)}, u32[]{:S(2)}, u32[]{:S(2)}) collective-permute-start(bf16[2,1024,128]{2,1,0:T(8,128)(2,1)S(1)} %get-tuple-element.28), channel_id=1, source_target_pairs={{0,8},{4,12},{8,0},{12,4},{16,24},{20,28},{24,16},{28,20},{1,9},{5... | collective-permute-start | bytes 1572872 | tf_op jit(solution)/shard_map/ppermute | solution.py:170
  111.1 9.2 %collective-permute-done.14 = bf16[2,1024,128]{2,1,0:T(8,128)(2,1)S(1)} collective-permute-done((bf16[2,1024,128]{2,1,0:T(8,128)(2,1)S(1)}, bf16[2,1024,128]{2,1,0:T(8,128)(2,1)S(1)}, u32[]{:S(2)}, u32[]{:S(2)}) %collective-permute-start.14) | collective-permute-done | bytes 524320 | tf_op jit(solution)/shard_map/ppermute | solution.py:170
  120.4 1.9 %collective-permute-start.15 = (bf16[1024,128]{1,0:T(8,128)(2,1)S(1)}, bf16[1024,128]{1,0:T(8,128)(2,1)S(1)}, u32[]{:S(2)}, u32[]{:S(2)}) collective-permute-start(bf16[1024,128]{1,0:T(8,128)(2,1)S(1)} %fusion.40), channel_id=1, source_target_pairs={{0,8},{4,12},{8,0},{12,4},{16,24},{20,28},{24,16},{28,20},{1,9},{5... | collective-permute-start | bytes 786440 | tf_op jit(solution)/shard_map/ppermute | solution.py:170
  122.3 1.3 collective-permute-start.13
  123.7 7.9 %collective-permute-done.6 = bf16[2,1024,128]{2,1,0:T(8,128)(2,1)S(1)} collective-permute-done((bf16[2,1024,128]{2,1,0:T(8,128)(2,1)S(1)}, bf16[2,1024,128]{2,1,0:T(8,128)(2,1)S(1)}, u32[]{:S(2)}, u32[]{:S(2)}) %collective-permute-start.6) | collective-permute-done | bytes 524320 | tf_op jit(solution)/shard_map/ppermute | solution.py:170
  131.6 1.9 %collective-permute-start.7 = (bf16[1024,128]{1,0:T(8,128)(2,1)S(1)}, bf16[1024,128]{1,0:T(8,128)(2,1)S(1)}, u32[]{:S(2)}, u32[]{:S(2)}) collective-permute-start(bf16[1024,128]{1,0:T(8,128)(2,1)S(1)} %fusion.36), channel_id=1, source_target_pairs={{0,8},{4,12},{8,0},{12,4},{16,24},{20,28},{24,16},{28,20},{1,9},{5... | collective-permute-start | bytes 786440 | tf_op jit(solution)/shard_map/ppermute | solution.py:170
  133.6 1.3 collective-permute-start.5
  134.9 4.2 %collective-permute-done.15 = bf16[1024,128]{1,0:T(8,128)(2,1)S(1)} collective-permute-done((bf16[1024,128]{1,0:T(8,128)(2,1)S(1)}, bf16[1024,128]{1,0:T(8,128)(2,1)S(1)}, u32[]{:S(2)}, u32[]{:S(2)}) %collective-permute-start.15) | collective-permute-done | bytes 262176 | tf_op jit(solution)/shard_map/ppermute | solution.py:170
  139.7 1.4 collective-permute-start.23
  141.1 3.6 %collective-permute-done.7 = bf16[1024,128]{1,0:T(8,128)(2,1)S(1)} collective-permute-done((bf16[1024,128]{1,0:T(8,128)(2,1)S(1)}, bf16[1024,128]{1,0:T(8,128)(2,1)S(1)}, u32[]{:S(2)}, u32[]{:S(2)}) %collective-permute-start.7) | collective-permute-done | bytes 262176 | tf_op jit(solution)/shard_map/ppermute | solution.py:170
  144.9 1.5 convolution_convert_fusion
  149.0 1.5 collective-permute-start.25
  151.7 1.5 collective-permute-start.18
  154.2 3.4 %collective-permute-start.29 = (bf16[256,128]{0,1:T(8,128)(2,1)S(1)}, bf16[256,128]{0,1:T(8,128)(2,1)S(1)}, u32[]{:S(2)}, u32[]{:S(2)}) collective-permute-start(bf16[256,128]{0,1:T(8,128)(2,1)S(1)} %add_convert_fusion.8), channel_id=1, source_target_pairs={{0,3},{1,2},{2,1},{3,0},{4,7},{5,6},{6,5},{7,4},{8,11},{9,10},{10,... | collective-permute-start | bytes 196616 | tf_op jit(solution)/shard_map/ppermute | solution.py:170
  157.6 10.2 %collective-permute-start.28 = (bf16[256,128]{0,1:T(8,128)(2,1)S(1)}, bf16[256,128]{0,1:T(8,128)(2,1)S(1)}, u32[]{:S(2)}, u32[]{:S(2)}) collective-permute-start(bf16[256,128]{0,1:T(8,128)(2,1)S(1)} %add_convert_fusion.8), channel_id=1, source_target_pairs={{0,2},{1,3},{2,0},{3,1},{4,6},{5,7},{6,4},{7,5},{8,10},{9,11},{10,... | collective-permute-start | bytes 196616 | tf_op jit(solution)/shard_map/ppermute | solution.py:170
  168.1 1.9 %collective-permute-start.22 = (bf16[256,128]{0,1:T(8,128)(2,1)S(1)}, bf16[256,128]{0,1:T(8,128)(2,1)S(1)}, u32[]{:S(2)}, u32[]{:S(2)}) collective-permute-start(bf16[256,128]{0,1:T(8,128)(2,1)S(1)} %add_convert_fusion.10), channel_id=1, source_target_pairs={{0,3},{1,2},{2,1},{3,0},{4,7},{5,6},{6,5},{7,4},{8,11},{9,10},{10,... | collective-permute-start | bytes 196616 | tf_op jit(solution)/shard_map/ppermute | solution.py:170
  171.7 2.1 %collective-permute-done.22 = bf16[256,128]{0,1:T(8,128)(2,1)S(1)} collective-permute-done((bf16[256,128]{0,1:T(8,128)(2,1)S(1)}, bf16[256,128]{0,1:T(8,128)(2,1)S(1)}, u32[]{:S(2)}, u32[]{:S(2)}) %collective-permute-start.22) | collective-permute-done | bytes 65568 | tf_op jit(solution)/shard_map/ppermute | solution.py:170
  173.9 4.1 %collective-permute-done.21 = bf16[256,128]{0,1:T(8,128)(2,1)S(1)} collective-permute-done((bf16[256,128]{0,1:T(8,128)(2,1)S(1)}, bf16[256,128]{0,1:T(8,128)(2,1)S(1)}, u32[]{:S(2)}, u32[]{:S(2)}) %collective-permute-start.21) | collective-permute-done | bytes 65568 | tf_op jit(solution)/shard_map/ppermute | solution.py:170
  (88 shorter events, 15.9 us)
Async XLA Ops:
  0.6 138.7 %copy-start = (bf16[2048,256]{1,0:T(8,128)(2,1)S(1)}, bf16[2048,256]{1,0:T(8,128)(2,1)}, u32[]{:S(2)}) copy-start(bf16[2048,256]{1,0:T(8,128)(2,1)} %param.10) | copy-start | bytes 3145732
  2.4 24.4 %collective-permute-start.8 = (bf16[2048,128]{1,0:T(8,128)(2,1)S(1)}, bf16[2048,128]{1,0:T(8,128)(2,1)}, u32[]{:S(2)}, u32[]{:S(2)}) collective-permute-start(bf16[2048,128]{1,0:T(8,128)(2,1)S(1)} %get-tuple-element.26.refs_0_), channel_id=1, source_target_pairs={{0,1},{1,0},{2,3},{3,2},{4,5},{5,4},{6,7},{7,6},{8,9},{9,8},{10,11... | collective-permute-start | bytes 1572872 | tf_op jit(solution)/shard_map/ppermute | solution.py:170
  4.6 24.8 %collective-permute-start.9 = (bf16[2048,128]{1,0:T(8,128)(2,1)S(1)}, bf16[2048,128]{1,0:T(8,128)(2,1)}, u32[]{:S(2)}, u32[]{:S(2)}) collective-permute-start(bf16[2048,128]{1,0:T(8,128)(2,1)S(1)} %get-tuple-element.26.refs_0_), channel_id=1, source_target_pairs={{0,2},{1,3},{2,0},{3,1},{4,6},{5,7},{6,4},{7,5},{8,10},{9,11},{10,... | collective-permute-start | bytes 1572872 | tf_op jit(solution)/shard_map/ppermute | solution.py:170
  6.9 33.9 %collective-permute-start.10 = (bf16[2048,128]{1,0:T(8,128)(2,1)S(1)}, bf16[2048,128]{1,0:T(8,128)(2,1)}, u32[]{:S(2)}, u32[]{:S(2)}) collective-permute-start(bf16[2048,128]{1,0:T(8,128)(2,1)S(1)} %get-tuple-element.26.refs_0_), channel_id=1, source_target_pairs={{0,3},{1,2},{2,1},{3,0},{4,7},{5,6},{6,5},{7,4},{8,11},{9,10},{10,... | collective-permute-start | bytes 1572872 | tf_op jit(solution)/shard_map/ppermute | solution.py:170
  6.9 49.6 %collective-permute-start = (bf16[2048,128]{1,0:T(8,128)(2,1)S(1)}, bf16[2048,128]{1,0:T(8,128)(2,1)S(1)}, u32[]{:S(2)}, u32[]{:S(2)}) collective-permute-start(bf16[2048,128]{1,0:T(8,128)(2,1)S(1)} %get-tuple-element.25.refs_0_), channel_id=1, source_target_pairs={{0,1},{1,0},{2,3},{3,2},{4,5},{5,4},{6,7},{7,6},{8,9},{9,8},{10,11... | collective-permute-start | bytes 1572872 | tf_op jit(solution)/shard_map/ppermute | solution.py:170
  7.2 78.3 %collective-permute-start.1 = (bf16[2048,128]{1,0:T(8,128)(2,1)S(1)}, bf16[2048,128]{1,0:T(8,128)(2,1)S(1)}, u32[]{:S(2)}, u32[]{:S(2)}) collective-permute-start(bf16[2048,128]{1,0:T(8,128)(2,1)S(1)} %get-tuple-element.25.refs_0_), channel_id=1, source_target_pairs={{0,2},{1,3},{2,0},{3,1},{4,6},{5,7},{6,4},{7,5},{8,10},{9,11},{10,... | collective-permute-start | bytes 1572872 | tf_op jit(solution)/shard_map/ppermute | solution.py:170
  26.8 58.7 %collective-permute-start.2 = (bf16[2048,128]{1,0:T(8,128)(2,1)S(1)}, bf16[2048,128]{1,0:T(8,128)(2,1)S(1)}, u32[]{:S(2)}, u32[]{:S(2)}) collective-permute-start(bf16[2048,128]{1,0:T(8,128)(2,1)S(1)} %get-tuple-element.25.refs_0_), channel_id=1, source_target_pairs={{0,3},{1,2},{2,1},{3,0},{4,7},{5,6},{6,5},{7,4},{8,11},{9,10},{10,... | collective-permute-start | bytes 1572872 | tf_op jit(solution)/shard_map/ppermute | solution.py:170
  53.3 51.4 %collective-permute-start.11 = (bf16[8192,128]{1,0:T(8,128)(2,1)}, bf16[8192,128]{1,0:T(8,128)(2,1)}, u32[]{:S(2)}, u32[]{:S(2)}) collective-permute-start(bf16[8192,128]{1,0:T(8,128)(2,1)} %get-tuple-element.9), channel_id=1, source_target_pairs={{0,4},{4,0},{8,12},{12,8},{16,20},{20,16},{24,28},{28,24},{1,5},{5... | collective-permute-start | bytes 6291464 | tf_op jit(solution)/shard_map/ppermute | solution.py:170
  56.5 29.0 %copy-start.4 = (bf16[2048,128]{1,0:T(8,128)(2,1)}, bf16[2048,128]{1,0:T(8,128)(2,1)S(1)}, u32[]{:S(2)}) copy-start(bf16[2048,128]{1,0:T(8,128)(2,1)S(1)} %collective-permute-done.refs_1_) | copy-start | bytes 1572868
  99.0 11.2 %collective-permute-start.3 = (bf16[8192,128]{1,0:T(8,128)(2,1)}, bf16[8192,128]{1,0:T(8,128)(2,1)S(1)}, u32[]{:S(2)}, u32[]{:S(2)}) collective-permute-start(bf16[8192,128]{1,0:T(8,128)(2,1)} %get-tuple-element.7), channel_id=1, source_target_pairs={{0,4},{4,0},{8,12},{12,8},{16,20},{20,16},{24,28},{28,24},{1,5},{5... | collective-permute-start | bytes 6291464 | tf_op jit(solution)/shard_map/ppermute | solution.py:170
  106.7 13.6 %collective-permute-start.14 = (bf16[2,1024,128]{2,1,0:T(8,128)(2,1)S(1)}, bf16[2,1024,128]{2,1,0:T(8,128)(2,1)S(1)}, u32[]{:S(2)}, u32[]{:S(2)}) collective-permute-start(bf16[2,1024,128]{2,1,0:T(8,128)(2,1)S(1)} %get-tuple-element.34), channel_id=1, source_target_pairs={{0,16},{4,20},{8,24},{12,28},{16,0},{20,4},{24,8},{28,12},{1,17},{... | collective-permute-start | bytes 1572872 | tf_op jit(solution)/shard_map/ppermute | solution.py:170
  108.0 14.3 %collective-permute-start.12 = (bf16[2,1024,128]{2,1,0:T(8,128)(2,1)S(1)}, bf16[2,1024,128]{2,1,0:T(8,128)(2,1)S(1)}, u32[]{:S(2)}, u32[]{:S(2)}) collective-permute-start(bf16[2,1024,128]{2,1,0:T(8,128)(2,1)S(1)} %get-tuple-element.28), channel_id=1, source_target_pairs={{0,8},{4,12},{8,0},{12,4},{16,24},{20,28},{24,16},{28,20},{1,9},{5... | collective-permute-start | bytes 1572872 | tf_op jit(solution)/shard_map/ppermute | solution.py:170
  110.6 20.9 %collective-permute-start.6 = (bf16[2,1024,128]{2,1,0:T(8,128)(2,1)S(1)}, bf16[2,1024,128]{2,1,0:T(8,128)(2,1)S(1)}, u32[]{:S(2)}, u32[]{:S(2)}) collective-permute-start(bf16[2,1024,128]{2,1,0:T(8,128)(2,1)S(1)} %get-tuple-element.24), channel_id=1, source_target_pairs={{0,16},{4,20},{8,24},{12,28},{16,0},{20,4},{24,8},{28,12},{1,17},{... | collective-permute-start | bytes 1572872 | tf_op jit(solution)/shard_map/ppermute | solution.py:170
  111.0 22.5 %collective-permute-start.4 = (bf16[2,1024,128]{2,1,0:T(8,128)(2,1)S(1)}, bf16[2,1024,128]{2,1,0:T(8,128)(2,1)S(1)}, u32[]{:S(2)}, u32[]{:S(2)}) collective-permute-start(bf16[2,1024,128]{2,1,0:T(8,128)(2,1)S(1)} %get-tuple-element.18), channel_id=1, source_target_pairs={{0,8},{4,12},{8,0},{12,4},{16,24},{20,28},{24,16},{28,20},{1,9},{5... | collective-permute-start | bytes 1572872 | tf_op jit(solution)/shard_map/ppermute | solution.py:170
  120.4 18.7 %collective-permute-start.15 = (bf16[1024,128]{1,0:T(8,128)(2,1)S(1)}, bf16[1024,128]{1,0:T(8,128)(2,1)S(1)}, u32[]{:S(2)}, u32[]{:S(2)}) collective-permute-start(bf16[1024,128]{1,0:T(8,128)(2,1)S(1)} %fusion.40), channel_id=1, source_target_pairs={{0,8},{4,12},{8,0},{12,4},{16,24},{20,28},{24,16},{28,20},{1,9},{5... | collective-permute-start | bytes 786440 | tf_op jit(solution)/shard_map/ppermute | solution.py:170
  122.3 16.8 %collective-permute-start.13 = (bf16[1024,128]{1,0:T(8,128)(2,1)S(1)}, bf16[1024,128]{1,0:T(8,128)(2,1)S(1)}, u32[]{:S(2)}, u32[]{:S(2)}) collective-permute-start(bf16[1024,128]{1,0:T(8,128)(2,1)S(1)} %fusion.38), channel_id=1, source_target_pairs={{0,16},{4,20},{8,24},{12,28},{16,0},{20,4},{24,8},{28,12},{1,17},{... | collective-permute-start | bytes 786440 | tf_op jit(solution)/shard_map/ppermute | solution.py:170
  131.6 13.1 %collective-permute-start.7 = (bf16[1024,128]{1,0:T(8,128)(2,1)S(1)}, bf16[1024,128]{1,0:T(8,128)(2,1)S(1)}, u32[]{:S(2)}, u32[]{:S(2)}) collective-permute-start(bf16[1024,128]{1,0:T(8,128)(2,1)S(1)} %fusion.36), channel_id=1, source_target_pairs={{0,8},{4,12},{8,0},{12,4},{16,24},{20,28},{24,16},{28,20},{1,9},{5... | collective-permute-start | bytes 786440 | tf_op jit(solution)/shard_map/ppermute | solution.py:170
  133.6 11.2 %collective-permute-start.5 = (bf16[1024,128]{1,0:T(8,128)(2,1)S(1)}, bf16[1024,128]{1,0:T(8,128)(2,1)S(1)}, u32[]{:S(2)}, u32[]{:S(2)}) collective-permute-start(bf16[1024,128]{1,0:T(8,128)(2,1)S(1)} %fusion.34), channel_id=1, source_target_pairs={{0,16},{4,20},{8,24},{12,28},{16,0},{20,4},{24,8},{28,12},{1,17},{... | collective-permute-start | bytes 786440 | tf_op jit(solution)/shard_map/ppermute | solution.py:170
  139.7 8.0 %collective-permute-start.23 = (bf16[256,128]{0,1:T(8,128)(2,1)S(1)}, bf16[256,128]{0,1:T(8,128)(2,1)S(1)}, u32[]{:S(2)}, u32[]{:S(2)}) collective-permute-start(bf16[256,128]{0,1:T(8,128)(2,1)S(1)} %fusion.1), channel_id=1, source_target_pairs={{0,4},{4,0},{8,12},{12,8},{16,20},{20,16},{24,28},{28,24},{1,5},{5... | collective-permute-start | bytes 196616 | tf_op jit(solution)/shard_map/ppermute | solution.py:170
  146.8 3.7 %collective-permute-start.16 = (bf16[256,128]{0,1:T(8,128)(2,1)S(1)}, bf16[256,128]{0,1:T(8,128)(2,1)S(1)}, u32[]{:S(2)}, u32[]{:S(2)}) collective-permute-start(bf16[256,128]{0,1:T(8,128)(2,1)S(1)} %fusion), channel_id=1, source_target_pairs={{0,4},{4,0},{8,12},{12,8},{16,20},{20,16},{24,28},{28,24},{1,5},{5... | collective-permute-start | bytes 196616 | tf_op jit(solution)/shard_map/ppermute | solution.py:170
  147.7 5.5 %collective-permute-start.26 = (bf16[256,128]{0,1:T(8,128)(2,1)S(1)}, bf16[256,128]{0,1:T(8,128)(2,1)S(1)}, u32[]{:S(2)}, u32[]{:S(2)}) collective-permute-start(bf16[256,128]{0,1:T(8,128)(2,1)S(1)} %add_convert_fusion.9), channel_id=1, source_target_pairs={{0,24},{4,28},{8,16},{12,20},{16,8},{20,12},{24,0},{28,4},{1,25},{... | collective-permute-start | bytes 196616 | tf_op jit(solution)/shard_map/ppermute | solution.py:170
  149.0 5.1 %collective-permute-start.25 = (bf16[256,128]{0,1:T(8,128)(2,1)S(1)}, bf16[256,128]{0,1:T(8,128)(2,1)S(1)}, u32[]{:S(2)}, u32[]{:S(2)}) collective-permute-start(bf16[256,128]{0,1:T(8,128)(2,1)S(1)} %add_convert_fusion.9), channel_id=1, source_target_pairs={{0,16},{4,20},{8,24},{12,28},{16,0},{20,4},{24,8},{28,12},{1,17},{... | collective-permute-start | bytes 196616 | tf_op jit(solution)/shard_map/ppermute | solution.py:170
  150.4 3.7 %collective-permute-start.24 = (bf16[256,128]{0,1:T(8,128)(2,1)S(1)}, bf16[256,128]{0,1:T(8,128)(2,1)S(1)}, u32[]{:S(2)}, u32[]{:S(2)}) collective-permute-start(bf16[256,128]{0,1:T(8,128)(2,1)S(1)} %add_convert_fusion.9), channel_id=1, source_target_pairs={{0,8},{4,12},{8,0},{12,4},{16,24},{20,28},{24,16},{28,20},{1,9},{5... | collective-permute-start | bytes 196616 | tf_op jit(solution)/shard_map/ppermute | solution.py:170
  150.5 17.4 %collective-permute-start.19 = (bf16[256,128]{0,1:T(8,128)(2,1)S(1)}, bf16[256,128]{0,1:T(8,128)(2,1)S(1)}, u32[]{:S(2)}, u32[]{:S(2)}) collective-permute-start(bf16[256,128]{0,1:T(8,128)(2,1)S(1)} %add_convert_fusion.11), channel_id=1, source_target_pairs={{0,24},{4,28},{8,16},{12,20},{16,8},{20,12},{24,0},{28,4},{1,25},{... | collective-permute-start | bytes 196616 | tf_op jit(solution)/shard_map/ppermute | solution.py:170
  151.7 16.3 %collective-permute-start.18 = (bf16[256,128]{0,1:T(8,128)(2,1)S(1)}, bf16[256,128]{0,1:T(8,128)(2,1)S(1)}, u32[]{:S(2)}, u32[]{:S(2)}) collective-permute-start(bf16[256,128]{0,1:T(8,128)(2,1)S(1)} %add_convert_fusion.11), channel_id=1, source_target_pairs={{0,16},{4,20},{8,24},{12,28},{16,0},{20,4},{24,8},{28,12},{1,17},{... | collective-permute-start | bytes 196616 | tf_op jit(solution)/shard_map/ppermute | solution.py:170
  153.2 14.9 %collective-permute-start.17 = (bf16[256,128]{0,1:T(8,128)(2,1)S(1)}, bf16[256,128]{0,1:T(8,128)(2,1)S(1)}, u32[]{:S(2)}, u32[]{:S(2)}) collective-permute-start(bf16[256,128]{0,1:T(8,128)(2,1)S(1)} %add_convert_fusion.11), channel_id=1, source_target_pairs={{0,8},{4,12},{8,0},{12,4},{16,24},{20,28},{24,16},{28,20},{1,9},{5... | collective-permute-start | bytes 196616 | tf_op jit(solution)/shard_map/ppermute | solution.py:170
  154.2 16.4 %collective-permute-start.29 = (bf16[256,128]{0,1:T(8,128)(2,1)S(1)}, bf16[256,128]{0,1:T(8,128)(2,1)S(1)}, u32[]{:S(2)}, u32[]{:S(2)}) collective-permute-start(bf16[256,128]{0,1:T(8,128)(2,1)S(1)} %add_convert_fusion.8), channel_id=1, source_target_pairs={{0,3},{1,2},{2,1},{3,0},{4,7},{5,6},{6,5},{7,4},{8,11},{9,10},{10,... | collective-permute-start | bytes 196616 | tf_op jit(solution)/shard_map/ppermute | solution.py:170
  157.6 14.1 %collective-permute-start.28 = (bf16[256,128]{0,1:T(8,128)(2,1)S(1)}, bf16[256,128]{0,1:T(8,128)(2,1)S(1)}, u32[]{:S(2)}, u32[]{:S(2)}) collective-permute-start(bf16[256,128]{0,1:T(8,128)(2,1)S(1)} %add_convert_fusion.8), channel_id=1, source_target_pairs={{0,2},{1,3},{2,0},{3,1},{4,6},{5,7},{6,4},{7,5},{8,10},{9,11},{10,... | collective-permute-start | bytes 196616 | tf_op jit(solution)/shard_map/ppermute | solution.py:170
  167.8 3.9 %collective-permute-start.27 = (bf16[256,128]{0,1:T(8,128)(2,1)S(1)}, bf16[256,128]{0,1:T(8,128)(2,1)S(1)}, u32[]{:S(2)}, u32[]{:S(2)}) collective-permute-start(bf16[256,128]{0,1:T(8,128)(2,1)S(1)} %add_convert_fusion.8), channel_id=1, source_target_pairs={{0,1},{1,0},{2,3},{3,2},{4,5},{5,4},{6,7},{7,6},{8,9},{9,8},{10,11... | collective-permute-start | bytes 196616 | tf_op jit(solution)/shard_map/ppermute | solution.py:170
  168.1 5.8 %collective-permute-start.22 = (bf16[256,128]{0,1:T(8,128)(2,1)S(1)}, bf16[256,128]{0,1:T(8,128)(2,1)S(1)}, u32[]{:S(2)}, u32[]{:S(2)}) collective-permute-start(bf16[256,128]{0,1:T(8,128)(2,1)S(1)} %add_convert_fusion.10), channel_id=1, source_target_pairs={{0,3},{1,2},{2,1},{3,0},{4,7},{5,6},{6,5},{7,4},{8,11},{9,10},{10,... | collective-permute-start | bytes 196616 | tf_op jit(solution)/shard_map/ppermute | solution.py:170
  169.9 8.1 %collective-permute-start.21 = (bf16[256,128]{0,1:T(8,128)(2,1)S(1)}, bf16[256,128]{0,1:T(8,128)(2,1)S(1)}, u32[]{:S(2)}, u32[]{:S(2)}) collective-permute-start(bf16[256,128]{0,1:T(8,128)(2,1)S(1)} %add_convert_fusion.10), channel_id=1, source_target_pairs={{0,2},{1,3},{2,0},{3,1},{4,6},{5,7},{6,4},{7,5},{8,10},{9,11},{10,... | collective-permute-start | bytes 196616 | tf_op jit(solution)/shard_map/ppermute | solution.py:170
  170.6 7.4 %collective-permute-start.20 = (bf16[256,128]{0,1:T(8,128)(2,1)S(1)}, bf16[256,128]{0,1:T(8,128)(2,1)S(1)}, u32[]{:S(2)}, u32[]{:S(2)}) collective-permute-start(bf16[256,128]{0,1:T(8,128)(2,1)S(1)} %add_convert_fusion.10), channel_id=1, source_target_pairs={{0,1},{1,0},{2,3},{3,2},{4,5},{5,4},{6,7},{7,6},{8,9},{9,8},{10,11... | collective-permute-start | bytes 196616 | tf_op jit(solution)/shard_map/ppermute | solution.py:170
  (9 other events, 91.1 us)

commit v2 on v1

--- a/solution.py
+++ b/solution.py
@@ -68,16 +68,19 @@
     )(order, tile_stack)
 
 
-def spmm_kernel(n_pieces, rows_ref, cols_ref, same_ref, count_ref, *refs):
-    pieces = refs[:n_pieces]
-    tiles_ref, send_ref, keep_ref, m_vmem, t_vmem, o_vmem, total_ref, piece_sem, tile_sem, out_sem = refs[n_pieces:]
-    nodes = pieces[0].shape[0]
+def spmm_kernel(layout, rows_ref, cols_ref, same_ref, info_ref, *refs):
+    n_refs = sum(layout)
+    refs_left = list(refs[:n_refs])
+    pieces = [[refs_left.pop(0) for _ in range(n)] for n in layout]
+    tiles_ref, send_ref, keep_ref, m_vmem, t_vmem, o_vmem, total_ref, piece_sem, tile_sem, out_sem = refs[n_refs:]
+    nodes = pieces[0][0].shape[0]
     slots = t_vmem.shape[0]
     groups = slots // PREP_GROUP
     half = send_ref.shape[0]
     width = o_vmem.shape[1]
     piece_copies = [
-        pltpu.make_async_copy(piece, m_vmem.at[pl.ds(p * nodes, nodes)], piece_sem.at[p]) for p, piece in enumerate(pieces)
+        [pltpu.make_async_copy(ref, m_vmem.at[pl.ds(p * nodes, nodes)], piece_sem.at[p]) for ref in refs_p]
+        for p, refs_p in enumerate(pieces)
     ]
     tile_copies = [
         pltpu.make_async_copy(
@@ -85,8 +88,12 @@
         )
         for g in range(groups)
     ]
-    for copy in piece_copies:
-        copy.start()
+    for copies in piece_copies:
+        if len(copies) == 1:
+            copies[0].start()
+        else:
+            pl.when(info_ref[1] == 1)(copies[0].start)
+            pl.when(info_ref[1] != 1)(copies[1].start)
     for copy in tile_copies:
         copy.start()
 
@@ -95,9 +102,9 @@
         return carry
 
     lax.fori_loop(0, 2 * half // 1024, zero, 0)
-    for copy in piece_copies:
-        copy.wait()
-    count = count_ref[0]
+    for copies in piece_copies:
+        copies[0].wait()
+    count = info_ref[0]
 
     def add_slots(step, carry):
         prods = []
@@ -131,19 +138,19 @@
         copy.wait()
 
 
-def spmm(rows, cols, same, count, pieces, tiles, n_row):
-    nodes, width = pieces[0].shape
+def spmm(rows, cols, same, info, pieces, tiles, n_row):
+    nodes, width = pieces[0][0].shape
     slots = tiles.shape[0]
     groups = slots // PREP_GROUP
     half = n_row // 2 * nodes
     out = jax.ShapeDtypeStruct((half, width), jnp.bfloat16)
     return pl.pallas_call(
-        functools.partial(spmm_kernel, len(pieces)),
+        functools.partial(spmm_kernel, [len(p) for p in pieces]),
         out_shape=(out, out),
         grid_spec=pltpu.PrefetchScalarGridSpec(
             num_scalar_prefetch=4,
             grid=(),
-            in_specs=[pl.BlockSpec(memory_space=pl.ANY)] * (len(pieces) + 1),
+            in_specs=[pl.BlockSpec(memory_space=pl.ANY)] * (sum(len(p) for p in pieces) + 1),
             out_specs=[pl.BlockSpec(memory_space=pl.ANY)] * 2,
             scratch_shapes=[
                 pltpu.VMEM((len(pieces) * nodes, width), jnp.bfloat16),
@@ -162,7 +169,7 @@
             transcendentals=0,
         ),
         name="spmm",
-    )(rows, cols, same, count, *pieces, tiles)
+    )(rows, cols, same, info, *[ref for p in pieces for ref in p], tiles)
 
 
 def xor_permute(value, axis, mask):
@@ -176,29 +183,100 @@
     return values[0]
 
 
-def add_bf16(a, b):
-    return (a.astype(jnp.float32) + b.astype(jnp.float32)).astype(jnp.bfloat16)
-
-
-def reduce_scatter(keep, recv, bits, row):
-    for pos in bits:
-        axis = [b for b in sorted(bits, reverse=True) if b in reduce_scatter_left(bits, pos)].index(pos)
-        mine = (row >> pos) & 1
-
-        def pick(which, axis=axis):
-            return add_bf16(
-                lax.dynamic_index_in_dim(keep, which, axis, keepdims=False),
-                lax.dynamic_index_in_dim(recv, which, axis, keepdims=False),
-            )
-
-        sent = pick(1 - mine)
-        keep = pick(mine)
-        recv = xor_permute(sent, "row", 1 << pos)
-    return keep.astype(jnp.float32) + recv.astype(jnp.float32)
-
-
-def reduce_scatter_left(bits, pos):
-    return bits[bits.index(pos):]
+def gather_first(own):
+    return xor_permute(own, "col", 1), xor_permute(own, "col", 2)
+
+
+def gather_second(own, by_two, n_col):
+    ends, middles = [], []
+    for low in range(0, n_col, 4):
+        ends += [(low + 1, low), (low + 2, low + 3)]
+        middles += [(low + 1, low + 2), (low + 2, low + 1)]
+    return lax.ppermute(own, "col", middles), lax.ppermute(by_two, "col", ends)
+
+
+def as_pieces(own, first, second, mid, n_col):
+    if n_col == 4:
+        return [[own], [first[0]], [first[1]], list(second)]
+    pieces = [own, first[0], first[1], jnp.where(mid, second[0], second[1])]
+    for high in range(4, n_col, 4):
+        pieces += [xor_permute(piece, "col", high) for piece in pieces[:4]]
+    return [[piece] for piece in pieces]
+
+
+def fence(*values):
+    return lax.optimization_barrier(values)
+
+
+def add_f32(a, b):
+    return a.astype(jnp.float32) + b.astype(jnp.float32)
+
+
+def plan_slots(tile_rows, tile_cols, count, row, col, n_row, per_dev):
+    slots = tile_rows.shape[0]
+    half, quarter = n_row // 2, n_row // 4
+    row_pos = ((tile_rows // per_dev) ^ col) * per_dev + tile_rows % per_dev
+    away = (tile_cols // per_dev) ^ row
+    near, local = away >> 1, tile_cols % per_dev
+    upper = local // (per_dev // 2)
+    spot = local % (per_dev // 2)
+    first_bit = jnp.where(upper == 0, near & 1, near // quarter)
+    rest = jnp.where(upper == 0, near >> 1, near % quarter)
+    group = (1 - (away & 1)) * 4 + upper * 2 + (1 - first_bit)
+    col_pos = (group * quarter + rest) * (per_dev // 2) + spot
+    ids = jnp.arange(slots, dtype=jnp.int32)
+    col_pos = jnp.where(ids < count, col_pos, n_row * per_dev)
+    before = (col_pos[None, :] < col_pos[:, None]) | ((col_pos[None, :] == col_pos[:, None]) & (ids[None, :] < ids[:, None]))
+    rank = jnp.sum(before.astype(jnp.int32), axis=1)
+    hit = rank[None, :] == ids[:, None]
+
+    def permuted(values):
+        return jnp.sum(jnp.where(hit, values[None, :], 0), axis=1)
+
+    order = permuted(ids)
+    rows_sorted = permuted(row_pos)
+    cols_sorted = permuted(col_pos)
+    same = jnp.concatenate([jnp.zeros((1,), jnp.int32), (cols_sorted[1:] == cols_sorted[:-1]).astype(jnp.int32)])
+    return order, rows_sorted, cols_sorted, same
+
+
+def core_sums(keep, recv):
+    size = keep.shape[0] // 4
+    return [add_f32(keep[g * size : (g + 1) * size], recv[g * size : (g + 1) * size]).astype(jnp.bfloat16) for g in range(4)]
+
+
+def halve(value, upper, rows):
+    blocks = value.shape[0] // rows
+    shape = (2, blocks // 2) if upper else (blocks // 2, 2)
+    cut = value.reshape(shape + (rows, value.shape[1]))
+    if upper:
+        sent, kept = cut[1], cut[0]
+    else:
+        sent, kept = cut[:, 1], cut[:, 0]
+    return sent.reshape(-1, value.shape[1]), kept.reshape(-1, value.shape[1])
+
+
+def exchange_first(sums, bits):
+    return xor_permute(sums[0], "row", bits[0]), xor_permute(sums[2], "row", bits[-1])
+
+
+def exchange_rest(sums, recv, bits, rows):
+    done = []
+    for upper in (0, 1):
+        value = add_f32(sums[2 * upper + 1], recv[upper])
+        for bit in (bits[::-1] if upper else bits)[1:]:
+            sent, kept = halve(value.astype(jnp.bfloat16), upper, rows)
+            value = add_f32(kept, xor_permute(sent, "row", bit))
+        done.append(value.astype(jnp.bfloat16))
+    return jnp.concatenate(done, axis=0)
+
+
+def weight_term(features_groups, sums):
+    terms = [
+        lax.dot_general(f, s, (((0,), (0,)), ((), ())), preferred_element_type=jnp.float32)
+        for f, s in zip(features_groups, sums)
+    ]
+    return tree_sum(terms)
 
 
 def body(grad_out, preact, features, weight, tiles, tile_rows, tile_cols, live_counts):
@@ -206,63 +284,70 @@
     n_row, n_col = lax.axis_size("row"), lax.axis_size("col")
     row, col = lax.axis_index("row"), lax.axis_index("col")
     slots = tiles.shape[2]
-    per_dev = nodes // SIDE
-    n_chunks = 2
-    cw = width // n_chunks
-
-    pieces = []
-    for h in range(n_chunks):
-        cols_h = slice(h * cw, (h + 1) * cw)
-        masked = jnp.where(preact[:, cols_h] > 0, grad_out[:, cols_h], jnp.zeros_like(grad_out[:, cols_h]))
-        pieces.append([masked] + [xor_permute(masked, "col", k) for k in range(1, n_col)])
-
-    count = live_counts.reshape(1)
-    row_index = tile_rows.reshape(slots)
-    col_index = tile_cols.reshape(slots)
-    row_pos = ((row_index // per_dev) ^ col) * per_dev + row_index % per_dev
-    target = col_index // per_dev
-    own_core = 1 - ((target & 1) ^ (row & 1))
-    col_pos = (own_core * (n_row // 2) + target // 2) * per_dev + col_index % per_dev
-    ids = jnp.arange(slots, dtype=jnp.int32)
-    col_pos = jnp.where(ids < count, col_pos, n_row * per_dev)
-    before = (col_pos[None, :] < col_pos[:, None]) | ((col_pos[None, :] == col_pos[:, None]) & (ids[None, :] < ids[:, None]))
-    rank = jnp.sum(before.astype(jnp.int32), axis=1)
-    hit = rank[None, :] == ids[:, None]
-
-    def permuted(values):
-        return jnp.sum(jnp.where(hit, values[None, :], 0), axis=1)
-
-    order = permuted(ids)
-    rows_sorted = permuted(row_pos)
-    cols_sorted = permuted(col_pos)
-    same = jnp.concatenate([jnp.zeros((1,), jnp.int32), (cols_sorted[1:] == cols_sorted[:-1]).astype(jnp.int32)])
+    cw = width // 2
+    rows = nodes // 2
+    bits = [1 << b for b in range(1, n_row.bit_length() - 1)]
+    mid = ((col & 3) == 1) | ((col & 3) == 2)
+    count = live_counts.reshape(())
+    info = jnp.stack([count, mid.astype(jnp.int32)])
+
+    own0, own1 = [
+        jnp.where(preact[:, cut] > 0, grad_out[:, cut], jnp.zeros_like(grad_out[:, cut]))
+        for cut in (slice(0, cw), slice(cw, width))
+    ]
+    first0 = gather_first(own0)
+    near = [features]
+    for bit in bits[:2]:
+        near.append(xor_permute(features, "row", bit))
+    order, rows_sorted, cols_sorted, same = plan_slots(
+        tile_rows.reshape(slots), tile_cols.reshape(slots), count, row, col, n_row, nodes // SIDE
+    )
     tiles_sorted = prep(order, tiles.reshape(slots, SIDE, SIDE))
-
-    bits = list(range(1, n_row.bit_length() - 1))
-    summed, terms = [], []
-    for h in range(n_chunks):
-        send, keep = spmm(rows_sorted, cols_sorted, same, count, pieces[h], tiles_sorted, n_row)
-        recv = xor_permute(send, "row", 1)
-        lead = (2,) * len(bits)
-        keep = keep.reshape(lead + (nodes, cw))
-        recv = recv.reshape(lead + (nodes, cw))
-        first = reduce_scatter(keep[..., : nodes // 2, :], recv[..., : nodes // 2, :], bits, row)
-        second = reduce_scatter(keep[..., nodes // 2 :, :], recv[..., nodes // 2 :, :], bits[::-1], row)
-        colgrad = jnp.concatenate([first, second], axis=0).astype(jnp.bfloat16)
-        summed.append(colgrad)
-        term = lax.dot_general(features, colgrad, (((0,), (0,)), ((), ())), preferred_element_type=jnp.float32)
-        term = term.astype(jnp.bfloat16)
-        term = term.astype(jnp.float32) + xor_permute(term, "row", 1).astype(jnp.float32)
-        for axis, masks in (("row", range(2, n_row, 2)), ("col", range(1, n_col))):
-            term = term.astype(jnp.bfloat16)
-            parts = [term] + [xor_permute(term, axis, m) for m in masks]
-            term = tree_sum([p.astype(jnp.float32) for p in parts])
-        terms.append(term)
-    colgrad = jnp.concatenate(summed, axis=1)
+    own0, own1, first0, near, tiles_sorted = fence(own0, own1, first0, near, tiles_sorted)
+
+    second0 = gather_second(own0, first0[1], n_col)
+    pieces0 = as_pieces(own0, first0, second0, mid, n_col)
+    pieces0, own1, near = fence(pieces0, own1, near)
+
+    first1 = gather_first(own1)
+    near.append(xor_permute(near[1], "row", bits[1]))
+    for bit in bits[2:]:
+        near += [xor_permute(f, "row", bit) for f in near]
+    send0, keep0 = spmm(rows_sorted, cols_sorted, same, info, pieces0, tiles_sorted, n_row)
+    own1, first1, near, send0, keep0 = fence(own1, first1, near, send0, keep0)
+
+    second1 = gather_second(own1, first1[1], n_col)
+    pieces1 = as_pieces(own1, first1, second1, mid, n_col)
+    sums0 = core_sums(keep0, xor_permute(send0, "row", 1))
+    features_groups = []
+    for upper in (0, 1):
+        own_bit = (n_row // 4) if upper else 1
+        for want in (1, 0):
+            parts = [f[upper * rows : (upper + 1) * rows] for q, f in enumerate(near) if (q & own_bit != 0) == want]
+            features_groups.append(jnp.concatenate(parts, axis=0))
+    pieces1, sums0, features_groups = fence(pieces1, sums0, features_groups)
+
+    recv0 = exchange_first(sums0, bits)
+    send1, keep1 = spmm(rows_sorted, cols_sorted, same, info, pieces1, tiles_sorted, n_row)
+    sums0, recv0, send1, keep1 = fence(sums0, recv0, send1, keep1)
+
+    colgrad0 = exchange_rest(sums0, recv0, bits, rows)
+    term0 = weight_term(features_groups, sums0)
+    sums1 = core_sums(keep1, xor_permute(send1, "row", 1))
+    colgrad0, term0, sums1 = fence(colgrad0, term0, sums1)
+
+    recv1 = exchange_first(sums1, bits)
+    term1 = weight_term(features_groups, sums1)
+    term = jnp.concatenate([term0, term1], axis=1).astype(jnp.bfloat16)
+    for axis, masks in (("row", [1]), ("col", range(1, n_col)), ("row", range(2, n_row, 2))):
+        parts = [term] + [xor_permute(term, axis, m) for m in masks]
+        grad_weight = tree_sum([p.astype(jnp.float32) for p in parts])
+        term = grad_weight.astype(jnp.bfloat16)
+    colgrad1 = exchange_rest(sums1, recv1, bits, rows)
+    colgrad = jnp.concatenate([colgrad0, colgrad1], axis=1)
     grad_features = lax.dot_general(
         colgrad, weight, (((1,), (1,)), ((), ())), preferred_element_type=jnp.float32
     ).astype(jnp.bfloat16)
-    grad_weight = jnp.concatenate(terms, axis=1)
     return (grad_features, grad_weight)
 
 

time: 181 us -> 158 us (0.87)
  waiting for transfers between devices: 72.4 us -> 51 us
  starting transfers between devices: 52.9 us -> 38.2 us
  other arithmetic: 5.7 us -> 12.4 us
  matrix products: 2.24 us -> 7.5 us
  Pallas kernels: 38 us -> 40.6 us
  local copies, waits for them, and re-layouts: 6.07 us -> 4.02 us
    ppermute x30 -> x24, waiting for transfers between devices: 72.4 us -> 30.7 us  [xor_permute(): return lax.ppermute(value, axis, [(i, i ^ mask) for i in range(size)])]
    ppermute x0 -> x4, waiting for transfers between devices: none -> 20.3 us  [the longest x2 20.3 us: gather_second(): lax.ppermute(by_two, 'col', ends)]
    ppermute x30 -> x24, starting transfers between devices: 52.9 us -> 33.5 us  [xor_permute(): return lax.ppermute(value, axis, [(i, i ^ mask) for i in range(size)])]
    dot_general x2 -> x8, matrix products: 0.78 us -> 6.06 us  [weight_term(): lax.dot_general(f, s, (((0,), (0,)), ((), ())), preferred_element_type=jn...]
    ppermute x0 -> x4, starting transfers between devices: none -> 4.74 us  [the longest x2 2.57 us: gather_second(): lax.ppermute(by_two, 'col', ends)]
    convert_element_type x12, other arithmetic: 1.51 us -> 5.34 us  [the longest x4 2.9 us: exchange_rest(): sent, kept = halve(value.astype(jnp.bfloat16), upper, rows)]
    pallas_call x2, Pallas kernels: 25 us -> 27.6 us  [spmm(): pl.pallas_call(functools.partial(spmm_kernel, [len(p) for p in pieces]),...]
    slice x4 -> x6, local copies, waits for them, and re-layouts: 3.81 us -> 1.52 us  [the longest x4 1.48 us: body(): f[upper * rows:(upper + 1) * rows]]
  transfers between devices with their start and end apart: 30 -> 28, of which waited for: 10 -> 10; matrix products, arithmetic and copies ran while one was open for 6% -> 11% of each run, Pallas kernels for 21% -> 26%
where the time goes in v2:
time: 158 us; the launch traced here: 155 us
  waiting for transfers between devices  51 us (32%)
  Pallas kernels  40.6 us (26%)
  starting transfers between devices  38.2 us (24%)
  other arithmetic  12.4 us (8%)
  matrix products  7.5 us (5%)
  local copies, waits for them, and re-layouts  4.02 us (3%)
  between operations  1.73 us (1%)
    ppermute x24, starting transfers between devices, xor_permute(): return lax.ppermute(value, axis, [(i, i ^ mask) for i in range(size)])  33.5 us
    ppermute x24, waiting for transfers between devices, xor_permute(): return lax.ppermute(value, axis, [(i, i ^ mask) for i in range(size)])  30.7 us
    pallas_call x2, Pallas kernels, spmm(): pl.pallas_call(functools.partial(spmm_kernel, [len(p) for p in pieces]),...  27.6 us
    ppermute x2, waiting for transfers between devices, gather_second(): lax.ppermute(by_two, 'col', ends)  20.3 us
    pallas_call x1, Pallas kernels, prep(): pl.pallas_call(prep_kernel, out_shape=jax.ShapeDtypeStruct(tile_stack.sha...  13 us
    dot_general x8, matrix products, weight_term(): lax.dot_general(f, s, (((0,), (0,)), ((), ())), preferred_element_type=jn...  6.06 us
  transfers between devices with their start and end apart: 28, of which 10 were waited for; matrix products, arithmetic and copies ran while one was open for 11% of the time, Pallas kernels for 26%

profile of v2, /device:TPU:1, one launch (start us, length us, event | category | flops | bytes accessed | tf_op | source)
XLA Modules:
  0.0 155.4 jit_solution(4530486567376991263)
XLA Ops:
  0.7 2.1 %collective-permute-start.2 = (bf16[2048,256]{1,0:T(8,128)(2,1)}, bf16[2048,256]{1,0:T(8,128)(2,1)S(1)}, u32[]{:S(2)}, u32[]{:S(2)}) collective-permute-start(bf16[2048,256]{1,0:T(8,128)(2,1)} %param.10), channel_id=1, source_target_pairs={{0,8},{4,12},{8,0},{12,4},{16,24},{20,28},{24,16},{28,20},{1,9},{5... | collective-permute-start | bytes 3145736 | tf_op jit(solution)/shard_map/ppermute | solution.py:177
  4.0 2.4 %compare_select_fusion = (bf16[2048,128]{1,0:T(8,128)(2,1)}, bf16[2048,128]{1,0:T(8,128)(2,1)S(1)}) fusion(bf16[2048,256]{1,0:T(8,128)(2,1)} %param.8, bf16[2048,256]{1,0:T(8,128)(2,1)} %param.9), kind=kLoop, calls=%fused_computation.29 | loop fusion | flops 1048576 | bytes 3145728 | tf_op jit(solution)/shard_map/jit(_where)/select_n | solution.py:295
  6.5 1.3 collective-permute-start
  7.8 2.3 %collective-permute-start.1 = (bf16[2048,128]{1,0:T(8,128)(2,1)S(1)}, bf16[2048,128]{1,0:T(8,128)(2,1)}, u32[]{:S(2)}, u32[]{:S(2)}) collective-permute-start(bf16[2048,128]{1,0:T(8,128)(2,1)S(1)} %get-tuple-element.70.refs_0_), channel_id=1, source_target_pairs={{0,2},{1,3},{2,0},{3,1},{4,6},{5,7},{6,4},{7,5},{8,10},{9,11},{10,... | collective-permute-start | bytes 1572872 | tf_op jit(solution)/shard_map/ppermute | solution.py:177
  12.0 13.0 %sort_tiles.1.refs_5_ = bf16[320,128,128]{2,1,0:T(8,128)(2,1)} custom-call(s32[320]{0:T(512)} %get-tuple-element.118.order_ref, bf16[320,128,128]{2,1,0:T(8,128)(2,1)} %bitcast.39), custom_call_target="tpu_custom_call" | custom-call | bytes 20971520 | tf_op jit(solution)/shard_map/sort_tiles/pallas_call | solution.py:50
  25.0 4.9 %collective-permute-done.refs_1_ = bf16[2048,128]{1,0:T(8,128)(2,1)S(1)} collective-permute-done((bf16[2048,128]{1,0:T(8,128)(2,1)S(1)}, bf16[2048,128]{1,0:T(8,128)(2,1)S(1)}, u32[]{:S(2)}, u32[]{:S(2)}) %collective-permute-start) | collective-permute-done | bytes 524320 | tf_op jit(solution)/shard_map/ppermute | solution.py:177
  30.6 1.3 collective-permute-start.5
  32.7 12.4 %collective-permute-done.5.refs_4_ = bf16[2048,128]{1,0:T(8,128)(2,1)S(1)} collective-permute-done((bf16[2048,128]{1,0:T(8,128)(2,1)}, bf16[2048,128]{1,0:T(8,128)(2,1)S(1)}, u32[]{:S(2)}, u32[]{:S(2)}) %collective-permute-start.5) | collective-permute-done | bytes 524320 | tf_op jit(solution)/shard_map/ppermute | solution.py:195
  47.3 1.4 collective-permute-start.7
  50.0 13.7 %spmm.2 = (bf16[8192,128]{1,0:T(8,128)(2,1)}, bf16[8192,128]{1,0:T(8,128)(2,1)}) custom-call(s32[320]{0:T(512)} %get-tuple-element.117.rows_ref, s32[320]{0:T(512)} %copy-done.11, s32[320]{0:T(512)} %add_convert_fusion.16.same_ref, s32[2]{0:T(128)} %pad_add_fusion.info_ref, bf16[2048,128]{1,0:T(8,128)(2,1)} %copy-done.5, bf16[2048,128]{1,0:T(8,128)(2,1)} %copy-done.8, ...), custom_call_target="tpu_custom_call" | custom-call | flops 1342177280 | bytes 16777216 | tf_op jit(solution)/shard_map/spmm/pallas_call | solution.py:147
  63.7 4.5 %collective-permute-done.6.refs_1_ = bf16[2048,128]{1,0:T(8,128)(2,1)S(1)} collective-permute-done((bf16[2048,128]{1,0:T(8,128)(2,1)}, bf16[2048,128]{1,0:T(8,128)(2,1)S(1)}, u32[]{:S(2)}, u32[]{:S(2)}) %collective-permute-start.6) | collective-permute-done | bytes 524320 | tf_op jit(solution)/shard_map/ppermute | solution.py:177
  68.3 5.8 %collective-permute-start.11 = (bf16[8192,128]{1,0:T(8,128)(2,1)}, bf16[8192,128]{1,0:T(8,128)(2,1)S(1)}, u32[]{:S(2)}, u32[]{:S(2)}) collective-permute-start(bf16[8192,128]{1,0:T(8,128)(2,1)} %get-tuple-element.82), channel_id=1, source_target_pairs={{0,4},{4,0},{8,12},{12,8},{16,20},{20,16},{24,28},{28,24},{1,5},{5... | collective-permute-start | bytes 6291464 | tf_op jit(solution)/shard_map/ppermute | solution.py:177
  74.1 1.3 collective-permute-start.10
  75.4 1.5 collective-permute-start.9
  77.2 1.3 fusion.34
  80.5 1.5 add_convert_fusion.8
  82.0 7.8 %collective-permute-done.10.refs_4_ = bf16[2048,128]{1,0:T(8,128)(2,1)} collective-permute-done((bf16[2048,128]{1,0:T(8,128)(2,1)}, bf16[2048,128]{1,0:T(8,128)(2,1)}, u32[]{:S(2)}, u32[]{:S(2)}) %collective-permute-start.10) | collective-permute-done | bytes 524320 | tf_op jit(solution)/shard_map/ppermute | solution.py:195
  91.4 13.9 %spmm.3 = (bf16[8192,128]{1,0:T(8,128)(2,1)}, bf16[8192,128]{1,0:T(8,128)(2,1)}) custom-call(s32[320]{0:T(512)} %get-tuple-element.117.rows_ref, s32[320]{0:T(512)} %copy-done.11, s32[320]{0:T(512)} %add_convert_fusion.16.same_ref, s32[2]{0:T(128)} %pad_add_fusion.info_ref, bf16[2048,128]{1,0:T(8,128)(2,1)} %get-tuple-element.91.refs_0_, ...), custom_call_target="tpu_custom_call" | custom-call | flops 1342177280 | bytes 16777216 | tf_op jit(solution)/shard_map/spmm/pallas_call | solution.py:147
  105.3 1.4 add_convert_fusion.7
  108.7 3.3 %collective-permute-start.15 = (bf16[1024,128]{1,0:T(8,128)(2,1)S(1)}, bf16[1024,128]{1,0:T(8,128)(2,1)S(1)}, u32[]{:S(2)}, u32[]{:S(2)}) collective-permute-start(bf16[1024,128]{1,0:T(8,128)(2,1)S(1)} %slice.163), channel_id=1, source_target_pairs={{0,8},{4,12},{8,0},{12,4},{16,24},{20,28},{24,16},{28,20},{1,9},{5... | collective-permute-start | bytes 786440 | tf_op jit(solution)/shard_map/ppermute | solution.py:177
  113.0 1.5 convolution_add_fusion.2
  114.5 1.7 %fusion.1 = bf16[256,128]{1,0:T(8,128)(2,1)S(1)} fusion(f32[256,128]{1,0:T(8,128)S(1)} %convolution_add_fusion.2, f32[256,128]{1,0:T(8,128)S(1)} %fusion.35, bf16[2048,256]{1,0:T(8,128)(2,1)S(1)} %pad_maximum_fusion, bf16[2048,128]{1,0:T(8,128)(2,1)} %get-tuple-element.103), kind=kOutput, calls=%fused_computation.6 | convolution fusion | flops 134316032 | bytes 1900544 | tf_op jit(solution)/shard_map/dot_general | solution.py:276
  116.3 2.1 %collective-permute-done.15 = bf16[1024,128]{1,0:T(8,128)(2,1)S(1)} collective-permute-done((bf16[1024,128]{1,0:T(8,128)(2,1)S(1)}, bf16[1024,128]{1,0:T(8,128)(2,1)S(1)}, u32[]{:S(2)}, u32[]{:S(2)}) %collective-permute-start.15) | collective-permute-done | bytes 262176 | tf_op jit(solution)/shard_map/ppermute | solution.py:177
  122.0 1.5 collective-permute-start.17
  123.5 2.5 %collective-permute-start.22 = (bf16[256,256]{1,0:T(8,128)(2,1)S(1)}, bf16[256,256]{1,0:T(8,128)(2,1)S(1)}, u32[]{:S(2)}, u32[]{:S(2)}) collective-permute-start(bf16[256,256]{1,0:T(8,128)(2,1)S(1)} %add_convert_fusion.15), channel_id=1, source_target_pairs={{0,1},{1,0},{2,3},{3,2},{4,5},{5,4},{6,7},{7,6},{8,9},{9,8},{10,11... | collective-permute-start | bytes 393224 | tf_op jit(solution)/shard_map/ppermute | solution.py:177
  126.0 2.9 %collective-permute-start.23 = (bf16[256,256]{1,0:T(8,128)(2,1)S(1)}, bf16[256,256]{1,0:T(8,128)(2,1)S(1)}, u32[]{:S(2)}, u32[]{:S(2)}) collective-permute-start(bf16[256,256]{1,0:T(8,128)(2,1)S(1)} %add_convert_fusion.15), channel_id=1, source_target_pairs={{0,2},{1,3},{2,0},{3,1},{4,6},{5,7},{6,4},{7,5},{8,10},{9,11},{10,... | collective-permute-start | bytes 393224 | tf_op jit(solution)/shard_map/ppermute | solution.py:177
  130.1 2.4 %collective-permute-done.23 = bf16[256,256]{1,0:T(8,128)(2,1)S(1)} collective-permute-done((bf16[256,256]{1,0:T(8,128)(2,1)S(1)}, bf16[256,256]{1,0:T(8,128)(2,1)S(1)}, u32[]{:S(2)}, u32[]{:S(2)}) %collective-permute-start.23) | collective-permute-done | bytes 131104 | tf_op jit(solution)/shard_map/ppermute | solution.py:177
  132.5 6.4 %collective-permute-done.24 = bf16[256,256]{1,0:T(8,128)(2,1)S(1)} collective-permute-done((bf16[256,256]{1,0:T(8,128)(2,1)S(1)}, bf16[256,256]{1,0:T(8,128)(2,1)S(1)}, u32[]{:S(2)}, u32[]{:S(2)}) %collective-permute-start.24) | collective-permute-done | bytes 131104 | tf_op jit(solution)/shard_map/ppermute | solution.py:177
  139.7 2.1 %collective-permute-start.27 = (bf16[256,256]{1,0:T(8,128)(2,1)S(1)}, bf16[256,256]{1,0:T(8,128)(2,1)S(1)}, u32[]{:S(2)}, u32[]{:S(2)}) collective-permute-start(bf16[256,256]{1,0:T(8,128)(2,1)S(1)} %add_convert_fusion.14), channel_id=1, source_target_pairs={{0,24},{4,28},{8,16},{12,20},{16,8},{20,12},{24,0},{28,4},{1,25},{... | collective-permute-start | bytes 393224 | tf_op jit(solution)/shard_map/ppermute | solution.py:177
  143.3 3.5 %collective-permute-done.26 = bf16[256,256]{1,0:T(8,128)(2,1)S(1)} collective-permute-done((bf16[256,256]{1,0:T(8,128)(2,1)S(1)}, bf16[256,256]{1,0:T(8,128)(2,1)S(1)}, u32[]{:S(2)}, u32[]{:S(2)}) %collective-permute-start.26) | collective-permute-done | bytes 131104 | tf_op jit(solution)/shard_map/ppermute | solution.py:177
  147.6 6.2 %collective-permute-done.18 = bf16[1024,128]{1,0:T(8,128)(2,1)S(1)} collective-permute-done((bf16[1024,128]{1,0:T(8,128)(2,1)S(1)}, bf16[1024,128]{1,0:T(8,128)(2,1)S(1)}, u32[]{:S(2)}, u32[]{:S(2)}) %collective-permute-start.18) | collective-permute-done | bytes 262176 | tf_op jit(solution)/shard_map/ppermute | solution.py:177
  154.0 1.4 convolution_convert_fusion
  (100 shorter events, 22.1 us)
Async XLA Ops:
  0.6 153.3 %copy-start = (bf16[256,256]{1,0:T(8,128)(2,1)S(1)}, bf16[256,256]{1,0:T(8,128)(2,1)}, u32[]{:S(2)}) copy-start(bf16[256,256]{1,0:T(8,128)(2,1)} %param.11) | copy-start | bytes 393220
  0.7 29.2 %collective-permute-start.2 = (bf16[2048,256]{1,0:T(8,128)(2,1)}, bf16[2048,256]{1,0:T(8,128)(2,1)S(1)}, u32[]{:S(2)}, u32[]{:S(2)}) collective-permute-start(bf16[2048,256]{1,0:T(8,128)(2,1)} %param.10), channel_id=1, source_target_pairs={{0,8},{4,12},{8,0},{12,4},{16,24},{20,28},{24,16},{28,20},{1,9},{5... | collective-permute-start | bytes 3145736 | tf_op jit(solution)/shard_map/ppermute | solution.py:177
  2.8 27.1 %collective-permute-start.3 = (bf16[2048,256]{1,0:T(8,128)(2,1)}, bf16[2048,256]{1,0:T(8,128)(2,1)S(1)}, u32[]{:S(2)}, u32[]{:S(2)}) collective-permute-start(bf16[2048,256]{1,0:T(8,128)(2,1)} %param.10), channel_id=1, source_target_pairs={{0,16},{4,20},{8,24},{12,28},{16,0},{20,4},{24,8},{28,12},{1,17},{... | collective-permute-start | bytes 3145736 | tf_op jit(solution)/shard_map/ppermute | solution.py:177
  6.5 23.4 %copy-start.5 = (bf16[2048,128]{1,0:T(8,128)(2,1)}, bf16[2048,128]{1,0:T(8,128)(2,1)S(1)}, u32[]{:S(2)}) copy-start(bf16[2048,128]{1,0:T(8,128)(2,1)S(1)} %get-tuple-element.70.refs_0_) | copy-start | bytes 1572868
  6.5 23.4 %collective-permute-start = (bf16[2048,128]{1,0:T(8,128)(2,1)S(1)}, bf16[2048,128]{1,0:T(8,128)(2,1)S(1)}, u32[]{:S(2)}, u32[]{:S(2)}) collective-permute-start(bf16[2048,128]{1,0:T(8,128)(2,1)S(1)} %get-tuple-element.70.refs_0_), channel_id=1, source_target_pairs={{0,1},{1,0},{2,3},{3,2},{4,5},{5,4},{6,7},{7,6},{8,9},{9,8},{10,11... | collective-permute-start | bytes 1572872 | tf_op jit(solution)/shard_map/ppermute | solution.py:177
  7.8 22.1 %collective-permute-start.1 = (bf16[2048,128]{1,0:T(8,128)(2,1)S(1)}, bf16[2048,128]{1,0:T(8,128)(2,1)}, u32[]{:S(2)}, u32[]{:S(2)}) collective-permute-start(bf16[2048,128]{1,0:T(8,128)(2,1)S(1)} %get-tuple-element.70.refs_0_), channel_id=1, source_target_pairs={{0,2},{1,3},{2,0},{3,1},{4,6},{5,7},{6,4},{7,5},{8,10},{9,11},{10,... | collective-permute-start | bytes 1572872 | tf_op jit(solution)/shard_map/ppermute | solution.py:177
  12.0 37.3 %copy-start.11 = (s32[320]{0:T(512)}, s32[320]{0:T(512)S(1)}, u32[]{:S(2)}) copy-start(s32[320]{0:T(512)S(1)} %get-tuple-element.116.cols_ref) | copy-start | bytes 3844
  29.9 2.0 %collective-permute-start.4 = (bf16[2048,128]{1,0:T(8,128)(2,1)S(1)}, bf16[2048,128]{1,0:T(8,128)(2,1)S(1)}, u32[]{:S(2)}, u32[]{:S(2)}) collective-permute-start(bf16[2048,128]{1,0:T(8,128)(2,1)S(1)} %get-tuple-element.70.refs_0_), channel_id=1, source_target_pairs={{1,2},{2,1},{5,6},{6,5},{9,10},{10,9},{13,14},{14,13},{17,18},{18,... | collective-permute-start | bytes 1572872 | tf_op jit(solution)/shard_map/ppermute | solution.py:195
  30.6 14.5 %collective-permute-start.5 = (bf16[2048,128]{1,0:T(8,128)(2,1)}, bf16[2048,128]{1,0:T(8,128)(2,1)S(1)}, u32[]{:S(2)}, u32[]{:S(2)}) collective-permute-start(bf16[2048,128]{1,0:T(8,128)(2,1)} %collective-permute-done.1.refs_2_), channel_id=1, source_target_pairs={{1,0},{2,3},{5,4},{6,7},{9,8},{10,11},{13,12},{14,15},{17,16},{18,... | collective-permute-start | bytes 1572872 | tf_op jit(solution)/shard_map/ppermute | solution.py:195
  45.9 22.3 %collective-permute-start.8 = (bf16[2048,256]{1,0:T(8,128)(2,1)S(1)}, bf16[2048,256]{1,0:T(8,128)(2,1)}, u32[]{:S(2)}, u32[]{:S(2)}) collective-permute-start(bf16[2048,256]{1,0:T(8,128)(2,1)S(1)} %collective-permute-done.2), channel_id=1, source_target_pairs={{0,16},{4,20},{8,24},{12,28},{16,0},{20,4},{24,8},{28,12},{1,17},{... | collective-permute-start | bytes 3145736 | tf_op jit(solution)/shard_map/ppermute | solution.py:177
  46.1 22.1 %collective-permute-start.6 = (bf16[2048,128]{1,0:T(8,128)(2,1)}, bf16[2048,128]{1,0:T(8,128)(2,1)S(1)}, u32[]{:S(2)}, u32[]{:S(2)}) collective-permute-start(bf16[2048,128]{1,0:T(8,128)(2,1)} %get-tuple-element.91.refs_0_), channel_id=1, source_target_pairs={{0,1},{1,0},{2,3},{3,2},{4,5},{5,4},{6,7},{7,6},{8,9},{9,8},{10,11... | collective-permute-start | bytes 1572872 | tf_op jit(solution)/shard_map/ppermute | solution.py:177
  47.3 21.0 %collective-permute-start.7 = (bf16[2048,128]{1,0:T(8,128)(2,1)}, bf16[2048,128]{1,0:T(8,128)(2,1)}, u32[]{:S(2)}, u32[]{:S(2)}) collective-permute-start(bf16[2048,128]{1,0:T(8,128)(2,1)} %get-tuple-element.91.refs_0_), channel_id=1, source_target_pairs={{0,2},{1,3},{2,0},{3,1},{4,6},{5,7},{6,4},{7,5},{8,10},{9,11},{10,... | collective-permute-start | bytes 1572872 | tf_op jit(solution)/shard_map/ppermute | solution.py:177
  50.0 26.9 %copy-start.6 = (bf16[2048,256]{1,0:T(8,128)(2,1)S(1)}, bf16[2048,256]{1,0:T(8,128)(2,1)}, u32[]{:S(2)}) copy-start(bf16[2048,256]{1,0:T(8,128)(2,1)} %param.10) | copy-start | bytes 3145732
  68.3 11.4 %collective-permute-start.11 = (bf16[8192,128]{1,0:T(8,128)(2,1)}, bf16[8192,128]{1,0:T(8,128)(2,1)S(1)}, u32[]{:S(2)}, u32[]{:S(2)}) collective-permute-start(bf16[8192,128]{1,0:T(8,128)(2,1)} %get-tuple-element.82), channel_id=1, source_target_pairs={{0,4},{4,0},{8,12},{12,8},{16,20},{20,16},{24,28},{28,24},{1,5},{5... | collective-permute-start | bytes 6291464 | tf_op jit(solution)/shard_map/ppermute | solution.py:177
  74.1 15.8 %collective-permute-start.10 = (bf16[2048,128]{1,0:T(8,128)(2,1)}, bf16[2048,128]{1,0:T(8,128)(2,1)}, u32[]{:S(2)}, u32[]{:S(2)}) collective-permute-start(bf16[2048,128]{1,0:T(8,128)(2,1)} %collective-permute-done.7.refs_2_), channel_id=1, source_target_pairs={{1,0},{2,3},{5,4},{6,7},{9,8},{10,11},{13,12},{14,15},{17,16},{18,... | collective-permute-start | bytes 1572872 | tf_op jit(solution)/shard_map/ppermute | solution.py:195
  75.4 14.5 %collective-permute-start.9 = (bf16[2048,128]{1,0:T(8,128)(2,1)}, bf16[2048,128]{1,0:T(8,128)(2,1)}, u32[]{:S(2)}, u32[]{:S(2)}) collective-permute-start(bf16[2048,128]{1,0:T(8,128)(2,1)} %get-tuple-element.91.refs_0_), channel_id=1, source_target_pairs={{1,2},{2,1},{5,6},{6,5},{9,10},{10,9},{13,14},{14,13},{17,18},{18,... | collective-permute-start | bytes 1572872 | tf_op jit(solution)/shard_map/ppermute | solution.py:195
  89.9 15.4 %collective-permute-start.12 = (bf16[2048,128]{1,0:T(8,128)(2,1)}, bf16[2048,128]{1,0:T(8,128)(2,1)}, u32[]{:S(2)}, u32[]{:S(2)}) collective-permute-start(bf16[2048,128]{1,0:T(8,128)(2,1)} %get-tuple-element.103), channel_id=1, source_target_pairs={{0,8},{4,12},{8,0},{12,4},{16,24},{20,28},{24,16},{28,20},{1,9},{5... | collective-permute-start | bytes 1572872 | tf_op jit(solution)/shard_map/ppermute | solution.py:177
  90.1 15.1 %collective-permute-start.13 = (bf16[2048,128]{1,0:T(8,128)(2,1)}, bf16[2048,128]{1,0:T(8,128)(2,1)}, u32[]{:S(2)}, u32[]{:S(2)}) collective-permute-start(bf16[2048,128]{1,0:T(8,128)(2,1)} %get-tuple-element.106), channel_id=1, source_target_pairs={{0,16},{4,20},{8,24},{12,28},{16,0},{20,4},{24,8},{28,12},{1,17},{... | collective-permute-start | bytes 1572872 | tf_op jit(solution)/shard_map/ppermute | solution.py:177
  105.3 13.3 %collective-permute-start.16 = (bf16[8192,128]{1,0:T(8,128)(2,1)}, bf16[8192,128]{1,0:T(8,128)(2,1)S(1)}, u32[]{:S(2)}, u32[]{:S(2)}) collective-permute-start(bf16[8192,128]{1,0:T(8,128)(2,1)} %get-tuple-element.109), channel_id=1, source_target_pairs={{0,4},{4,0},{8,12},{12,8},{16,20},{20,16},{24,28},{28,24},{1,5},{5... | collective-permute-start | bytes 6291464 | tf_op jit(solution)/shard_map/ppermute | solution.py:177
  106.8 9.4 %collective-permute-start.14 = (bf16[1024,128]{1,0:T(8,128)(2,1)S(1)}, bf16[1024,128]{1,0:T(8,128)(2,1)S(1)}, u32[]{:S(2)}, u32[]{:S(2)}) collective-permute-start(bf16[1024,128]{1,0:T(8,128)(2,1)S(1)} %slice_bitcast_fusion.2), channel_id=1, source_target_pairs={{0,16},{4,20},{8,24},{12,28},{16,0},{20,4},{24,8},{28,12},{1,17},{... | collective-permute-start | bytes 786440 | tf_op jit(solution)/shard_map/ppermute | solution.py:177
  108.7 9.7 %collective-permute-start.15 = (bf16[1024,128]{1,0:T(8,128)(2,1)S(1)}, bf16[1024,128]{1,0:T(8,128)(2,1)S(1)}, u32[]{:S(2)}, u32[]{:S(2)}) collective-permute-start(bf16[1024,128]{1,0:T(8,128)(2,1)S(1)} %slice.163), channel_id=1, source_target_pairs={{0,8},{4,12},{8,0},{12,4},{16,24},{20,28},{24,16},{28,20},{1,9},{5... | collective-permute-start | bytes 786440 | tf_op jit(solution)/shard_map/ppermute | solution.py:177
  121.0 2.5 %collective-permute-start.21 = (bf16[256,256]{1,0:T(8,128)(2,1)S(1)}, bf16[256,256]{1,0:T(8,128)(2,1)S(1)}, u32[]{:S(2)}, u32[]{:S(2)}) collective-permute-start(bf16[256,256]{1,0:T(8,128)(2,1)S(1)} %pad_maximum_fusion.5), channel_id=1, source_target_pairs={{0,4},{4,0},{8,12},{12,8},{16,20},{20,16},{24,28},{28,24},{1,5},{5... | collective-permute-start | bytes 393224 | tf_op jit(solution)/shard_map/ppermute | solution.py:177
  122.0 19.7 %collective-permute-start.17 = (bf16[2048,128]{1,0:T(8,128)(2,1)S(1)}, bf16[2048,128]{1,0:T(8,128)(2,1)S(1)}, u32[]{:S(2)}, u32[]{:S(2)}) collective-permute-start(bf16[2048,128]{1,0:T(8,128)(2,1)S(1)} %get-tuple-element.112), channel_id=1, source_target_pairs={{0,8},{4,12},{8,0},{12,4},{16,24},{20,28},{24,16},{28,20},{1,9},{5... | collective-permute-start | bytes 1572872 | tf_op jit(solution)/shard_map/ppermute | solution.py:177
  123.5 6.5 %collective-permute-start.22 = (bf16[256,256]{1,0:T(8,128)(2,1)S(1)}, bf16[256,256]{1,0:T(8,128)(2,1)S(1)}, u32[]{:S(2)}, u32[]{:S(2)}) collective-permute-start(bf16[256,256]{1,0:T(8,128)(2,1)S(1)} %add_convert_fusion.15), channel_id=1, source_target_pairs={{0,1},{1,0},{2,3},{3,2},{4,5},{5,4},{6,7},{7,6},{8,9},{9,8},{10,11... | collective-permute-start | bytes 393224 | tf_op jit(solution)/shard_map/ppermute | solution.py:177
  126.0 6.5 %collective-permute-start.23 = (bf16[256,256]{1,0:T(8,128)(2,1)S(1)}, bf16[256,256]{1,0:T(8,128)(2,1)S(1)}, u32[]{:S(2)}, u32[]{:S(2)}) collective-permute-start(bf16[256,256]{1,0:T(8,128)(2,1)S(1)} %add_convert_fusion.15), channel_id=1, source_target_pairs={{0,2},{1,3},{2,0},{3,1},{4,6},{5,7},{6,4},{7,5},{8,10},{9,11},{10,... | collective-permute-start | bytes 393224 | tf_op jit(solution)/shard_map/ppermute | solution.py:177
  129.0 10.0 %collective-permute-start.24 = (bf16[256,256]{1,0:T(8,128)(2,1)S(1)}, bf16[256,256]{1,0:T(8,128)(2,1)S(1)}, u32[]{:S(2)}, u32[]{:S(2)}) collective-permute-start(bf16[256,256]{1,0:T(8,128)(2,1)S(1)} %add_convert_fusion.15), channel_id=1, source_target_pairs={{0,3},{1,2},{2,1},{3,0},{4,7},{5,6},{6,5},{7,4},{8,11},{9,10},{10,... | collective-permute-start | bytes 393224 | tf_op jit(solution)/shard_map/ppermute | solution.py:177
  130.1 12.5 %collective-permute-start.19 = (bf16[2048,128]{1,0:T(8,128)(2,1)S(1)}, bf16[2048,128]{1,0:T(8,128)(2,1)S(1)}, u32[]{:S(2)}, u32[]{:S(2)}) collective-permute-start(bf16[2048,128]{1,0:T(8,128)(2,1)S(1)} %get-tuple-element.114), channel_id=1, source_target_pairs={{0,16},{4,20},{8,24},{12,28},{16,0},{20,4},{24,8},{28,12},{1,17},{... | collective-permute-start | bytes 1572872 | tf_op jit(solution)/shard_map/ppermute | solution.py:177
  139.1 4.3 %collective-permute-start.25 = (bf16[256,256]{1,0:T(8,128)(2,1)S(1)}, bf16[256,256]{1,0:T(8,128)(2,1)S(1)}, u32[]{:S(2)}, u32[]{:S(2)}) collective-permute-start(bf16[256,256]{1,0:T(8,128)(2,1)S(1)} %add_convert_fusion.14), channel_id=1, source_target_pairs={{0,8},{4,12},{8,0},{12,4},{16,24},{20,28},{24,16},{28,20},{1,9},{5... | collective-permute-start | bytes 393224 | tf_op jit(solution)/shard_map/ppermute | solution.py:177
  139.6 7.2 %collective-permute-start.26 = (bf16[256,256]{1,0:T(8,128)(2,1)S(1)}, bf16[256,256]{1,0:T(8,128)(2,1)S(1)}, u32[]{:S(2)}, u32[]{:S(2)}) collective-permute-start(bf16[256,256]{1,0:T(8,128)(2,1)S(1)} %add_convert_fusion.14), channel_id=1, source_target_pairs={{0,16},{4,20},{8,24},{12,28},{16,0},{20,4},{24,8},{28,12},{1,17},{... | collective-permute-start | bytes 393224 | tf_op jit(solution)/shard_map/ppermute | solution.py:177
  139.7 7.1 %collective-permute-start.27 = (bf16[256,256]{1,0:T(8,128)(2,1)S(1)}, bf16[256,256]{1,0:T(8,128)(2,1)S(1)}, u32[]{:S(2)}, u32[]{:S(2)}) collective-permute-start(bf16[256,256]{1,0:T(8,128)(2,1)S(1)} %add_convert_fusion.14), channel_id=1, source_target_pairs={{0,24},{4,28},{8,16},{12,20},{16,8},{20,12},{24,0},{28,4},{1,25},{... | collective-permute-start | bytes 393224 | tf_op jit(solution)/shard_map/ppermute | solution.py:177
  141.9 11.9 %collective-permute-start.18 = (bf16[1024,128]{1,0:T(8,128)(2,1)S(1)}, bf16[1024,128]{1,0:T(8,128)(2,1)S(1)}, u32[]{:S(2)}, u32[]{:S(2)}) collective-permute-start(bf16[1024,128]{1,0:T(8,128)(2,1)S(1)} %slice_bitcast_fusion), channel_id=1, source_target_pairs={{0,16},{4,20},{8,24},{12,28},{16,0},{20,4},{24,8},{28,12},{1,17},{... | collective-permute-start | bytes 786440 | tf_op jit(solution)/shard_map/ppermute | solution.py:177
  142.7 11.1 %collective-permute-start.20 = (bf16[1024,128]{1,0:T(8,128)(2,1)S(1)}, bf16[1024,128]{1,0:T(8,128)(2,1)S(1)}, u32[]{:S(2)}, u32[]{:S(2)}) collective-permute-start(bf16[1024,128]{1,0:T(8,128)(2,1)S(1)} %slice.171), channel_id=1, source_target_pairs={{0,8},{4,12},{8,0},{12,4},{16,24},{20,28},{24,16},{28,20},{1,9},{5... | collective-permute-start | bytes 786440 | tf_op jit(solution)/shard_map/ppermute | solution.py:177
  (10 other events, 66.4 us)

commit v3 on v2

v3 whole, which is shorter than its diff:
```python
import functools

import jax
import jax.numpy as jnp
from jax import lax
from jax.experimental import pallas as pl
from jax.experimental.pallas import tpu as pltpu
from jax.sharding import PartitionSpec as P

SIDE = 128
UNROLL = 4
FLIP_GROUP = 32
FLIP_BYTES = 24 * 1024 * 1024
SPMM_BYTES = 8 * 1024 * 1024


def flip_kernel(tiles_ref, out_ref, t_in, sems):
    slots = t_in.shape[0]
    groups = slots // FLIP_GROUP
    loads = [
        pltpu.make_async_copy(
            tiles_ref.at[pl.ds(g * FLIP_GROUP, FLIP_GROUP)], t_in.at[pl.ds(g * FLIP_GROUP, FLIP_GROUP)], sems.at[g]
        )
        for g in range(groups)
    ]
    for load in loads:
        load.start()
    out_ref[slots] = jnp.zeros((SIDE, SIDE), out_ref.dtype)
    for g in range(groups):
        loads[g].wait()

        def some(step, carry, g=g):
            for u in range(4):
                k = g * FLIP_GROUP + step * 4 + u
                out_ref[k] = t_in[k].T
            return carry

        lax.fori_loop(0, FLIP_GROUP // 4, some, 0)


def flip_tiles(tile_stack):
    slots = tile_stack.shape[0]
    return pl.pallas_call(
        flip_kernel,
        out_shape=jax.ShapeDtypeStruct((slots + 1, SIDE, SIDE), tile_stack.dtype),
        in_specs=[pl.BlockSpec(memory_space=pl.ANY)],
        out_specs=pl.BlockSpec(memory_space=pltpu.VMEM),
        scratch_shapes=[pltpu.VMEM(tile_stack.shape, tile_stack.dtype), pltpu.SemaphoreType.DMA((slots // FLIP_GROUP,))],
        compiler_params=pltpu.CompilerParams(vmem_limit_bytes=FLIP_BYTES),
        cost_estimate=pl.CostEstimate(flops=0, bytes_accessed=4096, transcendentals=0),
        name="flip_tiles",
    )(tile_stack)


def spmm_kernel(layout, tile_at_ref, block_at_ref, out_at_ref, same_ref, info_ref, *refs):
    n_refs = sum(layout)
    refs_left = list(refs[:n_refs])
    pieces = [[refs_left.pop(0) for _ in range(n)] for n in layout]
    tiles_ref, send_ref, keep_ref, m_vmem, total_ref = refs[n_refs:]
    nodes, width = pieces[0][0].shape

    for out_ref in (send_ref, keep_ref):

        def clear(step, carry, out_ref=out_ref):
            out_ref[pl.ds(pl.multiple_of(step * 1024, 1024), 1024), :] = jnp.zeros((1024, width), out_ref.dtype)
            return carry

        lax.fori_loop(0, out_ref.shape[0] // 1024, clear, 0)
    for p, options in enumerate(pieces):

        def take(ref, p=p):
            def some(step, carry):
                at = pl.multiple_of(step * 512, 512)
                m_vmem[pl.ds(pl.multiple_of(p * nodes + at, 512), 512), :] = ref[pl.ds(at, 512), :]
                return carry

            lax.fori_loop(0, nodes // 512, some, 0)

        if len(options) == 1:
            take(options[0])
        else:
            pl.when(info_ref[0] == 1)(functools.partial(take, options[0]))
            pl.when(info_ref[0] != 1)(functools.partial(take, options[1]))

    def block(index):
        return m_vmem[pl.ds(pl.multiple_of(index * SIDE, SIDE), SIDE), :]

    def add_pairs(out_ref, step, carry):
        total = total_ref[...]
        prods = []
        for u in range(UNROLL):
            k = 2 * (step * UNROLL + u)
            left = jnp.concatenate([tiles_ref[tile_at_ref[k]], tiles_ref[tile_at_ref[k + 1]]], axis=1)
            right = jnp.concatenate([block(block_at_ref[k]), block(block_at_ref[k + 1])], axis=0)
            prods.append(jnp.dot(left, right, preferred_element_type=jnp.float32))
        for u in range(UNROLL):
            k = step * UNROLL + u
            total = prods[u] + jnp.where(same_ref[k] == 1, total, jnp.zeros_like(total))
            out_ref[pl.ds(pl.multiple_of(out_at_ref[k] * SIDE, SIDE), SIDE), :] = total.astype(out_ref.dtype)
        total_ref[...] = total
        return carry

    total_ref[...] = jnp.zeros_like(total_ref)
    lax.fori_loop(0, info_ref[1], functools.partial(add_pairs, send_ref), 0)
    lax.fori_loop(info_ref[1], info_ref[2], functools.partial(add_pairs, keep_ref), 0)


def spmm(plan, pieces, tiles, n_row):
    nodes, width = pieces[0][0].shape
    half = n_row // 2 * nodes
    out = jax.ShapeDtypeStruct((half + SIDE, width), jnp.bfloat16)
    n_refs = sum(len(p) for p in pieces)
    return pl.pallas_call(
        functools.partial(spmm_kernel, [len(p) for p in pieces]),
        out_shape=(out, out),
        grid_spec=pltpu.PrefetchScalarGridSpec(
            num_scalar_prefetch=5,
            grid=(),
            in_specs=[pl.BlockSpec(memory_space=pltpu.VMEM)] * (n_refs + 1),
            out_specs=[pl.BlockSpec(memory_space=pltpu.VMEM)] * 2,
            scratch_shapes=[
                pltpu.VMEM((len(pieces) * nodes, width), jnp.bfloat16),
                pltpu.VMEM((SIDE, width), jnp.float32),
            ],
        ),
        compiler_params=pltpu.CompilerParams(vmem_limit_bytes=SPMM_BYTES),
        cost_estimate=pl.CostEstimate(flops=0, bytes_accessed=4096, transcendentals=0),
        name="spmm",
    )(*plan, *[ref for p in pieces for ref in p], tiles)


def xor_permute(value, axis, mask):
    size = lax.axis_size(axis)
    return lax.ppermute(value, axis, [(i, i ^ mask) for i in range(size)])


def tree_sum(values):
    while len(values) > 1:
        values = [a + b for a, b in zip(values[::2], values[1::2])]
    return values[0]


def gather_first(own):
    return xor_permute(own, "col", 1), xor_permute(own, "col", 2)


def gather_second(own, by_two, n_col):
    ends, middles = [], []
    for low in range(0, n_col, 4):
        ends += [(low + 1, low), (low + 2, low + 3)]
        middles += [(low + 1, low + 2), (low + 2, low + 1)]
    return lax.ppermute(own, "col", middles), lax.ppermute(by_two, "col", ends)


def as_pieces(own, first, second, mid, n_col):
    if n_col == 4:
        return [[own], [first[0]], [first[1]], list(second)]
    pieces = [own, first[0], first[1], jnp.where(mid, second[0], second[1])]
    for high in range(4, n_col, 4):
        pieces += [xor_permute(piece, "col", high) for piece in pieces[:4]]
    return [[piece] for piece in pieces]


def fence(*values):
    return lax.optimization_barrier(values)


def add_f32(a, b):
    return a.astype(jnp.float32) + b.astype(jnp.float32)


def plan_slots(tile_rows, tile_cols, count, row, col, mid, n_row, per_dev):
    slots = tile_rows.shape[0]
    half, quarter = n_row // 2, n_row // 4
    row_pos = ((tile_rows // per_dev) ^ col) * per_dev + tile_rows % per_dev
    away = (tile_cols // per_dev) ^ row
    near, local = away >> 1, tile_cols % per_dev
    upper = local // (per_dev // 2)
    spot = local % (per_dev // 2)
    first_bit = jnp.where(upper == 0, near & 1, near // quarter)
    rest = jnp.where(upper == 0, near >> 1, near % quarter)
    group = upper * 2 + (1 - first_bit)
    out_pos = (group * quarter + rest) * (per_dev // 2) + spot
    kept = 1 - (away & 1)
    n_out = half * per_dev
    ids = jnp.arange(slots, dtype=jnp.int32)
    live = ids < count
    key = jnp.where(live, kept * n_out + out_pos, 2 * n_out)
    equal = key[None, :] == key[:, None]
    below = key[None, :] < key[:, None]
    earlier = jnp.sum((equal & (ids[None, :] < ids[:, None])).astype(jnp.int32), axis=1)
    later = jnp.sum((equal & (ids[None, :] > ids[:, None])).astype(jnp.int32), axis=1)
    weight = jnp.where(live, 1 + ((later == 0) & (earlier % 2 == 0)).astype(jnp.int32), 0)
    spot_at = jnp.sum(jnp.where(below, weight[None, :], 0), axis=1) + earlier
    send_len = jnp.sum(jnp.where(kept == 0, weight, 0))
    all_len = jnp.sum(weight)
    step = 2 * UNROLL
    send_steps = (send_len + step - 1) // step
    keep_steps = (all_len - send_len + step - 1) // step
    spot_at = spot_at + kept * (send_steps * step - send_len)
    spot_at = jnp.where(live, spot_at, -1)
    size = -(-(slots + 2 * n_out + 2 * step) // (2 * step)) * 2 * step
    hit = spot_at[None, :] == jnp.arange(size, dtype=jnp.int32)[:, None]

    def placed(values, empty):
        return jnp.sum(jnp.where(hit, values[None, :] - empty, 0), axis=1) + empty

    tile_at = placed(ids, slots)
    block_at = placed(row_pos, 0)
    out_at = placed(out_pos, n_out)[::2]
    same = jnp.concatenate([jnp.zeros((1,), jnp.int32), (out_at[1:] == out_at[:-1]).astype(jnp.int32)])
    info = jnp.stack([mid.astype(jnp.int32), send_steps, send_steps + keep_steps])
    return tile_at, block_at, out_at, same, info


def core_sums(keep, recv):
    size = (keep.shape[0] - SIDE) // 4
    return [add_f32(keep[g * size : (g + 1) * size], recv[g * size : (g + 1) * size]).astype(jnp.bfloat16) for g in range(4)]


def halve(value, upper, rows):
    blocks = value.shape[0] // rows
    shape = (2, blocks // 2) if upper else (blocks // 2, 2)
    cut = value.reshape(shape + (rows, value.shape[1]))
    if upper:
        sent, kept = cut[1], cut[0]
    else:
        sent, kept = cut[:, 1], cut[:, 0]
    return sent.reshape(-1, value.shape[1]), kept.reshape(-1, value.shape[1])


def exchange_first(sums, bits):
    return xor_permute(sums[0], "row", bits[0]), xor_permute(sums[2], "row", bits[-1])


def exchange_rest(sums, recv, bits, rows):
    done = []
    for upper in (0, 1):
        value = add_f32(sums[2 * upper + 1], recv[upper])
        for bit in (bits[::-1] if upper else bits)[1:]:
            sent, kept = halve(value.astype(jnp.bfloat16), upper, rows)
            value = add_f32(kept, xor_permute(sent, "row", bit))
        done.append(value.astype(jnp.bfloat16))
    return jnp.concatenate(done, axis=0)


def weight_term(features_groups, sums):
    terms = [
        lax.dot_general(f, s, (((0,), (0,)), ((), ())), preferred_element_type=jnp.float32)
        for f, s in zip(features_groups, sums)
    ]
    return tree_sum(terms)


def sum_over(term, axis, masks):
    parts = [term] + [xor_permute(term, axis, m) for m in masks]
    return tree_sum([p.astype(jnp.float32) for p in parts])


def body(grad_out, preact, features, weight, tiles, tile_rows, tile_cols, live_counts):
    nodes, width = grad_out.shape
    n_row, n_col = lax.axis_size("row"), lax.axis_size("col")
    row, col = lax.axis_index("row"), lax.axis_index("col")
    slots = tiles.shape[2]
    cw = width // 2
    rows = nodes // 2
    bits = [1 << b for b in range(1, n_row.bit_length() - 1)]
    mid = ((col & 3) == 1) | ((col & 3) == 2)
    count = live_counts.reshape(())

    own0, own1 = [
        jnp.where(preact[:, cut] > 0, grad_out[:, cut], jnp.zeros_like(grad_out[:, cut]))
        for cut in (slice(0, cw), slice(cw, width))
    ]
    first0 = gather_first(own0)
    plan = plan_slots(tile_rows.reshape(slots), tile_cols.reshape(slots), count, row, col, mid, n_row, nodes // SIDE)
    flipped = flip_tiles(tiles.reshape(slots, SIDE, SIDE))
    features, flipped = fence(features, flipped)
    near = [features]
    for bit in bits[:2]:
        near.append(xor_permute(features, "row", bit))
    own0, own1, first0, flipped, plan = fence(own0, own1, first0, flipped, plan)

    second0 = gather_second(own0, first0[1], n_col)
    pieces0 = as_pieces(own0, first0, second0, mid, n_col)
    pieces0, own1, near = fence(pieces0, own1, near)

    first1 = gather_first(own1)
    near.append(xor_permute(near[1], "row", bits[1]))
    for bit in bits[2:]:
        near += [xor_permute(f, "row", bit) for f in near]
    send0, keep0 = spmm(plan, pieces0, flipped, n_row)
    own1, first1, near, send0, keep0 = fence(own1, first1, near, send0, keep0)

    second1 = gather_second(own1, first1[1], n_col)
    pieces1 = as_pieces(own1, first1, second1, mid, n_col)
    sums0 = core_sums(keep0, xor_permute(send0, "row", 1))
    features_groups = []
    for upper in (0, 1):
        own_bit = (n_row // 4) if upper else 1
        for want in (1, 0):
            parts = [f[upper * rows : (upper + 1) * rows] for q, f in enumerate(near) if (q & own_bit != 0) == want]
            features_groups.append(jnp.concatenate(parts, axis=0))
    pieces1, sums0, features_groups = fence(pieces1, sums0, features_groups)

    recv0 = exchange_first(sums0, bits)
    send1, keep1 = spmm(plan, pieces1, flipped, n_row)
    recv0, send1, keep1 = fence(recv0, send1, keep1)

    colgrad0 = exchange_rest(sums0, recv0, bits, rows)
    sums1 = core_sums(keep1, xor_permute(send1, "row", 1))
    colgrad0, sums1 = fence(colgrad0, sums1)
    term1 = weight_term(features_groups, sums1).astype(jnp.bfloat16)
    term0 = weight_term(features_groups, sums0).astype(jnp.bfloat16)
    term = jnp.concatenate([term0, term1], axis=1)
    sums1, term = fence(sums1, term)

    recv1 = exchange_first(sums1, bits)
    term = sum_over(term, "col", range(1, n_col)).astype(jnp.bfloat16)
    recv1, term = fence(recv1, term)

    colgrad1 = exchange_rest(sums1, recv1, bits, rows)
    term = sum_over(term, "row", range(2, n_row, 2)).astype(jnp.bfloat16)
    colgrad1, term = fence(colgrad1, term)

    grad_weight = sum_over(term, "row", [1])
    colgrad = jnp.concatenate([colgrad0, colgrad1], axis=1)
    grad_features = lax.dot_general(
        colgrad, weight, (((1,), (1,)), ((), ())), preferred_element_type=jnp.float32
    ).astype(jnp.bfloat16)
    return (grad_features, grad_weight)


def solution(mesh):
    in_specs = (
        P(("row", "col"), None),
        P(("row", "col"), None),
        P(("col", "row"), None),
        P(),
        P("row", "col", None, None, None),
        P("row", "col", None),
        P("row", "col", None),
        P("row", "col"),
    )
    out_specs = (P(("col", "row"), None), P())
    return jax.shard_map(body, mesh=mesh, in_specs=in_specs, out_specs=out_specs, check_vma=False)
```

time: 158 us -> 149 us (0.943); the launches traced: 155 us -> 149 us
  Pallas kernels: 40.6 us -> 26.7 us
  local copies, waits for them, and re-layouts: 4.02 us -> 16 us
  waiting for transfers between devices: 51 us -> 61.8 us
  starting transfers between devices: 38.2 us -> 29.9 us
  other arithmetic: 12.4 us -> 5.89 us
  matrix products: 7.5 us -> 4.31 us
  between operations: 1.73 us -> 4.2 us
    unnamed x28 -> x21, local copies, waits for them, and re-layouts: 2.47 us -> 12.8 us
    pallas_call x2, Pallas kernels: 27.6 us -> 18.8 us  [spmm(): pl.pallas_call(functools.partial(spmm_kernel, [len(p) for p in pieces]),...]
    ppermute x24, waiting for transfers between devices: 30.7 us -> 39.1 us  [xor_permute(): return lax.ppermute(value, axis, [(i, i ^ mask) for i in range(size)])]
    ppermute x24, starting transfers between devices: 33.5 us -> 25.9 us  [xor_permute(): return lax.ppermute(value, axis, [(i, i ^ mask) for i in range(size)])]
    pallas_call x1, Pallas kernels: 13 us -> 7.84 us  [flip_tiles(): pl.pallas_call(flip_kernel, out_shape=jax.ShapeDtypeStruct((slots + 1, SI...]
    dot_general x8, matrix products: 6.06 us -> 2.83 us  [weight_term(): lax.dot_general(f, s, (((0,), (0,)), ((), ())), preferred_element_type=jn...]
    ppermute x2, waiting for transfers between devices: 20.3 us -> 22.7 us  [gather_second(): lax.ppermute(by_two, 'col', ends)]
    convert_element_type x4, other arithmetic: 2.9 us -> 0.56 us  [exchange_rest(): sent, kept = halve(value.astype(jnp.bfloat16), upper, rows)]
  transfers between devices with their start and end apart: 28 -> 28, of which waited for: 10 -> 12; matrix products, arithmetic and copies ran while one was open for 11% -> 6% of each run, Pallas kernels for 26% -> 18%
where the time goes in v3:
time: 149 us
  waiting for transfers between devices  61.8 us (41%)
  starting transfers between devices  29.9 us (20%)
  Pallas kernels  26.7 us (18%)
  local copies, waits for them, and re-layouts  16 us (11%)
  other arithmetic  5.89 us (4%)
  matrix products  4.31 us (3%)
  between operations  4.2 us (3%)
    ppermute x24, waiting for transfers between devices, xor_permute(): return lax.ppermute(value, axis, [(i, i ^ mask) for i in range(size)])  39.1 us
    ppermute x24, starting transfers between devices, xor_permute(): return lax.ppermute(value, axis, [(i, i ^ mask) for i in range(size)])  25.9 us
    ppermute x2, waiting for transfers between devices, gather_second(): lax.ppermute(by_two, 'col', ends)  22.7 us
    pallas_call x2, Pallas kernels, spmm(): pl.pallas_call(functools.partial(spmm_kernel, [len(p) for p in pieces]),...  18.8 us
    unnamed x21, local copies, waits for them, and re-layouts  12.8 us
    pallas_call x1, Pallas kernels, flip_tiles(): pl.pallas_call(flip_kernel, out_shape=jax.ShapeDtypeStruct((slots + 1, SI...  7.84 us
  transfers between devices with their start and end apart: 28, of which 12 were waited for; matrix products, arithmetic and copies ran while one was open for 6% of the time, Pallas kernels for 18%

profile of v3, /device:TPU:1, one launch (start us, length us, event | category | flops | bytes accessed | tf_op | source)
XLA Modules:
  0.0 148.7 jit_solution(15524017097631052955)
XLA Ops:
  0.6 1.7 %compare_select_fusion = (bf16[2048,128]{1,0:T(8,128)(2,1)S(1)}, bf16[2048,128]{1,0:T(8,128)(2,1)S(1)}) fusion(bf16[2048,256]{1,0:T(8,128)(2,1)} %param.8, bf16[2048,256]{1,0:T(8,128)(2,1)} %param.9), kind=kLoop, calls=%fused_computation.28 | loop fusion | flops 1048576 | bytes 3145728 | tf_op jit(solution)/shard_map/jit(_where)/select_n | solution.py:272
  2.3 3.2 %collective-permute-start.1 = (bf16[2048,128]{1,0:T(8,128)(2,1)S(1)}, bf16[2048,128]{1,0:T(8,128)(2,1)S(1)}, u32[]{:S(2)}, u32[]{:S(2)}) collective-permute-start(bf16[2048,128]{1,0:T(8,128)(2,1)S(1)} %get-tuple-element.83.refs_0_), channel_id=1, source_target_pairs={{0,2},{1,3},{2,0},{3,1},{4,6},{5,7},{6,4},{7,5},{8,10},{9,11},{10,... | collective-permute-start | bytes 1572872 | tf_op jit(solution)/shard_map/ppermute | solution.py:134
  5.5 1.3 collective-permute-start
  6.8 4.0 %copy-done.3 = bf16[1,1,320,128,128]{4,3,2,1,0:T(8,128)(2,1)S(1)} copy-done((bf16[1,1,320,128,128]{4,3,2,1,0:T(8,128)(2,1)S(1)}, bf16[1,1,320,128,128]{4,3,2,1,0:T(8,128)(2,1)}, u32[]{:S(2)}) %copy-start.3) | copy-done | bytes 10485784
  10.8 7.8 %flip_tiles.1.refs_5_ = bf16[321,128,128]{2,1,0:T(8,128)(2,1)S(1)} custom-call(bf16[320,128,128]{2,1,0:T(8,128)(2,1)S(1)} %bitcast.43), custom_call_target="tpu_custom_call" | custom-call | bytes 4096 | tf_op jit(solution)/shard_map/flip_tiles/pallas_call | solution.py:43
  18.7 4.0 %copy-done.1 = bf16[321,128,128]{2,1,0:T(8,128)(2,1)} copy-done((bf16[321,128,128]{2,1,0:T(8,128)(2,1)}, bf16[321,128,128]{2,1,0:T(8,128)(2,1)S(1)}, u32[]{:S(2)}) %copy-start.1) | copy-done | bytes 10518552
  22.7 1.2 collective-permute-start.5
  23.9 1.2 collective-permute-start.4
  30.9 1.3 collective-permute-start.3
  32.3 12.3 %collective-permute-done.3.refs_4_ = bf16[2048,128]{1,0:T(8,128)(2,1)S(1)} collective-permute-done((bf16[2048,128]{1,0:T(8,128)(2,1)S(1)}, bf16[2048,128]{1,0:T(8,128)(2,1)S(1)}, u32[]{:S(2)}, u32[]{:S(2)}) %collective-permute-start.3) | collective-permute-done | bytes 524320 | tf_op jit(solution)/shard_map/ppermute | solution.py:152
  44.6 1.6 %collective-permute-done.5 = bf16[2048,256]{1,0:T(8,128)(2,1)} collective-permute-done((bf16[2048,256]{1,0:T(8,128)(2,1)S(1)}, bf16[2048,256]{1,0:T(8,128)(2,1)}, u32[]{:S(2)}, u32[]{:S(2)}) %collective-permute-start.5) | collective-permute-done | bytes 1048608 | tf_op jit(solution)/shard_map/ppermute | solution.py:134
  47.5 2.1 %collective-permute-start.6 = (bf16[2048,128]{1,0:T(8,128)(2,1)S(1)}, bf16[2048,128]{1,0:T(8,128)(2,1)S(1)}, u32[]{:S(2)}, u32[]{:S(2)}) collective-permute-start(bf16[2048,128]{1,0:T(8,128)(2,1)S(1)} %get-tuple-element.103.refs_0_), channel_id=1, source_target_pairs={{0,1},{1,0},{2,3},{3,2},{4,5},{5,4},{6,7},{7,6},{8,9},{9,8},{10,11... | collective-permute-start | bytes 1572872 | tf_op jit(solution)/shard_map/ppermute | solution.py:134
  49.6 4.0 %copy-done.2 = bf16[321,128,128]{2,1,0:T(8,128)(2,1)S(1)} copy-done((bf16[321,128,128]{2,1,0:T(8,128)(2,1)S(1)}, bf16[321,128,128]{2,1,0:T(8,128)(2,1)}, u32[]{:S(2)}) %copy-start.2) | copy-done | bytes 10518552
  53.6 9.4 %spmm.2 = (bf16[8320,128]{1,0:T(8,128)(2,1)S(1)}, bf16[8320,128]{1,0:T(8,128)(2,1)S(1)}) custom-call(s32[464]{0:T(512)S(1)} %broadcast_add_fusion.2.tile_at_ref, s32[464]{0:T(512)S(1)} %get-tuple-element.79.block_at_ref, s32[232]{0:T(256)S(1)} %slice.125.out_at_ref, s32[232]{0:T(256)S(1)} %add_convert_fusion.16.same_ref, s32[3]{0:T(128)S(1)} %pad_add_fusion.info_ref, ...), custom_call_target="tpu_custom_call" | custom-call | bytes 4096 | tf_op jit(solution)/shard_map/spmm/pallas_call | solution.py:113
  63.0 10.3 %collective-permute-done.7.refs_2_ = bf16[2048,128]{1,0:T(8,128)(2,1)S(1)} collective-permute-done((bf16[2048,128]{1,0:T(8,128)(2,1)S(1)}, bf16[2048,128]{1,0:T(8,128)(2,1)S(1)}, u32[]{:S(2)}, u32[]{:S(2)}) %collective-permute-start.7) | collective-permute-done | bytes 524320 | tf_op jit(solution)/shard_map/ppermute | solution.py:134
  74.5 1.3 collective-permute-start.10
  75.8 1.3 fusion.34
  77.4 1.4 fusion.35
  79.6 10.4 %collective-permute-done.10.refs_4_ = bf16[2048,128]{1,0:T(8,128)(2,1)S(1)} collective-permute-done((bf16[2048,128]{1,0:T(8,128)(2,1)S(1)}, bf16[2048,128]{1,0:T(8,128)(2,1)S(1)}, u32[]{:S(2)}, u32[]{:S(2)}) %collective-permute-start.10) | collective-permute-done | bytes 524320 | tf_op jit(solution)/shard_map/ppermute | solution.py:152
  92.7 9.4 %spmm.3 = (bf16[8320,128]{1,0:T(8,128)(2,1)S(1)}, bf16[8320,128]{1,0:T(8,128)(2,1)S(1)}) custom-call(s32[464]{0:T(512)S(1)} %broadcast_add_fusion.2.tile_at_ref, s32[464]{0:T(512)S(1)} %get-tuple-element.79.block_at_ref, s32[232]{0:T(256)S(1)} %slice.125.out_at_ref, s32[232]{0:T(256)S(1)} %add_convert_fusion.16.same_ref, s32[3]{0:T(128)S(1)} %pad_add_fusion.info_ref, ...), custom_call_target="tpu_custom_call" | custom-call | bytes 4096 | tf_op jit(solution)/shard_map/spmm/pallas_call | solution.py:113
  103.5 2.0 %collective-permute-start.16 = (bf16[8320,128]{1,0:T(8,128)(2,1)S(1)}, bf16[8320,128]{1,0:T(8,128)(2,1)S(1)}, u32[]{:S(2)}, u32[]{:S(2)}) collective-permute-start(bf16[8320,128]{1,0:T(8,128)(2,1)S(1)} %get-tuple-element.114), channel_id=1, source_target_pairs={{0,4},{4,0},{8,12},{12,8},{16,20},{20,16},{24,28},{28,24},{1,5},{5... | collective-permute-start | bytes 6389768 | tf_op jit(solution)/shard_map/ppermute | solution.py:134
  105.8 1.2 collective-permute-start.14
  107.7 6.1 %collective-permute-done.14 = bf16[1024,128]{1,0:T(8,128)(2,1)S(1)} collective-permute-done((bf16[1024,128]{1,0:T(8,128)(2,1)S(1)}, bf16[1024,128]{1,0:T(8,128)(2,1)S(1)}, u32[]{:S(2)}, u32[]{:S(2)}) %collective-permute-start.14) | collective-permute-done | bytes 262176 | tf_op jit(solution)/shard_map/ppermute | solution.py:134
  117.6 2.1 %collective-permute-start.21 = (bf16[256,256]{0,1:T(8,128)(2,1)S(1)}, bf16[256,256]{0,1:T(8,128)(2,1)S(1)}, u32[]{:S(2)}, u32[]{:S(2)}) collective-permute-start(bf16[256,256]{0,1:T(8,128)(2,1)S(1)} %pad_maximum_fusion.6), channel_id=1, source_target_pairs={{0,3},{1,2},{2,1},{3,0},{4,7},{5,6},{6,5},{7,4},{8,11},{9,10},{10,... | collective-permute-start | bytes 393224 | tf_op jit(solution)/shard_map/ppermute | solution.py:134
  119.7 1.4 collective-permute-start.19
  121.1 2.3 %collective-permute-done.21 = bf16[256,256]{0,1:T(8,128)(2,1)S(1)} collective-permute-done((bf16[256,256]{0,1:T(8,128)(2,1)S(1)}, bf16[256,256]{0,1:T(8,128)(2,1)S(1)}, u32[]{:S(2)}, u32[]{:S(2)}) %collective-permute-start.21) | collective-permute-done | bytes 131104 | tf_op jit(solution)/shard_map/ppermute | solution.py:134
  123.4 7.3 %collective-permute-done.20 = bf16[256,256]{0,1:T(8,128)(2,1)S(1)} collective-permute-done((bf16[256,256]{0,1:T(8,128)(2,1)S(1)}, bf16[256,256]{0,1:T(8,128)(2,1)S(1)}, u32[]{:S(2)}, u32[]{:S(2)}) %collective-permute-start.20) | collective-permute-done | bytes 131104 | tf_op jit(solution)/shard_map/ppermute | solution.py:134
  130.8 2.1 %collective-permute-start.26 = (bf16[256,256]{0,1:T(8,128)(2,1)S(1)}, bf16[256,256]{0,1:T(8,128)(2,1)S(1)}, u32[]{:S(2)}, u32[]{:S(2)}) collective-permute-start(bf16[256,256]{0,1:T(8,128)(2,1)S(1)} %add_convert_fusion.15), channel_id=1, source_target_pairs={{0,24},{4,28},{8,16},{12,20},{16,8},{20,12},{24,0},{28,4},{1,25},{... | collective-permute-start | bytes 393224 | tf_op jit(solution)/shard_map/ppermute | solution.py:134
  134.9 1.3 collective-permute-start.23
  136.2 3.6 %collective-permute-done.25 = bf16[256,256]{0,1:T(8,128)(2,1)S(1)} collective-permute-done((bf16[256,256]{0,1:T(8,128)(2,1)S(1)}, bf16[256,256]{0,1:T(8,128)(2,1)S(1)}, u32[]{:S(2)}, u32[]{:S(2)}) %collective-permute-start.25) | collective-permute-done | bytes 131104 | tf_op jit(solution)/shard_map/ppermute | solution.py:134
  139.9 5.5 %collective-permute-done.22 = bf16[1024,128]{1,0:T(8,128)(2,1)S(1)} collective-permute-done((bf16[1024,128]{1,0:T(8,128)(2,1)S(1)}, bf16[1024,128]{1,0:T(8,128)(2,1)S(1)}, u32[]{:S(2)}, u32[]{:S(2)}) %collective-permute-start.22) | collective-permute-done | bytes 262176 | tf_op jit(solution)/shard_map/ppermute | solution.py:134
  146.3 1.5 convolution_convert_fusion
  (102 shorter events, 18.9 us)
Async XLA Ops:
  0.6 145.7 %copy-start = (bf16[256,256]{1,0:T(8,128)(2,1)S(1)}, bf16[256,256]{1,0:T(8,128)(2,1)}, u32[]{:S(2)}) copy-start(bf16[256,256]{1,0:T(8,128)(2,1)} %param.11) | copy-start | bytes 393220
  2.3 27.9 %collective-permute-start.1 = (bf16[2048,128]{1,0:T(8,128)(2,1)S(1)}, bf16[2048,128]{1,0:T(8,128)(2,1)S(1)}, u32[]{:S(2)}, u32[]{:S(2)}) collective-permute-start(bf16[2048,128]{1,0:T(8,128)(2,1)S(1)} %get-tuple-element.83.refs_0_), channel_id=1, source_target_pairs={{0,2},{1,3},{2,0},{3,1},{4,6},{5,7},{6,4},{7,5},{8,10},{9,11},{10,... | collective-permute-start | bytes 1572872 | tf_op jit(solution)/shard_map/ppermute | solution.py:134
  5.5 24.7 %collective-permute-start = (bf16[2048,128]{1,0:T(8,128)(2,1)S(1)}, bf16[2048,128]{1,0:T(8,128)(2,1)S(1)}, u32[]{:S(2)}, u32[]{:S(2)}) collective-permute-start(bf16[2048,128]{1,0:T(8,128)(2,1)S(1)} %get-tuple-element.83.refs_0_), channel_id=1, source_target_pairs={{0,1},{1,0},{2,3},{3,2},{4,5},{5,4},{6,7},{7,6},{8,9},{9,8},{10,11... | collective-permute-start | bytes 1572872 | tf_op jit(solution)/shard_map/ppermute | solution.py:134
  10.8 17.8 %copy-start.6 = (s32[1,1,320]{2,1,0:T(1,128)S(1)}, s32[1,1,320]{2,1,0:T(1,128)}, u32[]{:S(2)}) copy-start(s32[1,1,320]{2,1,0:T(1,128)} %param.13) | copy-start | bytes 3844
  22.7 23.5 %collective-permute-start.5 = (bf16[2048,256]{1,0:T(8,128)(2,1)S(1)}, bf16[2048,256]{1,0:T(8,128)(2,1)}, u32[]{:S(2)}, u32[]{:S(2)}) collective-permute-start(bf16[2048,256]{1,0:T(8,128)(2,1)S(1)} %copy-done.4), channel_id=1, source_target_pairs={{0,16},{4,20},{8,24},{12,28},{16,0},{20,4},{24,8},{28,12},{1,17},{... | collective-permute-start | bytes 3145736 | tf_op jit(solution)/shard_map/ppermute | solution.py:134
  23.9 23.2 %collective-permute-start.4 = (bf16[2048,256]{1,0:T(8,128)(2,1)S(1)}, bf16[2048,256]{1,0:T(8,128)(2,1)}, u32[]{:S(2)}, u32[]{:S(2)}) collective-permute-start(bf16[2048,256]{1,0:T(8,128)(2,1)S(1)} %copy-done.4), channel_id=1, source_target_pairs={{0,8},{4,12},{8,0},{12,4},{16,24},{20,28},{24,16},{28,20},{1,9},{5... | collective-permute-start | bytes 3145736 | tf_op jit(solution)/shard_map/ppermute | solution.py:134
  30.2 2.0 %collective-permute-start.2 = (bf16[2048,128]{1,0:T(8,128)(2,1)S(1)}, bf16[2048,128]{1,0:T(8,128)(2,1)S(1)}, u32[]{:S(2)}, u32[]{:S(2)}) collective-permute-start(bf16[2048,128]{1,0:T(8,128)(2,1)S(1)} %get-tuple-element.83.refs_0_), channel_id=1, source_target_pairs={{1,2},{2,1},{5,6},{6,5},{9,10},{10,9},{13,14},{14,13},{17,18},{18,... | collective-permute-start | bytes 1572872 | tf_op jit(solution)/shard_map/ppermute | solution.py:152
  30.9 13.6 %collective-permute-start.3 = (bf16[2048,128]{1,0:T(8,128)(2,1)S(1)}, bf16[2048,128]{1,0:T(8,128)(2,1)S(1)}, u32[]{:S(2)}, u32[]{:S(2)}) collective-permute-start(bf16[2048,128]{1,0:T(8,128)(2,1)S(1)} %collective-permute-done.1.refs_2_), channel_id=1, source_target_pairs={{1,0},{2,3},{5,4},{6,7},{9,8},{10,11},{13,12},{14,15},{17,16},{18,... | collective-permute-start | bytes 1572872 | tf_op jit(solution)/shard_map/ppermute | solution.py:152
  47.2 26.2 %collective-permute-start.8 = (bf16[2048,256]{1,0:T(8,128)(2,1)}, bf16[2048,256]{1,0:T(8,128)(2,1)S(1)}, u32[]{:S(2)}, u32[]{:S(2)}) collective-permute-start(bf16[2048,256]{1,0:T(8,128)(2,1)} %collective-permute-done.4), channel_id=1, source_target_pairs={{0,16},{4,20},{8,24},{12,28},{16,0},{20,4},{24,8},{28,12},{1,17},{... | collective-permute-start | bytes 3145736 | tf_op jit(solution)/shard_map/ppermute | solution.py:134
  47.4 25.9 %collective-permute-start.7 = (bf16[2048,128]{1,0:T(8,128)(2,1)S(1)}, bf16[2048,128]{1,0:T(8,128)(2,1)S(1)}, u32[]{:S(2)}, u32[]{:S(2)}) collective-permute-start(bf16[2048,128]{1,0:T(8,128)(2,1)S(1)} %get-tuple-element.103.refs_0_), channel_id=1, source_target_pairs={{0,2},{1,3},{2,0},{3,1},{4,6},{5,7},{6,4},{7,5},{8,10},{9,11},{10,... | collective-permute-start | bytes 1572872 | tf_op jit(solution)/shard_map/ppermute | solution.py:134
  47.5 25.8 %collective-permute-start.6 = (bf16[2048,128]{1,0:T(8,128)(2,1)S(1)}, bf16[2048,128]{1,0:T(8,128)(2,1)S(1)}, u32[]{:S(2)}, u32[]{:S(2)}) collective-permute-start(bf16[2048,128]{1,0:T(8,128)(2,1)S(1)} %get-tuple-element.103.refs_0_), channel_id=1, source_target_pairs={{0,1},{1,0},{2,3},{3,2},{4,5},{5,4},{6,7},{7,6},{8,9},{9,8},{10,11... | collective-permute-start | bytes 1572872 | tf_op jit(solution)/shard_map/ppermute | solution.py:134
  73.3 5.7 %collective-permute-start.11 = (bf16[8320,128]{1,0:T(8,128)(2,1)S(1)}, bf16[8320,128]{1,0:T(8,128)(2,1)S(1)}, u32[]{:S(2)}, u32[]{:S(2)}) collective-permute-start(bf16[8320,128]{1,0:T(8,128)(2,1)S(1)} %get-tuple-element.95), channel_id=1, source_target_pairs={{0,4},{4,0},{8,12},{12,8},{16,20},{20,16},{24,28},{28,24},{1,5},{5... | collective-permute-start | bytes 6389768 | tf_op jit(solution)/shard_map/ppermute | solution.py:134
  73.8 5.8 %collective-permute-start.9 = (bf16[2048,128]{1,0:T(8,128)(2,1)S(1)}, bf16[2048,128]{1,0:T(8,128)(2,1)S(1)}, u32[]{:S(2)}, u32[]{:S(2)}) collective-permute-start(bf16[2048,128]{1,0:T(8,128)(2,1)S(1)} %get-tuple-element.103.refs_0_), channel_id=1, source_target_pairs={{1,2},{2,1},{5,6},{6,5},{9,10},{10,9},{13,14},{14,13},{17,18},{18,... | collective-permute-start | bytes 1572872 | tf_op jit(solution)/shard_map/ppermute | solution.py:152
  74.5 15.4 %collective-permute-start.10 = (bf16[2048,128]{1,0:T(8,128)(2,1)S(1)}, bf16[2048,128]{1,0:T(8,128)(2,1)S(1)}, u32[]{:S(2)}, u32[]{:S(2)}) collective-permute-start(bf16[2048,128]{1,0:T(8,128)(2,1)S(1)} %collective-permute-done.7.refs_2_), channel_id=1, source_target_pairs={{1,0},{2,3},{5,4},{6,7},{9,8},{10,11},{13,12},{14,15},{17,16},{18,... | collective-permute-start | bytes 1572872 | tf_op jit(solution)/shard_map/ppermute | solution.py:152
  77.1 15.6 %slice-start = ((s8[10518528]{0:T(1024)(128)(4,1)}), s8[4194304]{0:T(1024)(128)(4,1)S(1)}, s32[]{:S(2)}) async-start(s8[10518528]{0:T(1024)(128)(4,1)} %bitcast.41), calls=%async_computation | async-start | bytes 8388608
  77.3 15.4 %slice-start.1 = ((s8[10518528]{0:T(1024)(128)(4,1)}), s8[4194304]{0:T(1024)(128)(4,1)S(1)}, s32[]{:S(2)}) async-start(s8[10518528]{0:T(1024)(128)(4,1)} %bitcast.41), calls=%async_computation.1 | async-start | bytes 8388608
  89.9 13.0 %collective-permute-start.12 = (bf16[2048,128]{1,0:T(8,128)(2,1)S(1)}, bf16[2048,128]{1,0:T(8,128)(2,1)S(1)}, u32[]{:S(2)}, u32[]{:S(2)}) collective-permute-start(bf16[2048,128]{1,0:T(8,128)(2,1)S(1)} %get-tuple-element.101), channel_id=1, source_target_pairs={{0,8},{4,12},{8,0},{12,4},{16,24},{20,28},{24,16},{28,20},{1,9},{5... | collective-permute-start | bytes 1572872 | tf_op jit(solution)/shard_map/ppermute | solution.py:134
  91.1 12.3 %collective-permute-start.13 = (bf16[2048,128]{1,0:T(8,128)(2,1)S(1)}, bf16[2048,128]{1,0:T(8,128)(2,1)S(1)}, u32[]{:S(2)}, u32[]{:S(2)}) collective-permute-start(bf16[2048,128]{1,0:T(8,128)(2,1)S(1)} %get-tuple-element.102), channel_id=1, source_target_pairs={{0,16},{4,20},{8,24},{12,28},{16,0},{20,4},{24,8},{28,12},{1,17},{... | collective-permute-start | bytes 1572872 | tf_op jit(solution)/shard_map/ppermute | solution.py:134
  103.5 11.3 %collective-permute-start.16 = (bf16[8320,128]{1,0:T(8,128)(2,1)S(1)}, bf16[8320,128]{1,0:T(8,128)(2,1)S(1)}, u32[]{:S(2)}, u32[]{:S(2)}) collective-permute-start(bf16[8320,128]{1,0:T(8,128)(2,1)S(1)} %get-tuple-element.114), channel_id=1, source_target_pairs={{0,4},{4,0},{8,12},{12,8},{16,20},{20,16},{24,28},{28,24},{1,5},{5... | collective-permute-start | bytes 6389768 | tf_op jit(solution)/shard_map/ppermute | solution.py:134
  105.8 8.0 %collective-permute-start.14 = (bf16[1024,128]{1,0:T(8,128)(2,1)S(1)}, bf16[1024,128]{1,0:T(8,128)(2,1)S(1)}, u32[]{:S(2)}, u32[]{:S(2)}) collective-permute-start(bf16[1024,128]{1,0:T(8,128)(2,1)S(1)} %slice_bitcast_fusion.2), channel_id=1, source_target_pairs={{0,16},{4,20},{8,24},{12,28},{16,0},{20,4},{24,8},{28,12},{1,17},{... | collective-permute-start | bytes 786440 | tf_op jit(solution)/shard_map/ppermute | solution.py:134
  107.1 7.6 %collective-permute-start.15 = (bf16[1024,128]{1,0:T(8,128)(2,1)S(1)}, bf16[1024,128]{1,0:T(8,128)(2,1)S(1)}, u32[]{:S(2)}, u32[]{:S(2)}) collective-permute-start(bf16[1024,128]{1,0:T(8,128)(2,1)S(1)} %slice.167), channel_id=1, source_target_pairs={{0,8},{4,12},{8,0},{12,4},{16,24},{20,28},{24,16},{28,20},{1,9},{5... | collective-permute-start | bytes 786440 | tf_op jit(solution)/shard_map/ppermute | solution.py:134
  116.8 13.9 %collective-permute-start.17 = (bf16[2048,128]{1,0:T(8,128)(2,1)S(1)}, bf16[2048,128]{1,0:T(8,128)(2,1)S(1)}, u32[]{:S(2)}, u32[]{:S(2)}) collective-permute-start(bf16[2048,128]{1,0:T(8,128)(2,1)S(1)} %get-tuple-element.125), channel_id=1, source_target_pairs={{0,8},{4,12},{8,0},{12,4},{16,24},{20,28},{24,16},{28,20},{1,9},{5... | collective-permute-start | bytes 1572872 | tf_op jit(solution)/shard_map/ppermute | solution.py:134
  117.2 13.6 %collective-permute-start.18 = (bf16[2048,128]{1,0:T(8,128)(2,1)S(1)}, bf16[2048,128]{1,0:T(8,128)(2,1)S(1)}, u32[]{:S(2)}, u32[]{:S(2)}) collective-permute-start(bf16[2048,128]{1,0:T(8,128)(2,1)S(1)} %get-tuple-element.126), channel_id=1, source_target_pairs={{0,16},{4,20},{8,24},{12,28},{16,0},{20,4},{24,8},{28,12},{1,17},{... | collective-permute-start | bytes 1572872 | tf_op jit(solution)/shard_map/ppermute | solution.py:134
  117.6 5.8 %collective-permute-start.21 = (bf16[256,256]{0,1:T(8,128)(2,1)S(1)}, bf16[256,256]{0,1:T(8,128)(2,1)S(1)}, u32[]{:S(2)}, u32[]{:S(2)}) collective-permute-start(bf16[256,256]{0,1:T(8,128)(2,1)S(1)} %pad_maximum_fusion.6), channel_id=1, source_target_pairs={{0,3},{1,2},{2,1},{3,0},{4,7},{5,6},{6,5},{7,4},{8,11},{9,10},{10,... | collective-permute-start | bytes 393224 | tf_op jit(solution)/shard_map/ppermute | solution.py:134
  119.7 11.0 %collective-permute-start.20 = (bf16[256,256]{0,1:T(8,128)(2,1)S(1)}, bf16[256,256]{0,1:T(8,128)(2,1)S(1)}, u32[]{:S(2)}, u32[]{:S(2)}) collective-permute-start(bf16[256,256]{0,1:T(8,128)(2,1)S(1)} %pad_maximum_fusion.6), channel_id=1, source_target_pairs={{0,2},{1,3},{2,0},{3,1},{4,6},{5,7},{6,4},{7,5},{8,10},{9,11},{10,... | collective-permute-start | bytes 393224 | tf_op jit(solution)/shard_map/ppermute | solution.py:134
  119.7 11.0 %collective-permute-start.19 = (bf16[256,256]{0,1:T(8,128)(2,1)S(1)}, bf16[256,256]{0,1:T(8,128)(2,1)S(1)}, u32[]{:S(2)}, u32[]{:S(2)}) collective-permute-start(bf16[256,256]{0,1:T(8,128)(2,1)S(1)} %pad_maximum_fusion.6), channel_id=1, source_target_pairs={{0,1},{1,0},{2,3},{3,2},{4,5},{5,4},{6,7},{7,6},{8,9},{9,8},{10,11... | collective-permute-start | bytes 393224 | tf_op jit(solution)/shard_map/ppermute | solution.py:134
  130.8 5.5 %collective-permute-start.26 = (bf16[256,256]{0,1:T(8,128)(2,1)S(1)}, bf16[256,256]{0,1:T(8,128)(2,1)S(1)}, u32[]{:S(2)}, u32[]{:S(2)}) collective-permute-start(bf16[256,256]{0,1:T(8,128)(2,1)S(1)} %add_convert_fusion.15), channel_id=1, source_target_pairs={{0,24},{4,28},{8,16},{12,20},{16,8},{20,12},{24,0},{28,4},{1,25},{... | collective-permute-start | bytes 393224 | tf_op jit(solution)/shard_map/ppermute | solution.py:134
  132.8 7.0 %collective-permute-start.25 = (bf16[256,256]{0,1:T(8,128)(2,1)S(1)}, bf16[256,256]{0,1:T(8,128)(2,1)S(1)}, u32[]{:S(2)}, u32[]{:S(2)}) collective-permute-start(bf16[256,256]{0,1:T(8,128)(2,1)S(1)} %add_convert_fusion.15), channel_id=1, source_target_pairs={{0,16},{4,20},{8,24},{12,28},{16,0},{20,4},{24,8},{28,12},{1,17},{... | collective-permute-start | bytes 393224 | tf_op jit(solution)/shard_map/ppermute | solution.py:134
  133.2 6.6 %collective-permute-start.24 = (bf16[256,256]{0,1:T(8,128)(2,1)S(1)}, bf16[256,256]{0,1:T(8,128)(2,1)S(1)}, u32[]{:S(2)}, u32[]{:S(2)}) collective-permute-start(bf16[256,256]{0,1:T(8,128)(2,1)S(1)} %add_convert_fusion.15), channel_id=1, source_target_pairs={{0,8},{4,12},{8,0},{12,4},{16,24},{20,28},{24,16},{28,20},{1,9},{5... | collective-permute-start | bytes 393224 | tf_op jit(solution)/shard_map/ppermute | solution.py:134
  133.6 11.8 %collective-permute-start.22 = (bf16[1024,128]{1,0:T(8,128)(2,1)S(1)}, bf16[1024,128]{1,0:T(8,128)(2,1)S(1)}, u32[]{:S(2)}, u32[]{:S(2)}) collective-permute-start(bf16[1024,128]{1,0:T(8,128)(2,1)S(1)} %slice_bitcast_fusion), channel_id=1, source_target_pairs={{0,16},{4,20},{8,24},{12,28},{16,0},{20,4},{24,8},{28,12},{1,17},{... | collective-permute-start | bytes 786440 | tf_op jit(solution)/shard_map/ppermute | solution.py:134
  134.9 10.6 %collective-permute-start.23 = (bf16[1024,128]{1,0:T(8,128)(2,1)S(1)}, bf16[1024,128]{1,0:T(8,128)(2,1)S(1)}, u32[]{:S(2)}, u32[]{:S(2)}) collective-permute-start(bf16[1024,128]{1,0:T(8,128)(2,1)S(1)} %slice.175), channel_id=1, source_target_pairs={{0,8},{4,12},{8,0},{12,4},{16,24},{20,28},{24,16},{28,20},{1,9},{5... | collective-permute-start | bytes 786440 | tf_op jit(solution)/shard_map/ppermute | solution.py:134
  145.6 2.2 %collective-permute-start.27 = (bf16[256,256]{0,1:T(8,128)(2,1)S(1)}, bf16[256,256]{0,1:T(8,128)(2,1)S(1)}, u32[]{:S(2)}, u32[]{:S(2)}) collective-permute-start(bf16[256,256]{0,1:T(8,128)(2,1)S(1)} %add_convert_fusion.14), channel_id=1, source_target_pairs={{0,4},{4,0},{8,12},{12,8},{16,20},{20,16},{24,28},{28,24},{1,5},{5... | collective-permute-start | bytes 393224 | tf_op jit(solution)/shard_map/ppermute | solution.py:134
  (6 other events, 52.6 us)

commit v4 on v3

--- a/solution.py
+++ b/solution.py
@@ -8,7 +8,8 @@
 from jax.sharding import PartitionSpec as P
 
 SIDE = 128
-UNROLL = 4
+UNROLL = 8
+FIRST_PIECES = 3
 FLIP_GROUP = 32
 FLIP_BYTES = 24 * 1024 * 1024
 SPMM_BYTES = 8 * 1024 * 1024
@@ -52,20 +53,28 @@
     )(tile_stack)
 
 
-def spmm_kernel(layout, tile_at_ref, block_at_ref, out_at_ref, same_ref, info_ref, *refs):
+def spmm_kernel(layout, last, tile_at_ref, block_at_ref, out_at_ref, same_ref, info_ref, *refs):
     n_refs = sum(layout)
     refs_left = list(refs[:n_refs])
     pieces = [[refs_left.pop(0) for _ in range(n)] for n in layout]
-    tiles_ref, send_ref, keep_ref, m_vmem, total_ref = refs[n_refs:]
+    rest = list(refs[n_refs:])
+    tiles_ref = rest.pop(0)
+    acc_refs = (rest.pop(0), rest.pop(0)) if last else (None, None)
+    out_refs = (rest.pop(0), rest.pop(0))
+    m_vmem, total_ref = rest
     nodes, width = pieces[0][0].shape
 
-    for out_ref in (send_ref, keep_ref):
-
-        def clear(step, carry, out_ref=out_ref):
-            out_ref[pl.ds(pl.multiple_of(step * 1024, 1024), 1024), :] = jnp.zeros((1024, width), out_ref.dtype)
+    for out_ref, acc_ref in zip(out_refs, acc_refs):
+
+        def begin(step, carry, out_ref=out_ref, acc_ref=acc_ref):
+            at = pl.ds(pl.multiple_of(step * 256, 256), 256)
+            if last:
+                out_ref[at, :] = acc_ref[at, :].astype(out_ref.dtype)
+            else:
+                out_ref[at, :] = jnp.zeros((256, width), out_ref.dtype)
             return carry
 
-        lax.fori_loop(0, out_ref.shape[0] // 1024, clear, 0)
+        lax.fori_loop(0, out_ref.shape[0] // 256, begin, 0)
     for p, options in enumerate(pieces):
 
         def take(ref, p=p):
@@ -85,7 +94,7 @@
     def block(index):
         return m_vmem[pl.ds(pl.multiple_of(index * SIDE, SIDE), SIDE), :]
 
-    def add_pairs(out_ref, step, carry):
+    def add_pairs(out_ref, acc_ref, step, carry):
         total = total_ref[...]
         prods = []
         for u in range(UNROLL):
@@ -95,28 +104,31 @@
             prods.append(jnp.dot(left, right, preferred_element_type=jnp.float32))
         for u in range(UNROLL):
             k = step * UNROLL + u
-            total = prods[u] + jnp.where(same_ref[k] == 1, total, jnp.zeros_like(total))
-            out_ref[pl.ds(pl.multiple_of(out_at_ref[k] * SIDE, SIDE), SIDE), :] = total.astype(out_ref.dtype)
+            at = pl.ds(pl.multiple_of(out_at_ref[k] * SIDE, SIDE), SIDE)
+            before = acc_ref[at, :] if last else jnp.zeros_like(total)
+            total = prods[u] + jnp.where(same_ref[k] == 1, total, before)
+            out_ref[at, :] = total.astype(out_ref.dtype)
         total_ref[...] = total
         return carry
 
     total_ref[...] = jnp.zeros_like(total_ref)
-    lax.fori_loop(0, info_ref[1], functools.partial(add_pairs, send_ref), 0)
-    lax.fori_loop(info_ref[1], info_ref[2], functools.partial(add_pairs, keep_ref), 0)
-
-
-def spmm(plan, pieces, tiles, n_row):
+    lax.fori_loop(0, info_ref[1], functools.partial(add_pairs, out_refs[0], acc_refs[0]), 0)
+    lax.fori_loop(info_ref[1], info_ref[2], functools.partial(add_pairs, out_refs[1], acc_refs[1]), 0)
+
+
+def spmm(plan, pieces, tiles, acc, n_row):
     nodes, width = pieces[0][0].shape
     half = n_row // 2 * nodes
-    out = jax.ShapeDtypeStruct((half + SIDE, width), jnp.bfloat16)
-    n_refs = sum(len(p) for p in pieces)
+    last = acc is not None
+    out = jax.ShapeDtypeStruct((half + 2 * SIDE, width), jnp.bfloat16 if last else jnp.float32)
+    operands = [ref for p in pieces for ref in p] + [tiles] + list(acc or [])
     return pl.pallas_call(
-        functools.partial(spmm_kernel, [len(p) for p in pieces]),
+        functools.partial(spmm_kernel, [len(p) for p in pieces], last),
         out_shape=(out, out),
         grid_spec=pltpu.PrefetchScalarGridSpec(
             num_scalar_prefetch=5,
             grid=(),
-            in_specs=[pl.BlockSpec(memory_space=pltpu.VMEM)] * (n_refs + 1),
+            in_specs=[pl.BlockSpec(memory_space=pltpu.VMEM)] * len(operands),
             out_specs=[pl.BlockSpec(memory_space=pltpu.VMEM)] * 2,
             scratch_shapes=[
                 pltpu.VMEM((len(pieces) * nodes, width), jnp.bfloat16),
@@ -125,8 +137,8 @@
         ),
         compiler_params=pltpu.CompilerParams(vmem_limit_bytes=SPMM_BYTES),
         cost_estimate=pl.CostEstimate(flops=0, bytes_accessed=4096, transcendentals=0),
-        name="spmm",
-    )(*plan, *[ref for p in pieces for ref in p], tiles)
+        name="spmm_last" if last else "spmm_first",
+    )(*plan, *operands)
 
 
 def xor_permute(value, axis, mask):
@@ -169,7 +181,7 @@
     return a.astype(jnp.float32) + b.astype(jnp.float32)
 
 
-def plan_slots(tile_rows, tile_cols, count, row, col, mid, n_row, per_dev):
+def plan_slots(tile_rows, tile_cols, count, row, col, mid, n_row, per_dev, last):
     slots = tile_rows.shape[0]
     half, quarter = n_row // 2, n_row // 4
     row_pos = ((tile_rows // per_dev) ^ col) * per_dev + tile_rows % per_dev
@@ -184,7 +196,10 @@
     kept = 1 - (away & 1)
     n_out = half * per_dev
     ids = jnp.arange(slots, dtype=jnp.int32)
-    live = ids < count
+    start = FIRST_PIECES * per_dev
+    live = (ids < count) & ((row_pos >= start) == last)
+    if last:
+        row_pos = row_pos - start
     key = jnp.where(live, kept * n_out + out_pos, 2 * n_out)
     equal = key[None, :] == key[:, None]
     below = key[None, :] < key[:, None]
@@ -214,7 +229,7 @@
 
 
 def core_sums(keep, recv):
-    size = (keep.shape[0] - SIDE) // 4
+    size = (keep.shape[0] - 2 * SIDE) // 4
     return [add_f32(keep[g * size : (g + 1) * size], recv[g * size : (g + 1) * size]).astype(jnp.bfloat16) for g in range(4)]
 
 
@@ -233,28 +248,53 @@
     return xor_permute(sums[0], "row", bits[0]), xor_permute(sums[2], "row", bits[-1])
 
 
-def exchange_rest(sums, recv, bits, rows):
+def exchange_second(sums, recv, bits, rows):
+    sent, kept = [], []
+    for upper in (0, 1):
+        value = add_f32(sums[2 * upper + 1], recv[upper]).astype(jnp.bfloat16)
+        sent_u, kept_u = halve(value, upper, rows)
+        sent.append(sent_u)
+        kept.append(kept_u)
+    return kept, sent
+
+
+def exchange_last(kept, recv, bits, rows):
     done = []
     for upper in (0, 1):
-        value = add_f32(sums[2 * upper + 1], recv[upper])
-        for bit in (bits[::-1] if upper else bits)[1:]:
-            sent, kept = halve(value.astype(jnp.bfloat16), upper, rows)
-            value = add_f32(kept, xor_permute(sent, "row", bit))
+        value = add_f32(kept[upper], recv[upper])
+        for bit in (bits[::-1] if upper else bits)[2:]:
+            sent_u, kept_u = halve(value.astype(jnp.bfloat16), upper, rows)
+            value = add_f32(kept_u, xor_permute(sent_u, "row", bit))
         done.append(value.astype(jnp.bfloat16))
     return jnp.concatenate(done, axis=0)
 
 
-def weight_term(features_groups, sums):
-    terms = [
-        lax.dot_general(f, s, (((0,), (0,)), ((), ())), preferred_element_type=jnp.float32)
-        for f, s in zip(features_groups, sums)
-    ]
-    return tree_sum(terms)
+def exchange_rest(sums, recv, bits, rows):
+    kept, sent = exchange_second(sums, recv, bits, rows)
+    recv = [xor_permute(s, "row", bit) for s, bit in zip(sent, (bits[1], bits[-2]))]
+    return exchange_last(kept, recv, bits, rows)
+
+
+def weight_term(features_groups, sums0, sums1):
+    halves = []
+    for sums in (sums0, sums1):
+        terms = [
+            lax.dot_general(f, s, (((0,), (0,)), ((), ())), preferred_element_type=jnp.float32)
+            for f, s in zip(features_groups, sums)
+        ]
+        halves.append(tree_sum(terms).astype(jnp.bfloat16))
+    return jnp.concatenate(halves, axis=1)
 
 
 def sum_over(term, axis, masks):
     parts = [term] + [xor_permute(term, axis, m) for m in masks]
     return tree_sum([p.astype(jnp.float32) for p in parts])
+
+
+def grow(stack, bits):
+    for bit in bits:
+        stack = jnp.concatenate([stack, xor_permute(stack, "row", bit)], axis=0)
+    return stack
 
 
 def body(grad_out, preact, features, weight, tiles, tile_rows, tile_cols, live_counts):
@@ -273,57 +313,65 @@
         for cut in (slice(0, cw), slice(cw, width))
     ]
     first0 = gather_first(own0)
-    plan = plan_slots(tile_rows.reshape(slots), tile_cols.reshape(slots), count, row, col, mid, n_row, nodes // SIDE)
     flipped = flip_tiles(tiles.reshape(slots, SIDE, SIDE))
-    features, flipped = fence(features, flipped)
-    near = [features]
-    for bit in bits[:2]:
-        near.append(xor_permute(features, "row", bit))
-    own0, own1, first0, flipped, plan = fence(own0, own1, first0, flipped, plan)
+    count = count + flipped[slots, 0, 0].astype(jnp.int32)
+    kept_near = [grow(features[:rows], bits[1:]), grow(features[rows:], bits[:-1])]
+    plans = [
+        plan_slots(tile_rows.reshape(slots), tile_cols.reshape(slots), count, row, col, mid, n_row, nodes // SIDE, last)
+        for last in (False, True)
+    ]
+    sent_near = [xor_permute(stack, "row", bit) for stack, bit in zip(kept_near, (bits[0], bits[-1]))]
+    own0, own1, first0, plans, kept_near = fence(own0, own1, first0, plans, kept_near)
 
     second0 = gather_second(own0, first0[1], n_col)
     pieces0 = as_pieces(own0, first0, second0, mid, n_col)
-    pieces0, own1, near = fence(pieces0, own1, near)
+    features_groups = [sent_near[0], kept_near[0], sent_near[1], kept_near[1]]
+    pieces0, own1, features_groups = fence(pieces0, own1, features_groups)
+    core, in_half = row & 1, features.shape[1] // 2
+    features_theirs = [lax.dynamic_slice_in_dim(f, (1 - core) * in_half, in_half, 1) for f in features_groups]
+    features_mine = [lax.dynamic_slice_in_dim(f, core * in_half, in_half, 1) for f in features_groups]
 
     first1 = gather_first(own1)
-    near.append(xor_permute(near[1], "row", bits[1]))
-    for bit in bits[2:]:
-        near += [xor_permute(f, "row", bit) for f in near]
-    send0, keep0 = spmm(plan, pieces0, flipped, n_row)
-    own1, first1, near, send0, keep0 = fence(own1, first1, near, send0, keep0)
+    acc0 = spmm(plans[0], pieces0[:FIRST_PIECES], flipped, None, n_row)
+    send0, keep0 = spmm(plans[1], pieces0[FIRST_PIECES:], flipped, acc0, n_row)
+    own1, first1, send0, keep0, features_theirs, features_mine = fence(
+        own1, first1, send0, keep0, features_theirs, features_mine
+    )
 
     second1 = gather_second(own1, first1[1], n_col)
     pieces1 = as_pieces(own1, first1, second1, mid, n_col)
     sums0 = core_sums(keep0, xor_permute(send0, "row", 1))
-    features_groups = []
-    for upper in (0, 1):
-        own_bit = (n_row // 4) if upper else 1
-        for want in (1, 0):
-            parts = [f[upper * rows : (upper + 1) * rows] for q, f in enumerate(near) if (q & own_bit != 0) == want]
-            features_groups.append(jnp.concatenate(parts, axis=0))
-    pieces1, sums0, features_groups = fence(pieces1, sums0, features_groups)
-
     recv0 = exchange_first(sums0, bits)
-    send1, keep1 = spmm(plan, pieces1, flipped, n_row)
-    recv0, send1, keep1 = fence(recv0, send1, keep1)
-
-    colgrad0 = exchange_rest(sums0, recv0, bits, rows)
+    acc1 = spmm(plans[0], pieces1[:FIRST_PIECES], flipped, None, n_row)
+    pieces1, sums0, acc1 = fence(pieces1, sums0, acc1)
+
+    send1, keep1 = spmm(plans[1], pieces1[FIRST_PIECES:], flipped, acc1, n_row)
+    send1, keep1, recv0, sums0 = fence(send1, keep1, recv0, sums0)
+
     sums1 = core_sums(keep1, xor_permute(send1, "row", 1))
-    colgrad0, sums1 = fence(colgrad0, sums1)
-    term1 = weight_term(features_groups, sums1).astype(jnp.bfloat16)
-    term0 = weight_term(features_groups, sums0).astype(jnp.bfloat16)
-    term = jnp.concatenate([term0, term1], axis=1)
-    sums1, term = fence(sums1, term)
+    theirs = weight_term(features_theirs, sums0, sums1)
+    rest0, sent0 = exchange_second(sums0, recv0, bits, rows)
+    recv0 = [xor_permute(sent, "row", bit) for sent, bit in zip(sent0, (bits[1], bits[-2]))]
+    sums1, theirs = fence(sums1, theirs)
+    sums1, theirs, rest0, recv0 = fence(sums1, theirs, rest0, recv0)
 
     recv1 = exchange_first(sums1, bits)
-    term = sum_over(term, "col", range(1, n_col)).astype(jnp.bfloat16)
-    recv1, term = fence(recv1, term)
-
-    colgrad1 = exchange_rest(sums1, recv1, bits, rows)
-    term = sum_over(term, "row", range(2, n_row, 2)).astype(jnp.bfloat16)
-    colgrad1, term = fence(colgrad1, term)
-
-    grad_weight = sum_over(term, "row", [1])
+    mine = weight_term(features_mine, sums0, sums1)
+    mine = add_f32(mine, xor_permute(theirs, "row", 1)).astype(jnp.bfloat16)
+    mine = sum_over(mine, "col", range(1, n_col)).astype(jnp.bfloat16)
+    recv1, mine = fence(recv1, mine)
+
+    rest1, sent1 = exchange_second(sums1, recv1, bits, rows)
+    rest1, sent1, mine = fence(rest1, sent1, mine)
+    recv1 = [xor_permute(sent, "row", bit) for sent, bit in zip(sent1, (bits[1], bits[-2]))]
+    mine = sum_over(mine, "row", range(2, n_row, 2)).astype(jnp.bfloat16)
+    colgrad0 = exchange_last(rest0, recv0, bits, rows)
+    colgrad1 = exchange_last(rest1, recv1, bits, rows)
+    colgrad1, mine = fence(colgrad1, mine)
+
+    theirs = xor_permute(mine, "row", 1)
+    low, high = jnp.where(core == 0, mine, theirs), jnp.where(core == 0, theirs, mine)
+    grad_weight = jnp.concatenate([low, high], axis=0).astype(jnp.float32)
     colgrad = jnp.concatenate([colgrad0, colgrad1], axis=1)
     grad_features = lax.dot_general(
         colgrad, weight, (((1,), (1,)), ((), ())), preferred_element_type=jnp.float32

time: 149 us -> 158 us (1.060)
  waiting for transfers between devices: 61.8 us -> 32.9 us
  local copies, waits for them, and re-layouts: 16 us -> 28.8 us
  other arithmetic: 5.89 us -> 14.7 us
  matrix products: 4.31 us -> 11.2 us
  between operations: 4.2 us -> 8.01 us
  starting transfers between devices: 29.9 us -> 32.3 us
  Pallas kernels: 26.7 us -> 28.9 us
    ppermute x24 -> x26, waiting for transfers between devices: 39.1 us -> 21.9 us  [xor_permute(): return lax.ppermute(value, axis, [(i, i ^ mask) for i in range(size)])]
    ppermute x2, waiting for transfers between devices: 22.7 us -> 11 us  [gather_second(): lax.ppermute(by_two, 'col', ends)]
    dynamic_slice x0 -> x4, local copies, waits for them, and re-layouts: none -> 9.11 us  [body(): lax.dynamic_slice_in_dim(f, core * in_half, in_half, 1)]
    dot_general x8 -> x16, matrix products: 2.83 us -> 9.74 us  [weight_term(): lax.dot_general(f, s, (((0,), (0,)), ((), ())), preferred_element_type=jn...]
    unnamed x21 -> x43, local copies, waits for them, and re-layouts: 12.8 us -> 18.5 us
    concatenate x7 -> x4, other arithmetic: 0.36 us -> 4.23 us  [the longest x2 4.19 us: grow(): stack = jnp.concatenate([stack, xor_permute(stack, 'row', bit)], axis=0)]
    ppermute x24 -> x26, starting transfers between devices: 25.9 us -> 28.3 us  [xor_permute(): return lax.ppermute(value, axis, [(i, i ^ mask) for i in range(size)])]
    slice x4 -> x2, local copies, waits for them, and re-layouts: 2.84 us -> 0.58 us  [the longest x1 0.51 us: body(): count = count + flipped[slots, 0, 0].astype(jnp.int32)]
  transfers between devices with their start and end apart: 28 -> 30, of which waited for: 12 -> 8; matrix products, arithmetic and copies ran while one was open for 6% -> 22% of each run, Pallas kernels for 18% -> 18%
where the time goes in v4:
time: 158 us; the launch traced here: 157 us
  waiting for transfers between devices  32.9 us (21%)
  starting transfers between devices  32.3 us (20%)
  Pallas kernels  28.9 us (18%)
  local copies, waits for them, and re-layouts  28.8 us (18%)
  other arithmetic  14.7 us (9%)
  matrix products  11.2 us (7%)
  between operations  8.01 us (5%)
    ppermute x26, starting transfers between devices, xor_permute(): return lax.ppermute(value, axis, [(i, i ^ mask) for i in range(size)])  28.3 us
    ppermute x26, waiting for transfers between devices, xor_permute(): return lax.ppermute(value, axis, [(i, i ^ mask) for i in range(size)])  21.9 us
    pallas_call x4, Pallas kernels, spmm(): pl.pallas_call(functools.partial(spmm_kernel, [len(p) for p in pieces], l...  21 us
    unnamed x43, local copies, waits for them, and re-layouts  18.5 us
    ppermute x2, waiting for transfers between devices, gather_second(): lax.ppermute(by_two, 'col', ends)  11 us
    dot_general x16, matrix products, weight_term(): lax.dot_general(f, s, (((0,), (0,)), ((), ())), preferred_element_type=jn...  9.74 us
    dynamic_slice x4, local copies, waits for them, and re-layouts, body(): lax.dynamic_slice_in_dim(f, core * in_half, in_half, 1)  9.11 us
    pallas_call x1, Pallas kernels, flip_tiles(): pl.pallas_call(flip_kernel, out_shape=jax.ShapeDtypeStruct((slots + 1, SI...  7.84 us
  transfers between devices with their start and end apart: 30, of which 8 were waited for; matrix products, arithmetic and copies ran while one was open for 22% of the time, Pallas kernels for 18%

profile of v4, /device:TPU:1, one launch (start us, length us, event | category | flops | bytes accessed | tf_op | source)
XLA Modules:
  0.0 156.7 jit_solution(1397791254200616149)
XLA Ops:
  0.7 1.7 %compare_select_fusion = (bf16[2048,128]{1,0:T(8,128)(2,1)S(1)}, bf16[2048,128]{1,0:T(8,128)(2,1)S(1)}) fusion(bf16[2048,256]{1,0:T(8,128)(2,1)} %param.8, bf16[2048,256]{1,0:T(8,128)(2,1)} %param.9), kind=kLoop, calls=%fused_computation.36 | loop fusion | flops 1048576 | bytes 3145728 | tf_op jit(solution)/shard_map/jit(_where)/select_n | solution.py:312
  2.4 2.2 %collective-permute-start = (bf16[2048,128]{1,0:T(8,128)(2,1)S(1)}, bf16[2048,128]{1,0:T(8,128)(2,1)S(1)}, u32[]{:S(2)}, u32[]{:S(2)}) collective-permute-start(bf16[2048,128]{1,0:T(8,128)(2,1)S(1)} %get-tuple-element.108.refs_0_), channel_id=1, source_target_pairs={{0,1},{1,0},{2,3},{3,2},{4,5},{5,4},{6,7},{7,6},{8,9},{9,8},{10,11... | collective-permute-start | bytes 1572872 | tf_op jit(solution)/shard_map/ppermute | solution.py:146
  4.6 2.3 %collective-permute-start.1 = (bf16[2048,128]{1,0:T(8,128)(2,1)S(1)}, bf16[2048,128]{1,0:T(8,128)(2,1)S(1)}, u32[]{:S(2)}, u32[]{:S(2)}) collective-permute-start(bf16[2048,128]{1,0:T(8,128)(2,1)S(1)} %get-tuple-element.108.refs_0_), channel_id=1, source_target_pairs={{0,2},{1,3},{2,0},{3,1},{4,6},{5,7},{6,4},{7,5},{8,10},{9,11},{10,... | collective-permute-start | bytes 1572872 | tf_op jit(solution)/shard_map/ppermute | solution.py:146
  10.1 4.0 %copy-done.4 = bf16[1,1,320,128,128]{4,3,2,1,0:T(8,128)(2,1)S(1)} copy-done((bf16[1,1,320,128,128]{4,3,2,1,0:T(8,128)(2,1)S(1)}, bf16[1,1,320,128,128]{4,3,2,1,0:T(8,128)(2,1)}, u32[]{:S(2)}) %copy-start.4) | copy-done | bytes 10485784
  14.1 7.8 %flip_tiles.1.refs_3_.refs_2_ = bf16[321,128,128]{2,1,0:T(8,128)(2,1)S(1)} custom-call(bf16[320,128,128]{2,1,0:T(8,128)(2,1)S(1)} %bitcast.53), custom_call_target="tpu_custom_call" | custom-call | bytes 4096 | tf_op jit(solution)/shard_map/flip_tiles/pallas_call | solution.py:44
  22.5 4.0 %copy-done.1 = bf16[321,128,128]{2,1,0:T(8,128)(2,1)} copy-done((bf16[321,128,128]{2,1,0:T(8,128)(2,1)}, bf16[321,128,128]{2,1,0:T(8,128)(2,1)S(1)}, u32[]{:S(2)}) %copy-start.1) | copy-done | bytes 10518552
  36.4 2.1 %pad_maximum_fusion = bf16[2048,256]{1,0:T(8,128)(2,1)} fusion(bf16[1024,256]{1,0:T(8,128)(2,1)} %collective-permute-done.2, bf16[1024,256]{1,0:T(8,128)(2,1)S(1)} %get-tuple-element.222), kind=kLoop, calls=%fused_computation.17 | loop fusion | flops 2097152 | bytes 2097152 | tf_op jit(solution)/shard_map/concatenate | solution.py:296
  38.8 2.1 %pad_maximum_fusion.1 = bf16[2048,256]{1,0:T(8,128)(2,1)} fusion(bf16[1024,256]{1,0:T(8,128)(2,1)} %collective-permute-done.3, bf16[1024,256]{1,0:T(8,128)(2,1)S(1)} %get-tuple-element.221), kind=kLoop, calls=%fused_computation.18 | loop fusion | flops 2097152 | bytes 2097152 | tf_op jit(solution)/shard_map/concatenate | solution.py:296
  44.0 11.0 %collective-permute-done.5.refs_1_ = bf16[2048,128]{1,0:T(8,128)(2,1)S(1)} collective-permute-done((bf16[2048,128]{1,0:T(8,128)(2,1)S(1)}, bf16[2048,128]{1,0:T(8,128)(2,1)S(1)}, u32[]{:S(2)}, u32[]{:S(2)}) %collective-permute-start.5) | collective-permute-done | bytes 524320 | tf_op jit(solution)/shard_map/ppermute | solution.py:164
  55.8 5.9 %collective-permute-done.6 = bf16[2048,256]{1,0:T(8,128)(2,1)} collective-permute-done((bf16[2048,256]{1,0:T(8,128)(2,1)}, bf16[2048,256]{1,0:T(8,128)(2,1)}, u32[]{:S(2)}, u32[]{:S(2)}) %collective-permute-start.6) | collective-permute-done | bytes 1048608 | tf_op jit(solution)/shard_map/ppermute | solution.py:146
  61.7 2.1 %collective-permute-done.7 = bf16[2048,256]{1,0:T(8,128)(2,1)} collective-permute-done((bf16[2048,256]{1,0:T(8,128)(2,1)}, bf16[2048,256]{1,0:T(8,128)(2,1)}, u32[]{:S(2)}, u32[]{:S(2)}) %collective-permute-start.7) | collective-permute-done | bytes 1048608 | tf_op jit(solution)/shard_map/ppermute | solution.py:146
  64.0 2.3 %constant_dynamic-slice_fusion.3 = (bf16[2048,128]{1,0:T(8,128)(2,1)}, bf16[2048,128]{1,0:T(8,128)(2,1)}) fusion(bf16[2048,256]{1,0:T(8,128)(2,1)} %collective-permute-done.6, s32[]{:T(128)S(6)} %select_n.437, s32[]{:T(128)S(6)} %select_n.436), kind=kLoop, calls=%fused_computation.132 | loop fusion | bytes 2097160 | tf_op jit(solution)/shard_map/dynamic_slice | solution.py:332
  66.2 2.3 %constant_dynamic-slice_fusion.2 = (bf16[2048,128]{1,0:T(8,128)(2,1)}, bf16[2048,128]{1,0:T(8,128)(2,1)}) fusion(bf16[2048,256]{1,0:T(8,128)(2,1)} %pad_maximum_fusion, s32[]{:T(128)S(6)} %select_n.437, s32[]{:T(128)S(6)} %select_n.436), kind=kLoop, calls=%fused_computation.131 | loop fusion | bytes 2097160 | tf_op jit(solution)/shard_map/dynamic_slice | solution.py:332
  68.6 4.0 %copy-done.2 = bf16[321,128,128]{2,1,0:T(8,128)(2,1)S(1)} copy-done((bf16[321,128,128]{2,1,0:T(8,128)(2,1)S(1)}, bf16[321,128,128]{2,1,0:T(8,128)(2,1)}, u32[]{:S(2)}) %copy-start.2) | copy-done | bytes 10518552
  72.5 6.8 %spmm_first.2 = (f32[8448,128]{1,0:T(8,128)S(1)}, f32[8448,128]{1,0:T(8,128)S(1)}) custom-call(s32[480]{0:T(512)S(1)} %broadcast_add_fusion.5.tile_at_ref, s32[480]{0:T(512)S(1)} %get-tuple-element.104.block_at_ref, s32[240]{0:T(256)S(1)} %slice.120.out_at_ref, s32[240]{0:T(256)S(1)} %fusion.36.same_ref, s32[3]{0:T(128)S(1)} %get-tuple-element.107.info_ref, ...), custom_call_target="tpu_custom_call" | custom-call | bytes 4096 | tf_op jit(solution)/shard_map/spmm_first/pallas_call | solution.py:125
  79.3 3.7 %spmm_last.2 = (bf16[8448,128]{1,0:T(8,128)(2,1)S(1)}, bf16[8448,128]{1,0:T(8,128)(2,1)S(1)}) custom-call(s32[480]{0:T(512)S(1)} %broadcast_add_fusion.4.tile_at_ref, s32[480]{0:T(512)S(1)} %get-tuple-element.90.block_at_ref, s32[240]{0:T(256)S(1)} %slice.123.out_at_ref, s32[240]{0:T(256)S(1)} %fusion.37.same_ref, s32[3]{0:T(128)S(1)} %get-tuple-element.93.info_ref, ...), custom_call_target="tpu_custom_call" | custom-call | bytes 4096 | tf_op jit(solution)/shard_map/spmm_last/pallas_call | solution.py:125
  83.0 2.3 %constant_dynamic-slice_fusion.1 = (bf16[2048,128]{1,0:T(8,128)(2,1)}, bf16[2048,128]{1,0:T(8,128)(2,1)}) fusion(bf16[2048,256]{1,0:T(8,128)(2,1)} %collective-permute-done.7, s32[]{:T(128)S(6)} %select_n.437, s32[]{:T(128)S(6)} %select_n.436), kind=kLoop, calls=%fused_computation.130 | loop fusion | bytes 2097160 | tf_op jit(solution)/shard_map/dynamic_slice | solution.py:332
  85.3 2.3 %constant_dynamic-slice_fusion = (bf16[2048,128]{1,0:T(8,128)(2,1)}, bf16[2048,128]{1,0:T(8,128)(2,1)}) fusion(bf16[2048,256]{1,0:T(8,128)(2,1)} %pad_maximum_fusion.1, s32[]{:T(128)S(6)} %select_n.437, s32[]{:T(128)S(6)} %select_n.436), kind=kLoop, calls=%fused_computation.129 | loop fusion | bytes 2097160 | tf_op jit(solution)/shard_map/dynamic_slice | solution.py:332
  87.6 2.9 %collective-permute-start.12 = (bf16[8448,128]{1,0:T(8,128)(2,1)S(1)}, bf16[8448,128]{1,0:T(8,128)(2,1)S(1)}, u32[]{:S(2)}, u32[]{:S(2)}) collective-permute-start(bf16[8448,128]{1,0:T(8,128)(2,1)S(1)} %get-tuple-element.123), channel_id=1, source_target_pairs={{0,4},{4,0},{8,12},{12,8},{16,20},{20,16},{24,28},{28,24},{1,5},{5... | collective-permute-start | bytes 6488072 | tf_op jit(solution)/shard_map/ppermute | solution.py:146
  92.4 1.9 %collective-permute-done.12 = bf16[8448,128]{1,0:T(8,128)(2,1)S(1)} collective-permute-done((bf16[8448,128]{1,0:T(8,128)(2,1)S(1)}, bf16[8448,128]{1,0:T(8,128)(2,1)S(1)}, u32[]{:S(2)}, u32[]{:S(2)}) %collective-permute-start.12) | collective-permute-done | bytes 2162720 | tf_op jit(solution)/shard_map/ppermute | solution.py:146
  94.3 1.5 add_convert_fusion.8
  97.3 4.0 %copy-done.3 = bf16[321,128,128]{2,1,0:T(8,128)(2,1)S(1)} copy-done((bf16[321,128,128]{2,1,0:T(8,128)(2,1)S(1)}, bf16[321,128,128]{2,1,0:T(8,128)(2,1)}, u32[]{:S(2)}) %copy-start.3) | copy-done | bytes 10518552
  101.3 6.7 %spmm_first.3 = (f32[8448,128]{1,0:T(8,128)S(1)}, f32[8448,128]{1,0:T(8,128)S(1)}) custom-call(s32[480]{0:T(512)S(1)} %broadcast_add_fusion.5.tile_at_ref, s32[480]{0:T(512)S(1)} %get-tuple-element.104.block_at_ref, s32[240]{0:T(256)S(1)} %slice.120.out_at_ref, s32[240]{0:T(256)S(1)} %fusion.36.same_ref, s32[3]{0:T(128)S(1)} %get-tuple-element.107.info_ref, ...), custom_call_target="tpu_custom_call" | custom-call | bytes 4096 | tf_op jit(solution)/shard_map/spmm_first/pallas_call | solution.py:125
  108.1 3.9 %spmm_last.3 = (bf16[8448,128]{1,0:T(8,128)(2,1)S(1)}, bf16[8448,128]{1,0:T(8,128)(2,1)S(1)}) custom-call(s32[480]{0:T(512)S(1)} %broadcast_add_fusion.4.tile_at_ref, s32[480]{0:T(512)S(1)} %get-tuple-element.90.block_at_ref, s32[240]{0:T(256)S(1)} %slice.123.out_at_ref, s32[240]{0:T(256)S(1)} %fusion.37.same_ref, s32[3]{0:T(128)S(1)} %get-tuple-element.93.info_ref, ...), custom_call_target="tpu_custom_call" | custom-call | bytes 4096 | tf_op jit(solution)/shard_map/spmm_last/pallas_call | solution.py:125
  114.8 3.0 %collective-permute-start.17 = (bf16[1024,128]{1,0:T(8,128)(2,1)S(1)}, bf16[1024,128]{1,0:T(8,128)(2,1)S(1)}, u32[]{:S(2)}, u32[]{:S(2)}) collective-permute-start(bf16[1024,128]{1,0:T(8,128)(2,1)S(1)} %get-tuple-element.227), channel_id=1, source_target_pairs={{0,8},{4,12},{8,0},{12,4},{16,24},{20,28},{24,16},{28,20},{1,9},{5... | collective-permute-start | bytes 786440 | tf_op jit(solution)/shard_map/ppermute | solution.py:146
  130.8 1.8 %collective-permute-start.23 = (bf16[128,256]{0,1:T(8,128)(2,1)S(1)}, bf16[128,256]{0,1:T(8,128)(2,1)S(1)}, u32[]{:S(2)}, u32[]{:S(2)}) collective-permute-start(bf16[128,256]{0,1:T(8,128)(2,1)S(1)} %add_convert_fusion.18), channel_id=1, source_target_pairs={{0,3},{1,2},{2,1},{3,0},{4,7},{5,6},{6,5},{7,4},{8,11},{9,10},{10,... | collective-permute-start | bytes 196616 | tf_op jit(solution)/shard_map/ppermute | solution.py:146
  134.5 1.9 %collective-permute-done.23 = bf16[128,256]{0,1:T(8,128)(2,1)S(1)} collective-permute-done((bf16[128,256]{0,1:T(8,128)(2,1)S(1)}, bf16[128,256]{0,1:T(8,128)(2,1)S(1)}, u32[]{:S(2)}, u32[]{:S(2)}) %collective-permute-start.23) | collective-permute-done | bytes 65568 | tf_op jit(solution)/shard_map/ppermute | solution.py:146
  136.4 4.0 %collective-permute-done.22 = bf16[128,256]{0,1:T(8,128)(2,1)S(1)} collective-permute-done((bf16[128,256]{0,1:T(8,128)(2,1)S(1)}, bf16[128,256]{0,1:T(8,128)(2,1)S(1)}, u32[]{:S(2)}, u32[]{:S(2)}) %collective-permute-start.22) | collective-permute-done | bytes 65568 | tf_op jit(solution)/shard_map/ppermute | solution.py:146
  140.9 1.8 %collective-permute-start.28 = (bf16[128,256]{0,1:T(8,128)(2,1)S(1)}, bf16[128,256]{0,1:T(8,128)(2,1)S(1)}, u32[]{:S(2)}, u32[]{:S(2)}) collective-permute-start(bf16[128,256]{0,1:T(8,128)(2,1)S(1)} %add_convert_fusion.17), channel_id=1, source_target_pairs={{0,24},{4,28},{8,16},{12,20},{16,8},{20,12},{24,0},{28,4},{1,25},{... | collective-permute-start | bytes 196616 | tf_op jit(solution)/shard_map/ppermute | solution.py:146
  146.7 5.1 %collective-permute-done.25 = bf16[1024,128]{1,0:T(8,128)(2,1)S(1)} collective-permute-done((bf16[1024,128]{1,0:T(8,128)(2,1)S(1)}, bf16[1024,128]{1,0:T(8,128)(2,1)S(1)}, u32[]{:S(2)}, u32[]{:S(2)}) %collective-permute-start.25) | collective-permute-done | bytes 262176 | tf_op jit(solution)/shard_map/ppermute | solution.py:146
  152.0 2.3 %collective-permute-start.29 = (bf16[128,256]{0,1:T(8,128)(2,1)S(1)}, bf16[128,256]{0,1:T(8,128)(2,1)S(1)}, u32[]{:S(2)}, u32[]{:S(2)}) collective-permute-start(bf16[128,256]{0,1:T(8,128)(2,1)S(1)} %add_convert_fusion.16), channel_id=1, source_target_pairs={{0,4},{4,0},{8,12},{12,8},{16,20},{20,16},{24,28},{28,24},{1,5},{5... | collective-permute-start | bytes 196616 | tf_op jit(solution)/shard_map/ppermute | solution.py:146
  154.3 1.4 convolution_convert_fusion
  (147 shorter events, 37.7 us)
Async XLA Ops:
  0.6 153.7 %copy-start = (bf16[256,256]{1,0:T(8,128)(2,1)S(1)}, bf16[256,256]{1,0:T(8,128)(2,1)}, u32[]{:S(2)}) copy-start(bf16[256,256]{1,0:T(8,128)(2,1)} %param.11) | copy-start | bytes 393220
  2.4 38.8 %collective-permute-start = (bf16[2048,128]{1,0:T(8,128)(2,1)S(1)}, bf16[2048,128]{1,0:T(8,128)(2,1)S(1)}, u32[]{:S(2)}, u32[]{:S(2)}) collective-permute-start(bf16[2048,128]{1,0:T(8,128)(2,1)S(1)} %get-tuple-element.108.refs_0_), channel_id=1, source_target_pairs={{0,1},{1,0},{2,3},{3,2},{4,5},{5,4},{6,7},{7,6},{8,9},{9,8},{10,11... | collective-permute-start | bytes 1572872 | tf_op jit(solution)/shard_map/ppermute | solution.py:146
  4.6 36.6 %collective-permute-start.1 = (bf16[2048,128]{1,0:T(8,128)(2,1)S(1)}, bf16[2048,128]{1,0:T(8,128)(2,1)S(1)}, u32[]{:S(2)}, u32[]{:S(2)}) collective-permute-start(bf16[2048,128]{1,0:T(8,128)(2,1)S(1)} %get-tuple-element.108.refs_0_), channel_id=1, source_target_pairs={{0,2},{1,3},{2,0},{3,1},{4,6},{5,7},{6,4},{7,5},{8,10},{9,11},{10,... | collective-permute-start | bytes 1572872 | tf_op jit(solution)/shard_map/ppermute | solution.py:146
  7.0 29.5 %collective-permute-start.2 = (bf16[1024,256]{1,0:T(8,128)(2,1)S(1)}, bf16[1024,256]{1,0:T(8,128)(2,1)}, u32[]{:S(2)}, u32[]{:S(2)}) collective-permute-start(bf16[1024,256]{1,0:T(8,128)(2,1)S(1)} %get-tuple-element.222), channel_id=1, source_target_pairs={{0,16},{4,20},{8,24},{12,28},{16,0},{20,4},{24,8},{28,12},{1,17},{... | collective-permute-start | bytes 1572872 | tf_op jit(solution)/shard_map/ppermute | solution.py:146
  8.3 30.5 %collective-permute-start.3 = (bf16[1024,256]{1,0:T(8,128)(2,1)S(1)}, bf16[1024,256]{1,0:T(8,128)(2,1)}, u32[]{:S(2)}, u32[]{:S(2)}) collective-permute-start(bf16[1024,256]{1,0:T(8,128)(2,1)S(1)} %get-tuple-element.221), channel_id=1, source_target_pairs={{0,8},{4,12},{8,0},{12,4},{16,24},{20,28},{24,16},{28,20},{1,9},{5... | collective-permute-start | bytes 1572872 | tf_op jit(solution)/shard_map/ppermute | solution.py:146
  14.1 13.1 %copy-start.20 = (s32[1,1,320]{2,1,0:T(1,128)S(1)}, s32[1,1,320]{2,1,0:T(1,128)}, u32[]{:S(2)}) copy-start(s32[1,1,320]{2,1,0:T(1,128)} %param.14) | copy-start | bytes 3844
  38.5 23.2 %collective-permute-start.6 = (bf16[2048,256]{1,0:T(8,128)(2,1)}, bf16[2048,256]{1,0:T(8,128)(2,1)}, u32[]{:S(2)}, u32[]{:S(2)}) collective-permute-start(bf16[2048,256]{1,0:T(8,128)(2,1)} %pad_maximum_fusion), channel_id=1, source_target_pairs={{0,8},{4,12},{8,0},{12,4},{16,24},{20,28},{24,16},{28,20},{1,9},{5... | collective-permute-start | bytes 3145736 | tf_op jit(solution)/shard_map/ppermute | solution.py:146
  40.9 22.9 %collective-permute-start.7 = (bf16[2048,256]{1,0:T(8,128)(2,1)}, bf16[2048,256]{1,0:T(8,128)(2,1)}, u32[]{:S(2)}, u32[]{:S(2)}) collective-permute-start(bf16[2048,256]{1,0:T(8,128)(2,1)} %pad_maximum_fusion.1), channel_id=1, source_target_pairs={{0,16},{4,20},{8,24},{12,28},{16,0},{20,4},{24,8},{28,12},{1,17},{... | collective-permute-start | bytes 3145736 | tf_op jit(solution)/shard_map/ppermute | solution.py:146
  41.2 2.0 %collective-permute-start.4 = (bf16[2048,128]{1,0:T(8,128)(2,1)S(1)}, bf16[2048,128]{1,0:T(8,128)(2,1)S(1)}, u32[]{:S(2)}, u32[]{:S(2)}) collective-permute-start(bf16[2048,128]{1,0:T(8,128)(2,1)S(1)} %get-tuple-element.108.refs_0_), channel_id=1, source_target_pairs={{1,2},{2,1},{5,6},{6,5},{9,10},{10,9},{13,14},{14,13},{17,18},{18,... | collective-permute-start | bytes 1572872 | tf_op jit(solution)/shard_map/ppermute | solution.py:164
  41.9 13.1 %collective-permute-start.5 = (bf16[2048,128]{1,0:T(8,128)(2,1)S(1)}, bf16[2048,128]{1,0:T(8,128)(2,1)S(1)}, u32[]{:S(2)}, u32[]{:S(2)}) collective-permute-start(bf16[2048,128]{1,0:T(8,128)(2,1)S(1)} %collective-permute-done.1.refs_2_), channel_id=1, source_target_pairs={{1,0},{2,3},{5,4},{6,7},{9,8},{10,11},{13,12},{14,15},{17,16},{18,... | collective-permute-start | bytes 1572872 | tf_op jit(solution)/shard_map/ppermute | solution.py:164
  63.8 23.8 %collective-permute-start.8 = (bf16[2048,128]{1,0:T(8,128)(2,1)S(1)}, bf16[2048,128]{1,0:T(8,128)(2,1)S(1)}, u32[]{:S(2)}, u32[]{:S(2)}) collective-permute-start(bf16[2048,128]{1,0:T(8,128)(2,1)S(1)} %get-tuple-element.119.refs_0_), channel_id=1, source_target_pairs={{0,1},{1,0},{2,3},{3,2},{4,5},{5,4},{6,7},{7,6},{8,9},{9,8},{10,11... | collective-permute-start | bytes 1572872 | tf_op jit(solution)/shard_map/ppermute | solution.py:146
  63.9 23.6 %collective-permute-start.9 = (bf16[2048,128]{1,0:T(8,128)(2,1)S(1)}, bf16[2048,128]{1,0:T(8,128)(2,1)S(1)}, u32[]{:S(2)}, u32[]{:S(2)}) collective-permute-start(bf16[2048,128]{1,0:T(8,128)(2,1)S(1)} %get-tuple-element.119.refs_0_), channel_id=1, source_target_pairs={{0,2},{1,3},{2,0},{3,1},{4,6},{5,7},{6,4},{7,5},{8,10},{9,11},{10,... | collective-permute-start | bytes 1572872 | tf_op jit(solution)/shard_map/ppermute | solution.py:146
  87.6 6.8 %collective-permute-start.12 = (bf16[8448,128]{1,0:T(8,128)(2,1)S(1)}, bf16[8448,128]{1,0:T(8,128)(2,1)S(1)}, u32[]{:S(2)}, u32[]{:S(2)}) collective-permute-start(bf16[8448,128]{1,0:T(8,128)(2,1)S(1)} %get-tuple-element.123), channel_id=1, source_target_pairs={{0,4},{4,0},{8,12},{12,8},{16,20},{20,16},{24,28},{28,24},{1,5},{5... | collective-permute-start | bytes 6488072 | tf_op jit(solution)/shard_map/ppermute | solution.py:146
  90.5 17.6 %collective-permute-start.10 = (bf16[2048,128]{1,0:T(8,128)(2,1)S(1)}, bf16[2048,128]{1,0:T(8,128)(2,1)S(1)}, u32[]{:S(2)}, u32[]{:S(2)}) collective-permute-start(bf16[2048,128]{1,0:T(8,128)(2,1)S(1)} %get-tuple-element.119.refs_0_), channel_id=1, source_target_pairs={{1,2},{2,1},{5,6},{6,5},{9,10},{10,9},{13,14},{14,13},{17,18},{18,... | collective-permute-start | bytes 1572872 | tf_op jit(solution)/shard_map/ppermute | solution.py:164
  91.1 16.9 %collective-permute-start.11 = (bf16[2048,128]{1,0:T(8,128)(2,1)S(1)}, bf16[2048,128]{1,0:T(8,128)(2,1)S(1)}, u32[]{:S(2)}, u32[]{:S(2)}) collective-permute-start(bf16[2048,128]{1,0:T(8,128)(2,1)S(1)} %collective-permute-done.9.refs_2_), channel_id=1, source_target_pairs={{1,0},{2,3},{5,4},{6,7},{9,8},{10,11},{13,12},{14,15},{17,16},{18,... | collective-permute-start | bytes 1572872 | tf_op jit(solution)/shard_map/ppermute | solution.py:164
  95.9 16.1 %collective-permute-start.13 = (bf16[2048,128]{1,0:T(8,128)(2,1)}, bf16[2048,128]{1,0:T(8,128)(2,1)}, u32[]{:S(2)}, u32[]{:S(2)}) collective-permute-start(bf16[2048,128]{1,0:T(8,128)(2,1)} %get-tuple-element.139), channel_id=1, source_target_pairs={{0,8},{4,12},{8,0},{12,4},{16,24},{20,28},{24,16},{28,20},{1,9},{5... | collective-permute-start | bytes 1572872 | tf_op jit(solution)/shard_map/ppermute | solution.py:146
  97.1 14.9 %collective-permute-start.14 = (bf16[2048,128]{1,0:T(8,128)(2,1)}, bf16[2048,128]{1,0:T(8,128)(2,1)}, u32[]{:S(2)}, u32[]{:S(2)}) collective-permute-start(bf16[2048,128]{1,0:T(8,128)(2,1)} %get-tuple-element.143), channel_id=1, source_target_pairs={{0,16},{4,20},{8,24},{12,28},{16,0},{20,4},{24,8},{28,12},{1,17},{... | collective-permute-start | bytes 1572872 | tf_op jit(solution)/shard_map/ppermute | solution.py:146
  112.0 13.0 %collective-permute-start.15 = (bf16[8448,128]{1,0:T(8,128)(2,1)S(1)}, bf16[8448,128]{1,0:T(8,128)(2,1)S(1)}, u32[]{:S(2)}, u32[]{:S(2)}) collective-permute-start(bf16[8448,128]{1,0:T(8,128)(2,1)S(1)} %get-tuple-element.137), channel_id=1, source_target_pairs={{0,4},{4,0},{8,12},{12,8},{16,20},{20,16},{24,28},{28,24},{1,5},{5... | collective-permute-start | bytes 6488072 | tf_op jit(solution)/shard_map/ppermute | solution.py:146
  113.3 13.6 %collective-permute-start.16 = (bf16[1024,128]{1,0:T(8,128)(2,1)S(1)}, bf16[1024,128]{1,0:T(8,128)(2,1)S(1)}, u32[]{:S(2)}, u32[]{:S(2)}) collective-permute-start(bf16[1024,128]{1,0:T(8,128)(2,1)S(1)} %get-tuple-element.229), channel_id=1, source_target_pairs={{0,16},{4,20},{8,24},{12,28},{16,0},{20,4},{24,8},{28,12},{1,17},{... | collective-permute-start | bytes 786440 | tf_op jit(solution)/shard_map/ppermute | solution.py:146
  114.8 12.1 %collective-permute-start.17 = (bf16[1024,128]{1,0:T(8,128)(2,1)S(1)}, bf16[1024,128]{1,0:T(8,128)(2,1)S(1)}, u32[]{:S(2)}, u32[]{:S(2)}) collective-permute-start(bf16[1024,128]{1,0:T(8,128)(2,1)S(1)} %get-tuple-element.227), channel_id=1, source_target_pairs={{0,8},{4,12},{8,0},{12,4},{16,24},{20,28},{24,16},{28,20},{1,9},{5... | collective-permute-start | bytes 786440 | tf_op jit(solution)/shard_map/ppermute | solution.py:146
  126.9 13.6 %collective-permute-start.18 = (bf16[2048,128]{1,0:T(8,128)(2,1)S(1)}, bf16[2048,128]{1,0:T(8,128)(2,1)S(1)}, u32[]{:S(2)}, u32[]{:S(2)}) collective-permute-start(bf16[2048,128]{1,0:T(8,128)(2,1)S(1)} %get-tuple-element.158), channel_id=1, source_target_pairs={{0,8},{4,12},{8,0},{12,4},{16,24},{20,28},{24,16},{28,20},{1,9},{5... | collective-permute-start | bytes 1572872 | tf_op jit(solution)/shard_map/ppermute | solution.py:146
  127.0 13.5 %collective-permute-start.19 = (bf16[2048,128]{1,0:T(8,128)(2,1)S(1)}, bf16[2048,128]{1,0:T(8,128)(2,1)S(1)}, u32[]{:S(2)}, u32[]{:S(2)}) collective-permute-start(bf16[2048,128]{1,0:T(8,128)(2,1)S(1)} %get-tuple-element.159), channel_id=1, source_target_pairs={{0,16},{4,20},{8,24},{12,28},{16,0},{20,4},{24,8},{28,12},{1,17},{... | collective-permute-start | bytes 1572872 | tf_op jit(solution)/shard_map/ppermute | solution.py:146
  128.4 2.3 %collective-permute-start.20 = (bf16[128,256]{0,1:T(8,128)(2,1)S(1)}, bf16[128,256]{0,1:T(8,128)(2,1)S(1)}, u32[]{:S(2)}, u32[]{:S(2)}) collective-permute-start(bf16[128,256]{0,1:T(8,128)(2,1)S(1)} %pad_maximum_fusion.3), channel_id=1, source_target_pairs={{0,4},{4,0},{8,12},{12,8},{16,20},{20,16},{24,28},{28,24},{1,5},{5... | collective-permute-start | bytes 196616 | tf_op jit(solution)/shard_map/ppermute | solution.py:146
  130.8 5.6 %collective-permute-start.23 = (bf16[128,256]{0,1:T(8,128)(2,1)S(1)}, bf16[128,256]{0,1:T(8,128)(2,1)S(1)}, u32[]{:S(2)}, u32[]{:S(2)}) collective-permute-start(bf16[128,256]{0,1:T(8,128)(2,1)S(1)} %add_convert_fusion.18), channel_id=1, source_target_pairs={{0,3},{1,2},{2,1},{3,0},{4,7},{5,6},{6,5},{7,4},{8,11},{9,10},{10,... | collective-permute-start | bytes 196616 | tf_op jit(solution)/shard_map/ppermute | solution.py:146
  132.6 7.9 %collective-permute-start.22 = (bf16[128,256]{0,1:T(8,128)(2,1)S(1)}, bf16[128,256]{0,1:T(8,128)(2,1)S(1)}, u32[]{:S(2)}, u32[]{:S(2)}) collective-permute-start(bf16[128,256]{0,1:T(8,128)(2,1)S(1)} %add_convert_fusion.18), channel_id=1, source_target_pairs={{0,2},{1,3},{2,0},{3,1},{4,6},{5,7},{6,4},{7,5},{8,10},{9,11},{10,... | collective-permute-start | bytes 196616 | tf_op jit(solution)/shard_map/ppermute | solution.py:146
  133.9 6.5 %collective-permute-start.21 = (bf16[128,256]{0,1:T(8,128)(2,1)S(1)}, bf16[128,256]{0,1:T(8,128)(2,1)S(1)}, u32[]{:S(2)}, u32[]{:S(2)}) collective-permute-start(bf16[128,256]{0,1:T(8,128)(2,1)S(1)} %add_convert_fusion.18), channel_id=1, source_target_pairs={{0,1},{1,0},{2,3},{3,2},{4,5},{5,4},{6,7},{7,6},{8,9},{9,8},{10,11... | collective-permute-start | bytes 196616 | tf_op jit(solution)/shard_map/ppermute | solution.py:146
  140.9 4.9 %collective-permute-start.28 = (bf16[128,256]{0,1:T(8,128)(2,1)S(1)}, bf16[128,256]{0,1:T(8,128)(2,1)S(1)}, u32[]{:S(2)}, u32[]{:S(2)}) collective-permute-start(bf16[128,256]{0,1:T(8,128)(2,1)S(1)} %add_convert_fusion.17), channel_id=1, source_target_pairs={{0,24},{4,28},{8,16},{12,20},{16,8},{20,12},{24,0},{28,4},{1,25},{... | collective-permute-start | bytes 196616 | tf_op jit(solution)/shard_map/ppermute | solution.py:146
  142.7 4.0 %collective-permute-start.27 = (bf16[128,256]{0,1:T(8,128)(2,1)S(1)}, bf16[128,256]{0,1:T(8,128)(2,1)S(1)}, u32[]{:S(2)}, u32[]{:S(2)}) collective-permute-start(bf16[128,256]{0,1:T(8,128)(2,1)S(1)} %add_convert_fusion.17), channel_id=1, source_target_pairs={{0,16},{4,20},{8,24},{12,28},{16,0},{20,4},{24,8},{28,12},{1,17},{... | collective-permute-start | bytes 196616 | tf_op jit(solution)/shard_map/ppermute | solution.py:146
  143.1 3.6 %collective-permute-start.26 = (bf16[128,256]{0,1:T(8,128)(2,1)S(1)}, bf16[128,256]{0,1:T(8,128)(2,1)S(1)}, u32[]{:S(2)}, u32[]{:S(2)}) collective-permute-start(bf16[128,256]{0,1:T(8,128)(2,1)S(1)} %add_convert_fusion.17), channel_id=1, source_target_pairs={{0,8},{4,12},{8,0},{12,4},{16,24},{20,28},{24,16},{28,20},{1,9},{5... | collective-permute-start | bytes 196616 | tf_op jit(solution)/shard_map/ppermute | solution.py:146
  143.6 8.2 %collective-permute-start.25 = (bf16[1024,128]{1,0:T(8,128)(2,1)S(1)}, bf16[1024,128]{1,0:T(8,128)(2,1)S(1)}, u32[]{:S(2)}, u32[]{:S(2)}) collective-permute-start(bf16[1024,128]{1,0:T(8,128)(2,1)S(1)} %get-tuple-element.172), channel_id=1, source_target_pairs={{0,8},{4,12},{8,0},{12,4},{16,24},{20,28},{24,16},{28,20},{1,9},{5... | collective-permute-start | bytes 786440 | tf_op jit(solution)/shard_map/ppermute | solution.py:146
  144.6 7.3 %collective-permute-start.24 = (bf16[1024,128]{1,0:T(8,128)(2,1)S(1)}, bf16[1024,128]{1,0:T(8,128)(2,1)S(1)}, u32[]{:S(2)}, u32[]{:S(2)}) collective-permute-start(bf16[1024,128]{1,0:T(8,128)(2,1)S(1)} %get-tuple-element.170), channel_id=1, source_target_pairs={{0,16},{4,20},{8,24},{12,28},{16,0},{20,4},{24,8},{28,12},{1,17},{... | collective-permute-start | bytes 786440 | tf_op jit(solution)/shard_map/ppermute | solution.py:146
  152.0 3.7 %collective-permute-start.29 = (bf16[128,256]{0,1:T(8,128)(2,1)S(1)}, bf16[128,256]{0,1:T(8,128)(2,1)S(1)}, u32[]{:S(2)}, u32[]{:S(2)}) collective-permute-start(bf16[128,256]{0,1:T(8,128)(2,1)S(1)} %add_convert_fusion.16), channel_id=1, source_target_pairs={{0,4},{4,0},{8,12},{12,8},{16,20},{20,16},{24,28},{28,24},{1,5},{5... | collective-permute-start | bytes 196616 | tf_op jit(solution)/shard_map/ppermute | solution.py:146
  (19 other events, 85.9 us)

commit v5 on v4

v5 whole, which is shorter than its diff:
```python
import functools

import jax
import jax.numpy as jnp
from jax import lax
from jax.experimental import pallas as pl
from jax.experimental.pallas import tpu as pltpu
from jax.sharding import PartitionSpec as P

SIDE = 128
UNROLL = 8
GROUP = 32
FIRST_PIECES = 3
PLAN_ROWS = 8
FLIP_BYTES = 26 * 1024 * 1024
SPMM_BYTES = 24 * 1024 * 1024


def round_up(value, unit):
    return -(-value // unit) * unit


def total(mask, axis):
    return jnp.sum(jnp.where(mask, 1.0, 0.0), axis=axis, keepdims=True).astype(jnp.int32)


def total_of(values, axis):
    return jnp.sum(values.astype(jnp.float32), axis=axis, keepdims=True).astype(jnp.int32)


def plan_kernel(per_dev, n_out, place_ref, rows_r, cols_r, rows_c, cols_c, plan0_ref, plan1_ref, slot_ref):
    slots = rows_r.shape[1]
    size = plan0_ref.shape[1]
    count, row, col, mid = place_ref[0], place_ref[1], place_ref[2], place_ref[3]
    shift = per_dev.bit_length() - 1
    start = FIRST_PIECES * per_dev
    step = 2 * UNROLL

    def attributes(rows, cols, axis):
        ids = lax.broadcasted_iota(jnp.int32, rows.shape, axis)
        row_pos = (((rows >> shift) ^ col) << shift) + (rows & (per_dev - 1))
        away = (cols >> shift) ^ row
        out_pos = ((away >> 1) << shift) + (cols & (per_dev - 1))
        kept = 1 - (away & 1)
        last = (row_pos >= start).astype(jnp.int32)
        live = ids < count
        key = jnp.where(live, (2 * last + kept) * n_out + out_pos, 4 * n_out)
        return ids, row_pos, out_pos, 2 * last + kept, live, key

    ids_r, _, _, part_r, live_r, key_r = attributes(rows_r[...], cols_r[...], 1)
    ids_c, row_pos_c, out_pos_c, part_c, live_c, key_c = attributes(rows_c[...], cols_c[...], 0)
    equal = key_c == key_r
    below = key_r < key_c
    earlier_c = total(equal & (ids_r < ids_c), 1)
    earlier_r = total(equal & (ids_c < ids_r), 0)
    later_r = total(equal & (ids_c > ids_r), 0)
    odd_end = (later_r == 0) & ((earlier_r & 1) == 0)
    weight_r = jnp.where(live_r, jnp.where(odd_end, 2, 1), 0)
    rank_c = total(below, 1) + earlier_c
    rank_r = total(key_c < key_r, 0) + earlier_r
    padded_c = total_of(jnp.where(below, weight_r, 0), 1) + earlier_c
    length = [total_of(jnp.where(part_r == p, weight_r, 0), 1) for p in range(4)]
    n_first = total(live_r & (part_r < 2), 1)
    n_last = count - n_first
    last_base = ((n_first + GROUP - 1) >> 5) << 5
    slot_r = jnp.where(part_r >= 2, last_base + rank_r - n_first, rank_r)
    slot_ref[...] = jnp.where(live_r, slot_r, slots + GROUP)

    lane = lax.broadcasted_iota(jnp.int32, (1, size), 1)
    for p, plan_ref in enumerate((plan0_ref, plan1_ref)):
        sent, held = length[2 * p], length[2 * p + 1]
        sent_steps = (sent + step - 1) >> (step.bit_length() - 1)
        all_steps = sent_steps + ((held + step - 1) >> (step.bit_length() - 1))
        base = length[0] + length[1] if p else jnp.zeros_like(sent)
        in_plan = live_c & ((part_c >> 1) == p)
        pos = padded_c - base + jnp.where((part_c & 1) == 1, sent_steps * step - sent, 0)
        pos = jnp.where(in_plan, pos, -1)
        rank = rank_c - (n_first if p else 0)
        hit = pos == lane

        def placed(values, empty, hit=hit):
            return total_of(jnp.where(hit, values - empty, 0), 0) + empty

        plan_ref[0:1, :] = placed(rank, slots)
        plan_ref[1:2, :] = placed(row_pos_c - p * start, 0)
        taken = total(hit, 0) > 0
        ends = [
            jnp.max(jnp.where(in_plan & ((part_c & 1) == h), out_pos_c, 0).astype(jnp.float32), axis=0, keepdims=True)
            for h in range(2)
        ]
        end = jnp.where(lane < sent_steps * step, ends[0], ends[1]).astype(jnp.int32)
        plan_ref[2:3, :] = jnp.where(taken, placed(out_pos_c, 0), end)
        plan_ref[3:4, :] = jnp.where(taken, placed((earlier_c > 0).astype(jnp.int32), 0), 1)
        done = total(in_plan & (pos < (lane + 1) * step), 0)
        tiles = n_last if p else n_first
        info = [
            jnp.full((1, 1), mid, jnp.int32),
            sent_steps,
            (tiles + GROUP - 1) >> 5,
            last_base if p else jnp.zeros_like(last_base),
            jnp.zeros_like(last_base),
        ]
        for g in range(slots // GROUP):
            info.append(total((done <= (g + 1) * GROUP) & (lane < all_steps), 1))
        row_values = jnp.zeros((1, size), jnp.int32)
        for n, value in enumerate(info):
            row_values = jnp.where(lane == n, value, row_values)
        plan_ref[4:5, :] = row_values
        plan_ref[5:8, :] = jnp.zeros((3, size), jnp.int32)


def make_plans(tile_rows, tile_cols, place, n_row, per_dev):
    slots = tile_rows.size
    n_out = n_row // 2 * per_dev
    size = round_up(slots + 2 * n_out + 4 * UNROLL, SIDE)
    plan = jax.ShapeDtypeStruct((PLAN_ROWS, size), jnp.int32)
    return pl.pallas_call(
        functools.partial(plan_kernel, per_dev, n_out),
        out_shape=(plan, plan, jax.ShapeDtypeStruct((1, slots), jnp.int32)),
        in_specs=[pl.BlockSpec(memory_space=pltpu.SMEM)] + [pl.BlockSpec(memory_space=pltpu.VMEM)] * 4,
        out_specs=[pl.BlockSpec(memory_space=pltpu.VMEM)] * 3,
        compiler_params=pltpu.CompilerParams(vmem_limit_bytes=SPMM_BYTES),
        cost_estimate=pl.CostEstimate(flops=0, bytes_accessed=4096, transcendentals=0),
        name="plan_slots",
    )(place, tile_rows.reshape(1, slots), tile_cols.reshape(1, slots), tile_rows.reshape(slots, 1), tile_cols.reshape(slots, 1))


def flip_kernel(slot_ref, tiles_ref, out_ref, t_in, t_out, in_sem, out_sem):
    slots = t_in.shape[0]
    groups = slots // GROUP
    loads = [
        pltpu.make_async_copy(tiles_ref.at[pl.ds(g * GROUP, GROUP)], t_in.at[pl.ds(g * GROUP, GROUP)], in_sem.at[g])
        for g in range(groups)
    ]
    for load in loads:
        load.start()
    for g in range(groups):
        loads[g].wait()

        def some(step, carry, g=g):
            for u in range(4):
                k = g * GROUP + step * 4 + u
                t_out[slot_ref[0, k]] = t_in[k].T
            return carry

        lax.fori_loop(0, GROUP // 4, some, 0)
    stores = [
        pltpu.make_async_copy(t_out.at[pl.ds(g * GROUP, GROUP)], out_ref.at[pl.ds(g * GROUP, GROUP)], out_sem.at[g])
        for g in range(groups + 1)
    ]
    for store in stores:
        store.start()
    for store in stores:
        store.wait()


def flip_tiles(slot, tile_stack):
    slots = tile_stack.shape[0]
    groups = slots // GROUP
    return pl.pallas_call(
        flip_kernel,
        out_shape=jax.ShapeDtypeStruct((slots + GROUP, SIDE, SIDE), tile_stack.dtype),
        grid_spec=pltpu.PrefetchScalarGridSpec(
            num_scalar_prefetch=1,
            grid=(),
            in_specs=[pl.BlockSpec(memory_space=pl.ANY)],
            out_specs=pl.BlockSpec(memory_space=pl.ANY),
            scratch_shapes=[
                pltpu.VMEM(tile_stack.shape, tile_stack.dtype),
                pltpu.VMEM((slots + GROUP + 1, SIDE, SIDE), tile_stack.dtype),
                pltpu.SemaphoreType.DMA((groups,)),
                pltpu.SemaphoreType.DMA((groups + 1,)),
            ],
        ),
        compiler_params=pltpu.CompilerParams(vmem_limit_bytes=FLIP_BYTES),
        cost_estimate=pl.CostEstimate(flops=0, bytes_accessed=4096, transcendentals=0),
        name="flip_tiles",
    )(slot, tile_stack)


def spmm_kernel(layout, last, plan_ref, *refs):
    n_refs = sum(layout)
    refs_left = list(refs[:n_refs])
    pieces = [[refs_left.pop(0) for _ in range(n)] for n in layout]
    rest = list(refs[n_refs:])
    tiles_ref = rest.pop(0)
    acc_refs = (rest.pop(0), rest.pop(0)) if last else (None, None)
    out_refs = (rest.pop(0), rest.pop(0))
    m_vmem, t_vmem, total_ref, sems = rest
    nodes, width = pieces[0][0].shape
    slots = t_vmem.shape[0] - 1
    mid, sent_steps, n_groups, tile_base = [plan_ref[4, n] for n in range(4)]

    def group_copy(g):
        at = pl.multiple_of(g * GROUP, GROUP)
        return pltpu.make_async_copy(
            tiles_ref.at[pl.ds(tile_base + at, GROUP)], t_vmem.at[pl.ds(at, GROUP)], sems.at[g]
        )

    def begin_copy(g, carry):
        group_copy(g).start()
        return carry

    lax.fori_loop(0, n_groups, begin_copy, 0)
    t_vmem[slots] = jnp.zeros((SIDE, SIDE), t_vmem.dtype)
    for out_ref, acc_ref in zip(out_refs, acc_refs):

        def begin(step, carry, out_ref=out_ref, acc_ref=acc_ref):
            at = pl.ds(pl.multiple_of(step * 256, 256), 256)
            if last:
                out_ref[at, :] = acc_ref[at, :].astype(out_ref.dtype)
            else:
                out_ref[at, :] = jnp.zeros((256, width), out_ref.dtype)
            return carry

        lax.fori_loop(0, out_ref.shape[0] // 256, begin, 0)
    for p, options in enumerate(pieces):

        def take(ref, p=p):
            def some(step, carry):
                at = pl.multiple_of(step * 512, 512)
                m_vmem[pl.ds(pl.multiple_of(p * nodes + at, 512), 512), :] = ref[pl.ds(at, 512), :]
                return carry

            lax.fori_loop(0, nodes // 512, some, 0)

        if len(options) == 1:
            take(options[0])
        else:
            pl.when(mid == 1)(functools.partial(take, options[0]))
            pl.when(mid != 1)(functools.partial(take, options[1]))

    def block(index):
        return m_vmem[pl.ds(pl.multiple_of(index * SIDE, SIDE), SIDE), :]

    def add_pairs(out_ref, acc_ref, step, carry):
        running = total_ref[...]
        prods = []
        for u in range(UNROLL):
            k = 2 * (step * UNROLL + u)
            left = jnp.concatenate([t_vmem[plan_ref[0, k]], t_vmem[plan_ref[0, k + 1]]], axis=1)
            right = jnp.concatenate([block(plan_ref[1, k]), block(plan_ref[1, k + 1])], axis=0)
            prods.append(jnp.dot(left, right, preferred_element_type=jnp.float32))
        for u in range(UNROLL):
            k = 2 * (step * UNROLL + u)
            at = pl.ds(pl.multiple_of(plan_ref[2, k] * SIDE, SIDE), SIDE)
            before = acc_ref[at, :] if last else jnp.zeros_like(running)
            running = prods[u] + jnp.where(plan_ref[3, k] == 1, running, before)
            out_ref[at, :] = running.astype(out_ref.dtype)
        total_ref[...] = running
        return carry

    total_ref[...] = jnp.zeros_like(total_ref)

    def add_group(g, carry):
        group_copy(g).wait()
        low, high = plan_ref[4, 4 + g], plan_ref[4, 5 + g]
        lax.fori_loop(
            jnp.minimum(low, sent_steps), jnp.minimum(high, sent_steps),
            functools.partial(add_pairs, out_refs[0], acc_refs[0]), 0,
        )
        lax.fori_loop(
            jnp.maximum(low, sent_steps), jnp.maximum(high, sent_steps),
            functools.partial(add_pairs, out_refs[1], acc_refs[1]), 0,
        )
        return carry

    lax.fori_loop(0, n_groups, add_group, 0)


def spmm(plan, pieces, tiles, acc, n_row):
    nodes, width = pieces[0][0].shape
    half = n_row // 2 * nodes
    last = acc is not None
    slots = tiles.shape[0] - GROUP
    out = jax.ShapeDtypeStruct((half, width), jnp.bfloat16 if last else jnp.float32)
    blocks = [ref for p in pieces for ref in p]
    in_vmem, in_any = pl.BlockSpec(memory_space=pltpu.VMEM), pl.BlockSpec(memory_space=pl.ANY)
    return pl.pallas_call(
        functools.partial(spmm_kernel, [len(p) for p in pieces], last),
        out_shape=(out, out),
        grid_spec=pltpu.PrefetchScalarGridSpec(
            num_scalar_prefetch=1,
            grid=(),
            in_specs=[in_vmem] * len(blocks) + [in_any] + [in_vmem] * len(acc or []),
            out_specs=[in_vmem] * 2,
            scratch_shapes=[
                pltpu.VMEM((len(pieces) * nodes, width), jnp.bfloat16),
                pltpu.VMEM((slots + 1, SIDE, SIDE), jnp.bfloat16),
                pltpu.VMEM((SIDE, width), jnp.float32),
                pltpu.SemaphoreType.DMA((slots // GROUP,)),
            ],
        ),
        compiler_params=pltpu.CompilerParams(vmem_limit_bytes=SPMM_BYTES),
        cost_estimate=pl.CostEstimate(flops=0, bytes_accessed=4096, transcendentals=0),
        name="spmm_last" if last else "spmm_first",
    )(plan, *blocks, tiles, *(acc or []))


def xor_permute(value, axis, mask):
    size = lax.axis_size(axis)
    return lax.ppermute(value, axis, [(i, i ^ mask) for i in range(size)])


def tree_sum(values):
    while len(values) > 1:
        values = [a + b for a, b in zip(values[::2], values[1::2])]
    return values[0]


def gather_first(own):
    return xor_permute(own, "col", 1), xor_permute(own, "col", 2)


def gather_second(own, by_two, n_col):
    ends, middles = [], []
    for low in range(0, n_col, 4):
        ends += [(low + 1, low), (low + 2, low + 3)]
        middles += [(low + 1, low + 2), (low + 2, low + 1)]
    return lax.ppermute(own, "col", middles), lax.ppermute(by_two, "col", ends)


def as_pieces(own, first, second, mid, n_col):
    if n_col == 4:
        return [[own], [first[0]], [first[1]], list(second)]
    pieces = [own, first[0], first[1], jnp.where(mid, second[0], second[1])]
    for high in range(4, n_col, 4):
        pieces += [xor_permute(piece, "col", high) for piece in pieces[:4]]
    return [[piece] for piece in pieces]


def fence(*values):
    return lax.optimization_barrier(values)


def add_f32(a, b):
    return a.astype(jnp.float32) + b.astype(jnp.float32)


def stage_sums(keep, recv, n_blocks, rows):
    width = keep.shape[1]
    cut = (n_blocks // 2, 2, 2, rows, width)
    flat = (2, n_blocks // 2, 2, rows, width)

    def summed(shape, pick):
        both = add_f32(pick(keep.reshape(shape)), pick(recv.reshape(shape)))
        return both.astype(jnp.bfloat16).reshape(-1, width)

    stage = [
        summed(cut, lambda v: v[:, 1, 0]),
        summed(cut, lambda v: v[:, 0, 0]),
        summed(flat, lambda v: v[1, :, 1]),
        summed(flat, lambda v: v[0, :, 1]),
    ]
    return stage, add_f32(keep, recv).astype(jnp.bfloat16)


def halve(value, upper, rows):
    blocks = value.shape[0] // rows
    shape = (2, blocks // 2) if upper else (blocks // 2, 2)
    cut = value.reshape(shape + (rows, value.shape[1]))
    if upper:
        sent, kept = cut[1], cut[0]
    else:
        sent, kept = cut[:, 1], cut[:, 0]
    return sent.reshape(-1, value.shape[1]), kept.reshape(-1, value.shape[1])


def exchange_first(stage, bits):
    return xor_permute(stage[0], "row", bits[0]), xor_permute(stage[2], "row", bits[-1])


def exchange_second(stage, recv, bits, rows):
    sent, kept = [], []
    for upper in (0, 1):
        value = add_f32(stage[2 * upper + 1], recv[upper]).astype(jnp.bfloat16)
        sent_u, kept_u = halve(value, upper, rows)
        sent.append(sent_u)
        kept.append(kept_u)
    return kept, sent


def send_second(sent, bits):
    return [xor_permute(s, "row", bit) for s, bit in zip(sent, (bits[1], bits[-2]))]


def exchange_last(kept, recv, bits, rows):
    done = []
    for upper in (0, 1):
        value = add_f32(kept[upper], recv[upper])
        for bit in (bits[::-1] if upper else bits)[2:]:
            sent_u, kept_u = halve(value.astype(jnp.bfloat16), upper, rows)
            value = add_f32(kept_u, xor_permute(sent_u, "row", bit))
        done.append(value.astype(jnp.bfloat16))
    return jnp.concatenate(done, axis=0)


def weight_term(near, sums):
    nodes = near[0].shape[0]
    terms = [
        lax.dot_general(f, sums[q * nodes : (q + 1) * nodes], (((0,), (0,)), ((), ())), preferred_element_type=jnp.float32)
        for q, f in enumerate(near)
    ]
    return tree_sum(terms).astype(jnp.bfloat16)


def sum_over(term, axis, masks):
    parts = [term] + [xor_permute(term, axis, m) for m in masks]
    return tree_sum([p.astype(jnp.float32) for p in parts])


def body(grad_out, preact, features, weight, tiles, tile_rows, tile_cols, live_counts):
    nodes, width = grad_out.shape
    n_row, n_col = lax.axis_size("row"), lax.axis_size("col")
    row, col = lax.axis_index("row"), lax.axis_index("col")
    slots = tiles.shape[2]
    cw = width // 2
    rows = nodes // 2
    bits = [1 << b for b in range(1, n_row.bit_length() - 1)]
    mid = ((col & 3) == 1) | ((col & 3) == 2)

    own0, own1 = [
        jnp.where(preact[:, cut] > 0, grad_out[:, cut], jnp.zeros_like(grad_out[:, cut]))
        for cut in (slice(0, cw), slice(cw, width))
    ]
    first0 = gather_first(own0)
    place = jnp.stack([live_counts.reshape(()), row, col, mid.astype(jnp.int32)])
    plan0, plan1, slot = make_plans(tile_rows, tile_cols, place, n_row, nodes // SIDE)
    flipped = flip_tiles(slot, tiles.reshape(slots, SIDE, SIDE))
    features, flipped = fence(features, flipped)
    near = [features]
    for bit in bits[:2]:
        near.append(xor_permute(features, "row", bit))
    own0, own1, first0, plan0, plan1, flipped = fence(own0, own1, first0, plan0, plan1, flipped)

    second0 = gather_second(own0, first0[1], n_col)
    pieces0 = as_pieces(own0, first0, second0, mid, n_col)
    pieces0, own1, near = fence(pieces0, own1, near)

    first1 = gather_first(own1)
    near.append(xor_permute(near[1], "row", bits[1]))
    for bit in bits[2:]:
        near += [xor_permute(f, "row", bit) for f in near]
    acc0 = spmm(plan0, pieces0[:FIRST_PIECES], flipped, None, n_row)
    send0, keep0 = spmm(plan1, pieces0[FIRST_PIECES:], flipped, acc0, n_row)
    own1, first1, near, send0, keep0 = fence(own1, first1, near, send0, keep0)

    second1 = gather_second(own1, first1[1], n_col)
    pieces1 = as_pieces(own1, first1, second1, mid, n_col)
    stage0, sums0 = stage_sums(keep0, xor_permute(send0, "row", 1), n_row // 2, rows)
    recv0 = exchange_first(stage0, bits)
    acc1 = spmm(plan0, pieces1[:FIRST_PIECES], flipped, None, n_row)
    pieces1, stage0, acc1 = fence(pieces1, stage0, acc1)

    send1, keep1 = spmm(plan1, pieces1[FIRST_PIECES:], flipped, acc1, n_row)
    send1, keep1, recv0, stage0, sums0 = fence(send1, keep1, recv0, stage0, sums0)

    stage1, sums1 = stage_sums(keep1, xor_permute(send1, "row", 1), n_row // 2, rows)
    rest0, sent0 = exchange_second(stage0, recv0, bits, rows)
    recv0 = send_second(sent0, bits)
    term0 = weight_term(near, sums0)
    stage1, sums1, term0 = fence(stage1, sums1, term0)
    stage1, sums1, term0, rest0, recv0 = fence(stage1, sums1, term0, rest0, recv0)

    recv1 = exchange_first(stage1, bits)
    term1 = weight_term(near, sums1)
    even = (row & 1) == 0
    theirs, mine = jnp.where(even, term1, term0), jnp.where(even, term0, term1)
    mine = add_f32(mine, xor_permute(theirs, "row", 1)).astype(jnp.bfloat16)
    mine = sum_over(mine, "col", range(1, n_col)).astype(jnp.bfloat16)
    recv1, mine = fence(recv1, mine)

    rest1, sent1 = exchange_second(stage1, recv1, bits, rows)
    rest1, sent1, mine = fence(rest1, sent1, mine)
    recv1 = send_second(sent1, bits)
    mine = sum_over(mine, "row", range(2, n_row, 2)).astype(jnp.bfloat16)
    colgrad0 = exchange_last(rest0, recv0, bits, rows)
    colgrad1 = exchange_last(rest1, recv1, bits, rows)
    colgrad1, mine = fence(colgrad1, mine)

    theirs = xor_permute(mine, "row", 1)
    low, high = jnp.where(even, mine, theirs), jnp.where(even, theirs, mine)
    grad_weight = jnp.concatenate([low, high], axis=1).astype(jnp.float32)
    colgrad = jnp.concatenate([colgrad0, colgrad1], axis=1)
    grad_features = lax.dot_general(
        colgrad, weight, (((1,), (1,)), ((), ())), preferred_element_type=jnp.float32
    ).astype(jnp.bfloat16)
    return (grad_features, grad_weight)


def solution(mesh):
    in_specs = (
        P(("row", "col"), None),
        P(("row", "col"), None),
        P(("col", "row"), None),
        P(),
        P("row", "col", None, None, None),
        P("row", "col", None),
        P("row", "col", None),
        P("row", "col"),
    )
    out_specs = (P(("col", "row"), None), P())
    return jax.shard_map(body, mesh=mesh, in_specs=in_specs, out_specs=out_specs, check_vma=False)
```

time: 158 us -> 144 us (0.911)
  local copies, waits for them, and re-layouts: 28.8 us -> 4.68 us
  waiting for transfers between devices: 32.9 us -> 52.1 us
  Pallas kernels: 28.9 us -> 39.5 us
  between operations: 8.01 us -> 1.72 us
  matrix products: 11.2 us -> 5.27 us
  starting transfers between devices: 32.3 us -> 27.7 us
  other arithmetic: 14.7 us -> 12.3 us
    ppermute x26 -> x25, waiting for transfers between devices: 21.9 us -> 36.7 us  [xor_permute(): return lax.ppermute(value, axis, [(i, i ^ mask) for i in range(size)])]
    unnamed x43 -> x26, local copies, waits for them, and re-layouts: 18.5 us -> 4.26 us
    dynamic_slice x4 -> x0, local copies, waits for them, and re-layouts: 9.11 us -> none  [body(): lax.dynamic_slice_in_dim(f, core * in_half, in_half, 1)]
    pallas_call x4, Pallas kernels: 21 us -> 27.6 us  [spmm(): pl.pallas_call(functools.partial(spmm_kernel, [len(p) for p in pieces], l...]
    dot_general x16 -> x8, matrix products: 9.74 us -> 3.83 us  [weight_term(): lax.dot_general(f, sums[q * nodes:(q + 1) * nodes], (((0,), (0,)), ((), (...]
    convert_element_type x7 -> x10, other arithmetic: 4.87 us -> 10.2 us  [the longest x2 4.03 us: stage_sums(): return (stage, add_f32(keep, recv).astype(jnp.bfloat16))]
    ppermute x26 -> x25, starting transfers between devices: 28.3 us -> 23.7 us  [xor_permute(): return lax.ppermute(value, axis, [(i, i ^ mask) for i in range(size)])]
    ppermute x2, waiting for transfers between devices: 11 us -> 15.4 us  [gather_second(): lax.ppermute(by_two, 'col', ends)]
  transfers between devices with their start and end apart: 30 -> 29, of which waited for: 8 -> 16; matrix products, arithmetic and copies ran while one was open for 22% -> 9% of each run, Pallas kernels for 18% -> 28%
where the time goes in v5:
time: 144 us; the launch traced here: 143 us
  waiting for transfers between devices  52.1 us (36%)
  Pallas kernels  39.5 us (27%)
  starting transfers between devices  27.7 us (19%)
  other arithmetic  12.3 us (9%)
  matrix products  5.27 us (4%)
  local copies, waits for them, and re-layouts  4.68 us (3%)
  between operations  1.72 us (1%)
    ppermute x25, waiting for transfers between devices, xor_permute(): return lax.ppermute(value, axis, [(i, i ^ mask) for i in range(size)])  36.7 us
    pallas_call x4, Pallas kernels, spmm(): pl.pallas_call(functools.partial(spmm_kernel, [len(p) for p in pieces], l...  27.6 us
    ppermute x25, starting transfers between devices, xor_permute(): return lax.ppermute(value, axis, [(i, i ^ mask) for i in range(size)])  23.7 us
    ppermute x2, waiting for transfers between devices, gather_second(): lax.ppermute(by_two, 'col', ends)  15.4 us
    pallas_call x1, Pallas kernels, flip_tiles(): pl.pallas_call(flip_kernel, out_shape=jax.ShapeDtypeStruct((slots + GROUP...  9.59 us
    unnamed x26, local copies, waits for them, and re-layouts  4.26 us
    convert_element_type x2, other arithmetic, stage_sums(): return (stage, add_f32(keep, recv).astype(jnp.bfloat16))  4.03 us
    dot_general x8, matrix products, weight_term(): lax.dot_general(f, sums[q * nodes:(q + 1) * nodes], (((0,), (0,)), ((), (...  3.83 us
  transfers between devices with their start and end apart: 29, of which 16 were waited for; matrix products, arithmetic and copies ran while one was open for 9% of the time, Pallas kernels for 28%

profile of v5, /device:TPU:1, one launch (start us, length us, event | category | flops | bytes accessed | tf_op | source)
XLA Modules:
  0.0 143.3 jit_solution(1297644674699583107)
XLA Ops:
  0.7 1.7 %compare_select_fusion = (bf16[2048,128]{1,0:T(8,128)(2,1)S(1)}, bf16[2048,128]{1,0:T(8,128)(2,1)S(1)}) fusion(bf16[2048,256]{1,0:T(8,128)(2,1)} %param.8, bf16[2048,256]{1,0:T(8,128)(2,1)} %param.9), kind=kLoop, calls=%fused_computation.28 | loop fusion | flops 1048576 | bytes 3145728 | tf_op jit(solution)/shard_map/jit(_where)/select_n | solution.py:423
  2.3 3.2 %collective-permute-start.1 = (bf16[2048,128]{1,0:T(8,128)(2,1)S(1)}, bf16[2048,128]{1,0:T(8,128)(2,1)S(1)}, u32[]{:S(2)}, u32[]{:S(2)}) collective-permute-start(bf16[2048,128]{1,0:T(8,128)(2,1)S(1)} %get-tuple-element.97.refs_0_), channel_id=1, source_target_pairs={{0,2},{1,3},{2,0},{3,1},{4,6},{5,7},{6,4},{7,5},{8,10},{9,11},{10,... | collective-permute-start | bytes 1572872 | tf_op jit(solution)/shard_map/ppermute | solution.py:302
  5.5 1.3 collective-permute-start
  7.9 2.3 %plan_slots.1 = (s32[8,512]{1,0:T(8,128)S(1)}, s32[8,512]{1,0:T(8,128)S(1)}, s32[1,320]{1,0:T(1,128)S(1)}) custom-call(s32[4]{0:T(128)S(1)} %pad_add_fusion.place_ref, s32[1,320]{1,0:T(1,128)S(1)} %bitcast.47, s32[1,320]{1,0:T(1,128)S(1)} %bitcast.49, s32[320,1]{1,0:T(8,128)S(1)} %copy.10.rows_c, s32[320,1]{1,0:T(8,128)S(1)} %copy.11.cols_c), custom_call_target="tpu_custom_call" | custom-call | bytes 4096 | tf_op jit(solution)/shard_map/plan_slots/pallas_call | solution.py:117
  10.2 4.0 %copy-done.1 = bf16[1,1,320,128,128]{4,3,2,1,0:T(8,128)(2,1)S(1)} copy-done((bf16[1,1,320,128,128]{4,3,2,1,0:T(8,128)(2,1)S(1)}, bf16[1,1,320,128,128]{4,3,2,1,0:T(8,128)(2,1)}, u32[]{:S(2)}) %copy-start.1) | copy-done | bytes 10485784
  14.2 9.6 %flip_tiles.1.refs_3_.refs_2_ = bf16[352,128,128]{2,1,0:T(8,128)(2,1)S(1)} custom-call(s32[1,320]{1,0:T(1,128)S(1)} %get-tuple-element.81.slot_ref, bf16[320,128,128]{2,1,0:T(8,128)(2,1)S(1)} %bitcast.41), custom_call_target="tpu_custom_call" | custom-call | bytes 4096 | tf_op jit(solution)/shard_map/flip_tiles/pallas_call | solution.py:160
  23.8 1.3 collective-permute-start.5
  26.3 2.2 %collective-permute-done.1.refs_2_ = bf16[2048,128]{1,0:T(8,128)(2,1)S(1)} collective-permute-done((bf16[2048,128]{1,0:T(8,128)(2,1)S(1)}, bf16[2048,128]{1,0:T(8,128)(2,1)S(1)}, u32[]{:S(2)}, u32[]{:S(2)}) %collective-permute-start.1) | collective-permute-done | bytes 524320 | tf_op jit(solution)/shard_map/ppermute | solution.py:302
  29.2 1.3 collective-permute-start.3
  30.5 13.0 %collective-permute-done.3.refs_1_ = bf16[2048,128]{1,0:T(8,128)(2,1)S(1)} collective-permute-done((bf16[2048,128]{1,0:T(8,128)(2,1)S(1)}, bf16[2048,128]{1,0:T(8,128)(2,1)S(1)}, u32[]{:S(2)}, u32[]{:S(2)}) %collective-permute-start.3) | collective-permute-done | bytes 524320 | tf_op jit(solution)/shard_map/ppermute | solution.py:320
  43.5 3.8 %collective-permute-done.5 = bf16[2048,256]{1,0:T(8,128)(2,1)S(1)} collective-permute-done((bf16[2048,256]{1,0:T(8,128)(2,1)S(1)}, bf16[2048,256]{1,0:T(8,128)(2,1)S(1)}, u32[]{:S(2)}, u32[]{:S(2)}) %collective-permute-start.5) | collective-permute-done | bytes 1048608 | tf_op jit(solution)/shard_map/ppermute | solution.py:302
  49.6 9.2 %spmm_first.2 = (f32[8192,128]{1,0:T(8,128)S(1)}, f32[8192,128]{1,0:T(8,128)S(1)}) custom-call(s32[8,512]{1,0:T(8,128)S(1)} %get-tuple-element.96.plan_ref, bf16[2048,128]{1,0:T(8,128)(2,1)S(1)} %get-tuple-element.97.refs_0_, bf16[2048,128]{1,0:T(8,128)(2,1)S(1)} %collective-permute-done.refs_1_, bf16[2048,128]{1,0:T(8,128)(2,1)S(1)} %collective-permute-done.1.refs_2_, ...), custom_call_target="tpu_custom_call" | custom-call | bytes 4096 | tf_op jit(solution)/shard_map/spmm_first/pallas_call | solution.py:279
  58.8 3.9 %spmm_last.2 = (bf16[8192,128]{1,0:T(8,128)(2,1)S(1)}, bf16[8192,128]{1,0:T(8,128)(2,1)S(1)}) custom-call(s32[8,512]{1,0:T(8,128)S(1)} %get-tuple-element.83.plan_ref, bf16[2048,128]{1,0:T(8,128)(2,1)S(1)} %collective-permute-done.2.refs_0_, bf16[2048,128]{1,0:T(8,128)(2,1)S(1)} %collective-permute-done.3.refs_1_, ...), custom_call_target="tpu_custom_call" | custom-call | bytes 4096 | tf_op jit(solution)/shard_map/spmm_last/pallas_call | solution.py:279
  62.7 11.7 %collective-permute-done.7.refs_2_ = bf16[2048,128]{1,0:T(8,128)(2,1)S(1)} collective-permute-done((bf16[2048,128]{1,0:T(8,128)(2,1)S(1)}, bf16[2048,128]{1,0:T(8,128)(2,1)S(1)}, u32[]{:S(2)}, u32[]{:S(2)}) %collective-permute-start.7) | collective-permute-done | bytes 524320 | tf_op jit(solution)/shard_map/ppermute | solution.py:302
  77.0 9.2 %spmm_first.3 = (f32[8192,128]{1,0:T(8,128)S(1)}, f32[8192,128]{1,0:T(8,128)S(1)}) custom-call(s32[8,512]{1,0:T(8,128)S(1)} %get-tuple-element.96.plan_ref, bf16[2048,128]{1,0:T(8,128)(2,1)S(1)} %get-tuple-element.104.refs_0_, bf16[2048,128]{1,0:T(8,128)(2,1)S(1)} %collective-permute-done.6.refs_1_, bf16[2048,128]{1,0:T(8,128)(2,1)S(1)} %collective-permute-done.7.refs_2_, ...), custom_call_target="tpu_custom_call" | custom-call | bytes 4096 | tf_op jit(solution)/shard_map/spmm_first/pallas_call | solution.py:279
  86.9 1.9 %add_convert_fusion.1 = bf16[8192,128]{1,0:T(8,128)(2,1)} fusion(bf16[8192,128]{1,0:T(8,128)(2,1)S(1)} %collective-permute-done.11, bf16[8192,128]{1,0:T(8,128)(2,1)S(1)} %get-tuple-element.107), kind=kLoop, calls=%fused_computation.1 | loop fusion | flops 4194304 | bytes 6291456 | tf_op jit(solution)/shard_map/convert_element_type | solution.py:355
  88.8 2.4 %collective-permute-done.10.refs_1_ = bf16[2048,128]{1,0:T(8,128)(2,1)S(1)} collective-permute-done((bf16[2048,128]{1,0:T(8,128)(2,1)S(1)}, bf16[2048,128]{1,0:T(8,128)(2,1)S(1)}, u32[]{:S(2)}, u32[]{:S(2)}) %collective-permute-start.10) | collective-permute-done | bytes 524320 | tf_op jit(solution)/shard_map/ppermute | solution.py:320
  91.2 5.4 %spmm_last.3 = (bf16[8192,128]{1,0:T(8,128)(2,1)}, bf16[8192,128]{1,0:T(8,128)(2,1)S(1)}) custom-call(s32[8,512]{1,0:T(8,128)S(1)} %get-tuple-element.83.plan_ref, bf16[2048,128]{1,0:T(8,128)(2,1)S(1)} %collective-permute-done.9.refs_0_, bf16[2048,128]{1,0:T(8,128)(2,1)S(1)} %collective-permute-done.10.refs_1_, ...), custom_call_target="tpu_custom_call" | custom-call | bytes 4096 | tf_op jit(solution)/shard_map/spmm_last/pallas_call | solution.py:279
  97.9 1.3 collective-permute-done.13
  99.2 1.6 %add_convert_fusion.4 = (bf16[2048,128]{1,0:T(8,128)(2,1)S(1)}, bf16[2048,128]{1,0:T(8,128)(2,1)S(1)}) fusion(bf16[2048,128]{1,0:T(8,128)(2,1)} %collective-permute-done.13, bf16[2048,128]{1,0:T(8,128)(2,1)S(1)} %bitcast.57, bf16[2048,128]{1,0:T(8,128)(2,1)} %collective-permute-done.12, bf16[2048,128]{1,0:T(8,128)(2,1)S(1)} %bitcast.56), kind=kLoop, calls=%fused_computation.18 | loop fusion | flops 2097152 | bytes 3145728 | tf_op jit(solution)/shard_map/convert_element_type | solution.py:376
  101.1 2.0 %collective-permute-start.15 = (bf16[1024,128]{1,0:T(8,128)(2,1)S(1)}, bf16[1024,128]{1,0:T(8,128)(2,1)S(1)}, u32[]{:S(2)}, u32[]{:S(2)}) collective-permute-start(bf16[1024,128]{1,0:T(8,128)(2,1)S(1)} %get-tuple-element.172), channel_id=1, source_target_pairs={{0,16},{4,20},{8,24},{12,28},{16,0},{20,4},{24,8},{28,12},{1,17},{... | collective-permute-start | bytes 786440 | tf_op jit(solution)/shard_map/ppermute | solution.py:302
  105.3 1.5 %add_convert_fusion.8 = (bf16[2,1,1,1024,128]{4,3,2,1,0:T(8,128)(2,1)S(1)}, bf16[2,1,1,1024,128]{4,3,2,1,0:T(8,128)(2,1)S(1)}) fusion(bf16[2,2,2,1024,128]{4,3,2,1,0:T(8,128)(2,1)} %bitcast.16, bf16[2,2,2,1024,128]{4,3,2,1,0:T(8,128)(2,1)S(1)} %bitcast.42), kind=kLoop, calls=%fused_computation.22 | loop fusion | flops 2097152 | bytes 3145728 | tf_op jit(solution)/shard_map/convert_element_type | solution.py:347
  106.8 2.1 %add_convert_fusion = bf16[8192,128]{1,0:T(8,128)(2,1)S(1)} fusion(bf16[8192,128]{1,0:T(8,128)(2,1)} %collective-permute-done.14, bf16[8192,128]{1,0:T(8,128)(2,1)S(1)} %get-tuple-element.119), kind=kLoop, calls=%fused_computation | loop fusion | flops 4194304 | bytes 6291456 | tf_op jit(solution)/shard_map/convert_element_type | solution.py:355
  108.9 1.5 %add_convert_fusion.6 = (bf16[1,2,1,1024,128]{4,3,2,1,0:T(8,128)(2,1)S(1)}, bf16[1,2,1,1024,128]{4,3,2,1,0:T(8,128)(2,1)S(1)}) fusion(bf16[2,2,2,1024,128]{4,3,2,1,0:T(8,128)(2,1)} %bitcast.16, bf16[2,2,2,1024,128]{4,3,2,1,0:T(8,128)(2,1)S(1)} %bitcast.43), kind=kLoop, calls=%fused_computation.20 | loop fusion | flops 2097152 | bytes 3145728 | tf_op jit(solution)/shard_map/convert_element_type | solution.py:347
  112.8 1.7 %collective-permute-start.17 = (bf16[2048,128]{1,0:T(8,128)(2,1)S(1)}, bf16[2048,128]{1,0:T(8,128)(2,1)S(1)}, u32[]{:S(2)}, u32[]{:S(2)}) collective-permute-start(bf16[2048,128]{1,0:T(8,128)(2,1)S(1)} %bitcast.58), channel_id=1, source_target_pairs={{0,8},{4,12},{8,0},{12,4},{16,24},{20,28},{24,16},{28,20},{1,9},{5... | collective-permute-start | bytes 1572872 | tf_op jit(solution)/shard_map/ppermute | solution.py:302
  116.0 2.5 %collective-permute-start.21 = (bf16[256,128]{1,0:T(8,128)(2,1)S(1)}, bf16[256,128]{1,0:T(8,128)(2,1)S(1)}, u32[]{:S(2)}, u32[]{:S(2)}) collective-permute-start(bf16[256,128]{1,0:T(8,128)(2,1)S(1)} %add_convert_fusion.20), channel_id=1, source_target_pairs={{0,2},{1,3},{2,0},{3,1},{4,6},{5,7},{6,4},{7,5},{8,10},{9,11},{10,... | collective-permute-start | bytes 196616 | tf_op jit(solution)/shard_map/ppermute | solution.py:302
  119.0 1.4 collective-permute-done.22
  120.4 4.8 %collective-permute-done.21 = bf16[256,128]{1,0:T(8,128)(2,1)S(1)} collective-permute-done((bf16[256,128]{1,0:T(8,128)(2,1)S(1)}, bf16[256,128]{1,0:T(8,128)(2,1)S(1)}, u32[]{:S(2)}, u32[]{:S(2)}) %collective-permute-start.21) | collective-permute-done | bytes 65568 | tf_op jit(solution)/shard_map/ppermute | solution.py:302
  125.2 1.6 %collective-permute-done.17 = bf16[2048,128]{1,0:T(8,128)(2,1)S(1)} collective-permute-done((bf16[2048,128]{1,0:T(8,128)(2,1)S(1)}, bf16[2048,128]{1,0:T(8,128)(2,1)S(1)}, u32[]{:S(2)}, u32[]{:S(2)}) %collective-permute-start.17) | collective-permute-done | bytes 524320 | tf_op jit(solution)/shard_map/ppermute | solution.py:302
  133.4 5.4 %collective-permute-done.23 = bf16[1024,128]{1,0:T(8,128)(2,1)S(1)} collective-permute-done((bf16[1024,128]{1,0:T(8,128)(2,1)S(1)}, bf16[1024,128]{1,0:T(8,128)(2,1)S(1)}, u32[]{:S(2)}, u32[]{:S(2)}) %collective-permute-start.23) | collective-permute-done | bytes 262176 | tf_op jit(solution)/shard_map/ppermute | solution.py:302
  139.0 2.2 %collective-permute-start.28 = (bf16[256,128]{1,0:T(8,128)(2,1)S(1)}, bf16[256,128]{1,0:T(8,128)(2,1)S(1)}, u32[]{:S(2)}, u32[]{:S(2)}) collective-permute-start(bf16[256,128]{1,0:T(8,128)(2,1)S(1)} %add_convert_fusion.18), channel_id=1, source_target_pairs={{0,4},{4,0},{8,12},{12,8},{16,20},{20,16},{24,28},{28,24},{1,5},{5... | collective-permute-start | bytes 196616 | tf_op jit(solution)/shard_map/ppermute | solution.py:302
  141.2 1.4 convolution_convert_fusion
  (94 shorter events, 23.4 us)
Async XLA Ops:
  0.6 140.5 %copy-start = (bf16[256,256]{1,0:T(8,128)(2,1)S(1)}, bf16[256,256]{1,0:T(8,128)(2,1)}, u32[]{:S(2)}) copy-start(bf16[256,256]{1,0:T(8,128)(2,1)} %param.11) | copy-start | bytes 393220
  2.3 26.1 %collective-permute-start.1 = (bf16[2048,128]{1,0:T(8,128)(2,1)S(1)}, bf16[2048,128]{1,0:T(8,128)(2,1)S(1)}, u32[]{:S(2)}, u32[]{:S(2)}) collective-permute-start(bf16[2048,128]{1,0:T(8,128)(2,1)S(1)} %get-tuple-element.97.refs_0_), channel_id=1, source_target_pairs={{0,2},{1,3},{2,0},{3,1},{4,6},{5,7},{6,4},{7,5},{8,10},{9,11},{10,... | collective-permute-start | bytes 1572872 | tf_op jit(solution)/shard_map/ppermute | solution.py:302
  5.5 22.9 %collective-permute-start = (bf16[2048,128]{1,0:T(8,128)(2,1)S(1)}, bf16[2048,128]{1,0:T(8,128)(2,1)S(1)}, u32[]{:S(2)}, u32[]{:S(2)}) collective-permute-start(bf16[2048,128]{1,0:T(8,128)(2,1)S(1)} %get-tuple-element.97.refs_0_), channel_id=1, source_target_pairs={{0,1},{1,0},{2,3},{3,2},{4,5},{5,4},{6,7},{7,6},{8,9},{9,8},{10,11... | collective-permute-start | bytes 1572872 | tf_op jit(solution)/shard_map/ppermute | solution.py:302
  23.8 23.5 %collective-permute-start.5 = (bf16[2048,256]{1,0:T(8,128)(2,1)S(1)}, bf16[2048,256]{1,0:T(8,128)(2,1)S(1)}, u32[]{:S(2)}, u32[]{:S(2)}) collective-permute-start(bf16[2048,256]{1,0:T(8,128)(2,1)S(1)} %copy-done.7), channel_id=1, source_target_pairs={{0,16},{4,20},{8,24},{12,28},{16,0},{20,4},{24,8},{28,12},{1,17},{... | collective-permute-start | bytes 3145736 | tf_op jit(solution)/shard_map/ppermute | solution.py:302
  25.1 23.1 %collective-permute-start.4 = (bf16[2048,256]{1,0:T(8,128)(2,1)S(1)}, bf16[2048,256]{1,0:T(8,128)(2,1)S(1)}, u32[]{:S(2)}, u32[]{:S(2)}) collective-permute-start(bf16[2048,256]{1,0:T(8,128)(2,1)S(1)} %copy-done.7), channel_id=1, source_target_pairs={{0,8},{4,12},{8,0},{12,4},{16,24},{20,28},{24,16},{28,20},{1,9},{5... | collective-permute-start | bytes 3145736 | tf_op jit(solution)/shard_map/ppermute | solution.py:302
  28.5 2.0 %collective-permute-start.2 = (bf16[2048,128]{1,0:T(8,128)(2,1)S(1)}, bf16[2048,128]{1,0:T(8,128)(2,1)S(1)}, u32[]{:S(2)}, u32[]{:S(2)}) collective-permute-start(bf16[2048,128]{1,0:T(8,128)(2,1)S(1)} %get-tuple-element.97.refs_0_), channel_id=1, source_target_pairs={{1,2},{2,1},{5,6},{6,5},{9,10},{10,9},{13,14},{14,13},{17,18},{18,... | collective-permute-start | bytes 1572872 | tf_op jit(solution)/shard_map/ppermute | solution.py:320
  29.2 14.3 %collective-permute-start.3 = (bf16[2048,128]{1,0:T(8,128)(2,1)S(1)}, bf16[2048,128]{1,0:T(8,128)(2,1)S(1)}, u32[]{:S(2)}, u32[]{:S(2)}) collective-permute-start(bf16[2048,128]{1,0:T(8,128)(2,1)S(1)} %collective-permute-done.1.refs_2_), channel_id=1, source_target_pairs={{1,0},{2,3},{5,4},{6,7},{9,8},{10,11},{13,12},{14,15},{17,16},{18,... | collective-permute-start | bytes 1572872 | tf_op jit(solution)/shard_map/ppermute | solution.py:320
  48.2 10.6 %copy-start.9 = (bf16[2048,256]{1,0:T(8,128)(2,1)}, bf16[2048,256]{1,0:T(8,128)(2,1)S(1)}, u32[]{:S(2)}) copy-start(bf16[2048,256]{1,0:T(8,128)(2,1)S(1)} %collective-permute-done.4) | copy-start | bytes 3145732
  48.2 26.2 %collective-permute-start.8 = (bf16[2048,256]{1,0:T(8,128)(2,1)S(1)}, bf16[2048,256]{1,0:T(8,128)(2,1)S(1)}, u32[]{:S(2)}, u32[]{:S(2)}) collective-permute-start(bf16[2048,256]{1,0:T(8,128)(2,1)S(1)} %collective-permute-done.4), channel_id=1, source_target_pairs={{0,16},{4,20},{8,24},{12,28},{16,0},{20,4},{24,8},{28,12},{1,17},{... | collective-permute-start | bytes 3145736 | tf_op jit(solution)/shard_map/ppermute | solution.py:302
  48.6 25.9 %collective-permute-start.7 = (bf16[2048,128]{1,0:T(8,128)(2,1)S(1)}, bf16[2048,128]{1,0:T(8,128)(2,1)S(1)}, u32[]{:S(2)}, u32[]{:S(2)}) collective-permute-start(bf16[2048,128]{1,0:T(8,128)(2,1)S(1)} %get-tuple-element.104.refs_0_), channel_id=1, source_target_pairs={{0,2},{1,3},{2,0},{3,1},{4,6},{5,7},{6,4},{7,5},{8,10},{9,11},{10,... | collective-permute-start | bytes 1572872 | tf_op jit(solution)/shard_map/ppermute | solution.py:302
  48.7 25.8 %collective-permute-start.6 = (bf16[2048,128]{1,0:T(8,128)(2,1)S(1)}, bf16[2048,128]{1,0:T(8,128)(2,1)S(1)}, u32[]{:S(2)}, u32[]{:S(2)}) collective-permute-start(bf16[2048,128]{1,0:T(8,128)(2,1)S(1)} %get-tuple-element.104.refs_0_), channel_id=1, source_target_pairs={{0,1},{1,0},{2,3},{3,2},{4,5},{5,4},{6,7},{7,6},{8,9},{9,8},{10,11... | collective-permute-start | bytes 1572872 | tf_op jit(solution)/shard_map/ppermute | solution.py:302
  74.4 11.7 %copy-start.11 = (bf16[2048,256]{1,0:T(8,128)(2,1)}, bf16[2048,256]{1,0:T(8,128)(2,1)S(1)}, u32[]{:S(2)}) copy-start(bf16[2048,256]{1,0:T(8,128)(2,1)S(1)} %collective-permute-done.8) | copy-start | bytes 3145732
  74.5 11.7 %collective-permute-start.11 = (bf16[8192,128]{1,0:T(8,128)(2,1)S(1)}, bf16[8192,128]{1,0:T(8,128)(2,1)S(1)}, u32[]{:S(2)}, u32[]{:S(2)}) collective-permute-start(bf16[8192,128]{1,0:T(8,128)(2,1)S(1)} %get-tuple-element.108), channel_id=1, source_target_pairs={{0,4},{4,0},{8,12},{12,8},{16,20},{20,16},{24,28},{28,24},{1,5},{5... | collective-permute-start | bytes 6291464 | tf_op jit(solution)/shard_map/ppermute | solution.py:302
  75.0 13.8 %collective-permute-start.9 = (bf16[2048,128]{1,0:T(8,128)(2,1)S(1)}, bf16[2048,128]{1,0:T(8,128)(2,1)S(1)}, u32[]{:S(2)}, u32[]{:S(2)}) collective-permute-start(bf16[2048,128]{1,0:T(8,128)(2,1)S(1)} %get-tuple-element.104.refs_0_), channel_id=1, source_target_pairs={{1,2},{2,1},{5,6},{6,5},{9,10},{10,9},{13,14},{14,13},{17,18},{18,... | collective-permute-start | bytes 1572872 | tf_op jit(solution)/shard_map/ppermute | solution.py:320
  75.7 15.5 %collective-permute-start.10 = (bf16[2048,128]{1,0:T(8,128)(2,1)S(1)}, bf16[2048,128]{1,0:T(8,128)(2,1)S(1)}, u32[]{:S(2)}, u32[]{:S(2)}) collective-permute-start(bf16[2048,128]{1,0:T(8,128)(2,1)S(1)} %collective-permute-done.7.refs_2_), channel_id=1, source_target_pairs={{1,0},{2,3},{5,4},{6,7},{9,8},{10,11},{13,12},{14,15},{17,16},{18,... | collective-permute-start | bytes 1572872 | tf_op jit(solution)/shard_map/ppermute | solution.py:320
  86.8 11.1 %collective-permute-start.12 = (bf16[2048,128]{1,0:T(8,128)(2,1)S(1)}, bf16[2048,128]{1,0:T(8,128)(2,1)}, u32[]{:S(2)}, u32[]{:S(2)}) collective-permute-start(bf16[2048,128]{1,0:T(8,128)(2,1)S(1)} %bitcast.61), channel_id=1, source_target_pairs={{0,8},{4,12},{8,0},{12,4},{16,24},{20,28},{24,16},{28,20},{1,9},{5... | collective-permute-start | bytes 1572872 | tf_op jit(solution)/shard_map/ppermute | solution.py:302
  86.8 12.3 %collective-permute-start.13 = (bf16[2048,128]{1,0:T(8,128)(2,1)S(1)}, bf16[2048,128]{1,0:T(8,128)(2,1)}, u32[]{:S(2)}, u32[]{:S(2)}) collective-permute-start(bf16[2048,128]{1,0:T(8,128)(2,1)S(1)} %bitcast.60), channel_id=1, source_target_pairs={{0,16},{4,20},{8,24},{12,28},{16,0},{20,4},{24,8},{28,12},{1,17},{... | collective-permute-start | bytes 1572872 | tf_op jit(solution)/shard_map/ppermute | solution.py:302
  99.2 6.1 %collective-permute-start.14 = (bf16[8192,128]{1,0:T(8,128)(2,1)}, bf16[8192,128]{1,0:T(8,128)(2,1)}, u32[]{:S(2)}, u32[]{:S(2)}) collective-permute-start(bf16[8192,128]{1,0:T(8,128)(2,1)} %get-tuple-element.120), channel_id=1, source_target_pairs={{0,4},{4,0},{8,12},{12,8},{16,20},{20,16},{24,28},{28,24},{1,5},{5... | collective-permute-start | bytes 6291464 | tf_op jit(solution)/shard_map/ppermute | solution.py:302
  100.8 9.5 %collective-permute-start.16 = (bf16[1024,128]{1,0:T(8,128)(2,1)S(1)}, bf16[1024,128]{1,0:T(8,128)(2,1)S(1)}, u32[]{:S(2)}, u32[]{:S(2)}) collective-permute-start(bf16[1024,128]{1,0:T(8,128)(2,1)S(1)} %get-tuple-element.170), channel_id=1, source_target_pairs={{0,8},{4,12},{8,0},{12,4},{16,24},{20,28},{24,16},{28,20},{1,9},{5... | collective-permute-start | bytes 786440 | tf_op jit(solution)/shard_map/ppermute | solution.py:302
  101.1 9.3 %collective-permute-start.15 = (bf16[1024,128]{1,0:T(8,128)(2,1)S(1)}, bf16[1024,128]{1,0:T(8,128)(2,1)S(1)}, u32[]{:S(2)}, u32[]{:S(2)}) collective-permute-start(bf16[1024,128]{1,0:T(8,128)(2,1)S(1)} %get-tuple-element.172), channel_id=1, source_target_pairs={{0,16},{4,20},{8,24},{12,28},{16,0},{20,4},{24,8},{28,12},{1,17},{... | collective-permute-start | bytes 786440 | tf_op jit(solution)/shard_map/ppermute | solution.py:302
  112.3 2.9 %collective-permute-start.19 = (bf16[256,128]{1,0:T(8,128)(2,1)S(1)}, bf16[256,128]{1,0:T(8,128)(2,1)S(1)}, u32[]{:S(2)}, u32[]{:S(2)}) collective-permute-start(bf16[256,128]{1,0:T(8,128)(2,1)S(1)} %get-tuple-element.176), channel_id=1, source_target_pairs={{0,4},{4,0},{8,12},{12,8},{16,20},{20,16},{24,28},{28,24},{1,5},{5... | collective-permute-start | bytes 196616 | tf_op jit(solution)/shard_map/ppermute | solution.py:302
  112.8 13.9 %collective-permute-start.17 = (bf16[2048,128]{1,0:T(8,128)(2,1)S(1)}, bf16[2048,128]{1,0:T(8,128)(2,1)S(1)}, u32[]{:S(2)}, u32[]{:S(2)}) collective-permute-start(bf16[2048,128]{1,0:T(8,128)(2,1)S(1)} %bitcast.58), channel_id=1, source_target_pairs={{0,8},{4,12},{8,0},{12,4},{16,24},{20,28},{24,16},{28,20},{1,9},{5... | collective-permute-start | bytes 1572872 | tf_op jit(solution)/shard_map/ppermute | solution.py:302
  114.6 13.2 %collective-permute-start.18 = (bf16[2048,128]{1,0:T(8,128)(2,1)S(1)}, bf16[2048,128]{1,0:T(8,128)(2,1)S(1)}, u32[]{:S(2)}, u32[]{:S(2)}) collective-permute-start(bf16[2048,128]{1,0:T(8,128)(2,1)S(1)} %bitcast.59), channel_id=1, source_target_pairs={{0,16},{4,20},{8,24},{12,28},{16,0},{20,4},{24,8},{28,12},{1,17},{... | collective-permute-start | bytes 1572872 | tf_op jit(solution)/shard_map/ppermute | solution.py:302
  115.3 5.1 %collective-permute-start.22 = (bf16[256,128]{1,0:T(8,128)(2,1)S(1)}, bf16[256,128]{1,0:T(8,128)(2,1)S(1)}, u32[]{:S(2)}, u32[]{:S(2)}) collective-permute-start(bf16[256,128]{1,0:T(8,128)(2,1)S(1)} %add_convert_fusion.20), channel_id=1, source_target_pairs={{0,3},{1,2},{2,1},{3,0},{4,7},{5,6},{6,5},{7,4},{8,11},{9,10},{10,... | collective-permute-start | bytes 196616 | tf_op jit(solution)/shard_map/ppermute | solution.py:302
  116.0 9.1 %collective-permute-start.21 = (bf16[256,128]{1,0:T(8,128)(2,1)S(1)}, bf16[256,128]{1,0:T(8,128)(2,1)S(1)}, u32[]{:S(2)}, u32[]{:S(2)}) collective-permute-start(bf16[256,128]{1,0:T(8,128)(2,1)S(1)} %add_convert_fusion.20), channel_id=1, source_target_pairs={{0,2},{1,3},{2,0},{3,1},{4,6},{5,7},{6,4},{7,5},{8,10},{9,11},{10,... | collective-permute-start | bytes 196616 | tf_op jit(solution)/shard_map/ppermute | solution.py:302
  118.5 6.6 %collective-permute-start.20 = (bf16[256,128]{1,0:T(8,128)(2,1)S(1)}, bf16[256,128]{1,0:T(8,128)(2,1)S(1)}, u32[]{:S(2)}, u32[]{:S(2)}) collective-permute-start(bf16[256,128]{1,0:T(8,128)(2,1)S(1)} %add_convert_fusion.20), channel_id=1, source_target_pairs={{0,1},{1,0},{2,3},{3,2},{4,5},{5,4},{6,7},{7,6},{8,9},{9,8},{10,11... | collective-permute-start | bytes 196616 | tf_op jit(solution)/shard_map/ppermute | solution.py:302
  128.1 4.2 %collective-permute-start.27 = (bf16[256,128]{1,0:T(8,128)(2,1)S(1)}, bf16[256,128]{1,0:T(8,128)(2,1)S(1)}, u32[]{:S(2)}, u32[]{:S(2)}) collective-permute-start(bf16[256,128]{1,0:T(8,128)(2,1)S(1)} %add_convert_fusion.19), channel_id=1, source_target_pairs={{0,24},{4,28},{8,16},{12,20},{16,8},{20,12},{24,0},{28,4},{1,25},{... | collective-permute-start | bytes 196616 | tf_op jit(solution)/shard_map/ppermute | solution.py:302
  128.9 3.8 %collective-permute-start.26 = (bf16[256,128]{1,0:T(8,128)(2,1)S(1)}, bf16[256,128]{1,0:T(8,128)(2,1)S(1)}, u32[]{:S(2)}, u32[]{:S(2)}) collective-permute-start(bf16[256,128]{1,0:T(8,128)(2,1)S(1)} %add_convert_fusion.19), channel_id=1, source_target_pairs={{0,16},{4,20},{8,24},{12,28},{16,0},{20,4},{24,8},{28,12},{1,17},{... | collective-permute-start | bytes 196616 | tf_op jit(solution)/shard_map/ppermute | solution.py:302
  129.7 3.7 %collective-permute-start.25 = (bf16[256,128]{1,0:T(8,128)(2,1)S(1)}, bf16[256,128]{1,0:T(8,128)(2,1)S(1)}, u32[]{:S(2)}, u32[]{:S(2)}) collective-permute-start(bf16[256,128]{1,0:T(8,128)(2,1)S(1)} %add_convert_fusion.19), channel_id=1, source_target_pairs={{0,8},{4,12},{8,0},{12,4},{16,24},{20,28},{24,16},{28,20},{1,9},{5... | collective-permute-start | bytes 196616 | tf_op jit(solution)/shard_map/ppermute | solution.py:302
  130.8 8.0 %collective-permute-start.23 = (bf16[1024,128]{1,0:T(8,128)(2,1)S(1)}, bf16[1024,128]{1,0:T(8,128)(2,1)S(1)}, u32[]{:S(2)}, u32[]{:S(2)}) collective-permute-start(bf16[1024,128]{1,0:T(8,128)(2,1)S(1)} %get-tuple-element.150), channel_id=1, source_target_pairs={{0,16},{4,20},{8,24},{12,28},{16,0},{20,4},{24,8},{28,12},{1,17},{... | collective-permute-start | bytes 786440 | tf_op jit(solution)/shard_map/ppermute | solution.py:302
  131.6 7.3 %collective-permute-start.24 = (bf16[1024,128]{1,0:T(8,128)(2,1)S(1)}, bf16[1024,128]{1,0:T(8,128)(2,1)S(1)}, u32[]{:S(2)}, u32[]{:S(2)}) collective-permute-start(bf16[1024,128]{1,0:T(8,128)(2,1)S(1)} %get-tuple-element.152), channel_id=1, source_target_pairs={{0,8},{4,12},{8,0},{12,4},{16,24},{20,28},{24,16},{28,20},{1,9},{5... | collective-permute-start | bytes 786440 | tf_op jit(solution)/shard_map/ppermute | solution.py:302
  139.0 3.6 %collective-permute-start.28 = (bf16[256,128]{1,0:T(8,128)(2,1)S(1)}, bf16[256,128]{1,0:T(8,128)(2,1)S(1)}, u32[]{:S(2)}, u32[]{:S(2)}) collective-permute-start(bf16[256,128]{1,0:T(8,128)(2,1)S(1)} %add_convert_fusion.18), channel_id=1, source_target_pairs={{0,4},{4,0},{8,12},{12,8},{16,20},{20,16},{24,28},{28,24},{1,5},{5... | collective-permute-start | bytes 196616 | tf_op jit(solution)/shard_map/ppermute | solution.py:302
  (10 other events, 43.7 us)

commit v6 on v5

--- a/solution.py
+++ b/solution.py
@@ -10,10 +10,12 @@
 SIDE = 128
 UNROLL = 8
 GROUP = 32
+RING = 4
 FIRST_PIECES = 3
 PLAN_ROWS = 8
 FLIP_BYTES = 26 * 1024 * 1024
-SPMM_BYTES = 24 * 1024 * 1024
+PLAN_BYTES = 12 * 1024 * 1024
+SPMM_BYTES = 16 * 1024 * 1024
 
 
 def round_up(value, unit):
@@ -81,7 +83,7 @@
         def placed(values, empty, hit=hit):
             return total_of(jnp.where(hit, values - empty, 0), 0) + empty
 
-        plan_ref[0:1, :] = placed(rank, slots)
+        plan_ref[0:1, :] = placed(rank & (RING * GROUP - 1), RING * GROUP)
         plan_ref[1:2, :] = placed(row_pos_c - p * start, 0)
         taken = total(hit, 0) > 0
         ends = [
@@ -119,7 +121,7 @@
         out_shape=(plan, plan, jax.ShapeDtypeStruct((1, slots), jnp.int32)),
         in_specs=[pl.BlockSpec(memory_space=pltpu.SMEM)] + [pl.BlockSpec(memory_space=pltpu.VMEM)] * 4,
         out_specs=[pl.BlockSpec(memory_space=pltpu.VMEM)] * 3,
-        compiler_params=pltpu.CompilerParams(vmem_limit_bytes=SPMM_BYTES),
+        compiler_params=pltpu.CompilerParams(vmem_limit_bytes=PLAN_BYTES),
         cost_estimate=pl.CostEstimate(flops=0, bytes_accessed=4096, transcendentals=0),
         name="plan_slots",
     )(place, tile_rows.reshape(1, slots), tile_cols.reshape(1, slots), tile_rows.reshape(slots, 1), tile_cols.reshape(slots, 1))
@@ -188,29 +190,24 @@
     out_refs = (rest.pop(0), rest.pop(0))
     m_vmem, t_vmem, total_ref, sems = rest
     nodes, width = pieces[0][0].shape
-    slots = t_vmem.shape[0] - 1
     mid, sent_steps, n_groups, tile_base = [plan_ref[4, n] for n in range(4)]
 
     def group_copy(g):
-        at = pl.multiple_of(g * GROUP, GROUP)
+        place = g & (RING - 1)
         return pltpu.make_async_copy(
-            tiles_ref.at[pl.ds(tile_base + at, GROUP)], t_vmem.at[pl.ds(at, GROUP)], sems.at[g]
+            tiles_ref.at[pl.ds(tile_base + pl.multiple_of(g * GROUP, GROUP), GROUP)],
+            t_vmem.at[pl.ds(pl.multiple_of(place * GROUP, GROUP), GROUP)],
+            sems.at[place],
         )
 
-    def begin_copy(g, carry):
-        group_copy(g).start()
-        return carry
-
-    lax.fori_loop(0, n_groups, begin_copy, 0)
-    t_vmem[slots] = jnp.zeros((SIDE, SIDE), t_vmem.dtype)
+    for g in range(2):
+        pl.when(g < n_groups)(group_copy(g).start)
+    t_vmem[RING * GROUP] = jnp.zeros((SIDE, SIDE), t_vmem.dtype)
     for out_ref, acc_ref in zip(out_refs, acc_refs):
 
         def begin(step, carry, out_ref=out_ref, acc_ref=acc_ref):
             at = pl.ds(pl.multiple_of(step * 256, 256), 256)
-            if last:
-                out_ref[at, :] = acc_ref[at, :].astype(out_ref.dtype)
-            else:
-                out_ref[at, :] = jnp.zeros((256, width), out_ref.dtype)
+            out_ref[at, :] = acc_ref[at, :] if last else jnp.zeros((256, width), out_ref.dtype)
             return carry
 
         lax.fori_loop(0, out_ref.shape[0] // 256, begin, 0)
@@ -244,7 +241,7 @@
         for u in range(UNROLL):
             k = 2 * (step * UNROLL + u)
             at = pl.ds(pl.multiple_of(plan_ref[2, k] * SIDE, SIDE), SIDE)
-            before = acc_ref[at, :] if last else jnp.zeros_like(running)
+            before = acc_ref[at, :].astype(jnp.float32) if last else jnp.zeros_like(running)
             running = prods[u] + jnp.where(plan_ref[3, k] == 1, running, before)
             out_ref[at, :] = running.astype(out_ref.dtype)
         total_ref[...] = running
@@ -254,6 +251,11 @@
 
     def add_group(g, carry):
         group_copy(g).wait()
+
+        @pl.when(g + 2 < n_groups)
+        def _():
+            group_copy(g + 2).start()
+
         low, high = plan_ref[4, 4 + g], plan_ref[4, 5 + g]
         lax.fori_loop(
             jnp.minimum(low, sent_steps), jnp.minimum(high, sent_steps),
@@ -272,8 +274,7 @@
     nodes, width = pieces[0][0].shape
     half = n_row // 2 * nodes
     last = acc is not None
-    slots = tiles.shape[0] - GROUP
-    out = jax.ShapeDtypeStruct((half, width), jnp.bfloat16 if last else jnp.float32)
+    out = jax.ShapeDtypeStruct((half, width), jnp.bfloat16)
     blocks = [ref for p in pieces for ref in p]
     in_vmem, in_any = pl.BlockSpec(memory_space=pltpu.VMEM), pl.BlockSpec(memory_space=pl.ANY)
     return pl.pallas_call(
@@ -286,9 +287,9 @@
             out_specs=[in_vmem] * 2,
             scratch_shapes=[
                 pltpu.VMEM((len(pieces) * nodes, width), jnp.bfloat16),
-                pltpu.VMEM((slots + 1, SIDE, SIDE), jnp.bfloat16),
+                pltpu.VMEM((RING * GROUP + 1, SIDE, SIDE), jnp.bfloat16),
                 pltpu.VMEM((SIDE, width), jnp.float32),
-                pltpu.SemaphoreType.DMA((slots // GROUP,)),
+                pltpu.SemaphoreType.DMA((RING,)),
             ],
         ),
         compiler_params=pltpu.CompilerParams(vmem_limit_bytes=SPMM_BYTES),
@@ -427,7 +428,7 @@
     place = jnp.stack([live_counts.reshape(()), row, col, mid.astype(jnp.int32)])
     plan0, plan1, slot = make_plans(tile_rows, tile_cols, place, n_row, nodes // SIDE)
     flipped = flip_tiles(slot, tiles.reshape(slots, SIDE, SIDE))
-    features, flipped = fence(features, flipped)
+    features, plan0 = fence(features, plan0)
     near = [features]
     for bit in bits[:2]:
         near.append(xor_permute(features, "row", bit))
@@ -468,13 +469,13 @@
     theirs, mine = jnp.where(even, term1, term0), jnp.where(even, term0, term1)
     mine = add_f32(mine, xor_permute(theirs, "row", 1)).astype(jnp.bfloat16)
     mine = sum_over(mine, "col", range(1, n_col)).astype(jnp.bfloat16)
-    recv1, mine = fence(recv1, mine)
+    colgrad0 = exchange_last(rest0, recv0, bits, rows)
+    recv1, mine, colgrad0 = fence(recv1, mine, colgrad0)
 
     rest1, sent1 = exchange_second(stage1, recv1, bits, rows)
     rest1, sent1, mine = fence(rest1, sent1, mine)
     recv1 = send_second(sent1, bits)
     mine = sum_over(mine, "row", range(2, n_row, 2)).astype(jnp.bfloat16)
-    colgrad0 = exchange_last(rest0, recv0, bits, rows)
     colgrad1 = exchange_last(rest1, recv1, bits, rows)
     colgrad1, mine = fence(colgrad1, mine)
 

time: 144 us -> 141 us (0.979)
  waiting for transfers between devices: 52.1 us -> 41 us
  starting transfers between devices: 27.7 us -> 36.2 us
    ppermute x25, waiting for transfers between devices: 36.7 us -> 27.8 us  [xor_permute(): return lax.ppermute(value, axis, [(i, i ^ mask) for i in range(size)])]
    ppermute x25, starting transfers between devices: 23.7 us -> 32.2 us  [xor_permute(): return lax.ppermute(value, axis, [(i, i ^ mask) for i in range(size)])]
    ppermute x2, waiting for transfers between devices: 15.4 us -> 13.2 us  [gather_second(): lax.ppermute(by_two, 'col', ends)]
    pallas_call x4, Pallas kernels: 27.6 us -> 26.2 us  [spmm(): pl.pallas_call(functools.partial(spmm_kernel, [len(p) for p in pieces], l...]
    unnamed x26 -> x24, local copies, waits for them, and re-layouts: 4.26 us -> 4.4 us
  transfers between devices with their start and end apart: 29 -> 29, of which waited for: 16 -> 15; matrix products, arithmetic and copies ran while one was open for 9% -> 10% of each run, Pallas kernels for 28% -> 27%
where the time goes in v6:
time: 141 us; the launch traced here: 140 us
  waiting for transfers between devices  41 us (29%)
  Pallas kernels  38.1 us (27%)
  starting transfers between devices  36.2 us (26%)
  other arithmetic  12.4 us (9%)
  matrix products  5.27 us (4%)
  local copies, waits for them, and re-layouts  4.82 us (3%)
  between operations  1.72 us (1%)
    ppermute x25, starting transfers between devices, xor_permute(): return lax.ppermute(value, axis, [(i, i ^ mask) for i in range(size)])  32.2 us
    ppermute x25, waiting for transfers between devices, xor_permute(): return lax.ppermute(value, axis, [(i, i ^ mask) for i in range(size)])  27.8 us
    pallas_call x4, Pallas kernels, spmm(): pl.pallas_call(functools.partial(spmm_kernel, [len(p) for p in pieces], l...  26.2 us
    ppermute x2, waiting for transfers between devices, gather_second(): lax.ppermute(by_two, 'col', ends)  13.2 us
    pallas_call x1, Pallas kernels, flip_tiles(): pl.pallas_call(flip_kernel, out_shape=jax.ShapeDtypeStruct((slots + GROUP...  9.59 us
    unnamed x24, local copies, waits for them, and re-layouts  4.4 us
    convert_element_type x2, other arithmetic, stage_sums(): return (stage, add_f32(keep, recv).astype(jnp.bfloat16))  4.03 us
    dot_general x8, matrix products, weight_term(): lax.dot_general(f, sums[q * nodes:(q + 1) * nodes], (((0,), (0,)), ((), (...  3.82 us
  transfers between devices with their start and end apart: 29, of which 15 were waited for; matrix products, arithmetic and copies ran while one was open for 10% of the time, Pallas kernels for 27%

profile of v6, /device:TPU:1, one launch (start us, length us, event | category | flops | bytes accessed | tf_op | source)
XLA Modules:
  0.0 139.5 jit_solution(1167422596805521692)
XLA Ops:
  0.7 1.7 %compare_select_fusion = (bf16[2048,128]{1,0:T(8,128)(2,1)S(1)}, bf16[2048,128]{1,0:T(8,128)(2,1)S(1)}) fusion(bf16[2048,256]{1,0:T(8,128)(2,1)} %param.8, bf16[2048,256]{1,0:T(8,128)(2,1)} %param.9), kind=kLoop, calls=%fused_computation.26 | loop fusion | flops 1048576 | bytes 3145728 | tf_op jit(solution)/shard_map/jit(_where)/select_n | solution.py:424
  2.3 3.2 %collective-permute-start.1 = (bf16[2048,128]{1,0:T(8,128)(2,1)S(1)}, bf16[2048,128]{1,0:T(8,128)(2,1)S(1)}, u32[]{:S(2)}, u32[]{:S(2)}) collective-permute-start(bf16[2048,128]{1,0:T(8,128)(2,1)S(1)} %get-tuple-element.98.refs_0_), channel_id=1, source_target_pairs={{0,2},{1,3},{2,0},{3,1},{4,6},{5,7},{6,4},{7,5},{8,10},{9,11},{10,... | collective-permute-start | bytes 1572872 | tf_op jit(solution)/shard_map/ppermute | solution.py:303
  5.5 1.3 collective-permute-start
  7.9 2.3 %plan_slots.1 = (s32[8,512]{1,0:T(8,128)S(1)}, s32[8,512]{1,0:T(8,128)S(1)}, s32[1,320]{1,0:T(1,128)S(1)}) custom-call(s32[4]{0:T(128)S(1)} %pad_add_fusion.place_ref, s32[1,320]{1,0:T(1,128)S(1)} %bitcast.47, s32[1,320]{1,0:T(1,128)S(1)} %bitcast.49, s32[320,1]{1,0:T(8,128)S(1)} %copy.10.rows_c, s32[320,1]{1,0:T(8,128)S(1)} %copy.11.cols_c), custom_call_target="tpu_custom_call" | custom-call | bytes 4096 | tf_op jit(solution)/shard_map/plan_slots/pallas_call | solution.py:119
  10.2 1.3 collective-permute-start.5
  12.7 4.0 %copy-done.1 = bf16[1,1,320,128,128]{4,3,2,1,0:T(8,128)(2,1)S(1)} copy-done((bf16[1,1,320,128,128]{4,3,2,1,0:T(8,128)(2,1)S(1)}, bf16[1,1,320,128,128]{4,3,2,1,0:T(8,128)(2,1)}, u32[]{:S(2)}) %copy-start.1) | copy-done | bytes 10485784
  16.7 9.6 %flip_tiles.1.refs_3_.refs_2_ = bf16[352,128,128]{2,1,0:T(8,128)(2,1)S(1)} custom-call(s32[1,320]{1,0:T(1,128)S(1)} %get-tuple-element.83.slot_ref, bf16[320,128,128]{2,1,0:T(8,128)(2,1)S(1)} %bitcast.41), custom_call_target="tpu_custom_call" | custom-call | bytes 4096 | tf_op jit(solution)/shard_map/flip_tiles/pallas_call | solution.py:162
  26.3 2.2 %collective-permute-done.1.refs_2_ = bf16[2048,128]{1,0:T(8,128)(2,1)S(1)} collective-permute-done((bf16[2048,128]{1,0:T(8,128)(2,1)S(1)}, bf16[2048,128]{1,0:T(8,128)(2,1)S(1)}, u32[]{:S(2)}, u32[]{:S(2)}) %collective-permute-start.1) | collective-permute-done | bytes 524320 | tf_op jit(solution)/shard_map/ppermute | solution.py:303
  30.5 3.4 %collective-permute-done.5 = bf16[2048,256]{1,0:T(8,128)(2,1)S(1)} collective-permute-done((bf16[2048,256]{1,0:T(8,128)(2,1)}, bf16[2048,256]{1,0:T(8,128)(2,1)S(1)}, u32[]{:S(2)}, u32[]{:S(2)}) %collective-permute-start.5) | collective-permute-done | bytes 1048608 | tf_op jit(solution)/shard_map/ppermute | solution.py:303
  34.9 8.6 %collective-permute-done.3.refs_1_ = bf16[2048,128]{1,0:T(8,128)(2,1)S(1)} collective-permute-done((bf16[2048,128]{1,0:T(8,128)(2,1)S(1)}, bf16[2048,128]{1,0:T(8,128)(2,1)S(1)}, u32[]{:S(2)}, u32[]{:S(2)}) %collective-permute-start.3) | collective-permute-done | bytes 524320 | tf_op jit(solution)/shard_map/ppermute | solution.py:321
  44.7 2.6 %collective-permute-start.7 = (bf16[2048,128]{1,0:T(8,128)(2,1)S(1)}, bf16[2048,128]{1,0:T(8,128)(2,1)S(1)}, u32[]{:S(2)}, u32[]{:S(2)}) collective-permute-start(bf16[2048,128]{1,0:T(8,128)(2,1)S(1)} %get-tuple-element.105.refs_0_), channel_id=1, source_target_pairs={{0,2},{1,3},{2,0},{3,1},{4,6},{5,7},{6,4},{7,5},{8,10},{9,11},{10,... | collective-permute-start | bytes 1572872 | tf_op jit(solution)/shard_map/ppermute | solution.py:303
  47.3 2.2 %collective-permute-start.6 = (bf16[2048,128]{1,0:T(8,128)(2,1)S(1)}, bf16[2048,128]{1,0:T(8,128)(2,1)S(1)}, u32[]{:S(2)}, u32[]{:S(2)}) collective-permute-start(bf16[2048,128]{1,0:T(8,128)(2,1)S(1)} %get-tuple-element.105.refs_0_), channel_id=1, source_target_pairs={{0,1},{1,0},{2,3},{3,2},{4,5},{5,4},{6,7},{7,6},{8,9},{9,8},{10,11... | collective-permute-start | bytes 1572872 | tf_op jit(solution)/shard_map/ppermute | solution.py:303
  49.5 7.9 %spmm_first.2 = (bf16[8192,128]{1,0:T(8,128)(2,1)S(1)}, bf16[8192,128]{1,0:T(8,128)(2,1)S(1)}) custom-call(s32[8,512]{1,0:T(8,128)S(1)} %get-tuple-element.97.plan_ref, bf16[2048,128]{1,0:T(8,128)(2,1)S(1)} %get-tuple-element.98.refs_0_, bf16[2048,128]{1,0:T(8,128)(2,1)S(1)} %collective-permute-done.refs_1_, ...), custom_call_target="tpu_custom_call" | custom-call | bytes 4096 | tf_op jit(solution)/shard_map/spmm_first/pallas_call | solution.py:280
  57.4 4.4 %spmm_last.2 = (bf16[8192,128]{1,0:T(8,128)(2,1)S(1)}, bf16[8192,128]{1,0:T(8,128)(2,1)S(1)}) custom-call(s32[8,512]{1,0:T(8,128)S(1)} %get-tuple-element.84.plan_ref, bf16[2048,128]{1,0:T(8,128)(2,1)S(1)} %collective-permute-done.2.refs_0_, bf16[2048,128]{1,0:T(8,128)(2,1)S(1)} %collective-permute-done.3.refs_1_, ...), custom_call_target="tpu_custom_call" | custom-call | bytes 4096 | tf_op jit(solution)/shard_map/spmm_last/pallas_call | solution.py:280
  61.9 7.1 %collective-permute-done.7.refs_2_ = bf16[2048,128]{1,0:T(8,128)(2,1)S(1)} collective-permute-done((bf16[2048,128]{1,0:T(8,128)(2,1)S(1)}, bf16[2048,128]{1,0:T(8,128)(2,1)S(1)}, u32[]{:S(2)}, u32[]{:S(2)}) %collective-permute-start.7) | collective-permute-done | bytes 524320 | tf_op jit(solution)/shard_map/ppermute | solution.py:303
  69.0 2.6 %collective-permute-start.11 = (bf16[8192,128]{1,0:T(8,128)(2,1)S(1)}, bf16[8192,128]{1,0:T(8,128)(2,1)S(1)}, u32[]{:S(2)}, u32[]{:S(2)}) collective-permute-start(bf16[8192,128]{1,0:T(8,128)(2,1)S(1)} %get-tuple-element.109), channel_id=1, source_target_pairs={{0,4},{4,0},{8,12},{12,8},{16,20},{20,16},{24,28},{28,24},{1,5},{5... | collective-permute-start | bytes 6291464 | tf_op jit(solution)/shard_map/ppermute | solution.py:303
  73.6 7.9 %spmm_first.3 = (bf16[8192,128]{1,0:T(8,128)(2,1)S(1)}, bf16[8192,128]{1,0:T(8,128)(2,1)S(1)}) custom-call(s32[8,512]{1,0:T(8,128)S(1)} %get-tuple-element.97.plan_ref, bf16[2048,128]{1,0:T(8,128)(2,1)S(1)} %get-tuple-element.105.refs_0_, bf16[2048,128]{1,0:T(8,128)(2,1)S(1)} %collective-permute-done.6.refs_1_, ...), custom_call_target="tpu_custom_call" | custom-call | bytes 4096 | tf_op jit(solution)/shard_map/spmm_first/pallas_call | solution.py:280
  82.8 1.9 %add_convert_fusion.1 = bf16[8192,128]{1,0:T(8,128)(2,1)} fusion(bf16[8192,128]{1,0:T(8,128)(2,1)S(1)} %collective-permute-done.11, bf16[8192,128]{1,0:T(8,128)(2,1)S(1)} %get-tuple-element.108), kind=kLoop, calls=%fused_computation.1 | loop fusion | flops 4194304 | bytes 6291456 | tf_op jit(solution)/shard_map/convert_element_type | solution.py:356
  84.7 4.6 %collective-permute-done.10.refs_1_ = bf16[2048,128]{1,0:T(8,128)(2,1)S(1)} collective-permute-done((bf16[2048,128]{1,0:T(8,128)(2,1)S(1)}, bf16[2048,128]{1,0:T(8,128)(2,1)S(1)}, u32[]{:S(2)}, u32[]{:S(2)}) %collective-permute-start.10) | collective-permute-done | bytes 524320 | tf_op jit(solution)/shard_map/ppermute | solution.py:321
  89.3 6.0 %spmm_last.3 = (bf16[8192,128]{1,0:T(8,128)(2,1)}, bf16[8192,128]{1,0:T(8,128)(2,1)S(1)}) custom-call(s32[8,512]{1,0:T(8,128)S(1)} %get-tuple-element.84.plan_ref, bf16[2048,128]{1,0:T(8,128)(2,1)S(1)} %collective-permute-done.9.refs_0_, bf16[2048,128]{1,0:T(8,128)(2,1)S(1)} %collective-permute-done.10.refs_1_, ...), custom_call_target="tpu_custom_call" | custom-call | bytes 4096 | tf_op jit(solution)/shard_map/spmm_last/pallas_call | solution.py:280
  96.7 1.6 %add_convert_fusion.4 = (bf16[2048,128]{1,0:T(8,128)(2,1)S(1)}, bf16[2048,128]{1,0:T(8,128)(2,1)S(1)}) fusion(bf16[2048,128]{1,0:T(8,128)(2,1)} %collective-permute-done.13, bf16[2048,128]{1,0:T(8,128)(2,1)S(1)} %bitcast.57, bf16[2048,128]{1,0:T(8,128)(2,1)} %collective-permute-done.12, bf16[2048,128]{1,0:T(8,128)(2,1)S(1)} %bitcast.56), kind=kLoop, calls=%fused_computation.16 | loop fusion | flops 2097152 | bytes 3145728 | tf_op jit(solution)/shard_map/convert_element_type | solution.py:377
  101.5 1.5 %add_convert_fusion.8 = (bf16[2,1,1,1024,128]{4,3,2,1,0:T(8,128)(2,1)S(1)}, bf16[2,1,1,1024,128]{4,3,2,1,0:T(8,128)(2,1)S(1)}) fusion(bf16[2,2,2,1024,128]{4,3,2,1,0:T(8,128)(2,1)} %bitcast.16, bf16[2,2,2,1024,128]{4,3,2,1,0:T(8,128)(2,1)S(1)} %bitcast.42), kind=kLoop, calls=%fused_computation.20 | loop fusion | flops 2097152 | bytes 3145728 | tf_op jit(solution)/shard_map/convert_element_type | solution.py:348
  103.0 2.1 %add_convert_fusion = bf16[8192,128]{1,0:T(8,128)(2,1)S(1)} fusion(bf16[8192,128]{1,0:T(8,128)(2,1)} %collective-permute-done.14, bf16[8192,128]{1,0:T(8,128)(2,1)S(1)} %get-tuple-element.120), kind=kLoop, calls=%fused_computation | loop fusion | flops 4194304 | bytes 6291456 | tf_op jit(solution)/shard_map/convert_element_type | solution.py:356
  105.1 1.5 %add_convert_fusion.6 = (bf16[1,2,1,1024,128]{4,3,2,1,0:T(8,128)(2,1)S(1)}, bf16[1,2,1,1024,128]{4,3,2,1,0:T(8,128)(2,1)S(1)}) fusion(bf16[2,2,2,1024,128]{4,3,2,1,0:T(8,128)(2,1)} %bitcast.16, bf16[2,2,2,1024,128]{4,3,2,1,0:T(8,128)(2,1)S(1)} %bitcast.43), kind=kLoop, calls=%fused_computation.18 | loop fusion | flops 2097152 | bytes 3145728 | tf_op jit(solution)/shard_map/convert_element_type | solution.py:348
  109.3 1.5 %collective-permute-start.17 = (bf16[2048,128]{1,0:T(8,128)(2,1)S(1)}, bf16[2048,128]{1,0:T(8,128)(2,1)S(1)}, u32[]{:S(2)}, u32[]{:S(2)}) collective-permute-start(bf16[2048,128]{1,0:T(8,128)(2,1)S(1)} %bitcast.58), channel_id=1, source_target_pairs={{0,8},{4,12},{8,0},{12,4},{16,24},{20,28},{24,16},{28,20},{1,9},{5... | collective-permute-start | bytes 1572872 | tf_op jit(solution)/shard_map/ppermute | solution.py:303
  111.6 3.7 %collective-permute-start.22 = (bf16[256,128]{1,0:T(8,128)(2,1)S(1)}, bf16[256,128]{1,0:T(8,128)(2,1)S(1)}, u32[]{:S(2)}, u32[]{:S(2)}) collective-permute-start(bf16[256,128]{1,0:T(8,128)(2,1)S(1)} %add_convert_fusion.20), channel_id=1, source_target_pairs={{0,3},{1,2},{2,1},{3,0},{4,7},{5,6},{6,5},{7,4},{8,11},{9,10},{10,... | collective-permute-start | bytes 196616 | tf_op jit(solution)/shard_map/ppermute | solution.py:303
  115.3 1.8 %collective-permute-start.21 = (bf16[256,128]{1,0:T(8,128)(2,1)S(1)}, bf16[256,128]{1,0:T(8,128)(2,1)S(1)}, u32[]{:S(2)}, u32[]{:S(2)}) collective-permute-start(bf16[256,128]{1,0:T(8,128)(2,1)S(1)} %add_convert_fusion.20), channel_id=1, source_target_pairs={{0,2},{1,3},{2,0},{3,1},{4,6},{5,7},{6,4},{7,5},{8,10},{9,11},{10,... | collective-permute-start | bytes 196616 | tf_op jit(solution)/shard_map/ppermute | solution.py:303
  117.1 2.6 %collective-permute-done.21 = bf16[256,128]{1,0:T(8,128)(2,1)S(1)} collective-permute-done((bf16[256,128]{1,0:T(8,128)(2,1)S(1)}, bf16[256,128]{1,0:T(8,128)(2,1)S(1)}, u32[]{:S(2)}, u32[]{:S(2)}) %collective-permute-start.21) | collective-permute-done | bytes 65568 | tf_op jit(solution)/shard_map/ppermute | solution.py:303
  120.6 2.2 %collective-permute-done.17 = bf16[2048,128]{1,0:T(8,128)(2,1)S(1)} collective-permute-done((bf16[2048,128]{1,0:T(8,128)(2,1)S(1)}, bf16[2048,128]{1,0:T(8,128)(2,1)S(1)}, u32[]{:S(2)}, u32[]{:S(2)}) %collective-permute-start.17) | collective-permute-done | bytes 524320 | tf_op jit(solution)/shard_map/ppermute | solution.py:303
  129.3 6.1 %collective-permute-done.23 = bf16[1024,128]{1,0:T(8,128)(2,1)S(1)} collective-permute-done((bf16[1024,128]{1,0:T(8,128)(2,1)S(1)}, bf16[1024,128]{1,0:T(8,128)(2,1)S(1)}, u32[]{:S(2)}, u32[]{:S(2)}) %collective-permute-start.23) | collective-permute-done | bytes 262176 | tf_op jit(solution)/shard_map/ppermute | solution.py:303
  135.6 1.7 %collective-permute-start.28 = (bf16[256,128]{1,0:T(8,128)(2,1)S(1)}, bf16[256,128]{1,0:T(8,128)(2,1)S(1)}, u32[]{:S(2)}, u32[]{:S(2)}) collective-permute-start(bf16[256,128]{1,0:T(8,128)(2,1)S(1)} %add_convert_fusion.18), channel_id=1, source_target_pairs={{0,4},{4,0},{8,12},{12,8},{16,20},{20,16},{24,28},{28,24},{1,5},{5... | collective-permute-start | bytes 196616 | tf_op jit(solution)/shard_map/ppermute | solution.py:303
  137.3 1.4 %convolution_convert_fusion = bf16[2048,256]{1,0:T(8,128)(2,1)} fusion(bf16[256,256]{1,0:T(8,128)(2,1)S(1)} %copy-done, bf16[2048,128]{1,0:T(8,128)(2,1)S(1)} %pad_maximum_fusion.1, bf16[2048,128]{1,0:T(8,128)(2,1)S(1)} %pad_maximum_fusion), kind=kOutput, calls=%fused_computation.2 | convolution fusion | flops 271056896 | bytes 2228224 | tf_op jit(solution)/shard_map/dot_general | solution.py:486
  (93 shorter events, 25.3 us)
Async XLA Ops:
  0.6 136.7 %copy-start = (bf16[256,256]{1,0:T(8,128)(2,1)S(1)}, bf16[256,256]{1,0:T(8,128)(2,1)}, u32[]{:S(2)}) copy-start(bf16[256,256]{1,0:T(8,128)(2,1)} %param.11) | copy-start | bytes 393220
  2.3 26.1 %collective-permute-start.1 = (bf16[2048,128]{1,0:T(8,128)(2,1)S(1)}, bf16[2048,128]{1,0:T(8,128)(2,1)S(1)}, u32[]{:S(2)}, u32[]{:S(2)}) collective-permute-start(bf16[2048,128]{1,0:T(8,128)(2,1)S(1)} %get-tuple-element.98.refs_0_), channel_id=1, source_target_pairs={{0,2},{1,3},{2,0},{3,1},{4,6},{5,7},{6,4},{7,5},{8,10},{9,11},{10,... | collective-permute-start | bytes 1572872 | tf_op jit(solution)/shard_map/ppermute | solution.py:303
  5.5 22.9 %collective-permute-start = (bf16[2048,128]{1,0:T(8,128)(2,1)S(1)}, bf16[2048,128]{1,0:T(8,128)(2,1)S(1)}, u32[]{:S(2)}, u32[]{:S(2)}) collective-permute-start(bf16[2048,128]{1,0:T(8,128)(2,1)S(1)} %get-tuple-element.98.refs_0_), channel_id=1, source_target_pairs={{0,1},{1,0},{2,3},{3,2},{4,5},{5,4},{6,7},{7,6},{8,9},{9,8},{10,11... | collective-permute-start | bytes 1572872 | tf_op jit(solution)/shard_map/ppermute | solution.py:303
  10.2 23.7 %collective-permute-start.5 = (bf16[2048,256]{1,0:T(8,128)(2,1)}, bf16[2048,256]{1,0:T(8,128)(2,1)S(1)}, u32[]{:S(2)}, u32[]{:S(2)}) collective-permute-start(bf16[2048,256]{1,0:T(8,128)(2,1)} %param.10), channel_id=1, source_target_pairs={{0,16},{4,20},{8,24},{12,28},{16,0},{20,4},{24,8},{28,12},{1,17},{... | collective-permute-start | bytes 3145736 | tf_op jit(solution)/shard_map/ppermute | solution.py:303
  11.5 23.3 %collective-permute-start.4 = (bf16[2048,256]{1,0:T(8,128)(2,1)}, bf16[2048,256]{1,0:T(8,128)(2,1)S(1)}, u32[]{:S(2)}, u32[]{:S(2)}) collective-permute-start(bf16[2048,256]{1,0:T(8,128)(2,1)} %param.10), channel_id=1, source_target_pairs={{0,8},{4,12},{8,0},{12,4},{16,24},{20,28},{24,16},{28,20},{1,9},{5... | collective-permute-start | bytes 3145736 | tf_op jit(solution)/shard_map/ppermute | solution.py:303
  28.5 6.4 %collective-permute-start.2 = (bf16[2048,128]{1,0:T(8,128)(2,1)S(1)}, bf16[2048,128]{1,0:T(8,128)(2,1)S(1)}, u32[]{:S(2)}, u32[]{:S(2)}) collective-permute-start(bf16[2048,128]{1,0:T(8,128)(2,1)S(1)} %get-tuple-element.98.refs_0_), channel_id=1, source_target_pairs={{1,2},{2,1},{5,6},{6,5},{9,10},{10,9},{13,14},{14,13},{17,18},{18,... | collective-permute-start | bytes 1572872 | tf_op jit(solution)/shard_map/ppermute | solution.py:321
  29.2 14.3 %collective-permute-start.3 = (bf16[2048,128]{1,0:T(8,128)(2,1)S(1)}, bf16[2048,128]{1,0:T(8,128)(2,1)S(1)}, u32[]{:S(2)}, u32[]{:S(2)}) collective-permute-start(bf16[2048,128]{1,0:T(8,128)(2,1)S(1)} %collective-permute-done.1.refs_2_), channel_id=1, source_target_pairs={{1,0},{2,3},{5,4},{6,7},{9,8},{10,11},{13,12},{14,15},{17,16},{18,... | collective-permute-start | bytes 1572872 | tf_op jit(solution)/shard_map/ppermute | solution.py:321
  33.9 23.5 %copy-start.5 = (bf16[2048,256]{1,0:T(8,128)(2,1)}, bf16[2048,256]{1,0:T(8,128)(2,1)S(1)}, u32[]{:S(2)}) copy-start(bf16[2048,256]{1,0:T(8,128)(2,1)S(1)} %collective-permute-done.5) | copy-start | bytes 3145732
  34.9 22.6 %copy-start.8 = (bf16[2048,256]{1,0:T(8,128)(2,1)}, bf16[2048,256]{1,0:T(8,128)(2,1)S(1)}, u32[]{:S(2)}) copy-start(bf16[2048,256]{1,0:T(8,128)(2,1)S(1)} %collective-permute-done.4) | copy-start | bytes 3145732
  43.5 25.6 %collective-permute-start.8 = (bf16[2048,256]{1,0:T(8,128)(2,1)S(1)}, bf16[2048,256]{1,0:T(8,128)(2,1)S(1)}, u32[]{:S(2)}, u32[]{:S(2)}) collective-permute-start(bf16[2048,256]{1,0:T(8,128)(2,1)S(1)} %collective-permute-done.4), channel_id=1, source_target_pairs={{0,16},{4,20},{8,24},{12,28},{16,0},{20,4},{24,8},{28,12},{1,17},{... | collective-permute-start | bytes 3145736 | tf_op jit(solution)/shard_map/ppermute | solution.py:303
  44.7 24.3 %collective-permute-start.7 = (bf16[2048,128]{1,0:T(8,128)(2,1)S(1)}, bf16[2048,128]{1,0:T(8,128)(2,1)S(1)}, u32[]{:S(2)}, u32[]{:S(2)}) collective-permute-start(bf16[2048,128]{1,0:T(8,128)(2,1)S(1)} %get-tuple-element.105.refs_0_), channel_id=1, source_target_pairs={{0,2},{1,3},{2,0},{3,1},{4,6},{5,7},{6,4},{7,5},{8,10},{9,11},{10,... | collective-permute-start | bytes 1572872 | tf_op jit(solution)/shard_map/ppermute | solution.py:303
  47.3 21.7 %collective-permute-start.6 = (bf16[2048,128]{1,0:T(8,128)(2,1)S(1)}, bf16[2048,128]{1,0:T(8,128)(2,1)S(1)}, u32[]{:S(2)}, u32[]{:S(2)}) collective-permute-start(bf16[2048,128]{1,0:T(8,128)(2,1)S(1)} %get-tuple-element.105.refs_0_), channel_id=1, source_target_pairs={{0,1},{1,0},{2,3},{3,2},{4,5},{5,4},{6,7},{7,6},{8,9},{9,8},{10,11... | collective-permute-start | bytes 1572872 | tf_op jit(solution)/shard_map/ppermute | solution.py:303
  69.0 12.5 %collective-permute-start.11 = (bf16[8192,128]{1,0:T(8,128)(2,1)S(1)}, bf16[8192,128]{1,0:T(8,128)(2,1)S(1)}, u32[]{:S(2)}, u32[]{:S(2)}) collective-permute-start(bf16[8192,128]{1,0:T(8,128)(2,1)S(1)} %get-tuple-element.109), channel_id=1, source_target_pairs={{0,4},{4,0},{8,12},{12,8},{16,20},{20,16},{24,28},{28,24},{1,5},{5... | collective-permute-start | bytes 6291464 | tf_op jit(solution)/shard_map/ppermute | solution.py:303
  71.6 13.1 %collective-permute-start.9 = (bf16[2048,128]{1,0:T(8,128)(2,1)S(1)}, bf16[2048,128]{1,0:T(8,128)(2,1)S(1)}, u32[]{:S(2)}, u32[]{:S(2)}) collective-permute-start(bf16[2048,128]{1,0:T(8,128)(2,1)S(1)} %get-tuple-element.105.refs_0_), channel_id=1, source_target_pairs={{1,2},{2,1},{5,6},{6,5},{9,10},{10,9},{13,14},{14,13},{17,18},{18,... | collective-permute-start | bytes 1572872 | tf_op jit(solution)/shard_map/ppermute | solution.py:321
  72.3 17.0 %collective-permute-start.10 = (bf16[2048,128]{1,0:T(8,128)(2,1)S(1)}, bf16[2048,128]{1,0:T(8,128)(2,1)S(1)}, u32[]{:S(2)}, u32[]{:S(2)}) collective-permute-start(bf16[2048,128]{1,0:T(8,128)(2,1)S(1)} %collective-permute-done.7.refs_2_), channel_id=1, source_target_pairs={{1,0},{2,3},{5,4},{6,7},{9,8},{10,11},{13,12},{14,15},{17,16},{18,... | collective-permute-start | bytes 1572872 | tf_op jit(solution)/shard_map/ppermute | solution.py:321
  82.1 13.2 %collective-permute-start.12 = (bf16[2048,128]{1,0:T(8,128)(2,1)S(1)}, bf16[2048,128]{1,0:T(8,128)(2,1)}, u32[]{:S(2)}, u32[]{:S(2)}) collective-permute-start(bf16[2048,128]{1,0:T(8,128)(2,1)S(1)} %bitcast.61), channel_id=1, source_target_pairs={{0,8},{4,12},{8,0},{12,4},{16,24},{20,28},{24,16},{28,20},{1,9},{5... | collective-permute-start | bytes 1572872 | tf_op jit(solution)/shard_map/ppermute | solution.py:303
  82.2 13.2 %collective-permute-start.13 = (bf16[2048,128]{1,0:T(8,128)(2,1)S(1)}, bf16[2048,128]{1,0:T(8,128)(2,1)}, u32[]{:S(2)}, u32[]{:S(2)}) collective-permute-start(bf16[2048,128]{1,0:T(8,128)(2,1)S(1)} %bitcast.60), channel_id=1, source_target_pairs={{0,16},{4,20},{8,24},{12,28},{16,0},{20,4},{24,8},{28,12},{1,17},{... | collective-permute-start | bytes 1572872 | tf_op jit(solution)/shard_map/ppermute | solution.py:303
  95.4 6.0 %collective-permute-start.14 = (bf16[8192,128]{1,0:T(8,128)(2,1)}, bf16[8192,128]{1,0:T(8,128)(2,1)}, u32[]{:S(2)}, u32[]{:S(2)}) collective-permute-start(bf16[8192,128]{1,0:T(8,128)(2,1)} %get-tuple-element.121), channel_id=1, source_target_pairs={{0,4},{4,0},{8,12},{12,8},{16,20},{20,16},{24,28},{28,24},{1,5},{5... | collective-permute-start | bytes 6291464 | tf_op jit(solution)/shard_map/ppermute | solution.py:303
  98.4 8.2 %collective-permute-start.16 = (bf16[1024,128]{1,0:T(8,128)(2,1)S(1)}, bf16[1024,128]{1,0:T(8,128)(2,1)S(1)}, u32[]{:S(2)}, u32[]{:S(2)}) collective-permute-start(bf16[1024,128]{1,0:T(8,128)(2,1)S(1)} %get-tuple-element.172), channel_id=1, source_target_pairs={{0,8},{4,12},{8,0},{12,4},{16,24},{20,28},{24,16},{28,20},{1,9},{5... | collective-permute-start | bytes 786440 | tf_op jit(solution)/shard_map/ppermute | solution.py:303
  98.5 8.1 %collective-permute-start.15 = (bf16[1024,128]{1,0:T(8,128)(2,1)S(1)}, bf16[1024,128]{1,0:T(8,128)(2,1)S(1)}, u32[]{:S(2)}, u32[]{:S(2)}) collective-permute-start(bf16[1024,128]{1,0:T(8,128)(2,1)S(1)} %get-tuple-element.174), channel_id=1, source_target_pairs={{0,16},{4,20},{8,24},{12,28},{16,0},{20,4},{24,8},{28,12},{1,17},{... | collective-permute-start | bytes 786440 | tf_op jit(solution)/shard_map/ppermute | solution.py:303
  108.5 3.0 %collective-permute-start.19 = (bf16[256,128]{1,0:T(8,128)(2,1)S(1)}, bf16[256,128]{1,0:T(8,128)(2,1)S(1)}, u32[]{:S(2)}, u32[]{:S(2)}) collective-permute-start(bf16[256,128]{1,0:T(8,128)(2,1)S(1)} %get-tuple-element.178), channel_id=1, source_target_pairs={{0,4},{4,0},{8,12},{12,8},{16,20},{20,16},{24,28},{28,24},{1,5},{5... | collective-permute-start | bytes 196616 | tf_op jit(solution)/shard_map/ppermute | solution.py:303
  109.3 13.5 %collective-permute-start.17 = (bf16[2048,128]{1,0:T(8,128)(2,1)S(1)}, bf16[2048,128]{1,0:T(8,128)(2,1)S(1)}, u32[]{:S(2)}, u32[]{:S(2)}) collective-permute-start(bf16[2048,128]{1,0:T(8,128)(2,1)S(1)} %bitcast.58), channel_id=1, source_target_pairs={{0,8},{4,12},{8,0},{12,4},{16,24},{20,28},{24,16},{28,20},{1,9},{5... | collective-permute-start | bytes 1572872 | tf_op jit(solution)/shard_map/ppermute | solution.py:303
  110.7 13.2 %collective-permute-start.18 = (bf16[2048,128]{1,0:T(8,128)(2,1)S(1)}, bf16[2048,128]{1,0:T(8,128)(2,1)S(1)}, u32[]{:S(2)}, u32[]{:S(2)}) collective-permute-start(bf16[2048,128]{1,0:T(8,128)(2,1)S(1)} %bitcast.59), channel_id=1, source_target_pairs={{0,16},{4,20},{8,24},{12,28},{16,0},{20,4},{24,8},{28,12},{1,17},{... | collective-permute-start | bytes 1572872 | tf_op jit(solution)/shard_map/ppermute | solution.py:303
  111.6 5.5 %collective-permute-start.22 = (bf16[256,128]{1,0:T(8,128)(2,1)S(1)}, bf16[256,128]{1,0:T(8,128)(2,1)S(1)}, u32[]{:S(2)}, u32[]{:S(2)}) collective-permute-start(bf16[256,128]{1,0:T(8,128)(2,1)S(1)} %add_convert_fusion.20), channel_id=1, source_target_pairs={{0,3},{1,2},{2,1},{3,0},{4,7},{5,6},{6,5},{7,4},{8,11},{9,10},{10,... | collective-permute-start | bytes 196616 | tf_op jit(solution)/shard_map/ppermute | solution.py:303
  115.3 4.4 %collective-permute-start.21 = (bf16[256,128]{1,0:T(8,128)(2,1)S(1)}, bf16[256,128]{1,0:T(8,128)(2,1)S(1)}, u32[]{:S(2)}, u32[]{:S(2)}) collective-permute-start(bf16[256,128]{1,0:T(8,128)(2,1)S(1)} %add_convert_fusion.20), channel_id=1, source_target_pairs={{0,2},{1,3},{2,0},{3,1},{4,6},{5,7},{6,4},{7,5},{8,10},{9,11},{10,... | collective-permute-start | bytes 196616 | tf_op jit(solution)/shard_map/ppermute | solution.py:303
  117.0 3.5 %collective-permute-start.20 = (bf16[256,128]{1,0:T(8,128)(2,1)S(1)}, bf16[256,128]{1,0:T(8,128)(2,1)S(1)}, u32[]{:S(2)}, u32[]{:S(2)}) collective-permute-start(bf16[256,128]{1,0:T(8,128)(2,1)S(1)} %add_convert_fusion.20), channel_id=1, source_target_pairs={{0,1},{1,0},{2,3},{3,2},{4,5},{5,4},{6,7},{7,6},{8,9},{9,8},{10,11... | collective-permute-start | bytes 196616 | tf_op jit(solution)/shard_map/ppermute | solution.py:303
  124.3 4.2 %collective-permute-start.27 = (bf16[256,128]{1,0:T(8,128)(2,1)S(1)}, bf16[256,128]{1,0:T(8,128)(2,1)S(1)}, u32[]{:S(2)}, u32[]{:S(2)}) collective-permute-start(bf16[256,128]{1,0:T(8,128)(2,1)S(1)} %add_convert_fusion.19), channel_id=1, source_target_pairs={{0,24},{4,28},{8,16},{12,20},{16,8},{20,12},{24,0},{28,4},{1,25},{... | collective-permute-start | bytes 196616 | tf_op jit(solution)/shard_map/ppermute | solution.py:303
  125.2 3.8 %collective-permute-start.26 = (bf16[256,128]{1,0:T(8,128)(2,1)S(1)}, bf16[256,128]{1,0:T(8,128)(2,1)S(1)}, u32[]{:S(2)}, u32[]{:S(2)}) collective-permute-start(bf16[256,128]{1,0:T(8,128)(2,1)S(1)} %add_convert_fusion.19), channel_id=1, source_target_pairs={{0,16},{4,20},{8,24},{12,28},{16,0},{20,4},{24,8},{28,12},{1,17},{... | collective-permute-start | bytes 196616 | tf_op jit(solution)/shard_map/ppermute | solution.py:303
  125.9 3.4 %collective-permute-start.25 = (bf16[256,128]{1,0:T(8,128)(2,1)S(1)}, bf16[256,128]{1,0:T(8,128)(2,1)S(1)}, u32[]{:S(2)}, u32[]{:S(2)}) collective-permute-start(bf16[256,128]{1,0:T(8,128)(2,1)S(1)} %add_convert_fusion.19), channel_id=1, source_target_pairs={{0,8},{4,12},{8,0},{12,4},{16,24},{20,28},{24,16},{28,20},{1,9},{5... | collective-permute-start | bytes 196616 | tf_op jit(solution)/shard_map/ppermute | solution.py:303
  127.0 8.4 %collective-permute-start.23 = (bf16[1024,128]{1,0:T(8,128)(2,1)S(1)}, bf16[1024,128]{1,0:T(8,128)(2,1)S(1)}, u32[]{:S(2)}, u32[]{:S(2)}) collective-permute-start(bf16[1024,128]{1,0:T(8,128)(2,1)S(1)} %get-tuple-element.152), channel_id=1, source_target_pairs={{0,16},{4,20},{8,24},{12,28},{16,0},{20,4},{24,8},{28,12},{1,17},{... | collective-permute-start | bytes 786440 | tf_op jit(solution)/shard_map/ppermute | solution.py:303
  127.7 7.8 %collective-permute-start.24 = (bf16[1024,128]{1,0:T(8,128)(2,1)S(1)}, bf16[1024,128]{1,0:T(8,128)(2,1)S(1)}, u32[]{:S(2)}, u32[]{:S(2)}) collective-permute-start(bf16[1024,128]{1,0:T(8,128)(2,1)S(1)} %get-tuple-element.154), channel_id=1, source_target_pairs={{0,8},{4,12},{8,0},{12,4},{16,24},{20,28},{24,16},{28,20},{1,9},{5... | collective-permute-start | bytes 786440 | tf_op jit(solution)/shard_map/ppermute | solution.py:303
  135.6 3.1 %collective-permute-start.28 = (bf16[256,128]{1,0:T(8,128)(2,1)S(1)}, bf16[256,128]{1,0:T(8,128)(2,1)S(1)}, u32[]{:S(2)}, u32[]{:S(2)}) collective-permute-start(bf16[256,128]{1,0:T(8,128)(2,1)S(1)} %add_convert_fusion.18), channel_id=1, source_target_pairs={{0,4},{4,0},{8,12},{12,8},{16,20},{20,16},{24,28},{28,24},{1,5},{5... | collective-permute-start | bytes 196616 | tf_op jit(solution)/shard_map/ppermute | solution.py:303
  (9 other events, 39.6 us)

commit v7 on v6

--- a/solution.py
+++ b/solution.py
@@ -108,7 +108,8 @@
         for n, value in enumerate(info):
             row_values = jnp.where(lane == n, value, row_values)
         plan_ref[4:5, :] = row_values
-        plan_ref[5:8, :] = jnp.zeros((3, size), jnp.int32)
+        plan_ref[5:6, :] = jnp.full((1, size), row & 1, jnp.int32)
+        plan_ref[6:8, :] = jnp.zeros((2, size), jnp.int32)
 
 
 def make_plans(tile_rows, tile_cols, place, n_row, per_dev):
@@ -180,14 +181,19 @@
     )(slot, tile_stack)
 
 
-def spmm_kernel(layout, last, plan_ref, *refs):
+def spmm_kernel(layout, last, by_core, plan_ref, *refs):
     n_refs = sum(layout)
     refs_left = list(refs[:n_refs])
     pieces = [[refs_left.pop(0) for _ in range(n)] for n in layout]
     rest = list(refs[n_refs:])
     tiles_ref = rest.pop(0)
     acc_refs = (rest.pop(0), rest.pop(0)) if last else (None, None)
-    out_refs = (rest.pop(0), rest.pop(0))
+    if by_core:
+        core = plan_ref[5, 0]
+        out_ref = rest.pop(0)
+        out_refs = (out_ref.at[1 - core], out_ref.at[core])
+    else:
+        out_refs = (rest.pop(0), rest.pop(0))
     m_vmem, t_vmem, total_ref, sems = rest
     nodes, width = pieces[0][0].shape
     mid, sent_steps, n_groups, tile_base = [plan_ref[4, n] for n in range(4)]
@@ -270,21 +276,21 @@
     lax.fori_loop(0, n_groups, add_group, 0)
 
 
-def spmm(plan, pieces, tiles, acc, n_row):
+def spmm(plan, pieces, tiles, acc, n_row, by_core=False):
     nodes, width = pieces[0][0].shape
     half = n_row // 2 * nodes
     last = acc is not None
-    out = jax.ShapeDtypeStruct((half, width), jnp.bfloat16)
+    out = jax.ShapeDtypeStruct((2, half, width) if by_core else (half, width), jnp.bfloat16)
     blocks = [ref for p in pieces for ref in p]
     in_vmem, in_any = pl.BlockSpec(memory_space=pltpu.VMEM), pl.BlockSpec(memory_space=pl.ANY)
     return pl.pallas_call(
-        functools.partial(spmm_kernel, [len(p) for p in pieces], last),
-        out_shape=(out, out),
+        functools.partial(spmm_kernel, [len(p) for p in pieces], last, by_core),
+        out_shape=(out,) if by_core else (out, out),
         grid_spec=pltpu.PrefetchScalarGridSpec(
             num_scalar_prefetch=1,
             grid=(),
             in_specs=[in_vmem] * len(blocks) + [in_any] + [in_vmem] * len(acc or []),
-            out_specs=[in_vmem] * 2,
+            out_specs=[in_vmem] * (1 if by_core else 2),
             scratch_shapes=[
                 pltpu.VMEM((len(pieces) * nodes, width), jnp.bfloat16),
                 pltpu.VMEM((RING * GROUP + 1, SIDE, SIDE), jnp.bfloat16),
@@ -330,6 +336,11 @@
     return [[piece] for piece in pieces]
 
 
+def swap_cores(both):
+    pairs = [[i, i + 1] for i in range(0, lax.axis_size("row"), 2)]
+    return lax.all_to_all(both, "row", 0, 0, axis_index_groups=pairs)
+
+
 def fence(*values):
     return lax.optimization_barrier(values)
 
@@ -338,12 +349,17 @@
     return a.astype(jnp.float32) + b.astype(jnp.float32)
 
 
-def stage_sums(keep, recv, n_blocks, rows):
+def stage_sums(keep, recv, n_blocks, rows, at_once=False):
     width = keep.shape[1]
     cut = (n_blocks // 2, 2, 2, rows, width)
     flat = (2, n_blocks // 2, 2, rows, width)
+    sums = add_f32(keep, recv).astype(jnp.bfloat16)
+    if at_once:
+        (sums,) = fence(sums)
 
     def summed(shape, pick):
+        if at_once:
+            return pick(sums.reshape(shape)).reshape(-1, width)
         both = add_f32(pick(keep.reshape(shape)), pick(recv.reshape(shape)))
         return both.astype(jnp.bfloat16).reshape(-1, width)
 
@@ -353,7 +369,7 @@
         summed(flat, lambda v: v[1, :, 1]),
         summed(flat, lambda v: v[0, :, 1]),
     ]
-    return stage, add_f32(keep, recv).astype(jnp.bfloat16)
+    return stage, sums
 
 
 def halve(value, upper, rows):
@@ -435,20 +451,22 @@
     own0, own1, first0, plan0, plan1, flipped = fence(own0, own1, first0, plan0, plan1, flipped)
 
     second0 = gather_second(own0, first0[1], n_col)
+    acc0 = spmm(plan0, [[own0], [first0[0]], [first0[1]]], flipped, None, n_row)
+    own1, acc0 = fence(own1, acc0)
+    first1 = gather_first(own1)
     pieces0 = as_pieces(own0, first0, second0, mid, n_col)
-    pieces0, own1, near = fence(pieces0, own1, near)
-
-    first1 = gather_first(own1)
+    pieces0, near, acc0 = fence(pieces0, near, acc0)
+
     near.append(xor_permute(near[1], "row", bits[1]))
     for bit in bits[2:]:
         near += [xor_permute(f, "row", bit) for f in near]
-    acc0 = spmm(plan0, pieces0[:FIRST_PIECES], flipped, None, n_row)
-    send0, keep0 = spmm(plan1, pieces0[FIRST_PIECES:], flipped, acc0, n_row)
-    own1, first1, near, send0, keep0 = fence(own1, first1, near, send0, keep0)
+    (both0,) = spmm(plan1, pieces0[FIRST_PIECES:], flipped, acc0, n_row, by_core=True)
+    got0 = swap_cores(both0)
+    stage0, sums0 = stage_sums(got0[0], got0[1], n_row // 2, rows, at_once=True)
+    own1, first1, near, stage0, sums0 = fence(own1, first1, near, stage0, sums0)
 
     second1 = gather_second(own1, first1[1], n_col)
     pieces1 = as_pieces(own1, first1, second1, mid, n_col)
-    stage0, sums0 = stage_sums(keep0, xor_permute(send0, "row", 1), n_row // 2, rows)
     recv0 = exchange_first(stage0, bits)
     acc1 = spmm(plan0, pieces1[:FIRST_PIECES], flipped, None, n_row)
     pieces1, stage0, acc1 = fence(pieces1, stage0, acc1)
@@ -456,7 +474,7 @@
     send1, keep1 = spmm(plan1, pieces1[FIRST_PIECES:], flipped, acc1, n_row)
     send1, keep1, recv0, stage0, sums0 = fence(send1, keep1, recv0, stage0, sums0)
 
-    stage1, sums1 = stage_sums(keep1, xor_permute(send1, "row", 1), n_row // 2, rows)
+    stage1, sums1 = stage_sums(keep1, xor_permute(send1, "row", 1), n_row // 2, rows, at_once=True)
     rest0, sent0 = exchange_second(stage0, recv0, bits, rows)
     recv0 = send_second(sent0, bits)
     term0 = weight_term(near, sums0)

time: 141 us -> 138 us (0.979)
  blocking collectives: 0 us -> 10.1 us
  waiting for transfers between devices: 41 us -> 31.1 us
  other arithmetic: 12.4 us -> 7.53 us
  Pallas kernels: 38.1 us -> 39.6 us
    all_to_all x0 -> x1, blocking collectives: none -> 10.1 us  [swap_cores(): return lax.all_to_all(both, 'row', 0, 0, axis_index_groups=pairs)]
    ppermute x2, waiting for transfers between devices: 13.2 us -> 7.76 us  [gather_second(): lax.ppermute(by_two, 'col', ends)]
    convert_element_type x6 -> x2, other arithmetic: 7.54 us -> 2.68 us  [stage_sums(): sums = add_f32(keep, recv).astype(jnp.bfloat16)]
    ppermute x25 -> x24, waiting for transfers between devices: 27.8 us -> 23.4 us  [xor_permute(): return lax.ppermute(value, axis, [(i, i ^ mask) for i in range(size)])]
    pallas_call x4, Pallas kernels: 26.2 us -> 27.7 us  [spmm(): pl.pallas_call(functools.partial(spmm_kernel, [len(p) for p in pieces], l...]
    unnamed x24 -> x26, local copies, waits for them, and re-layouts: 4.4 us -> 5.45 us
    ppermute x25 -> x24, starting transfers between devices: 32.2 us -> 31.3 us  [xor_permute(): return lax.ppermute(value, axis, [(i, i ^ mask) for i in range(size)])]
  transfers between devices with their start and end apart: 29 -> 28, of which waited for: 15 -> 11; matrix products, arithmetic and copies ran while one was open for 10% -> 6% of each run, Pallas kernels for 27% -> 29%
where the time goes in v7:
time: 138 us; the launch traced here: 137 us
  Pallas kernels  39.6 us (29%)
  starting transfers between devices  35.3 us (26%)
  waiting for transfers between devices  31.1 us (23%)
  blocking collectives  10.1 us (7%)
  other arithmetic  7.53 us (5%)
  local copies, waits for them, and re-layouts  6.15 us (4%)
  matrix products  5.26 us (4%)
  between operations  1.73 us (1%)
    ppermute x24, starting transfers between devices, xor_permute(): return lax.ppermute(value, axis, [(i, i ^ mask) for i in range(size)])  31.3 us
    pallas_call x4, Pallas kernels, spmm(): pl.pallas_call(functools.partial(spmm_kernel, [len(p) for p in pieces], l...  27.7 us
    ppermute x24, waiting for transfers between devices, xor_permute(): return lax.ppermute(value, axis, [(i, i ^ mask) for i in range(size)])  23.4 us
    all_to_all x1, blocking collectives, swap_cores(): return lax.all_to_all(both, 'row', 0, 0, axis_index_groups=pairs)  10.1 us
    pallas_call x1, Pallas kernels, flip_tiles(): pl.pallas_call(flip_kernel, out_shape=jax.ShapeDtypeStruct((slots + GROUP...  9.59 us
    ppermute x2, waiting for transfers between devices, gather_second(): lax.ppermute(by_two, 'col', ends)  7.76 us
    unnamed x26, local copies, waits for them, and re-layouts  5.45 us
    dot_general x8, matrix products, weight_term(): lax.dot_general(f, sums[q * nodes:(q + 1) * nodes], (((0,), (0,)), ((), (...  3.83 us
  transfers between devices with their start and end apart: 28, of which 11 were waited for; matrix products, arithmetic and copies ran while one was open for 6% of the time, Pallas kernels for 29%

profile of v7, /device:TPU:1, one launch (start us, length us, event | category | flops | bytes accessed | tf_op | source)
XLA Modules:
  0.0 136.8 jit_solution(16590309499973992268)
XLA Ops:
  0.7 1.7 %compare_select_fusion = (bf16[2048,128]{1,0:T(8,128)(2,1)S(1)}, bf16[2048,128]{1,0:T(8,128)(2,1)S(1)}) fusion(bf16[2048,256]{1,0:T(8,128)(2,1)} %param.8, bf16[2048,256]{1,0:T(8,128)(2,1)} %param.9), kind=kLoop, calls=%fused_computation.19 | loop fusion | flops 1048576 | bytes 3145728 | tf_op jit(solution)/shard_map/jit(_where)/select_n | solution.py:440
  2.3 3.2 %collective-permute-start.1 = (bf16[2048,128]{1,0:T(8,128)(2,1)S(1)}, bf16[2048,128]{1,0:T(8,128)(2,1)S(1)}, u32[]{:S(2)}, u32[]{:S(2)}) collective-permute-start(bf16[2048,128]{1,0:T(8,128)(2,1)S(1)} %get-tuple-element.89.refs_0_), channel_id=1, source_target_pairs={{0,2},{1,3},{2,0},{3,1},{4,6},{5,7},{6,4},{7,5},{8,10},{9,11},{10,... | collective-permute-start | bytes 1572872 | tf_op jit(solution)/shard_map/ppermute | solution.py:309
  5.5 1.3 collective-permute-start
  7.9 2.3 %plan_slots.1 = (s32[8,512]{1,0:T(8,128)S(1)}, s32[8,512]{1,0:T(8,128)S(1)}, s32[1,320]{1,0:T(1,128)S(1)}) custom-call(s32[4]{0:T(128)S(1)} %pad_add_fusion.place_ref, s32[1,320]{1,0:T(1,128)S(1)} %bitcast.43, s32[1,320]{1,0:T(1,128)S(1)} %bitcast.45, s32[320,1]{1,0:T(8,128)S(1)} %copy.10.rows_c, s32[320,1]{1,0:T(8,128)S(1)} %copy.11.cols_c), custom_call_target="tpu_custom_call" | custom-call | bytes 4096 | tf_op jit(solution)/shard_map/plan_slots/pallas_call | solution.py:120
  10.2 1.3 collective-permute-start.7
  12.7 4.0 %copy-done.1 = bf16[1,1,320,128,128]{4,3,2,1,0:T(8,128)(2,1)S(1)} copy-done((bf16[1,1,320,128,128]{4,3,2,1,0:T(8,128)(2,1)S(1)}, bf16[1,1,320,128,128]{4,3,2,1,0:T(8,128)(2,1)}, u32[]{:S(2)}) %copy-start.1) | copy-done | bytes 10485784
  16.7 9.6 %flip_tiles.1.refs_3_.refs_2_ = bf16[352,128,128]{2,1,0:T(8,128)(2,1)S(1)} custom-call(s32[1,320]{1,0:T(1,128)S(1)} %get-tuple-element.85.slot_ref, bf16[320,128,128]{2,1,0:T(8,128)(2,1)S(1)} %bitcast.41), custom_call_target="tpu_custom_call" | custom-call | bytes 4096 | tf_op jit(solution)/shard_map/flip_tiles/pallas_call | solution.py:163
  26.3 2.2 %collective-permute-done.1.refs_2_ = bf16[2048,128]{1,0:T(8,128)(2,1)S(1)} collective-permute-done((bf16[2048,128]{1,0:T(8,128)(2,1)S(1)}, bf16[2048,128]{1,0:T(8,128)(2,1)S(1)}, u32[]{:S(2)}, u32[]{:S(2)}) %collective-permute-start.1) | collective-permute-done | bytes 524320 | tf_op jit(solution)/shard_map/ppermute | solution.py:309
  29.2 1.3 collective-permute-start.5
  30.5 8.6 %spmm_first.2 = (bf16[8192,128]{1,0:T(8,128)(2,1)S(1)}, bf16[8192,128]{1,0:T(8,128)(2,1)S(1)}) custom-call(s32[8,512]{1,0:T(8,128)S(1)} %get-tuple-element.88.plan_ref, bf16[2048,128]{1,0:T(8,128)(2,1)S(1)} %get-tuple-element.89.refs_0_, bf16[2048,128]{1,0:T(8,128)(2,1)S(1)} %collective-permute-done.refs_1_, ...), custom_call_target="tpu_custom_call" | custom-call | bytes 4096 | tf_op jit(solution)/shard_map/spmm_first/pallas_call | solution.py:286
  39.1 2.5 %collective-permute-start.3 = (bf16[2048,128]{1,0:T(8,128)(2,1)S(1)}, bf16[2048,128]{1,0:T(8,128)(2,1)S(1)}, u32[]{:S(2)}, u32[]{:S(2)}) collective-permute-start(bf16[2048,128]{1,0:T(8,128)(2,1)S(1)} %get-tuple-element.106.refs_0_), channel_id=1, source_target_pairs={{0,2},{1,3},{2,0},{3,1},{4,6},{5,7},{6,4},{7,5},{8,10},{9,11},{10,... | collective-permute-start | bytes 1572872 | tf_op jit(solution)/shard_map/ppermute | solution.py:309
  41.6 1.5 %collective-permute-start.2 = (bf16[2048,128]{1,0:T(8,128)(2,1)S(1)}, bf16[2048,128]{1,0:T(8,128)(2,1)S(1)}, u32[]{:S(2)}, u32[]{:S(2)}) collective-permute-start(bf16[2048,128]{1,0:T(8,128)(2,1)S(1)} %get-tuple-element.106.refs_0_), channel_id=1, source_target_pairs={{0,1},{1,0},{2,3},{3,2},{4,5},{5,4},{6,7},{7,6},{8,9},{9,8},{10,11... | collective-permute-start | bytes 1572872 | tf_op jit(solution)/shard_map/ppermute | solution.py:309
  44.7 4.5 %spmm_last.2 = bf16[2,8192,128]{2,1,0:T(8,128)(2,1)S(1)} custom-call(s32[8,512]{1,0:T(8,128)S(1)} %get-tuple-element.86.plan_ref, bf16[2048,128]{1,0:T(8,128)(2,1)S(1)} %collective-permute-done.4.refs_0_, bf16[2048,128]{1,0:T(8,128)(2,1)S(1)} %collective-permute-done.5.refs_1_, bf16[352,128,128]{2,1,0:T(8,128)(2,1)S(1)} %flip_tiles.1.refs_3_.refs_2_, ...), custom_call_target="tpu_custom_call" | custom-call | bytes 4096 | tf_op jit(solution)/shard_map/spmm_last/pallas_call | solution.py:286
  49.2 10.1 %all_to_all.5 = bf16[2,8192,128]{2,1,0:T(8,128)(2,1)S(1)} all-to-all(bf16[2,8192,128]{2,1,0:T(8,128)(2,1)S(1)} %spmm_last.2), channel_id=1, replica_groups={{0,4},{8,12},{16,20},{24,28},{1,5},{9,13},{17,21},{25,29},{2,6},{10,14}..., dimensions={0} | all-to-all | bytes 8388608 | tf_op jit(solution)/shard_map/all_to_all | solution.py:341
  61.2 4.4 %collective-permute-done.3.refs_2_ = bf16[2048,128]{1,0:T(8,128)(2,1)S(1)} collective-permute-done((bf16[2048,128]{1,0:T(8,128)(2,1)S(1)}, bf16[2048,128]{1,0:T(8,128)(2,1)S(1)}, u32[]{:S(2)}, u32[]{:S(2)}) %collective-permute-start.3) | collective-permute-done | bytes 524320 | tf_op jit(solution)/shard_map/ppermute | solution.py:309
  66.3 1.3 collective-permute-start.10
  67.6 1.3 collective-permute-start.11
  70.1 8.6 %spmm_first.3 = (bf16[8192,128]{1,0:T(8,128)(2,1)S(1)}, bf16[8192,128]{1,0:T(8,128)(2,1)S(1)}) custom-call(s32[8,512]{1,0:T(8,128)S(1)} %get-tuple-element.88.plan_ref, bf16[2048,128]{1,0:T(8,128)(2,1)S(1)} %get-tuple-element.106.refs_0_, bf16[2048,128]{1,0:T(8,128)(2,1)S(1)} %collective-permute-done.2.refs_1_, ...), custom_call_target="tpu_custom_call" | custom-call | bytes 4096 | tf_op jit(solution)/shard_map/spmm_first/pallas_call | solution.py:286
  78.8 7.0 %collective-permute-done.10.refs_1_ = bf16[2048,128]{1,0:T(8,128)(2,1)S(1)} collective-permute-done((bf16[2048,128]{1,0:T(8,128)(2,1)S(1)}, bf16[2048,128]{1,0:T(8,128)(2,1)S(1)}, u32[]{:S(2)}, u32[]{:S(2)}) %collective-permute-start.10) | collective-permute-done | bytes 524320 | tf_op jit(solution)/shard_map/ppermute | solution.py:327
  85.8 6.0 %spmm_last.3 = (bf16[8192,128]{1,0:T(8,128)(2,1)}, bf16[8192,128]{1,0:T(8,128)(2,1)S(1)}) custom-call(s32[8,512]{1,0:T(8,128)S(1)} %get-tuple-element.86.plan_ref, bf16[2048,128]{1,0:T(8,128)(2,1)S(1)} %collective-permute-done.9.refs_0_, bf16[2048,128]{1,0:T(8,128)(2,1)S(1)} %collective-permute-done.10.refs_1_, ...), custom_call_target="tpu_custom_call" | custom-call | bytes 4096 | tf_op jit(solution)/shard_map/spmm_last/pallas_call | solution.py:286
  91.8 1.8 %collective-permute-start.13 = (bf16[8192,128]{1,0:T(8,128)(2,1)}, bf16[8192,128]{1,0:T(8,128)(2,1)}, u32[]{:S(2)}, u32[]{:S(2)}) collective-permute-start(bf16[8192,128]{1,0:T(8,128)(2,1)} %get-tuple-element.125), channel_id=1, source_target_pairs={{0,4},{4,0},{8,12},{12,8},{16,20},{20,16},{24,28},{28,24},{1,5},{5... | collective-permute-start | bytes 6291464 | tf_op jit(solution)/shard_map/ppermute | solution.py:309
  93.6 1.6 %add_convert_fusion.4 = (bf16[2048,128]{1,0:T(8,128)(2,1)S(1)}, bf16[2048,128]{1,0:T(8,128)(2,1)S(1)}) fusion(bf16[2048,128]{1,0:T(8,128)(2,1)} %collective-permute-done.12, bf16[2048,128]{1,0:T(8,128)(2,1)S(1)} %bitcast.55, bf16[2048,128]{1,0:T(8,128)(2,1)} %collective-permute-done.11, bf16[2048,128]{1,0:T(8,128)(2,1)S(1)} %bitcast.54), kind=kLoop, calls=%fused_computation.17 | loop fusion | flops 2097152 | bytes 3145728 | tf_op jit(solution)/shard_map/convert_element_type | solution.py:393
  95.2 1.3 collective-permute-start.15
  99.9 2.1 %add_convert_fusion = bf16[8192,128]{1,0:T(8,128)(2,1)S(1)} fusion(bf16[8192,128]{1,0:T(8,128)(2,1)} %collective-permute-done.13, bf16[8192,128]{1,0:T(8,128)(2,1)S(1)} %get-tuple-element.124), kind=kLoop, calls=%fused_computation | loop fusion | flops 4194304 | bytes 6291456 | tf_op jit(solution)/shard_map/convert_element_type | solution.py:356
  108.6 3.1 %collective-permute-start.21 = (bf16[256,128]{1,0:T(8,128)(2,1)S(1)}, bf16[256,128]{1,0:T(8,128)(2,1)S(1)}, u32[]{:S(2)}, u32[]{:S(2)}) collective-permute-start(bf16[256,128]{1,0:T(8,128)(2,1)S(1)} %add_convert_fusion.12), channel_id=1, source_target_pairs={{0,3},{1,2},{2,1},{3,0},{4,7},{5,6},{6,5},{7,4},{8,11},{9,10},{10,... | collective-permute-start | bytes 196616 | tf_op jit(solution)/shard_map/ppermute | solution.py:309
  112.3 1.4 %collective-permute-done.21 = bf16[256,128]{1,0:T(8,128)(2,1)S(1)} collective-permute-done((bf16[256,128]{1,0:T(8,128)(2,1)S(1)}, bf16[256,128]{1,0:T(8,128)(2,1)S(1)}, u32[]{:S(2)}, u32[]{:S(2)}) %collective-permute-start.21) | collective-permute-done | bytes 65568 | tf_op jit(solution)/shard_map/ppermute | solution.py:309
  113.7 4.2 %collective-permute-done.20 = bf16[256,128]{1,0:T(8,128)(2,1)S(1)} collective-permute-done((bf16[256,128]{1,0:T(8,128)(2,1)S(1)}, bf16[256,128]{1,0:T(8,128)(2,1)S(1)}, u32[]{:S(2)}, u32[]{:S(2)}) %collective-permute-start.20) | collective-permute-done | bytes 65568 | tf_op jit(solution)/shard_map/ppermute | solution.py:309
  117.9 3.0 %collective-permute-done.16 = bf16[2048,128]{1,0:T(8,128)(2,1)S(1)} collective-permute-done((bf16[2048,128]{1,0:T(8,128)(2,1)S(1)}, bf16[2048,128]{1,0:T(8,128)(2,1)S(1)}, u32[]{:S(2)}, u32[]{:S(2)}) %collective-permute-start.16) | collective-permute-done | bytes 524320 | tf_op jit(solution)/shard_map/ppermute | solution.py:309
  121.3 1.9 %collective-permute-start.26 = (bf16[256,128]{1,0:T(8,128)(2,1)S(1)}, bf16[256,128]{1,0:T(8,128)(2,1)S(1)}, u32[]{:S(2)}, u32[]{:S(2)}) collective-permute-start(bf16[256,128]{1,0:T(8,128)(2,1)S(1)} %add_convert_fusion.11), channel_id=1, source_target_pairs={{0,24},{4,28},{8,16},{12,20},{16,8},{20,12},{24,0},{28,4},{1,25},{... | collective-permute-start | bytes 196616 | tf_op jit(solution)/shard_map/ppermute | solution.py:309
  127.4 5.0 %collective-permute-done.22 = bf16[1024,128]{1,0:T(8,128)(2,1)S(1)} collective-permute-done((bf16[1024,128]{1,0:T(8,128)(2,1)S(1)}, bf16[1024,128]{1,0:T(8,128)(2,1)S(1)}, u32[]{:S(2)}, u32[]{:S(2)}) %collective-permute-start.22) | collective-permute-done | bytes 262176 | tf_op jit(solution)/shard_map/ppermute | solution.py:309
  132.6 2.0 %collective-permute-start.27 = (bf16[256,128]{1,0:T(8,128)(2,1)S(1)}, bf16[256,128]{1,0:T(8,128)(2,1)S(1)}, u32[]{:S(2)}, u32[]{:S(2)}) collective-permute-start(bf16[256,128]{1,0:T(8,128)(2,1)S(1)} %add_convert_fusion.10), channel_id=1, source_target_pairs={{0,4},{4,0},{8,12},{12,8},{16,20},{20,16},{24,28},{28,24},{1,5},{5... | collective-permute-start | bytes 196616 | tf_op jit(solution)/shard_map/ppermute | solution.py:309
  134.6 1.4 %convolution_convert_fusion = bf16[2048,256]{1,0:T(8,128)(2,1)} fusion(bf16[256,256]{1,0:T(8,128)(2,1)S(1)} %copy-done, bf16[2048,128]{1,0:T(8,128)(2,1)S(1)} %pad_maximum_fusion.1, bf16[2048,128]{1,0:T(8,128)(2,1)S(1)} %pad_maximum_fusion), kind=kOutput, calls=%fused_computation.2 | convolution fusion | flops 271056896 | bytes 2228224 | tf_op jit(solution)/shard_map/dot_general | solution.py:504
  (94 shorter events, 23.6 us)
Async XLA Ops:
  0.6 134.0 %copy-start = (bf16[256,256]{1,0:T(8,128)(2,1)S(1)}, bf16[256,256]{1,0:T(8,128)(2,1)}, u32[]{:S(2)}) copy-start(bf16[256,256]{1,0:T(8,128)(2,1)} %param.11) | copy-start | bytes 393220
  0.6 6.8 %copy-start.3 = (s32[1,1,320]{2,1,0:T(1,128)S(1)}, s32[1,1,320]{2,1,0:T(1,128)}, u32[]{:S(2)}) copy-start(s32[1,1,320]{2,1,0:T(1,128)} %param.14) | copy-start | bytes 3844
  0.7 7.0 %copy-start.2 = (s32[1,1,320]{2,1,0:T(1,128)S(1)}, s32[1,1,320]{2,1,0:T(1,128)}, u32[]{:S(2)}) copy-start(s32[1,1,320]{2,1,0:T(1,128)} %param.13) | copy-start | bytes 3844
  2.3 26.1 %collective-permute-start.1 = (bf16[2048,128]{1,0:T(8,128)(2,1)S(1)}, bf16[2048,128]{1,0:T(8,128)(2,1)S(1)}, u32[]{:S(2)}, u32[]{:S(2)}) collective-permute-start(bf16[2048,128]{1,0:T(8,128)(2,1)S(1)} %get-tuple-element.89.refs_0_), channel_id=1, source_target_pairs={{0,2},{1,3},{2,0},{3,1},{4,6},{5,7},{6,4},{7,5},{8,10},{9,11},{10,... | collective-permute-start | bytes 1572872 | tf_op jit(solution)/shard_map/ppermute | solution.py:309
  5.5 22.9 %collective-permute-start = (bf16[2048,128]{1,0:T(8,128)(2,1)S(1)}, bf16[2048,128]{1,0:T(8,128)(2,1)S(1)}, u32[]{:S(2)}, u32[]{:S(2)}) collective-permute-start(bf16[2048,128]{1,0:T(8,128)(2,1)S(1)} %get-tuple-element.89.refs_0_), channel_id=1, source_target_pairs={{0,1},{1,0},{2,3},{3,2},{4,5},{5,4},{6,7},{7,6},{8,9},{9,8},{10,11... | collective-permute-start | bytes 1572872 | tf_op jit(solution)/shard_map/ppermute | solution.py:309
  10.2 31.4 %collective-permute-start.7 = (bf16[2048,256]{1,0:T(8,128)(2,1)}, bf16[2048,256]{1,0:T(8,128)(2,1)S(1)}, u32[]{:S(2)}, u32[]{:S(2)}) collective-permute-start(bf16[2048,256]{1,0:T(8,128)(2,1)} %param.10), channel_id=1, source_target_pairs={{0,16},{4,20},{8,24},{12,28},{16,0},{20,4},{24,8},{28,12},{1,17},{... | collective-permute-start | bytes 3145736 | tf_op jit(solution)/shard_map/ppermute | solution.py:309
  11.5 31.6 %collective-permute-start.6 = (bf16[2048,256]{1,0:T(8,128)(2,1)}, bf16[2048,256]{1,0:T(8,128)(2,1)S(1)}, u32[]{:S(2)}, u32[]{:S(2)}) collective-permute-start(bf16[2048,256]{1,0:T(8,128)(2,1)} %param.10), channel_id=1, source_target_pairs={{0,8},{4,12},{8,0},{12,4},{16,24},{20,28},{24,16},{28,20},{1,9},{5... | collective-permute-start | bytes 3145736 | tf_op jit(solution)/shard_map/ppermute | solution.py:309
  28.5 14.6 %collective-permute-start.4 = (bf16[2048,128]{1,0:T(8,128)(2,1)S(1)}, bf16[2048,128]{1,0:T(8,128)(2,1)S(1)}, u32[]{:S(2)}, u32[]{:S(2)}) collective-permute-start(bf16[2048,128]{1,0:T(8,128)(2,1)S(1)} %get-tuple-element.89.refs_0_), channel_id=1, source_target_pairs={{1,2},{2,1},{5,6},{6,5},{9,10},{10,9},{13,14},{14,13},{17,18},{18,... | collective-permute-start | bytes 1572872 | tf_op jit(solution)/shard_map/ppermute | solution.py:327
  29.2 14.7 %collective-permute-start.5 = (bf16[2048,128]{1,0:T(8,128)(2,1)S(1)}, bf16[2048,128]{1,0:T(8,128)(2,1)S(1)}, u32[]{:S(2)}, u32[]{:S(2)}) collective-permute-start(bf16[2048,128]{1,0:T(8,128)(2,1)S(1)} %collective-permute-done.1.refs_2_), channel_id=1, source_target_pairs={{1,0},{2,3},{5,4},{6,7},{9,8},{10,11},{13,12},{14,15},{17,16},{18,... | collective-permute-start | bytes 1572872 | tf_op jit(solution)/shard_map/ppermute | solution.py:327
  39.1 26.5 %collective-permute-start.3 = (bf16[2048,128]{1,0:T(8,128)(2,1)S(1)}, bf16[2048,128]{1,0:T(8,128)(2,1)S(1)}, u32[]{:S(2)}, u32[]{:S(2)}) collective-permute-start(bf16[2048,128]{1,0:T(8,128)(2,1)S(1)} %get-tuple-element.106.refs_0_), channel_id=1, source_target_pairs={{0,2},{1,3},{2,0},{3,1},{4,6},{5,7},{6,4},{7,5},{8,10},{9,11},{10,... | collective-permute-start | bytes 1572872 | tf_op jit(solution)/shard_map/ppermute | solution.py:309
  41.6 24.0 %collective-permute-start.2 = (bf16[2048,128]{1,0:T(8,128)(2,1)S(1)}, bf16[2048,128]{1,0:T(8,128)(2,1)S(1)}, u32[]{:S(2)}, u32[]{:S(2)}) collective-permute-start(bf16[2048,128]{1,0:T(8,128)(2,1)S(1)} %get-tuple-element.106.refs_0_), channel_id=1, source_target_pairs={{0,1},{1,0},{2,3},{3,2},{4,5},{5,4},{6,7},{7,6},{8,9},{9,8},{10,11... | collective-permute-start | bytes 1572872 | tf_op jit(solution)/shard_map/ppermute | solution.py:309
  43.8 21.8 %collective-permute-start.8 = (bf16[2048,256]{1,0:T(8,128)(2,1)S(1)}, bf16[2048,256]{1,0:T(8,128)(2,1)S(1)}, u32[]{:S(2)}, u32[]{:S(2)}) collective-permute-start(bf16[2048,256]{1,0:T(8,128)(2,1)S(1)} %collective-permute-done.6), channel_id=1, source_target_pairs={{0,16},{4,20},{8,24},{12,28},{16,0},{20,4},{24,8},{28,12},{1,17},{... | collective-permute-start | bytes 3145736 | tf_op jit(solution)/shard_map/ppermute | solution.py:309
  65.6 13.1 %copy-start.11 = (bf16[2048,256]{1,0:T(8,128)(2,1)}, bf16[2048,256]{1,0:T(8,128)(2,1)S(1)}, u32[]{:S(2)}) copy-start(bf16[2048,256]{1,0:T(8,128)(2,1)S(1)} %collective-permute-done.8) | copy-start | bytes 3145732
  65.6 13.2 %collective-permute-start.9 = (bf16[2048,128]{1,0:T(8,128)(2,1)S(1)}, bf16[2048,128]{1,0:T(8,128)(2,1)S(1)}, u32[]{:S(2)}, u32[]{:S(2)}) collective-permute-start(bf16[2048,128]{1,0:T(8,128)(2,1)S(1)} %get-tuple-element.106.refs_0_), channel_id=1, source_target_pairs={{1,2},{2,1},{5,6},{6,5},{9,10},{10,9},{13,14},{14,13},{17,18},{18,... | collective-permute-start | bytes 1572872 | tf_op jit(solution)/shard_map/ppermute | solution.py:327
  66.3 19.5 %collective-permute-start.10 = (bf16[2048,128]{1,0:T(8,128)(2,1)S(1)}, bf16[2048,128]{1,0:T(8,128)(2,1)S(1)}, u32[]{:S(2)}, u32[]{:S(2)}) collective-permute-start(bf16[2048,128]{1,0:T(8,128)(2,1)S(1)} %collective-permute-done.3.refs_2_), channel_id=1, source_target_pairs={{1,0},{2,3},{5,4},{6,7},{9,8},{10,11},{13,12},{14,15},{17,16},{18,... | collective-permute-start | bytes 1572872 | tf_op jit(solution)/shard_map/ppermute | solution.py:327
  67.6 24.2 %collective-permute-start.11 = (bf16[2048,128]{1,0:T(8,128)(2,1)S(1)}, bf16[2048,128]{1,0:T(8,128)(2,1)}, u32[]{:S(2)}, u32[]{:S(2)}) collective-permute-start(bf16[2048,128]{1,0:T(8,128)(2,1)S(1)} %bitcast.59), channel_id=1, source_target_pairs={{0,8},{4,12},{8,0},{12,4},{16,24},{20,28},{24,16},{28,20},{1,9},{5... | collective-permute-start | bytes 1572872 | tf_op jit(solution)/shard_map/ppermute | solution.py:309
  68.9 22.9 %collective-permute-start.12 = (bf16[2048,128]{1,0:T(8,128)(2,1)S(1)}, bf16[2048,128]{1,0:T(8,128)(2,1)}, u32[]{:S(2)}, u32[]{:S(2)}) collective-permute-start(bf16[2048,128]{1,0:T(8,128)(2,1)S(1)} %bitcast.58), channel_id=1, source_target_pairs={{0,16},{4,20},{8,24},{12,28},{16,0},{20,4},{24,8},{28,12},{1,17},{... | collective-permute-start | bytes 1572872 | tf_op jit(solution)/shard_map/ppermute | solution.py:309
  91.8 8.1 %collective-permute-start.13 = (bf16[8192,128]{1,0:T(8,128)(2,1)}, bf16[8192,128]{1,0:T(8,128)(2,1)}, u32[]{:S(2)}, u32[]{:S(2)}) collective-permute-start(bf16[8192,128]{1,0:T(8,128)(2,1)} %get-tuple-element.125), channel_id=1, source_target_pairs={{0,4},{4,0},{8,12},{12,8},{16,20},{20,16},{24,28},{28,24},{1,5},{5... | collective-permute-start | bytes 6291464 | tf_op jit(solution)/shard_map/ppermute | solution.py:309
  95.2 8.0 %collective-permute-start.15 = (bf16[1024,128]{1,0:T(8,128)(2,1)S(1)}, bf16[1024,128]{1,0:T(8,128)(2,1)S(1)}, u32[]{:S(2)}, u32[]{:S(2)}) collective-permute-start(bf16[1024,128]{1,0:T(8,128)(2,1)S(1)} %get-tuple-element.176), channel_id=1, source_target_pairs={{0,8},{4,12},{8,0},{12,4},{16,24},{20,28},{24,16},{28,20},{1,9},{5... | collective-permute-start | bytes 786440 | tf_op jit(solution)/shard_map/ppermute | solution.py:309
  96.6 7.6 %collective-permute-start.14 = (bf16[1024,128]{1,0:T(8,128)(2,1)S(1)}, bf16[1024,128]{1,0:T(8,128)(2,1)S(1)}, u32[]{:S(2)}, u32[]{:S(2)}) collective-permute-start(bf16[1024,128]{1,0:T(8,128)(2,1)S(1)} %get-tuple-element.178), channel_id=1, source_target_pairs={{0,16},{4,20},{8,24},{12,28},{16,0},{20,4},{24,8},{28,12},{1,17},{... | collective-permute-start | bytes 786440 | tf_op jit(solution)/shard_map/ppermute | solution.py:309
  106.2 2.4 %collective-permute-start.18 = (bf16[256,128]{1,0:T(8,128)(2,1)S(1)}, bf16[256,128]{1,0:T(8,128)(2,1)S(1)}, u32[]{:S(2)}, u32[]{:S(2)}) collective-permute-start(bf16[256,128]{1,0:T(8,128)(2,1)S(1)} %get-tuple-element.182), channel_id=1, source_target_pairs={{0,4},{4,0},{8,12},{12,8},{16,20},{20,16},{24,28},{28,24},{1,5},{5... | collective-permute-start | bytes 196616 | tf_op jit(solution)/shard_map/ppermute | solution.py:309
  107.4 13.5 %collective-permute-start.16 = (bf16[2048,128]{1,0:T(8,128)(2,1)S(1)}, bf16[2048,128]{1,0:T(8,128)(2,1)S(1)}, u32[]{:S(2)}, u32[]{:S(2)}) collective-permute-start(bf16[2048,128]{1,0:T(8,128)(2,1)S(1)} %bitcast.57), channel_id=1, source_target_pairs={{0,8},{4,12},{8,0},{12,4},{16,24},{20,28},{24,16},{28,20},{1,9},{5... | collective-permute-start | bytes 1572872 | tf_op jit(solution)/shard_map/ppermute | solution.py:309
  107.6 13.3 %collective-permute-start.17 = (bf16[2048,128]{1,0:T(8,128)(2,1)S(1)}, bf16[2048,128]{1,0:T(8,128)(2,1)S(1)}, u32[]{:S(2)}, u32[]{:S(2)}) collective-permute-start(bf16[2048,128]{1,0:T(8,128)(2,1)S(1)} %bitcast.56), channel_id=1, source_target_pairs={{0,16},{4,20},{8,24},{12,28},{16,0},{20,4},{24,8},{28,12},{1,17},{... | collective-permute-start | bytes 1572872 | tf_op jit(solution)/shard_map/ppermute | solution.py:309
  108.6 5.1 %collective-permute-start.21 = (bf16[256,128]{1,0:T(8,128)(2,1)S(1)}, bf16[256,128]{1,0:T(8,128)(2,1)S(1)}, u32[]{:S(2)}, u32[]{:S(2)}) collective-permute-start(bf16[256,128]{1,0:T(8,128)(2,1)S(1)} %add_convert_fusion.12), channel_id=1, source_target_pairs={{0,3},{1,2},{2,1},{3,0},{4,7},{5,6},{6,5},{7,4},{8,11},{9,10},{10,... | collective-permute-start | bytes 196616 | tf_op jit(solution)/shard_map/ppermute | solution.py:309
  111.8 6.1 %collective-permute-start.20 = (bf16[256,128]{1,0:T(8,128)(2,1)S(1)}, bf16[256,128]{1,0:T(8,128)(2,1)S(1)}, u32[]{:S(2)}, u32[]{:S(2)}) collective-permute-start(bf16[256,128]{1,0:T(8,128)(2,1)S(1)} %add_convert_fusion.12), channel_id=1, source_target_pairs={{0,2},{1,3},{2,0},{3,1},{4,6},{5,7},{6,4},{7,5},{8,10},{9,11},{10,... | collective-permute-start | bytes 196616 | tf_op jit(solution)/shard_map/ppermute | solution.py:309
  111.8 6.1 %collective-permute-start.19 = (bf16[256,128]{1,0:T(8,128)(2,1)S(1)}, bf16[256,128]{1,0:T(8,128)(2,1)S(1)}, u32[]{:S(2)}, u32[]{:S(2)}) collective-permute-start(bf16[256,128]{1,0:T(8,128)(2,1)S(1)} %add_convert_fusion.12), channel_id=1, source_target_pairs={{0,1},{1,0},{2,3},{3,2},{4,5},{5,4},{6,7},{7,6},{8,9},{9,8},{10,11... | collective-permute-start | bytes 196616 | tf_op jit(solution)/shard_map/ppermute | solution.py:309
  121.3 4.9 %collective-permute-start.26 = (bf16[256,128]{1,0:T(8,128)(2,1)S(1)}, bf16[256,128]{1,0:T(8,128)(2,1)S(1)}, u32[]{:S(2)}, u32[]{:S(2)}) collective-permute-start(bf16[256,128]{1,0:T(8,128)(2,1)S(1)} %add_convert_fusion.11), channel_id=1, source_target_pairs={{0,24},{4,28},{8,16},{12,20},{16,8},{20,12},{24,0},{28,4},{1,25},{... | collective-permute-start | bytes 196616 | tf_op jit(solution)/shard_map/ppermute | solution.py:309
  123.2 4.1 %collective-permute-start.25 = (bf16[256,128]{1,0:T(8,128)(2,1)S(1)}, bf16[256,128]{1,0:T(8,128)(2,1)S(1)}, u32[]{:S(2)}, u32[]{:S(2)}) collective-permute-start(bf16[256,128]{1,0:T(8,128)(2,1)S(1)} %add_convert_fusion.11), channel_id=1, source_target_pairs={{0,16},{4,20},{8,24},{12,28},{16,0},{20,4},{24,8},{28,12},{1,17},{... | collective-permute-start | bytes 196616 | tf_op jit(solution)/shard_map/ppermute | solution.py:309
  123.7 3.6 %collective-permute-start.24 = (bf16[256,128]{1,0:T(8,128)(2,1)S(1)}, bf16[256,128]{1,0:T(8,128)(2,1)S(1)}, u32[]{:S(2)}, u32[]{:S(2)}) collective-permute-start(bf16[256,128]{1,0:T(8,128)(2,1)S(1)} %add_convert_fusion.11), channel_id=1, source_target_pairs={{0,8},{4,12},{8,0},{12,4},{16,24},{20,28},{24,16},{28,20},{1,9},{5... | collective-permute-start | bytes 196616 | tf_op jit(solution)/shard_map/ppermute | solution.py:309
  124.0 8.4 %collective-permute-start.22 = (bf16[1024,128]{1,0:T(8,128)(2,1)S(1)}, bf16[1024,128]{1,0:T(8,128)(2,1)S(1)}, u32[]{:S(2)}, u32[]{:S(2)}) collective-permute-start(bf16[1024,128]{1,0:T(8,128)(2,1)S(1)} %get-tuple-element.156), channel_id=1, source_target_pairs={{0,16},{4,20},{8,24},{12,28},{16,0},{20,4},{24,8},{28,12},{1,17},{... | collective-permute-start | bytes 786440 | tf_op jit(solution)/shard_map/ppermute | solution.py:309
  125.0 7.4 %collective-permute-start.23 = (bf16[1024,128]{1,0:T(8,128)(2,1)S(1)}, bf16[1024,128]{1,0:T(8,128)(2,1)S(1)}, u32[]{:S(2)}, u32[]{:S(2)}) collective-permute-start(bf16[1024,128]{1,0:T(8,128)(2,1)S(1)} %get-tuple-element.158), channel_id=1, source_target_pairs={{0,8},{4,12},{8,0},{12,4},{16,24},{20,28},{24,16},{28,20},{1,9},{5... | collective-permute-start | bytes 786440 | tf_op jit(solution)/shard_map/ppermute | solution.py:309
  132.6 3.5 %collective-permute-start.27 = (bf16[256,128]{1,0:T(8,128)(2,1)S(1)}, bf16[256,128]{1,0:T(8,128)(2,1)S(1)}, u32[]{:S(2)}, u32[]{:S(2)}) collective-permute-start(bf16[256,128]{1,0:T(8,128)(2,1)S(1)} %add_convert_fusion.10), channel_id=1, source_target_pairs={{0,4},{4,0},{8,12},{12,8},{16,20},{20,16},{24,28},{28,24},{1,5},{5... | collective-permute-start | bytes 196616 | tf_op jit(solution)/shard_map/ppermute | solution.py:309
  (9 other events, 29.1 us)

commit v8 on v7

--- a/solution.py
+++ b/solution.py
@@ -413,12 +413,12 @@
 
 
 def weight_term(near, sums):
-    nodes = near[0].shape[0]
-    terms = [
-        lax.dot_general(f, sums[q * nodes : (q + 1) * nodes], (((0,), (0,)), ((), ())), preferred_element_type=jnp.float32)
-        for q, f in enumerate(near)
-    ]
-    return tree_sum(terms).astype(jnp.bfloat16)
+    terms, at = [], 0
+    for f in [part for parts in near for part in parts]:
+        own = sums[at : at + f.shape[0]]
+        terms.append(lax.dot_general(f, own, (((0,), (0,)), ((), ())), preferred_element_type=jnp.float32))
+        at += f.shape[0]
+    return sum(terms[1:], terms[0]).astype(jnp.bfloat16)
 
 
 def sum_over(term, axis, masks):
@@ -445,9 +445,9 @@
     plan0, plan1, slot = make_plans(tile_rows, tile_cols, place, n_row, nodes // SIDE)
     flipped = flip_tiles(slot, tiles.reshape(slots, SIDE, SIDE))
     features, plan0 = fence(features, plan0)
-    near = [features]
+    near = [[features]]
     for bit in bits[:2]:
-        near.append(xor_permute(features, "row", bit))
+        near.append([xor_permute(features, "row", bit)])
     own0, own1, first0, plan0, plan1, flipped = fence(own0, own1, first0, plan0, plan1, flipped)
 
     second0 = gather_second(own0, first0[1], n_col)
@@ -457,25 +457,26 @@
     pieces0 = as_pieces(own0, first0, second0, mid, n_col)
     pieces0, near, acc0 = fence(pieces0, near, acc0)
 
-    near.append(xor_permute(near[1], "row", bits[1]))
+    near.append([xor_permute(near[1][0][:rows], "row", bits[1]), xor_permute(near[2][0][rows:], "row", bits[0])])
     for bit in bits[2:]:
-        near += [xor_permute(f, "row", bit) for f in near]
+        near += [[xor_permute(f, "row", bit) for f in parts] for parts in near]
     (both0,) = spmm(plan1, pieces0[FIRST_PIECES:], flipped, acc0, n_row, by_core=True)
     got0 = swap_cores(both0)
+    got0, near = fence(got0, near)
     stage0, sums0 = stage_sums(got0[0], got0[1], n_row // 2, rows, at_once=True)
-    own1, first1, near, stage0, sums0 = fence(own1, first1, near, stage0, sums0)
+    own1, first1, stage0, sums0 = fence(own1, first1, stage0, sums0)
 
     second1 = gather_second(own1, first1[1], n_col)
     pieces1 = as_pieces(own1, first1, second1, mid, n_col)
     recv0 = exchange_first(stage0, bits)
     acc1 = spmm(plan0, pieces1[:FIRST_PIECES], flipped, None, n_row)
-    pieces1, stage0, acc1 = fence(pieces1, stage0, acc1)
+    rest0, sent0 = exchange_second(stage0, recv0, bits, rows)
+    pieces1, rest0, sent0, acc1 = fence(pieces1, rest0, sent0, acc1)
 
     send1, keep1 = spmm(plan1, pieces1[FIRST_PIECES:], flipped, acc1, n_row)
-    send1, keep1, recv0, stage0, sums0 = fence(send1, keep1, recv0, stage0, sums0)
+    send1, keep1, sent0, sums0 = fence(send1, keep1, sent0, sums0)
 
     stage1, sums1 = stage_sums(keep1, xor_permute(send1, "row", 1), n_row // 2, rows, at_once=True)
-    rest0, sent0 = exchange_second(stage0, recv0, bits, rows)
     recv0 = send_second(sent0, bits)
     term0 = weight_term(near, sums0)
     stage1, sums1, term0 = fence(stage1, sums1, term0)

time: 138 us -> 139 us (level)
  Pallas kernels: 39.6 us -> 30.4 us
  waiting for transfers between devices: 31.1 us -> 35 us
  matrix products: 5.26 us -> 9.01 us
  starting transfers between devices: 35.3 us -> 37.8 us
    pallas_call x4, Pallas kernels: 27.7 us -> 18.5 us  [spmm(): pl.pallas_call(functools.partial(spmm_kernel, [len(p) for p in pieces], l...]
    dot_general x8 -> x10, matrix products: 3.83 us -> 7.58 us  [weight_term(): lax.dot_general(f, own, (((0,), (0,)), ((), ())), preferred_element_type=...]
    ppermute x24 -> x25, starting transfers between devices: 31.3 us -> 33.8 us  [xor_permute(): return lax.ppermute(value, axis, [(i, i ^ mask) for i in range(size)])]
    ppermute x2, waiting for transfers between devices: 7.76 us -> 9.76 us  [gather_second(): lax.ppermute(by_two, 'col', ends)]
    ppermute x24 -> x25, waiting for transfers between devices: 23.4 us -> 25.2 us  [xor_permute(): return lax.ppermute(value, axis, [(i, i ^ mask) for i in range(size)])]
    unnamed x26 -> x24, local copies, waits for them, and re-layouts: 5.45 us -> 5.07 us
  transfers between devices with their start and end apart: 28 -> 29, of which waited for: 11 -> 12; matrix products, arithmetic and copies ran while one was open for 6% -> 9% of each run, Pallas kernels for 29% -> 19%
where the time goes in v8:
time: 139 us; the launch traced here: 137 us
  starting transfers between devices  37.8 us (27%)
  waiting for transfers between devices  35 us (25%)
  Pallas kernels  30.4 us (22%)
  blocking collectives  9.6 us (7%)
  matrix products  9.01 us (6%)
  local copies, waits for them, and re-layouts  7.41 us (5%)
  other arithmetic  6.18 us (4%)
  between operations  1.79 us (1%)
    ppermute x25, starting transfers between devices, xor_permute(): return lax.ppermute(value, axis, [(i, i ^ mask) for i in range(size)])  33.8 us
    ppermute x25, waiting for transfers between devices, xor_permute(): return lax.ppermute(value, axis, [(i, i ^ mask) for i in range(size)])  25.2 us
    pallas_call x4, Pallas kernels, spmm(): pl.pallas_call(functools.partial(spmm_kernel, [len(p) for p in pieces], l...  18.5 us
    ppermute x2, waiting for transfers between devices, gather_second(): lax.ppermute(by_two, 'col', ends)  9.76 us
    all_to_all x1, blocking collectives, swap_cores(): return lax.all_to_all(both, 'row', 0, 0, axis_index_groups=pairs)  9.6 us
    pallas_call x1, Pallas kernels, flip_tiles(): pl.pallas_call(flip_kernel, out_shape=jax.ShapeDtypeStruct((slots + GROUP...  9.59 us
    dot_general x10, matrix products, weight_term(): lax.dot_general(f, own, (((0,), (0,)), ((), ())), preferred_element_type=...  7.58 us
    unnamed x24, local copies, waits for them, and re-layouts  5.07 us
  transfers between devices with their start and end apart: 29, of which 12 were waited for; matrix products, arithmetic and copies ran while one was open for 9% of the time, Pallas kernels for 19%

profile of v8, /device:TPU:1, one launch (start us, length us, event | category | flops | bytes accessed | tf_op | source)
XLA Modules:
  0.0 137.2 jit_solution(2042207397182104723)
XLA Ops:
  0.7 1.7 %compare_select_fusion = (bf16[2048,128]{1,0:T(8,128)(2,1)S(1)}, bf16[2048,128]{1,0:T(8,128)(2,1)S(1)}) fusion(bf16[2048,256]{1,0:T(8,128)(2,1)} %param.8, bf16[2048,256]{1,0:T(8,128)(2,1)} %param.9), kind=kLoop, calls=%fused_computation.21 | loop fusion | flops 1048576 | bytes 3145728 | tf_op jit(solution)/shard_map/jit(_where)/select_n | solution.py:440
  2.3 3.2 %collective-permute-start.1 = (bf16[2048,128]{1,0:T(8,128)(2,1)S(1)}, bf16[2048,128]{1,0:T(8,128)(2,1)S(1)}, u32[]{:S(2)}, u32[]{:S(2)}) collective-permute-start(bf16[2048,128]{1,0:T(8,128)(2,1)S(1)} %get-tuple-element.91.refs_0_), channel_id=1, source_target_pairs={{0,2},{1,3},{2,0},{3,1},{4,6},{5,7},{6,4},{7,5},{8,10},{9,11},{10,... | collective-permute-start | bytes 1572872 | tf_op jit(solution)/shard_map/ppermute | solution.py:309
  5.5 1.3 collective-permute-start
  7.9 2.3 %plan_slots.1 = (s32[8,512]{1,0:T(8,128)S(1)}, s32[8,512]{1,0:T(8,128)S(1)}, s32[1,320]{1,0:T(1,128)S(1)}) custom-call(s32[4]{0:T(128)S(1)} %pad_add_fusion.place_ref, s32[1,320]{1,0:T(1,128)S(1)} %bitcast.45, s32[1,320]{1,0:T(1,128)S(1)} %bitcast.47, s32[320,1]{1,0:T(8,128)S(1)} %copy.10.rows_c, s32[320,1]{1,0:T(8,128)S(1)} %copy.11.cols_c), custom_call_target="tpu_custom_call" | custom-call | bytes 4096 | tf_op jit(solution)/shard_map/plan_slots/pallas_call | solution.py:120
  10.2 1.3 collective-permute-start.7
  12.7 4.0 %copy-done.1 = bf16[1,1,320,128,128]{4,3,2,1,0:T(8,128)(2,1)S(1)} copy-done((bf16[1,1,320,128,128]{4,3,2,1,0:T(8,128)(2,1)S(1)}, bf16[1,1,320,128,128]{4,3,2,1,0:T(8,128)(2,1)}, u32[]{:S(2)}) %copy-start.1) | copy-done | bytes 10485784
  16.7 9.6 %flip_tiles.1.refs_3_.refs_2_ = bf16[352,128,128]{2,1,0:T(8,128)(2,1)S(1)} custom-call(s32[1,320]{1,0:T(1,128)S(1)} %get-tuple-element.87.slot_ref, bf16[320,128,128]{2,1,0:T(8,128)(2,1)S(1)} %bitcast.43), custom_call_target="tpu_custom_call" | custom-call | bytes 4096 | tf_op jit(solution)/shard_map/flip_tiles/pallas_call | solution.py:163
  26.3 2.2 %collective-permute-done.1.refs_2_ = bf16[2048,128]{1,0:T(8,128)(2,1)S(1)} collective-permute-done((bf16[2048,128]{1,0:T(8,128)(2,1)S(1)}, bf16[2048,128]{1,0:T(8,128)(2,1)S(1)}, u32[]{:S(2)}, u32[]{:S(2)}) %collective-permute-start.1) | collective-permute-done | bytes 524320 | tf_op jit(solution)/shard_map/ppermute | solution.py:309
  29.2 1.3 collective-permute-start.5
  30.5 5.5 %spmm_first.2 = (bf16[8192,128]{1,0:T(8,128)(2,1)S(1)}, bf16[8192,128]{1,0:T(8,128)(2,1)S(1)}) custom-call(s32[8,512]{1,0:T(8,128)S(1)} %get-tuple-element.90.plan_ref, bf16[2048,128]{1,0:T(8,128)(2,1)S(1)} %get-tuple-element.91.refs_0_, bf16[2048,128]{1,0:T(8,128)(2,1)S(1)} %collective-permute-done.refs_1_, ...), custom_call_target="tpu_custom_call" | custom-call | bytes 4096 | tf_op jit(solution)/shard_map/spmm_first/pallas_call | solution.py:286
  36.0 7.5 %collective-permute-done.5.refs_1_ = bf16[2048,128]{1,0:T(8,128)(2,1)S(1)} collective-permute-done((bf16[2048,128]{1,0:T(8,128)(2,1)S(1)}, bf16[2048,128]{1,0:T(8,128)(2,1)S(1)}, u32[]{:S(2)}, u32[]{:S(2)}) %collective-permute-start.5) | collective-permute-done | bytes 524320 | tf_op jit(solution)/shard_map/ppermute | solution.py:327
  46.1 2.6 %collective-permute-start.3 = (bf16[2048,128]{1,0:T(8,128)(2,1)S(1)}, bf16[2048,128]{1,0:T(8,128)(2,1)S(1)}, u32[]{:S(2)}, u32[]{:S(2)}) collective-permute-start(bf16[2048,128]{1,0:T(8,128)(2,1)S(1)} %get-tuple-element.109.refs_0_), channel_id=1, source_target_pairs={{0,2},{1,3},{2,0},{3,1},{4,6},{5,7},{6,4},{7,5},{8,10},{9,11},{10,... | collective-permute-start | bytes 1572872 | tf_op jit(solution)/shard_map/ppermute | solution.py:309
  48.7 2.2 %collective-permute-start.2 = (bf16[2048,128]{1,0:T(8,128)(2,1)S(1)}, bf16[2048,128]{1,0:T(8,128)(2,1)S(1)}, u32[]{:S(2)}, u32[]{:S(2)}) collective-permute-start(bf16[2048,128]{1,0:T(8,128)(2,1)S(1)} %get-tuple-element.109.refs_0_), channel_id=1, source_target_pairs={{0,1},{1,0},{2,3},{3,2},{4,5},{5,4},{6,7},{7,6},{8,9},{9,8},{10,11... | collective-permute-start | bytes 1572872 | tf_op jit(solution)/shard_map/ppermute | solution.py:309
  50.9 3.0 %spmm_last.2 = bf16[2,8192,128]{2,1,0:T(8,128)(2,1)S(1)} custom-call(s32[8,512]{1,0:T(8,128)S(1)} %get-tuple-element.88.plan_ref, bf16[2048,128]{1,0:T(8,128)(2,1)S(1)} %collective-permute-done.4.refs_0_, bf16[2048,128]{1,0:T(8,128)(2,1)S(1)} %collective-permute-done.5.refs_1_, bf16[352,128,128]{2,1,0:T(8,128)(2,1)S(1)} %flip_tiles.1.refs_3_.refs_2_, ...), custom_call_target="tpu_custom_call" | custom-call | bytes 4096 | tf_op jit(solution)/shard_map/spmm_last/pallas_call | solution.py:286
  53.9 9.6 %all_to_all.5 = bf16[2,8192,128]{2,1,0:T(8,128)(2,1)S(1)} all-to-all(bf16[2,8192,128]{2,1,0:T(8,128)(2,1)S(1)} %spmm_last.2), channel_id=1, replica_groups={{0,4},{8,12},{16,20},{24,28},{1,5},{9,13},{17,21},{25,29},{2,6},{10,14}..., dimensions={0} | all-to-all | bytes 8388608 | tf_op jit(solution)/shard_map/all_to_all | solution.py:341
  64.3 6.1 %collective-permute-done.3.refs_2_ = bf16[2048,128]{1,0:T(8,128)(2,1)S(1)} collective-permute-done((bf16[2048,128]{1,0:T(8,128)(2,1)S(1)}, bf16[2048,128]{1,0:T(8,128)(2,1)S(1)}, u32[]{:S(2)}, u32[]{:S(2)}) %collective-permute-start.3) | collective-permute-done | bytes 524320 | tf_op jit(solution)/shard_map/ppermute | solution.py:309
  71.5 1.3 collective-permute-start.11
  72.8 5.5 %spmm_first.3 = (bf16[8192,128]{1,0:T(8,128)(2,1)S(1)}, bf16[8192,128]{1,0:T(8,128)(2,1)S(1)}) custom-call(s32[8,512]{1,0:T(8,128)S(1)} %get-tuple-element.90.plan_ref, bf16[2048,128]{1,0:T(8,128)(2,1)S(1)} %get-tuple-element.109.refs_0_, bf16[2048,128]{1,0:T(8,128)(2,1)S(1)} %collective-permute-done.2.refs_1_, ...), custom_call_target="tpu_custom_call" | custom-call | bytes 4096 | tf_op jit(solution)/shard_map/spmm_first/pallas_call | solution.py:286
  78.3 2.9 %collective-permute-done.12 = bf16[2048,128]{1,0:T(8,128)(2,1)S(1)} collective-permute-done((bf16[2048,128]{1,0:T(8,128)(2,1)S(1)}, bf16[2048,128]{1,0:T(8,128)(2,1)S(1)}, u32[]{:S(2)}, u32[]{:S(2)}) %collective-permute-start.12) | collective-permute-done | bytes 524320 | tf_op jit(solution)/shard_map/ppermute | solution.py:309
  83.1 2.3 %collective-permute-done.11.refs_1_ = bf16[2048,128]{1,0:T(8,128)(2,1)S(1)} collective-permute-done((bf16[2048,128]{1,0:T(8,128)(2,1)S(1)}, bf16[2048,128]{1,0:T(8,128)(2,1)S(1)}, u32[]{:S(2)}, u32[]{:S(2)}) %collective-permute-start.11) | collective-permute-done | bytes 524320 | tf_op jit(solution)/shard_map/ppermute | solution.py:327
  85.4 4.5 %spmm_last.3 = (bf16[8192,128]{1,0:T(8,128)(2,1)}, bf16[8192,128]{1,0:T(8,128)(2,1)S(1)}) custom-call(s32[8,512]{1,0:T(8,128)S(1)} %get-tuple-element.88.plan_ref, bf16[2048,128]{1,0:T(8,128)(2,1)S(1)} %collective-permute-done.10.refs_0_, bf16[2048,128]{1,0:T(8,128)(2,1)S(1)} %collective-permute-done.11.refs_1_, ...), custom_call_target="tpu_custom_call" | custom-call | bytes 4096 | tf_op jit(solution)/shard_map/spmm_last/pallas_call | solution.py:286
  89.9 4.5 %collective-permute-start.14 = (bf16[8192,128]{1,0:T(8,128)(2,1)}, bf16[8192,128]{1,0:T(8,128)(2,1)}, u32[]{:S(2)}, u32[]{:S(2)}) collective-permute-start(bf16[8192,128]{1,0:T(8,128)(2,1)} %get-tuple-element.128), channel_id=1, source_target_pairs={{0,4},{4,0},{8,12},{12,8},{16,20},{20,16},{24,28},{28,24},{1,5},{5... | collective-permute-start | bytes 6291464 | tf_op jit(solution)/shard_map/ppermute | solution.py:309
  97.2 1.4 %fusion.28 = f32[256,128]{1,0:T(8,128)S(1)} fusion(bf16[1024,256]{1,0:T(8,128)(2,1)S(1)} %collective-permute-done.8, bf16[8192,128]{1,0:T(8,128)(2,1)} %copy-done.4), kind=kOutput, calls=%fused_computation.49 | convolution fusion | flops 67108864 | bytes 917504 | tf_op jit(solution)/shard_map/dot_general | solution.py:419
  98.5 1.8 %fusion.17 = f32[256,128]{1,0:T(8,128)S(1)} fusion(bf16[2048,256]{1,0:T(8,128)(2,1)} %copy-done.8, bf16[8192,128]{1,0:T(8,128)(2,1)} %copy-done.4), kind=kOutput, calls=%fused_computation.34 | convolution fusion | flops 134217728 | bytes 1703936 | tf_op jit(solution)/shard_map/dot_general | solution.py:419
  101.4 2.1 %add_convert_fusion = bf16[8192,128]{1,0:T(8,128)(2,1)S(1)} fusion(bf16[8192,128]{1,0:T(8,128)(2,1)} %collective-permute-done.14, bf16[8192,128]{1,0:T(8,128)(2,1)S(1)} %get-tuple-element.127), kind=kLoop, calls=%fused_computation | loop fusion | flops 4194304 | bytes 6291456 | tf_op jit(solution)/shard_map/convert_element_type | solution.py:356
  109.3 4.5 %collective-permute-start.22 = (bf16[256,128]{1,0:T(8,128)(2,1)S(1)}, bf16[256,128]{1,0:T(8,128)(2,1)S(1)}, u32[]{:S(2)}, u32[]{:S(2)}) collective-permute-start(bf16[256,128]{1,0:T(8,128)(2,1)S(1)} %add_convert_fusion.12), channel_id=1, source_target_pairs={{0,3},{1,2},{2,1},{3,0},{4,7},{5,6},{6,5},{7,4},{8,11},{9,10},{10,... | collective-permute-start | bytes 196616 | tf_op jit(solution)/shard_map/ppermute | solution.py:309
  114.3 1.7 %collective-permute-done.22 = bf16[256,128]{1,0:T(8,128)(2,1)S(1)} collective-permute-done((bf16[256,128]{1,0:T(8,128)(2,1)S(1)}, bf16[256,128]{1,0:T(8,128)(2,1)S(1)}, u32[]{:S(2)}, u32[]{:S(2)}) %collective-permute-start.22) | collective-permute-done | bytes 65568 | tf_op jit(solution)/shard_map/ppermute | solution.py:309
  116.0 2.5 %collective-permute-done.21 = bf16[256,128]{1,0:T(8,128)(2,1)S(1)} collective-permute-done((bf16[256,128]{1,0:T(8,128)(2,1)S(1)}, bf16[256,128]{1,0:T(8,128)(2,1)S(1)}, u32[]{:S(2)}, u32[]{:S(2)}) %collective-permute-start.21) | collective-permute-done | bytes 65568 | tf_op jit(solution)/shard_map/ppermute | solution.py:309
  118.5 2.7 %collective-permute-done.17 = bf16[2048,128]{1,0:T(8,128)(2,1)S(1)} collective-permute-done((bf16[2048,128]{1,0:T(8,128)(2,1)S(1)}, bf16[2048,128]{1,0:T(8,128)(2,1)S(1)}, u32[]{:S(2)}, u32[]{:S(2)}) %collective-permute-start.17) | collective-permute-done | bytes 524320 | tf_op jit(solution)/shard_map/ppermute | solution.py:309
  127.8 5.1 %collective-permute-done.23 = bf16[1024,128]{1,0:T(8,128)(2,1)S(1)} collective-permute-done((bf16[1024,128]{1,0:T(8,128)(2,1)S(1)}, bf16[1024,128]{1,0:T(8,128)(2,1)S(1)}, u32[]{:S(2)}, u32[]{:S(2)}) %collective-permute-start.23) | collective-permute-done | bytes 262176 | tf_op jit(solution)/shard_map/ppermute | solution.py:309
  133.1 1.8 %collective-permute-start.28 = (bf16[256,128]{1,0:T(8,128)(2,1)S(1)}, bf16[256,128]{1,0:T(8,128)(2,1)S(1)}, u32[]{:S(2)}, u32[]{:S(2)}) collective-permute-start(bf16[256,128]{1,0:T(8,128)(2,1)S(1)} %add_convert_fusion.10), channel_id=1, source_target_pairs={{0,4},{4,0},{8,12},{12,8},{16,20},{20,16},{24,28},{28,24},{1,5},{5... | collective-permute-start | bytes 196616 | tf_op jit(solution)/shard_map/ppermute | solution.py:309
  135.0 1.4 %convolution_convert_fusion = bf16[2048,256]{1,0:T(8,128)(2,1)} fusion(bf16[256,256]{1,0:T(8,128)(2,1)S(1)} %copy-done, bf16[2048,128]{1,0:T(8,128)(2,1)S(1)} %pad_maximum_fusion.1, bf16[2048,128]{1,0:T(8,128)(2,1)S(1)} %pad_maximum_fusion), kind=kOutput, calls=%fused_computation.2 | convolution fusion | flops 271056896 | bytes 2228224 | tf_op jit(solution)/shard_map/dot_general | solution.py:505
  (98 shorter events, 26.1 us)
Async XLA Ops:
  0.6 134.4 %copy-start = (bf16[256,256]{1,0:T(8,128)(2,1)S(1)}, bf16[256,256]{1,0:T(8,128)(2,1)}, u32[]{:S(2)}) copy-start(bf16[256,256]{1,0:T(8,128)(2,1)} %param.11) | copy-start | bytes 393220
  2.3 26.1 %collective-permute-start.1 = (bf16[2048,128]{1,0:T(8,128)(2,1)S(1)}, bf16[2048,128]{1,0:T(8,128)(2,1)S(1)}, u32[]{:S(2)}, u32[]{:S(2)}) collective-permute-start(bf16[2048,128]{1,0:T(8,128)(2,1)S(1)} %get-tuple-element.91.refs_0_), channel_id=1, source_target_pairs={{0,2},{1,3},{2,0},{3,1},{4,6},{5,7},{6,4},{7,5},{8,10},{9,11},{10,... | collective-permute-start | bytes 1572872 | tf_op jit(solution)/shard_map/ppermute | solution.py:309
  5.5 22.9 %collective-permute-start = (bf16[2048,128]{1,0:T(8,128)(2,1)S(1)}, bf16[2048,128]{1,0:T(8,128)(2,1)S(1)}, u32[]{:S(2)}, u32[]{:S(2)}) collective-permute-start(bf16[2048,128]{1,0:T(8,128)(2,1)S(1)} %get-tuple-element.91.refs_0_), channel_id=1, source_target_pairs={{0,1},{1,0},{2,3},{3,2},{4,5},{5,4},{6,7},{7,6},{8,9},{9,8},{10,11... | collective-permute-start | bytes 1572872 | tf_op jit(solution)/shard_map/ppermute | solution.py:309
  10.2 25.7 %collective-permute-start.7 = (bf16[2048,256]{1,0:T(8,128)(2,1)}, bf16[2048,256]{1,0:T(8,128)(2,1)S(1)}, u32[]{:S(2)}, u32[]{:S(2)}) collective-permute-start(bf16[2048,256]{1,0:T(8,128)(2,1)} %param.10), channel_id=1, source_target_pairs={{0,16},{4,20},{8,24},{12,28},{16,0},{20,4},{24,8},{28,12},{1,17},{... | collective-permute-start | bytes 3145736 | tf_op jit(solution)/shard_map/ppermute | solution.py:309
  11.5 24.4 %collective-permute-start.6 = (bf16[2048,256]{1,0:T(8,128)(2,1)}, bf16[2048,256]{1,0:T(8,128)(2,1)S(1)}, u32[]{:S(2)}, u32[]{:S(2)}) collective-permute-start(bf16[2048,256]{1,0:T(8,128)(2,1)} %param.10), channel_id=1, source_target_pairs={{0,8},{4,12},{8,0},{12,4},{16,24},{20,28},{24,16},{28,20},{1,9},{5... | collective-permute-start | bytes 3145736 | tf_op jit(solution)/shard_map/ppermute | solution.py:309
  28.5 7.5 %collective-permute-start.4 = (bf16[2048,128]{1,0:T(8,128)(2,1)S(1)}, bf16[2048,128]{1,0:T(8,128)(2,1)S(1)}, u32[]{:S(2)}, u32[]{:S(2)}) collective-permute-start(bf16[2048,128]{1,0:T(8,128)(2,1)S(1)} %get-tuple-element.91.refs_0_), channel_id=1, source_target_pairs={{1,2},{2,1},{5,6},{6,5},{9,10},{10,9},{13,14},{14,13},{17,18},{18,... | collective-permute-start | bytes 1572872 | tf_op jit(solution)/shard_map/ppermute | solution.py:327
  29.2 14.3 %collective-permute-start.5 = (bf16[2048,128]{1,0:T(8,128)(2,1)S(1)}, bf16[2048,128]{1,0:T(8,128)(2,1)S(1)}, u32[]{:S(2)}, u32[]{:S(2)}) collective-permute-start(bf16[2048,128]{1,0:T(8,128)(2,1)S(1)} %collective-permute-done.1.refs_2_), channel_id=1, source_target_pairs={{1,0},{2,3},{5,4},{6,7},{9,8},{10,11},{13,12},{14,15},{17,16},{18,... | collective-permute-start | bytes 1572872 | tf_op jit(solution)/shard_map/ppermute | solution.py:327
  35.9 14.9 %copy-start.8 = (bf16[2048,256]{1,0:T(8,128)(2,1)}, bf16[2048,256]{1,0:T(8,128)(2,1)S(1)}, u32[]{:S(2)}) copy-start(bf16[2048,256]{1,0:T(8,128)(2,1)S(1)} %collective-permute-done.7) | copy-start | bytes 3145732
  36.0 14.9 %copy-start.10 = (bf16[2048,256]{1,0:T(8,128)(2,1)}, bf16[2048,256]{1,0:T(8,128)(2,1)S(1)}, u32[]{:S(2)}) copy-start(bf16[2048,256]{1,0:T(8,128)(2,1)S(1)} %collective-permute-done.6) | copy-start | bytes 3145732
  43.5 20.0 %collective-permute-start.9 = (bf16[1024,256]{1,0:T(8,128)(2,1)S(1)}, bf16[1024,256]{1,0:T(8,128)(2,1)S(1)}, u32[]{:S(2)}, u32[]{:S(2)}) collective-permute-start(bf16[1024,256]{1,0:T(8,128)(2,1)S(1)} %slice.111), channel_id=1, source_target_pairs={{0,8},{4,12},{8,0},{12,4},{16,24},{20,28},{24,16},{28,20},{1,9},{5... | collective-permute-start | bytes 1572872 | tf_op jit(solution)/shard_map/ppermute | solution.py:309
  44.8 18.7 %collective-permute-start.8 = (bf16[1024,256]{1,0:T(8,128)(2,1)S(1)}, bf16[1024,256]{1,0:T(8,128)(2,1)S(1)}, u32[]{:S(2)}, u32[]{:S(2)}) collective-permute-start(bf16[1024,256]{1,0:T(8,128)(2,1)S(1)} %slice.110), channel_id=1, source_target_pairs={{0,16},{4,20},{8,24},{12,28},{16,0},{20,4},{24,8},{28,12},{1,17},{... | collective-permute-start | bytes 1572872 | tf_op jit(solution)/shard_map/ppermute | solution.py:309
  46.1 24.3 %collective-permute-start.3 = (bf16[2048,128]{1,0:T(8,128)(2,1)S(1)}, bf16[2048,128]{1,0:T(8,128)(2,1)S(1)}, u32[]{:S(2)}, u32[]{:S(2)}) collective-permute-start(bf16[2048,128]{1,0:T(8,128)(2,1)S(1)} %get-tuple-element.109.refs_0_), channel_id=1, source_target_pairs={{0,2},{1,3},{2,0},{3,1},{4,6},{5,7},{6,4},{7,5},{8,10},{9,11},{10,... | collective-permute-start | bytes 1572872 | tf_op jit(solution)/shard_map/ppermute | solution.py:309
  48.7 21.7 %collective-permute-start.2 = (bf16[2048,128]{1,0:T(8,128)(2,1)S(1)}, bf16[2048,128]{1,0:T(8,128)(2,1)S(1)}, u32[]{:S(2)}, u32[]{:S(2)}) collective-permute-start(bf16[2048,128]{1,0:T(8,128)(2,1)S(1)} %get-tuple-element.109.refs_0_), channel_id=1, source_target_pairs={{0,1},{1,0},{2,3},{3,2},{4,5},{5,4},{6,7},{7,6},{8,9},{9,8},{10,11... | collective-permute-start | bytes 1572872 | tf_op jit(solution)/shard_map/ppermute | solution.py:309
  70.4 10.8 %collective-permute-start.12 = (bf16[2048,128]{1,0:T(8,128)(2,1)S(1)}, bf16[2048,128]{1,0:T(8,128)(2,1)S(1)}, u32[]{:S(2)}, u32[]{:S(2)}) collective-permute-start(bf16[2048,128]{1,0:T(8,128)(2,1)S(1)} %bitcast.61), channel_id=1, source_target_pairs={{0,8},{4,12},{8,0},{12,4},{16,24},{20,28},{24,16},{28,20},{1,9},{5... | collective-permute-start | bytes 1572872 | tf_op jit(solution)/shard_map/ppermute | solution.py:309
  70.6 10.7 %collective-permute-start.13 = (bf16[2048,128]{1,0:T(8,128)(2,1)S(1)}, bf16[2048,128]{1,0:T(8,128)(2,1)S(1)}, u32[]{:S(2)}, u32[]{:S(2)}) collective-permute-start(bf16[2048,128]{1,0:T(8,128)(2,1)S(1)} %bitcast.60), channel_id=1, source_target_pairs={{0,16},{4,20},{8,24},{12,28},{16,0},{20,4},{24,8},{28,12},{1,17},{... | collective-permute-start | bytes 1572872 | tf_op jit(solution)/shard_map/ppermute | solution.py:309
  70.8 12.3 %collective-permute-start.10 = (bf16[2048,128]{1,0:T(8,128)(2,1)S(1)}, bf16[2048,128]{1,0:T(8,128)(2,1)S(1)}, u32[]{:S(2)}, u32[]{:S(2)}) collective-permute-start(bf16[2048,128]{1,0:T(8,128)(2,1)S(1)} %get-tuple-element.109.refs_0_), channel_id=1, source_target_pairs={{1,2},{2,1},{5,6},{6,5},{9,10},{10,9},{13,14},{14,13},{17,18},{18,... | collective-permute-start | bytes 1572872 | tf_op jit(solution)/shard_map/ppermute | solution.py:327
  71.5 13.9 %collective-permute-start.11 = (bf16[2048,128]{1,0:T(8,128)(2,1)S(1)}, bf16[2048,128]{1,0:T(8,128)(2,1)S(1)}, u32[]{:S(2)}, u32[]{:S(2)}) collective-permute-start(bf16[2048,128]{1,0:T(8,128)(2,1)S(1)} %collective-permute-done.3.refs_2_), channel_id=1, source_target_pairs={{1,0},{2,3},{5,4},{6,7},{9,8},{10,11},{13,12},{14,15},{17,16},{18,... | collective-permute-start | bytes 1572872 | tf_op jit(solution)/shard_map/ppermute | solution.py:327
  89.9 11.5 %collective-permute-start.14 = (bf16[8192,128]{1,0:T(8,128)(2,1)}, bf16[8192,128]{1,0:T(8,128)(2,1)}, u32[]{:S(2)}, u32[]{:S(2)}) collective-permute-start(bf16[8192,128]{1,0:T(8,128)(2,1)} %get-tuple-element.128), channel_id=1, source_target_pairs={{0,4},{4,0},{8,12},{12,8},{16,20},{20,16},{24,28},{28,24},{1,5},{5... | collective-permute-start | bytes 6291464 | tf_op jit(solution)/shard_map/ppermute | solution.py:309
  94.4 9.3 %collective-permute-start.15 = (bf16[1024,128]{1,0:T(8,128)(2,1)}, bf16[1024,128]{1,0:T(8,128)(2,1)S(1)}, u32[]{:S(2)}, u32[]{:S(2)}) collective-permute-start(bf16[1024,128]{1,0:T(8,128)(2,1)} %get-tuple-element.143), channel_id=1, source_target_pairs={{0,16},{4,20},{8,24},{12,28},{16,0},{20,4},{24,8},{28,12},{1,17},{... | collective-permute-start | bytes 786440 | tf_op jit(solution)/shard_map/ppermute | solution.py:309
  95.0 8.8 %collective-permute-start.16 = (bf16[1024,128]{1,0:T(8,128)(2,1)}, bf16[1024,128]{1,0:T(8,128)(2,1)S(1)}, u32[]{:S(2)}, u32[]{:S(2)}) collective-permute-start(bf16[1024,128]{1,0:T(8,128)(2,1)} %get-tuple-element.144), channel_id=1, source_target_pairs={{0,8},{4,12},{8,0},{12,4},{16,24},{20,28},{24,16},{28,20},{1,9},{5... | collective-permute-start | bytes 786440 | tf_op jit(solution)/shard_map/ppermute | solution.py:309
  106.9 2.4 %collective-permute-start.19 = (bf16[256,128]{1,0:T(8,128)(2,1)S(1)}, bf16[256,128]{1,0:T(8,128)(2,1)S(1)}, u32[]{:S(2)}, u32[]{:S(2)}) collective-permute-start(bf16[256,128]{1,0:T(8,128)(2,1)S(1)} %get-tuple-element.186), channel_id=1, source_target_pairs={{0,4},{4,0},{8,12},{12,8},{16,20},{20,16},{24,28},{28,24},{1,5},{5... | collective-permute-start | bytes 196616 | tf_op jit(solution)/shard_map/ppermute | solution.py:309
  107.6 13.5 %collective-permute-start.17 = (bf16[2048,128]{1,0:T(8,128)(2,1)S(1)}, bf16[2048,128]{1,0:T(8,128)(2,1)S(1)}, u32[]{:S(2)}, u32[]{:S(2)}) collective-permute-start(bf16[2048,128]{1,0:T(8,128)(2,1)S(1)} %bitcast.59), channel_id=1, source_target_pairs={{0,8},{4,12},{8,0},{12,4},{16,24},{20,28},{24,16},{28,20},{1,9},{5... | collective-permute-start | bytes 1572872 | tf_op jit(solution)/shard_map/ppermute | solution.py:309
  108.2 13.2 %collective-permute-start.18 = (bf16[2048,128]{1,0:T(8,128)(2,1)S(1)}, bf16[2048,128]{1,0:T(8,128)(2,1)S(1)}, u32[]{:S(2)}, u32[]{:S(2)}) collective-permute-start(bf16[2048,128]{1,0:T(8,128)(2,1)S(1)} %bitcast.58), channel_id=1, source_target_pairs={{0,16},{4,20},{8,24},{12,28},{16,0},{20,4},{24,8},{28,12},{1,17},{... | collective-permute-start | bytes 1572872 | tf_op jit(solution)/shard_map/ppermute | solution.py:309
  109.3 6.6 %collective-permute-start.22 = (bf16[256,128]{1,0:T(8,128)(2,1)S(1)}, bf16[256,128]{1,0:T(8,128)(2,1)S(1)}, u32[]{:S(2)}, u32[]{:S(2)}) collective-permute-start(bf16[256,128]{1,0:T(8,128)(2,1)S(1)} %add_convert_fusion.12), channel_id=1, source_target_pairs={{0,3},{1,2},{2,1},{3,0},{4,7},{5,6},{6,5},{7,4},{8,11},{9,10},{10,... | collective-permute-start | bytes 196616 | tf_op jit(solution)/shard_map/ppermute | solution.py:309
  113.9 4.6 %collective-permute-start.21 = (bf16[256,128]{1,0:T(8,128)(2,1)S(1)}, bf16[256,128]{1,0:T(8,128)(2,1)S(1)}, u32[]{:S(2)}, u32[]{:S(2)}) collective-permute-start(bf16[256,128]{1,0:T(8,128)(2,1)S(1)} %add_convert_fusion.12), channel_id=1, source_target_pairs={{0,2},{1,3},{2,0},{3,1},{4,6},{5,7},{6,4},{7,5},{8,10},{9,11},{10,... | collective-permute-start | bytes 196616 | tf_op jit(solution)/shard_map/ppermute | solution.py:309
  113.9 4.6 %collective-permute-start.20 = (bf16[256,128]{1,0:T(8,128)(2,1)S(1)}, bf16[256,128]{1,0:T(8,128)(2,1)S(1)}, u32[]{:S(2)}, u32[]{:S(2)}) collective-permute-start(bf16[256,128]{1,0:T(8,128)(2,1)S(1)} %add_convert_fusion.12), channel_id=1, source_target_pairs={{0,1},{1,0},{2,3},{3,2},{4,5},{5,4},{6,7},{7,6},{8,9},{9,8},{10,11... | collective-permute-start | bytes 196616 | tf_op jit(solution)/shard_map/ppermute | solution.py:309
  121.7 4.1 %collective-permute-start.27 = (bf16[256,128]{1,0:T(8,128)(2,1)S(1)}, bf16[256,128]{1,0:T(8,128)(2,1)S(1)}, u32[]{:S(2)}, u32[]{:S(2)}) collective-permute-start(bf16[256,128]{1,0:T(8,128)(2,1)S(1)} %add_convert_fusion.11), channel_id=1, source_target_pairs={{0,24},{4,28},{8,16},{12,20},{16,8},{20,12},{24,0},{28,4},{1,25},{... | collective-permute-start | bytes 196616 | tf_op jit(solution)/shard_map/ppermute | solution.py:309
  122.9 3.6 %collective-permute-start.26 = (bf16[256,128]{1,0:T(8,128)(2,1)S(1)}, bf16[256,128]{1,0:T(8,128)(2,1)S(1)}, u32[]{:S(2)}, u32[]{:S(2)}) collective-permute-start(bf16[256,128]{1,0:T(8,128)(2,1)S(1)} %add_convert_fusion.11), channel_id=1, source_target_pairs={{0,16},{4,20},{8,24},{12,28},{16,0},{20,4},{24,8},{28,12},{1,17},{... | collective-permute-start | bytes 196616 | tf_op jit(solution)/shard_map/ppermute | solution.py:309
  123.9 3.9 %collective-permute-start.25 = (bf16[256,128]{1,0:T(8,128)(2,1)S(1)}, bf16[256,128]{1,0:T(8,128)(2,1)S(1)}, u32[]{:S(2)}, u32[]{:S(2)}) collective-permute-start(bf16[256,128]{1,0:T(8,128)(2,1)S(1)} %add_convert_fusion.11), channel_id=1, source_target_pairs={{0,8},{4,12},{8,0},{12,4},{16,24},{20,28},{24,16},{28,20},{1,9},{5... | collective-permute-start | bytes 196616 | tf_op jit(solution)/shard_map/ppermute | solution.py:309
  124.4 8.5 %collective-permute-start.23 = (bf16[1024,128]{1,0:T(8,128)(2,1)S(1)}, bf16[1024,128]{1,0:T(8,128)(2,1)S(1)}, u32[]{:S(2)}, u32[]{:S(2)}) collective-permute-start(bf16[1024,128]{1,0:T(8,128)(2,1)S(1)} %get-tuple-element.160), channel_id=1, source_target_pairs={{0,16},{4,20},{8,24},{12,28},{16,0},{20,4},{24,8},{28,12},{1,17},{... | collective-permute-start | bytes 786440 | tf_op jit(solution)/shard_map/ppermute | solution.py:309
  125.4 7.6 %collective-permute-start.24 = (bf16[1024,128]{1,0:T(8,128)(2,1)S(1)}, bf16[1024,128]{1,0:T(8,128)(2,1)S(1)}, u32[]{:S(2)}, u32[]{:S(2)}) collective-permute-start(bf16[1024,128]{1,0:T(8,128)(2,1)S(1)} %get-tuple-element.162), channel_id=1, source_target_pairs={{0,8},{4,12},{8,0},{12,4},{16,24},{20,28},{24,16},{28,20},{1,9},{5... | collective-permute-start | bytes 786440 | tf_op jit(solution)/shard_map/ppermute | solution.py:309
  133.1 3.3 %collective-permute-start.28 = (bf16[256,128]{1,0:T(8,128)(2,1)S(1)}, bf16[256,128]{1,0:T(8,128)(2,1)S(1)}, u32[]{:S(2)}, u32[]{:S(2)}) collective-permute-start(bf16[256,128]{1,0:T(8,128)(2,1)S(1)} %add_convert_fusion.10), channel_id=1, source_target_pairs={{0,4},{4,0},{8,12},{12,8},{16,20},{20,16},{24,28},{28,24},{1,5},{5... | collective-permute-start | bytes 196616 | tf_op jit(solution)/shard_map/ppermute | solution.py:309
  (9 other events, 45.3 us)

commit v9 on v8

--- a/solution.py
+++ b/solution.py
@@ -470,13 +470,13 @@
     pieces1 = as_pieces(own1, first1, second1, mid, n_col)
     recv0 = exchange_first(stage0, bits)
     acc1 = spmm(plan0, pieces1[:FIRST_PIECES], flipped, None, n_row)
+    pieces1, stage0, acc1 = fence(pieces1, stage0, acc1)
+
+    send1, keep1 = spmm(plan1, pieces1[FIRST_PIECES:], flipped, acc1, n_row)
+    send1, keep1, recv0, stage0, sums0 = fence(send1, keep1, recv0, stage0, sums0)
+
+    stage1, sums1 = stage_sums(keep1, xor_permute(send1, "row", 1), n_row // 2, rows, at_once=True)
     rest0, sent0 = exchange_second(stage0, recv0, bits, rows)
-    pieces1, rest0, sent0, acc1 = fence(pieces1, rest0, sent0, acc1)
-
-    send1, keep1 = spmm(plan1, pieces1[FIRST_PIECES:], flipped, acc1, n_row)
-    send1, keep1, sent0, sums0 = fence(send1, keep1, sent0, sums0)
-
-    stage1, sums1 = stage_sums(keep1, xor_permute(send1, "row", 1), n_row // 2, rows, at_once=True)
     recv0 = send_second(sent0, bits)
     term0 = weight_term(near, sums0)
     stage1, sums1, term0 = fence(stage1, sums1, term0)
@@ -494,9 +494,10 @@
     rest1, sent1 = exchange_second(stage1, recv1, bits, rows)
     rest1, sent1, mine = fence(rest1, sent1, mine)
     recv1 = send_second(sent1, bits)
-    mine = sum_over(mine, "row", range(2, n_row, 2)).astype(jnp.bfloat16)
+    others = [xor_permute(mine, "row", m) for m in range(2, n_row, 2)]
     colgrad1 = exchange_last(rest1, recv1, bits, rows)
     colgrad1, mine = fence(colgrad1, mine)
+    mine = tree_sum([p.astype(jnp.float32) for p in [mine] + others]).astype(jnp.bfloat16)
 
     theirs = xor_permute(mine, "row", 1)
     low, high = jnp.where(even, mine, theirs), jnp.where(even, theirs, mine)

time: 139 us -> 139 us (level)
  the two profiles are of different devices: /device:TPU:1 before, /device:TPU:9 now
where the time goes in v9:
time: 139 us
  starting transfers between devices  42.7 us (31%)
  waiting for transfers between devices  33.1 us (24%)
  Pallas kernels  25.8 us (19%)
  local copies, waits for them, and re-layouts  11.1 us (8%)
  blocking collectives  10.6 us (8%)
  matrix products  7.85 us (6%)
  other arithmetic  5.79 us (4%)
  between operations  1.8 us (1%)
    ppermute x25, starting transfers between devices, xor_permute(): return lax.ppermute(value, axis, [(i, i ^ mask) for i in range(size)])  36 us
    ppermute x25, waiting for transfers between devices, xor_permute(): return lax.ppermute(value, axis, [(i, i ^ mask) for i in range(size)])  25.9 us
    pallas_call x4, Pallas kernels, spmm(): pl.pallas_call(functools.partial(spmm_kernel, [len(p) for p in pieces], l...  13.9 us
    all_to_all x1, blocking collectives, swap_cores(): return lax.all_to_all(both, 'row', 0, 0, axis_index_groups=pairs)  10.6 us
    pallas_call x1, Pallas kernels, flip_tiles(): pl.pallas_call(flip_kernel, out_shape=jax.ShapeDtypeStruct((slots + GROUP...  9.59 us
    unnamed x30, local copies, waits for them, and re-layouts  8.32 us
    ppermute x2, waiting for transfers between devices, gather_second(): lax.ppermute(own, 'col', middles)  7.17 us
    dot_general x10, matrix products, weight_term(): lax.dot_general(f, own, (((0,), (0,)), ((), ())), preferred_element_type=...  6.41 us
  transfers between devices with their start and end apart: 29, of which 14 were waited for; matrix products, arithmetic and copies ran while one was open for 8% of the time, Pallas kernels for 19%

profile of v9, /device:TPU:9, one launch (start us, length us, event | category | flops | bytes accessed | tf_op | source)
XLA Modules:
  0.0 138.8 jit_solution(12827575181502998367)
XLA Ops:
  0.7 1.7 %compare_select_fusion = (bf16[2048,128]{1,0:T(8,128)(2,1)S(1)}, bf16[2048,128]{1,0:T(8,128)(2,1)S(1)}) fusion(bf16[2048,256]{1,0:T(8,128)(2,1)} %param.8, bf16[2048,256]{1,0:T(8,128)(2,1)} %param.9), kind=kLoop, calls=%fused_computation.21 | loop fusion | flops 1048576 | bytes 3145728 | tf_op jit(solution)/shard_map/jit(_where)/select_n | solution.py:440
  2.3 2.4 %collective-permute-start.1 = (bf16[2048,128]{1,0:T(8,128)(2,1)S(1)}, bf16[2048,128]{1,0:T(8,128)(2,1)S(1)}, u32[]{:S(2)}, u32[]{:S(2)}) collective-permute-start(bf16[2048,128]{1,0:T(8,128)(2,1)S(1)} %get-tuple-element.91.refs_0_), channel_id=1, source_target_pairs={{0,2},{1,3},{2,0},{3,1},{4,6},{5,7},{6,4},{7,5},{8,10},{9,11},{10,... | collective-permute-start | bytes 1572872 | tf_op jit(solution)/shard_map/ppermute | solution.py:309
  5.9 2.3 %plan_slots.1 = (s32[8,512]{1,0:T(8,128)S(1)}, s32[8,512]{1,0:T(8,128)S(1)}, s32[1,320]{1,0:T(1,128)S(1)}) custom-call(s32[4]{0:T(128)S(1)} %pad_add_fusion.place_ref, s32[1,320]{1,0:T(1,128)S(1)} %bitcast.45, s32[1,320]{1,0:T(1,128)S(1)} %bitcast.47, s32[320,1]{1,0:T(8,128)S(1)} %copy.10.rows_c, s32[320,1]{1,0:T(8,128)S(1)} %copy.11.cols_c), custom_call_target="tpu_custom_call" | custom-call | bytes 4096 | tf_op jit(solution)/shard_map/plan_slots/pallas_call | solution.py:120
  10.8 4.0 %copy-done.3 = bf16[1,1,320,128,128]{4,3,2,1,0:T(8,128)(2,1)S(1)} copy-done((bf16[1,1,320,128,128]{4,3,2,1,0:T(8,128)(2,1)S(1)}, bf16[1,1,320,128,128]{4,3,2,1,0:T(8,128)(2,1)}, u32[]{:S(2)}) %copy-start.3) | copy-done | bytes 10485784
  14.7 9.6 %flip_tiles.1.refs_3_.refs_2_ = bf16[352,128,128]{2,1,0:T(8,128)(2,1)S(1)} custom-call(s32[1,320]{1,0:T(1,128)S(1)} %get-tuple-element.87.slot_ref, bf16[320,128,128]{2,1,0:T(8,128)(2,1)S(1)} %bitcast.43), custom_call_target="tpu_custom_call" | custom-call | bytes 4096 | tf_op jit(solution)/shard_map/flip_tiles/pallas_call | solution.py:163
  24.4 3.1 %collective-permute-done.1.refs_2_ = bf16[2048,128]{1,0:T(8,128)(2,1)S(1)} collective-permute-done((bf16[2048,128]{1,0:T(8,128)(2,1)S(1)}, bf16[2048,128]{1,0:T(8,128)(2,1)S(1)}, u32[]{:S(2)}, u32[]{:S(2)}) %collective-permute-start.1) | collective-permute-done | bytes 524320 | tf_op jit(solution)/shard_map/ppermute | solution.py:309
  27.5 2.1 %collective-permute-start.4 = (bf16[2048,128]{1,0:T(8,128)(2,1)S(1)}, bf16[2048,128]{1,0:T(8,128)(2,1)S(1)}, u32[]{:S(2)}, u32[]{:S(2)}) collective-permute-start(bf16[2048,128]{1,0:T(8,128)(2,1)S(1)} %get-tuple-element.91.refs_0_), channel_id=1, source_target_pairs={{1,2},{2,1},{5,6},{6,5},{9,10},{10,9},{13,14},{14,13},{17,18},{18,... | collective-permute-start | bytes 1572872 | tf_op jit(solution)/shard_map/ppermute | solution.py:327
  30.9 4.4 %spmm_first.2 = (bf16[8192,128]{1,0:T(8,128)(2,1)S(1)}, bf16[8192,128]{1,0:T(8,128)(2,1)S(1)}) custom-call(s32[8,512]{1,0:T(8,128)S(1)} %get-tuple-element.90.plan_ref, bf16[2048,128]{1,0:T(8,128)(2,1)S(1)} %get-tuple-element.91.refs_0_, bf16[2048,128]{1,0:T(8,128)(2,1)S(1)} %collective-permute-done.refs_1_, ...), custom_call_target="tpu_custom_call" | custom-call | bytes 4096 | tf_op jit(solution)/shard_map/spmm_first/pallas_call | solution.py:286
  35.4 5.8 %collective-permute-done.4.refs_0_ = bf16[2048,128]{1,0:T(8,128)(2,1)S(1)} collective-permute-done((bf16[2048,128]{1,0:T(8,128)(2,1)S(1)}, bf16[2048,128]{1,0:T(8,128)(2,1)S(1)}, u32[]{:S(2)}, u32[]{:S(2)}) %collective-permute-start.4) | collective-permute-done | bytes 524320 | tf_op jit(solution)/shard_map/ppermute | solution.py:327
  43.8 4.9 %collective-permute-start.3 = (bf16[2048,128]{1,0:T(8,128)(2,1)S(1)}, bf16[2048,128]{1,0:T(8,128)(2,1)S(1)}, u32[]{:S(2)}, u32[]{:S(2)}) collective-permute-start(bf16[2048,128]{1,0:T(8,128)(2,1)S(1)} %get-tuple-element.109.refs_0_), channel_id=1, source_target_pairs={{0,2},{1,3},{2,0},{3,1},{4,6},{5,7},{6,4},{7,5},{8,10},{9,11},{10,... | collective-permute-start | bytes 1572872 | tf_op jit(solution)/shard_map/ppermute | solution.py:309
  48.8 2.4 %spmm_last.2 = bf16[2,8192,128]{2,1,0:T(8,128)(2,1)S(1)} custom-call(s32[8,512]{1,0:T(8,128)S(1)} %get-tuple-element.88.plan_ref, bf16[2048,128]{1,0:T(8,128)(2,1)S(1)} %collective-permute-done.4.refs_0_, bf16[2048,128]{1,0:T(8,128)(2,1)S(1)} %collective-permute-done.5.refs_1_, bf16[352,128,128]{2,1,0:T(8,128)(2,1)S(1)} %flip_tiles.1.refs_3_.refs_2_, ...), custom_call_target="tpu_custom_call" | custom-call | bytes 4096 | tf_op jit(solution)/shard_map/spmm_last/pallas_call | solution.py:286
  51.2 10.6 %all_to_all.5 = bf16[2,8192,128]{2,1,0:T(8,128)(2,1)S(1)} all-to-all(bf16[2,8192,128]{2,1,0:T(8,128)(2,1)S(1)} %spmm_last.2), channel_id=1, replica_groups={{0,4},{8,12},{16,20},{24,28},{1,5},{9,13},{17,21},{25,29},{2,6},{10,14}..., dimensions={0} | all-to-all | bytes 8388608 | tf_op jit(solution)/shard_map/all_to_all | solution.py:341
  64.6 6.0 %collective-permute-done.3.refs_2_ = bf16[2048,128]{1,0:T(8,128)(2,1)S(1)} collective-permute-done((bf16[2048,128]{1,0:T(8,128)(2,1)S(1)}, bf16[2048,128]{1,0:T(8,128)(2,1)S(1)}, u32[]{:S(2)}, u32[]{:S(2)}) %collective-permute-start.3) | collective-permute-done | bytes 524320 | tf_op jit(solution)/shard_map/ppermute | solution.py:309
  70.7 1.9 %collective-permute-start.10 = (bf16[2048,128]{1,0:T(8,128)(2,1)S(1)}, bf16[2048,128]{1,0:T(8,128)(2,1)S(1)}, u32[]{:S(2)}, u32[]{:S(2)}) collective-permute-start(bf16[2048,128]{1,0:T(8,128)(2,1)S(1)} %get-tuple-element.109.refs_0_), channel_id=1, source_target_pairs={{1,2},{2,1},{5,6},{6,5},{9,10},{10,9},{13,14},{14,13},{17,18},{18,... | collective-permute-start | bytes 1572872 | tf_op jit(solution)/shard_map/ppermute | solution.py:327
  74.5 4.3 %copy-done.2 = bf16[352,128,128]{2,1,0:T(8,128)(2,1)S(1)} copy-done((bf16[352,128,128]{2,1,0:T(8,128)(2,1)S(1)}, bf16[352,128,128]{2,1,0:T(8,128)(2,1)}, u32[]{:S(2)}) %copy-start.2) | copy-done | bytes 11534360
  78.8 4.4 %spmm_first.3 = (bf16[8192,128]{1,0:T(8,128)(2,1)S(1)}, bf16[8192,128]{1,0:T(8,128)(2,1)S(1)}) custom-call(s32[8,512]{1,0:T(8,128)S(1)} %get-tuple-element.90.plan_ref, bf16[2048,128]{1,0:T(8,128)(2,1)S(1)} %get-tuple-element.109.refs_0_, bf16[2048,128]{1,0:T(8,128)(2,1)S(1)} %collective-permute-done.2.refs_1_, ...), custom_call_target="tpu_custom_call" | custom-call | bytes 4096 | tf_op jit(solution)/shard_map/spmm_first/pallas_call | solution.py:286
  84.6 2.6 %spmm_last.3 = (bf16[8192,128]{1,0:T(8,128)(2,1)S(1)}, bf16[8192,128]{1,0:T(8,128)(2,1)S(1)}) custom-call(s32[8,512]{1,0:T(8,128)S(1)} %get-tuple-element.88.plan_ref, bf16[2048,128]{1,0:T(8,128)(2,1)S(1)} %collective-permute-done.10.refs_0_, bf16[2048,128]{1,0:T(8,128)(2,1)S(1)} %collective-permute-done.11.refs_1_, bf16[352,128,128]{2,1,0:T(8,128)(2,1)S(1)} %copy-done.2, ...), custom_call_target="tpu_custom_call" | custom-call | bytes 4096 | tf_op jit(solution)/shard_map/spmm_last/pallas_call | solution.py:286
  87.2 7.0 %collective-permute-start.14 = (bf16[8192,128]{1,0:T(8,128)(2,1)S(1)}, bf16[8192,128]{1,0:T(8,128)(2,1)S(1)}, u32[]{:S(2)}, u32[]{:S(2)}) collective-permute-start(bf16[8192,128]{1,0:T(8,128)(2,1)S(1)} %get-tuple-element.128), channel_id=1, source_target_pairs={{0,4},{4,0},{8,12},{12,8},{16,20},{20,16},{24,28},{28,24},{1,5},{5... | collective-permute-start | bytes 6291464 | tf_op jit(solution)/shard_map/ppermute | solution.py:309
  94.2 1.5 %add_convert_fusion.4 = (bf16[2048,128]{1,0:T(8,128)(2,1)S(1)}, bf16[2048,128]{1,0:T(8,128)(2,1)S(1)}) fusion(bf16[2048,128]{1,0:T(8,128)(2,1)} %collective-permute-done.13, bf16[2048,128]{1,0:T(8,128)(2,1)S(1)} %bitcast.57, bf16[2048,128]{1,0:T(8,128)(2,1)} %collective-permute-done.12, bf16[2048,128]{1,0:T(8,128)(2,1)S(1)} %bitcast.56), kind=kLoop, calls=%fused_computation.19 | loop fusion | flops 2097152 | bytes 3145728 | tf_op jit(solution)/shard_map/convert_element_type | solution.py:393
  95.9 3.2 %collective-permute-start.15 = (bf16[1024,128]{1,0:T(8,128)(2,1)S(1)}, bf16[1024,128]{1,0:T(8,128)(2,1)S(1)}, u32[]{:S(2)}, u32[]{:S(2)}) collective-permute-start(bf16[1024,128]{1,0:T(8,128)(2,1)S(1)} %get-tuple-element.182), channel_id=1, source_target_pairs={{0,16},{4,20},{8,24},{12,28},{16,0},{20,4},{24,8},{28,12},{1,17},{... | collective-permute-start | bytes 786440 | tf_op jit(solution)/shard_map/ppermute | solution.py:309
  99.4 1.5 %fusion.28 = f32[256,128]{1,0:T(8,128)S(1)} fusion(bf16[1024,256]{1,0:T(8,128)(2,1)} %collective-permute-done.8, bf16[8192,128]{1,0:T(8,128)(2,1)S(1)} %copy-done.7), kind=kOutput, calls=%fused_computation.49 | convolution fusion | flops 67108864 | bytes 917504 | tf_op jit(solution)/shard_map/dot_general | solution.py:419
  103.5 1.8 %collective-permute-done.15 = bf16[1024,128]{1,0:T(8,128)(2,1)S(1)} collective-permute-done((bf16[1024,128]{1,0:T(8,128)(2,1)S(1)}, bf16[1024,128]{1,0:T(8,128)(2,1)S(1)}, u32[]{:S(2)}, u32[]{:S(2)}) %collective-permute-start.15) | collective-permute-done | bytes 262176 | tf_op jit(solution)/shard_map/ppermute | solution.py:309
  109.6 1.5 %collective-permute-start.18 = (bf16[2048,128]{1,0:T(8,128)(2,1)S(1)}, bf16[2048,128]{1,0:T(8,128)(2,1)S(1)}, u32[]{:S(2)}, u32[]{:S(2)}) collective-permute-start(bf16[2048,128]{1,0:T(8,128)(2,1)S(1)} %bitcast.58), channel_id=1, source_target_pairs={{0,16},{4,20},{8,24},{12,28},{16,0},{20,4},{24,8},{28,12},{1,17},{... | collective-permute-start | bytes 1572872 | tf_op jit(solution)/shard_map/ppermute | solution.py:309
  111.6 2.4 %collective-permute-start.20 = (bf16[256,128]{1,0:T(8,128)(2,1)S(1)}, bf16[256,128]{1,0:T(8,128)(2,1)S(1)}, u32[]{:S(2)}, u32[]{:S(2)}) collective-permute-start(bf16[256,128]{1,0:T(8,128)(2,1)S(1)} %add_convert_fusion.12), channel_id=1, source_target_pairs={{0,1},{1,0},{2,3},{3,2},{4,5},{5,4},{6,7},{7,6},{8,9},{9,8},{10,11... | collective-permute-start | bytes 196616 | tf_op jit(solution)/shard_map/ppermute | solution.py:309
  115.6 2.0 %collective-permute-done.20 = bf16[256,128]{1,0:T(8,128)(2,1)S(1)} collective-permute-done((bf16[256,128]{1,0:T(8,128)(2,1)S(1)}, bf16[256,128]{1,0:T(8,128)(2,1)S(1)}, u32[]{:S(2)}, u32[]{:S(2)}) %collective-permute-start.20) | collective-permute-done | bytes 65568 | tf_op jit(solution)/shard_map/ppermute | solution.py:309
  117.6 5.4 %collective-permute-done.17 = bf16[2048,128]{1,0:T(8,128)(2,1)S(1)} collective-permute-done((bf16[2048,128]{1,0:T(8,128)(2,1)S(1)}, bf16[2048,128]{1,0:T(8,128)(2,1)S(1)}, u32[]{:S(2)}, u32[]{:S(2)}) %collective-permute-start.17) | collective-permute-done | bytes 524320 | tf_op jit(solution)/shard_map/ppermute | solution.py:309
  123.4 1.5 %collective-permute-start.23 = (bf16[1024,128]{1,0:T(8,128)(2,1)S(1)}, bf16[1024,128]{1,0:T(8,128)(2,1)S(1)}, u32[]{:S(2)}, u32[]{:S(2)}) collective-permute-start(bf16[1024,128]{1,0:T(8,128)(2,1)S(1)} %get-tuple-element.160), channel_id=1, source_target_pairs={{0,16},{4,20},{8,24},{12,28},{16,0},{20,4},{24,8},{28,12},{1,17},{... | collective-permute-start | bytes 786440 | tf_op jit(solution)/shard_map/ppermute | solution.py:309
  126.2 1.4 collective-permute-start.26
  128.7 1.7 %collective-permute-done.23 = bf16[1024,128]{1,0:T(8,128)(2,1)S(1)} collective-permute-done((bf16[1024,128]{1,0:T(8,128)(2,1)S(1)}, bf16[1024,128]{1,0:T(8,128)(2,1)S(1)}, u32[]{:S(2)}, u32[]{:S(2)}) %collective-permute-start.23) | collective-permute-done | bytes 262176 | tf_op jit(solution)/shard_map/ppermute | solution.py:309
  132.6 1.8 %collective-permute-done.25 = bf16[256,128]{1,0:T(8,128)(2,1)S(1)} collective-permute-done((bf16[256,128]{1,0:T(8,128)(2,1)S(1)}, bf16[256,128]{1,0:T(8,128)(2,1)S(1)}, u32[]{:S(2)}, u32[]{:S(2)}) %collective-permute-start.25) | collective-permute-done | bytes 65568 | tf_op jit(solution)/shard_map/ppermute | solution.py:309
  134.5 2.1 %collective-permute-start.28 = (bf16[256,128]{1,0:T(8,128)(2,1)S(1)}, bf16[256,128]{1,0:T(8,128)(2,1)S(1)}, u32[]{:S(2)}, u32[]{:S(2)}) collective-permute-start(bf16[256,128]{1,0:T(8,128)(2,1)S(1)} %add_convert_fusion.10), channel_id=1, source_target_pairs={{0,4},{4,0},{8,12},{12,8},{16,20},{20,16},{24,28},{28,24},{1,5},{5... | collective-permute-start | bytes 196616 | tf_op jit(solution)/shard_map/ppermute | solution.py:309
  136.6 1.4 %convolution_convert_fusion = bf16[2048,256]{1,0:T(8,128)(2,1)} fusion(bf16[256,256]{1,0:T(8,128)(2,1)S(1)} %copy-done, bf16[2048,128]{1,0:T(8,128)(2,1)S(1)} %pad_maximum_fusion.1, bf16[2048,128]{1,0:T(8,128)(2,1)S(1)} %pad_maximum_fusion), kind=kOutput, calls=%fused_computation.2 | convolution fusion | flops 271056896 | bytes 2228224 | tf_op jit(solution)/shard_map/dot_general | solution.py:506
  (104 shorter events, 28.1 us)
Async XLA Ops:
  0.6 136.0 %copy-start = (bf16[256,256]{1,0:T(8,128)(2,1)S(1)}, bf16[256,256]{1,0:T(8,128)(2,1)}, u32[]{:S(2)}) copy-start(bf16[256,256]{1,0:T(8,128)(2,1)} %param.11) | copy-start | bytes 393220
  2.3 25.1 %collective-permute-start.1 = (bf16[2048,128]{1,0:T(8,128)(2,1)S(1)}, bf16[2048,128]{1,0:T(8,128)(2,1)S(1)}, u32[]{:S(2)}, u32[]{:S(2)}) collective-permute-start(bf16[2048,128]{1,0:T(8,128)(2,1)S(1)} %get-tuple-element.91.refs_0_), channel_id=1, source_target_pairs={{0,2},{1,3},{2,0},{3,1},{4,6},{5,7},{6,4},{7,5},{8,10},{9,11},{10,... | collective-permute-start | bytes 1572872 | tf_op jit(solution)/shard_map/ppermute | solution.py:309
  4.7 22.8 %collective-permute-start = (bf16[2048,128]{1,0:T(8,128)(2,1)S(1)}, bf16[2048,128]{1,0:T(8,128)(2,1)S(1)}, u32[]{:S(2)}, u32[]{:S(2)}) collective-permute-start(bf16[2048,128]{1,0:T(8,128)(2,1)S(1)} %get-tuple-element.91.refs_0_), channel_id=1, source_target_pairs={{0,1},{1,0},{2,3},{3,2},{4,5},{5,4},{6,7},{7,6},{8,9},{9,8},{10,11... | collective-permute-start | bytes 1572872 | tf_op jit(solution)/shard_map/ppermute | solution.py:309
  8.2 27.1 %collective-permute-start.7 = (bf16[2048,256]{1,0:T(8,128)(2,1)}, bf16[2048,256]{1,0:T(8,128)(2,1)S(1)}, u32[]{:S(2)}, u32[]{:S(2)}) collective-permute-start(bf16[2048,256]{1,0:T(8,128)(2,1)} %param.10), channel_id=1, source_target_pairs={{0,16},{4,20},{8,24},{12,28},{16,0},{20,4},{24,8},{28,12},{1,17},{... | collective-permute-start | bytes 3145736 | tf_op jit(solution)/shard_map/ppermute | solution.py:309
  9.6 25.8 %collective-permute-start.6 = (bf16[2048,256]{1,0:T(8,128)(2,1)}, bf16[2048,256]{1,0:T(8,128)(2,1)S(1)}, u32[]{:S(2)}, u32[]{:S(2)}) collective-permute-start(bf16[2048,256]{1,0:T(8,128)(2,1)} %param.10), channel_id=1, source_target_pairs={{0,8},{4,12},{8,0},{12,4},{16,24},{20,28},{24,16},{28,20},{1,9},{5... | collective-permute-start | bytes 3145736 | tf_op jit(solution)/shard_map/ppermute | solution.py:309
  24.3 24.4 %copy-start.1 = (bf16[352,128,128]{2,1,0:T(8,128)(2,1)}, bf16[352,128,128]{2,1,0:T(8,128)(2,1)S(1)}, u32[]{:S(2)}) copy-start(bf16[352,128,128]{2,1,0:T(8,128)(2,1)S(1)} %flip_tiles.1.refs_3_.refs_2_) | copy-start | bytes 34603012
  27.5 13.8 %collective-permute-start.4 = (bf16[2048,128]{1,0:T(8,128)(2,1)S(1)}, bf16[2048,128]{1,0:T(8,128)(2,1)S(1)}, u32[]{:S(2)}, u32[]{:S(2)}) collective-permute-start(bf16[2048,128]{1,0:T(8,128)(2,1)S(1)} %get-tuple-element.91.refs_0_), channel_id=1, source_target_pairs={{1,2},{2,1},{5,6},{6,5},{9,10},{10,9},{13,14},{14,13},{17,18},{18,... | collective-permute-start | bytes 1572872 | tf_op jit(solution)/shard_map/ppermute | solution.py:327
  29.6 11.6 %collective-permute-start.5 = (bf16[2048,128]{1,0:T(8,128)(2,1)S(1)}, bf16[2048,128]{1,0:T(8,128)(2,1)S(1)}, u32[]{:S(2)}, u32[]{:S(2)}) collective-permute-start(bf16[2048,128]{1,0:T(8,128)(2,1)S(1)} %collective-permute-done.1.refs_2_), channel_id=1, source_target_pairs={{1,0},{2,3},{5,4},{6,7},{9,8},{10,11},{13,12},{14,15},{17,16},{18,... | collective-permute-start | bytes 1572872 | tf_op jit(solution)/shard_map/ppermute | solution.py:327
  35.4 15.8 %copy-start.11 = (bf16[2048,256]{1,0:T(8,128)(2,1)}, bf16[2048,256]{1,0:T(8,128)(2,1)S(1)}, u32[]{:S(2)}) copy-start(bf16[2048,256]{1,0:T(8,128)(2,1)S(1)} %collective-permute-done.7) | copy-start | bytes 3145732
  41.3 20.5 %collective-permute-start.9 = (bf16[1024,256]{1,0:T(8,128)(2,1)S(1)}, bf16[1024,256]{1,0:T(8,128)(2,1)S(1)}, u32[]{:S(2)}, u32[]{:S(2)}) collective-permute-start(bf16[1024,256]{1,0:T(8,128)(2,1)S(1)} %slice.111), channel_id=1, source_target_pairs={{0,8},{4,12},{8,0},{12,4},{16,24},{20,28},{24,16},{28,20},{1,9},{5... | collective-permute-start | bytes 1572872 | tf_op jit(solution)/shard_map/ppermute | solution.py:309
  42.6 19.3 %collective-permute-start.8 = (bf16[1024,256]{1,0:T(8,128)(2,1)S(1)}, bf16[1024,256]{1,0:T(8,128)(2,1)}, u32[]{:S(2)}, u32[]{:S(2)}) collective-permute-start(bf16[1024,256]{1,0:T(8,128)(2,1)S(1)} %slice.110), channel_id=1, source_target_pairs={{0,16},{4,20},{8,24},{12,28},{16,0},{20,4},{24,8},{28,12},{1,17},{... | collective-permute-start | bytes 1572872 | tf_op jit(solution)/shard_map/ppermute | solution.py:309
  43.8 26.8 %collective-permute-start.3 = (bf16[2048,128]{1,0:T(8,128)(2,1)S(1)}, bf16[2048,128]{1,0:T(8,128)(2,1)S(1)}, u32[]{:S(2)}, u32[]{:S(2)}) collective-permute-start(bf16[2048,128]{1,0:T(8,128)(2,1)S(1)} %get-tuple-element.109.refs_0_), channel_id=1, source_target_pairs={{0,2},{1,3},{2,0},{3,1},{4,6},{5,7},{6,4},{7,5},{8,10},{9,11},{10,... | collective-permute-start | bytes 1572872 | tf_op jit(solution)/shard_map/ppermute | solution.py:309
  48.8 21.9 %collective-permute-start.2 = (bf16[2048,128]{1,0:T(8,128)(2,1)S(1)}, bf16[2048,128]{1,0:T(8,128)(2,1)S(1)}, u32[]{:S(2)}, u32[]{:S(2)}) collective-permute-start(bf16[2048,128]{1,0:T(8,128)(2,1)S(1)} %get-tuple-element.109.refs_0_), channel_id=1, source_target_pairs={{0,1},{1,0},{2,3},{3,2},{4,5},{5,4},{6,7},{7,6},{8,9},{9,8},{10,11... | collective-permute-start | bytes 1572872 | tf_op jit(solution)/shard_map/ppermute | solution.py:309
  70.7 13.9 %collective-permute-start.10 = (bf16[2048,128]{1,0:T(8,128)(2,1)S(1)}, bf16[2048,128]{1,0:T(8,128)(2,1)S(1)}, u32[]{:S(2)}, u32[]{:S(2)}) collective-permute-start(bf16[2048,128]{1,0:T(8,128)(2,1)S(1)} %get-tuple-element.109.refs_0_), channel_id=1, source_target_pairs={{1,2},{2,1},{5,6},{6,5},{9,10},{10,9},{13,14},{14,13},{17,18},{18,... | collective-permute-start | bytes 1572872 | tf_op jit(solution)/shard_map/ppermute | solution.py:327
  72.6 12.0 %collective-permute-start.11 = (bf16[2048,128]{1,0:T(8,128)(2,1)S(1)}, bf16[2048,128]{1,0:T(8,128)(2,1)S(1)}, u32[]{:S(2)}, u32[]{:S(2)}) collective-permute-start(bf16[2048,128]{1,0:T(8,128)(2,1)S(1)} %collective-permute-done.3.refs_2_), channel_id=1, source_target_pairs={{1,0},{2,3},{5,4},{6,7},{9,8},{10,11},{13,12},{14,15},{17,16},{18,... | collective-permute-start | bytes 1572872 | tf_op jit(solution)/shard_map/ppermute | solution.py:327
  73.9 13.2 %collective-permute-start.12 = (bf16[2048,128]{1,0:T(8,128)(2,1)}, bf16[2048,128]{1,0:T(8,128)(2,1)}, u32[]{:S(2)}, u32[]{:S(2)}) collective-permute-start(bf16[2048,128]{1,0:T(8,128)(2,1)} %bitcast.11), channel_id=1, source_target_pairs={{0,8},{4,12},{8,0},{12,4},{16,24},{20,28},{24,16},{28,20},{1,9},{5... | collective-permute-start | bytes 1572872 | tf_op jit(solution)/shard_map/ppermute | solution.py:309
  74.3 12.9 %collective-permute-start.13 = (bf16[2048,128]{1,0:T(8,128)(2,1)}, bf16[2048,128]{1,0:T(8,128)(2,1)}, u32[]{:S(2)}, u32[]{:S(2)}) collective-permute-start(bf16[2048,128]{1,0:T(8,128)(2,1)} %bitcast.13), channel_id=1, source_target_pairs={{0,16},{4,20},{8,24},{12,28},{16,0},{20,4},{24,8},{28,12},{1,17},{... | collective-permute-start | bytes 1572872 | tf_op jit(solution)/shard_map/ppermute | solution.py:309
  87.2 15.2 %collective-permute-start.14 = (bf16[8192,128]{1,0:T(8,128)(2,1)S(1)}, bf16[8192,128]{1,0:T(8,128)(2,1)S(1)}, u32[]{:S(2)}, u32[]{:S(2)}) collective-permute-start(bf16[8192,128]{1,0:T(8,128)(2,1)S(1)} %get-tuple-element.128), channel_id=1, source_target_pairs={{0,4},{4,0},{8,12},{12,8},{16,20},{20,16},{24,28},{28,24},{1,5},{5... | collective-permute-start | bytes 6291464 | tf_op jit(solution)/shard_map/ppermute | solution.py:309
  95.7 7.8 %collective-permute-start.16 = (bf16[1024,128]{1,0:T(8,128)(2,1)S(1)}, bf16[1024,128]{1,0:T(8,128)(2,1)S(1)}, u32[]{:S(2)}, u32[]{:S(2)}) collective-permute-start(bf16[1024,128]{1,0:T(8,128)(2,1)S(1)} %get-tuple-element.180), channel_id=1, source_target_pairs={{0,8},{4,12},{8,0},{12,4},{16,24},{20,28},{24,16},{28,20},{1,9},{5... | collective-permute-start | bytes 786440 | tf_op jit(solution)/shard_map/ppermute | solution.py:309
  95.9 9.5 %collective-permute-start.15 = (bf16[1024,128]{1,0:T(8,128)(2,1)S(1)}, bf16[1024,128]{1,0:T(8,128)(2,1)S(1)}, u32[]{:S(2)}, u32[]{:S(2)}) collective-permute-start(bf16[1024,128]{1,0:T(8,128)(2,1)S(1)} %get-tuple-element.182), channel_id=1, source_target_pairs={{0,16},{4,20},{8,24},{12,28},{16,0},{20,4},{24,8},{28,12},{1,17},{... | collective-permute-start | bytes 786440 | tf_op jit(solution)/shard_map/ppermute | solution.py:309
  108.5 2.7 %collective-permute-start.19 = (bf16[256,128]{1,0:T(8,128)(2,1)S(1)}, bf16[256,128]{1,0:T(8,128)(2,1)S(1)}, u32[]{:S(2)}, u32[]{:S(2)}) collective-permute-start(bf16[256,128]{1,0:T(8,128)(2,1)S(1)} %get-tuple-element.186), channel_id=1, source_target_pairs={{0,4},{4,0},{8,12},{12,8},{16,20},{20,16},{24,28},{28,24},{1,5},{5... | collective-permute-start | bytes 196616 | tf_op jit(solution)/shard_map/ppermute | solution.py:309
  109.5 13.5 %collective-permute-start.17 = (bf16[2048,128]{1,0:T(8,128)(2,1)S(1)}, bf16[2048,128]{1,0:T(8,128)(2,1)S(1)}, u32[]{:S(2)}, u32[]{:S(2)}) collective-permute-start(bf16[2048,128]{1,0:T(8,128)(2,1)S(1)} %bitcast.59), channel_id=1, source_target_pairs={{0,8},{4,12},{8,0},{12,4},{16,24},{20,28},{24,16},{28,20},{1,9},{5... | collective-permute-start | bytes 1572872 | tf_op jit(solution)/shard_map/ppermute | solution.py:309
  109.6 13.5 %collective-permute-start.18 = (bf16[2048,128]{1,0:T(8,128)(2,1)S(1)}, bf16[2048,128]{1,0:T(8,128)(2,1)S(1)}, u32[]{:S(2)}, u32[]{:S(2)}) collective-permute-start(bf16[2048,128]{1,0:T(8,128)(2,1)S(1)} %bitcast.58), channel_id=1, source_target_pairs={{0,16},{4,20},{8,24},{12,28},{16,0},{20,4},{24,8},{28,12},{1,17},{... | collective-permute-start | bytes 1572872 | tf_op jit(solution)/shard_map/ppermute | solution.py:309
  111.2 3.7 %collective-permute-start.22 = (bf16[256,128]{1,0:T(8,128)(2,1)S(1)}, bf16[256,128]{1,0:T(8,128)(2,1)S(1)}, u32[]{:S(2)}, u32[]{:S(2)}) collective-permute-start(bf16[256,128]{1,0:T(8,128)(2,1)S(1)} %add_convert_fusion.12), channel_id=1, source_target_pairs={{0,3},{1,2},{2,1},{3,0},{4,7},{5,6},{6,5},{7,4},{8,11},{9,10},{10,... | collective-permute-start | bytes 196616 | tf_op jit(solution)/shard_map/ppermute | solution.py:309
  111.3 4.3 %collective-permute-start.21 = (bf16[256,128]{1,0:T(8,128)(2,1)S(1)}, bf16[256,128]{1,0:T(8,128)(2,1)S(1)}, u32[]{:S(2)}, u32[]{:S(2)}) collective-permute-start(bf16[256,128]{1,0:T(8,128)(2,1)S(1)} %add_convert_fusion.12), channel_id=1, source_target_pairs={{0,2},{1,3},{2,0},{3,1},{4,6},{5,7},{6,4},{7,5},{8,10},{9,11},{10,... | collective-permute-start | bytes 196616 | tf_op jit(solution)/shard_map/ppermute | solution.py:309
  111.6 6.0 %collective-permute-start.20 = (bf16[256,128]{1,0:T(8,128)(2,1)S(1)}, bf16[256,128]{1,0:T(8,128)(2,1)S(1)}, u32[]{:S(2)}, u32[]{:S(2)}) collective-permute-start(bf16[256,128]{1,0:T(8,128)(2,1)S(1)} %add_convert_fusion.12), channel_id=1, source_target_pairs={{0,1},{1,0},{2,3},{3,2},{4,5},{5,4},{6,7},{7,6},{8,9},{9,8},{10,11... | collective-permute-start | bytes 196616 | tf_op jit(solution)/shard_map/ppermute | solution.py:309
  123.4 7.0 %collective-permute-start.23 = (bf16[1024,128]{1,0:T(8,128)(2,1)S(1)}, bf16[1024,128]{1,0:T(8,128)(2,1)S(1)}, u32[]{:S(2)}, u32[]{:S(2)}) collective-permute-start(bf16[1024,128]{1,0:T(8,128)(2,1)S(1)} %get-tuple-element.160), channel_id=1, source_target_pairs={{0,16},{4,20},{8,24},{12,28},{16,0},{20,4},{24,8},{28,12},{1,17},{... | collective-permute-start | bytes 786440 | tf_op jit(solution)/shard_map/ppermute | solution.py:309
  125.0 6.6 %collective-permute-start.24 = (bf16[1024,128]{1,0:T(8,128)(2,1)S(1)}, bf16[1024,128]{1,0:T(8,128)(2,1)S(1)}, u32[]{:S(2)}, u32[]{:S(2)}) collective-permute-start(bf16[1024,128]{1,0:T(8,128)(2,1)S(1)} %get-tuple-element.162), channel_id=1, source_target_pairs={{0,8},{4,12},{8,0},{12,4},{16,24},{20,28},{24,16},{28,20},{1,9},{5... | collective-permute-start | bytes 786440 | tf_op jit(solution)/shard_map/ppermute | solution.py:309
  126.1 6.5 %collective-permute-start.27 = (bf16[256,128]{1,0:T(8,128)(2,1)S(1)}, bf16[256,128]{1,0:T(8,128)(2,1)S(1)}, u32[]{:S(2)}, u32[]{:S(2)}) collective-permute-start(bf16[256,128]{1,0:T(8,128)(2,1)S(1)} %add_convert_fusion.11), channel_id=1, source_target_pairs={{0,24},{4,28},{8,16},{12,20},{16,8},{20,12},{24,0},{28,4},{1,25},{... | collective-permute-start | bytes 196616 | tf_op jit(solution)/shard_map/ppermute | solution.py:309
  126.2 6.4 %collective-permute-start.26 = (bf16[256,128]{1,0:T(8,128)(2,1)S(1)}, bf16[256,128]{1,0:T(8,128)(2,1)S(1)}, u32[]{:S(2)}, u32[]{:S(2)}) collective-permute-start(bf16[256,128]{1,0:T(8,128)(2,1)S(1)} %add_convert_fusion.11), channel_id=1, source_target_pairs={{0,16},{4,20},{8,24},{12,28},{16,0},{20,4},{24,8},{28,12},{1,17},{... | collective-permute-start | bytes 196616 | tf_op jit(solution)/shard_map/ppermute | solution.py:309
  127.6 6.8 %collective-permute-start.25 = (bf16[256,128]{1,0:T(8,128)(2,1)S(1)}, bf16[256,128]{1,0:T(8,128)(2,1)S(1)}, u32[]{:S(2)}, u32[]{:S(2)}) collective-permute-start(bf16[256,128]{1,0:T(8,128)(2,1)S(1)} %add_convert_fusion.11), channel_id=1, source_target_pairs={{0,8},{4,12},{8,0},{12,4},{16,24},{20,28},{24,16},{28,20},{1,9},{5... | collective-permute-start | bytes 196616 | tf_op jit(solution)/shard_map/ppermute | solution.py:309
  134.5 3.6 %collective-permute-start.28 = (bf16[256,128]{1,0:T(8,128)(2,1)S(1)}, bf16[256,128]{1,0:T(8,128)(2,1)S(1)}, u32[]{:S(2)}, u32[]{:S(2)}) collective-permute-start(bf16[256,128]{1,0:T(8,128)(2,1)S(1)} %add_convert_fusion.10), channel_id=1, source_target_pairs={{0,4},{4,0},{8,12},{12,8},{16,20},{20,16},{24,28},{28,24},{1,5},{5... | collective-permute-start | bytes 196616 | tf_op jit(solution)/shard_map/ppermute | solution.py:309
  (12 other events, 80.5 us)

commit v10 on v9

--- a/solution.py
+++ b/solution.py
@@ -444,7 +444,7 @@
     place = jnp.stack([live_counts.reshape(()), row, col, mid.astype(jnp.int32)])
     plan0, plan1, slot = make_plans(tile_rows, tile_cols, place, n_row, nodes // SIDE)
     flipped = flip_tiles(slot, tiles.reshape(slots, SIDE, SIDE))
-    features, plan0 = fence(features, plan0)
+    features, own1 = fence(features, own1)
     near = [[features]]
     for bit in bits[:2]:
         near.append([xor_permute(features, "row", bit)])
@@ -454,15 +454,15 @@
     acc0 = spmm(plan0, [[own0], [first0[0]], [first0[1]]], flipped, None, n_row)
     own1, acc0 = fence(own1, acc0)
     first1 = gather_first(own1)
-    pieces0 = as_pieces(own0, first0, second0, mid, n_col)
-    pieces0, near, acc0 = fence(pieces0, near, acc0)
-
     near.append([xor_permute(near[1][0][:rows], "row", bits[1]), xor_permute(near[2][0][rows:], "row", bits[0])])
     for bit in bits[2:]:
         near += [[xor_permute(f, "row", bit) for f in parts] for parts in near]
+    pieces0 = as_pieces(own0, first0, second0, mid, n_col)
+    pieces0, acc0 = fence(pieces0, acc0)
+
     (both0,) = spmm(plan1, pieces0[FIRST_PIECES:], flipped, acc0, n_row, by_core=True)
+    both0, near = fence(both0, near)
     got0 = swap_cores(both0)
-    got0, near = fence(got0, near)
     stage0, sums0 = stage_sums(got0[0], got0[1], n_row // 2, rows, at_once=True)
     own1, first1, stage0, sums0 = fence(own1, first1, stage0, sums0)
 
@@ -478,12 +478,11 @@
     stage1, sums1 = stage_sums(keep1, xor_permute(send1, "row", 1), n_row // 2, rows, at_once=True)
     rest0, sent0 = exchange_second(stage0, recv0, bits, rows)
     recv0 = send_second(sent0, bits)
-    term0 = weight_term(near, sums0)
-    stage1, sums1, term0 = fence(stage1, sums1, term0)
-    stage1, sums1, term0, rest0, recv0 = fence(stage1, sums1, term0, rest0, recv0)
+    term0, term1 = weight_term(near, sums0), weight_term(near, sums1)
+    stage1, term0, term1 = fence(stage1, term0, term1)
+    stage1, term0, term1, rest0, recv0 = fence(stage1, term0, term1, rest0, recv0)
 
     recv1 = exchange_first(stage1, bits)
-    term1 = weight_term(near, sums1)
     even = (row & 1) == 0
     theirs, mine = jnp.where(even, term1, term0), jnp.where(even, term0, term1)
     mine = add_f32(mine, xor_permute(theirs, "row", 1)).astype(jnp.bfloat16)

time: 139 us -> 141 us (1.014)
  the two profiles are of different devices: /device:TPU:9 before, /device:TPU:1 now
where the time goes in v10:
time: 141 us; the launch traced here: 139 us
  Pallas kernels  35.3 us (25%)
  starting transfers between devices  35.1 us (25%)
  waiting for transfers between devices  24.9 us (18%)
  local copies, waits for them, and re-layouts  14 us (10%)
  matrix products  13 us (9%)
  blocking collectives  8.8 us (6%)
  other arithmetic  5.8 us (4%)
  between operations  1.81 us (1%)
    ppermute x25, starting transfers between devices, xor_permute(): return lax.ppermute(value, axis, [(i, i ^ mask) for i in range(size)])  31.1 us
    ppermute x25, waiting for transfers between devices, xor_permute(): return lax.ppermute(value, axis, [(i, i ^ mask) for i in range(size)])  24.9 us
    pallas_call x4, Pallas kernels, spmm(): pl.pallas_call(functools.partial(spmm_kernel, [len(p) for p in pieces], l...  23.4 us
    dot_general x10, matrix products, weight_term(): lax.dot_general(f, own, (((0,), (0,)), ((), ())), preferred_element_type=...  11.6 us
    pallas_call x1, Pallas kernels, flip_tiles(): pl.pallas_call(flip_kernel, out_shape=jax.ShapeDtypeStruct((slots + GROUP...  9.59 us
    unnamed x28, local copies, waits for them, and re-layouts  9.07 us
    all_to_all x1, blocking collectives, swap_cores(): return lax.all_to_all(both, 'row', 0, 0, axis_index_groups=pairs)  8.8 us
  transfers between devices with their start and end apart: 29, of which 10 were waited for; matrix products, arithmetic and copies ran while one was open for 15% of the time, Pallas kernels for 25%

profile of v10, /device:TPU:1, one launch (start us, length us, event | category | flops | bytes accessed | tf_op | source)
XLA Modules:
  0.0 138.8 jit_solution(11851687047871859204)
XLA Ops:
  0.7 1.7 %compare_select_fusion = (bf16[2048,128]{1,0:T(8,128)(2,1)S(1)}, bf16[2048,128]{1,0:T(8,128)(2,1)S(1)}) fusion(bf16[2048,256]{1,0:T(8,128)(2,1)} %param.8, bf16[2048,256]{1,0:T(8,128)(2,1)} %param.9), kind=kLoop, calls=%fused_computation.21 | loop fusion | flops 1048576 | bytes 3145728 | tf_op jit(solution)/shard_map/jit(_where)/select_n | solution.py:440
  2.3 2.1 %collective-permute-start.7 = (bf16[2048,256]{1,0:T(8,128)(2,1)}, bf16[2048,256]{1,0:T(8,128)(2,1)}, u32[]{:S(2)}, u32[]{:S(2)}) collective-permute-start(bf16[2048,256]{1,0:T(8,128)(2,1)} %param.10), channel_id=1, source_target_pairs={{0,16},{4,20},{8,24},{12,28},{16,0},{20,4},{24,8},{28,12},{1,17},{... | collective-permute-start | bytes 3145736 | tf_op jit(solution)/shard_map/ppermute | solution.py:309
  5.7 2.3 %collective-permute-start.1 = (bf16[2048,128]{1,0:T(8,128)(2,1)S(1)}, bf16[2048,128]{1,0:T(8,128)(2,1)S(1)}, u32[]{:S(2)}, u32[]{:S(2)}) collective-permute-start(bf16[2048,128]{1,0:T(8,128)(2,1)S(1)} %get-tuple-element.88.refs_0_), channel_id=1, source_target_pairs={{0,2},{1,3},{2,0},{3,1},{4,6},{5,7},{6,4},{7,5},{8,10},{9,11},{10,... | collective-permute-start | bytes 1572872 | tf_op jit(solution)/shard_map/ppermute | solution.py:309
  10.3 2.3 %plan_slots.1 = (s32[8,512]{1,0:T(8,128)S(1)}, s32[8,512]{1,0:T(8,128)S(1)}, s32[1,320]{1,0:T(1,128)S(1)}) custom-call(s32[4]{0:T(128)S(1)} %pad_add_fusion.place_ref, s32[1,320]{1,0:T(1,128)S(1)} %bitcast.45, s32[1,320]{1,0:T(1,128)S(1)} %bitcast.47, s32[320,1]{1,0:T(8,128)S(1)} %copy.10.rows_c, s32[320,1]{1,0:T(8,128)S(1)} %copy.11.cols_c), custom_call_target="tpu_custom_call" | custom-call | bytes 4096 | tf_op jit(solution)/shard_map/plan_slots/pallas_call | solution.py:120
  12.7 4.0 %copy-done.3 = bf16[1,1,320,128,128]{4,3,2,1,0:T(8,128)(2,1)S(1)} copy-done((bf16[1,1,320,128,128]{4,3,2,1,0:T(8,128)(2,1)S(1)}, bf16[1,1,320,128,128]{4,3,2,1,0:T(8,128)(2,1)}, u32[]{:S(2)}) %copy-start.3) | copy-done | bytes 10485784
  16.6 9.6 %flip_tiles.1.refs_3_.refs_2_ = bf16[352,128,128]{2,1,0:T(8,128)(2,1)S(1)} custom-call(s32[1,320]{1,0:T(1,128)S(1)} %get-tuple-element.84.slot_ref, bf16[320,128,128]{2,1,0:T(8,128)(2,1)S(1)} %bitcast.43), custom_call_target="tpu_custom_call" | custom-call | bytes 4096 | tf_op jit(solution)/shard_map/flip_tiles/pallas_call | solution.py:163
  26.3 4.4 %collective-permute-done.1.refs_2_ = bf16[2048,128]{1,0:T(8,128)(2,1)S(1)} collective-permute-done((bf16[2048,128]{1,0:T(8,128)(2,1)S(1)}, bf16[2048,128]{1,0:T(8,128)(2,1)S(1)}, u32[]{:S(2)}, u32[]{:S(2)}) %collective-permute-start.1) | collective-permute-done | bytes 524320 | tf_op jit(solution)/shard_map/ppermute | solution.py:309
  35.3 7.9 %spmm_first.2 = (bf16[8192,128]{1,0:T(8,128)(2,1)S(1)}, bf16[8192,128]{1,0:T(8,128)(2,1)S(1)}) custom-call(s32[8,512]{1,0:T(8,128)S(1)} %get-tuple-element.87.plan_ref, bf16[2048,128]{1,0:T(8,128)(2,1)S(1)} %get-tuple-element.88.refs_0_, bf16[2048,128]{1,0:T(8,128)(2,1)S(1)} %collective-permute-done.refs_1_, ...), custom_call_target="tpu_custom_call" | custom-call | bytes 4096 | tf_op jit(solution)/shard_map/spmm_first/pallas_call | solution.py:286
  43.2 3.2 %collective-permute-start.3 = (bf16[2048,128]{1,0:T(8,128)(2,1)S(1)}, bf16[2048,128]{1,0:T(8,128)(2,1)S(1)}, u32[]{:S(2)}, u32[]{:S(2)}) collective-permute-start(bf16[2048,128]{1,0:T(8,128)(2,1)S(1)} %get-tuple-element.103.refs_0_), channel_id=1, source_target_pairs={{0,2},{1,3},{2,0},{3,1},{4,6},{5,7},{6,4},{7,5},{8,10},{9,11},{10,... | collective-permute-start | bytes 1572872 | tf_op jit(solution)/shard_map/ppermute | solution.py:309
  46.5 3.7 %spmm_last.2 = bf16[2,8192,128]{2,1,0:T(8,128)(2,1)S(1)} custom-call(s32[8,512]{1,0:T(8,128)S(1)} %get-tuple-element.85.plan_ref, bf16[2048,128]{1,0:T(8,128)(2,1)S(1)} %collective-permute-done.4.refs_0_, bf16[2048,128]{1,0:T(8,128)(2,1)S(1)} %collective-permute-done.5.refs_1_, bf16[352,128,128]{2,1,0:T(8,128)(2,1)S(1)} %flip_tiles.1.refs_3_.refs_2_, ...), custom_call_target="tpu_custom_call" | custom-call | bytes 4096 | tf_op jit(solution)/shard_map/spmm_last/pallas_call | solution.py:286
  51.0 8.8 %all_to_all.5 = bf16[2,8192,128]{2,1,0:T(8,128)(2,1)S(1)} all-to-all(bf16[2,8192,128]{2,1,0:T(8,128)(2,1)S(1)} %spmm_last.2), channel_id=1, replica_groups={{0,4},{8,12},{16,20},{24,28},{1,5},{9,13},{17,21},{25,29},{2,6},{10,14}..., dimensions={0} | all-to-all | bytes 8388608 | tf_op jit(solution)/shard_map/all_to_all | solution.py:341
  62.6 6.7 %collective-permute-done.3.refs_2_ = bf16[2048,128]{1,0:T(8,128)(2,1)S(1)} collective-permute-done((bf16[2048,128]{1,0:T(8,128)(2,1)S(1)}, bf16[2048,128]{1,0:T(8,128)(2,1)S(1)}, u32[]{:S(2)}, u32[]{:S(2)}) %collective-permute-start.3) | collective-permute-done | bytes 524320 | tf_op jit(solution)/shard_map/ppermute | solution.py:309
  71.3 2.2 %collective-permute-start.12 = (bf16[2048,128]{1,0:T(8,128)(2,1)}, bf16[2048,128]{1,0:T(8,128)(2,1)}, u32[]{:S(2)}, u32[]{:S(2)}) collective-permute-start(bf16[2048,128]{1,0:T(8,128)(2,1)} %bitcast.11), channel_id=1, source_target_pairs={{0,8},{4,12},{8,0},{12,4},{16,24},{20,28},{24,16},{28,20},{1,9},{5... | collective-permute-start | bytes 1572872 | tf_op jit(solution)/shard_map/ppermute | solution.py:309
  73.9 4.3 %copy-done.2 = bf16[352,128,128]{2,1,0:T(8,128)(2,1)S(1)} copy-done((bf16[352,128,128]{2,1,0:T(8,128)(2,1)S(1)}, bf16[352,128,128]{2,1,0:T(8,128)(2,1)}, u32[]{:S(2)}) %copy-start.2) | copy-done | bytes 11534360
  78.1 7.9 %spmm_first.3 = (bf16[8192,128]{1,0:T(8,128)(2,1)S(1)}, bf16[8192,128]{1,0:T(8,128)(2,1)S(1)}) custom-call(s32[8,512]{1,0:T(8,128)S(1)} %get-tuple-element.87.plan_ref, bf16[2048,128]{1,0:T(8,128)(2,1)S(1)} %get-tuple-element.103.refs_0_, bf16[2048,128]{1,0:T(8,128)(2,1)S(1)} %collective-permute-done.2.refs_1_, ...), custom_call_target="tpu_custom_call" | custom-call | bytes 4096 | tf_op jit(solution)/shard_map/spmm_first/pallas_call | solution.py:286
  86.1 3.9 %spmm_last.3 = (bf16[8192,128]{1,0:T(8,128)(2,1)S(1)}, bf16[8192,128]{1,0:T(8,128)(2,1)S(1)}) custom-call(s32[8,512]{1,0:T(8,128)S(1)} %get-tuple-element.85.plan_ref, bf16[2048,128]{1,0:T(8,128)(2,1)S(1)} %collective-permute-done.10.refs_0_, bf16[2048,128]{1,0:T(8,128)(2,1)S(1)} %collective-permute-done.11.refs_1_, bf16[352,128,128]{2,1,0:T(8,128)(2,1)S(1)} %copy-done.2, ...), custom_call_target="tpu_custom_call" | custom-call | bytes 4096 | tf_op jit(solution)/shard_map/spmm_last/pallas_call | solution.py:286
  90.0 3.5 %collective-permute-start.14 = (bf16[8192,128]{1,0:T(8,128)(2,1)S(1)}, bf16[8192,128]{1,0:T(8,128)(2,1)S(1)}, u32[]{:S(2)}, u32[]{:S(2)}) collective-permute-start(bf16[8192,128]{1,0:T(8,128)(2,1)S(1)} %get-tuple-element.122), channel_id=1, source_target_pairs={{0,4},{4,0},{8,12},{12,8},{16,20},{20,16},{24,28},{28,24},{1,5},{5... | collective-permute-start | bytes 6291464 | tf_op jit(solution)/shard_map/ppermute | solution.py:309
  93.5 1.5 %add_convert_fusion.4 = (bf16[2048,128]{1,0:T(8,128)(2,1)S(1)}, bf16[2048,128]{1,0:T(8,128)(2,1)S(1)}) fusion(bf16[2048,128]{1,0:T(8,128)(2,1)} %collective-permute-done.13, bf16[2048,128]{1,0:T(8,128)(2,1)S(1)} %bitcast.57, bf16[2048,128]{1,0:T(8,128)(2,1)} %collective-permute-done.12, bf16[2048,128]{1,0:T(8,128)(2,1)S(1)} %bitcast.56), kind=kLoop, calls=%fused_computation.19 | loop fusion | flops 2097152 | bytes 3145728 | tf_op jit(solution)/shard_map/convert_element_type | solution.py:393
  96.5 1.7 %fusion.17 = f32[256,128]{1,0:T(8,128)S(1)} fusion(bf16[2048,256]{1,0:T(8,128)(2,1)} %collective-permute-done.7, bf16[8192,128]{1,0:T(8,128)(2,1)S(1)} %copy-done.7), kind=kOutput, calls=%fused_computation.34 | convolution fusion | flops 134217728 | bytes 1703936 | tf_op jit(solution)/shard_map/dot_general | solution.py:419
  98.2 1.7 %fusion.19 = f32[256,128]{1,0:T(8,128)S(1)} fusion(bf16[2048,256]{1,0:T(8,128)(2,1)} %collective-permute-done.6, bf16[8192,128]{1,0:T(8,128)(2,1)S(1)} %copy-done.7), kind=kOutput, calls=%fused_computation.36 | convolution fusion | flops 134217728 | bytes 1703936 | tf_op jit(solution)/shard_map/dot_general | solution.py:419
  99.9 1.7 %fusion.7 = bf16[256,128]{1,0:T(8,128)(2,1)S(1)} fusion(f32[256,128]{1,0:T(8,128)S(1)} %fusion.26, f32[256,128]{1,0:T(8,128)S(1)} %fusion.28, f32[256,128]{1,0:T(8,128)S(1)} %fusion.17, f32[256,128]{1,0:T(8,128)S(1)} %fusion.19, bf16[2048,256]{1,0:T(8,128)(2,1)} %param.10, bf16[8192,128]{1,0:T(8,128)(2,1)S(1)} %copy-done.7), kind=kOutput, calls=%fused_computation.12 | convolution fusion | flops 134381568 | bytes 2162688 | tf_op jit(solution)/shard_map/dot_general | solution.py:419
  102.2 1.7 %fusion.12 = f32[256,128]{1,0:T(8,128)S(1)} fusion(bf16[2048,256]{1,0:T(8,128)(2,1)} %collective-permute-done.7, bf16[8192,128]{1,0:T(8,128)(2,1)S(1)} %add_convert_fusion), kind=kOutput, calls=%fused_computation.23 | convolution fusion | flops 134217728 | bytes 1703936 | tf_op jit(solution)/shard_map/dot_general | solution.py:419
  103.9 1.7 %fusion.14 = f32[256,128]{1,0:T(8,128)S(1)} fusion(bf16[2048,256]{1,0:T(8,128)(2,1)} %collective-permute-done.6, bf16[8192,128]{1,0:T(8,128)(2,1)S(1)} %add_convert_fusion), kind=kOutput, calls=%fused_computation.25 | convolution fusion | flops 134217728 | bytes 1703936 | tf_op jit(solution)/shard_map/dot_general | solution.py:419
  106.3 1.7 %fusion.8 = bf16[256,128]{1,0:T(8,128)(2,1)S(1)} fusion(f32[256,128]{1,0:T(8,128)S(1)} %fusion.22, f32[256,128]{1,0:T(8,128)S(1)} %fusion.24, f32[256,128]{1,0:T(8,128)S(1)} %fusion.12, f32[256,128]{1,0:T(8,128)S(1)} %fusion.14, bf16[2048,256]{1,0:T(8,128)(2,1)} %param.10, bf16[8192,128]{1,0:T(8,128)(2,1)S(1)} %add_convert_fusion), kind=kOutput, calls=%fused_computation.13 | convolution fusion | flops 134381568 | bytes 2162688 | tf_op jit(solution)/shard_map/dot_general | solution.py:419
  109.7 1.7 %collective-permute-start.18 = (bf16[2048,128]{1,0:T(8,128)(2,1)S(1)}, bf16[2048,128]{1,0:T(8,128)(2,1)S(1)}, u32[]{:S(2)}, u32[]{:S(2)}) collective-permute-start(bf16[2048,128]{1,0:T(8,128)(2,1)S(1)} %bitcast.59), channel_id=1, source_target_pairs={{0,16},{4,20},{8,24},{12,28},{16,0},{20,4},{24,8},{28,12},{1,17},{... | collective-permute-start | bytes 1572872 | tf_op jit(solution)/shard_map/ppermute | solution.py:309
  112.3 2.5 %collective-permute-start.21 = (bf16[256,128]{1,0:T(8,128)(2,1)S(1)}, bf16[256,128]{1,0:T(8,128)(2,1)S(1)}, u32[]{:S(2)}, u32[]{:S(2)}) collective-permute-start(bf16[256,128]{1,0:T(8,128)(2,1)S(1)} %add_convert_fusion.12), channel_id=1, source_target_pairs={{0,2},{1,3},{2,0},{3,1},{4,6},{5,7},{6,4},{7,5},{8,10},{9,11},{10,... | collective-permute-start | bytes 196616 | tf_op jit(solution)/shard_map/ppermute | solution.py:309
  115.2 1.4 %collective-permute-done.22 = bf16[256,128]{1,0:T(8,128)(2,1)S(1)} collective-permute-done((bf16[256,128]{1,0:T(8,128)(2,1)S(1)}, bf16[256,128]{1,0:T(8,128)(2,1)S(1)}, u32[]{:S(2)}, u32[]{:S(2)}) %collective-permute-start.22) | collective-permute-done | bytes 65568 | tf_op jit(solution)/shard_map/ppermute | solution.py:309
  116.7 4.7 %collective-permute-done.21 = bf16[256,128]{1,0:T(8,128)(2,1)S(1)} collective-permute-done((bf16[256,128]{1,0:T(8,128)(2,1)S(1)}, bf16[256,128]{1,0:T(8,128)(2,1)S(1)}, u32[]{:S(2)}, u32[]{:S(2)}) %collective-permute-start.21) | collective-permute-done | bytes 65568 | tf_op jit(solution)/shard_map/ppermute | solution.py:309
  128.2 2.6 %collective-permute-done.23 = bf16[1024,128]{1,0:T(8,128)(2,1)S(1)} collective-permute-done((bf16[1024,128]{1,0:T(8,128)(2,1)S(1)}, bf16[1024,128]{1,0:T(8,128)(2,1)S(1)}, u32[]{:S(2)}, u32[]{:S(2)}) %collective-permute-start.23) | collective-permute-done | bytes 262176 | tf_op jit(solution)/shard_map/ppermute | solution.py:309
  132.7 1.4 %collective-permute-done.25 = bf16[256,128]{1,0:T(8,128)(2,1)S(1)} collective-permute-done((bf16[256,128]{1,0:T(8,128)(2,1)S(1)}, bf16[256,128]{1,0:T(8,128)(2,1)S(1)}, u32[]{:S(2)}, u32[]{:S(2)}) %collective-permute-start.25) | collective-permute-done | bytes 65568 | tf_op jit(solution)/shard_map/ppermute | solution.py:309
  134.2 2.4 %collective-permute-start.28 = (bf16[256,128]{1,0:T(8,128)(2,1)S(1)}, bf16[256,128]{1,0:T(8,128)(2,1)S(1)}, u32[]{:S(2)}, u32[]{:S(2)}) collective-permute-start(bf16[256,128]{1,0:T(8,128)(2,1)S(1)} %add_convert_fusion.10), channel_id=1, source_target_pairs={{0,4},{4,0},{8,12},{12,8},{16,20},{20,16},{24,28},{28,24},{1,5},{5... | collective-permute-start | bytes 196616 | tf_op jit(solution)/shard_map/ppermute | solution.py:309
  136.6 1.4 %convolution_convert_fusion = bf16[2048,256]{1,0:T(8,128)(2,1)} fusion(bf16[256,256]{1,0:T(8,128)(2,1)S(1)} %copy-done, bf16[2048,128]{1,0:T(8,128)(2,1)S(1)} %pad_maximum_fusion.1, bf16[2048,128]{1,0:T(8,128)(2,1)S(1)} %pad_maximum_fusion), kind=kOutput, calls=%fused_computation.2 | convolution fusion | flops 271056896 | bytes 2228224 | tf_op jit(solution)/shard_map/dot_general | solution.py:505
  (103 shorter events, 28.7 us)
Async XLA Ops:
  0.6 136.0 %copy-start = (bf16[256,256]{1,0:T(8,128)(2,1)S(1)}, bf16[256,256]{1,0:T(8,128)(2,1)}, u32[]{:S(2)}) copy-start(bf16[256,256]{1,0:T(8,128)(2,1)} %param.11) | copy-start | bytes 393220
  0.7 9.4 %copy-start.4 = (s32[1,1,320]{2,1,0:T(1,128)S(1)}, s32[1,1,320]{2,1,0:T(1,128)}, u32[]{:S(2)}) copy-start(s32[1,1,320]{2,1,0:T(1,128)} %param.13) | copy-start | bytes 3844
  2.3 30.3 %collective-permute-start.7 = (bf16[2048,256]{1,0:T(8,128)(2,1)}, bf16[2048,256]{1,0:T(8,128)(2,1)}, u32[]{:S(2)}, u32[]{:S(2)}) collective-permute-start(bf16[2048,256]{1,0:T(8,128)(2,1)} %param.10), channel_id=1, source_target_pairs={{0,16},{4,20},{8,24},{12,28},{16,0},{20,4},{24,8},{28,12},{1,17},{... | collective-permute-start | bytes 3145736 | tf_op jit(solution)/shard_map/ppermute | solution.py:309
  4.5 29.6 %collective-permute-start.6 = (bf16[2048,256]{1,0:T(8,128)(2,1)}, bf16[2048,256]{1,0:T(8,128)(2,1)}, u32[]{:S(2)}, u32[]{:S(2)}) collective-permute-start(bf16[2048,256]{1,0:T(8,128)(2,1)} %param.10), channel_id=1, source_target_pairs={{0,8},{4,12},{8,0},{12,4},{16,24},{20,28},{24,16},{28,20},{1,9},{5... | collective-permute-start | bytes 3145736 | tf_op jit(solution)/shard_map/ppermute | solution.py:309
  5.7 24.9 %collective-permute-start.1 = (bf16[2048,128]{1,0:T(8,128)(2,1)S(1)}, bf16[2048,128]{1,0:T(8,128)(2,1)S(1)}, u32[]{:S(2)}, u32[]{:S(2)}) collective-permute-start(bf16[2048,128]{1,0:T(8,128)(2,1)S(1)} %get-tuple-element.88.refs_0_), channel_id=1, source_target_pairs={{0,2},{1,3},{2,0},{3,1},{4,6},{5,7},{6,4},{7,5},{8,10},{9,11},{10,... | collective-permute-start | bytes 1572872 | tf_op jit(solution)/shard_map/ppermute | solution.py:309
  8.0 22.6 %collective-permute-start = (bf16[2048,128]{1,0:T(8,128)(2,1)S(1)}, bf16[2048,128]{1,0:T(8,128)(2,1)S(1)}, u32[]{:S(2)}, u32[]{:S(2)}) collective-permute-start(bf16[2048,128]{1,0:T(8,128)(2,1)S(1)} %get-tuple-element.88.refs_0_), channel_id=1, source_target_pairs={{0,1},{1,0},{2,3},{3,2},{4,5},{5,4},{6,7},{7,6},{8,9},{9,8},{10,11... | collective-permute-start | bytes 1572872 | tf_op jit(solution)/shard_map/ppermute | solution.py:309
  26.2 20.2 %copy-start.1 = (bf16[352,128,128]{2,1,0:T(8,128)(2,1)}, bf16[352,128,128]{2,1,0:T(8,128)(2,1)S(1)}, u32[]{:S(2)}) copy-start(bf16[352,128,128]{2,1,0:T(8,128)(2,1)S(1)} %flip_tiles.1.refs_3_.refs_2_) | copy-start | bytes 34603012
  30.6 15.8 %collective-permute-start.4 = (bf16[2048,128]{1,0:T(8,128)(2,1)S(1)}, bf16[2048,128]{1,0:T(8,128)(2,1)S(1)}, u32[]{:S(2)}, u32[]{:S(2)}) collective-permute-start(bf16[2048,128]{1,0:T(8,128)(2,1)S(1)} %get-tuple-element.88.refs_0_), channel_id=1, source_target_pairs={{1,2},{2,1},{5,6},{6,5},{9,10},{10,9},{13,14},{14,13},{17,18},{18,... | collective-permute-start | bytes 1572872 | tf_op jit(solution)/shard_map/ppermute | solution.py:327
  31.3 15.2 %collective-permute-start.5 = (bf16[2048,128]{1,0:T(8,128)(2,1)S(1)}, bf16[2048,128]{1,0:T(8,128)(2,1)S(1)}, u32[]{:S(2)}, u32[]{:S(2)}) collective-permute-start(bf16[2048,128]{1,0:T(8,128)(2,1)S(1)} %collective-permute-done.1.refs_2_), channel_id=1, source_target_pairs={{1,0},{2,3},{5,4},{6,7},{9,8},{10,11},{13,12},{14,15},{17,16},{18,... | collective-permute-start | bytes 1572872 | tf_op jit(solution)/shard_map/ppermute | solution.py:327
  33.7 16.5 %collective-permute-start.9 = (bf16[1024,256]{1,0:T(8,128)(2,1)S(1)}, bf16[1024,256]{1,0:T(8,128)(2,1)S(1)}, u32[]{:S(2)}, u32[]{:S(2)}) collective-permute-start(bf16[1024,256]{1,0:T(8,128)(2,1)S(1)} %slice.141), channel_id=1, source_target_pairs={{0,8},{4,12},{8,0},{12,4},{16,24},{20,28},{24,16},{28,20},{1,9},{5... | collective-permute-start | bytes 1572872 | tf_op jit(solution)/shard_map/ppermute | solution.py:309
  35.1 15.2 %collective-permute-start.8 = (bf16[1024,256]{1,0:T(8,128)(2,1)S(1)}, bf16[1024,256]{1,0:T(8,128)(2,1)S(1)}, u32[]{:S(2)}, u32[]{:S(2)}) collective-permute-start(bf16[1024,256]{1,0:T(8,128)(2,1)S(1)} %slice.140), channel_id=1, source_target_pairs={{0,16},{4,20},{8,24},{12,28},{16,0},{20,4},{24,8},{28,12},{1,17},{... | collective-permute-start | bytes 1572872 | tf_op jit(solution)/shard_map/ppermute | solution.py:309
  43.2 26.1 %collective-permute-start.3 = (bf16[2048,128]{1,0:T(8,128)(2,1)S(1)}, bf16[2048,128]{1,0:T(8,128)(2,1)S(1)}, u32[]{:S(2)}, u32[]{:S(2)}) collective-permute-start(bf16[2048,128]{1,0:T(8,128)(2,1)S(1)} %get-tuple-element.103.refs_0_), channel_id=1, source_target_pairs={{0,2},{1,3},{2,0},{3,1},{4,6},{5,7},{6,4},{7,5},{8,10},{9,11},{10,... | collective-permute-start | bytes 1572872 | tf_op jit(solution)/shard_map/ppermute | solution.py:309
  46.4 22.9 %collective-permute-start.2 = (bf16[2048,128]{1,0:T(8,128)(2,1)S(1)}, bf16[2048,128]{1,0:T(8,128)(2,1)S(1)}, u32[]{:S(2)}, u32[]{:S(2)}) collective-permute-start(bf16[2048,128]{1,0:T(8,128)(2,1)S(1)} %get-tuple-element.103.refs_0_), channel_id=1, source_target_pairs={{0,1},{1,0},{2,3},{3,2},{4,5},{5,4},{6,7},{7,6},{8,9},{9,8},{10,11... | collective-permute-start | bytes 1572872 | tf_op jit(solution)/shard_map/ppermute | solution.py:309
  69.3 16.8 %collective-permute-start.10 = (bf16[2048,128]{1,0:T(8,128)(2,1)S(1)}, bf16[2048,128]{1,0:T(8,128)(2,1)S(1)}, u32[]{:S(2)}, u32[]{:S(2)}) collective-permute-start(bf16[2048,128]{1,0:T(8,128)(2,1)S(1)} %get-tuple-element.103.refs_0_), channel_id=1, source_target_pairs={{1,2},{2,1},{5,6},{6,5},{9,10},{10,9},{13,14},{14,13},{17,18},{18,... | collective-permute-start | bytes 1572872 | tf_op jit(solution)/shard_map/ppermute | solution.py:327
  70.0 16.1 %collective-permute-start.11 = (bf16[2048,128]{1,0:T(8,128)(2,1)S(1)}, bf16[2048,128]{1,0:T(8,128)(2,1)S(1)}, u32[]{:S(2)}, u32[]{:S(2)}) collective-permute-start(bf16[2048,128]{1,0:T(8,128)(2,1)S(1)} %collective-permute-done.3.refs_2_), channel_id=1, source_target_pairs={{1,0},{2,3},{5,4},{6,7},{9,8},{10,11},{13,12},{14,15},{17,16},{18,... | collective-permute-start | bytes 1572872 | tf_op jit(solution)/shard_map/ppermute | solution.py:327
  71.3 18.7 %collective-permute-start.12 = (bf16[2048,128]{1,0:T(8,128)(2,1)}, bf16[2048,128]{1,0:T(8,128)(2,1)}, u32[]{:S(2)}, u32[]{:S(2)}) collective-permute-start(bf16[2048,128]{1,0:T(8,128)(2,1)} %bitcast.11), channel_id=1, source_target_pairs={{0,8},{4,12},{8,0},{12,4},{16,24},{20,28},{24,16},{28,20},{1,9},{5... | collective-permute-start | bytes 1572872 | tf_op jit(solution)/shard_map/ppermute | solution.py:309
  73.5 16.6 %collective-permute-start.13 = (bf16[2048,128]{1,0:T(8,128)(2,1)}, bf16[2048,128]{1,0:T(8,128)(2,1)}, u32[]{:S(2)}, u32[]{:S(2)}) collective-permute-start(bf16[2048,128]{1,0:T(8,128)(2,1)} %bitcast.13), channel_id=1, source_target_pairs={{0,16},{4,20},{8,24},{12,28},{16,0},{20,4},{24,8},{28,12},{1,17},{... | collective-permute-start | bytes 1572872 | tf_op jit(solution)/shard_map/ppermute | solution.py:309
  90.0 11.6 %collective-permute-start.14 = (bf16[8192,128]{1,0:T(8,128)(2,1)S(1)}, bf16[8192,128]{1,0:T(8,128)(2,1)S(1)}, u32[]{:S(2)}, u32[]{:S(2)}) collective-permute-start(bf16[8192,128]{1,0:T(8,128)(2,1)S(1)} %get-tuple-element.122), channel_id=1, source_target_pairs={{0,4},{4,0},{8,12},{12,8},{16,20},{20,16},{24,28},{28,24},{1,5},{5... | collective-permute-start | bytes 6291464 | tf_op jit(solution)/shard_map/ppermute | solution.py:309
  95.1 13.1 %collective-permute-start.16 = (bf16[1024,128]{1,0:T(8,128)(2,1)S(1)}, bf16[1024,128]{1,0:T(8,128)(2,1)S(1)}, u32[]{:S(2)}, u32[]{:S(2)}) collective-permute-start(bf16[1024,128]{1,0:T(8,128)(2,1)S(1)} %get-tuple-element.174), channel_id=1, source_target_pairs={{0,8},{4,12},{8,0},{12,4},{16,24},{20,28},{24,16},{28,20},{1,9},{5... | collective-permute-start | bytes 786440 | tf_op jit(solution)/shard_map/ppermute | solution.py:309
  95.7 12.5 %collective-permute-start.15 = (bf16[1024,128]{1,0:T(8,128)(2,1)S(1)}, bf16[1024,128]{1,0:T(8,128)(2,1)S(1)}, u32[]{:S(2)}, u32[]{:S(2)}) collective-permute-start(bf16[1024,128]{1,0:T(8,128)(2,1)S(1)} %get-tuple-element.176), channel_id=1, source_target_pairs={{0,16},{4,20},{8,24},{12,28},{16,0},{20,4},{24,8},{28,12},{1,17},{... | collective-permute-start | bytes 786440 | tf_op jit(solution)/shard_map/ppermute | solution.py:309
  108.2 3.4 %collective-permute-start.19 = (bf16[256,128]{1,0:T(8,128)(2,1)S(1)}, bf16[256,128]{1,0:T(8,128)(2,1)S(1)}, u32[]{:S(2)}, u32[]{:S(2)}) collective-permute-start(bf16[256,128]{1,0:T(8,128)(2,1)S(1)} %broadcast_select_fusion.2), channel_id=1, source_target_pairs={{0,4},{4,0},{8,12},{12,8},{16,20},{20,16},{24,28},{28,24},{1,5},{5... | collective-permute-start | bytes 196616 | tf_op jit(solution)/shard_map/ppermute | solution.py:309
  108.7 13.5 %collective-permute-start.17 = (bf16[2048,128]{1,0:T(8,128)(2,1)S(1)}, bf16[2048,128]{1,0:T(8,128)(2,1)S(1)}, u32[]{:S(2)}, u32[]{:S(2)}) collective-permute-start(bf16[2048,128]{1,0:T(8,128)(2,1)S(1)} %bitcast.58), channel_id=1, source_target_pairs={{0,8},{4,12},{8,0},{12,4},{16,24},{20,28},{24,16},{28,20},{1,9},{5... | collective-permute-start | bytes 1572872 | tf_op jit(solution)/shard_map/ppermute | solution.py:309
  109.7 13.7 %collective-permute-start.18 = (bf16[2048,128]{1,0:T(8,128)(2,1)S(1)}, bf16[2048,128]{1,0:T(8,128)(2,1)S(1)}, u32[]{:S(2)}, u32[]{:S(2)}) collective-permute-start(bf16[2048,128]{1,0:T(8,128)(2,1)S(1)} %bitcast.59), channel_id=1, source_target_pairs={{0,16},{4,20},{8,24},{12,28},{16,0},{20,4},{24,8},{28,12},{1,17},{... | collective-permute-start | bytes 1572872 | tf_op jit(solution)/shard_map/ppermute | solution.py:309
  111.6 5.1 %collective-permute-start.22 = (bf16[256,128]{1,0:T(8,128)(2,1)S(1)}, bf16[256,128]{1,0:T(8,128)(2,1)S(1)}, u32[]{:S(2)}, u32[]{:S(2)}) collective-permute-start(bf16[256,128]{1,0:T(8,128)(2,1)S(1)} %add_convert_fusion.12), channel_id=1, source_target_pairs={{0,3},{1,2},{2,1},{3,0},{4,7},{5,6},{6,5},{7,4},{8,11},{9,10},{10,... | collective-permute-start | bytes 196616 | tf_op jit(solution)/shard_map/ppermute | solution.py:309
  112.3 9.1 %collective-permute-start.21 = (bf16[256,128]{1,0:T(8,128)(2,1)S(1)}, bf16[256,128]{1,0:T(8,128)(2,1)S(1)}, u32[]{:S(2)}, u32[]{:S(2)}) collective-permute-start(bf16[256,128]{1,0:T(8,128)(2,1)S(1)} %add_convert_fusion.12), channel_id=1, source_target_pairs={{0,2},{1,3},{2,0},{3,1},{4,6},{5,7},{6,4},{7,5},{8,10},{9,11},{10,... | collective-permute-start | bytes 196616 | tf_op jit(solution)/shard_map/ppermute | solution.py:309
  114.8 6.6 %collective-permute-start.20 = (bf16[256,128]{1,0:T(8,128)(2,1)S(1)}, bf16[256,128]{1,0:T(8,128)(2,1)S(1)}, u32[]{:S(2)}, u32[]{:S(2)}) collective-permute-start(bf16[256,128]{1,0:T(8,128)(2,1)S(1)} %add_convert_fusion.12), channel_id=1, source_target_pairs={{0,1},{1,0},{2,3},{3,2},{4,5},{5,4},{6,7},{7,6},{8,9},{9,8},{10,11... | collective-permute-start | bytes 196616 | tf_op jit(solution)/shard_map/ppermute | solution.py:309
  123.7 7.0 %collective-permute-start.23 = (bf16[1024,128]{1,0:T(8,128)(2,1)S(1)}, bf16[1024,128]{1,0:T(8,128)(2,1)S(1)}, u32[]{:S(2)}, u32[]{:S(2)}) collective-permute-start(bf16[1024,128]{1,0:T(8,128)(2,1)S(1)} %get-tuple-element.154), channel_id=1, source_target_pairs={{0,16},{4,20},{8,24},{12,28},{16,0},{20,4},{24,8},{28,12},{1,17},{... | collective-permute-start | bytes 786440 | tf_op jit(solution)/shard_map/ppermute | solution.py:309
  125.0 6.3 %collective-permute-start.24 = (bf16[1024,128]{1,0:T(8,128)(2,1)S(1)}, bf16[1024,128]{1,0:T(8,128)(2,1)S(1)}, u32[]{:S(2)}, u32[]{:S(2)}) collective-permute-start(bf16[1024,128]{1,0:T(8,128)(2,1)S(1)} %get-tuple-element.156), channel_id=1, source_target_pairs={{0,8},{4,12},{8,0},{12,4},{16,24},{20,28},{24,16},{28,20},{1,9},{5... | collective-permute-start | bytes 786440 | tf_op jit(solution)/shard_map/ppermute | solution.py:309
  125.5 7.2 %collective-permute-start.27 = (bf16[256,128]{1,0:T(8,128)(2,1)S(1)}, bf16[256,128]{1,0:T(8,128)(2,1)S(1)}, u32[]{:S(2)}, u32[]{:S(2)}) collective-permute-start(bf16[256,128]{1,0:T(8,128)(2,1)S(1)} %add_convert_fusion.11), channel_id=1, source_target_pairs={{0,24},{4,28},{8,16},{12,20},{16,8},{20,12},{24,0},{28,4},{1,25},{... | collective-permute-start | bytes 196616 | tf_op jit(solution)/shard_map/ppermute | solution.py:309
  126.4 6.3 %collective-permute-start.26 = (bf16[256,128]{1,0:T(8,128)(2,1)S(1)}, bf16[256,128]{1,0:T(8,128)(2,1)S(1)}, u32[]{:S(2)}, u32[]{:S(2)}) collective-permute-start(bf16[256,128]{1,0:T(8,128)(2,1)S(1)} %add_convert_fusion.11), channel_id=1, source_target_pairs={{0,16},{4,20},{8,24},{12,28},{16,0},{20,4},{24,8},{28,12},{1,17},{... | collective-permute-start | bytes 196616 | tf_op jit(solution)/shard_map/ppermute | solution.py:309
  127.6 6.5 %collective-permute-start.25 = (bf16[256,128]{1,0:T(8,128)(2,1)S(1)}, bf16[256,128]{1,0:T(8,128)(2,1)S(1)}, u32[]{:S(2)}, u32[]{:S(2)}) collective-permute-start(bf16[256,128]{1,0:T(8,128)(2,1)S(1)} %add_convert_fusion.11), channel_id=1, source_target_pairs={{0,8},{4,12},{8,0},{12,4},{16,24},{20,28},{24,16},{28,20},{1,9},{5... | collective-permute-start | bytes 196616 | tf_op jit(solution)/shard_map/ppermute | solution.py:309
  134.2 3.9 %collective-permute-start.28 = (bf16[256,128]{1,0:T(8,128)(2,1)S(1)}, bf16[256,128]{1,0:T(8,128)(2,1)S(1)}, u32[]{:S(2)}, u32[]{:S(2)}) collective-permute-start(bf16[256,128]{1,0:T(8,128)(2,1)S(1)} %add_convert_fusion.10), channel_id=1, source_target_pairs={{0,4},{4,0},{8,12},{12,8},{16,20},{20,16},{24,28},{28,24},{1,5},{5... | collective-permute-start | bytes 196616 | tf_op jit(solution)/shard_map/ppermute | solution.py:309
  (11 other events, 56.9 us)

commit v11 on v10

--- a/solution.py
+++ b/solution.py
@@ -444,7 +444,7 @@
     place = jnp.stack([live_counts.reshape(()), row, col, mid.astype(jnp.int32)])
     plan0, plan1, slot = make_plans(tile_rows, tile_cols, place, n_row, nodes // SIDE)
     flipped = flip_tiles(slot, tiles.reshape(slots, SIDE, SIDE))
-    features, own1 = fence(features, own1)
+    features, plan0 = fence(features, plan0)
     near = [[features]]
     for bit in bits[:2]:
         near.append([xor_permute(features, "row", bit)])
@@ -454,15 +454,14 @@
     acc0 = spmm(plan0, [[own0], [first0[0]], [first0[1]]], flipped, None, n_row)
     own1, acc0 = fence(own1, acc0)
     first1 = gather_first(own1)
-    near.append([xor_permute(near[1][0][:rows], "row", bits[1]), xor_permute(near[2][0][rows:], "row", bits[0])])
-    for bit in bits[2:]:
-        near += [[xor_permute(f, "row", bit) for f in parts] for parts in near]
     pieces0 = as_pieces(own0, first0, second0, mid, n_col)
-    pieces0, acc0 = fence(pieces0, acc0)
+    pieces0, near, acc0 = fence(pieces0, near, acc0)
 
     (both0,) = spmm(plan1, pieces0[FIRST_PIECES:], flipped, acc0, n_row, by_core=True)
-    both0, near = fence(both0, near)
     got0 = swap_cores(both0)
+    for m in range(6, n_row, 2):
+        near.append([xor_permute(features, "row", m)])
+    got0, near = fence(got0, near)
     stage0, sums0 = stage_sums(got0[0], got0[1], n_row // 2, rows, at_once=True)
     own1, first1, stage0, sums0 = fence(own1, first1, stage0, sums0)
 

time: 141 us -> 145 us (1.028)
  blocking collectives: 8.8 us -> 0 us
  waiting for transfers between devices: 24.9 us -> 32.5 us
  starting transfers between devices: 35.1 us -> 42 us
  matrix products: 13 us -> 7.71 us
  other arithmetic: 5.8 us -> 9.76 us
    all_to_all x1 -> x0, blocking collectives: 8.8 us -> none  [swap_cores(): return lax.all_to_all(both, 'row', 0, 0, axis_index_groups=pairs)]
    ppermute x2, waiting for transfers between devices: 0.01 us -> 8.66 us  [gather_second(): lax.ppermute(by_two, 'col', ends)]
    all_to_all x0 -> x1, starting transfers between devices: none -> 6.75 us  [swap_cores(): return lax.all_to_all(both, 'row', 0, 0, axis_index_groups=pairs)]
    dot_general x10 -> x8, matrix products: 11.6 us -> 6.27 us  [weight_term(): lax.dot_general(f, own, (((0,), (0,)), ((), ())), preferred_element_type=...]
    ppermute x25 -> x24, waiting for transfers between devices: 24.9 us -> 20.6 us  [xor_permute(): return lax.ppermute(value, axis, [(i, i ^ mask) for i in range(size)])]
    unnamed x28 -> x34, local copies, waits for them, and re-layouts: 9.07 us -> 13.2 us
    convert_element_type x2, other arithmetic: 1.09 us -> 4.9 us  [stage_sums(): sums = add_f32(keep, recv).astype(jnp.bfloat16)]
    all_to_all x0 -> x1, waiting for transfers between devices: none -> 3.23 us  [swap_cores(): return lax.all_to_all(both, 'row', 0, 0, axis_index_groups=pairs)]
  transfers between devices with their start and end apart: 29 -> 29, of which waited for: 10 -> 14; matrix products, arithmetic and copies ran while one was open for 15% -> 11% of each run, Pallas kernels for 25% -> 24%
where the time goes in v11:
time: 145 us; the launch traced here: 143 us
  starting transfers between devices  42 us (29%)
  Pallas kernels  34.9 us (24%)
  waiting for transfers between devices  32.5 us (22%)
  local copies, waits for them, and re-layouts  14.8 us (10%)
  other arithmetic  9.76 us (7%)
  matrix products  7.71 us (5%)
  between operations  1.77 us (1%)
    ppermute x24, starting transfers between devices, xor_permute(): return lax.ppermute(value, axis, [(i, i ^ mask) for i in range(size)])  31.3 us
    pallas_call x4, Pallas kernels, spmm(): pl.pallas_call(functools.partial(spmm_kernel, [len(p) for p in pieces], l...  23 us
    ppermute x24, waiting for transfers between devices, xor_permute(): return lax.ppermute(value, axis, [(i, i ^ mask) for i in range(size)])  20.6 us
    unnamed x34, local copies, waits for them, and re-layouts  13.2 us
    pallas_call x1, Pallas kernels, flip_tiles(): pl.pallas_call(flip_kernel, out_shape=jax.ShapeDtypeStruct((slots + GROUP...  9.59 us
    ppermute x2, waiting for transfers between devices, gather_second(): lax.ppermute(by_two, 'col', ends)  8.66 us
    all_to_all x1, starting transfers between devices, swap_cores(): return lax.all_to_all(both, 'row', 0, 0, axis_index_groups=pairs)  6.75 us
    dot_general x8, matrix products, weight_term(): lax.dot_general(f, own, (((0,), (0,)), ((), ())), preferred_element_type=...  6.27 us
  transfers between devices with their start and end apart: 29, of which 14 were waited for; matrix products, arithmetic and copies ran while one was open for 11% of the time, Pallas kernels for 24%

profile of v11, /device:TPU:1, one launch (start us, length us, event | category | flops | bytes accessed | tf_op | source)
XLA Modules:
  0.0 143.4 jit_solution(4669714382002083786)
XLA Ops:
  0.7 1.7 %compare_select_fusion = (bf16[2048,128]{1,0:T(8,128)(2,1)S(1)}, bf16[2048,128]{1,0:T(8,128)(2,1)S(1)}) fusion(bf16[2048,256]{1,0:T(8,128)(2,1)} %param.8, bf16[2048,256]{1,0:T(8,128)(2,1)} %param.9), kind=kLoop, calls=%fused_computation.19 | loop fusion | flops 1048576 | bytes 3145728 | tf_op jit(solution)/shard_map/jit(_where)/select_n | solution.py:440
  2.3 3.2 %collective-permute-start.1 = (bf16[2048,128]{1,0:T(8,128)(2,1)S(1)}, bf16[2048,128]{1,0:T(8,128)(2,1)S(1)}, u32[]{:S(2)}, u32[]{:S(2)}) collective-permute-start(bf16[2048,128]{1,0:T(8,128)(2,1)S(1)} %get-tuple-element.90.refs_0_), channel_id=1, source_target_pairs={{0,2},{1,3},{2,0},{3,1},{4,6},{5,7},{6,4},{7,5},{8,10},{9,11},{10,... | collective-permute-start | bytes 1572872 | tf_op jit(solution)/shard_map/ppermute | solution.py:309
  7.9 2.3 %plan_slots.1 = (s32[8,512]{1,0:T(8,128)S(1)}, s32[8,512]{1,0:T(8,128)S(1)}, s32[1,320]{1,0:T(1,128)S(1)}) custom-call(s32[4]{0:T(128)S(1)} %pad_add_fusion.place_ref, s32[1,320]{1,0:T(1,128)S(1)} %bitcast.43, s32[1,320]{1,0:T(1,128)S(1)} %bitcast.45, s32[320,1]{1,0:T(8,128)S(1)} %copy.10.rows_c, s32[320,1]{1,0:T(8,128)S(1)} %copy.11.cols_c), custom_call_target="tpu_custom_call" | custom-call | bytes 4096 | tf_op jit(solution)/shard_map/plan_slots/pallas_call | solution.py:120
  12.9 4.0 %copy-done.4 = bf16[1,1,320,128,128]{4,3,2,1,0:T(8,128)(2,1)S(1)} copy-done((bf16[1,1,320,128,128]{4,3,2,1,0:T(8,128)(2,1)S(1)}, bf16[1,1,320,128,128]{4,3,2,1,0:T(8,128)(2,1)}, u32[]{:S(2)}) %copy-start.4) | copy-done | bytes 10485784
  16.9 9.6 %flip_tiles.1.refs_3_.refs_2_ = bf16[352,128,128]{2,1,0:T(8,128)(2,1)S(1)} custom-call(s32[1,320]{1,0:T(1,128)S(1)} %get-tuple-element.86.slot_ref, bf16[320,128,128]{2,1,0:T(8,128)(2,1)S(1)} %bitcast.41), custom_call_target="tpu_custom_call" | custom-call | bytes 4096 | tf_op jit(solution)/shard_map/flip_tiles/pallas_call | solution.py:163
  26.5 2.0 %collective-permute-done.1.refs_2_ = bf16[2048,128]{1,0:T(8,128)(2,1)S(1)} collective-permute-done((bf16[2048,128]{1,0:T(8,128)(2,1)S(1)}, bf16[2048,128]{1,0:T(8,128)(2,1)S(1)}, u32[]{:S(2)}, u32[]{:S(2)}) %collective-permute-start.1) | collective-permute-done | bytes 524320 | tf_op jit(solution)/shard_map/ppermute | solution.py:309
  30.5 7.3 %spmm_first.2 = (bf16[8192,128]{1,0:T(8,128)(2,1)S(1)}, bf16[8192,128]{1,0:T(8,128)(2,1)S(1)}) custom-call(s32[8,512]{1,0:T(8,128)S(1)} %get-tuple-element.89.plan_ref, bf16[2048,128]{1,0:T(8,128)(2,1)S(1)} %get-tuple-element.90.refs_0_, bf16[2048,128]{1,0:T(8,128)(2,1)S(1)} %collective-permute-done.refs_1_, ...), custom_call_target="tpu_custom_call" | custom-call | bytes 4096 | tf_op jit(solution)/shard_map/spmm_first/pallas_call | solution.py:286
  37.8 5.5 %collective-permute-start.3 = (bf16[2048,128]{1,0:T(8,128)(2,1)S(1)}, bf16[2048,128]{1,0:T(8,128)(2,1)S(1)}, u32[]{:S(2)}, u32[]{:S(2)}) collective-permute-start(bf16[2048,128]{1,0:T(8,128)(2,1)S(1)} %get-tuple-element.108.refs_0_), channel_id=1, source_target_pairs={{0,2},{1,3},{2,0},{3,1},{4,6},{5,7},{6,4},{7,5},{8,10},{9,11},{10,... | collective-permute-start | bytes 1572872 | tf_op jit(solution)/shard_map/ppermute | solution.py:309
  44.3 3.4 %spmm_last.2 = bf16[2,8192,128]{2,1,0:T(8,128)(2,1)S(1)} custom-call(s32[8,512]{1,0:T(8,128)S(1)} %get-tuple-element.87.plan_ref, bf16[2048,128]{1,0:T(8,128)(2,1)S(1)} %collective-permute-done.4.refs_0_, bf16[2048,128]{1,0:T(8,128)(2,1)S(1)} %collective-permute-done.5.refs_1_, bf16[352,128,128]{2,1,0:T(8,128)(2,1)S(1)} %flip_tiles.1.refs_3_.refs_2_, ...), custom_call_target="tpu_custom_call" | custom-call | bytes 4096 | tf_op jit(solution)/shard_map/spmm_last/pallas_call | solution.py:286
  47.8 1.9 %copy-done.3 = bf16[2,8192,128]{2,1,0:T(8,128)(2,1)} copy-done((bf16[2,8192,128]{2,1,0:T(8,128)(2,1)}, bf16[2,8192,128]{2,1,0:T(8,128)(2,1)S(1)}, u32[]{:S(2)}) %copy-start.3) | copy-done | bytes 4194328
  49.7 6.8 %all-to-all-start = ((bf16[2,8192,128]{2,1,0:T(8,128)(2,1)}), bf16[2,8192,128]{2,1,0:T(8,128)(2,1)}, u32[]{:S(2)}, u32[]{:S(2)}) async-start(bf16[2,8192,128]{2,1,0:T(8,128)(2,1)} %copy-done.3), calls=%async_computation | async-start | bytes 8388608 | tf_op jit(solution)/shard_map/all_to_all | solution.py:341
  57.4 3.2 %all-to-all-done = bf16[2,8192,128]{2,1,0:T(8,128)(2,1)} async-done(((bf16[2,8192,128]{2,1,0:T(8,128)(2,1)}), bf16[2,8192,128]{2,1,0:T(8,128)(2,1)}, u32[]{:S(2)}, u32[]{:S(2)}) %all-to-all-start) | async-done | bytes 4194336 | tf_op jit(solution)/shard_map/all_to_all | solution.py:341
  60.6 2.8 %fusion = bf16[8192,128]{1,0:T(8,128)(2,1)S(1)} fusion(bf16[2,8192,128]{2,1,0:T(8,128)(2,1)} %all-to-all-done), kind=kLoop, calls=%fused_computation.3 | loop fusion | flops 4194304 | bytes 6291456 | tf_op jit(solution)/shard_map/convert_element_type | solution.py:356
  66.1 1.5 %collective-permute-done.2.refs_1_ = bf16[2048,128]{1,0:T(8,128)(2,1)S(1)} collective-permute-done((bf16[2048,128]{1,0:T(8,128)(2,1)S(1)}, bf16[2048,128]{1,0:T(8,128)(2,1)S(1)}, u32[]{:S(2)}, u32[]{:S(2)}) %collective-permute-start.2) | collective-permute-done | bytes 524320 | tf_op jit(solution)/shard_map/ppermute | solution.py:309
  70.1 2.0 %collective-permute-start.12 = (bf16[2048,128]{1,0:T(8,128)(2,1)S(1)}, bf16[2048,128]{1,0:T(8,128)(2,1)S(1)}, u32[]{:S(2)}, u32[]{:S(2)}) collective-permute-start(bf16[2048,128]{1,0:T(8,128)(2,1)S(1)} %bitcast.58), channel_id=1, source_target_pairs={{0,16},{4,20},{8,24},{12,28},{16,0},{20,4},{24,8},{28,12},{1,17},{... | collective-permute-start | bytes 1572872 | tf_op jit(solution)/shard_map/ppermute | solution.py:309
  72.2 4.3 %copy-done.2 = bf16[352,128,128]{2,1,0:T(8,128)(2,1)S(1)} copy-done((bf16[352,128,128]{2,1,0:T(8,128)(2,1)S(1)}, bf16[352,128,128]{2,1,0:T(8,128)(2,1)}, u32[]{:S(2)}) %copy-start.2) | copy-done | bytes 11534360
  76.5 7.3 %spmm_first.3 = (bf16[8192,128]{1,0:T(8,128)(2,1)S(1)}, bf16[8192,128]{1,0:T(8,128)(2,1)S(1)}) custom-call(s32[8,512]{1,0:T(8,128)S(1)} %get-tuple-element.89.plan_ref, bf16[2048,128]{1,0:T(8,128)(2,1)S(1)} %get-tuple-element.108.refs_0_, bf16[2048,128]{1,0:T(8,128)(2,1)S(1)} %collective-permute-done.2.refs_1_, ...), custom_call_target="tpu_custom_call" | custom-call | bytes 4096 | tf_op jit(solution)/shard_map/spmm_first/pallas_call | solution.py:286
  83.8 8.4 %collective-permute-done.10.refs_1_ = bf16[2048,128]{1,0:T(8,128)(2,1)S(1)} collective-permute-done((bf16[2048,128]{1,0:T(8,128)(2,1)S(1)}, bf16[2048,128]{1,0:T(8,128)(2,1)S(1)}, u32[]{:S(2)}, u32[]{:S(2)}) %collective-permute-start.10) | collective-permute-done | bytes 524320 | tf_op jit(solution)/shard_map/ppermute | solution.py:327
  92.2 5.0 %spmm_last.3 = (bf16[8192,128]{1,0:T(8,128)(2,1)}, bf16[8192,128]{1,0:T(8,128)(2,1)S(1)}) custom-call(s32[8,512]{1,0:T(8,128)S(1)} %get-tuple-element.87.plan_ref, bf16[2048,128]{1,0:T(8,128)(2,1)S(1)} %collective-permute-done.9.refs_0_, bf16[2048,128]{1,0:T(8,128)(2,1)S(1)} %collective-permute-done.10.refs_1_, bf16[352,128,128]{2,1,0:T(8,128)(2,1)S(1)} %copy-done.2, ...), custom_call_target="tpu_custom_call" | custom-call | bytes 4096 | tf_op jit(solution)/shard_map/spmm_last/pallas_call | solution.py:286
  99.5 1.6 %add_convert_fusion.4 = (bf16[2048,128]{1,0:T(8,128)(2,1)S(1)}, bf16[2048,128]{1,0:T(8,128)(2,1)S(1)}) fusion(bf16[2048,128]{1,0:T(8,128)(2,1)} %copy-done.12, bf16[2048,128]{1,0:T(8,128)(2,1)S(1)} %bitcast.55, bf16[2048,128]{1,0:T(8,128)(2,1)} %copy-done.11, bf16[2048,128]{1,0:T(8,128)(2,1)S(1)} %bitcast.54), kind=kLoop, calls=%fused_computation.17 | loop fusion | flops 2097152 | bytes 3145728 | tf_op jit(solution)/shard_map/convert_element_type | solution.py:393
  102.6 3.0 %collective-permute-start.14 = (bf16[1024,128]{1,0:T(8,128)(2,1)S(1)}, bf16[1024,128]{1,0:T(8,128)(2,1)S(1)}, u32[]{:S(2)}, u32[]{:S(2)}) collective-permute-start(bf16[1024,128]{1,0:T(8,128)(2,1)S(1)} %get-tuple-element.180), channel_id=1, source_target_pairs={{0,16},{4,20},{8,24},{12,28},{16,0},{20,4},{24,8},{28,12},{1,17},{... | collective-permute-start | bytes 786440 | tf_op jit(solution)/shard_map/ppermute | solution.py:309
  105.6 1.7 %fusion.17 = f32[256,128]{1,0:T(8,128)S(1)} fusion(bf16[2048,256]{1,0:T(8,128)(2,1)} %collective-permute-done.8, bf16[8192,128]{1,0:T(8,128)(2,1)S(1)} %copy-done.8), kind=kOutput, calls=%fused_computation.34 | convolution fusion | flops 134217728 | bytes 1703936 | tf_op jit(solution)/shard_map/dot_general | solution.py:419
  109.0 2.1 %add_convert_fusion = bf16[8192,128]{1,0:T(8,128)(2,1)S(1)} fusion(bf16[8192,128]{1,0:T(8,128)(2,1)} %collective-permute-done.13, bf16[8192,128]{1,0:T(8,128)(2,1)S(1)} %get-tuple-element.126), kind=kLoop, calls=%fused_computation | loop fusion | flops 4194304 | bytes 6291456 | tf_op jit(solution)/shard_map/convert_element_type | solution.py:356
  111.2 1.7 %fusion.10 = f32[256,128]{1,0:T(8,128)S(1)} fusion(bf16[2048,256]{1,0:T(8,128)(2,1)} %collective-permute-done.8, bf16[8192,128]{1,0:T(8,128)(2,1)S(1)} %add_convert_fusion), kind=kOutput, calls=%fused_computation.21 | convolution fusion | flops 134217728 | bytes 1703936 | tf_op jit(solution)/shard_map/dot_general | solution.py:419
  116.1 2.3 %collective-permute-start.21 = (bf16[256,128]{1,0:T(8,128)(2,1)S(1)}, bf16[256,128]{1,0:T(8,128)(2,1)S(1)}, u32[]{:S(2)}, u32[]{:S(2)}) collective-permute-start(bf16[256,128]{1,0:T(8,128)(2,1)S(1)} %add_convert_fusion.12), channel_id=1, source_target_pairs={{0,3},{1,2},{2,1},{3,0},{4,7},{5,6},{6,5},{7,4},{8,11},{9,10},{10,... | collective-permute-start | bytes 196616 | tf_op jit(solution)/shard_map/ppermute | solution.py:309
  119.8 1.4 collective-permute-done.21
  121.2 4.9 %collective-permute-done.20 = bf16[256,128]{1,0:T(8,128)(2,1)S(1)} collective-permute-done((bf16[256,128]{1,0:T(8,128)(2,1)S(1)}, bf16[256,128]{1,0:T(8,128)(2,1)S(1)}, u32[]{:S(2)}, u32[]{:S(2)}) %collective-permute-start.20) | collective-permute-done | bytes 65568 | tf_op jit(solution)/shard_map/ppermute | solution.py:309
  126.2 2.5 %collective-permute-done.16 = bf16[2048,128]{1,0:T(8,128)(2,1)S(1)} collective-permute-done((bf16[2048,128]{1,0:T(8,128)(2,1)S(1)}, bf16[2048,128]{1,0:T(8,128)(2,1)S(1)}, u32[]{:S(2)}, u32[]{:S(2)}) %collective-permute-start.16) | collective-permute-done | bytes 524320 | tf_op jit(solution)/shard_map/ppermute | solution.py:309
  133.0 3.0 %collective-permute-done.22 = bf16[1024,128]{1,0:T(8,128)(2,1)S(1)} collective-permute-done((bf16[1024,128]{1,0:T(8,128)(2,1)S(1)}, bf16[1024,128]{1,0:T(8,128)(2,1)S(1)}, u32[]{:S(2)}, u32[]{:S(2)}) %collective-permute-start.22) | collective-permute-done | bytes 262176 | tf_op jit(solution)/shard_map/ppermute | solution.py:309
  136.2 1.8 %collective-permute-done.26 = bf16[256,128]{1,0:T(8,128)(2,1)S(1)} collective-permute-done((bf16[256,128]{1,0:T(8,128)(2,1)S(1)}, bf16[256,128]{1,0:T(8,128)(2,1)S(1)}, u32[]{:S(2)}, u32[]{:S(2)}) %collective-permute-start.26) | collective-permute-done | bytes 65568 | tf_op jit(solution)/shard_map/ppermute | solution.py:309
  138.7 2.6 %collective-permute-start.27 = (bf16[256,128]{1,0:T(8,128)(2,1)S(1)}, bf16[256,128]{1,0:T(8,128)(2,1)S(1)}, u32[]{:S(2)}, u32[]{:S(2)}) collective-permute-start(bf16[256,128]{1,0:T(8,128)(2,1)S(1)} %add_convert_fusion.10), channel_id=1, source_target_pairs={{0,4},{4,0},{8,12},{12,8},{16,20},{20,16},{24,28},{28,24},{1,5},{5... | collective-permute-start | bytes 196616 | tf_op jit(solution)/shard_map/ppermute | solution.py:309
  141.2 1.4 convolution_convert_fusion
  (104 shorter events, 29.4 us)
Async XLA Ops:
  0.6 140.6 %copy-start = (bf16[256,256]{1,0:T(8,128)(2,1)S(1)}, bf16[256,256]{1,0:T(8,128)(2,1)}, u32[]{:S(2)}) copy-start(bf16[256,256]{1,0:T(8,128)(2,1)} %param.11) | copy-start | bytes 393220
  2.3 26.1 %collective-permute-start.1 = (bf16[2048,128]{1,0:T(8,128)(2,1)S(1)}, bf16[2048,128]{1,0:T(8,128)(2,1)S(1)}, u32[]{:S(2)}, u32[]{:S(2)}) collective-permute-start(bf16[2048,128]{1,0:T(8,128)(2,1)S(1)} %get-tuple-element.90.refs_0_), channel_id=1, source_target_pairs={{0,2},{1,3},{2,0},{3,1},{4,6},{5,7},{6,4},{7,5},{8,10},{9,11},{10,... | collective-permute-start | bytes 1572872 | tf_op jit(solution)/shard_map/ppermute | solution.py:309
  5.5 22.9 %collective-permute-start = (bf16[2048,128]{1,0:T(8,128)(2,1)S(1)}, bf16[2048,128]{1,0:T(8,128)(2,1)S(1)}, u32[]{:S(2)}, u32[]{:S(2)}) collective-permute-start(bf16[2048,128]{1,0:T(8,128)(2,1)S(1)} %get-tuple-element.90.refs_0_), channel_id=1, source_target_pairs={{0,1},{1,0},{2,3},{3,2},{4,5},{5,4},{6,7},{7,6},{8,9},{9,8},{10,11... | collective-permute-start | bytes 1572872 | tf_op jit(solution)/shard_map/ppermute | solution.py:309
  10.2 27.6 %collective-permute-start.7 = (bf16[2048,256]{1,0:T(8,128)(2,1)}, bf16[2048,256]{1,0:T(8,128)(2,1)S(1)}, u32[]{:S(2)}, u32[]{:S(2)}) collective-permute-start(bf16[2048,256]{1,0:T(8,128)(2,1)} %param.10), channel_id=1, source_target_pairs={{0,16},{4,20},{8,24},{12,28},{16,0},{20,4},{24,8},{28,12},{1,17},{... | collective-permute-start | bytes 3145736 | tf_op jit(solution)/shard_map/ppermute | solution.py:309
  11.5 31.8 %collective-permute-start.6 = (bf16[2048,256]{1,0:T(8,128)(2,1)}, bf16[2048,256]{1,0:T(8,128)(2,1)S(1)}, u32[]{:S(2)}, u32[]{:S(2)}) collective-permute-start(bf16[2048,256]{1,0:T(8,128)(2,1)} %param.10), channel_id=1, source_target_pairs={{0,8},{4,12},{8,0},{12,4},{16,24},{20,28},{24,16},{28,20},{1,9},{5... | collective-permute-start | bytes 3145736 | tf_op jit(solution)/shard_map/ppermute | solution.py:309
  12.7 44.7 %collective-permute-start.8 = (bf16[2048,256]{1,0:T(8,128)(2,1)}, bf16[2048,256]{1,0:T(8,128)(2,1)}, u32[]{:S(2)}, u32[]{:S(2)}) collective-permute-start(bf16[2048,256]{1,0:T(8,128)(2,1)} %param.10), channel_id=1, source_target_pairs={{0,24},{4,28},{8,16},{12,20},{16,8},{20,12},{24,0},{28,4},{1,25},{... | collective-permute-start | bytes 3145736 | tf_op jit(solution)/shard_map/ppermute | solution.py:309
  26.5 17.1 %copy-start.1 = (bf16[352,128,128]{2,1,0:T(8,128)(2,1)}, bf16[352,128,128]{2,1,0:T(8,128)(2,1)S(1)}, u32[]{:S(2)}) copy-start(bf16[352,128,128]{2,1,0:T(8,128)(2,1)S(1)} %flip_tiles.1.refs_3_.refs_2_) | copy-start | bytes 34603012
  28.5 14.9 %collective-permute-start.4 = (bf16[2048,128]{1,0:T(8,128)(2,1)S(1)}, bf16[2048,128]{1,0:T(8,128)(2,1)S(1)}, u32[]{:S(2)}, u32[]{:S(2)}) collective-permute-start(bf16[2048,128]{1,0:T(8,128)(2,1)S(1)} %get-tuple-element.90.refs_0_), channel_id=1, source_target_pairs={{1,2},{2,1},{5,6},{6,5},{9,10},{10,9},{13,14},{14,13},{17,18},{18,... | collective-permute-start | bytes 1572872 | tf_op jit(solution)/shard_map/ppermute | solution.py:327
  29.2 14.4 %collective-permute-start.5 = (bf16[2048,128]{1,0:T(8,128)(2,1)S(1)}, bf16[2048,128]{1,0:T(8,128)(2,1)S(1)}, u32[]{:S(2)}, u32[]{:S(2)}) collective-permute-start(bf16[2048,128]{1,0:T(8,128)(2,1)S(1)} %collective-permute-done.1.refs_2_), channel_id=1, source_target_pairs={{1,0},{2,3},{5,4},{6,7},{9,8},{10,11},{13,12},{14,15},{17,16},{18,... | collective-permute-start | bytes 1572872 | tf_op jit(solution)/shard_map/ppermute | solution.py:327
  37.8 28.3 %collective-permute-start.3 = (bf16[2048,128]{1,0:T(8,128)(2,1)S(1)}, bf16[2048,128]{1,0:T(8,128)(2,1)S(1)}, u32[]{:S(2)}, u32[]{:S(2)}) collective-permute-start(bf16[2048,128]{1,0:T(8,128)(2,1)S(1)} %get-tuple-element.108.refs_0_), channel_id=1, source_target_pairs={{0,2},{1,3},{2,0},{3,1},{4,6},{5,7},{6,4},{7,5},{8,10},{9,11},{10,... | collective-permute-start | bytes 1572872 | tf_op jit(solution)/shard_map/ppermute | solution.py:309
  43.3 24.3 %collective-permute-start.2 = (bf16[2048,128]{1,0:T(8,128)(2,1)S(1)}, bf16[2048,128]{1,0:T(8,128)(2,1)S(1)}, u32[]{:S(2)}, u32[]{:S(2)}) collective-permute-start(bf16[2048,128]{1,0:T(8,128)(2,1)S(1)} %get-tuple-element.108.refs_0_), channel_id=1, source_target_pairs={{0,1},{1,0},{2,3},{3,2},{4,5},{5,4},{6,7},{7,6},{8,9},{9,8},{10,11... | collective-permute-start | bytes 1572872 | tf_op jit(solution)/shard_map/ppermute | solution.py:309
  49.7 10.9 %all-to-all-start = ((bf16[2,8192,128]{2,1,0:T(8,128)(2,1)}), bf16[2,8192,128]{2,1,0:T(8,128)(2,1)}, u32[]{:S(2)}, u32[]{:S(2)}) async-start(bf16[2,8192,128]{2,1,0:T(8,128)(2,1)} %copy-done.3), calls=%async_computation | async-start | bytes 8388608 | tf_op jit(solution)/shard_map/all_to_all | solution.py:341
  67.7 16.1 %collective-permute-start.9 = (bf16[2048,128]{1,0:T(8,128)(2,1)S(1)}, bf16[2048,128]{1,0:T(8,128)(2,1)S(1)}, u32[]{:S(2)}, u32[]{:S(2)}) collective-permute-start(bf16[2048,128]{1,0:T(8,128)(2,1)S(1)} %get-tuple-element.108.refs_0_), channel_id=1, source_target_pairs={{1,2},{2,1},{5,6},{6,5},{9,10},{10,9},{13,14},{14,13},{17,18},{18,... | collective-permute-start | bytes 1572872 | tf_op jit(solution)/shard_map/ppermute | solution.py:327
  68.4 23.8 %collective-permute-start.10 = (bf16[2048,128]{1,0:T(8,128)(2,1)S(1)}, bf16[2048,128]{1,0:T(8,128)(2,1)S(1)}, u32[]{:S(2)}, u32[]{:S(2)}) collective-permute-start(bf16[2048,128]{1,0:T(8,128)(2,1)S(1)} %collective-permute-done.3.refs_2_), channel_id=1, source_target_pairs={{1,0},{2,3},{5,4},{6,7},{9,8},{10,11},{13,12},{14,15},{17,16},{18,... | collective-permute-start | bytes 1572872 | tf_op jit(solution)/shard_map/ppermute | solution.py:327
  69.7 27.5 %collective-permute-start.11 = (bf16[2048,128]{1,0:T(8,128)(2,1)S(1)}, bf16[2048,128]{1,0:T(8,128)(2,1)S(1)}, u32[]{:S(2)}, u32[]{:S(2)}) collective-permute-start(bf16[2048,128]{1,0:T(8,128)(2,1)S(1)} %bitcast.59), channel_id=1, source_target_pairs={{0,8},{4,12},{8,0},{12,4},{16,24},{20,28},{24,16},{28,20},{1,9},{5... | collective-permute-start | bytes 1572872 | tf_op jit(solution)/shard_map/ppermute | solution.py:309
  70.1 27.0 %collective-permute-start.12 = (bf16[2048,128]{1,0:T(8,128)(2,1)S(1)}, bf16[2048,128]{1,0:T(8,128)(2,1)S(1)}, u32[]{:S(2)}, u32[]{:S(2)}) collective-permute-start(bf16[2048,128]{1,0:T(8,128)(2,1)S(1)} %bitcast.58), channel_id=1, source_target_pairs={{0,16},{4,20},{8,24},{12,28},{16,0},{20,4},{24,8},{28,12},{1,17},{... | collective-permute-start | bytes 1572872 | tf_op jit(solution)/shard_map/ppermute | solution.py:309
  92.2 7.3 %copy-start.10 = (bf16[1,2,1,1024,128]{4,3,2,1,0:T(8,128)(2,1)S(1)}, bf16[1,2,1,1024,128]{4,3,2,1,0:T(8,128)(2,1)}, u32[]{:S(2)}) copy-start(bf16[1,2,1,1024,128]{4,3,2,1,0:T(8,128)(2,1)} %get-tuple-element.168) | copy-start | bytes 1572868
  98.8 10.3 %collective-permute-start.13 = (bf16[8192,128]{1,0:T(8,128)(2,1)}, bf16[8192,128]{1,0:T(8,128)(2,1)}, u32[]{:S(2)}, u32[]{:S(2)}) collective-permute-start(bf16[8192,128]{1,0:T(8,128)(2,1)} %get-tuple-element.127), channel_id=1, source_target_pairs={{0,4},{4,0},{8,12},{12,8},{16,20},{20,16},{24,28},{28,24},{1,5},{5... | collective-permute-start | bytes 6291464 | tf_op jit(solution)/shard_map/ppermute | solution.py:309
  101.2 13.3 %collective-permute-start.15 = (bf16[1024,128]{1,0:T(8,128)(2,1)S(1)}, bf16[1024,128]{1,0:T(8,128)(2,1)S(1)}, u32[]{:S(2)}, u32[]{:S(2)}) collective-permute-start(bf16[1024,128]{1,0:T(8,128)(2,1)S(1)} %get-tuple-element.178), channel_id=1, source_target_pairs={{0,8},{4,12},{8,0},{12,4},{16,24},{20,28},{24,16},{28,20},{1,9},{5... | collective-permute-start | bytes 786440 | tf_op jit(solution)/shard_map/ppermute | solution.py:309
  102.6 11.9 %collective-permute-start.14 = (bf16[1024,128]{1,0:T(8,128)(2,1)S(1)}, bf16[1024,128]{1,0:T(8,128)(2,1)S(1)}, u32[]{:S(2)}, u32[]{:S(2)}) collective-permute-start(bf16[1024,128]{1,0:T(8,128)(2,1)S(1)} %get-tuple-element.180), channel_id=1, source_target_pairs={{0,16},{4,20},{8,24},{12,28},{16,0},{20,4},{24,8},{28,12},{1,17},{... | collective-permute-start | bytes 786440 | tf_op jit(solution)/shard_map/ppermute | solution.py:309
  114.5 1.5 %collective-permute-start.18 = (bf16[256,128]{1,0:T(8,128)(2,1)S(1)}, bf16[256,128]{1,0:T(8,128)(2,1)S(1)}, u32[]{:S(2)}, u32[]{:S(2)}) collective-permute-start(bf16[256,128]{1,0:T(8,128)(2,1)S(1)} %broadcast_select_fusion.2), channel_id=1, source_target_pairs={{0,4},{4,0},{8,12},{12,8},{16,20},{20,16},{24,28},{28,24},{1,5},{5... | collective-permute-start | bytes 196616 | tf_op jit(solution)/shard_map/ppermute | solution.py:309
  115.2 13.5 %collective-permute-start.16 = (bf16[2048,128]{1,0:T(8,128)(2,1)S(1)}, bf16[2048,128]{1,0:T(8,128)(2,1)S(1)}, u32[]{:S(2)}, u32[]{:S(2)}) collective-permute-start(bf16[2048,128]{1,0:T(8,128)(2,1)S(1)} %bitcast.56), channel_id=1, source_target_pairs={{0,8},{4,12},{8,0},{12,4},{16,24},{20,28},{24,16},{28,20},{1,9},{5... | collective-permute-start | bytes 1572872 | tf_op jit(solution)/shard_map/ppermute | solution.py:309
  115.3 13.4 %collective-permute-start.17 = (bf16[2048,128]{1,0:T(8,128)(2,1)S(1)}, bf16[2048,128]{1,0:T(8,128)(2,1)S(1)}, u32[]{:S(2)}, u32[]{:S(2)}) collective-permute-start(bf16[2048,128]{1,0:T(8,128)(2,1)S(1)} %bitcast.57), channel_id=1, source_target_pairs={{0,16},{4,20},{8,24},{12,28},{16,0},{20,4},{24,8},{28,12},{1,17},{... | collective-permute-start | bytes 1572872 | tf_op jit(solution)/shard_map/ppermute | solution.py:309
  116.1 5.1 %collective-permute-start.21 = (bf16[256,128]{1,0:T(8,128)(2,1)S(1)}, bf16[256,128]{1,0:T(8,128)(2,1)S(1)}, u32[]{:S(2)}, u32[]{:S(2)}) collective-permute-start(bf16[256,128]{1,0:T(8,128)(2,1)S(1)} %add_convert_fusion.12), channel_id=1, source_target_pairs={{0,3},{1,2},{2,1},{3,0},{4,7},{5,6},{6,5},{7,4},{8,11},{9,10},{10,... | collective-permute-start | bytes 196616 | tf_op jit(solution)/shard_map/ppermute | solution.py:309
  118.4 7.7 %collective-permute-start.20 = (bf16[256,128]{1,0:T(8,128)(2,1)S(1)}, bf16[256,128]{1,0:T(8,128)(2,1)S(1)}, u32[]{:S(2)}, u32[]{:S(2)}) collective-permute-start(bf16[256,128]{1,0:T(8,128)(2,1)S(1)} %add_convert_fusion.12), channel_id=1, source_target_pairs={{0,2},{1,3},{2,0},{3,1},{4,6},{5,7},{6,4},{7,5},{8,10},{9,11},{10,... | collective-permute-start | bytes 196616 | tf_op jit(solution)/shard_map/ppermute | solution.py:309
  119.5 6.7 %collective-permute-start.19 = (bf16[256,128]{1,0:T(8,128)(2,1)S(1)}, bf16[256,128]{1,0:T(8,128)(2,1)S(1)}, u32[]{:S(2)}, u32[]{:S(2)}) collective-permute-start(bf16[256,128]{1,0:T(8,128)(2,1)S(1)} %add_convert_fusion.12), channel_id=1, source_target_pairs={{0,1},{1,0},{2,3},{3,2},{4,5},{5,4},{6,7},{7,6},{8,9},{9,8},{10,11... | collective-permute-start | bytes 196616 | tf_op jit(solution)/shard_map/ppermute | solution.py:309
  129.1 6.9 %collective-permute-start.22 = (bf16[1024,128]{1,0:T(8,128)(2,1)S(1)}, bf16[1024,128]{1,0:T(8,128)(2,1)S(1)}, u32[]{:S(2)}, u32[]{:S(2)}) collective-permute-start(bf16[1024,128]{1,0:T(8,128)(2,1)S(1)} %get-tuple-element.158), channel_id=1, source_target_pairs={{0,16},{4,20},{8,24},{12,28},{16,0},{20,4},{24,8},{28,12},{1,17},{... | collective-permute-start | bytes 786440 | tf_op jit(solution)/shard_map/ppermute | solution.py:309
  129.1 6.9 %collective-permute-start.23 = (bf16[1024,128]{1,0:T(8,128)(2,1)S(1)}, bf16[1024,128]{1,0:T(8,128)(2,1)S(1)}, u32[]{:S(2)}, u32[]{:S(2)}) collective-permute-start(bf16[1024,128]{1,0:T(8,128)(2,1)S(1)} %get-tuple-element.160), channel_id=1, source_target_pairs={{0,8},{4,12},{8,0},{12,4},{16,24},{20,28},{24,16},{28,20},{1,9},{5... | collective-permute-start | bytes 786440 | tf_op jit(solution)/shard_map/ppermute | solution.py:309
  130.3 7.6 %collective-permute-start.26 = (bf16[256,128]{1,0:T(8,128)(2,1)S(1)}, bf16[256,128]{1,0:T(8,128)(2,1)S(1)}, u32[]{:S(2)}, u32[]{:S(2)}) collective-permute-start(bf16[256,128]{1,0:T(8,128)(2,1)S(1)} %add_convert_fusion.11), channel_id=1, source_target_pairs={{0,24},{4,28},{8,16},{12,20},{16,8},{20,12},{24,0},{28,4},{1,25},{... | collective-permute-start | bytes 196616 | tf_op jit(solution)/shard_map/ppermute | solution.py:309
  131.8 6.2 %collective-permute-start.25 = (bf16[256,128]{1,0:T(8,128)(2,1)S(1)}, bf16[256,128]{1,0:T(8,128)(2,1)S(1)}, u32[]{:S(2)}, u32[]{:S(2)}) collective-permute-start(bf16[256,128]{1,0:T(8,128)(2,1)S(1)} %add_convert_fusion.11), channel_id=1, source_target_pairs={{0,16},{4,20},{8,24},{12,28},{16,0},{20,4},{24,8},{28,12},{1,17},{... | collective-permute-start | bytes 196616 | tf_op jit(solution)/shard_map/ppermute | solution.py:309
  131.8 6.8 %collective-permute-start.24 = (bf16[256,128]{1,0:T(8,128)(2,1)S(1)}, bf16[256,128]{1,0:T(8,128)(2,1)S(1)}, u32[]{:S(2)}, u32[]{:S(2)}) collective-permute-start(bf16[256,128]{1,0:T(8,128)(2,1)S(1)} %add_convert_fusion.11), channel_id=1, source_target_pairs={{0,8},{4,12},{8,0},{12,4},{16,24},{20,28},{24,16},{28,20},{1,9},{5... | collective-permute-start | bytes 196616 | tf_op jit(solution)/shard_map/ppermute | solution.py:309
  138.7 4.0 %collective-permute-start.27 = (bf16[256,128]{1,0:T(8,128)(2,1)S(1)}, bf16[256,128]{1,0:T(8,128)(2,1)S(1)}, u32[]{:S(2)}, u32[]{:S(2)}) collective-permute-start(bf16[256,128]{1,0:T(8,128)(2,1)S(1)} %add_convert_fusion.10), channel_id=1, source_target_pairs={{0,4},{4,0},{8,12},{12,8},{16,20},{20,16},{24,28},{28,24},{1,5},{5... | collective-permute-start | bytes 196616 | tf_op jit(solution)/shard_map/ppermute | solution.py:309
  (14 other events, 52.7 us)

commit v12 on v11

--- a/solution.py
+++ b/solution.py
@@ -457,25 +457,27 @@
     pieces0 = as_pieces(own0, first0, second0, mid, n_col)
     pieces0, near, acc0 = fence(pieces0, near, acc0)
 
+    near.append([xor_permute(near[1][0][:rows], "row", bits[1]), xor_permute(near[2][0][rows:], "row", bits[0])])
+    for bit in bits[2:]:
+        near += [[xor_permute(f, "row", bit) for f in parts] for parts in near]
     (both0,) = spmm(plan1, pieces0[FIRST_PIECES:], flipped, acc0, n_row, by_core=True)
     got0 = swap_cores(both0)
-    for m in range(6, n_row, 2):
-        near.append([xor_permute(features, "row", m)])
     got0, near = fence(got0, near)
     stage0, sums0 = stage_sums(got0[0], got0[1], n_row // 2, rows, at_once=True)
+    recv0 = exchange_first(stage0, bits)
     own1, first1, stage0, sums0 = fence(own1, first1, stage0, sums0)
 
     second1 = gather_second(own1, first1[1], n_col)
     pieces1 = as_pieces(own1, first1, second1, mid, n_col)
-    recv0 = exchange_first(stage0, bits)
     acc1 = spmm(plan0, pieces1[:FIRST_PIECES], flipped, None, n_row)
-    pieces1, stage0, acc1 = fence(pieces1, stage0, acc1)
+    acc1, recv0 = fence(acc1, recv0)
+    rest0, sent0 = exchange_second(stage0, recv0, bits, rows)
+    pieces1, acc1, rest0, sent0 = fence(pieces1, acc1, rest0, sent0)
 
     send1, keep1 = spmm(plan1, pieces1[FIRST_PIECES:], flipped, acc1, n_row)
-    send1, keep1, recv0, stage0, sums0 = fence(send1, keep1, recv0, stage0, sums0)
+    send1, keep1, rest0, sent0, sums0 = fence(send1, keep1, rest0, sent0, sums0)
 
     stage1, sums1 = stage_sums(keep1, xor_permute(send1, "row", 1), n_row // 2, rows, at_once=True)
-    rest0, sent0 = exchange_second(stage0, recv0, bits, rows)
     recv0 = send_second(sent0, bits)
     term0, term1 = weight_term(near, sums0), weight_term(near, sums1)
     stage1, term0, term1 = fence(stage1, term0, term1)

time: 145 us -> 136 us (0.938)
  blocking collectives: 0 us -> 8.47 us
  local copies, waits for them, and re-layouts: 14.8 us -> 6.36 us
  waiting for transfers between devices: 32.5 us -> 28.9 us
  other arithmetic: 9.76 us -> 6.27 us
  starting transfers between devices: 42 us -> 38.8 us
    unnamed x34 -> x24, local copies, waits for them, and re-layouts: 13.2 us -> 4.03 us
    all_to_all x0 -> x1, blocking collectives: none -> 8.47 us  [swap_cores(): return lax.all_to_all(both, 'row', 0, 0, axis_index_groups=pairs)]
    all_to_all x1 -> x0, starting transfers between devices: 6.75 us -> none  [swap_cores(): return lax.all_to_all(both, 'row', 0, 0, axis_index_groups=pairs)]
    ppermute x24 -> x25, starting transfers between devices: 31.3 us -> 34.8 us  [xor_permute(): return lax.ppermute(value, axis, [(i, i ^ mask) for i in range(size)])]
    all_to_all x1 -> x0, waiting for transfers between devices: 3.23 us -> none  [swap_cores(): return lax.all_to_all(both, 'row', 0, 0, axis_index_groups=pairs)]
    convert_element_type x2, other arithmetic: 4.9 us -> 2.76 us  [stage_sums(): sums = add_f32(keep, recv).astype(jnp.bfloat16)]
    dot_general x8 -> x10, matrix products: 6.27 us -> 7.58 us  [weight_term(): lax.dot_general(f, own, (((0,), (0,)), ((), ())), preferred_element_type=...]
    ppermute x24 -> x25, waiting for transfers between devices: 20.6 us -> 20 us  [xor_permute(): return lax.ppermute(value, axis, [(i, i ^ mask) for i in range(size)])]
  transfers between devices with their start and end apart: 29 -> 29, of which waited for: 14 -> 12; matrix products, arithmetic and copies ran while one was open for 11% -> 11% of each run, Pallas kernels for 24% -> 23%
where the time goes in v12:
time: 136 us; the launch traced here: 135 us
  starting transfers between devices  38.8 us (29%)
  Pallas kernels  35.5 us (26%)
  waiting for transfers between devices  28.9 us (21%)
  matrix products  9.03 us (7%)
  blocking collectives  8.47 us (6%)
  local copies, waits for them, and re-layouts  6.36 us (5%)
  other arithmetic  6.27 us (5%)
  between operations  1.8 us (1%)
    ppermute x25, starting transfers between devices, xor_permute(): return lax.ppermute(value, axis, [(i, i ^ mask) for i in range(size)])  34.8 us
    pallas_call x4, Pallas kernels, spmm(): pl.pallas_call(functools.partial(spmm_kernel, [len(p) for p in pieces], l...  23.6 us
    ppermute x25, waiting for transfers between devices, xor_permute(): return lax.ppermute(value, axis, [(i, i ^ mask) for i in range(size)])  20 us
    pallas_call x1, Pallas kernels, flip_tiles(): pl.pallas_call(flip_kernel, out_shape=jax.ShapeDtypeStruct((slots + GROUP...  9.59 us
    ppermute x2, waiting for transfers between devices, gather_second(): lax.ppermute(by_two, 'col', ends)  8.9 us
    all_to_all x1, blocking collectives, swap_cores(): return lax.all_to_all(both, 'row', 0, 0, axis_index_groups=pairs)  8.47 us
    dot_general x10, matrix products, weight_term(): lax.dot_general(f, own, (((0,), (0,)), ((), ())), preferred_element_type=...  7.58 us
    unnamed x24, local copies, waits for them, and re-layouts  4.03 us
  transfers between devices with their start and end apart: 29, of which 12 were waited for; matrix products, arithmetic and copies ran while one was open for 11% of the time, Pallas kernels for 23%

profile of v12, /device:TPU:1, one launch (start us, length us, event | category | flops | bytes accessed | tf_op | source)
XLA Modules:
  0.0 135.1 jit_solution(12828181304728891913)
XLA Ops:
  0.7 1.7 %compare_select_fusion = (bf16[2048,128]{1,0:T(8,128)(2,1)S(1)}, bf16[2048,128]{1,0:T(8,128)(2,1)S(1)}) fusion(bf16[2048,256]{1,0:T(8,128)(2,1)} %param.8, bf16[2048,256]{1,0:T(8,128)(2,1)} %param.9), kind=kLoop, calls=%fused_computation.21 | loop fusion | flops 1048576 | bytes 3145728 | tf_op jit(solution)/shard_map/jit(_where)/select_n | solution.py:440
  2.3 3.2 %collective-permute-start.1 = (bf16[2048,128]{1,0:T(8,128)(2,1)S(1)}, bf16[2048,128]{1,0:T(8,128)(2,1)S(1)}, u32[]{:S(2)}, u32[]{:S(2)}) collective-permute-start(bf16[2048,128]{1,0:T(8,128)(2,1)S(1)} %get-tuple-element.95.refs_0_), channel_id=1, source_target_pairs={{0,2},{1,3},{2,0},{3,1},{4,6},{5,7},{6,4},{7,5},{8,10},{9,11},{10,... | collective-permute-start | bytes 1572872 | tf_op jit(solution)/shard_map/ppermute | solution.py:309
  5.5 1.3 collective-permute-start
  7.9 2.3 %plan_slots.1 = (s32[8,512]{1,0:T(8,128)S(1)}, s32[8,512]{1,0:T(8,128)S(1)}, s32[1,320]{1,0:T(1,128)S(1)}) custom-call(s32[4]{0:T(128)S(1)} %pad_add_fusion.place_ref, s32[1,320]{1,0:T(1,128)S(1)} %bitcast.45, s32[1,320]{1,0:T(1,128)S(1)} %bitcast.47, s32[320,1]{1,0:T(8,128)S(1)} %copy.10.rows_c, s32[320,1]{1,0:T(8,128)S(1)} %copy.11.cols_c), custom_call_target="tpu_custom_call" | custom-call | bytes 4096 | tf_op jit(solution)/shard_map/plan_slots/pallas_call | solution.py:120
  10.2 1.3 collective-permute-start.7
  12.7 4.0 %copy-done.1 = bf16[1,1,320,128,128]{4,3,2,1,0:T(8,128)(2,1)S(1)} copy-done((bf16[1,1,320,128,128]{4,3,2,1,0:T(8,128)(2,1)S(1)}, bf16[1,1,320,128,128]{4,3,2,1,0:T(8,128)(2,1)}, u32[]{:S(2)}) %copy-start.1) | copy-done | bytes 10485784
  16.7 9.6 %flip_tiles.1.refs_3_.refs_2_ = bf16[352,128,128]{2,1,0:T(8,128)(2,1)S(1)} custom-call(s32[1,320]{1,0:T(1,128)S(1)} %get-tuple-element.91.slot_ref, bf16[320,128,128]{2,1,0:T(8,128)(2,1)S(1)} %bitcast.43), custom_call_target="tpu_custom_call" | custom-call | bytes 4096 | tf_op jit(solution)/shard_map/flip_tiles/pallas_call | solution.py:163
  26.3 2.2 %collective-permute-done.1.refs_2_ = bf16[2048,128]{1,0:T(8,128)(2,1)S(1)} collective-permute-done((bf16[2048,128]{1,0:T(8,128)(2,1)S(1)}, bf16[2048,128]{1,0:T(8,128)(2,1)S(1)}, u32[]{:S(2)}, u32[]{:S(2)}) %collective-permute-start.1) | collective-permute-done | bytes 524320 | tf_op jit(solution)/shard_map/ppermute | solution.py:309
  29.2 1.3 collective-permute-start.5
  30.5 7.6 %spmm_first.2 = (bf16[8192,128]{1,0:T(8,128)(2,1)S(1)}, bf16[8192,128]{1,0:T(8,128)(2,1)S(1)}) custom-call(s32[8,512]{1,0:T(8,128)S(1)} %get-tuple-element.94.plan_ref, bf16[2048,128]{1,0:T(8,128)(2,1)S(1)} %get-tuple-element.95.refs_0_, bf16[2048,128]{1,0:T(8,128)(2,1)S(1)} %collective-permute-done.refs_1_, ...), custom_call_target="tpu_custom_call" | custom-call | bytes 4096 | tf_op jit(solution)/shard_map/spmm_first/pallas_call | solution.py:286
  38.1 5.3 %collective-permute-done.5.refs_1_ = bf16[2048,128]{1,0:T(8,128)(2,1)S(1)} collective-permute-done((bf16[2048,128]{1,0:T(8,128)(2,1)S(1)}, bf16[2048,128]{1,0:T(8,128)(2,1)S(1)}, u32[]{:S(2)}, u32[]{:S(2)}) %collective-permute-start.5) | collective-permute-done | bytes 524320 | tf_op jit(solution)/shard_map/ppermute | solution.py:327
  46.1 2.6 %collective-permute-start.3 = (bf16[2048,128]{1,0:T(8,128)(2,1)S(1)}, bf16[2048,128]{1,0:T(8,128)(2,1)S(1)}, u32[]{:S(2)}, u32[]{:S(2)}) collective-permute-start(bf16[2048,128]{1,0:T(8,128)(2,1)S(1)} %get-tuple-element.113.refs_0_), channel_id=1, source_target_pairs={{0,2},{1,3},{2,0},{3,1},{4,6},{5,7},{6,4},{7,5},{8,10},{9,11},{10,... | collective-permute-start | bytes 1572872 | tf_op jit(solution)/shard_map/ppermute | solution.py:309
  48.7 2.2 %collective-permute-start.2 = (bf16[2048,128]{1,0:T(8,128)(2,1)S(1)}, bf16[2048,128]{1,0:T(8,128)(2,1)S(1)}, u32[]{:S(2)}, u32[]{:S(2)}) collective-permute-start(bf16[2048,128]{1,0:T(8,128)(2,1)S(1)} %get-tuple-element.113.refs_0_), channel_id=1, source_target_pairs={{0,1},{1,0},{2,3},{3,2},{4,5},{5,4},{6,7},{7,6},{8,9},{9,8},{10,11... | collective-permute-start | bytes 1572872 | tf_op jit(solution)/shard_map/ppermute | solution.py:309
  50.9 3.4 %spmm_last.2 = bf16[2,8192,128]{2,1,0:T(8,128)(2,1)S(1)} custom-call(s32[8,512]{1,0:T(8,128)S(1)} %get-tuple-element.92.plan_ref, bf16[2048,128]{1,0:T(8,128)(2,1)S(1)} %collective-permute-done.4.refs_0_, bf16[2048,128]{1,0:T(8,128)(2,1)S(1)} %collective-permute-done.5.refs_1_, bf16[352,128,128]{2,1,0:T(8,128)(2,1)S(1)} %flip_tiles.1.refs_3_.refs_2_, ...), custom_call_target="tpu_custom_call" | custom-call | bytes 4096 | tf_op jit(solution)/shard_map/spmm_last/pallas_call | solution.py:286
  54.4 8.5 %all_to_all.5 = bf16[2,8192,128]{2,1,0:T(8,128)(2,1)S(1)} all-to-all(bf16[2,8192,128]{2,1,0:T(8,128)(2,1)S(1)} %spmm_last.2), channel_id=1, replica_groups={{0,4},{8,12},{16,20},{24,28},{1,5},{9,13},{17,21},{25,29},{2,6},{10,14}..., dimensions={0} | all-to-all | bytes 8388608 | tf_op jit(solution)/shard_map/all_to_all | solution.py:341
  63.5 1.6 %collective-permute-start.12 = (bf16[2048,128]{1,0:T(8,128)(2,1)S(1)}, bf16[2048,128]{1,0:T(8,128)(2,1)S(1)}, u32[]{:S(2)}, u32[]{:S(2)}) collective-permute-start(bf16[2048,128]{1,0:T(8,128)(2,1)S(1)} %bitcast.61), channel_id=1, source_target_pairs={{0,8},{4,12},{8,0},{12,4},{16,24},{20,28},{24,16},{28,20},{1,9},{5... | collective-permute-start | bytes 1572872 | tf_op jit(solution)/shard_map/ppermute | solution.py:309
  65.5 4.8 %collective-permute-done.3.refs_2_ = bf16[2048,128]{1,0:T(8,128)(2,1)S(1)} collective-permute-done((bf16[2048,128]{1,0:T(8,128)(2,1)S(1)}, bf16[2048,128]{1,0:T(8,128)(2,1)S(1)}, u32[]{:S(2)}, u32[]{:S(2)}) %collective-permute-start.3) | collective-permute-done | bytes 524320 | tf_op jit(solution)/shard_map/ppermute | solution.py:309
  72.4 7.6 %spmm_first.3 = (bf16[8192,128]{1,0:T(8,128)(2,1)S(1)}, bf16[8192,128]{1,0:T(8,128)(2,1)S(1)}) custom-call(s32[8,512]{1,0:T(8,128)S(1)} %get-tuple-element.94.plan_ref, bf16[2048,128]{1,0:T(8,128)(2,1)S(1)} %get-tuple-element.113.refs_0_, bf16[2048,128]{1,0:T(8,128)(2,1)S(1)} %collective-permute-done.2.refs_1_, ...), custom_call_target="tpu_custom_call" | custom-call | bytes 4096 | tf_op jit(solution)/shard_map/spmm_first/pallas_call | solution.py:286
  81.9 3.6 %collective-permute-done.11.refs_1_ = bf16[2048,128]{1,0:T(8,128)(2,1)S(1)} collective-permute-done((bf16[2048,128]{1,0:T(8,128)(2,1)S(1)}, bf16[2048,128]{1,0:T(8,128)(2,1)S(1)}, u32[]{:S(2)}, u32[]{:S(2)}) %collective-permute-start.11) | collective-permute-done | bytes 524320 | tf_op jit(solution)/shard_map/ppermute | solution.py:327
  85.5 5.0 %spmm_last.3 = (bf16[8192,128]{1,0:T(8,128)(2,1)}, bf16[8192,128]{1,0:T(8,128)(2,1)S(1)}) custom-call(s32[8,512]{1,0:T(8,128)S(1)} %get-tuple-element.92.plan_ref, bf16[2048,128]{1,0:T(8,128)(2,1)S(1)} %collective-permute-done.10.refs_0_, bf16[2048,128]{1,0:T(8,128)(2,1)S(1)} %collective-permute-done.11.refs_1_, ...), custom_call_target="tpu_custom_call" | custom-call | bytes 4096 | tf_op jit(solution)/shard_map/spmm_last/pallas_call | solution.py:286
  90.5 2.8 %collective-permute-start.14 = (bf16[8192,128]{1,0:T(8,128)(2,1)}, bf16[8192,128]{1,0:T(8,128)(2,1)}, u32[]{:S(2)}, u32[]{:S(2)}) collective-permute-start(bf16[8192,128]{1,0:T(8,128)(2,1)} %get-tuple-element.136), channel_id=1, source_target_pairs={{0,4},{4,0},{8,12},{12,8},{16,20},{20,16},{24,28},{28,24},{1,5},{5... | collective-permute-start | bytes 6291464 | tf_op jit(solution)/shard_map/ppermute | solution.py:309
  93.2 1.7 %collective-permute-start.15 = (bf16[1024,128]{1,0:T(8,128)(2,1)}, bf16[1024,128]{1,0:T(8,128)(2,1)S(1)}, u32[]{:S(2)}, u32[]{:S(2)}) collective-permute-start(bf16[1024,128]{1,0:T(8,128)(2,1)} %get-tuple-element.151), channel_id=1, source_target_pairs={{0,16},{4,20},{8,24},{12,28},{16,0},{20,4},{24,8},{28,12},{1,17},{... | collective-permute-start | bytes 786440 | tf_op jit(solution)/shard_map/ppermute | solution.py:309
  96.5 1.4 %fusion.28 = f32[256,128]{1,0:T(8,128)S(1)} fusion(bf16[1024,256]{1,0:T(8,128)(2,1)S(1)} %collective-permute-done.8, bf16[8192,128]{1,0:T(8,128)(2,1)} %copy-done.4), kind=kOutput, calls=%fused_computation.49 | convolution fusion | flops 67108864 | bytes 917504 | tf_op jit(solution)/shard_map/dot_general | solution.py:419
  97.8 1.8 %fusion.17 = f32[256,128]{1,0:T(8,128)S(1)} fusion(bf16[2048,256]{1,0:T(8,128)(2,1)} %copy-done.8, bf16[8192,128]{1,0:T(8,128)(2,1)} %copy-done.4), kind=kOutput, calls=%fused_computation.34 | convolution fusion | flops 134217728 | bytes 1703936 | tf_op jit(solution)/shard_map/dot_general | solution.py:419
  100.7 2.2 %add_convert_fusion = bf16[8192,128]{1,0:T(8,128)(2,1)S(1)} fusion(bf16[8192,128]{1,0:T(8,128)(2,1)} %collective-permute-done.14, bf16[8192,128]{1,0:T(8,128)(2,1)S(1)} %get-tuple-element.135), kind=kLoop, calls=%fused_computation | loop fusion | flops 4194304 | bytes 6291456 | tf_op jit(solution)/shard_map/convert_element_type | solution.py:356
  107.4 4.9 %collective-permute-start.22 = (bf16[256,128]{1,0:T(8,128)(2,1)S(1)}, bf16[256,128]{1,0:T(8,128)(2,1)S(1)}, u32[]{:S(2)}, u32[]{:S(2)}) collective-permute-start(bf16[256,128]{1,0:T(8,128)(2,1)S(1)} %add_convert_fusion.12), channel_id=1, source_target_pairs={{0,3},{1,2},{2,1},{3,0},{4,7},{5,6},{6,5},{7,4},{8,11},{9,10},{10,... | collective-permute-start | bytes 196616 | tf_op jit(solution)/shard_map/ppermute | solution.py:309
  114.0 2.9 %collective-permute-done.21 = bf16[256,128]{1,0:T(8,128)(2,1)S(1)} collective-permute-done((bf16[256,128]{1,0:T(8,128)(2,1)S(1)}, bf16[256,128]{1,0:T(8,128)(2,1)S(1)}, u32[]{:S(2)}, u32[]{:S(2)}) %collective-permute-start.21) | collective-permute-done | bytes 65568 | tf_op jit(solution)/shard_map/ppermute | solution.py:309
  117.0 2.5 %collective-permute-done.17 = bf16[2048,128]{1,0:T(8,128)(2,1)S(1)} collective-permute-done((bf16[2048,128]{1,0:T(8,128)(2,1)S(1)}, bf16[2048,128]{1,0:T(8,128)(2,1)S(1)}, u32[]{:S(2)}, u32[]{:S(2)}) %collective-permute-start.17) | collective-permute-done | bytes 524320 | tf_op jit(solution)/shard_map/ppermute | solution.py:309
  124.9 2.6 %collective-permute-done.23 = bf16[1024,128]{1,0:T(8,128)(2,1)S(1)} collective-permute-done((bf16[1024,128]{1,0:T(8,128)(2,1)S(1)}, bf16[1024,128]{1,0:T(8,128)(2,1)S(1)}, u32[]{:S(2)}, u32[]{:S(2)}) %collective-permute-start.23) | collective-permute-done | bytes 262176 | tf_op jit(solution)/shard_map/ppermute | solution.py:309
  127.8 1.7 %collective-permute-done.27 = bf16[256,128]{1,0:T(8,128)(2,1)S(1)} collective-permute-done((bf16[256,128]{1,0:T(8,128)(2,1)S(1)}, bf16[256,128]{1,0:T(8,128)(2,1)S(1)}, u32[]{:S(2)}, u32[]{:S(2)}) %collective-permute-start.27) | collective-permute-done | bytes 65568 | tf_op jit(solution)/shard_map/ppermute | solution.py:309
  130.5 2.4 %collective-permute-start.28 = (bf16[256,128]{1,0:T(8,128)(2,1)S(1)}, bf16[256,128]{1,0:T(8,128)(2,1)S(1)}, u32[]{:S(2)}, u32[]{:S(2)}) collective-permute-start(bf16[256,128]{1,0:T(8,128)(2,1)S(1)} %add_convert_fusion.10), channel_id=1, source_target_pairs={{0,4},{4,0},{8,12},{12,8},{16,20},{20,16},{24,28},{28,24},{1,5},{5... | collective-permute-start | bytes 196616 | tf_op jit(solution)/shard_map/ppermute | solution.py:309
  133.0 1.4 %convolution_convert_fusion = bf16[2048,256]{1,0:T(8,128)(2,1)} fusion(bf16[256,256]{1,0:T(8,128)(2,1)S(1)} %copy-done, bf16[2048,128]{1,0:T(8,128)(2,1)S(1)} %pad_maximum_fusion.1, bf16[2048,128]{1,0:T(8,128)(2,1)S(1)} %pad_maximum_fusion), kind=kOutput, calls=%fused_computation.2 | convolution fusion | flops 271056896 | bytes 2228224 | tf_op jit(solution)/shard_map/dot_general | solution.py:506
  (99 shorter events, 25.8 us)
Async XLA Ops:
  0.6 132.3 %copy-start = (bf16[256,256]{1,0:T(8,128)(2,1)S(1)}, bf16[256,256]{1,0:T(8,128)(2,1)}, u32[]{:S(2)}) copy-start(bf16[256,256]{1,0:T(8,128)(2,1)} %param.11) | copy-start | bytes 393220
  2.3 26.1 %collective-permute-start.1 = (bf16[2048,128]{1,0:T(8,128)(2,1)S(1)}, bf16[2048,128]{1,0:T(8,128)(2,1)S(1)}, u32[]{:S(2)}, u32[]{:S(2)}) collective-permute-start(bf16[2048,128]{1,0:T(8,128)(2,1)S(1)} %get-tuple-element.95.refs_0_), channel_id=1, source_target_pairs={{0,2},{1,3},{2,0},{3,1},{4,6},{5,7},{6,4},{7,5},{8,10},{9,11},{10,... | collective-permute-start | bytes 1572872 | tf_op jit(solution)/shard_map/ppermute | solution.py:309
  5.5 22.9 %collective-permute-start = (bf16[2048,128]{1,0:T(8,128)(2,1)S(1)}, bf16[2048,128]{1,0:T(8,128)(2,1)S(1)}, u32[]{:S(2)}, u32[]{:S(2)}) collective-permute-start(bf16[2048,128]{1,0:T(8,128)(2,1)S(1)} %get-tuple-element.95.refs_0_), channel_id=1, source_target_pairs={{0,1},{1,0},{2,3},{3,2},{4,5},{5,4},{6,7},{7,6},{8,9},{9,8},{10,11... | collective-permute-start | bytes 1572872 | tf_op jit(solution)/shard_map/ppermute | solution.py:309
  10.2 27.9 %collective-permute-start.7 = (bf16[2048,256]{1,0:T(8,128)(2,1)}, bf16[2048,256]{1,0:T(8,128)(2,1)S(1)}, u32[]{:S(2)}, u32[]{:S(2)}) collective-permute-start(bf16[2048,256]{1,0:T(8,128)(2,1)} %param.10), channel_id=1, source_target_pairs={{0,16},{4,20},{8,24},{12,28},{16,0},{20,4},{24,8},{28,12},{1,17},{... | collective-permute-start | bytes 3145736 | tf_op jit(solution)/shard_map/ppermute | solution.py:309
  11.5 26.6 %collective-permute-start.6 = (bf16[2048,256]{1,0:T(8,128)(2,1)}, bf16[2048,256]{1,0:T(8,128)(2,1)S(1)}, u32[]{:S(2)}, u32[]{:S(2)}) collective-permute-start(bf16[2048,256]{1,0:T(8,128)(2,1)} %param.10), channel_id=1, source_target_pairs={{0,8},{4,12},{8,0},{12,4},{16,24},{20,28},{24,16},{28,20},{1,9},{5... | collective-permute-start | bytes 3145736 | tf_op jit(solution)/shard_map/ppermute | solution.py:309
  28.5 9.7 %collective-permute-start.4 = (bf16[2048,128]{1,0:T(8,128)(2,1)S(1)}, bf16[2048,128]{1,0:T(8,128)(2,1)S(1)}, u32[]{:S(2)}, u32[]{:S(2)}) collective-permute-start(bf16[2048,128]{1,0:T(8,128)(2,1)S(1)} %get-tuple-element.95.refs_0_), channel_id=1, source_target_pairs={{1,2},{2,1},{5,6},{6,5},{9,10},{10,9},{13,14},{14,13},{17,18},{18,... | collective-permute-start | bytes 1572872 | tf_op jit(solution)/shard_map/ppermute | solution.py:327
  29.2 14.3 %collective-permute-start.5 = (bf16[2048,128]{1,0:T(8,128)(2,1)S(1)}, bf16[2048,128]{1,0:T(8,128)(2,1)S(1)}, u32[]{:S(2)}, u32[]{:S(2)}) collective-permute-start(bf16[2048,128]{1,0:T(8,128)(2,1)S(1)} %collective-permute-done.1.refs_2_), channel_id=1, source_target_pairs={{1,0},{2,3},{5,4},{6,7},{9,8},{10,11},{13,12},{14,15},{17,16},{18,... | collective-permute-start | bytes 1572872 | tf_op jit(solution)/shard_map/ppermute | solution.py:327
  38.1 12.8 %copy-start.8 = (bf16[2048,256]{1,0:T(8,128)(2,1)}, bf16[2048,256]{1,0:T(8,128)(2,1)S(1)}, u32[]{:S(2)}) copy-start(bf16[2048,256]{1,0:T(8,128)(2,1)S(1)} %collective-permute-done.7) | copy-start | bytes 3145732
  38.1 12.8 %copy-start.10 = (bf16[2048,256]{1,0:T(8,128)(2,1)}, bf16[2048,256]{1,0:T(8,128)(2,1)S(1)}, u32[]{:S(2)}) copy-start(bf16[2048,256]{1,0:T(8,128)(2,1)S(1)} %collective-permute-done.6) | copy-start | bytes 3145732
  43.5 19.3 %collective-permute-start.9 = (bf16[1024,256]{1,0:T(8,128)(2,1)S(1)}, bf16[1024,256]{1,0:T(8,128)(2,1)S(1)}, u32[]{:S(2)}, u32[]{:S(2)}) collective-permute-start(bf16[1024,256]{1,0:T(8,128)(2,1)S(1)} %slice.111), channel_id=1, source_target_pairs={{0,8},{4,12},{8,0},{12,4},{16,24},{20,28},{24,16},{28,20},{1,9},{5... | collective-permute-start | bytes 1572872 | tf_op jit(solution)/shard_map/ppermute | solution.py:309
  44.8 18.0 %collective-permute-start.8 = (bf16[1024,256]{1,0:T(8,128)(2,1)S(1)}, bf16[1024,256]{1,0:T(8,128)(2,1)S(1)}, u32[]{:S(2)}, u32[]{:S(2)}) collective-permute-start(bf16[1024,256]{1,0:T(8,128)(2,1)S(1)} %slice.110), channel_id=1, source_target_pairs={{0,16},{4,20},{8,24},{12,28},{16,0},{20,4},{24,8},{28,12},{1,17},{... | collective-permute-start | bytes 1572872 | tf_op jit(solution)/shard_map/ppermute | solution.py:309
  46.1 24.3 %collective-permute-start.3 = (bf16[2048,128]{1,0:T(8,128)(2,1)S(1)}, bf16[2048,128]{1,0:T(8,128)(2,1)S(1)}, u32[]{:S(2)}, u32[]{:S(2)}) collective-permute-start(bf16[2048,128]{1,0:T(8,128)(2,1)S(1)} %get-tuple-element.113.refs_0_), channel_id=1, source_target_pairs={{0,2},{1,3},{2,0},{3,1},{4,6},{5,7},{6,4},{7,5},{8,10},{9,11},{10,... | collective-permute-start | bytes 1572872 | tf_op jit(solution)/shard_map/ppermute | solution.py:309
  48.7 21.7 %collective-permute-start.2 = (bf16[2048,128]{1,0:T(8,128)(2,1)S(1)}, bf16[2048,128]{1,0:T(8,128)(2,1)S(1)}, u32[]{:S(2)}, u32[]{:S(2)}) collective-permute-start(bf16[2048,128]{1,0:T(8,128)(2,1)S(1)} %get-tuple-element.113.refs_0_), channel_id=1, source_target_pairs={{0,1},{1,0},{2,3},{3,2},{4,5},{5,4},{6,7},{7,6},{8,9},{9,8},{10,11... | collective-permute-start | bytes 1572872 | tf_op jit(solution)/shard_map/ppermute | solution.py:309
  63.5 16.4 %collective-permute-start.12 = (bf16[2048,128]{1,0:T(8,128)(2,1)S(1)}, bf16[2048,128]{1,0:T(8,128)(2,1)S(1)}, u32[]{:S(2)}, u32[]{:S(2)}) collective-permute-start(bf16[2048,128]{1,0:T(8,128)(2,1)S(1)} %bitcast.61), channel_id=1, source_target_pairs={{0,8},{4,12},{8,0},{12,4},{16,24},{20,28},{24,16},{28,20},{1,9},{5... | collective-permute-start | bytes 1572872 | tf_op jit(solution)/shard_map/ppermute | solution.py:309
  65.2 14.8 %collective-permute-start.13 = (bf16[2048,128]{1,0:T(8,128)(2,1)S(1)}, bf16[2048,128]{1,0:T(8,128)(2,1)S(1)}, u32[]{:S(2)}, u32[]{:S(2)}) collective-permute-start(bf16[2048,128]{1,0:T(8,128)(2,1)S(1)} %bitcast.60), channel_id=1, source_target_pairs={{0,16},{4,20},{8,24},{12,28},{16,0},{20,4},{24,8},{28,12},{1,17},{... | collective-permute-start | bytes 1572872 | tf_op jit(solution)/shard_map/ppermute | solution.py:309
  70.4 11.5 %collective-permute-start.10 = (bf16[2048,128]{1,0:T(8,128)(2,1)S(1)}, bf16[2048,128]{1,0:T(8,128)(2,1)S(1)}, u32[]{:S(2)}, u32[]{:S(2)}) collective-permute-start(bf16[2048,128]{1,0:T(8,128)(2,1)S(1)} %get-tuple-element.113.refs_0_), channel_id=1, source_target_pairs={{1,2},{2,1},{5,6},{6,5},{9,10},{10,9},{13,14},{14,13},{17,18},{18,... | collective-permute-start | bytes 1572872 | tf_op jit(solution)/shard_map/ppermute | solution.py:327
  71.1 14.4 %collective-permute-start.11 = (bf16[2048,128]{1,0:T(8,128)(2,1)S(1)}, bf16[2048,128]{1,0:T(8,128)(2,1)S(1)}, u32[]{:S(2)}, u32[]{:S(2)}) collective-permute-start(bf16[2048,128]{1,0:T(8,128)(2,1)S(1)} %collective-permute-done.3.refs_2_), channel_id=1, source_target_pairs={{1,0},{2,3},{5,4},{6,7},{9,8},{10,11},{13,12},{14,15},{17,16},{18,... | collective-permute-start | bytes 1572872 | tf_op jit(solution)/shard_map/ppermute | solution.py:327
  90.5 10.2 %collective-permute-start.14 = (bf16[8192,128]{1,0:T(8,128)(2,1)}, bf16[8192,128]{1,0:T(8,128)(2,1)}, u32[]{:S(2)}, u32[]{:S(2)}) collective-permute-start(bf16[8192,128]{1,0:T(8,128)(2,1)} %get-tuple-element.136), channel_id=1, source_target_pairs={{0,4},{4,0},{8,12},{12,8},{16,20},{20,16},{24,28},{28,24},{1,5},{5... | collective-permute-start | bytes 6291464 | tf_op jit(solution)/shard_map/ppermute | solution.py:309
  93.2 12.0 %collective-permute-start.15 = (bf16[1024,128]{1,0:T(8,128)(2,1)}, bf16[1024,128]{1,0:T(8,128)(2,1)S(1)}, u32[]{:S(2)}, u32[]{:S(2)}) collective-permute-start(bf16[1024,128]{1,0:T(8,128)(2,1)} %get-tuple-element.151), channel_id=1, source_target_pairs={{0,16},{4,20},{8,24},{12,28},{16,0},{20,4},{24,8},{28,12},{1,17},{... | collective-permute-start | bytes 786440 | tf_op jit(solution)/shard_map/ppermute | solution.py:309
  94.9 10.4 %collective-permute-start.16 = (bf16[1024,128]{1,0:T(8,128)(2,1)}, bf16[1024,128]{1,0:T(8,128)(2,1)S(1)}, u32[]{:S(2)}, u32[]{:S(2)}) collective-permute-start(bf16[1024,128]{1,0:T(8,128)(2,1)} %get-tuple-element.152), channel_id=1, source_target_pairs={{0,8},{4,12},{8,0},{12,4},{16,24},{20,28},{24,16},{28,20},{1,9},{5... | collective-permute-start | bytes 786440 | tf_op jit(solution)/shard_map/ppermute | solution.py:309
  105.3 2.1 %collective-permute-start.19 = (bf16[256,128]{1,0:T(8,128)(2,1)S(1)}, bf16[256,128]{1,0:T(8,128)(2,1)S(1)}, u32[]{:S(2)}, u32[]{:S(2)}) collective-permute-start(bf16[256,128]{1,0:T(8,128)(2,1)S(1)} %broadcast_select_fusion.2), channel_id=1, source_target_pairs={{0,4},{4,0},{8,12},{12,8},{16,20},{20,16},{24,28},{28,24},{1,5},{5... | collective-permute-start | bytes 196616 | tf_op jit(solution)/shard_map/ppermute | solution.py:309
  106.0 13.5 %collective-permute-start.17 = (bf16[2048,128]{1,0:T(8,128)(2,1)S(1)}, bf16[2048,128]{1,0:T(8,128)(2,1)S(1)}, u32[]{:S(2)}, u32[]{:S(2)}) collective-permute-start(bf16[2048,128]{1,0:T(8,128)(2,1)S(1)} %bitcast.58), channel_id=1, source_target_pairs={{0,8},{4,12},{8,0},{12,4},{16,24},{20,28},{24,16},{28,20},{1,9},{5... | collective-permute-start | bytes 1572872 | tf_op jit(solution)/shard_map/ppermute | solution.py:309
  107.2 13.2 %collective-permute-start.18 = (bf16[2048,128]{1,0:T(8,128)(2,1)S(1)}, bf16[2048,128]{1,0:T(8,128)(2,1)S(1)}, u32[]{:S(2)}, u32[]{:S(2)}) collective-permute-start(bf16[2048,128]{1,0:T(8,128)(2,1)S(1)} %bitcast.59), channel_id=1, source_target_pairs={{0,16},{4,20},{8,24},{12,28},{16,0},{20,4},{24,8},{28,12},{1,17},{... | collective-permute-start | bytes 1572872 | tf_op jit(solution)/shard_map/ppermute | solution.py:309
  107.4 6.6 %collective-permute-start.22 = (bf16[256,128]{1,0:T(8,128)(2,1)S(1)}, bf16[256,128]{1,0:T(8,128)(2,1)S(1)}, u32[]{:S(2)}, u32[]{:S(2)}) collective-permute-start(bf16[256,128]{1,0:T(8,128)(2,1)S(1)} %add_convert_fusion.12), channel_id=1, source_target_pairs={{0,3},{1,2},{2,1},{3,0},{4,7},{5,6},{6,5},{7,4},{8,11},{9,10},{10,... | collective-permute-start | bytes 196616 | tf_op jit(solution)/shard_map/ppermute | solution.py:309
  112.4 4.5 %collective-permute-start.21 = (bf16[256,128]{1,0:T(8,128)(2,1)S(1)}, bf16[256,128]{1,0:T(8,128)(2,1)S(1)}, u32[]{:S(2)}, u32[]{:S(2)}) collective-permute-start(bf16[256,128]{1,0:T(8,128)(2,1)S(1)} %add_convert_fusion.12), channel_id=1, source_target_pairs={{0,2},{1,3},{2,0},{3,1},{4,6},{5,7},{6,4},{7,5},{8,10},{9,11},{10,... | collective-permute-start | bytes 196616 | tf_op jit(solution)/shard_map/ppermute | solution.py:309
  112.4 4.5 %collective-permute-start.20 = (bf16[256,128]{1,0:T(8,128)(2,1)S(1)}, bf16[256,128]{1,0:T(8,128)(2,1)S(1)}, u32[]{:S(2)}, u32[]{:S(2)}) collective-permute-start(bf16[256,128]{1,0:T(8,128)(2,1)S(1)} %add_convert_fusion.12), channel_id=1, source_target_pairs={{0,1},{1,0},{2,3},{3,2},{4,5},{5,4},{6,7},{7,6},{8,9},{9,8},{10,11... | collective-permute-start | bytes 196616 | tf_op jit(solution)/shard_map/ppermute | solution.py:309
  120.8 6.7 %collective-permute-start.23 = (bf16[1024,128]{1,0:T(8,128)(2,1)S(1)}, bf16[1024,128]{1,0:T(8,128)(2,1)S(1)}, u32[]{:S(2)}, u32[]{:S(2)}) collective-permute-start(bf16[1024,128]{1,0:T(8,128)(2,1)S(1)} %get-tuple-element.168), channel_id=1, source_target_pairs={{0,16},{4,20},{8,24},{12,28},{16,0},{20,4},{24,8},{28,12},{1,17},{... | collective-permute-start | bytes 786440 | tf_op jit(solution)/shard_map/ppermute | solution.py:309
  121.1 6.6 %collective-permute-start.24 = (bf16[1024,128]{1,0:T(8,128)(2,1)S(1)}, bf16[1024,128]{1,0:T(8,128)(2,1)S(1)}, u32[]{:S(2)}, u32[]{:S(2)}) collective-permute-start(bf16[1024,128]{1,0:T(8,128)(2,1)S(1)} %get-tuple-element.170), channel_id=1, source_target_pairs={{0,8},{4,12},{8,0},{12,4},{16,24},{20,28},{24,16},{28,20},{1,9},{5... | collective-permute-start | bytes 786440 | tf_op jit(solution)/shard_map/ppermute | solution.py:309
  122.2 7.3 %collective-permute-start.27 = (bf16[256,128]{1,0:T(8,128)(2,1)S(1)}, bf16[256,128]{1,0:T(8,128)(2,1)S(1)}, u32[]{:S(2)}, u32[]{:S(2)}) collective-permute-start(bf16[256,128]{1,0:T(8,128)(2,1)S(1)} %add_convert_fusion.11), channel_id=1, source_target_pairs={{0,24},{4,28},{8,16},{12,20},{16,8},{20,12},{24,0},{28,4},{1,25},{... | collective-permute-start | bytes 196616 | tf_op jit(solution)/shard_map/ppermute | solution.py:309
  123.5 6.0 %collective-permute-start.26 = (bf16[256,128]{1,0:T(8,128)(2,1)S(1)}, bf16[256,128]{1,0:T(8,128)(2,1)S(1)}, u32[]{:S(2)}, u32[]{:S(2)}) collective-permute-start(bf16[256,128]{1,0:T(8,128)(2,1)S(1)} %add_convert_fusion.11), channel_id=1, source_target_pairs={{0,16},{4,20},{8,24},{12,28},{16,0},{20,4},{24,8},{28,12},{1,17},{... | collective-permute-start | bytes 196616 | tf_op jit(solution)/shard_map/ppermute | solution.py:309
  123.7 6.7 %collective-permute-start.25 = (bf16[256,128]{1,0:T(8,128)(2,1)S(1)}, bf16[256,128]{1,0:T(8,128)(2,1)S(1)}, u32[]{:S(2)}, u32[]{:S(2)}) collective-permute-start(bf16[256,128]{1,0:T(8,128)(2,1)S(1)} %add_convert_fusion.11), channel_id=1, source_target_pairs={{0,8},{4,12},{8,0},{12,4},{16,24},{20,28},{24,16},{28,20},{1,9},{5... | collective-permute-start | bytes 196616 | tf_op jit(solution)/shard_map/ppermute | solution.py:309
  130.5 3.9 %collective-permute-start.28 = (bf16[256,128]{1,0:T(8,128)(2,1)S(1)}, bf16[256,128]{1,0:T(8,128)(2,1)S(1)}, u32[]{:S(2)}, u32[]{:S(2)}) collective-permute-start(bf16[256,128]{1,0:T(8,128)(2,1)S(1)} %add_convert_fusion.10), channel_id=1, source_target_pairs={{0,4},{4,0},{8,12},{12,8},{16,20},{20,16},{24,28},{28,24},{1,5},{5... | collective-permute-start | bytes 196616 | tf_op jit(solution)/shard_map/ppermute | solution.py:309
  (9 other events, 47.0 us)

commit v13 on v12

--- a/solution.py
+++ b/solution.py
@@ -15,6 +15,8 @@
 PLAN_ROWS = 8
 FLIP_BYTES = 26 * 1024 * 1024
 PLAN_BYTES = 12 * 1024 * 1024
+TERM_BYTES = 14 * 1024 * 1024
+TERM_ROWS = 512
 SPMM_BYTES = 16 * 1024 * 1024
 
 
@@ -421,6 +423,40 @@
     return sum(terms[1:], terms[0]).astype(jnp.bfloat16)
 
 
+def term_kernel(*refs):
+    *parts, sums_ref, out_ref, acc_ref = refs
+    acc_ref[...] = jnp.zeros_like(acc_ref)
+    first = 0
+    for part in parts:
+
+        def add_rows(step, carry, part=part, first=first):
+            at = pl.multiple_of(step * TERM_ROWS, TERM_ROWS)
+            acc_ref[...] += lax.dot_general(
+                sums_ref[pl.ds(first + at, TERM_ROWS), :], part[pl.ds(at, TERM_ROWS), :],
+                (((0,), (0,)), ((), ())), preferred_element_type=jnp.float32,
+            )
+            return carry
+
+        lax.fori_loop(0, part.shape[0] // TERM_ROWS, add_rows, 0)
+        first += part.shape[0]
+    out_ref[...] = acc_ref[...].T.astype(out_ref.dtype)
+
+
+def weight_term_early(near, sums):
+    parts = [part for group in near for part in group]
+    shape = (parts[0].shape[1], sums.shape[1])
+    return pl.pallas_call(
+        term_kernel,
+        out_shape=jax.ShapeDtypeStruct(shape, jnp.bfloat16),
+        in_specs=[pl.BlockSpec(memory_space=pltpu.VMEM)] * (len(parts) + 1),
+        out_specs=pl.BlockSpec(memory_space=pltpu.VMEM),
+        scratch_shapes=[pltpu.VMEM(shape[::-1], jnp.float32)],
+        compiler_params=pltpu.CompilerParams(vmem_limit_bytes=TERM_BYTES),
+        cost_estimate=pl.CostEstimate(flops=0, bytes_accessed=4096, transcendentals=0),
+        name="weight_term",
+    )(*parts, sums)
+
+
 def sum_over(term, axis, masks):
     parts = [term] + [xor_permute(term, axis, m) for m in masks]
     return tree_sum([p.astype(jnp.float32) for p in parts])
@@ -465,7 +501,8 @@
     got0, near = fence(got0, near)
     stage0, sums0 = stage_sums(got0[0], got0[1], n_row // 2, rows, at_once=True)
     recv0 = exchange_first(stage0, bits)
-    own1, first1, stage0, sums0 = fence(own1, first1, stage0, sums0)
+    term0 = weight_term_early(near, sums0)
+    own1, first1, stage0, term0 = fence(own1, first1, stage0, term0)
 
     second1 = gather_second(own1, first1[1], n_col)
     pieces1 = as_pieces(own1, first1, second1, mid, n_col)
@@ -475,11 +512,11 @@
     pieces1, acc1, rest0, sent0 = fence(pieces1, acc1, rest0, sent0)
 
     send1, keep1 = spmm(plan1, pieces1[FIRST_PIECES:], flipped, acc1, n_row)
-    send1, keep1, rest0, sent0, sums0 = fence(send1, keep1, rest0, sent0, sums0)
+    send1, keep1, rest0, sent0 = fence(send1, keep1, rest0, sent0)
 
     stage1, sums1 = stage_sums(keep1, xor_permute(send1, "row", 1), n_row // 2, rows, at_once=True)
     recv0 = send_second(sent0, bits)
-    term0, term1 = weight_term(near, sums0), weight_term(near, sums1)
+    term1 = weight_term(near, sums1)
     stage1, term0, term1 = fence(stage1, term0, term1)
     stage1, term0, term1, rest0, recv0 = fence(stage1, term0, term1, rest0, recv0)
 

time: 136 us -> 136 us (level)
  Pallas kernels: 35.5 us -> 43.3 us
  matrix products: 9.03 us -> 3.56 us
  starting transfers between devices: 38.8 us -> 35.7 us
  waiting for transfers between devices: 28.9 us -> 27.2 us
  other arithmetic: 6.27 us -> 7.86 us
  local copies, waits for them, and re-layouts: 6.36 us -> 7.84 us
    dot_general x10 -> x5, matrix products: 7.58 us -> 2.12 us  [weight_term(): lax.dot_general(f, own, (((0,), (0,)), ((), ())), preferred_element_type=...]
    pallas_call x4, Pallas kernels: 23.6 us -> 27.6 us  [spmm(): pl.pallas_call(functools.partial(spmm_kernel, [len(p) for p in pieces], l...]
    pallas_call x0 -> x1, Pallas kernels: none -> 3.8 us  [weight_term_early(): pl.pallas_call(term_kernel, out_shape=jax.ShapeDtypeStruct(shape, jnp.bfl...]
    ppermute x25, starting transfers between devices: 34.8 us -> 31.8 us  [xor_permute(): return lax.ppermute(value, axis, [(i, i ^ mask) for i in range(size)])]
    ppermute x2, waiting for transfers between devices: 8.9 us -> 6.97 us  [gather_second(): lax.ppermute(by_two, 'col', ends)]
    unnamed x24 -> x26, local copies, waits for them, and re-layouts: 4.03 us -> 5.44 us
  transfers between devices with their start and end apart: 29 -> 29, of which waited for: 12 -> 13; matrix products, arithmetic and copies ran while one was open for 11% -> 7% of each run, Pallas kernels for 23% -> 28%
where the time goes in v13:
time: 136 us; the launch traced here: 134 us
  Pallas kernels  43.3 us (32%)
  starting transfers between devices  35.7 us (26%)
  waiting for transfers between devices  27.2 us (20%)
  other arithmetic  7.86 us (6%)
  local copies, waits for them, and re-layouts  7.84 us (6%)
  blocking collectives  7.15 us (5%)
  matrix products  3.56 us (3%)
  between operations  1.77 us (1%)
    ppermute x25, starting transfers between devices, xor_permute(): return lax.ppermute(value, axis, [(i, i ^ mask) for i in range(size)])  31.8 us
    pallas_call x4, Pallas kernels, spmm(): pl.pallas_call(functools.partial(spmm_kernel, [len(p) for p in pieces], l...  27.6 us
    ppermute x25, waiting for transfers between devices, xor_permute(): return lax.ppermute(value, axis, [(i, i ^ mask) for i in range(size)])  20.2 us
    pallas_call x1, Pallas kernels, flip_tiles(): pl.pallas_call(flip_kernel, out_shape=jax.ShapeDtypeStruct((slots + GROUP...  9.59 us
    all_to_all x1, blocking collectives, swap_cores(): return lax.all_to_all(both, 'row', 0, 0, axis_index_groups=pairs)  7.15 us
    ppermute x2, waiting for transfers between devices, gather_second(): lax.ppermute(by_two, 'col', ends)  6.97 us
    unnamed x26, local copies, waits for them, and re-layouts  5.44 us
    pallas_call x1, Pallas kernels, weight_term_early(): pl.pallas_call(term_kernel, out_shape=jax.ShapeDtypeStruct(shape, jnp.bfl...  3.8 us
  transfers between devices with their start and end apart: 29, of which 13 were waited for; matrix products, arithmetic and copies ran while one was open for 7% of the time, Pallas kernels for 28%

profile of v13, /device:TPU:1, one launch (start us, length us, event | category | flops | bytes accessed | tf_op | source)
XLA Modules:
  0.0 134.4 jit_solution(14435716632969632845)
XLA Ops:
  0.7 2.7 %compare_select_fusion = (bf16[2048,128]{1,0:T(8,128)(2,1)}, bf16[2048,128]{1,0:T(8,128)(2,1)}) fusion(bf16[2048,256]{1,0:T(8,128)(2,1)} %param.8, bf16[2048,256]{1,0:T(8,128)(2,1)} %param.9), kind=kLoop, calls=%fused_computation.16 | loop fusion | flops 1048576 | bytes 3145728 | tf_op jit(solution)/shard_map/jit(_where)/select_n | solution.py:476
  3.4 3.1 %collective-permute-start.1 = (bf16[2048,128]{1,0:T(8,128)(2,1)}, bf16[2048,128]{1,0:T(8,128)(2,1)}, u32[]{:S(2)}, u32[]{:S(2)}) collective-permute-start(bf16[2048,128]{1,0:T(8,128)(2,1)} %get-tuple-element.94.refs_0_), channel_id=1, source_target_pairs={{0,2},{1,3},{2,0},{3,1},{4,6},{5,7},{6,4},{7,5},{8,10},{9,11},{10,... | collective-permute-start | bytes 1572872 | tf_op jit(solution)/shard_map/ppermute | solution.py:311
  6.5 1.3 collective-permute-start
  8.9 2.3 %plan_slots.1 = (s32[8,512]{1,0:T(8,128)S(1)}, s32[8,512]{1,0:T(8,128)S(1)}, s32[1,320]{1,0:T(1,128)S(1)}) custom-call(s32[4]{0:T(128)S(1)} %pad_add_fusion.place_ref, s32[1,320]{1,0:T(1,128)S(1)} %bitcast.42, s32[1,320]{1,0:T(1,128)S(1)} %bitcast.44, s32[320,1]{1,0:T(8,128)S(1)} %copy.10.rows_c, s32[320,1]{1,0:T(8,128)S(1)} %copy.11.cols_c), custom_call_target="tpu_custom_call" | custom-call | bytes 4096 | tf_op jit(solution)/shard_map/plan_slots/pallas_call | solution.py:122
  11.2 1.3 collective-permute-start.7
  13.7 4.0 %copy-done.1 = bf16[1,1,320,128,128]{4,3,2,1,0:T(8,128)(2,1)S(1)} copy-done((bf16[1,1,320,128,128]{4,3,2,1,0:T(8,128)(2,1)S(1)}, bf16[1,1,320,128,128]{4,3,2,1,0:T(8,128)(2,1)}, u32[]{:S(2)}) %copy-start.1) | copy-done | bytes 10485784
  17.7 9.6 %flip_tiles.1.refs_3_.refs_2_ = bf16[352,128,128]{2,1,0:T(8,128)(2,1)S(1)} custom-call(s32[1,320]{1,0:T(1,128)S(1)} %get-tuple-element.90.slot_ref, bf16[320,128,128]{2,1,0:T(8,128)(2,1)S(1)} %bitcast.40), custom_call_target="tpu_custom_call" | custom-call | bytes 4096 | tf_op jit(solution)/shard_map/flip_tiles/pallas_call | solution.py:165
  27.3 2.5 %collective-permute-done.1.refs_2_ = bf16[2048,128]{1,0:T(8,128)(2,1)} collective-permute-done((bf16[2048,128]{1,0:T(8,128)(2,1)}, bf16[2048,128]{1,0:T(8,128)(2,1)}, u32[]{:S(2)}, u32[]{:S(2)}) %collective-permute-start.1) | collective-permute-done | bytes 524320 | tf_op jit(solution)/shard_map/ppermute | solution.py:311
  30.5 1.3 collective-permute-start.5
  31.8 9.2 %spmm_first.2 = (bf16[8192,128]{1,0:T(8,128)(2,1)S(1)}, bf16[8192,128]{1,0:T(8,128)(2,1)S(1)}) custom-call(s32[8,512]{1,0:T(8,128)S(1)} %get-tuple-element.93.plan_ref, bf16[2048,128]{1,0:T(8,128)(2,1)} %get-tuple-element.94.refs_0_, bf16[2048,128]{1,0:T(8,128)(2,1)} %collective-permute-done.refs_1_, bf16[2048,128]{1,0:T(8,128)(2,1)} %collective-permute-done.1.refs_2_, ...), custom_call_target="tpu_custom_call" | custom-call | bytes 4096 | tf_op jit(solution)/shard_map/spmm_first/pallas_call | solution.py:288
  41.1 3.9 %collective-permute-done.5.refs_1_ = bf16[2048,128]{1,0:T(8,128)(2,1)S(1)} collective-permute-done((bf16[2048,128]{1,0:T(8,128)(2,1)}, bf16[2048,128]{1,0:T(8,128)(2,1)S(1)}, u32[]{:S(2)}, u32[]{:S(2)}) %collective-permute-start.5) | collective-permute-done | bytes 524320 | tf_op jit(solution)/shard_map/ppermute | solution.py:329
  47.6 2.7 %collective-permute-start.3 = (bf16[2048,128]{1,0:T(8,128)(2,1)S(1)}, bf16[2048,128]{1,0:T(8,128)(2,1)S(1)}, u32[]{:S(2)}, u32[]{:S(2)}) collective-permute-start(bf16[2048,128]{1,0:T(8,128)(2,1)S(1)} %copy-done.8), channel_id=1, source_target_pairs={{0,2},{1,3},{2,0},{3,1},{4,6},{5,7},{6,4},{7,5},{8,10},{9,11},{10,... | collective-permute-start | bytes 1572872 | tf_op jit(solution)/shard_map/ppermute | solution.py:311
  50.3 2.1 %collective-permute-start.2 = (bf16[2048,128]{1,0:T(8,128)(2,1)S(1)}, bf16[2048,128]{1,0:T(8,128)(2,1)S(1)}, u32[]{:S(2)}, u32[]{:S(2)}) collective-permute-start(bf16[2048,128]{1,0:T(8,128)(2,1)S(1)} %copy-done.8), channel_id=1, source_target_pairs={{0,1},{1,0},{2,3},{3,2},{4,5},{5,4},{6,7},{7,6},{8,9},{9,8},{10,11... | collective-permute-start | bytes 1572872 | tf_op jit(solution)/shard_map/ppermute | solution.py:311
  52.4 4.5 %spmm_last.2 = bf16[2,8192,128]{2,1,0:T(8,128)(2,1)S(1)} custom-call(s32[8,512]{1,0:T(8,128)S(1)} %get-tuple-element.91.plan_ref, bf16[2048,128]{1,0:T(8,128)(2,1)S(1)} %collective-permute-done.4.refs_0_, bf16[2048,128]{1,0:T(8,128)(2,1)S(1)} %collective-permute-done.5.refs_1_, bf16[352,128,128]{2,1,0:T(8,128)(2,1)S(1)} %flip_tiles.1.refs_3_.refs_2_, ...), custom_call_target="tpu_custom_call" | custom-call | bytes 4096 | tf_op jit(solution)/shard_map/spmm_last/pallas_call | solution.py:288
  56.9 7.2 %all_to_all.5 = bf16[2,8192,128]{2,1,0:T(8,128)(2,1)S(1)} all-to-all(bf16[2,8192,128]{2,1,0:T(8,128)(2,1)S(1)} %spmm_last.2), channel_id=1, replica_groups={{0,4},{8,12},{16,20},{24,28},{1,5},{9,13},{17,21},{25,29},{2,6},{10,14}..., dimensions={0} | all-to-all | bytes 8388608 | tf_op jit(solution)/shard_map/all_to_all | solution.py:343
  66.3 3.8 %weight_term.1 = bf16[256,128]{1,0:T(8,128)(2,1)S(1)} custom-call(bf16[2048,256]{1,0:T(8,128)(2,1)S(1)} %copy-done.2, bf16[2048,256]{1,0:T(8,128)(2,1)S(1)} %collective-permute-done.6.refs_1_, bf16[2048,256]{1,0:T(8,128)(2,1)S(1)} %collective-permute-done.7.refs_2_, bf16[1024,256]{1,0:T(8,128)(2,1)S(1)} %collective-permute-done.8.refs_3_, ...), custom_call_target="tpu_custom_call" | custom-call | bytes 4096 | tf_op jit(solution)/shard_map/weight_term/pallas_call | solution.py:448
  70.1 2.0 %collective-permute-done.3.refs_2_ = bf16[2048,128]{1,0:T(8,128)(2,1)S(1)} collective-permute-done((bf16[2048,128]{1,0:T(8,128)(2,1)S(1)}, bf16[2048,128]{1,0:T(8,128)(2,1)S(1)}, u32[]{:S(2)}, u32[]{:S(2)}) %collective-permute-start.3) | collective-permute-done | bytes 524320 | tf_op jit(solution)/shard_map/ppermute | solution.py:311
  74.1 7.9 %spmm_first.3 = (bf16[8192,128]{1,0:T(8,128)(2,1)S(1)}, bf16[8192,128]{1,0:T(8,128)(2,1)S(1)}) custom-call(s32[8,512]{1,0:T(8,128)S(1)} %get-tuple-element.93.plan_ref, bf16[2048,128]{1,0:T(8,128)(2,1)S(1)} %copy-done.8, bf16[2048,128]{1,0:T(8,128)(2,1)S(1)} %collective-permute-done.2.refs_1_, bf16[2048,128]{1,0:T(8,128)(2,1)S(1)} %collective-permute-done.3.refs_2_, ...), custom_call_target="tpu_custom_call" | custom-call | bytes 4096 | tf_op jit(solution)/shard_map/spmm_first/pallas_call | solution.py:288
  84.0 3.1 %collective-permute-done.11.refs_1_ = bf16[2048,128]{1,0:T(8,128)(2,1)S(1)} collective-permute-done((bf16[2048,128]{1,0:T(8,128)(2,1)S(1)}, bf16[2048,128]{1,0:T(8,128)(2,1)S(1)}, u32[]{:S(2)}, u32[]{:S(2)}) %collective-permute-start.11) | collective-permute-done | bytes 524320 | tf_op jit(solution)/shard_map/ppermute | solution.py:329
  87.1 6.0 %spmm_last.3 = (bf16[8192,128]{1,0:T(8,128)(2,1)}, bf16[8192,128]{1,0:T(8,128)(2,1)S(1)}) custom-call(s32[8,512]{1,0:T(8,128)S(1)} %get-tuple-element.91.plan_ref, bf16[2048,128]{1,0:T(8,128)(2,1)S(1)} %collective-permute-done.10.refs_0_, bf16[2048,128]{1,0:T(8,128)(2,1)S(1)} %collective-permute-done.11.refs_1_, ...), custom_call_target="tpu_custom_call" | custom-call | bytes 4096 | tf_op jit(solution)/shard_map/spmm_last/pallas_call | solution.py:288
  93.0 1.4 %copy-done.3 = bf16[8192,128]{1,0:T(8,128)(2,1)} copy-done((bf16[8192,128]{1,0:T(8,128)(2,1)}, bf16[8192,128]{1,0:T(8,128)(2,1)S(1)}, u32[]{:S(2)}) %copy-start.3) | copy-done | bytes 2097176
  94.4 1.3 collective-permute-start.14
  97.2 2.6 %collective-permute-done.14 = bf16[8192,128]{1,0:T(8,128)(2,1)} collective-permute-done((bf16[8192,128]{1,0:T(8,128)(2,1)}, bf16[8192,128]{1,0:T(8,128)(2,1)}, u32[]{:S(2)}, u32[]{:S(2)}) %collective-permute-start.14) | collective-permute-done | bytes 2097184 | tf_op jit(solution)/shard_map/ppermute | solution.py:311
  99.9 2.8 %add_convert_fusion = bf16[8192,128]{1,0:T(8,128)(2,1)S(1)} fusion(bf16[8192,128]{1,0:T(8,128)(2,1)} %collective-permute-done.14, bf16[8192,128]{1,0:T(8,128)(2,1)} %copy-done.3), kind=kLoop, calls=%fused_computation | loop fusion | flops 4194304 | bytes 6291456 | tf_op jit(solution)/shard_map/convert_element_type | solution.py:358
  107.2 4.0 %collective-permute-start.22 = (bf16[256,128]{1,0:T(8,128)(2,1)S(1)}, bf16[256,128]{1,0:T(8,128)(2,1)S(1)}, u32[]{:S(2)}, u32[]{:S(2)}) collective-permute-start(bf16[256,128]{1,0:T(8,128)(2,1)S(1)} %add_convert_fusion.12), channel_id=1, source_target_pairs={{0,3},{1,2},{2,1},{3,0},{4,7},{5,6},{6,5},{7,4},{8,11},{9,10},{10,... | collective-permute-start | bytes 196616 | tf_op jit(solution)/shard_map/ppermute | solution.py:311
  111.6 1.4 %collective-permute-done.22 = bf16[256,128]{1,0:T(8,128)(2,1)S(1)} collective-permute-done((bf16[256,128]{1,0:T(8,128)(2,1)S(1)}, bf16[256,128]{1,0:T(8,128)(2,1)S(1)}, u32[]{:S(2)}, u32[]{:S(2)}) %collective-permute-start.22) | collective-permute-done | bytes 65568 | tf_op jit(solution)/shard_map/ppermute | solution.py:311
  113.0 3.6 %collective-permute-done.21 = bf16[256,128]{1,0:T(8,128)(2,1)S(1)} collective-permute-done((bf16[256,128]{1,0:T(8,128)(2,1)S(1)}, bf16[256,128]{1,0:T(8,128)(2,1)S(1)}, u32[]{:S(2)}, u32[]{:S(2)}) %collective-permute-start.21) | collective-permute-done | bytes 65568 | tf_op jit(solution)/shard_map/ppermute | solution.py:311
  116.7 2.5 %collective-permute-done.17 = bf16[2048,128]{1,0:T(8,128)(2,1)S(1)} collective-permute-done((bf16[2048,128]{1,0:T(8,128)(2,1)S(1)}, bf16[2048,128]{1,0:T(8,128)(2,1)S(1)}, u32[]{:S(2)}, u32[]{:S(2)}) %collective-permute-start.17) | collective-permute-done | bytes 524320 | tf_op jit(solution)/shard_map/ppermute | solution.py:311
  124.1 2.4 %collective-permute-done.23 = bf16[1024,128]{1,0:T(8,128)(2,1)S(1)} collective-permute-done((bf16[1024,128]{1,0:T(8,128)(2,1)S(1)}, bf16[1024,128]{1,0:T(8,128)(2,1)S(1)}, u32[]{:S(2)}, u32[]{:S(2)}) %collective-permute-start.23) | collective-permute-done | bytes 262176 | tf_op jit(solution)/shard_map/ppermute | solution.py:311
  126.9 1.6 %collective-permute-done.27 = bf16[256,128]{1,0:T(8,128)(2,1)S(1)} collective-permute-done((bf16[256,128]{1,0:T(8,128)(2,1)S(1)}, bf16[256,128]{1,0:T(8,128)(2,1)S(1)}, u32[]{:S(2)}, u32[]{:S(2)}) %collective-permute-start.27) | collective-permute-done | bytes 65568 | tf_op jit(solution)/shard_map/ppermute | solution.py:311
  129.6 2.5 %collective-permute-start.28 = (bf16[256,128]{1,0:T(8,128)(2,1)S(1)}, bf16[256,128]{1,0:T(8,128)(2,1)S(1)}, u32[]{:S(2)}, u32[]{:S(2)}) collective-permute-start(bf16[256,128]{1,0:T(8,128)(2,1)S(1)} %add_convert_fusion.10), channel_id=1, source_target_pairs={{0,4},{4,0},{8,12},{12,8},{16,20},{20,16},{24,28},{28,24},{1,5},{5... | collective-permute-start | bytes 196616 | tf_op jit(solution)/shard_map/ppermute | solution.py:311
  132.2 1.4 %convolution_convert_fusion = bf16[2048,256]{1,0:T(8,128)(2,1)} fusion(bf16[256,256]{1,0:T(8,128)(2,1)S(1)} %copy-done, bf16[2048,128]{1,0:T(8,128)(2,1)S(1)} %pad_maximum_fusion.1, bf16[2048,128]{1,0:T(8,128)(2,1)S(1)} %pad_maximum_fusion), kind=kOutput, calls=%fused_computation.2 | convolution fusion | flops 271056896 | bytes 2228224 | tf_op jit(solution)/shard_map/dot_general | solution.py:543
  (97 shorter events, 24.6 us)
Async XLA Ops:
  0.6 131.5 %copy-start = (bf16[256,256]{1,0:T(8,128)(2,1)S(1)}, bf16[256,256]{1,0:T(8,128)(2,1)}, u32[]{:S(2)}) copy-start(bf16[256,256]{1,0:T(8,128)(2,1)} %param.11) | copy-start | bytes 393220
  0.7 8.0 %copy-start.9 = (s32[1,1,320]{2,1,0:T(1,128)S(1)}, s32[1,1,320]{2,1,0:T(1,128)}, u32[]{:S(2)}) copy-start(s32[1,1,320]{2,1,0:T(1,128)} %param.13) | copy-start | bytes 3844
  0.7 10.5 %copy-start.2 = (bf16[2048,256]{1,0:T(8,128)(2,1)S(1)}, bf16[2048,256]{1,0:T(8,128)(2,1)}, u32[]{:S(2)}) copy-start(bf16[2048,256]{1,0:T(8,128)(2,1)} %refs_0_) | copy-start | bytes 3145732
  3.4 26.4 %collective-permute-start.1 = (bf16[2048,128]{1,0:T(8,128)(2,1)}, bf16[2048,128]{1,0:T(8,128)(2,1)}, u32[]{:S(2)}, u32[]{:S(2)}) collective-permute-start(bf16[2048,128]{1,0:T(8,128)(2,1)} %get-tuple-element.94.refs_0_), channel_id=1, source_target_pairs={{0,2},{1,3},{2,0},{3,1},{4,6},{5,7},{6,4},{7,5},{8,10},{9,11},{10,... | collective-permute-start | bytes 1572872 | tf_op jit(solution)/shard_map/ppermute | solution.py:311
  6.5 23.2 %collective-permute-start = (bf16[2048,128]{1,0:T(8,128)(2,1)}, bf16[2048,128]{1,0:T(8,128)(2,1)}, u32[]{:S(2)}, u32[]{:S(2)}) collective-permute-start(bf16[2048,128]{1,0:T(8,128)(2,1)} %get-tuple-element.94.refs_0_), channel_id=1, source_target_pairs={{0,1},{1,0},{2,3},{3,2},{4,5},{5,4},{6,7},{7,6},{8,9},{9,8},{10,11... | collective-permute-start | bytes 1572872 | tf_op jit(solution)/shard_map/ppermute | solution.py:311
  11.2 29.8 %collective-permute-start.7 = (bf16[2048,256]{1,0:T(8,128)(2,1)S(1)}, bf16[2048,256]{1,0:T(8,128)(2,1)S(1)}, u32[]{:S(2)}, u32[]{:S(2)}) collective-permute-start(bf16[2048,256]{1,0:T(8,128)(2,1)S(1)} %copy-done.2), channel_id=1, source_target_pairs={{0,16},{4,20},{8,24},{12,28},{16,0},{20,4},{24,8},{28,12},{1,17},{... | collective-permute-start | bytes 3145736 | tf_op jit(solution)/shard_map/ppermute | solution.py:311
  12.5 28.5 %collective-permute-start.6 = (bf16[2048,256]{1,0:T(8,128)(2,1)S(1)}, bf16[2048,256]{1,0:T(8,128)(2,1)S(1)}, u32[]{:S(2)}, u32[]{:S(2)}) collective-permute-start(bf16[2048,256]{1,0:T(8,128)(2,1)S(1)} %copy-done.2), channel_id=1, source_target_pairs={{0,8},{4,12},{8,0},{12,4},{16,24},{20,28},{24,16},{28,20},{1,9},{5... | collective-permute-start | bytes 3145736 | tf_op jit(solution)/shard_map/ppermute | solution.py:311
  29.8 11.3 %collective-permute-start.4 = (bf16[2048,128]{1,0:T(8,128)(2,1)}, bf16[2048,128]{1,0:T(8,128)(2,1)S(1)}, u32[]{:S(2)}, u32[]{:S(2)}) collective-permute-start(bf16[2048,128]{1,0:T(8,128)(2,1)} %get-tuple-element.94.refs_0_), channel_id=1, source_target_pairs={{1,2},{2,1},{5,6},{6,5},{9,10},{10,9},{13,14},{14,13},{17,18},{18,... | collective-permute-start | bytes 1572872 | tf_op jit(solution)/shard_map/ppermute | solution.py:329
  30.5 14.5 %collective-permute-start.5 = (bf16[2048,128]{1,0:T(8,128)(2,1)}, bf16[2048,128]{1,0:T(8,128)(2,1)S(1)}, u32[]{:S(2)}, u32[]{:S(2)}) collective-permute-start(bf16[2048,128]{1,0:T(8,128)(2,1)} %collective-permute-done.1.refs_2_), channel_id=1, source_target_pairs={{1,0},{2,3},{5,4},{6,7},{9,8},{10,11},{13,12},{14,15},{17,16},{18,... | collective-permute-start | bytes 1572872 | tf_op jit(solution)/shard_map/ppermute | solution.py:329
  45.0 19.0 %collective-permute-start.9 = (bf16[1024,256]{1,0:T(8,128)(2,1)S(1)}, bf16[1024,256]{1,0:T(8,128)(2,1)S(1)}, u32[]{:S(2)}, u32[]{:S(2)}) collective-permute-start(bf16[1024,256]{1,0:T(8,128)(2,1)S(1)} %slice.96), channel_id=1, source_target_pairs={{0,8},{4,12},{8,0},{12,4},{16,24},{20,28},{24,16},{28,20},{1,9},{5... | collective-permute-start | bytes 1572872 | tf_op jit(solution)/shard_map/ppermute | solution.py:311
  46.3 17.7 %collective-permute-start.8 = (bf16[1024,256]{1,0:T(8,128)(2,1)S(1)}, bf16[1024,256]{1,0:T(8,128)(2,1)S(1)}, u32[]{:S(2)}, u32[]{:S(2)}) collective-permute-start(bf16[1024,256]{1,0:T(8,128)(2,1)S(1)} %slice.95), channel_id=1, source_target_pairs={{0,16},{4,20},{8,24},{12,28},{16,0},{20,4},{24,8},{28,12},{1,17},{... | collective-permute-start | bytes 1572872 | tf_op jit(solution)/shard_map/ppermute | solution.py:311
  47.6 24.5 %collective-permute-start.3 = (bf16[2048,128]{1,0:T(8,128)(2,1)S(1)}, bf16[2048,128]{1,0:T(8,128)(2,1)S(1)}, u32[]{:S(2)}, u32[]{:S(2)}) collective-permute-start(bf16[2048,128]{1,0:T(8,128)(2,1)S(1)} %copy-done.8), channel_id=1, source_target_pairs={{0,2},{1,3},{2,0},{3,1},{4,6},{5,7},{6,4},{7,5},{8,10},{9,11},{10,... | collective-permute-start | bytes 1572872 | tf_op jit(solution)/shard_map/ppermute | solution.py:311
  50.3 21.8 %collective-permute-start.2 = (bf16[2048,128]{1,0:T(8,128)(2,1)S(1)}, bf16[2048,128]{1,0:T(8,128)(2,1)S(1)}, u32[]{:S(2)}, u32[]{:S(2)}) collective-permute-start(bf16[2048,128]{1,0:T(8,128)(2,1)S(1)} %copy-done.8), channel_id=1, source_target_pairs={{0,1},{1,0},{2,3},{3,2},{4,5},{5,4},{6,7},{7,6},{8,9},{9,8},{10,11... | collective-permute-start | bytes 1572872 | tf_op jit(solution)/shard_map/ppermute | solution.py:311
  64.8 17.2 %collective-permute-start.12 = (bf16[2048,128]{1,0:T(8,128)(2,1)S(1)}, bf16[2048,128]{1,0:T(8,128)(2,1)S(1)}, u32[]{:S(2)}, u32[]{:S(2)}) collective-permute-start(bf16[2048,128]{1,0:T(8,128)(2,1)S(1)} %bitcast.56), channel_id=1, source_target_pairs={{0,8},{4,12},{8,0},{12,4},{16,24},{20,28},{24,16},{28,20},{1,9},{5... | collective-permute-start | bytes 1572872 | tf_op jit(solution)/shard_map/ppermute | solution.py:311
  65.4 16.6 %collective-permute-start.13 = (bf16[2048,128]{1,0:T(8,128)(2,1)S(1)}, bf16[2048,128]{1,0:T(8,128)(2,1)S(1)}, u32[]{:S(2)}, u32[]{:S(2)}) collective-permute-start(bf16[2048,128]{1,0:T(8,128)(2,1)S(1)} %bitcast.55), channel_id=1, source_target_pairs={{0,16},{4,20},{8,24},{12,28},{16,0},{20,4},{24,8},{28,12},{1,17},{... | collective-permute-start | bytes 1572872 | tf_op jit(solution)/shard_map/ppermute | solution.py:311
  72.1 11.9 %collective-permute-start.10 = (bf16[2048,128]{1,0:T(8,128)(2,1)S(1)}, bf16[2048,128]{1,0:T(8,128)(2,1)S(1)}, u32[]{:S(2)}, u32[]{:S(2)}) collective-permute-start(bf16[2048,128]{1,0:T(8,128)(2,1)S(1)} %copy-done.8), channel_id=1, source_target_pairs={{1,2},{2,1},{5,6},{6,5},{9,10},{10,9},{13,14},{14,13},{17,18},{18,... | collective-permute-start | bytes 1572872 | tf_op jit(solution)/shard_map/ppermute | solution.py:329
  72.8 14.3 %collective-permute-start.11 = (bf16[2048,128]{1,0:T(8,128)(2,1)S(1)}, bf16[2048,128]{1,0:T(8,128)(2,1)S(1)}, u32[]{:S(2)}, u32[]{:S(2)}) collective-permute-start(bf16[2048,128]{1,0:T(8,128)(2,1)S(1)} %collective-permute-done.3.refs_2_), channel_id=1, source_target_pairs={{1,0},{2,3},{5,4},{6,7},{9,8},{10,11},{13,12},{14,15},{17,16},{18,... | collective-permute-start | bytes 1572872 | tf_op jit(solution)/shard_map/ppermute | solution.py:329
  94.4 5.5 %collective-permute-start.14 = (bf16[8192,128]{1,0:T(8,128)(2,1)}, bf16[8192,128]{1,0:T(8,128)(2,1)}, u32[]{:S(2)}, u32[]{:S(2)}) collective-permute-start(bf16[8192,128]{1,0:T(8,128)(2,1)} %get-tuple-element.139), channel_id=1, source_target_pairs={{0,4},{4,0},{8,12},{12,8},{16,20},{20,16},{24,28},{28,24},{1,5},{5... | collective-permute-start | bytes 6291464 | tf_op jit(solution)/shard_map/ppermute | solution.py:311
  95.7 9.3 %collective-permute-start.15 = (bf16[1024,128]{1,0:T(8,128)(2,1)}, bf16[1024,128]{1,0:T(8,128)(2,1)S(1)}, u32[]{:S(2)}, u32[]{:S(2)}) collective-permute-start(bf16[1024,128]{1,0:T(8,128)(2,1)} %get-tuple-element.149), channel_id=1, source_target_pairs={{0,16},{4,20},{8,24},{12,28},{16,0},{20,4},{24,8},{28,12},{1,17},{... | collective-permute-start | bytes 786440 | tf_op jit(solution)/shard_map/ppermute | solution.py:311
  96.7 8.4 %collective-permute-start.16 = (bf16[1024,128]{1,0:T(8,128)(2,1)}, bf16[1024,128]{1,0:T(8,128)(2,1)S(1)}, u32[]{:S(2)}, u32[]{:S(2)}) collective-permute-start(bf16[1024,128]{1,0:T(8,128)(2,1)} %get-tuple-element.150), channel_id=1, source_target_pairs={{0,8},{4,12},{8,0},{12,4},{16,24},{20,28},{24,16},{28,20},{1,9},{5... | collective-permute-start | bytes 786440 | tf_op jit(solution)/shard_map/ppermute | solution.py:311
  105.1 2.1 %collective-permute-start.19 = (bf16[256,128]{1,0:T(8,128)(2,1)S(1)}, bf16[256,128]{1,0:T(8,128)(2,1)S(1)}, u32[]{:S(2)}, u32[]{:S(2)}) collective-permute-start(bf16[256,128]{1,0:T(8,128)(2,1)S(1)} %broadcast_select_fusion.2), channel_id=1, source_target_pairs={{0,4},{4,0},{8,12},{12,8},{16,20},{20,16},{24,28},{28,24},{1,5},{5... | collective-permute-start | bytes 196616 | tf_op jit(solution)/shard_map/ppermute | solution.py:311
  105.7 13.5 %collective-permute-start.17 = (bf16[2048,128]{1,0:T(8,128)(2,1)S(1)}, bf16[2048,128]{1,0:T(8,128)(2,1)S(1)}, u32[]{:S(2)}, u32[]{:S(2)}) collective-permute-start(bf16[2048,128]{1,0:T(8,128)(2,1)S(1)} %bitcast.53), channel_id=1, source_target_pairs={{0,8},{4,12},{8,0},{12,4},{16,24},{20,28},{24,16},{28,20},{1,9},{5... | collective-permute-start | bytes 1572872 | tf_op jit(solution)/shard_map/ppermute | solution.py:311
  106.3 13.2 %collective-permute-start.18 = (bf16[2048,128]{1,0:T(8,128)(2,1)S(1)}, bf16[2048,128]{1,0:T(8,128)(2,1)S(1)}, u32[]{:S(2)}, u32[]{:S(2)}) collective-permute-start(bf16[2048,128]{1,0:T(8,128)(2,1)S(1)} %bitcast.54), channel_id=1, source_target_pairs={{0,16},{4,20},{8,24},{12,28},{16,0},{20,4},{24,8},{28,12},{1,17},{... | collective-permute-start | bytes 1572872 | tf_op jit(solution)/shard_map/ppermute | solution.py:311
  107.2 5.7 %collective-permute-start.22 = (bf16[256,128]{1,0:T(8,128)(2,1)S(1)}, bf16[256,128]{1,0:T(8,128)(2,1)S(1)}, u32[]{:S(2)}, u32[]{:S(2)}) collective-permute-start(bf16[256,128]{1,0:T(8,128)(2,1)S(1)} %add_convert_fusion.12), channel_id=1, source_target_pairs={{0,3},{1,2},{2,1},{3,0},{4,7},{5,6},{6,5},{7,4},{8,11},{9,10},{10,... | collective-permute-start | bytes 196616 | tf_op jit(solution)/shard_map/ppermute | solution.py:311
  111.2 5.4 %collective-permute-start.21 = (bf16[256,128]{1,0:T(8,128)(2,1)S(1)}, bf16[256,128]{1,0:T(8,128)(2,1)S(1)}, u32[]{:S(2)}, u32[]{:S(2)}) collective-permute-start(bf16[256,128]{1,0:T(8,128)(2,1)S(1)} %add_convert_fusion.12), channel_id=1, source_target_pairs={{0,2},{1,3},{2,0},{3,1},{4,6},{5,7},{6,4},{7,5},{8,10},{9,11},{10,... | collective-permute-start | bytes 196616 | tf_op jit(solution)/shard_map/ppermute | solution.py:311
  111.2 5.4 %collective-permute-start.20 = (bf16[256,128]{1,0:T(8,128)(2,1)S(1)}, bf16[256,128]{1,0:T(8,128)(2,1)S(1)}, u32[]{:S(2)}, u32[]{:S(2)}) collective-permute-start(bf16[256,128]{1,0:T(8,128)(2,1)S(1)} %add_convert_fusion.12), channel_id=1, source_target_pairs={{0,1},{1,0},{2,3},{3,2},{4,5},{5,4},{6,7},{7,6},{8,9},{9,8},{10,11... | collective-permute-start | bytes 196616 | tf_op jit(solution)/shard_map/ppermute | solution.py:311
  119.8 6.7 %collective-permute-start.23 = (bf16[1024,128]{1,0:T(8,128)(2,1)S(1)}, bf16[1024,128]{1,0:T(8,128)(2,1)S(1)}, u32[]{:S(2)}, u32[]{:S(2)}) collective-permute-start(bf16[1024,128]{1,0:T(8,128)(2,1)S(1)} %get-tuple-element.166), channel_id=1, source_target_pairs={{0,16},{4,20},{8,24},{12,28},{16,0},{20,4},{24,8},{28,12},{1,17},{... | collective-permute-start | bytes 786440 | tf_op jit(solution)/shard_map/ppermute | solution.py:311
  120.5 6.2 %collective-permute-start.24 = (bf16[1024,128]{1,0:T(8,128)(2,1)S(1)}, bf16[1024,128]{1,0:T(8,128)(2,1)S(1)}, u32[]{:S(2)}, u32[]{:S(2)}) collective-permute-start(bf16[1024,128]{1,0:T(8,128)(2,1)S(1)} %get-tuple-element.168), channel_id=1, source_target_pairs={{0,8},{4,12},{8,0},{12,4},{16,24},{20,28},{24,16},{28,20},{1,9},{5... | collective-permute-start | bytes 786440 | tf_op jit(solution)/shard_map/ppermute | solution.py:311
  121.4 7.1 %collective-permute-start.27 = (bf16[256,128]{1,0:T(8,128)(2,1)S(1)}, bf16[256,128]{1,0:T(8,128)(2,1)S(1)}, u32[]{:S(2)}, u32[]{:S(2)}) collective-permute-start(bf16[256,128]{1,0:T(8,128)(2,1)S(1)} %add_convert_fusion.11), channel_id=1, source_target_pairs={{0,24},{4,28},{8,16},{12,20},{16,8},{20,12},{24,0},{28,4},{1,25},{... | collective-permute-start | bytes 196616 | tf_op jit(solution)/shard_map/ppermute | solution.py:311
  122.5 6.0 %collective-permute-start.26 = (bf16[256,128]{1,0:T(8,128)(2,1)S(1)}, bf16[256,128]{1,0:T(8,128)(2,1)S(1)}, u32[]{:S(2)}, u32[]{:S(2)}) collective-permute-start(bf16[256,128]{1,0:T(8,128)(2,1)S(1)} %add_convert_fusion.11), channel_id=1, source_target_pairs={{0,16},{4,20},{8,24},{12,28},{16,0},{20,4},{24,8},{28,12},{1,17},{... | collective-permute-start | bytes 196616 | tf_op jit(solution)/shard_map/ppermute | solution.py:311
  123.2 6.4 %collective-permute-start.25 = (bf16[256,128]{1,0:T(8,128)(2,1)S(1)}, bf16[256,128]{1,0:T(8,128)(2,1)S(1)}, u32[]{:S(2)}, u32[]{:S(2)}) collective-permute-start(bf16[256,128]{1,0:T(8,128)(2,1)S(1)} %add_convert_fusion.11), channel_id=1, source_target_pairs={{0,8},{4,12},{8,0},{12,4},{16,24},{20,28},{24,16},{28,20},{1,9},{5... | collective-permute-start | bytes 196616 | tf_op jit(solution)/shard_map/ppermute | solution.py:311
  129.6 4.0 %collective-permute-start.28 = (bf16[256,128]{1,0:T(8,128)(2,1)S(1)}, bf16[256,128]{1,0:T(8,128)(2,1)S(1)}, u32[]{:S(2)}, u32[]{:S(2)}) collective-permute-start(bf16[256,128]{1,0:T(8,128)(2,1)S(1)} %add_convert_fusion.10), channel_id=1, source_target_pairs={{0,4},{4,0},{8,12},{12,8},{16,20},{20,16},{24,28},{28,24},{1,5},{5... | collective-permute-start | bytes 196616 | tf_op jit(solution)/shard_map/ppermute | solution.py:311
  (10 other events, 31.9 us)

commit v14 on v13

--- a/solution.py
+++ b/solution.py
@@ -13,11 +13,11 @@
 RING = 4
 FIRST_PIECES = 3
 PLAN_ROWS = 8
-FLIP_BYTES = 26 * 1024 * 1024
+FLIP_BYTES = 50 * 1024 * 1024
 PLAN_BYTES = 12 * 1024 * 1024
 TERM_BYTES = 14 * 1024 * 1024
 TERM_ROWS = 512
-SPMM_BYTES = 16 * 1024 * 1024
+SPMM_BYTES = 40 * 1024 * 1024
 
 
 def round_up(value, unit):

time: 136 us -> 136 us (level); the launches traced: 134 us -> 136 us
  waiting for transfers between devices: 27.2 us -> 32.2 us
  local copies, waits for them, and re-layouts: 7.84 us -> 3.81 us
  blocking collectives: 7.15 us -> 9.8 us
  Pallas kernels: 43.3 us -> 41.4 us
    pallas_call x4, Pallas kernels: 27.6 us -> 21.7 us  [spmm(): pl.pallas_call(functools.partial(spmm_kernel, [len(p) for p in pieces], l...]
    ppermute x2, waiting for transfers between devices: 6.97 us -> 11.2 us  [gather_second(): lax.ppermute(by_two, 'col', ends)]
    unnamed x26 -> x24, local copies, waits for them, and re-layouts: 5.44 us -> 1.46 us
    pallas_call x1, Pallas kernels: 9.59 us -> 13.6 us  [flip_tiles(): pl.pallas_call(flip_kernel, out_shape=jax.ShapeDtypeStruct((slots + GROUP...]
    all_to_all x1, blocking collectives: 7.15 us -> 9.8 us  [swap_cores(): return lax.all_to_all(both, 'row', 0, 0, axis_index_groups=pairs)]
  transfers between devices with their start and end apart: 29 -> 29, of which waited for: 13 -> 12; matrix products, arithmetic and copies ran while one was open for 7% -> 7% of each run, Pallas kernels for 28% -> 27%
where the time goes in v14:
time: 136 us
  Pallas kernels  41.4 us (30%)
  starting transfers between devices  35.5 us (26%)
  waiting for transfers between devices  32.2 us (24%)
  blocking collectives  9.8 us (7%)
  other arithmetic  7.86 us (6%)
  local copies, waits for them, and re-layouts  3.81 us (3%)
  matrix products  3.55 us (3%)
  between operations  1.76 us (1%)
    ppermute x25, starting transfers between devices, xor_permute(): return lax.ppermute(value, axis, [(i, i ^ mask) for i in range(size)])  31.5 us
    pallas_call x4, Pallas kernels, spmm(): pl.pallas_call(functools.partial(spmm_kernel, [len(p) for p in pieces], l...  21.7 us
    ppermute x25, waiting for transfers between devices, xor_permute(): return lax.ppermute(value, axis, [(i, i ^ mask) for i in range(size)])  21 us
    pallas_call x1, Pallas kernels, flip_tiles(): pl.pallas_call(flip_kernel, out_shape=jax.ShapeDtypeStruct((slots + GROUP...  13.6 us
    ppermute x2, waiting for transfers between devices, gather_second(): lax.ppermute(by_two, 'col', ends)  11.2 us
    all_to_all x1, blocking collectives, swap_cores(): return lax.all_to_all(both, 'row', 0, 0, axis_index_groups=pairs)  9.8 us
    pallas_call x1, Pallas kernels, weight_term_early(): pl.pallas_call(term_kernel, out_shape=jax.ShapeDtypeStruct(shape, jnp.bfl...  3.8 us
    convert_element_type x2, other arithmetic, stage_sums(): sums = add_f32(keep, recv).astype(jnp.bfloat16)  3.31 us
  transfers between devices with their start and end apart: 29, of which 12 were waited for; matrix products, arithmetic and copies ran while one was open for 7% of the time, Pallas kernels for 27%

profile of v14, /device:TPU:1, one launch (start us, length us, event | category | flops | bytes accessed | tf_op | source)
XLA Modules:
  0.0 135.8 jit_solution(5031192427638446252)
XLA Ops:
  0.7 2.7 %compare_select_fusion = (bf16[2048,128]{1,0:T(8,128)(2,1)}, bf16[2048,128]{1,0:T(8,128)(2,1)}) fusion(bf16[2048,256]{1,0:T(8,128)(2,1)} %param.8, bf16[2048,256]{1,0:T(8,128)(2,1)} %param.9), kind=kLoop, calls=%fused_computation.16 | loop fusion | flops 1048576 | bytes 3145728 | tf_op jit(solution)/shard_map/jit(_where)/select_n | solution.py:476
  3.4 3.1 %collective-permute-start.1 = (bf16[2048,128]{1,0:T(8,128)(2,1)}, bf16[2048,128]{1,0:T(8,128)(2,1)}, u32[]{:S(2)}, u32[]{:S(2)}) collective-permute-start(bf16[2048,128]{1,0:T(8,128)(2,1)} %get-tuple-element.94.refs_0_), channel_id=1, source_target_pairs={{0,2},{1,3},{2,0},{3,1},{4,6},{5,7},{6,4},{7,5},{8,10},{9,11},{10,... | collective-permute-start | bytes 1572872 | tf_op jit(solution)/shard_map/ppermute | solution.py:311
  6.5 1.3 collective-permute-start
  8.9 2.3 %plan_slots.1 = (s32[8,512]{1,0:T(8,128)S(1)}, s32[8,512]{1,0:T(8,128)S(1)}, s32[1,320]{1,0:T(1,128)S(1)}) custom-call(s32[4]{0:T(128)S(1)} %pad_add_fusion.place_ref, s32[1,320]{1,0:T(1,128)S(1)} %bitcast.41, s32[1,320]{1,0:T(1,128)S(1)} %bitcast.43, s32[320,1]{1,0:T(8,128)S(1)} %copy.10.rows_c, s32[320,1]{1,0:T(8,128)S(1)} %copy.11.cols_c), custom_call_target="tpu_custom_call" | custom-call | bytes 4096 | tf_op jit(solution)/shard_map/plan_slots/pallas_call | solution.py:122
  11.2 1.3 collective-permute-start.7
  13.7 13.6 %flip_tiles.1.refs_3_.refs_2_ = bf16[352,128,128]{2,1,0:T(8,128)(2,1)} custom-call(s32[1,320]{1,0:T(1,128)S(1)} %get-tuple-element.90.slot_ref, bf16[320,128,128]{2,1,0:T(8,128)(2,1)} %bitcast.46), custom_call_target="tpu_custom_call" | custom-call | bytes 4096 | tf_op jit(solution)/shard_map/flip_tiles/pallas_call | solution.py:165
  27.3 2.5 %collective-permute-done.1.refs_2_ = bf16[2048,128]{1,0:T(8,128)(2,1)} collective-permute-done((bf16[2048,128]{1,0:T(8,128)(2,1)}, bf16[2048,128]{1,0:T(8,128)(2,1)}, u32[]{:S(2)}, u32[]{:S(2)}) %collective-permute-start.1) | collective-permute-done | bytes 524320 | tf_op jit(solution)/shard_map/ppermute | solution.py:311
  30.5 1.3 collective-permute-start.5
  31.8 7.2 %spmm_first.2 = (bf16[8192,128]{1,0:T(8,128)(2,1)S(1)}, bf16[8192,128]{1,0:T(8,128)(2,1)S(1)}) custom-call(s32[8,512]{1,0:T(8,128)S(1)} %get-tuple-element.93.plan_ref, bf16[2048,128]{1,0:T(8,128)(2,1)} %get-tuple-element.94.refs_0_, bf16[2048,128]{1,0:T(8,128)(2,1)} %collective-permute-done.refs_1_, bf16[2048,128]{1,0:T(8,128)(2,1)} %collective-permute-done.1.refs_2_, ...), custom_call_target="tpu_custom_call" | custom-call | bytes 4096 | tf_op jit(solution)/shard_map/spmm_first/pallas_call | solution.py:288
  39.0 6.0 %collective-permute-done.5.refs_1_ = bf16[2048,128]{1,0:T(8,128)(2,1)S(1)} collective-permute-done((bf16[2048,128]{1,0:T(8,128)(2,1)}, bf16[2048,128]{1,0:T(8,128)(2,1)S(1)}, u32[]{:S(2)}, u32[]{:S(2)}) %collective-permute-start.5) | collective-permute-done | bytes 524320 | tf_op jit(solution)/shard_map/ppermute | solution.py:329
  45.1 1.3 collective-permute-start.9
  47.6 2.7 %collective-permute-start.3 = (bf16[2048,128]{1,0:T(8,128)(2,1)S(1)}, bf16[2048,128]{1,0:T(8,128)(2,1)S(1)}, u32[]{:S(2)}, u32[]{:S(2)}) collective-permute-start(bf16[2048,128]{1,0:T(8,128)(2,1)S(1)} %copy-done.7), channel_id=1, source_target_pairs={{0,2},{1,3},{2,0},{3,1},{4,6},{5,7},{6,4},{7,5},{8,10},{9,11},{10,... | collective-permute-start | bytes 1572872 | tf_op jit(solution)/shard_map/ppermute | solution.py:311
  50.3 2.1 %collective-permute-start.2 = (bf16[2048,128]{1,0:T(8,128)(2,1)S(1)}, bf16[2048,128]{1,0:T(8,128)(2,1)S(1)}, u32[]{:S(2)}, u32[]{:S(2)}) collective-permute-start(bf16[2048,128]{1,0:T(8,128)(2,1)S(1)} %copy-done.7), channel_id=1, source_target_pairs={{0,1},{1,0},{2,3},{3,2},{4,5},{5,4},{6,7},{7,6},{8,9},{9,8},{10,11... | collective-permute-start | bytes 1572872 | tf_op jit(solution)/shard_map/ppermute | solution.py:311
  52.4 3.6 %spmm_last.2 = bf16[2,8192,128]{2,1,0:T(8,128)(2,1)S(1)} custom-call(s32[8,512]{1,0:T(8,128)S(1)} %get-tuple-element.91.plan_ref, bf16[2048,128]{1,0:T(8,128)(2,1)S(1)} %collective-permute-done.4.refs_0_, bf16[2048,128]{1,0:T(8,128)(2,1)S(1)} %collective-permute-done.5.refs_1_, bf16[352,128,128]{2,1,0:T(8,128)(2,1)} %flip_tiles.1.refs_3_.refs_2_, ...), custom_call_target="tpu_custom_call" | custom-call | bytes 4096 | tf_op jit(solution)/shard_map/spmm_last/pallas_call | solution.py:288
  56.0 9.8 %all_to_all.5 = bf16[2,8192,128]{2,1,0:T(8,128)(2,1)S(1)} all-to-all(bf16[2,8192,128]{2,1,0:T(8,128)(2,1)S(1)} %spmm_last.2), channel_id=1, replica_groups={{0,4},{8,12},{16,20},{24,28},{1,5},{9,13},{17,21},{25,29},{2,6},{10,14}..., dimensions={0} | all-to-all | bytes 8388608 | tf_op jit(solution)/shard_map/all_to_all | solution.py:343
  67.3 3.8 %weight_term.1 = bf16[256,128]{1,0:T(8,128)(2,1)S(1)} custom-call(bf16[2048,256]{1,0:T(8,128)(2,1)S(1)} %copy-done.1, bf16[2048,256]{1,0:T(8,128)(2,1)S(1)} %collective-permute-done.6.refs_1_, bf16[2048,256]{1,0:T(8,128)(2,1)S(1)} %collective-permute-done.7.refs_2_, bf16[1024,256]{1,0:T(8,128)(2,1)S(1)} %collective-permute-done.8.refs_3_, ...), custom_call_target="tpu_custom_call" | custom-call | bytes 4096 | tf_op jit(solution)/shard_map/weight_term/pallas_call | solution.py:448
  72.8 1.3 collective-permute-start.11
  74.1 5.8 %spmm_first.3 = (bf16[8192,128]{1,0:T(8,128)(2,1)S(1)}, bf16[8192,128]{1,0:T(8,128)(2,1)S(1)}) custom-call(s32[8,512]{1,0:T(8,128)S(1)} %get-tuple-element.93.plan_ref, bf16[2048,128]{1,0:T(8,128)(2,1)S(1)} %copy-done.7, bf16[2048,128]{1,0:T(8,128)(2,1)S(1)} %collective-permute-done.2.refs_1_, bf16[2048,128]{1,0:T(8,128)(2,1)S(1)} %collective-permute-done.3.refs_2_, ...), custom_call_target="tpu_custom_call" | custom-call | bytes 4096 | tf_op jit(solution)/shard_map/spmm_first/pallas_call | solution.py:288
  81.8 5.2 %collective-permute-done.11.refs_1_ = bf16[2048,128]{1,0:T(8,128)(2,1)S(1)} collective-permute-done((bf16[2048,128]{1,0:T(8,128)(2,1)S(1)}, bf16[2048,128]{1,0:T(8,128)(2,1)S(1)}, u32[]{:S(2)}, u32[]{:S(2)}) %collective-permute-start.11) | collective-permute-done | bytes 524320 | tf_op jit(solution)/shard_map/ppermute | solution.py:329
  87.1 5.2 %spmm_last.3 = (bf16[8192,128]{1,0:T(8,128)(2,1)}, bf16[8192,128]{1,0:T(8,128)(2,1)S(1)}) custom-call(s32[8,512]{1,0:T(8,128)S(1)} %get-tuple-element.91.plan_ref, bf16[2048,128]{1,0:T(8,128)(2,1)S(1)} %collective-permute-done.10.refs_0_, bf16[2048,128]{1,0:T(8,128)(2,1)S(1)} %collective-permute-done.11.refs_1_, ...), custom_call_target="tpu_custom_call" | custom-call | bytes 4096 | tf_op jit(solution)/shard_map/spmm_last/pallas_call | solution.py:288
  92.2 1.3 copy-done.2
  93.6 4.0 %collective-permute-start.14 = (bf16[8192,128]{1,0:T(8,128)(2,1)}, bf16[8192,128]{1,0:T(8,128)(2,1)}, u32[]{:S(2)}, u32[]{:S(2)}) collective-permute-start(bf16[8192,128]{1,0:T(8,128)(2,1)} %get-tuple-element.139), channel_id=1, source_target_pairs={{0,4},{4,0},{8,12},{12,8},{16,20},{20,16},{24,28},{28,24},{1,5},{5... | collective-permute-start | bytes 6291464 | tf_op jit(solution)/shard_map/ppermute | solution.py:311
  98.1 3.6 %collective-permute-done.14 = bf16[8192,128]{1,0:T(8,128)(2,1)} collective-permute-done((bf16[8192,128]{1,0:T(8,128)(2,1)}, bf16[8192,128]{1,0:T(8,128)(2,1)}, u32[]{:S(2)}, u32[]{:S(2)}) %collective-permute-start.14) | collective-permute-done | bytes 2097184 | tf_op jit(solution)/shard_map/ppermute | solution.py:311
  101.7 2.8 %add_convert_fusion = bf16[8192,128]{1,0:T(8,128)(2,1)S(1)} fusion(bf16[8192,128]{1,0:T(8,128)(2,1)} %collective-permute-done.14, bf16[8192,128]{1,0:T(8,128)(2,1)} %copy-done.2), kind=kLoop, calls=%fused_computation | loop fusion | flops 4194304 | bytes 6291456 | tf_op jit(solution)/shard_map/convert_element_type | solution.py:358
  108.3 3.7 %collective-permute-start.22 = (bf16[256,128]{1,0:T(8,128)(2,1)S(1)}, bf16[256,128]{1,0:T(8,128)(2,1)S(1)}, u32[]{:S(2)}, u32[]{:S(2)}) collective-permute-start(bf16[256,128]{1,0:T(8,128)(2,1)S(1)} %add_convert_fusion.12), channel_id=1, source_target_pairs={{0,3},{1,2},{2,1},{3,0},{4,7},{5,6},{6,5},{7,4},{8,11},{9,10},{10,... | collective-permute-start | bytes 196616 | tf_op jit(solution)/shard_map/ppermute | solution.py:311
  113.6 2.9 %collective-permute-done.21 = bf16[256,128]{1,0:T(8,128)(2,1)S(1)} collective-permute-done((bf16[256,128]{1,0:T(8,128)(2,1)S(1)}, bf16[256,128]{1,0:T(8,128)(2,1)S(1)}, u32[]{:S(2)}, u32[]{:S(2)}) %collective-permute-start.21) | collective-permute-done | bytes 65568 | tf_op jit(solution)/shard_map/ppermute | solution.py:311
  116.5 4.2 %collective-permute-done.17 = bf16[2048,128]{1,0:T(8,128)(2,1)S(1)} collective-permute-done((bf16[2048,128]{1,0:T(8,128)(2,1)S(1)}, bf16[2048,128]{1,0:T(8,128)(2,1)S(1)}, u32[]{:S(2)}, u32[]{:S(2)}) %collective-permute-start.17) | collective-permute-done | bytes 524320 | tf_op jit(solution)/shard_map/ppermute | solution.py:311
  125.8 2.3 %collective-permute-done.23 = bf16[1024,128]{1,0:T(8,128)(2,1)S(1)} collective-permute-done((bf16[1024,128]{1,0:T(8,128)(2,1)S(1)}, bf16[1024,128]{1,0:T(8,128)(2,1)S(1)}, u32[]{:S(2)}, u32[]{:S(2)}) %collective-permute-start.23) | collective-permute-done | bytes 262176 | tf_op jit(solution)/shard_map/ppermute | solution.py:311
  128.8 1.3 collective-permute-done.27
  130.1 1.4 %collective-permute-done.25 = bf16[256,128]{1,0:T(8,128)(2,1)S(1)} collective-permute-done((bf16[256,128]{1,0:T(8,128)(2,1)S(1)}, bf16[256,128]{1,0:T(8,128)(2,1)S(1)}, u32[]{:S(2)}, u32[]{:S(2)}) %collective-permute-start.25) | collective-permute-done | bytes 65568 | tf_op jit(solution)/shard_map/ppermute | solution.py:311
  131.5 2.1 %collective-permute-start.28 = (bf16[256,128]{1,0:T(8,128)(2,1)S(1)}, bf16[256,128]{1,0:T(8,128)(2,1)S(1)}, u32[]{:S(2)}, u32[]{:S(2)}) collective-permute-start(bf16[256,128]{1,0:T(8,128)(2,1)S(1)} %add_convert_fusion.10), channel_id=1, source_target_pairs={{0,4},{4,0},{8,12},{12,8},{16,20},{20,16},{24,28},{28,24},{1,5},{5... | collective-permute-start | bytes 196616 | tf_op jit(solution)/shard_map/ppermute | solution.py:311
  133.7 1.4 %convolution_convert_fusion = bf16[2048,256]{1,0:T(8,128)(2,1)} fusion(bf16[256,256]{1,0:T(8,128)(2,1)S(1)} %copy-done, bf16[2048,128]{1,0:T(8,128)(2,1)S(1)} %pad_maximum_fusion.1, bf16[2048,128]{1,0:T(8,128)(2,1)S(1)} %pad_maximum_fusion), kind=kOutput, calls=%fused_computation.2 | convolution fusion | flops 271056896 | bytes 2228224 | tf_op jit(solution)/shard_map/dot_general | solution.py:543
  (95 shorter events, 21.1 us)
Async XLA Ops:
  0.6 133.0 %copy-start = (bf16[256,256]{1,0:T(8,128)(2,1)S(1)}, bf16[256,256]{1,0:T(8,128)(2,1)}, u32[]{:S(2)}) copy-start(bf16[256,256]{1,0:T(8,128)(2,1)} %param.11) | copy-start | bytes 393220
  0.7 10.5 %copy-start.1 = (bf16[2048,256]{1,0:T(8,128)(2,1)S(1)}, bf16[2048,256]{1,0:T(8,128)(2,1)}, u32[]{:S(2)}) copy-start(bf16[2048,256]{1,0:T(8,128)(2,1)} %refs_0_) | copy-start | bytes 3145732
  3.4 26.4 %collective-permute-start.1 = (bf16[2048,128]{1,0:T(8,128)(2,1)}, bf16[2048,128]{1,0:T(8,128)(2,1)}, u32[]{:S(2)}, u32[]{:S(2)}) collective-permute-start(bf16[2048,128]{1,0:T(8,128)(2,1)} %get-tuple-element.94.refs_0_), channel_id=1, source_target_pairs={{0,2},{1,3},{2,0},{3,1},{4,6},{5,7},{6,4},{7,5},{8,10},{9,11},{10,... | collective-permute-start | bytes 1572872 | tf_op jit(solution)/shard_map/ppermute | solution.py:311
  6.5 23.2 %collective-permute-start = (bf16[2048,128]{1,0:T(8,128)(2,1)}, bf16[2048,128]{1,0:T(8,128)(2,1)}, u32[]{:S(2)}, u32[]{:S(2)}) collective-permute-start(bf16[2048,128]{1,0:T(8,128)(2,1)} %get-tuple-element.94.refs_0_), channel_id=1, source_target_pairs={{0,1},{1,0},{2,3},{3,2},{4,5},{5,4},{6,7},{7,6},{8,9},{9,8},{10,11... | collective-permute-start | bytes 1572872 | tf_op jit(solution)/shard_map/ppermute | solution.py:311
  11.2 27.7 %collective-permute-start.7 = (bf16[2048,256]{1,0:T(8,128)(2,1)S(1)}, bf16[2048,256]{1,0:T(8,128)(2,1)S(1)}, u32[]{:S(2)}, u32[]{:S(2)}) collective-permute-start(bf16[2048,256]{1,0:T(8,128)(2,1)S(1)} %copy-done.1), channel_id=1, source_target_pairs={{0,16},{4,20},{8,24},{12,28},{16,0},{20,4},{24,8},{28,12},{1,17},{... | collective-permute-start | bytes 3145736 | tf_op jit(solution)/shard_map/ppermute | solution.py:311
  12.5 26.4 %collective-permute-start.6 = (bf16[2048,256]{1,0:T(8,128)(2,1)S(1)}, bf16[2048,256]{1,0:T(8,128)(2,1)S(1)}, u32[]{:S(2)}, u32[]{:S(2)}) collective-permute-start(bf16[2048,256]{1,0:T(8,128)(2,1)S(1)} %copy-done.1), channel_id=1, source_target_pairs={{0,8},{4,12},{8,0},{12,4},{16,24},{20,28},{24,16},{28,20},{1,9},{5... | collective-permute-start | bytes 3145736 | tf_op jit(solution)/shard_map/ppermute | solution.py:311
  29.8 9.2 %collective-permute-start.4 = (bf16[2048,128]{1,0:T(8,128)(2,1)}, bf16[2048,128]{1,0:T(8,128)(2,1)S(1)}, u32[]{:S(2)}, u32[]{:S(2)}) collective-permute-start(bf16[2048,128]{1,0:T(8,128)(2,1)} %get-tuple-element.94.refs_0_), channel_id=1, source_target_pairs={{1,2},{2,1},{5,6},{6,5},{9,10},{10,9},{13,14},{14,13},{17,18},{18,... | collective-permute-start | bytes 1572872 | tf_op jit(solution)/shard_map/ppermute | solution.py:329
  30.5 14.5 %collective-permute-start.5 = (bf16[2048,128]{1,0:T(8,128)(2,1)}, bf16[2048,128]{1,0:T(8,128)(2,1)S(1)}, u32[]{:S(2)}, u32[]{:S(2)}) collective-permute-start(bf16[2048,128]{1,0:T(8,128)(2,1)} %collective-permute-done.1.refs_2_), channel_id=1, source_target_pairs={{1,0},{2,3},{5,4},{6,7},{9,8},{10,11},{13,12},{14,15},{17,16},{18,... | collective-permute-start | bytes 1572872 | tf_op jit(solution)/shard_map/ppermute | solution.py:329
  38.9 8.6 %copy-start.7 = (bf16[2048,128]{1,0:T(8,128)(2,1)S(1)}, bf16[2048,128]{1,0:T(8,128)(2,1)}, u32[]{:S(2)}) copy-start(bf16[2048,128]{1,0:T(8,128)(2,1)} %get-tuple-element.117.refs_0_) | copy-start | bytes 1572868
  45.1 20.8 %collective-permute-start.9 = (bf16[1024,256]{1,0:T(8,128)(2,1)S(1)}, bf16[1024,256]{1,0:T(8,128)(2,1)S(1)}, u32[]{:S(2)}, u32[]{:S(2)}) collective-permute-start(bf16[1024,256]{1,0:T(8,128)(2,1)S(1)} %slice.96), channel_id=1, source_target_pairs={{0,8},{4,12},{8,0},{12,4},{16,24},{20,28},{24,16},{28,20},{1,9},{5... | collective-permute-start | bytes 1572872 | tf_op jit(solution)/shard_map/ppermute | solution.py:311
  46.3 19.5 %collective-permute-start.8 = (bf16[1024,256]{1,0:T(8,128)(2,1)S(1)}, bf16[1024,256]{1,0:T(8,128)(2,1)S(1)}, u32[]{:S(2)}, u32[]{:S(2)}) collective-permute-start(bf16[1024,256]{1,0:T(8,128)(2,1)S(1)} %slice.95), channel_id=1, source_target_pairs={{0,16},{4,20},{8,24},{12,28},{16,0},{20,4},{24,8},{28,12},{1,17},{... | collective-permute-start | bytes 1572872 | tf_op jit(solution)/shard_map/ppermute | solution.py:311
  47.6 24.5 %collective-permute-start.3 = (bf16[2048,128]{1,0:T(8,128)(2,1)S(1)}, bf16[2048,128]{1,0:T(8,128)(2,1)S(1)}, u32[]{:S(2)}, u32[]{:S(2)}) collective-permute-start(bf16[2048,128]{1,0:T(8,128)(2,1)S(1)} %copy-done.7), channel_id=1, source_target_pairs={{0,2},{1,3},{2,0},{3,1},{4,6},{5,7},{6,4},{7,5},{8,10},{9,11},{10,... | collective-permute-start | bytes 1572872 | tf_op jit(solution)/shard_map/ppermute | solution.py:311
  50.3 21.8 %collective-permute-start.2 = (bf16[2048,128]{1,0:T(8,128)(2,1)S(1)}, bf16[2048,128]{1,0:T(8,128)(2,1)S(1)}, u32[]{:S(2)}, u32[]{:S(2)}) collective-permute-start(bf16[2048,128]{1,0:T(8,128)(2,1)S(1)} %copy-done.7), channel_id=1, source_target_pairs={{0,1},{1,0},{2,3},{3,2},{4,5},{5,4},{6,7},{7,6},{8,9},{9,8},{10,11... | collective-permute-start | bytes 1572872 | tf_op jit(solution)/shard_map/ppermute | solution.py:311
  66.5 13.4 %collective-permute-start.12 = (bf16[2048,128]{1,0:T(8,128)(2,1)S(1)}, bf16[2048,128]{1,0:T(8,128)(2,1)S(1)}, u32[]{:S(2)}, u32[]{:S(2)}) collective-permute-start(bf16[2048,128]{1,0:T(8,128)(2,1)S(1)} %bitcast.56), channel_id=1, source_target_pairs={{0,8},{4,12},{8,0},{12,4},{16,24},{20,28},{24,16},{28,20},{1,9},{5... | collective-permute-start | bytes 1572872 | tf_op jit(solution)/shard_map/ppermute | solution.py:311
  66.6 13.3 %collective-permute-start.13 = (bf16[2048,128]{1,0:T(8,128)(2,1)S(1)}, bf16[2048,128]{1,0:T(8,128)(2,1)S(1)}, u32[]{:S(2)}, u32[]{:S(2)}) collective-permute-start(bf16[2048,128]{1,0:T(8,128)(2,1)S(1)} %bitcast.55), channel_id=1, source_target_pairs={{0,16},{4,20},{8,24},{12,28},{16,0},{20,4},{24,8},{28,12},{1,17},{... | collective-permute-start | bytes 1572872 | tf_op jit(solution)/shard_map/ppermute | solution.py:311
  72.1 9.8 %collective-permute-start.10 = (bf16[2048,128]{1,0:T(8,128)(2,1)S(1)}, bf16[2048,128]{1,0:T(8,128)(2,1)S(1)}, u32[]{:S(2)}, u32[]{:S(2)}) collective-permute-start(bf16[2048,128]{1,0:T(8,128)(2,1)S(1)} %copy-done.7), channel_id=1, source_target_pairs={{1,2},{2,1},{5,6},{6,5},{9,10},{10,9},{13,14},{14,13},{17,18},{18,... | collective-permute-start | bytes 1572872 | tf_op jit(solution)/shard_map/ppermute | solution.py:329
  72.8 14.3 %collective-permute-start.11 = (bf16[2048,128]{1,0:T(8,128)(2,1)S(1)}, bf16[2048,128]{1,0:T(8,128)(2,1)S(1)}, u32[]{:S(2)}, u32[]{:S(2)}) collective-permute-start(bf16[2048,128]{1,0:T(8,128)(2,1)S(1)} %collective-permute-done.3.refs_2_), channel_id=1, source_target_pairs={{1,0},{2,3},{5,4},{6,7},{9,8},{10,11},{13,12},{14,15},{17,16},{18,... | collective-permute-start | bytes 1572872 | tf_op jit(solution)/shard_map/ppermute | solution.py:329
  93.6 8.1 %collective-permute-start.14 = (bf16[8192,128]{1,0:T(8,128)(2,1)}, bf16[8192,128]{1,0:T(8,128)(2,1)}, u32[]{:S(2)}, u32[]{:S(2)}) collective-permute-start(bf16[8192,128]{1,0:T(8,128)(2,1)} %get-tuple-element.139), channel_id=1, source_target_pairs={{0,4},{4,0},{8,12},{12,8},{16,20},{20,16},{24,28},{28,24},{1,5},{5... | collective-permute-start | bytes 6291464 | tf_op jit(solution)/shard_map/ppermute | solution.py:311
  97.6 9.3 %collective-permute-start.15 = (bf16[1024,128]{1,0:T(8,128)(2,1)}, bf16[1024,128]{1,0:T(8,128)(2,1)S(1)}, u32[]{:S(2)}, u32[]{:S(2)}) collective-permute-start(bf16[1024,128]{1,0:T(8,128)(2,1)} %get-tuple-element.149), channel_id=1, source_target_pairs={{0,16},{4,20},{8,24},{12,28},{16,0},{20,4},{24,8},{28,12},{1,17},{... | collective-permute-start | bytes 786440 | tf_op jit(solution)/shard_map/ppermute | solution.py:311
  98.1 8.8 %collective-permute-start.16 = (bf16[1024,128]{1,0:T(8,128)(2,1)}, bf16[1024,128]{1,0:T(8,128)(2,1)S(1)}, u32[]{:S(2)}, u32[]{:S(2)}) collective-permute-start(bf16[1024,128]{1,0:T(8,128)(2,1)} %get-tuple-element.150), channel_id=1, source_target_pairs={{0,8},{4,12},{8,0},{12,4},{16,24},{20,28},{24,16},{28,20},{1,9},{5... | collective-permute-start | bytes 786440 | tf_op jit(solution)/shard_map/ppermute | solution.py:311
  106.9 1.3 collective-permute-start.19
  107.4 13.4 %collective-permute-start.17 = (bf16[2048,128]{1,0:T(8,128)(2,1)S(1)}, bf16[2048,128]{1,0:T(8,128)(2,1)S(1)}, u32[]{:S(2)}, u32[]{:S(2)}) collective-permute-start(bf16[2048,128]{1,0:T(8,128)(2,1)S(1)} %bitcast.53), channel_id=1, source_target_pairs={{0,8},{4,12},{8,0},{12,4},{16,24},{20,28},{24,16},{28,20},{1,9},{5... | collective-permute-start | bytes 1572872 | tf_op jit(solution)/shard_map/ppermute | solution.py:311
  107.4 13.4 %collective-permute-start.18 = (bf16[2048,128]{1,0:T(8,128)(2,1)S(1)}, bf16[2048,128]{1,0:T(8,128)(2,1)S(1)}, u32[]{:S(2)}, u32[]{:S(2)}) collective-permute-start(bf16[2048,128]{1,0:T(8,128)(2,1)S(1)} %bitcast.54), channel_id=1, source_target_pairs={{0,16},{4,20},{8,24},{12,28},{16,0},{20,4},{24,8},{28,12},{1,17},{... | collective-permute-start | bytes 1572872 | tf_op jit(solution)/shard_map/ppermute | solution.py:311
  108.3 5.3 %collective-permute-start.22 = (bf16[256,128]{1,0:T(8,128)(2,1)S(1)}, bf16[256,128]{1,0:T(8,128)(2,1)S(1)}, u32[]{:S(2)}, u32[]{:S(2)}) collective-permute-start(bf16[256,128]{1,0:T(8,128)(2,1)S(1)} %add_convert_fusion.12), channel_id=1, source_target_pairs={{0,3},{1,2},{2,1},{3,0},{4,7},{5,6},{6,5},{7,4},{8,11},{9,10},{10,... | collective-permute-start | bytes 196616 | tf_op jit(solution)/shard_map/ppermute | solution.py:311
  112.0 4.5 %collective-permute-start.21 = (bf16[256,128]{1,0:T(8,128)(2,1)S(1)}, bf16[256,128]{1,0:T(8,128)(2,1)S(1)}, u32[]{:S(2)}, u32[]{:S(2)}) collective-permute-start(bf16[256,128]{1,0:T(8,128)(2,1)S(1)} %add_convert_fusion.12), channel_id=1, source_target_pairs={{0,2},{1,3},{2,0},{3,1},{4,6},{5,7},{6,4},{7,5},{8,10},{9,11},{10,... | collective-permute-start | bytes 196616 | tf_op jit(solution)/shard_map/ppermute | solution.py:311
  112.0 4.5 %collective-permute-start.20 = (bf16[256,128]{1,0:T(8,128)(2,1)S(1)}, bf16[256,128]{1,0:T(8,128)(2,1)S(1)}, u32[]{:S(2)}, u32[]{:S(2)}) collective-permute-start(bf16[256,128]{1,0:T(8,128)(2,1)S(1)} %add_convert_fusion.12), channel_id=1, source_target_pairs={{0,1},{1,0},{2,3},{3,2},{4,5},{5,4},{6,7},{7,6},{8,9},{9,8},{10,11... | collective-permute-start | bytes 196616 | tf_op jit(solution)/shard_map/ppermute | solution.py:311
  121.1 6.9 %collective-permute-start.23 = (bf16[1024,128]{1,0:T(8,128)(2,1)S(1)}, bf16[1024,128]{1,0:T(8,128)(2,1)S(1)}, u32[]{:S(2)}, u32[]{:S(2)}) collective-permute-start(bf16[1024,128]{1,0:T(8,128)(2,1)S(1)} %get-tuple-element.166), channel_id=1, source_target_pairs={{0,16},{4,20},{8,24},{12,28},{16,0},{20,4},{24,8},{28,12},{1,17},{... | collective-permute-start | bytes 786440 | tf_op jit(solution)/shard_map/ppermute | solution.py:311
  122.0 6.7 %collective-permute-start.24 = (bf16[1024,128]{1,0:T(8,128)(2,1)S(1)}, bf16[1024,128]{1,0:T(8,128)(2,1)S(1)}, u32[]{:S(2)}, u32[]{:S(2)}) collective-permute-start(bf16[1024,128]{1,0:T(8,128)(2,1)S(1)} %get-tuple-element.168), channel_id=1, source_target_pairs={{0,8},{4,12},{8,0},{12,4},{16,24},{20,28},{24,16},{28,20},{1,9},{5... | collective-permute-start | bytes 786440 | tf_op jit(solution)/shard_map/ppermute | solution.py:311
  123.2 6.9 %collective-permute-start.27 = (bf16[256,128]{1,0:T(8,128)(2,1)S(1)}, bf16[256,128]{1,0:T(8,128)(2,1)S(1)}, u32[]{:S(2)}, u32[]{:S(2)}) collective-permute-start(bf16[256,128]{1,0:T(8,128)(2,1)S(1)} %add_convert_fusion.11), channel_id=1, source_target_pairs={{0,24},{4,28},{8,16},{12,20},{16,8},{20,12},{24,0},{28,4},{1,25},{... | collective-permute-start | bytes 196616 | tf_op jit(solution)/shard_map/ppermute | solution.py:311
  123.9 6.2 %collective-permute-start.26 = (bf16[256,128]{1,0:T(8,128)(2,1)S(1)}, bf16[256,128]{1,0:T(8,128)(2,1)S(1)}, u32[]{:S(2)}, u32[]{:S(2)}) collective-permute-start(bf16[256,128]{1,0:T(8,128)(2,1)S(1)} %add_convert_fusion.11), channel_id=1, source_target_pairs={{0,16},{4,20},{8,24},{12,28},{16,0},{20,4},{24,8},{28,12},{1,17},{... | collective-permute-start | bytes 196616 | tf_op jit(solution)/shard_map/ppermute | solution.py:311
  124.7 6.8 %collective-permute-start.25 = (bf16[256,128]{1,0:T(8,128)(2,1)S(1)}, bf16[256,128]{1,0:T(8,128)(2,1)S(1)}, u32[]{:S(2)}, u32[]{:S(2)}) collective-permute-start(bf16[256,128]{1,0:T(8,128)(2,1)S(1)} %add_convert_fusion.11), channel_id=1, source_target_pairs={{0,8},{4,12},{8,0},{12,4},{16,24},{20,28},{24,16},{28,20},{1,9},{5... | collective-permute-start | bytes 196616 | tf_op jit(solution)/shard_map/ppermute | solution.py:311
  131.5 3.6 %collective-permute-start.28 = (bf16[256,128]{1,0:T(8,128)(2,1)S(1)}, bf16[256,128]{1,0:T(8,128)(2,1)S(1)}, u32[]{:S(2)}, u32[]{:S(2)}) collective-permute-start(bf16[256,128]{1,0:T(8,128)(2,1)S(1)} %add_convert_fusion.10), channel_id=1, source_target_pairs={{0,4},{4,0},{8,12},{12,8},{16,20},{20,16},{24,28},{28,24},{1,5},{5... | collective-permute-start | bytes 196616 | tf_op jit(solution)/shard_map/ppermute | solution.py:311
  (9 other events, 26.1 us)

commit v15 on v13

--- a/solution.py
+++ b/solution.py
@@ -414,15 +414,6 @@
     return jnp.concatenate(done, axis=0)
 
 
-def weight_term(near, sums):
-    terms, at = [], 0
-    for f in [part for parts in near for part in parts]:
-        own = sums[at : at + f.shape[0]]
-        terms.append(lax.dot_general(f, own, (((0,), (0,)), ((), ())), preferred_element_type=jnp.float32))
-        at += f.shape[0]
-    return sum(terms[1:], terms[0]).astype(jnp.bfloat16)
-
-
 def term_kernel(*refs):
     *parts, sums_ref, out_ref, acc_ref = refs
     acc_ref[...] = jnp.zeros_like(acc_ref)
@@ -442,7 +433,7 @@
     out_ref[...] = acc_ref[...].T.astype(out_ref.dtype)
 
 
-def weight_term_early(near, sums):
+def weight_term(near, sums):
     parts = [part for group in near for part in group]
     shape = (parts[0].shape[1], sums.shape[1])
     return pl.pallas_call(
@@ -472,10 +463,12 @@
     bits = [1 << b for b in range(1, n_row.bit_length() - 1)]
     mid = ((col & 3) == 1) | ((col & 3) == 2)
 
-    own0, own1 = [
-        jnp.where(preact[:, cut] > 0, grad_out[:, cut], jnp.zeros_like(grad_out[:, cut]))
-        for cut in (slice(0, cw), slice(cw, width))
-    ]
+    def masked(preact, grad_out, cut):
+        return jnp.where(preact[:, cut] > 0, grad_out[:, cut], jnp.zeros_like(grad_out[:, cut]))
+
+    own0 = masked(preact, grad_out, slice(0, cw))
+    own0, preact, grad_out = fence(own0, preact, grad_out)
+    own1 = masked(preact, grad_out, slice(cw, width))
     first0 = gather_first(own0)
     place = jnp.stack([live_counts.reshape(()), row, col, mid.astype(jnp.int32)])
     plan0, plan1, slot = make_plans(tile_rows, tile_cols, place, n_row, nodes // SIDE)
@@ -501,7 +494,7 @@
     got0, near = fence(got0, near)
     stage0, sums0 = stage_sums(got0[0], got0[1], n_row // 2, rows, at_once=True)
     recv0 = exchange_first(stage0, bits)
-    term0 = weight_term_early(near, sums0)
+    term0 = weight_term(near, sums0)
     own1, first1, stage0, term0 = fence(own1, first1, stage0, term0)
 
     second1 = gather_second(own1, first1[1], n_col)

time: 136 us -> 137 us (level)
  local copies, waits for them, and re-layouts: 7.84 us -> 10.5 us
  Pallas kernels: 43.3 us -> 45.7 us
  matrix products: 3.56 us -> 1.43 us
  starting transfers between devices: 35.7 us -> 33.6 us
  blocking collectives: 7.15 us -> 8.78 us
    pallas_call x1 -> x2, Pallas kernels: 3.8 us -> 7.59 us  [weight_term(): pl.pallas_call(term_kernel, out_shape=jax.ShapeDtypeStruct(shape, jnp.bfl...]
    ppermute x25, starting transfers between devices: 31.8 us -> 29.6 us  [xor_permute(): return lax.ppermute(value, axis, [(i, i ^ mask) for i in range(size)])]
    dot_general x5 -> x0, matrix products: 2.12 us -> none  [weight_term(): lax.dot_general(f, own, (((0,), (0,)), ((), ())), preferred_element_type=...]
    all_to_all x1, blocking collectives: 7.15 us -> 8.78 us  [swap_cores(): return lax.all_to_all(both, 'row', 0, 0, axis_index_groups=pairs)]
    pallas_call x4, Pallas kernels: 27.6 us -> 26.2 us  [spmm(): pl.pallas_call(functools.partial(spmm_kernel, [len(p) for p in pieces], l...]
    unnamed x26 -> x28, local copies, waits for them, and re-layouts: 5.44 us -> 6.74 us
  transfers between devices with their start and end apart: 29 -> 29, of which waited for: 13 -> 12; matrix products, arithmetic and copies ran while one was open for 7% -> 7% of each run, Pallas kernels for 28% -> 29%
where the time goes in v15:
time: 137 us; the launch traced here: 136 us
  Pallas kernels  45.7 us (33%)
  starting transfers between devices  33.6 us (25%)
  waiting for transfers between devices  27.3 us (20%)
  local copies, waits for them, and re-layouts  10.5 us (8%)
  blocking collectives  8.78 us (6%)
  other arithmetic  7.38 us (5%)
  between operations  1.74 us (1%)
  matrix products  1.43 us (1%)
    ppermute x25, starting transfers between devices, xor_permute(): return lax.ppermute(value, axis, [(i, i ^ mask) for i in range(size)])  29.6 us
    pallas_call x4, Pallas kernels, spmm(): pl.pallas_call(functools.partial(spmm_kernel, [len(p) for p in pieces], l...  26.2 us
    ppermute x25, waiting for transfers between devices, xor_permute(): return lax.ppermute(value, axis, [(i, i ^ mask) for i in range(size)])  19.4 us
    pallas_call x1, Pallas kernels, flip_tiles(): pl.pallas_call(flip_kernel, out_shape=jax.ShapeDtypeStruct((slots + GROUP...  9.59 us
    all_to_all x1, blocking collectives, swap_cores(): return lax.all_to_all(both, 'row', 0, 0, axis_index_groups=pairs)  8.78 us
    ppermute x2, waiting for transfers between devices, gather_second(): lax.ppermute(by_two, 'col', ends)  7.86 us
    pallas_call x2, Pallas kernels, weight_term(): pl.pallas_call(term_kernel, out_shape=jax.ShapeDtypeStruct(shape, jnp.bfl...  7.59 us
    unnamed x28, local copies, waits for them, and re-layouts  6.74 us
  transfers between devices with their start and end apart: 29, of which 12 were waited for; matrix products, arithmetic and copies ran while one was open for 7% of the time, Pallas kernels for 29%

profile of v15, /device:TPU:1, one launch (start us, length us, event | category | flops | bytes accessed | tf_op | source)
XLA Modules:
  0.0 136.3 jit_solution(11035898285036846559)
XLA Ops:
  0.7 2.1 %compare_select_fusion.1.refs_0_ = bf16[2048,128]{1,0:T(8,128)(2,1)} fusion(bf16[2048,256]{1,0:T(8,128)(2,1)} %param.8, bf16[2048,256]{1,0:T(8,128)(2,1)} %param.9), kind=kLoop, calls=%fused_computation.12 | loop fusion | flops 524288 | bytes 1572864 | tf_op jit(solution)/shard_map/jit(_where)/select_n | solution.py:467
  2.8 3.1 %collective-permute-start.1 = (bf16[2048,128]{1,0:T(8,128)(2,1)}, bf16[2048,128]{1,0:T(8,128)(2,1)}, u32[]{:S(2)}, u32[]{:S(2)}) collective-permute-start(bf16[2048,128]{1,0:T(8,128)(2,1)} %compare_select_fusion.1.refs_0_), channel_id=1, source_target_pairs={{0,2},{1,3},{2,0},{3,1},{4,6},{5,7},{6,4},{7,5},{8,10},{9,11},{10,... | collective-permute-start | bytes 1572872 | tf_op jit(solution)/shard_map/ppermute | solution.py:311
  5.9 1.3 collective-permute-start
  11.0 2.3 %plan_slots.1 = (s32[8,512]{1,0:T(8,128)S(1)}, s32[8,512]{1,0:T(8,128)S(1)}, s32[1,320]{1,0:T(1,128)S(1)}) custom-call(s32[4]{0:T(128)S(1)} %pad_add_fusion.place_ref, s32[1,320]{1,0:T(1,128)S(1)} %bitcast.39, s32[1,320]{1,0:T(1,128)S(1)} %bitcast.41, s32[320,1]{1,0:T(8,128)S(1)} %copy.10.rows_c, s32[320,1]{1,0:T(8,128)S(1)} %copy.11.cols_c), custom_call_target="tpu_custom_call" | custom-call | bytes 4096 | tf_op jit(solution)/shard_map/plan_slots/pallas_call | solution.py:122
  13.3 1.3 collective-permute-start.7
  15.8 4.0 %copy-done.1 = bf16[1,1,320,128,128]{4,3,2,1,0:T(8,128)(2,1)S(1)} copy-done((bf16[1,1,320,128,128]{4,3,2,1,0:T(8,128)(2,1)S(1)}, bf16[1,1,320,128,128]{4,3,2,1,0:T(8,128)(2,1)}, u32[]{:S(2)}) %copy-start.1) | copy-done | bytes 10485784
  19.8 9.6 %flip_tiles.1.refs_3_.refs_2_ = bf16[352,128,128]{2,1,0:T(8,128)(2,1)S(1)} custom-call(s32[1,320]{1,0:T(1,128)S(1)} %get-tuple-element.96.slot_ref, bf16[320,128,128]{2,1,0:T(8,128)(2,1)S(1)} %bitcast.37), custom_call_target="tpu_custom_call" | custom-call | bytes 4096 | tf_op jit(solution)/shard_map/flip_tiles/pallas_call | solution.py:165
  30.3 1.3 collective-permute-start.5
  31.6 8.5 %spmm_first.2 = (bf16[8192,128]{1,0:T(8,128)(2,1)S(1)}, bf16[8192,128]{1,0:T(8,128)(2,1)S(1)}) custom-call(s32[8,512]{1,0:T(8,128)S(1)} %get-tuple-element.99.plan_ref, bf16[2048,128]{1,0:T(8,128)(2,1)} %compare_select_fusion.1.refs_0_, bf16[2048,128]{1,0:T(8,128)(2,1)} %collective-permute-done.refs_1_, bf16[2048,128]{1,0:T(8,128)(2,1)} %collective-permute-done.1.refs_2_, ...), custom_call_target="tpu_custom_call" | custom-call | bytes 4096 | tf_op jit(solution)/shard_map/spmm_first/pallas_call | solution.py:288
  40.1 4.1 %collective-permute-done.5.refs_1_ = bf16[2048,128]{1,0:T(8,128)(2,1)S(1)} collective-permute-done((bf16[2048,128]{1,0:T(8,128)(2,1)}, bf16[2048,128]{1,0:T(8,128)(2,1)S(1)}, u32[]{:S(2)}, u32[]{:S(2)}) %collective-permute-start.5) | collective-permute-done | bytes 524320 | tf_op jit(solution)/shard_map/ppermute | solution.py:329
  44.3 1.4 %collective-permute-start.9 = (bf16[1024,256]{1,0:T(8,128)(2,1)S(1)}, bf16[1024,256]{1,0:T(8,128)(2,1)S(1)}, u32[]{:S(2)}, u32[]{:S(2)}) collective-permute-start(bf16[1024,256]{1,0:T(8,128)(2,1)S(1)} %slice.81), channel_id=1, source_target_pairs={{0,8},{4,12},{8,0},{12,4},{16,24},{20,28},{24,16},{28,20},{1,9},{5... | collective-permute-start | bytes 1572872 | tf_op jit(solution)/shard_map/ppermute | solution.py:311
  47.0 2.7 %collective-permute-start.3 = (bf16[2048,128]{1,0:T(8,128)(2,1)S(1)}, bf16[2048,128]{1,0:T(8,128)(2,1)S(1)}, u32[]{:S(2)}, u32[]{:S(2)}) collective-permute-start(bf16[2048,128]{1,0:T(8,128)(2,1)S(1)} %compare_select_fusion.refs_0_), channel_id=1, source_target_pairs={{0,2},{1,3},{2,0},{3,1},{4,6},{5,7},{6,4},{7,5},{8,10},{9,11},{10,... | collective-permute-start | bytes 1572872 | tf_op jit(solution)/shard_map/ppermute | solution.py:311
  49.7 2.1 %collective-permute-start.2 = (bf16[2048,128]{1,0:T(8,128)(2,1)S(1)}, bf16[2048,128]{1,0:T(8,128)(2,1)S(1)}, u32[]{:S(2)}, u32[]{:S(2)}) collective-permute-start(bf16[2048,128]{1,0:T(8,128)(2,1)S(1)} %compare_select_fusion.refs_0_), channel_id=1, source_target_pairs={{0,1},{1,0},{2,3},{3,2},{4,5},{5,4},{6,7},{7,6},{8,9},{9,8},{10,11... | collective-permute-start | bytes 1572872 | tf_op jit(solution)/shard_map/ppermute | solution.py:311
  51.8 4.5 %spmm_last.2 = bf16[2,8192,128]{2,1,0:T(8,128)(2,1)S(1)} custom-call(s32[8,512]{1,0:T(8,128)S(1)} %get-tuple-element.97.plan_ref, bf16[2048,128]{1,0:T(8,128)(2,1)S(1)} %collective-permute-done.4.refs_0_, bf16[2048,128]{1,0:T(8,128)(2,1)S(1)} %collective-permute-done.5.refs_1_, bf16[352,128,128]{2,1,0:T(8,128)(2,1)S(1)} %flip_tiles.1.refs_3_.refs_2_, ...), custom_call_target="tpu_custom_call" | custom-call | bytes 4096 | tf_op jit(solution)/shard_map/spmm_last/pallas_call | solution.py:288
  56.3 8.8 %all_to_all.5 = bf16[2,8192,128]{2,1,0:T(8,128)(2,1)S(1)} all-to-all(bf16[2,8192,128]{2,1,0:T(8,128)(2,1)S(1)} %spmm_last.2), channel_id=1, replica_groups={{0,4},{8,12},{16,20},{24,28},{1,5},{9,13},{17,21},{25,29},{2,6},{10,14}..., dimensions={0} | all-to-all | bytes 8388608 | tf_op jit(solution)/shard_map/all_to_all | solution.py:343
  66.2 3.8 %weight_term.2 = bf16[256,128]{1,0:T(8,128)(2,1)S(1)} custom-call(bf16[2048,256]{1,0:T(8,128)(2,1)S(1)} %copy-done.2, bf16[2048,256]{1,0:T(8,128)(2,1)S(1)} %collective-permute-done.6.refs_1_, bf16[2048,256]{1,0:T(8,128)(2,1)S(1)} %collective-permute-done.7.refs_2_, bf16[1024,256]{1,0:T(8,128)(2,1)S(1)} %collective-permute-done.8.refs_3_, ...), custom_call_target="tpu_custom_call" | custom-call | bytes 4096 | tf_op jit(solution)/shard_map/weight_term/pallas_call | solution.py:439
  70.0 1.5 %collective-permute-done.3.refs_2_ = bf16[2048,128]{1,0:T(8,128)(2,1)S(1)} collective-permute-done((bf16[2048,128]{1,0:T(8,128)(2,1)S(1)}, bf16[2048,128]{1,0:T(8,128)(2,1)S(1)}, u32[]{:S(2)}, u32[]{:S(2)}) %collective-permute-start.3) | collective-permute-done | bytes 524320 | tf_op jit(solution)/shard_map/ppermute | solution.py:311
  73.5 7.2 %spmm_first.3 = (bf16[8192,128]{1,0:T(8,128)(2,1)S(1)}, bf16[8192,128]{1,0:T(8,128)(2,1)S(1)}) custom-call(s32[8,512]{1,0:T(8,128)S(1)} %get-tuple-element.99.plan_ref, bf16[2048,128]{1,0:T(8,128)(2,1)S(1)} %compare_select_fusion.refs_0_, bf16[2048,128]{1,0:T(8,128)(2,1)S(1)} %collective-permute-done.2.refs_1_, ...), custom_call_target="tpu_custom_call" | custom-call | bytes 4096 | tf_op jit(solution)/shard_map/spmm_first/pallas_call | solution.py:288
  82.7 3.8 %collective-permute-done.11.refs_1_ = bf16[2048,128]{1,0:T(8,128)(2,1)S(1)} collective-permute-done((bf16[2048,128]{1,0:T(8,128)(2,1)S(1)}, bf16[2048,128]{1,0:T(8,128)(2,1)S(1)}, u32[]{:S(2)}, u32[]{:S(2)}) %collective-permute-start.11) | collective-permute-done | bytes 524320 | tf_op jit(solution)/shard_map/ppermute | solution.py:329
  86.5 6.0 %spmm_last.3 = (bf16[8192,128]{1,0:T(8,128)(2,1)}, bf16[8192,128]{1,0:T(8,128)(2,1)S(1)}) custom-call(s32[8,512]{1,0:T(8,128)S(1)} %get-tuple-element.97.plan_ref, bf16[2048,128]{1,0:T(8,128)(2,1)S(1)} %collective-permute-done.10.refs_0_, bf16[2048,128]{1,0:T(8,128)(2,1)S(1)} %collective-permute-done.11.refs_1_, ...), custom_call_target="tpu_custom_call" | custom-call | bytes 4096 | tf_op jit(solution)/shard_map/spmm_last/pallas_call | solution.py:288
  92.5 1.4 copy-done.3
  93.8 3.0 %collective-permute-start.14 = (bf16[8192,128]{1,0:T(8,128)(2,1)}, bf16[8192,128]{1,0:T(8,128)(2,1)}, u32[]{:S(2)}, u32[]{:S(2)}) collective-permute-start(bf16[8192,128]{1,0:T(8,128)(2,1)} %get-tuple-element.145), channel_id=1, source_target_pairs={{0,4},{4,0},{8,12},{12,8},{16,20},{20,16},{24,28},{28,24},{1,5},{5... | collective-permute-start | bytes 6291464 | tf_op jit(solution)/shard_map/ppermute | solution.py:311
  97.2 3.8 %collective-permute-done.14 = bf16[8192,128]{1,0:T(8,128)(2,1)} collective-permute-done((bf16[8192,128]{1,0:T(8,128)(2,1)}, bf16[8192,128]{1,0:T(8,128)(2,1)}, u32[]{:S(2)}, u32[]{:S(2)}) %collective-permute-start.14) | collective-permute-done | bytes 2097184 | tf_op jit(solution)/shard_map/ppermute | solution.py:311
  100.9 2.8 %add_convert_fusion.refs_5_ = bf16[8192,128]{1,0:T(8,128)(2,1)S(1)} fusion(bf16[8192,128]{1,0:T(8,128)(2,1)} %collective-permute-done.14, bf16[8192,128]{1,0:T(8,128)(2,1)} %copy-done.3), kind=kLoop, calls=%fused_computation | loop fusion | flops 4194304 | bytes 6291456 | tf_op jit(solution)/shard_map/convert_element_type | solution.py:358
  103.7 3.8 %weight_term.3 = bf16[256,128]{1,0:T(8,128)(2,1)S(1)} custom-call(bf16[2048,256]{1,0:T(8,128)(2,1)S(1)} %copy-done.2, bf16[2048,256]{1,0:T(8,128)(2,1)S(1)} %collective-permute-done.6.refs_1_, bf16[2048,256]{1,0:T(8,128)(2,1)S(1)} %collective-permute-done.7.refs_2_, bf16[1024,256]{1,0:T(8,128)(2,1)S(1)} %copy-done.7, bf16[1024,256]{1,0:T(8,128)(2,1)S(1)} %copy-done.5, ...), custom_call_target="tpu_custom_call" | custom-call | bytes 4096 | tf_op jit(solution)/shard_map/weight_term/pallas_call | solution.py:439
  109.1 3.7 %collective-permute-start.22 = (bf16[256,128]{1,0:T(8,128)(2,1)S(1)}, bf16[256,128]{1,0:T(8,128)(2,1)S(1)}, u32[]{:S(2)}, u32[]{:S(2)}) collective-permute-start(bf16[256,128]{1,0:T(8,128)(2,1)S(1)} %add_convert_fusion.12), channel_id=1, source_target_pairs={{0,3},{1,2},{2,1},{3,0},{4,7},{5,6},{6,5},{7,4},{8,11},{9,10},{10,... | collective-permute-start | bytes 196616 | tf_op jit(solution)/shard_map/ppermute | solution.py:311
  114.4 2.9 %collective-permute-done.21 = bf16[256,128]{1,0:T(8,128)(2,1)S(1)} collective-permute-done((bf16[256,128]{1,0:T(8,128)(2,1)S(1)}, bf16[256,128]{1,0:T(8,128)(2,1)S(1)}, u32[]{:S(2)}, u32[]{:S(2)}) %collective-permute-start.21) | collective-permute-done | bytes 65568 | tf_op jit(solution)/shard_map/ppermute | solution.py:311
  117.3 4.2 %collective-permute-done.17 = bf16[2048,128]{1,0:T(8,128)(2,1)S(1)} collective-permute-done((bf16[2048,128]{1,0:T(8,128)(2,1)S(1)}, bf16[2048,128]{1,0:T(8,128)(2,1)S(1)}, u32[]{:S(2)}, u32[]{:S(2)}) %collective-permute-start.17) | collective-permute-done | bytes 524320 | tf_op jit(solution)/shard_map/ppermute | solution.py:311
  126.1 2.5 %collective-permute-done.23 = bf16[1024,128]{1,0:T(8,128)(2,1)S(1)} collective-permute-done((bf16[1024,128]{1,0:T(8,128)(2,1)S(1)}, bf16[1024,128]{1,0:T(8,128)(2,1)S(1)}, u32[]{:S(2)}, u32[]{:S(2)}) %collective-permute-start.23) | collective-permute-done | bytes 262176 | tf_op jit(solution)/shard_map/ppermute | solution.py:311
  129.0 1.5 %collective-permute-done.27 = bf16[256,128]{1,0:T(8,128)(2,1)S(1)} collective-permute-done((bf16[256,128]{1,0:T(8,128)(2,1)S(1)}, bf16[256,128]{1,0:T(8,128)(2,1)S(1)}, u32[]{:S(2)}, u32[]{:S(2)}) %collective-permute-start.27) | collective-permute-done | bytes 65568 | tf_op jit(solution)/shard_map/ppermute | solution.py:311
  131.8 2.4 %collective-permute-start.28 = (bf16[256,128]{1,0:T(8,128)(2,1)S(1)}, bf16[256,128]{1,0:T(8,128)(2,1)S(1)}, u32[]{:S(2)}, u32[]{:S(2)}) collective-permute-start(bf16[256,128]{1,0:T(8,128)(2,1)S(1)} %add_convert_fusion.10), channel_id=1, source_target_pairs={{0,4},{4,0},{8,12},{12,8},{16,20},{20,16},{24,28},{28,24},{1,5},{5... | collective-permute-start | bytes 196616 | tf_op jit(solution)/shard_map/ppermute | solution.py:311
  134.2 1.4 %convolution_convert_fusion = bf16[2048,256]{1,0:T(8,128)(2,1)} fusion(bf16[256,256]{1,0:T(8,128)(2,1)S(1)} %copy-done, bf16[2048,128]{1,0:T(8,128)(2,1)S(1)} %pad_maximum_fusion.1, bf16[2048,128]{1,0:T(8,128)(2,1)S(1)} %pad_maximum_fusion), kind=kOutput, calls=%fused_computation.2 | convolution fusion | flops 271056896 | bytes 2228224 | tf_op jit(solution)/shard_map/dot_general | solution.py:536
  (96 shorter events, 22.0 us)
Async XLA Ops:
  0.6 133.5 %copy-start = (bf16[256,256]{1,0:T(8,128)(2,1)S(1)}, bf16[256,256]{1,0:T(8,128)(2,1)}, u32[]{:S(2)}) copy-start(bf16[256,256]{1,0:T(8,128)(2,1)} %param.11) | copy-start | bytes 393220
  0.6 12.7 %copy-start.2 = (bf16[2048,256]{1,0:T(8,128)(2,1)S(1)}, bf16[2048,256]{1,0:T(8,128)(2,1)}, u32[]{:S(2)}) copy-start(bf16[2048,256]{1,0:T(8,128)(2,1)} %refs_0_.1) | copy-start | bytes 3145732
  2.8 26.7 %collective-permute-start.1 = (bf16[2048,128]{1,0:T(8,128)(2,1)}, bf16[2048,128]{1,0:T(8,128)(2,1)}, u32[]{:S(2)}, u32[]{:S(2)}) collective-permute-start(bf16[2048,128]{1,0:T(8,128)(2,1)} %compare_select_fusion.1.refs_0_), channel_id=1, source_target_pairs={{0,2},{1,3},{2,0},{3,1},{4,6},{5,7},{6,4},{7,5},{8,10},{9,11},{10,... | collective-permute-start | bytes 1572872 | tf_op jit(solution)/shard_map/ppermute | solution.py:311
  5.9 23.6 %collective-permute-start = (bf16[2048,128]{1,0:T(8,128)(2,1)}, bf16[2048,128]{1,0:T(8,128)(2,1)}, u32[]{:S(2)}, u32[]{:S(2)}) collective-permute-start(bf16[2048,128]{1,0:T(8,128)(2,1)} %compare_select_fusion.1.refs_0_), channel_id=1, source_target_pairs={{0,1},{1,0},{2,3},{3,2},{4,5},{5,4},{6,7},{7,6},{8,9},{9,8},{10,11... | collective-permute-start | bytes 1572872 | tf_op jit(solution)/shard_map/ppermute | solution.py:311
  13.3 26.8 %collective-permute-start.7 = (bf16[2048,256]{1,0:T(8,128)(2,1)S(1)}, bf16[2048,256]{1,0:T(8,128)(2,1)S(1)}, u32[]{:S(2)}, u32[]{:S(2)}) collective-permute-start(bf16[2048,256]{1,0:T(8,128)(2,1)S(1)} %copy-done.2), channel_id=1, source_target_pairs={{0,16},{4,20},{8,24},{12,28},{16,0},{20,4},{24,8},{28,12},{1,17},{... | collective-permute-start | bytes 3145736 | tf_op jit(solution)/shard_map/ppermute | solution.py:311
  14.6 25.5 %collective-permute-start.6 = (bf16[2048,256]{1,0:T(8,128)(2,1)S(1)}, bf16[2048,256]{1,0:T(8,128)(2,1)S(1)}, u32[]{:S(2)}, u32[]{:S(2)}) collective-permute-start(bf16[2048,256]{1,0:T(8,128)(2,1)S(1)} %copy-done.2), channel_id=1, source_target_pairs={{0,8},{4,12},{8,0},{12,4},{16,24},{20,28},{24,16},{28,20},{1,9},{5... | collective-permute-start | bytes 3145736 | tf_op jit(solution)/shard_map/ppermute | solution.py:311
  19.8 9.6 %copy-start.11 = (bf16[2048,256]{1,0:T(8,128)(2,1)S(1)}, bf16[2048,256]{1,0:T(8,128)(2,1)}, u32[]{:S(2)}) copy-start(bf16[2048,256]{1,0:T(8,128)(2,1)} %param.9) | copy-start | bytes 3145732
  29.6 10.6 %collective-permute-start.4 = (bf16[2048,128]{1,0:T(8,128)(2,1)}, bf16[2048,128]{1,0:T(8,128)(2,1)S(1)}, u32[]{:S(2)}, u32[]{:S(2)}) collective-permute-start(bf16[2048,128]{1,0:T(8,128)(2,1)} %compare_select_fusion.1.refs_0_), channel_id=1, source_target_pairs={{1,2},{2,1},{5,6},{6,5},{9,10},{10,9},{13,14},{14,13},{17,18},{18,... | collective-permute-start | bytes 1572872 | tf_op jit(solution)/shard_map/ppermute | solution.py:329
  30.3 14.0 %collective-permute-start.5 = (bf16[2048,128]{1,0:T(8,128)(2,1)}, bf16[2048,128]{1,0:T(8,128)(2,1)S(1)}, u32[]{:S(2)}, u32[]{:S(2)}) collective-permute-start(bf16[2048,128]{1,0:T(8,128)(2,1)} %collective-permute-done.1.refs_2_), channel_id=1, source_target_pairs={{1,0},{2,3},{5,4},{6,7},{9,8},{10,11},{13,12},{14,15},{17,16},{18,... | collective-permute-start | bytes 1572872 | tf_op jit(solution)/shard_map/ppermute | solution.py:329
  44.3 20.8 %collective-permute-start.9 = (bf16[1024,256]{1,0:T(8,128)(2,1)S(1)}, bf16[1024,256]{1,0:T(8,128)(2,1)S(1)}, u32[]{:S(2)}, u32[]{:S(2)}) collective-permute-start(bf16[1024,256]{1,0:T(8,128)(2,1)S(1)} %slice.81), channel_id=1, source_target_pairs={{0,8},{4,12},{8,0},{12,4},{16,24},{20,28},{24,16},{28,20},{1,9},{5... | collective-permute-start | bytes 1572872 | tf_op jit(solution)/shard_map/ppermute | solution.py:311
  45.7 19.3 %collective-permute-start.8 = (bf16[1024,256]{1,0:T(8,128)(2,1)S(1)}, bf16[1024,256]{1,0:T(8,128)(2,1)S(1)}, u32[]{:S(2)}, u32[]{:S(2)}) collective-permute-start(bf16[1024,256]{1,0:T(8,128)(2,1)S(1)} %slice.80), channel_id=1, source_target_pairs={{0,16},{4,20},{8,24},{12,28},{16,0},{20,4},{24,8},{28,12},{1,17},{... | collective-permute-start | bytes 1572872 | tf_op jit(solution)/shard_map/ppermute | solution.py:311
  47.0 24.5 %collective-permute-start.3 = (bf16[2048,128]{1,0:T(8,128)(2,1)S(1)}, bf16[2048,128]{1,0:T(8,128)(2,1)S(1)}, u32[]{:S(2)}, u32[]{:S(2)}) collective-permute-start(bf16[2048,128]{1,0:T(8,128)(2,1)S(1)} %compare_select_fusion.refs_0_), channel_id=1, source_target_pairs={{0,2},{1,3},{2,0},{3,1},{4,6},{5,7},{6,4},{7,5},{8,10},{9,11},{10,... | collective-permute-start | bytes 1572872 | tf_op jit(solution)/shard_map/ppermute | solution.py:311
  49.7 21.8 %collective-permute-start.2 = (bf16[2048,128]{1,0:T(8,128)(2,1)S(1)}, bf16[2048,128]{1,0:T(8,128)(2,1)S(1)}, u32[]{:S(2)}, u32[]{:S(2)}) collective-permute-start(bf16[2048,128]{1,0:T(8,128)(2,1)S(1)} %compare_select_fusion.refs_0_), channel_id=1, source_target_pairs={{0,1},{1,0},{2,3},{3,2},{4,5},{5,4},{6,7},{7,6},{8,9},{9,8},{10,11... | collective-permute-start | bytes 1572872 | tf_op jit(solution)/shard_map/ppermute | solution.py:311
  65.8 14.9 %collective-permute-start.12 = (bf16[2048,128]{1,0:T(8,128)(2,1)S(1)}, bf16[2048,128]{1,0:T(8,128)(2,1)S(1)}, u32[]{:S(2)}, u32[]{:S(2)}) collective-permute-start(bf16[2048,128]{1,0:T(8,128)(2,1)S(1)} %bitcast.51), channel_id=1, source_target_pairs={{0,8},{4,12},{8,0},{12,4},{16,24},{20,28},{24,16},{28,20},{1,9},{5... | collective-permute-start | bytes 1572872 | tf_op jit(solution)/shard_map/ppermute | solution.py:311
  66.2 14.5 %collective-permute-start.13 = (bf16[2048,128]{1,0:T(8,128)(2,1)S(1)}, bf16[2048,128]{1,0:T(8,128)(2,1)S(1)}, u32[]{:S(2)}, u32[]{:S(2)}) collective-permute-start(bf16[2048,128]{1,0:T(8,128)(2,1)S(1)} %bitcast.50), channel_id=1, source_target_pairs={{0,16},{4,20},{8,24},{12,28},{16,0},{20,4},{24,8},{28,12},{1,17},{... | collective-permute-start | bytes 1572872 | tf_op jit(solution)/shard_map/ppermute | solution.py:311
  71.5 11.2 %collective-permute-start.10 = (bf16[2048,128]{1,0:T(8,128)(2,1)S(1)}, bf16[2048,128]{1,0:T(8,128)(2,1)S(1)}, u32[]{:S(2)}, u32[]{:S(2)}) collective-permute-start(bf16[2048,128]{1,0:T(8,128)(2,1)S(1)} %compare_select_fusion.refs_0_), channel_id=1, source_target_pairs={{1,2},{2,1},{5,6},{6,5},{9,10},{10,9},{13,14},{14,13},{17,18},{18,... | collective-permute-start | bytes 1572872 | tf_op jit(solution)/shard_map/ppermute | solution.py:329
  72.2 14.3 %collective-permute-start.11 = (bf16[2048,128]{1,0:T(8,128)(2,1)S(1)}, bf16[2048,128]{1,0:T(8,128)(2,1)S(1)}, u32[]{:S(2)}, u32[]{:S(2)}) collective-permute-start(bf16[2048,128]{1,0:T(8,128)(2,1)S(1)} %collective-permute-done.3.refs_2_), channel_id=1, source_target_pairs={{1,0},{2,3},{5,4},{6,7},{9,8},{10,11},{13,12},{14,15},{17,16},{18,... | collective-permute-start | bytes 1572872 | tf_op jit(solution)/shard_map/ppermute | solution.py:329
  93.8 7.1 %collective-permute-start.14 = (bf16[8192,128]{1,0:T(8,128)(2,1)}, bf16[8192,128]{1,0:T(8,128)(2,1)}, u32[]{:S(2)}, u32[]{:S(2)}) collective-permute-start(bf16[8192,128]{1,0:T(8,128)(2,1)} %get-tuple-element.145), channel_id=1, source_target_pairs={{0,4},{4,0},{8,12},{12,8},{16,20},{20,16},{24,28},{28,24},{1,5},{5... | collective-permute-start | bytes 6291464 | tf_op jit(solution)/shard_map/ppermute | solution.py:311
  96.8 10.9 %collective-permute-start.15 = (bf16[1024,128]{1,0:T(8,128)(2,1)}, bf16[1024,128]{1,0:T(8,128)(2,1)S(1)}, u32[]{:S(2)}, u32[]{:S(2)}) collective-permute-start(bf16[1024,128]{1,0:T(8,128)(2,1)} %get-tuple-element.155), channel_id=1, source_target_pairs={{0,16},{4,20},{8,24},{12,28},{16,0},{20,4},{24,8},{28,12},{1,17},{... | collective-permute-start | bytes 786440 | tf_op jit(solution)/shard_map/ppermute | solution.py:311
  96.8 10.9 %collective-permute-start.16 = (bf16[1024,128]{1,0:T(8,128)(2,1)}, bf16[1024,128]{1,0:T(8,128)(2,1)S(1)}, u32[]{:S(2)}, u32[]{:S(2)}) collective-permute-start(bf16[1024,128]{1,0:T(8,128)(2,1)} %get-tuple-element.156), channel_id=1, source_target_pairs={{0,8},{4,12},{8,0},{12,4},{16,24},{20,28},{24,16},{28,20},{1,9},{5... | collective-permute-start | bytes 786440 | tf_op jit(solution)/shard_map/ppermute | solution.py:311
  107.7 1.3 collective-permute-start.19
  108.2 13.4 %collective-permute-start.17 = (bf16[2048,128]{1,0:T(8,128)(2,1)S(1)}, bf16[2048,128]{1,0:T(8,128)(2,1)S(1)}, u32[]{:S(2)}, u32[]{:S(2)}) collective-permute-start(bf16[2048,128]{1,0:T(8,128)(2,1)S(1)} %bitcast.49), channel_id=1, source_target_pairs={{0,8},{4,12},{8,0},{12,4},{16,24},{20,28},{24,16},{28,20},{1,9},{5... | collective-permute-start | bytes 1572872 | tf_op jit(solution)/shard_map/ppermute | solution.py:311
  108.5 13.1 %collective-permute-start.18 = (bf16[2048,128]{1,0:T(8,128)(2,1)S(1)}, bf16[2048,128]{1,0:T(8,128)(2,1)S(1)}, u32[]{:S(2)}, u32[]{:S(2)}) collective-permute-start(bf16[2048,128]{1,0:T(8,128)(2,1)S(1)} %bitcast.48), channel_id=1, source_target_pairs={{0,16},{4,20},{8,24},{12,28},{16,0},{20,4},{24,8},{28,12},{1,17},{... | collective-permute-start | bytes 1572872 | tf_op jit(solution)/shard_map/ppermute | solution.py:311
  109.1 5.3 %collective-permute-start.22 = (bf16[256,128]{1,0:T(8,128)(2,1)S(1)}, bf16[256,128]{1,0:T(8,128)(2,1)S(1)}, u32[]{:S(2)}, u32[]{:S(2)}) collective-permute-start(bf16[256,128]{1,0:T(8,128)(2,1)S(1)} %add_convert_fusion.12), channel_id=1, source_target_pairs={{0,3},{1,2},{2,1},{3,0},{4,7},{5,6},{6,5},{7,4},{8,11},{9,10},{10,... | collective-permute-start | bytes 196616 | tf_op jit(solution)/shard_map/ppermute | solution.py:311
  112.8 4.5 %collective-permute-start.21 = (bf16[256,128]{1,0:T(8,128)(2,1)S(1)}, bf16[256,128]{1,0:T(8,128)(2,1)S(1)}, u32[]{:S(2)}, u32[]{:S(2)}) collective-permute-start(bf16[256,128]{1,0:T(8,128)(2,1)S(1)} %add_convert_fusion.12), channel_id=1, source_target_pairs={{0,2},{1,3},{2,0},{3,1},{4,6},{5,7},{6,4},{7,5},{8,10},{9,11},{10,... | collective-permute-start | bytes 196616 | tf_op jit(solution)/shard_map/ppermute | solution.py:311
  112.8 4.5 %collective-permute-start.20 = (bf16[256,128]{1,0:T(8,128)(2,1)S(1)}, bf16[256,128]{1,0:T(8,128)(2,1)S(1)}, u32[]{:S(2)}, u32[]{:S(2)}) collective-permute-start(bf16[256,128]{1,0:T(8,128)(2,1)S(1)} %add_convert_fusion.12), channel_id=1, source_target_pairs={{0,1},{1,0},{2,3},{3,2},{4,5},{5,4},{6,7},{7,6},{8,9},{9,8},{10,11... | collective-permute-start | bytes 196616 | tf_op jit(solution)/shard_map/ppermute | solution.py:311
  122.0 6.6 %collective-permute-start.23 = (bf16[1024,128]{1,0:T(8,128)(2,1)S(1)}, bf16[1024,128]{1,0:T(8,128)(2,1)S(1)}, u32[]{:S(2)}, u32[]{:S(2)}) collective-permute-start(bf16[1024,128]{1,0:T(8,128)(2,1)S(1)} %get-tuple-element.172), channel_id=1, source_target_pairs={{0,16},{4,20},{8,24},{12,28},{16,0},{20,4},{24,8},{28,12},{1,17},{... | collective-permute-start | bytes 786440 | tf_op jit(solution)/shard_map/ppermute | solution.py:311
  122.4 6.6 %collective-permute-start.24 = (bf16[1024,128]{1,0:T(8,128)(2,1)S(1)}, bf16[1024,128]{1,0:T(8,128)(2,1)S(1)}, u32[]{:S(2)}, u32[]{:S(2)}) collective-permute-start(bf16[1024,128]{1,0:T(8,128)(2,1)S(1)} %get-tuple-element.174), channel_id=1, source_target_pairs={{0,8},{4,12},{8,0},{12,4},{16,24},{20,28},{24,16},{28,20},{1,9},{5... | collective-permute-start | bytes 786440 | tf_op jit(solution)/shard_map/ppermute | solution.py:311
  123.5 7.1 %collective-permute-start.27 = (bf16[256,128]{1,0:T(8,128)(2,1)S(1)}, bf16[256,128]{1,0:T(8,128)(2,1)S(1)}, u32[]{:S(2)}, u32[]{:S(2)}) collective-permute-start(bf16[256,128]{1,0:T(8,128)(2,1)S(1)} %add_convert_fusion.11), channel_id=1, source_target_pairs={{0,24},{4,28},{8,16},{12,20},{16,8},{20,12},{24,0},{28,4},{1,25},{... | collective-permute-start | bytes 196616 | tf_op jit(solution)/shard_map/ppermute | solution.py:311
  124.7 5.9 %collective-permute-start.26 = (bf16[256,128]{1,0:T(8,128)(2,1)S(1)}, bf16[256,128]{1,0:T(8,128)(2,1)S(1)}, u32[]{:S(2)}, u32[]{:S(2)}) collective-permute-start(bf16[256,128]{1,0:T(8,128)(2,1)S(1)} %add_convert_fusion.11), channel_id=1, source_target_pairs={{0,16},{4,20},{8,24},{12,28},{16,0},{20,4},{24,8},{28,12},{1,17},{... | collective-permute-start | bytes 196616 | tf_op jit(solution)/shard_map/ppermute | solution.py:311
  125.0 6.7 %collective-permute-start.25 = (bf16[256,128]{1,0:T(8,128)(2,1)S(1)}, bf16[256,128]{1,0:T(8,128)(2,1)S(1)}, u32[]{:S(2)}, u32[]{:S(2)}) collective-permute-start(bf16[256,128]{1,0:T(8,128)(2,1)S(1)} %add_convert_fusion.11), channel_id=1, source_target_pairs={{0,8},{4,12},{8,0},{12,4},{16,24},{20,28},{24,16},{28,20},{1,9},{5... | collective-permute-start | bytes 196616 | tf_op jit(solution)/shard_map/ppermute | solution.py:311
  131.8 3.8 %collective-permute-start.28 = (bf16[256,128]{1,0:T(8,128)(2,1)S(1)}, bf16[256,128]{1,0:T(8,128)(2,1)S(1)}, u32[]{:S(2)}, u32[]{:S(2)}) collective-permute-start(bf16[256,128]{1,0:T(8,128)(2,1)S(1)} %add_convert_fusion.10), channel_id=1, source_target_pairs={{0,4},{4,0},{8,12},{12,8},{16,20},{20,16},{24,28},{28,24},{1,5},{5... | collective-permute-start | bytes 196616 | tf_op jit(solution)/shard_map/ppermute | solution.py:311
  (11 other events, 34.5 us)

commit v16 on v13

--- a/solution.py
+++ b/solution.py
@@ -471,6 +471,7 @@
     rows = nodes // 2
     bits = [1 << b for b in range(1, n_row.bit_length() - 1)]
     mid = ((col & 3) == 1) | ((col & 3) == 2)
+    even = (row & 1) == 0
 
     own0, own1 = [
         jnp.where(preact[:, cut] > 0, grad_out[:, cut], jnp.zeros_like(grad_out[:, cut]))
@@ -484,7 +485,7 @@
     near = [[features]]
     for bit in bits[:2]:
         near.append([xor_permute(features, "row", bit)])
-    own0, own1, first0, plan0, plan1, flipped = fence(own0, own1, first0, plan0, plan1, flipped)
+    own0, own1, first0, plan0, plan1, flipped, even = fence(own0, own1, first0, plan0, plan1, flipped, even)
 
     second0 = gather_second(own0, first0[1], n_col)
     acc0 = spmm(plan0, [[own0], [first0[0]], [first0[1]]], flipped, None, n_row)
@@ -521,7 +522,6 @@
     stage1, term0, term1, rest0, recv0 = fence(stage1, term0, term1, rest0, recv0)
 
     recv1 = exchange_first(stage1, bits)
-    even = (row & 1) == 0
     theirs, mine = jnp.where(even, term1, term0), jnp.where(even, term0, term1)
     mine = add_f32(mine, xor_permute(theirs, "row", 1)).astype(jnp.bfloat16)
     mine = sum_over(mine, "col", range(1, n_col)).astype(jnp.bfloat16)

time: 136 us -> 133 us (0.978)
  Pallas kernels: 43.3 us -> 31.5 us
  waiting for transfers between devices: 27.2 us -> 36.1 us
  starting transfers between devices: 35.7 us -> 39.1 us
  local copies, waits for them, and re-layouts: 7.84 us -> 4.77 us
  blocking collectives: 7.15 us -> 9.9 us
  other arithmetic: 7.86 us -> 5.63 us
    pallas_call x4, Pallas kernels: 27.6 us -> 15.8 us  [spmm(): pl.pallas_call(functools.partial(spmm_kernel, [len(p) for p in pieces], l...]
    ppermute x2, waiting for transfers between devices: 6.97 us -> 15 us  [gather_second(): lax.ppermute(by_two, 'col', ends)]
    ppermute x25, starting transfers between devices: 31.8 us -> 35.2 us  [xor_permute(): return lax.ppermute(value, axis, [(i, i ^ mask) for i in range(size)])]
    all_to_all x1, blocking collectives: 7.15 us -> 9.9 us  [swap_cores(): return lax.all_to_all(both, 'row', 0, 0, axis_index_groups=pairs)]
    convert_element_type x2, other arithmetic: 3.31 us -> 1.09 us  [stage_sums(): sums = add_f32(keep, recv).astype(jnp.bfloat16)]
    unnamed x26 -> x12, local copies, waits for them, and re-layouts: 5.44 us -> 4.01 us
  transfers between devices with their start and end apart: 29 -> 29, of which waited for: 13 -> 16; matrix products, arithmetic and copies ran while one was open for 7% -> 5% of each run, Pallas kernels for 28% -> 22%
where the time goes in v16:
time: 133 us; the launch traced here: 132 us
  starting transfers between devices  39.1 us (29%)
  waiting for transfers between devices  36.1 us (27%)
  Pallas kernels  31.5 us (24%)
  blocking collectives  9.9 us (7%)
  other arithmetic  5.63 us (4%)
  local copies, waits for them, and re-layouts  4.77 us (4%)
  matrix products  3.56 us (3%)
  between operations  1.69 us (1%)
    ppermute x25, starting transfers between devices, xor_permute(): return lax.ppermute(value, axis, [(i, i ^ mask) for i in range(size)])  35.2 us
    ppermute x25, waiting for transfers between devices, xor_permute(): return lax.ppermute(value, axis, [(i, i ^ mask) for i in range(size)])  21.1 us
    pallas_call x4, Pallas kernels, spmm(): pl.pallas_call(functools.partial(spmm_kernel, [len(p) for p in pieces], l...  15.8 us
    ppermute x2, waiting for transfers between devices, gather_second(): lax.ppermute(by_two, 'col', ends)  15 us
    all_to_all x1, blocking collectives, swap_cores(): return lax.all_to_all(both, 'row', 0, 0, axis_index_groups=pairs)  9.9 us
    pallas_call x1, Pallas kernels, flip_tiles(): pl.pallas_call(flip_kernel, out_shape=jax.ShapeDtypeStruct((slots + GROUP...  9.59 us
    unnamed x12, local copies, waits for them, and re-layouts  4.01 us
    pallas_call x1, Pallas kernels, weight_term_early(): pl.pallas_call(term_kernel, out_shape=jax.ShapeDtypeStruct(shape, jnp.bfl...  3.79 us
  transfers between devices with their start and end apart: 29, of which 16 were waited for; matrix products, arithmetic and copies ran while one was open for 5% of the time, Pallas kernels for 22%

profile of v16, /device:TPU:1, one launch (start us, length us, event | category | flops | bytes accessed | tf_op | source)
XLA Modules:
  0.0 132.4 jit_solution(10451937989310445056)
XLA Ops:
  0.7 2.7 %compare_select_fusion = (bf16[2048,128]{1,0:T(8,128)(2,1)}, bf16[2048,128]{1,0:T(8,128)(2,1)}) fusion(bf16[2048,256]{1,0:T(8,128)(2,1)} %param.8, bf16[2048,256]{1,0:T(8,128)(2,1)} %param.9), kind=kLoop, calls=%fused_computation.16 | loop fusion | flops 1048576 | bytes 3145728 | tf_op jit(solution)/shard_map/jit(_where)/select_n | solution.py:477
  3.4 3.1 %collective-permute-start.1 = (bf16[2048,128]{1,0:T(8,128)(2,1)}, bf16[2048,128]{1,0:T(8,128)(2,1)}, u32[]{:S(2)}, u32[]{:S(2)}) collective-permute-start(bf16[2048,128]{1,0:T(8,128)(2,1)} %get-tuple-element.95.refs_0_), channel_id=1, source_target_pairs={{0,2},{1,3},{2,0},{3,1},{4,6},{5,7},{6,4},{7,5},{8,10},{9,11},{10,... | collective-permute-start | bytes 1572872 | tf_op jit(solution)/shard_map/ppermute | solution.py:311
  6.5 1.3 collective-permute-start
  8.9 2.3 %plan_slots.1 = (s32[8,512]{1,0:T(8,128)S(1)}, s32[8,512]{1,0:T(8,128)S(1)}, s32[1,320]{1,0:T(1,128)S(1)}) custom-call(s32[4]{0:T(128)S(1)} %pad_add_fusion.place_ref, s32[1,320]{1,0:T(1,128)S(1)} %bitcast.42, s32[1,320]{1,0:T(1,128)S(1)} %bitcast.44, s32[320,1]{1,0:T(8,128)S(1)} %copy.10.rows_c, s32[320,1]{1,0:T(8,128)S(1)} %copy.11.cols_c), custom_call_target="tpu_custom_call" | custom-call | bytes 4096 | tf_op jit(solution)/shard_map/plan_slots/pallas_call | solution.py:122
  11.2 1.3 collective-permute-start.7
  13.7 4.0 %copy-done.1 = bf16[1,1,320,128,128]{4,3,2,1,0:T(8,128)(2,1)S(1)} copy-done((bf16[1,1,320,128,128]{4,3,2,1,0:T(8,128)(2,1)S(1)}, bf16[1,1,320,128,128]{4,3,2,1,0:T(8,128)(2,1)}, u32[]{:S(2)}) %copy-start.1) | copy-done | bytes 10485784
  17.7 9.6 %flip_tiles.1.refs_3_.refs_2_ = bf16[352,128,128]{2,1,0:T(8,128)(2,1)S(1)} custom-call(s32[1,320]{1,0:T(1,128)S(1)} %get-tuple-element.91.slot_ref, bf16[320,128,128]{2,1,0:T(8,128)(2,1)S(1)} %bitcast.40), custom_call_target="tpu_custom_call" | custom-call | bytes 4096 | tf_op jit(solution)/shard_map/flip_tiles/pallas_call | solution.py:165
  27.3 2.5 %collective-permute-done.1.refs_2_ = bf16[2048,128]{1,0:T(8,128)(2,1)} collective-permute-done((bf16[2048,128]{1,0:T(8,128)(2,1)}, bf16[2048,128]{1,0:T(8,128)(2,1)}, u32[]{:S(2)}, u32[]{:S(2)}) %collective-permute-start.1) | collective-permute-done | bytes 524320 | tf_op jit(solution)/shard_map/ppermute | solution.py:311
  30.5 1.3 collective-permute-start.5
  31.8 5.8 %spmm_first.2 = (bf16[8192,128]{1,0:T(8,128)(2,1)S(1)}, bf16[8192,128]{1,0:T(8,128)(2,1)S(1)}) custom-call(s32[8,512]{1,0:T(8,128)S(1)} %get-tuple-element.94.plan_ref, bf16[2048,128]{1,0:T(8,128)(2,1)} %get-tuple-element.95.refs_0_, bf16[2048,128]{1,0:T(8,128)(2,1)} %collective-permute-done.refs_1_, bf16[2048,128]{1,0:T(8,128)(2,1)} %collective-permute-done.1.refs_2_, ...), custom_call_target="tpu_custom_call" | custom-call | bytes 4096 | tf_op jit(solution)/shard_map/spmm_first/pallas_call | solution.py:288
  37.6 7.4 %collective-permute-done.5.refs_1_ = bf16[2048,128]{1,0:T(8,128)(2,1)S(1)} collective-permute-done((bf16[2048,128]{1,0:T(8,128)(2,1)}, bf16[2048,128]{1,0:T(8,128)(2,1)S(1)}, u32[]{:S(2)}, u32[]{:S(2)}) %collective-permute-start.5) | collective-permute-done | bytes 524320 | tf_op jit(solution)/shard_map/ppermute | solution.py:329
  47.6 2.7 %collective-permute-start.3 = (bf16[2048,128]{1,0:T(8,128)(2,1)S(1)}, bf16[2048,128]{1,0:T(8,128)(2,1)S(1)}, u32[]{:S(2)}, u32[]{:S(2)}) collective-permute-start(bf16[2048,128]{1,0:T(8,128)(2,1)S(1)} %copy-done.3), channel_id=1, source_target_pairs={{0,2},{1,3},{2,0},{3,1},{4,6},{5,7},{6,4},{7,5},{8,10},{9,11},{10,... | collective-permute-start | bytes 1572872 | tf_op jit(solution)/shard_map/ppermute | solution.py:311
  50.3 2.1 %collective-permute-start.2 = (bf16[2048,128]{1,0:T(8,128)(2,1)S(1)}, bf16[2048,128]{1,0:T(8,128)(2,1)S(1)}, u32[]{:S(2)}, u32[]{:S(2)}) collective-permute-start(bf16[2048,128]{1,0:T(8,128)(2,1)S(1)} %copy-done.3), channel_id=1, source_target_pairs={{0,1},{1,0},{2,3},{3,2},{4,5},{5,4},{6,7},{7,6},{8,9},{9,8},{10,11... | collective-permute-start | bytes 1572872 | tf_op jit(solution)/shard_map/ppermute | solution.py:311
  52.4 2.7 %spmm_last.2 = bf16[2,8192,128]{2,1,0:T(8,128)(2,1)S(1)} custom-call(s32[8,512]{1,0:T(8,128)S(1)} %get-tuple-element.92.plan_ref, bf16[2048,128]{1,0:T(8,128)(2,1)S(1)} %collective-permute-done.4.refs_0_, bf16[2048,128]{1,0:T(8,128)(2,1)S(1)} %collective-permute-done.5.refs_1_, bf16[352,128,128]{2,1,0:T(8,128)(2,1)S(1)} %flip_tiles.1.refs_3_.refs_2_, ...), custom_call_target="tpu_custom_call" | custom-call | bytes 4096 | tf_op jit(solution)/shard_map/spmm_last/pallas_call | solution.py:288
  55.1 9.9 %all_to_all.5 = bf16[2,8192,128]{2,1,0:T(8,128)(2,1)S(1)} all-to-all(bf16[2,8192,128]{2,1,0:T(8,128)(2,1)S(1)} %spmm_last.2), channel_id=1, replica_groups={{0,4},{8,12},{16,20},{24,28},{1,5},{9,13},{17,21},{25,29},{2,6},{10,14}..., dimensions={0} | all-to-all | bytes 8388608 | tf_op jit(solution)/shard_map/all_to_all | solution.py:343
  65.8 1.5 %collective-permute-start.13 = (bf16[2048,128]{1,0:T(8,128)(2,1)S(1)}, bf16[2048,128]{1,0:T(8,128)(2,1)S(1)}, u32[]{:S(2)}, u32[]{:S(2)}) collective-permute-start(bf16[2048,128]{1,0:T(8,128)(2,1)S(1)} %bitcast.55), channel_id=1, source_target_pairs={{0,16},{4,20},{8,24},{12,28},{16,0},{20,4},{24,8},{28,12},{1,17},{... | collective-permute-start | bytes 1572872 | tf_op jit(solution)/shard_map/ppermute | solution.py:311
  67.3 3.8 %weight_term.1 = bf16[256,128]{1,0:T(8,128)(2,1)S(1)} custom-call(bf16[2048,256]{1,0:T(8,128)(2,1)S(1)} %copy-done.2, bf16[2048,256]{1,0:T(8,128)(2,1)S(1)} %collective-permute-done.6.refs_1_, bf16[2048,256]{1,0:T(8,128)(2,1)S(1)} %collective-permute-done.7.refs_2_, bf16[1024,256]{1,0:T(8,128)(2,1)S(1)} %collective-permute-done.8.refs_3_, ...), custom_call_target="tpu_custom_call" | custom-call | bytes 4096 | tf_op jit(solution)/shard_map/weight_term/pallas_call | solution.py:448
  72.8 1.3 collective-permute-start.11
  74.1 4.4 %spmm_first.3 = (bf16[8192,128]{1,0:T(8,128)(2,1)S(1)}, bf16[8192,128]{1,0:T(8,128)(2,1)S(1)}) custom-call(s32[8,512]{1,0:T(8,128)S(1)} %get-tuple-element.94.plan_ref, bf16[2048,128]{1,0:T(8,128)(2,1)S(1)} %copy-done.3, bf16[2048,128]{1,0:T(8,128)(2,1)S(1)} %collective-permute-done.2.refs_1_, bf16[2048,128]{1,0:T(8,128)(2,1)S(1)} %collective-permute-done.3.refs_2_, ...), custom_call_target="tpu_custom_call" | custom-call | bytes 4096 | tf_op jit(solution)/shard_map/spmm_first/pallas_call | solution.py:288
  79.4 7.7 %collective-permute-done.11.refs_1_ = bf16[2048,128]{1,0:T(8,128)(2,1)S(1)} collective-permute-done((bf16[2048,128]{1,0:T(8,128)(2,1)S(1)}, bf16[2048,128]{1,0:T(8,128)(2,1)S(1)}, u32[]{:S(2)}, u32[]{:S(2)}) %collective-permute-start.11) | collective-permute-done | bytes 524320 | tf_op jit(solution)/shard_map/ppermute | solution.py:329
  87.1 2.9 %spmm_last.3 = (bf16[8192,128]{1,0:T(8,128)(2,1)S(1)}, bf16[8192,128]{1,0:T(8,128)(2,1)S(1)}) custom-call(s32[8,512]{1,0:T(8,128)S(1)} %get-tuple-element.92.plan_ref, bf16[2048,128]{1,0:T(8,128)(2,1)S(1)} %collective-permute-done.10.refs_0_, bf16[2048,128]{1,0:T(8,128)(2,1)S(1)} %collective-permute-done.11.refs_1_, ...), custom_call_target="tpu_custom_call" | custom-call | bytes 4096 | tf_op jit(solution)/shard_map/spmm_last/pallas_call | solution.py:288
  89.9 4.2 %collective-permute-start.14 = (bf16[8192,128]{1,0:T(8,128)(2,1)S(1)}, bf16[8192,128]{1,0:T(8,128)(2,1)S(1)}, u32[]{:S(2)}, u32[]{:S(2)}) collective-permute-start(bf16[8192,128]{1,0:T(8,128)(2,1)S(1)} %get-tuple-element.140), channel_id=1, source_target_pairs={{0,4},{4,0},{8,12},{12,8},{16,20},{20,16},{24,28},{28,24},{1,5},{5... | collective-permute-start | bytes 6291464 | tf_op jit(solution)/shard_map/ppermute | solution.py:311
  94.1 1.5 %collective-permute-start.16 = (bf16[1024,128]{1,0:T(8,128)(2,1)S(1)}, bf16[1024,128]{1,0:T(8,128)(2,1)S(1)}, u32[]{:S(2)}, u32[]{:S(2)}) collective-permute-start(bf16[1024,128]{1,0:T(8,128)(2,1)S(1)} %get-tuple-element.151), channel_id=1, source_target_pairs={{0,8},{4,12},{8,0},{12,4},{16,24},{20,28},{24,16},{28,20},{1,9},{5... | collective-permute-start | bytes 786440 | tf_op jit(solution)/shard_map/ppermute | solution.py:311
  95.6 2.3 %collective-permute-done.14 = bf16[8192,128]{1,0:T(8,128)(2,1)S(1)} collective-permute-done((bf16[8192,128]{1,0:T(8,128)(2,1)S(1)}, bf16[8192,128]{1,0:T(8,128)(2,1)S(1)}, u32[]{:S(2)}, u32[]{:S(2)}) %collective-permute-start.14) | collective-permute-done | bytes 2097184 | tf_op jit(solution)/shard_map/ppermute | solution.py:311
  103.0 1.5 %collective-permute-start.17 = (bf16[2048,128]{1,0:T(8,128)(2,1)S(1)}, bf16[2048,128]{1,0:T(8,128)(2,1)S(1)}, u32[]{:S(2)}, u32[]{:S(2)}) collective-permute-start(bf16[2048,128]{1,0:T(8,128)(2,1)S(1)} %bitcast.53), channel_id=1, source_target_pairs={{0,8},{4,12},{8,0},{12,4},{16,24},{20,28},{24,16},{28,20},{1,9},{5... | collective-permute-start | bytes 1572872 | tf_op jit(solution)/shard_map/ppermute | solution.py:311
  104.7 4.4 %collective-permute-start.22 = (bf16[256,128]{1,0:T(8,128)(2,1)S(1)}, bf16[256,128]{1,0:T(8,128)(2,1)S(1)}, u32[]{:S(2)}, u32[]{:S(2)}) collective-permute-start(bf16[256,128]{1,0:T(8,128)(2,1)S(1)} %add_convert_fusion.12), channel_id=1, source_target_pairs={{0,3},{1,2},{2,1},{3,0},{4,7},{5,6},{6,5},{7,4},{8,11},{9,10},{10,... | collective-permute-start | bytes 196616 | tf_op jit(solution)/shard_map/ppermute | solution.py:311
  110.7 2.9 %collective-permute-done.21 = bf16[256,128]{1,0:T(8,128)(2,1)S(1)} collective-permute-done((bf16[256,128]{1,0:T(8,128)(2,1)S(1)}, bf16[256,128]{1,0:T(8,128)(2,1)S(1)}, u32[]{:S(2)}, u32[]{:S(2)}) %collective-permute-start.21) | collective-permute-done | bytes 65568 | tf_op jit(solution)/shard_map/ppermute | solution.py:311
  113.6 2.9 %collective-permute-done.17 = bf16[2048,128]{1,0:T(8,128)(2,1)S(1)} collective-permute-done((bf16[2048,128]{1,0:T(8,128)(2,1)S(1)}, bf16[2048,128]{1,0:T(8,128)(2,1)S(1)}, u32[]{:S(2)}, u32[]{:S(2)}) %collective-permute-start.17) | collective-permute-done | bytes 524320 | tf_op jit(solution)/shard_map/ppermute | solution.py:311
  122.1 2.6 %collective-permute-done.23 = bf16[1024,128]{1,0:T(8,128)(2,1)S(1)} collective-permute-done((bf16[1024,128]{1,0:T(8,128)(2,1)S(1)}, bf16[1024,128]{1,0:T(8,128)(2,1)S(1)}, u32[]{:S(2)}, u32[]{:S(2)}) %collective-permute-start.23) | collective-permute-done | bytes 262176 | tf_op jit(solution)/shard_map/ppermute | solution.py:311
  125.1 1.6 %collective-permute-done.27 = bf16[256,128]{1,0:T(8,128)(2,1)S(1)} collective-permute-done((bf16[256,128]{1,0:T(8,128)(2,1)S(1)}, bf16[256,128]{1,0:T(8,128)(2,1)S(1)}, u32[]{:S(2)}, u32[]{:S(2)}) %collective-permute-start.27) | collective-permute-done | bytes 65568 | tf_op jit(solution)/shard_map/ppermute | solution.py:311
  127.8 2.4 %collective-permute-start.28 = (bf16[256,128]{1,0:T(8,128)(2,1)S(1)}, bf16[256,128]{1,0:T(8,128)(2,1)S(1)}, u32[]{:S(2)}, u32[]{:S(2)}) collective-permute-start(bf16[256,128]{1,0:T(8,128)(2,1)S(1)} %add_convert_fusion.10), channel_id=1, source_target_pairs={{0,4},{4,0},{8,12},{12,8},{16,20},{20,16},{24,28},{28,24},{1,5},{5... | collective-permute-start | bytes 196616 | tf_op jit(solution)/shard_map/ppermute | solution.py:311
  130.2 1.4 %convolution_convert_fusion = bf16[2048,256]{1,0:T(8,128)(2,1)} fusion(bf16[256,256]{1,0:T(8,128)(2,1)S(1)} %copy-done, bf16[2048,128]{1,0:T(8,128)(2,1)S(1)} %pad_maximum_fusion.1, bf16[2048,128]{1,0:T(8,128)(2,1)S(1)} %pad_maximum_fusion), kind=kOutput, calls=%fused_computation.2 | convolution fusion | flops 271056896 | bytes 2228224 | tf_op jit(solution)/shard_map/dot_general | solution.py:543
  (83 shorter events, 22.9 us)
Async XLA Ops:
  0.6 129.6 %copy-start = (bf16[256,256]{1,0:T(8,128)(2,1)S(1)}, bf16[256,256]{1,0:T(8,128)(2,1)}, u32[]{:S(2)}) copy-start(bf16[256,256]{1,0:T(8,128)(2,1)} %param.11) | copy-start | bytes 393220
  0.7 10.5 %copy-start.2 = (bf16[2048,256]{1,0:T(8,128)(2,1)S(1)}, bf16[2048,256]{1,0:T(8,128)(2,1)}, u32[]{:S(2)}) copy-start(bf16[2048,256]{1,0:T(8,128)(2,1)} %refs_0_) | copy-start | bytes 3145732
  3.4 26.4 %collective-permute-start.1 = (bf16[2048,128]{1,0:T(8,128)(2,1)}, bf16[2048,128]{1,0:T(8,128)(2,1)}, u32[]{:S(2)}, u32[]{:S(2)}) collective-permute-start(bf16[2048,128]{1,0:T(8,128)(2,1)} %get-tuple-element.95.refs_0_), channel_id=1, source_target_pairs={{0,2},{1,3},{2,0},{3,1},{4,6},{5,7},{6,4},{7,5},{8,10},{9,11},{10,... | collective-permute-start | bytes 1572872 | tf_op jit(solution)/shard_map/ppermute | solution.py:311
  6.5 23.2 %collective-permute-start = (bf16[2048,128]{1,0:T(8,128)(2,1)}, bf16[2048,128]{1,0:T(8,128)(2,1)}, u32[]{:S(2)}, u32[]{:S(2)}) collective-permute-start(bf16[2048,128]{1,0:T(8,128)(2,1)} %get-tuple-element.95.refs_0_), channel_id=1, source_target_pairs={{0,1},{1,0},{2,3},{3,2},{4,5},{5,4},{6,7},{7,6},{8,9},{9,8},{10,11... | collective-permute-start | bytes 1572872 | tf_op jit(solution)/shard_map/ppermute | solution.py:311
  11.2 26.4 %collective-permute-start.7 = (bf16[2048,256]{1,0:T(8,128)(2,1)S(1)}, bf16[2048,256]{1,0:T(8,128)(2,1)S(1)}, u32[]{:S(2)}, u32[]{:S(2)}) collective-permute-start(bf16[2048,256]{1,0:T(8,128)(2,1)S(1)} %copy-done.2), channel_id=1, source_target_pairs={{0,16},{4,20},{8,24},{12,28},{16,0},{20,4},{24,8},{28,12},{1,17},{... | collective-permute-start | bytes 3145736 | tf_op jit(solution)/shard_map/ppermute | solution.py:311
  12.5 25.1 %collective-permute-start.6 = (bf16[2048,256]{1,0:T(8,128)(2,1)S(1)}, bf16[2048,256]{1,0:T(8,128)(2,1)S(1)}, u32[]{:S(2)}, u32[]{:S(2)}) collective-permute-start(bf16[2048,256]{1,0:T(8,128)(2,1)S(1)} %copy-done.2), channel_id=1, source_target_pairs={{0,8},{4,12},{8,0},{12,4},{16,24},{20,28},{24,16},{28,20},{1,9},{5... | collective-permute-start | bytes 3145736 | tf_op jit(solution)/shard_map/ppermute | solution.py:311
  29.8 7.8 %collective-permute-start.4 = (bf16[2048,128]{1,0:T(8,128)(2,1)}, bf16[2048,128]{1,0:T(8,128)(2,1)S(1)}, u32[]{:S(2)}, u32[]{:S(2)}) collective-permute-start(bf16[2048,128]{1,0:T(8,128)(2,1)} %get-tuple-element.95.refs_0_), channel_id=1, source_target_pairs={{1,2},{2,1},{5,6},{6,5},{9,10},{10,9},{13,14},{14,13},{17,18},{18,... | collective-permute-start | bytes 1572872 | tf_op jit(solution)/shard_map/ppermute | solution.py:329
  30.5 14.5 %collective-permute-start.5 = (bf16[2048,128]{1,0:T(8,128)(2,1)}, bf16[2048,128]{1,0:T(8,128)(2,1)S(1)}, u32[]{:S(2)}, u32[]{:S(2)}) collective-permute-start(bf16[2048,128]{1,0:T(8,128)(2,1)} %collective-permute-done.1.refs_2_), channel_id=1, source_target_pairs={{1,0},{2,3},{5,4},{6,7},{9,8},{10,11},{13,12},{14,15},{17,16},{18,... | collective-permute-start | bytes 1572872 | tf_op jit(solution)/shard_map/ppermute | solution.py:329
  37.5 10.0 %copy-start.3 = (bf16[2048,128]{1,0:T(8,128)(2,1)S(1)}, bf16[2048,128]{1,0:T(8,128)(2,1)}, u32[]{:S(2)}) copy-start(bf16[2048,128]{1,0:T(8,128)(2,1)} %get-tuple-element.118.refs_0_) | copy-start | bytes 1572868
  45.0 20.0 %collective-permute-start.9 = (bf16[1024,256]{1,0:T(8,128)(2,1)S(1)}, bf16[1024,256]{1,0:T(8,128)(2,1)S(1)}, u32[]{:S(2)}, u32[]{:S(2)}) collective-permute-start(bf16[1024,256]{1,0:T(8,128)(2,1)S(1)} %slice.96), channel_id=1, source_target_pairs={{0,8},{4,12},{8,0},{12,4},{16,24},{20,28},{24,16},{28,20},{1,9},{5... | collective-permute-start | bytes 1572872 | tf_op jit(solution)/shard_map/ppermute | solution.py:311
  46.3 18.7 %collective-permute-start.8 = (bf16[1024,256]{1,0:T(8,128)(2,1)S(1)}, bf16[1024,256]{1,0:T(8,128)(2,1)S(1)}, u32[]{:S(2)}, u32[]{:S(2)}) collective-permute-start(bf16[1024,256]{1,0:T(8,128)(2,1)S(1)} %slice.95), channel_id=1, source_target_pairs={{0,16},{4,20},{8,24},{12,28},{16,0},{20,4},{24,8},{28,12},{1,17},{... | collective-permute-start | bytes 1572872 | tf_op jit(solution)/shard_map/ppermute | solution.py:311
  47.6 24.5 %collective-permute-start.3 = (bf16[2048,128]{1,0:T(8,128)(2,1)S(1)}, bf16[2048,128]{1,0:T(8,128)(2,1)S(1)}, u32[]{:S(2)}, u32[]{:S(2)}) collective-permute-start(bf16[2048,128]{1,0:T(8,128)(2,1)S(1)} %copy-done.3), channel_id=1, source_target_pairs={{0,2},{1,3},{2,0},{3,1},{4,6},{5,7},{6,4},{7,5},{8,10},{9,11},{10,... | collective-permute-start | bytes 1572872 | tf_op jit(solution)/shard_map/ppermute | solution.py:311
  50.3 21.8 %collective-permute-start.2 = (bf16[2048,128]{1,0:T(8,128)(2,1)S(1)}, bf16[2048,128]{1,0:T(8,128)(2,1)S(1)}, u32[]{:S(2)}, u32[]{:S(2)}) collective-permute-start(bf16[2048,128]{1,0:T(8,128)(2,1)S(1)} %copy-done.3), channel_id=1, source_target_pairs={{0,1},{1,0},{2,3},{3,2},{4,5},{5,4},{6,7},{7,6},{8,9},{9,8},{10,11... | collective-permute-start | bytes 1572872 | tf_op jit(solution)/shard_map/ppermute | solution.py:311
  65.7 13.2 %collective-permute-start.12 = (bf16[2048,128]{1,0:T(8,128)(2,1)S(1)}, bf16[2048,128]{1,0:T(8,128)(2,1)S(1)}, u32[]{:S(2)}, u32[]{:S(2)}) collective-permute-start(bf16[2048,128]{1,0:T(8,128)(2,1)S(1)} %bitcast.56), channel_id=1, source_target_pairs={{0,8},{4,12},{8,0},{12,4},{16,24},{20,28},{24,16},{28,20},{1,9},{5... | collective-permute-start | bytes 1572872 | tf_op jit(solution)/shard_map/ppermute | solution.py:311
  65.8 13.2 %collective-permute-start.13 = (bf16[2048,128]{1,0:T(8,128)(2,1)S(1)}, bf16[2048,128]{1,0:T(8,128)(2,1)S(1)}, u32[]{:S(2)}, u32[]{:S(2)}) collective-permute-start(bf16[2048,128]{1,0:T(8,128)(2,1)S(1)} %bitcast.55), channel_id=1, source_target_pairs={{0,16},{4,20},{8,24},{12,28},{16,0},{20,4},{24,8},{28,12},{1,17},{... | collective-permute-start | bytes 1572872 | tf_op jit(solution)/shard_map/ppermute | solution.py:311
  72.1 7.3 %collective-permute-start.10 = (bf16[2048,128]{1,0:T(8,128)(2,1)S(1)}, bf16[2048,128]{1,0:T(8,128)(2,1)S(1)}, u32[]{:S(2)}, u32[]{:S(2)}) collective-permute-start(bf16[2048,128]{1,0:T(8,128)(2,1)S(1)} %copy-done.3), channel_id=1, source_target_pairs={{1,2},{2,1},{5,6},{6,5},{9,10},{10,9},{13,14},{14,13},{17,18},{18,... | collective-permute-start | bytes 1572872 | tf_op jit(solution)/shard_map/ppermute | solution.py:329
  72.8 14.3 %collective-permute-start.11 = (bf16[2048,128]{1,0:T(8,128)(2,1)S(1)}, bf16[2048,128]{1,0:T(8,128)(2,1)S(1)}, u32[]{:S(2)}, u32[]{:S(2)}) collective-permute-start(bf16[2048,128]{1,0:T(8,128)(2,1)S(1)} %collective-permute-done.3.refs_2_), channel_id=1, source_target_pairs={{1,0},{2,3},{5,4},{6,7},{9,8},{10,11},{13,12},{14,15},{17,16},{18,... | collective-permute-start | bytes 1572872 | tf_op jit(solution)/shard_map/ppermute | solution.py:329
  89.9 7.9 %collective-permute-start.14 = (bf16[8192,128]{1,0:T(8,128)(2,1)S(1)}, bf16[8192,128]{1,0:T(8,128)(2,1)S(1)}, u32[]{:S(2)}, u32[]{:S(2)}) collective-permute-start(bf16[8192,128]{1,0:T(8,128)(2,1)S(1)} %get-tuple-element.140), channel_id=1, source_target_pairs={{0,4},{4,0},{8,12},{12,8},{16,20},{20,16},{24,28},{28,24},{1,5},{5... | collective-permute-start | bytes 6291464 | tf_op jit(solution)/shard_map/ppermute | solution.py:311
  94.1 7.9 %collective-permute-start.15 = (bf16[1024,128]{1,0:T(8,128)(2,1)S(1)}, bf16[1024,128]{1,0:T(8,128)(2,1)S(1)}, u32[]{:S(2)}, u32[]{:S(2)}) collective-permute-start(bf16[1024,128]{1,0:T(8,128)(2,1)S(1)} %get-tuple-element.150), channel_id=1, source_target_pairs={{0,16},{4,20},{8,24},{12,28},{16,0},{20,4},{24,8},{28,12},{1,17},{... | collective-permute-start | bytes 786440 | tf_op jit(solution)/shard_map/ppermute | solution.py:311
  94.1 7.9 %collective-permute-start.16 = (bf16[1024,128]{1,0:T(8,128)(2,1)S(1)}, bf16[1024,128]{1,0:T(8,128)(2,1)S(1)}, u32[]{:S(2)}, u32[]{:S(2)}) collective-permute-start(bf16[1024,128]{1,0:T(8,128)(2,1)S(1)} %get-tuple-element.151), channel_id=1, source_target_pairs={{0,8},{4,12},{8,0},{12,4},{16,24},{20,28},{24,16},{28,20},{1,9},{5... | collective-permute-start | bytes 786440 | tf_op jit(solution)/shard_map/ppermute | solution.py:311
  102.0 2.6 %collective-permute-start.19 = (bf16[256,128]{1,0:T(8,128)(2,1)S(1)}, bf16[256,128]{1,0:T(8,128)(2,1)S(1)}, u32[]{:S(2)}, u32[]{:S(2)}) collective-permute-start(bf16[256,128]{1,0:T(8,128)(2,1)S(1)} %broadcast_select_fusion.2), channel_id=1, source_target_pairs={{0,4},{4,0},{8,12},{12,8},{16,20},{20,16},{24,28},{28,24},{1,5},{5... | collective-permute-start | bytes 196616 | tf_op jit(solution)/shard_map/ppermute | solution.py:311
  103.0 13.5 %collective-permute-start.17 = (bf16[2048,128]{1,0:T(8,128)(2,1)S(1)}, bf16[2048,128]{1,0:T(8,128)(2,1)S(1)}, u32[]{:S(2)}, u32[]{:S(2)}) collective-permute-start(bf16[2048,128]{1,0:T(8,128)(2,1)S(1)} %bitcast.53), channel_id=1, source_target_pairs={{0,8},{4,12},{8,0},{12,4},{16,24},{20,28},{24,16},{28,20},{1,9},{5... | collective-permute-start | bytes 1572872 | tf_op jit(solution)/shard_map/ppermute | solution.py:311
  104.4 13.2 %collective-permute-start.18 = (bf16[2048,128]{1,0:T(8,128)(2,1)S(1)}, bf16[2048,128]{1,0:T(8,128)(2,1)S(1)}, u32[]{:S(2)}, u32[]{:S(2)}) collective-permute-start(bf16[2048,128]{1,0:T(8,128)(2,1)S(1)} %bitcast.54), channel_id=1, source_target_pairs={{0,16},{4,20},{8,24},{12,28},{16,0},{20,4},{24,8},{28,12},{1,17},{... | collective-permute-start | bytes 1572872 | tf_op jit(solution)/shard_map/ppermute | solution.py:311
  104.7 6.0 %collective-permute-start.22 = (bf16[256,128]{1,0:T(8,128)(2,1)S(1)}, bf16[256,128]{1,0:T(8,128)(2,1)S(1)}, u32[]{:S(2)}, u32[]{:S(2)}) collective-permute-start(bf16[256,128]{1,0:T(8,128)(2,1)S(1)} %add_convert_fusion.12), channel_id=1, source_target_pairs={{0,3},{1,2},{2,1},{3,0},{4,7},{5,6},{6,5},{7,4},{8,11},{9,10},{10,... | collective-permute-start | bytes 196616 | tf_op jit(solution)/shard_map/ppermute | solution.py:311
  109.0 4.5 %collective-permute-start.21 = (bf16[256,128]{1,0:T(8,128)(2,1)S(1)}, bf16[256,128]{1,0:T(8,128)(2,1)S(1)}, u32[]{:S(2)}, u32[]{:S(2)}) collective-permute-start(bf16[256,128]{1,0:T(8,128)(2,1)S(1)} %add_convert_fusion.12), channel_id=1, source_target_pairs={{0,2},{1,3},{2,0},{3,1},{4,6},{5,7},{6,4},{7,5},{8,10},{9,11},{10,... | collective-permute-start | bytes 196616 | tf_op jit(solution)/shard_map/ppermute | solution.py:311
  109.0 4.5 %collective-permute-start.20 = (bf16[256,128]{1,0:T(8,128)(2,1)S(1)}, bf16[256,128]{1,0:T(8,128)(2,1)S(1)}, u32[]{:S(2)}, u32[]{:S(2)}) collective-permute-start(bf16[256,128]{1,0:T(8,128)(2,1)S(1)} %add_convert_fusion.12), channel_id=1, source_target_pairs={{0,1},{1,0},{2,3},{3,2},{4,5},{5,4},{6,7},{7,6},{8,9},{9,8},{10,11... | collective-permute-start | bytes 196616 | tf_op jit(solution)/shard_map/ppermute | solution.py:311
  118.0 6.7 %collective-permute-start.23 = (bf16[1024,128]{1,0:T(8,128)(2,1)S(1)}, bf16[1024,128]{1,0:T(8,128)(2,1)S(1)}, u32[]{:S(2)}, u32[]{:S(2)}) collective-permute-start(bf16[1024,128]{1,0:T(8,128)(2,1)S(1)} %get-tuple-element.168), channel_id=1, source_target_pairs={{0,16},{4,20},{8,24},{12,28},{16,0},{20,4},{24,8},{28,12},{1,17},{... | collective-permute-start | bytes 786440 | tf_op jit(solution)/shard_map/ppermute | solution.py:311
  118.3 6.6 %collective-permute-start.24 = (bf16[1024,128]{1,0:T(8,128)(2,1)S(1)}, bf16[1024,128]{1,0:T(8,128)(2,1)S(1)}, u32[]{:S(2)}, u32[]{:S(2)}) collective-permute-start(bf16[1024,128]{1,0:T(8,128)(2,1)S(1)} %get-tuple-element.170), channel_id=1, source_target_pairs={{0,8},{4,12},{8,0},{12,4},{16,24},{20,28},{24,16},{28,20},{1,9},{5... | collective-permute-start | bytes 786440 | tf_op jit(solution)/shard_map/ppermute | solution.py:311
  119.5 7.2 %collective-permute-start.27 = (bf16[256,128]{1,0:T(8,128)(2,1)S(1)}, bf16[256,128]{1,0:T(8,128)(2,1)S(1)}, u32[]{:S(2)}, u32[]{:S(2)}) collective-permute-start(bf16[256,128]{1,0:T(8,128)(2,1)S(1)} %add_convert_fusion.11), channel_id=1, source_target_pairs={{0,24},{4,28},{8,16},{12,20},{16,8},{20,12},{24,0},{28,4},{1,25},{... | collective-permute-start | bytes 196616 | tf_op jit(solution)/shard_map/ppermute | solution.py:311
  120.7 6.0 %collective-permute-start.26 = (bf16[256,128]{1,0:T(8,128)(2,1)S(1)}, bf16[256,128]{1,0:T(8,128)(2,1)S(1)}, u32[]{:S(2)}, u32[]{:S(2)}) collective-permute-start(bf16[256,128]{1,0:T(8,128)(2,1)S(1)} %add_convert_fusion.11), channel_id=1, source_target_pairs={{0,16},{4,20},{8,24},{12,28},{16,0},{20,4},{24,8},{28,12},{1,17},{... | collective-permute-start | bytes 196616 | tf_op jit(solution)/shard_map/ppermute | solution.py:311
  121.0 6.8 %collective-permute-start.25 = (bf16[256,128]{1,0:T(8,128)(2,1)S(1)}, bf16[256,128]{1,0:T(8,128)(2,1)S(1)}, u32[]{:S(2)}, u32[]{:S(2)}) collective-permute-start(bf16[256,128]{1,0:T(8,128)(2,1)S(1)} %add_convert_fusion.11), channel_id=1, source_target_pairs={{0,8},{4,12},{8,0},{12,4},{16,24},{20,28},{24,16},{28,20},{1,9},{5... | collective-permute-start | bytes 196616 | tf_op jit(solution)/shard_map/ppermute | solution.py:311
  127.8 3.8 %collective-permute-start.28 = (bf16[256,128]{1,0:T(8,128)(2,1)S(1)}, bf16[256,128]{1,0:T(8,128)(2,1)S(1)}, u32[]{:S(2)}, u32[]{:S(2)}) collective-permute-start(bf16[256,128]{1,0:T(8,128)(2,1)S(1)} %add_convert_fusion.10), channel_id=1, source_target_pairs={{0,4},{4,0},{8,12},{12,8},{16,20},{20,16},{24,28},{28,24},{1,5},{5... | collective-permute-start | bytes 196616 | tf_op jit(solution)/shard_map/ppermute | solution.py:311
  (3 other events, 19.8 us)

commit v17 on v16

--- a/solution.py
+++ b/solution.py
@@ -510,16 +510,15 @@
     acc1 = spmm(plan0, pieces1[:FIRST_PIECES], flipped, None, n_row)
     acc1, recv0 = fence(acc1, recv0)
     rest0, sent0 = exchange_second(stage0, recv0, bits, rows)
-    pieces1, acc1, rest0, sent0 = fence(pieces1, acc1, rest0, sent0)
+    recv0 = send_second(sent0, bits)
+    pieces1, acc1 = fence(pieces1, acc1)
 
     send1, keep1 = spmm(plan1, pieces1[FIRST_PIECES:], flipped, acc1, n_row)
-    send1, keep1, rest0, sent0 = fence(send1, keep1, rest0, sent0)
+    send1, keep1, rest0, recv0 = fence(send1, keep1, rest0, recv0)
 
     stage1, sums1 = stage_sums(keep1, xor_permute(send1, "row", 1), n_row // 2, rows, at_once=True)
-    recv0 = send_second(sent0, bits)
     term1 = weight_term(near, sums1)
     stage1, term0, term1 = fence(stage1, term0, term1)
-    stage1, term0, term1, rest0, recv0 = fence(stage1, term0, term1, rest0, recv0)
 
     recv1 = exchange_first(stage1, bits)
     theirs, mine = jnp.where(even, term1, term0), jnp.where(even, term0, term1)

time: 133 us -> 131 us (0.985)
  Pallas kernels: 31.5 us -> 40.7 us
  starting transfers between devices: 39.1 us -> 33.7 us
  waiting for transfers between devices: 36.1 us -> 31 us
    pallas_call x4, Pallas kernels: 15.8 us -> 25 us  [spmm(): pl.pallas_call(functools.partial(spmm_kernel, [len(p) for p in pieces], l...]
    ppermute x2, waiting for transfers between devices: 15 us -> 7.66 us  [gather_second(): lax.ppermute(by_two, 'col', ends)]
    ppermute x25, starting transfers between devices: 35.2 us -> 29.7 us  [xor_permute(): return lax.ppermute(value, axis, [(i, i ^ mask) for i in range(size)])]
    ppermute x25, waiting for transfers between devices: 21.1 us -> 23.3 us  [xor_permute(): return lax.ppermute(value, axis, [(i, i ^ mask) for i in range(size)])]
  transfers between devices with their start and end apart: 29 -> 29, of which waited for: 16 -> 14; matrix products, arithmetic and copies ran while one was open for 5% -> 2% of each run, Pallas kernels for 22% -> 31%
where the time goes in v17:
time: 131 us; the launch traced here: 130 us
  Pallas kernels  40.7 us (31%)
  starting transfers between devices  33.7 us (26%)
  waiting for transfers between devices  31 us (24%)
  blocking collectives  9.08 us (7%)
  other arithmetic  5.63 us (4%)
  local copies, waits for them, and re-layouts  4.77 us (4%)
  matrix products  3.55 us (3%)
  between operations  1.74 us (1%)
    ppermute x25, starting transfers between devices, xor_permute(): return lax.ppermute(value, axis, [(i, i ^ mask) for i in range(size)])  29.7 us
    pallas_call x4, Pallas kernels, spmm(): pl.pallas_call(functools.partial(spmm_kernel, [len(p) for p in pieces], l...  25 us
    ppermute x25, waiting for transfers between devices, xor_permute(): return lax.ppermute(value, axis, [(i, i ^ mask) for i in range(size)])  23.3 us
    pallas_call x1, Pallas kernels, flip_tiles(): pl.pallas_call(flip_kernel, out_shape=jax.ShapeDtypeStruct((slots + GROUP...  9.59 us
    all_to_all x1, blocking collectives, swap_cores(): return lax.all_to_all(both, 'row', 0, 0, axis_index_groups=pairs)  9.08 us
    ppermute x2, waiting for transfers between devices, gather_second(): lax.ppermute(by_two, 'col', ends)  7.66 us
    unnamed x12, local copies, waits for them, and re-layouts  4.01 us
    pallas_call x1, Pallas kernels, weight_term_early(): pl.pallas_call(term_kernel, out_shape=jax.ShapeDtypeStruct(shape, jnp.bfl...  3.8 us
  transfers between devices with their start and end apart: 29, of which 14 were waited for; matrix products, arithmetic and copies ran while one was open for 2% of the time, Pallas kernels for 31%

profile of v17, /device:TPU:1, one launch (start us, length us, event | category | flops | bytes accessed | tf_op | source)
XLA Modules:
  0.0 130.2 jit_solution(11356700852069451229)
XLA Ops:
  0.7 2.7 %compare_select_fusion = (bf16[2048,128]{1,0:T(8,128)(2,1)}, bf16[2048,128]{1,0:T(8,128)(2,1)}) fusion(bf16[2048,256]{1,0:T(8,128)(2,1)} %param.8, bf16[2048,256]{1,0:T(8,128)(2,1)} %param.9), kind=kLoop, calls=%fused_computation.16 | loop fusion | flops 1048576 | bytes 3145728 | tf_op jit(solution)/shard_map/jit(_where)/select_n | solution.py:477
  3.4 3.1 %collective-permute-start.1 = (bf16[2048,128]{1,0:T(8,128)(2,1)}, bf16[2048,128]{1,0:T(8,128)(2,1)}, u32[]{:S(2)}, u32[]{:S(2)}) collective-permute-start(bf16[2048,128]{1,0:T(8,128)(2,1)} %get-tuple-element.81.refs_0_), channel_id=1, source_target_pairs={{0,2},{1,3},{2,0},{3,1},{4,6},{5,7},{6,4},{7,5},{8,10},{9,11},{10,... | collective-permute-start | bytes 1572872 | tf_op jit(solution)/shard_map/ppermute | solution.py:311
  6.5 1.3 collective-permute-start
  8.9 2.3 %plan_slots.1 = (s32[8,512]{1,0:T(8,128)S(1)}, s32[8,512]{1,0:T(8,128)S(1)}, s32[1,320]{1,0:T(1,128)S(1)}) custom-call(s32[4]{0:T(128)S(1)} %pad_add_fusion.place_ref, s32[1,320]{1,0:T(1,128)S(1)} %bitcast.42, s32[1,320]{1,0:T(1,128)S(1)} %bitcast.44, s32[320,1]{1,0:T(8,128)S(1)} %copy.10.rows_c, s32[320,1]{1,0:T(8,128)S(1)} %copy.11.cols_c), custom_call_target="tpu_custom_call" | custom-call | bytes 4096 | tf_op jit(solution)/shard_map/plan_slots/pallas_call | solution.py:122
  11.2 1.3 %collective-permute-start.7 = (bf16[2048,256]{1,0:T(8,128)(2,1)S(1)}, bf16[2048,256]{1,0:T(8,128)(2,1)S(1)}, u32[]{:S(2)}, u32[]{:S(2)}) collective-permute-start(bf16[2048,256]{1,0:T(8,128)(2,1)S(1)} %copy-done.2), channel_id=1, source_target_pairs={{0,16},{4,20},{8,24},{12,28},{16,0},{20,4},{24,8},{28,12},{1,17},{... | collective-permute-start | bytes 3145736 | tf_op jit(solution)/shard_map/ppermute | solution.py:311
  13.7 4.0 %copy-done.1 = bf16[1,1,320,128,128]{4,3,2,1,0:T(8,128)(2,1)S(1)} copy-done((bf16[1,1,320,128,128]{4,3,2,1,0:T(8,128)(2,1)S(1)}, bf16[1,1,320,128,128]{4,3,2,1,0:T(8,128)(2,1)}, u32[]{:S(2)}) %copy-start.1) | copy-done | bytes 10485784
  17.7 9.6 %flip_tiles.1.refs_3_.refs_2_ = bf16[352,128,128]{2,1,0:T(8,128)(2,1)S(1)} custom-call(s32[1,320]{1,0:T(1,128)S(1)} %get-tuple-element.77.slot_ref, bf16[320,128,128]{2,1,0:T(8,128)(2,1)S(1)} %bitcast.40), custom_call_target="tpu_custom_call" | custom-call | bytes 4096 | tf_op jit(solution)/shard_map/flip_tiles/pallas_call | solution.py:165
  27.3 2.5 %collective-permute-done.1.refs_2_ = bf16[2048,128]{1,0:T(8,128)(2,1)} collective-permute-done((bf16[2048,128]{1,0:T(8,128)(2,1)}, bf16[2048,128]{1,0:T(8,128)(2,1)}, u32[]{:S(2)}, u32[]{:S(2)}) %collective-permute-start.1) | collective-permute-done | bytes 524320 | tf_op jit(solution)/shard_map/ppermute | solution.py:311
  30.5 1.3 collective-permute-start.5
  31.8 8.9 %spmm_first.2 = (bf16[8192,128]{1,0:T(8,128)(2,1)S(1)}, bf16[8192,128]{1,0:T(8,128)(2,1)S(1)}) custom-call(s32[8,512]{1,0:T(8,128)S(1)} %get-tuple-element.80.plan_ref, bf16[2048,128]{1,0:T(8,128)(2,1)} %get-tuple-element.81.refs_0_, bf16[2048,128]{1,0:T(8,128)(2,1)} %collective-permute-done.refs_1_, bf16[2048,128]{1,0:T(8,128)(2,1)} %collective-permute-done.1.refs_2_, ...), custom_call_target="tpu_custom_call" | custom-call | bytes 4096 | tf_op jit(solution)/shard_map/spmm_first/pallas_call | solution.py:288
  40.7 4.2 %collective-permute-done.5.refs_1_ = bf16[2048,128]{1,0:T(8,128)(2,1)S(1)} collective-permute-done((bf16[2048,128]{1,0:T(8,128)(2,1)}, bf16[2048,128]{1,0:T(8,128)(2,1)S(1)}, u32[]{:S(2)}, u32[]{:S(2)}) %collective-permute-start.5) | collective-permute-done | bytes 524320 | tf_op jit(solution)/shard_map/ppermute | solution.py:329
  47.6 2.7 %collective-permute-start.3 = (bf16[2048,128]{1,0:T(8,128)(2,1)S(1)}, bf16[2048,128]{1,0:T(8,128)(2,1)S(1)}, u32[]{:S(2)}, u32[]{:S(2)}) collective-permute-start(bf16[2048,128]{1,0:T(8,128)(2,1)S(1)} %copy-done.3), channel_id=1, source_target_pairs={{0,2},{1,3},{2,0},{3,1},{4,6},{5,7},{6,4},{7,5},{8,10},{9,11},{10,... | collective-permute-start | bytes 1572872 | tf_op jit(solution)/shard_map/ppermute | solution.py:311
  50.3 2.1 %collective-permute-start.2 = (bf16[2048,128]{1,0:T(8,128)(2,1)S(1)}, bf16[2048,128]{1,0:T(8,128)(2,1)S(1)}, u32[]{:S(2)}, u32[]{:S(2)}) collective-permute-start(bf16[2048,128]{1,0:T(8,128)(2,1)S(1)} %copy-done.3), channel_id=1, source_target_pairs={{0,1},{1,0},{2,3},{3,2},{4,5},{5,4},{6,7},{7,6},{8,9},{9,8},{10,11... | collective-permute-start | bytes 1572872 | tf_op jit(solution)/shard_map/ppermute | solution.py:311
  52.4 4.2 %spmm_last.2 = bf16[2,8192,128]{2,1,0:T(8,128)(2,1)S(1)} custom-call(s32[8,512]{1,0:T(8,128)S(1)} %get-tuple-element.78.plan_ref, bf16[2048,128]{1,0:T(8,128)(2,1)S(1)} %collective-permute-done.4.refs_0_, bf16[2048,128]{1,0:T(8,128)(2,1)S(1)} %collective-permute-done.5.refs_1_, bf16[352,128,128]{2,1,0:T(8,128)(2,1)S(1)} %flip_tiles.1.refs_3_.refs_2_, ...), custom_call_target="tpu_custom_call" | custom-call | bytes 4096 | tf_op jit(solution)/shard_map/spmm_last/pallas_call | solution.py:288
  56.6 9.1 %all_to_all.5 = bf16[2,8192,128]{2,1,0:T(8,128)(2,1)S(1)} all-to-all(bf16[2,8192,128]{2,1,0:T(8,128)(2,1)S(1)} %spmm_last.2), channel_id=1, replica_groups={{0,4},{8,12},{16,20},{24,28},{1,5},{9,13},{17,21},{25,29},{2,6},{10,14}..., dimensions={0} | all-to-all | bytes 8388608 | tf_op jit(solution)/shard_map/all_to_all | solution.py:343
  66.5 3.8 %weight_term.1 = bf16[256,128]{1,0:T(8,128)(2,1)S(1)} custom-call(bf16[2048,256]{1,0:T(8,128)(2,1)S(1)} %copy-done.2, bf16[2048,256]{1,0:T(8,128)(2,1)S(1)} %collective-permute-done.6.refs_1_, bf16[2048,256]{1,0:T(8,128)(2,1)S(1)} %collective-permute-done.7.refs_2_, bf16[1024,256]{1,0:T(8,128)(2,1)S(1)} %collective-permute-done.8.refs_3_, ...), custom_call_target="tpu_custom_call" | custom-call | bytes 4096 | tf_op jit(solution)/shard_map/weight_term/pallas_call | solution.py:448
  70.3 1.8 %collective-permute-done.3.refs_2_ = bf16[2048,128]{1,0:T(8,128)(2,1)S(1)} collective-permute-done((bf16[2048,128]{1,0:T(8,128)(2,1)S(1)}, bf16[2048,128]{1,0:T(8,128)(2,1)S(1)}, u32[]{:S(2)}, u32[]{:S(2)}) %collective-permute-start.3) | collective-permute-done | bytes 524320 | tf_op jit(solution)/shard_map/ppermute | solution.py:311
  72.8 1.3 collective-permute-start.11
  74.1 7.6 %spmm_first.3 = (bf16[8192,128]{1,0:T(8,128)(2,1)S(1)}, bf16[8192,128]{1,0:T(8,128)(2,1)S(1)}) custom-call(s32[8,512]{1,0:T(8,128)S(1)} %get-tuple-element.80.plan_ref, bf16[2048,128]{1,0:T(8,128)(2,1)S(1)} %copy-done.3, bf16[2048,128]{1,0:T(8,128)(2,1)S(1)} %collective-permute-done.2.refs_1_, bf16[2048,128]{1,0:T(8,128)(2,1)S(1)} %collective-permute-done.3.refs_2_, ...), custom_call_target="tpu_custom_call" | custom-call | bytes 4096 | tf_op jit(solution)/shard_map/spmm_first/pallas_call | solution.py:288
  82.2 1.4 %collective-permute-start.14 = (bf16[1024,128]{1,0:T(8,128)(2,1)S(1)}, bf16[1024,128]{1,0:T(8,128)(2,1)S(1)}, u32[]{:S(2)}, u32[]{:S(2)}) collective-permute-start(bf16[1024,128]{1,0:T(8,128)(2,1)S(1)} %get-tuple-element.162), channel_id=1, source_target_pairs={{0,16},{4,20},{8,24},{12,28},{16,0},{20,4},{24,8},{28,12},{1,17},{... | collective-permute-start | bytes 786440 | tf_op jit(solution)/shard_map/ppermute | solution.py:311
  83.6 3.4 %collective-permute-done.11.refs_1_ = bf16[2048,128]{1,0:T(8,128)(2,1)S(1)} collective-permute-done((bf16[2048,128]{1,0:T(8,128)(2,1)S(1)}, bf16[2048,128]{1,0:T(8,128)(2,1)S(1)}, u32[]{:S(2)}, u32[]{:S(2)}) %collective-permute-start.11) | collective-permute-done | bytes 524320 | tf_op jit(solution)/shard_map/ppermute | solution.py:329
  87.1 4.3 %spmm_last.3 = (bf16[8192,128]{1,0:T(8,128)(2,1)S(1)}, bf16[8192,128]{1,0:T(8,128)(2,1)S(1)}) custom-call(s32[8,512]{1,0:T(8,128)S(1)} %get-tuple-element.78.plan_ref, bf16[2048,128]{1,0:T(8,128)(2,1)S(1)} %collective-permute-done.10.refs_0_, bf16[2048,128]{1,0:T(8,128)(2,1)S(1)} %collective-permute-done.11.refs_1_, ...), custom_call_target="tpu_custom_call" | custom-call | bytes 4096 | tf_op jit(solution)/shard_map/spmm_last/pallas_call | solution.py:288
  91.4 3.3 %collective-permute-start.16 = (bf16[8192,128]{1,0:T(8,128)(2,1)S(1)}, bf16[8192,128]{1,0:T(8,128)(2,1)S(1)}, u32[]{:S(2)}, u32[]{:S(2)}) collective-permute-start(bf16[8192,128]{1,0:T(8,128)(2,1)S(1)} %get-tuple-element.122), channel_id=1, source_target_pairs={{0,4},{4,0},{8,12},{12,8},{16,20},{20,16},{24,28},{28,24},{1,5},{5... | collective-permute-start | bytes 6291464 | tf_op jit(solution)/shard_map/ppermute | solution.py:311
  94.8 3.7 %collective-permute-done.16 = bf16[8192,128]{1,0:T(8,128)(2,1)S(1)} collective-permute-done((bf16[8192,128]{1,0:T(8,128)(2,1)S(1)}, bf16[8192,128]{1,0:T(8,128)(2,1)S(1)}, u32[]{:S(2)}, u32[]{:S(2)}) %collective-permute-start.16) | collective-permute-done | bytes 2097184 | tf_op jit(solution)/shard_map/ppermute | solution.py:311
  102.8 3.1 %collective-permute-start.22 = (bf16[256,128]{1,0:T(8,128)(2,1)S(1)}, bf16[256,128]{1,0:T(8,128)(2,1)S(1)}, u32[]{:S(2)}, u32[]{:S(2)}) collective-permute-start(bf16[256,128]{1,0:T(8,128)(2,1)S(1)} %add_convert_fusion.12), channel_id=1, source_target_pairs={{0,3},{1,2},{2,1},{3,0},{4,7},{5,6},{6,5},{7,4},{8,11},{9,10},{10,... | collective-permute-start | bytes 196616 | tf_op jit(solution)/shard_map/ppermute | solution.py:311
  106.4 1.4 %collective-permute-done.22 = bf16[256,128]{1,0:T(8,128)(2,1)S(1)} collective-permute-done((bf16[256,128]{1,0:T(8,128)(2,1)S(1)}, bf16[256,128]{1,0:T(8,128)(2,1)S(1)}, u32[]{:S(2)}, u32[]{:S(2)}) %collective-permute-start.22) | collective-permute-done | bytes 65568 | tf_op jit(solution)/shard_map/ppermute | solution.py:311
  107.8 4.9 %collective-permute-done.21 = bf16[256,128]{1,0:T(8,128)(2,1)S(1)} collective-permute-done((bf16[256,128]{1,0:T(8,128)(2,1)S(1)}, bf16[256,128]{1,0:T(8,128)(2,1)S(1)}, u32[]{:S(2)}, u32[]{:S(2)}) %collective-permute-start.21) | collective-permute-done | bytes 65568 | tf_op jit(solution)/shard_map/ppermute | solution.py:311
  112.8 2.5 %collective-permute-done.17 = bf16[2048,128]{1,0:T(8,128)(2,1)S(1)} collective-permute-done((bf16[2048,128]{1,0:T(8,128)(2,1)S(1)}, bf16[2048,128]{1,0:T(8,128)(2,1)S(1)}, u32[]{:S(2)}, u32[]{:S(2)}) %collective-permute-start.17) | collective-permute-done | bytes 524320 | tf_op jit(solution)/shard_map/ppermute | solution.py:311
  119.9 2.8 %collective-permute-done.23 = bf16[1024,128]{1,0:T(8,128)(2,1)S(1)} collective-permute-done((bf16[1024,128]{1,0:T(8,128)(2,1)S(1)}, bf16[1024,128]{1,0:T(8,128)(2,1)S(1)}, u32[]{:S(2)}, u32[]{:S(2)}) %collective-permute-start.23) | collective-permute-done | bytes 262176 | tf_op jit(solution)/shard_map/ppermute | solution.py:311
  123.1 1.6 %collective-permute-done.27 = bf16[256,128]{1,0:T(8,128)(2,1)S(1)} collective-permute-done((bf16[256,128]{1,0:T(8,128)(2,1)S(1)}, bf16[256,128]{1,0:T(8,128)(2,1)S(1)}, u32[]{:S(2)}, u32[]{:S(2)}) %collective-permute-start.27) | collective-permute-done | bytes 65568 | tf_op jit(solution)/shard_map/ppermute | solution.py:311
  125.8 2.2 %collective-permute-start.28 = (bf16[256,128]{1,0:T(8,128)(2,1)S(1)}, bf16[256,128]{1,0:T(8,128)(2,1)S(1)}, u32[]{:S(2)}, u32[]{:S(2)}) collective-permute-start(bf16[256,128]{1,0:T(8,128)(2,1)S(1)} %add_convert_fusion.10), channel_id=1, source_target_pairs={{0,4},{4,0},{8,12},{12,8},{16,20},{20,16},{24,28},{28,24},{1,5},{5... | collective-permute-start | bytes 196616 | tf_op jit(solution)/shard_map/ppermute | solution.py:311
  128.0 1.4 %convolution_convert_fusion = bf16[2048,256]{1,0:T(8,128)(2,1)} fusion(bf16[256,256]{1,0:T(8,128)(2,1)S(1)} %copy-done, bf16[2048,128]{1,0:T(8,128)(2,1)S(1)} %pad_maximum_fusion.1, bf16[2048,128]{1,0:T(8,128)(2,1)S(1)} %pad_maximum_fusion), kind=kOutput, calls=%fused_computation.2 | convolution fusion | flops 271056896 | bytes 2228224 | tf_op jit(solution)/shard_map/dot_general | solution.py:542
  (83 shorter events, 18.4 us)
Async XLA Ops:
  0.6 127.4 %copy-start = (bf16[256,256]{1,0:T(8,128)(2,1)S(1)}, bf16[256,256]{1,0:T(8,128)(2,1)}, u32[]{:S(2)}) copy-start(bf16[256,256]{1,0:T(8,128)(2,1)} %param.11) | copy-start | bytes 393220
  0.7 8.0 %copy-start.4 = (s32[1,1,320]{2,1,0:T(1,128)S(1)}, s32[1,1,320]{2,1,0:T(1,128)}, u32[]{:S(2)}) copy-start(s32[1,1,320]{2,1,0:T(1,128)} %param.13) | copy-start | bytes 3844
  0.7 10.5 %copy-start.2 = (bf16[2048,256]{1,0:T(8,128)(2,1)S(1)}, bf16[2048,256]{1,0:T(8,128)(2,1)}, u32[]{:S(2)}) copy-start(bf16[2048,256]{1,0:T(8,128)(2,1)} %refs_0_) | copy-start | bytes 3145732
  3.4 26.4 %collective-permute-start.1 = (bf16[2048,128]{1,0:T(8,128)(2,1)}, bf16[2048,128]{1,0:T(8,128)(2,1)}, u32[]{:S(2)}, u32[]{:S(2)}) collective-permute-start(bf16[2048,128]{1,0:T(8,128)(2,1)} %get-tuple-element.81.refs_0_), channel_id=1, source_target_pairs={{0,2},{1,3},{2,0},{3,1},{4,6},{5,7},{6,4},{7,5},{8,10},{9,11},{10,... | collective-permute-start | bytes 1572872 | tf_op jit(solution)/shard_map/ppermute | solution.py:311
  6.5 23.2 %collective-permute-start = (bf16[2048,128]{1,0:T(8,128)(2,1)}, bf16[2048,128]{1,0:T(8,128)(2,1)}, u32[]{:S(2)}, u32[]{:S(2)}) collective-permute-start(bf16[2048,128]{1,0:T(8,128)(2,1)} %get-tuple-element.81.refs_0_), channel_id=1, source_target_pairs={{0,1},{1,0},{2,3},{3,2},{4,5},{5,4},{6,7},{7,6},{8,9},{9,8},{10,11... | collective-permute-start | bytes 1572872 | tf_op jit(solution)/shard_map/ppermute | solution.py:311
  11.2 29.5 %collective-permute-start.7 = (bf16[2048,256]{1,0:T(8,128)(2,1)S(1)}, bf16[2048,256]{1,0:T(8,128)(2,1)S(1)}, u32[]{:S(2)}, u32[]{:S(2)}) collective-permute-start(bf16[2048,256]{1,0:T(8,128)(2,1)S(1)} %copy-done.2), channel_id=1, source_target_pairs={{0,16},{4,20},{8,24},{12,28},{16,0},{20,4},{24,8},{28,12},{1,17},{... | collective-permute-start | bytes 3145736 | tf_op jit(solution)/shard_map/ppermute | solution.py:311
  12.5 28.2 %collective-permute-start.6 = (bf16[2048,256]{1,0:T(8,128)(2,1)S(1)}, bf16[2048,256]{1,0:T(8,128)(2,1)S(1)}, u32[]{:S(2)}, u32[]{:S(2)}) collective-permute-start(bf16[2048,256]{1,0:T(8,128)(2,1)S(1)} %copy-done.2), channel_id=1, source_target_pairs={{0,8},{4,12},{8,0},{12,4},{16,24},{20,28},{24,16},{28,20},{1,9},{5... | collective-permute-start | bytes 3145736 | tf_op jit(solution)/shard_map/ppermute | solution.py:311
  29.8 11.0 %collective-permute-start.4 = (bf16[2048,128]{1,0:T(8,128)(2,1)}, bf16[2048,128]{1,0:T(8,128)(2,1)S(1)}, u32[]{:S(2)}, u32[]{:S(2)}) collective-permute-start(bf16[2048,128]{1,0:T(8,128)(2,1)} %get-tuple-element.81.refs_0_), channel_id=1, source_target_pairs={{1,2},{2,1},{5,6},{6,5},{9,10},{10,9},{13,14},{14,13},{17,18},{18,... | collective-permute-start | bytes 1572872 | tf_op jit(solution)/shard_map/ppermute | solution.py:329
  30.5 14.5 %collective-permute-start.5 = (bf16[2048,128]{1,0:T(8,128)(2,1)}, bf16[2048,128]{1,0:T(8,128)(2,1)S(1)}, u32[]{:S(2)}, u32[]{:S(2)}) collective-permute-start(bf16[2048,128]{1,0:T(8,128)(2,1)} %collective-permute-done.1.refs_2_), channel_id=1, source_target_pairs={{1,0},{2,3},{5,4},{6,7},{9,8},{10,11},{13,12},{14,15},{17,16},{18,... | collective-permute-start | bytes 1572872 | tf_op jit(solution)/shard_map/ppermute | solution.py:329
  45.0 20.6 %collective-permute-start.9 = (bf16[1024,256]{1,0:T(8,128)(2,1)S(1)}, bf16[1024,256]{1,0:T(8,128)(2,1)S(1)}, u32[]{:S(2)}, u32[]{:S(2)}) collective-permute-start(bf16[1024,256]{1,0:T(8,128)(2,1)S(1)} %slice.96), channel_id=1, source_target_pairs={{0,8},{4,12},{8,0},{12,4},{16,24},{20,28},{24,16},{28,20},{1,9},{5... | collective-permute-start | bytes 1572872 | tf_op jit(solution)/shard_map/ppermute | solution.py:311
  46.3 19.3 %collective-permute-start.8 = (bf16[1024,256]{1,0:T(8,128)(2,1)S(1)}, bf16[1024,256]{1,0:T(8,128)(2,1)S(1)}, u32[]{:S(2)}, u32[]{:S(2)}) collective-permute-start(bf16[1024,256]{1,0:T(8,128)(2,1)S(1)} %slice.95), channel_id=1, source_target_pairs={{0,16},{4,20},{8,24},{12,28},{16,0},{20,4},{24,8},{28,12},{1,17},{... | collective-permute-start | bytes 1572872 | tf_op jit(solution)/shard_map/ppermute | solution.py:311
  47.6 24.5 %collective-permute-start.3 = (bf16[2048,128]{1,0:T(8,128)(2,1)S(1)}, bf16[2048,128]{1,0:T(8,128)(2,1)S(1)}, u32[]{:S(2)}, u32[]{:S(2)}) collective-permute-start(bf16[2048,128]{1,0:T(8,128)(2,1)S(1)} %copy-done.3), channel_id=1, source_target_pairs={{0,2},{1,3},{2,0},{3,1},{4,6},{5,7},{6,4},{7,5},{8,10},{9,11},{10,... | collective-permute-start | bytes 1572872 | tf_op jit(solution)/shard_map/ppermute | solution.py:311
  50.3 21.8 %collective-permute-start.2 = (bf16[2048,128]{1,0:T(8,128)(2,1)S(1)}, bf16[2048,128]{1,0:T(8,128)(2,1)S(1)}, u32[]{:S(2)}, u32[]{:S(2)}) collective-permute-start(bf16[2048,128]{1,0:T(8,128)(2,1)S(1)} %copy-done.3), channel_id=1, source_target_pairs={{0,1},{1,0},{2,3},{3,2},{4,5},{5,4},{6,7},{7,6},{8,9},{9,8},{10,11... | collective-permute-start | bytes 1572872 | tf_op jit(solution)/shard_map/ppermute | solution.py:311
  66.4 15.3 %collective-permute-start.12 = (bf16[2048,128]{1,0:T(8,128)(2,1)S(1)}, bf16[2048,128]{1,0:T(8,128)(2,1)S(1)}, u32[]{:S(2)}, u32[]{:S(2)}) collective-permute-start(bf16[2048,128]{1,0:T(8,128)(2,1)S(1)} %bitcast.56), channel_id=1, source_target_pairs={{0,8},{4,12},{8,0},{12,4},{16,24},{20,28},{24,16},{28,20},{1,9},{5... | collective-permute-start | bytes 1572872 | tf_op jit(solution)/shard_map/ppermute | solution.py:311
  66.4 15.3 %collective-permute-start.13 = (bf16[2048,128]{1,0:T(8,128)(2,1)S(1)}, bf16[2048,128]{1,0:T(8,128)(2,1)S(1)}, u32[]{:S(2)}, u32[]{:S(2)}) collective-permute-start(bf16[2048,128]{1,0:T(8,128)(2,1)S(1)} %bitcast.55), channel_id=1, source_target_pairs={{0,16},{4,20},{8,24},{12,28},{16,0},{20,4},{24,8},{28,12},{1,17},{... | collective-permute-start | bytes 1572872 | tf_op jit(solution)/shard_map/ppermute | solution.py:311
  72.1 11.5 %collective-permute-start.10 = (bf16[2048,128]{1,0:T(8,128)(2,1)S(1)}, bf16[2048,128]{1,0:T(8,128)(2,1)S(1)}, u32[]{:S(2)}, u32[]{:S(2)}) collective-permute-start(bf16[2048,128]{1,0:T(8,128)(2,1)S(1)} %copy-done.3), channel_id=1, source_target_pairs={{1,2},{2,1},{5,6},{6,5},{9,10},{10,9},{13,14},{14,13},{17,18},{18,... | collective-permute-start | bytes 1572872 | tf_op jit(solution)/shard_map/ppermute | solution.py:329
  72.8 14.3 %collective-permute-start.11 = (bf16[2048,128]{1,0:T(8,128)(2,1)S(1)}, bf16[2048,128]{1,0:T(8,128)(2,1)S(1)}, u32[]{:S(2)}, u32[]{:S(2)}) collective-permute-start(bf16[2048,128]{1,0:T(8,128)(2,1)S(1)} %collective-permute-done.3.refs_2_), channel_id=1, source_target_pairs={{1,0},{2,3},{5,4},{6,7},{9,8},{10,11},{13,12},{14,15},{17,16},{18,... | collective-permute-start | bytes 1572872 | tf_op jit(solution)/shard_map/ppermute | solution.py:329
  82.0 9.3 %collective-permute-start.15 = (bf16[1024,128]{1,0:T(8,128)(2,1)S(1)}, bf16[1024,128]{1,0:T(8,128)(2,1)S(1)}, u32[]{:S(2)}, u32[]{:S(2)}) collective-permute-start(bf16[1024,128]{1,0:T(8,128)(2,1)S(1)} %get-tuple-element.160), channel_id=1, source_target_pairs={{0,8},{4,12},{8,0},{12,4},{16,24},{20,28},{24,16},{28,20},{1,9},{5... | collective-permute-start | bytes 786440 | tf_op jit(solution)/shard_map/ppermute | solution.py:311
  82.2 9.2 %collective-permute-start.14 = (bf16[1024,128]{1,0:T(8,128)(2,1)S(1)}, bf16[1024,128]{1,0:T(8,128)(2,1)S(1)}, u32[]{:S(2)}, u32[]{:S(2)}) collective-permute-start(bf16[1024,128]{1,0:T(8,128)(2,1)S(1)} %get-tuple-element.162), channel_id=1, source_target_pairs={{0,16},{4,20},{8,24},{12,28},{16,0},{20,4},{24,8},{28,12},{1,17},{... | collective-permute-start | bytes 786440 | tf_op jit(solution)/shard_map/ppermute | solution.py:311
  91.4 7.1 %collective-permute-start.16 = (bf16[8192,128]{1,0:T(8,128)(2,1)S(1)}, bf16[8192,128]{1,0:T(8,128)(2,1)S(1)}, u32[]{:S(2)}, u32[]{:S(2)}) collective-permute-start(bf16[8192,128]{1,0:T(8,128)(2,1)S(1)} %get-tuple-element.122), channel_id=1, source_target_pairs={{0,4},{4,0},{8,12},{12,8},{16,20},{20,16},{24,28},{28,24},{1,5},{5... | collective-permute-start | bytes 6291464 | tf_op jit(solution)/shard_map/ppermute | solution.py:311
  101.4 1.3 %collective-permute-start.19 = (bf16[256,128]{1,0:T(8,128)(2,1)S(1)}, bf16[256,128]{1,0:T(8,128)(2,1)S(1)}, u32[]{:S(2)}, u32[]{:S(2)}) collective-permute-start(bf16[256,128]{1,0:T(8,128)(2,1)S(1)} %broadcast_select_fusion.2), channel_id=1, source_target_pairs={{0,4},{4,0},{8,12},{12,8},{16,20},{20,16},{24,28},{28,24},{1,5},{5... | collective-permute-start | bytes 196616 | tf_op jit(solution)/shard_map/ppermute | solution.py:311
  101.9 13.4 %collective-permute-start.17 = (bf16[2048,128]{1,0:T(8,128)(2,1)S(1)}, bf16[2048,128]{1,0:T(8,128)(2,1)S(1)}, u32[]{:S(2)}, u32[]{:S(2)}) collective-permute-start(bf16[2048,128]{1,0:T(8,128)(2,1)S(1)} %bitcast.54), channel_id=1, source_target_pairs={{0,8},{4,12},{8,0},{12,4},{16,24},{20,28},{24,16},{28,20},{1,9},{5... | collective-permute-start | bytes 1572872 | tf_op jit(solution)/shard_map/ppermute | solution.py:311
  102.0 13.4 %collective-permute-start.18 = (bf16[2048,128]{1,0:T(8,128)(2,1)S(1)}, bf16[2048,128]{1,0:T(8,128)(2,1)S(1)}, u32[]{:S(2)}, u32[]{:S(2)}) collective-permute-start(bf16[2048,128]{1,0:T(8,128)(2,1)S(1)} %bitcast.53), channel_id=1, source_target_pairs={{0,16},{4,20},{8,24},{12,28},{16,0},{20,4},{24,8},{28,12},{1,17},{... | collective-permute-start | bytes 1572872 | tf_op jit(solution)/shard_map/ppermute | solution.py:311
  102.8 5.1 %collective-permute-start.22 = (bf16[256,128]{1,0:T(8,128)(2,1)S(1)}, bf16[256,128]{1,0:T(8,128)(2,1)S(1)}, u32[]{:S(2)}, u32[]{:S(2)}) collective-permute-start(bf16[256,128]{1,0:T(8,128)(2,1)S(1)} %add_convert_fusion.12), channel_id=1, source_target_pairs={{0,3},{1,2},{2,1},{3,0},{4,7},{5,6},{6,5},{7,4},{8,11},{9,10},{10,... | collective-permute-start | bytes 196616 | tf_op jit(solution)/shard_map/ppermute | solution.py:311
  105.9 6.9 %collective-permute-start.21 = (bf16[256,128]{1,0:T(8,128)(2,1)S(1)}, bf16[256,128]{1,0:T(8,128)(2,1)S(1)}, u32[]{:S(2)}, u32[]{:S(2)}) collective-permute-start(bf16[256,128]{1,0:T(8,128)(2,1)S(1)} %add_convert_fusion.12), channel_id=1, source_target_pairs={{0,2},{1,3},{2,0},{3,1},{4,6},{5,7},{6,4},{7,5},{8,10},{9,11},{10,... | collective-permute-start | bytes 196616 | tf_op jit(solution)/shard_map/ppermute | solution.py:311
  106.1 6.6 %collective-permute-start.20 = (bf16[256,128]{1,0:T(8,128)(2,1)S(1)}, bf16[256,128]{1,0:T(8,128)(2,1)S(1)}, u32[]{:S(2)}, u32[]{:S(2)}) collective-permute-start(bf16[256,128]{1,0:T(8,128)(2,1)S(1)} %add_convert_fusion.12), channel_id=1, source_target_pairs={{0,1},{1,0},{2,3},{3,2},{4,5},{5,4},{6,7},{7,6},{8,9},{9,8},{10,11... | collective-permute-start | bytes 196616 | tf_op jit(solution)/shard_map/ppermute | solution.py:311
  115.8 6.9 %collective-permute-start.23 = (bf16[1024,128]{1,0:T(8,128)(2,1)S(1)}, bf16[1024,128]{1,0:T(8,128)(2,1)S(1)}, u32[]{:S(2)}, u32[]{:S(2)}) collective-permute-start(bf16[1024,128]{1,0:T(8,128)(2,1)S(1)} %get-tuple-element.140), channel_id=1, source_target_pairs={{0,16},{4,20},{8,24},{12,28},{16,0},{20,4},{24,8},{28,12},{1,17},{... | collective-permute-start | bytes 786440 | tf_op jit(solution)/shard_map/ppermute | solution.py:311
  116.1 6.8 %collective-permute-start.24 = (bf16[1024,128]{1,0:T(8,128)(2,1)S(1)}, bf16[1024,128]{1,0:T(8,128)(2,1)S(1)}, u32[]{:S(2)}, u32[]{:S(2)}) collective-permute-start(bf16[1024,128]{1,0:T(8,128)(2,1)S(1)} %get-tuple-element.142), channel_id=1, source_target_pairs={{0,8},{4,12},{8,0},{12,4},{16,24},{20,28},{24,16},{28,20},{1,9},{5... | collective-permute-start | bytes 786440 | tf_op jit(solution)/shard_map/ppermute | solution.py:311
  117.3 7.5 %collective-permute-start.27 = (bf16[256,128]{1,0:T(8,128)(2,1)S(1)}, bf16[256,128]{1,0:T(8,128)(2,1)S(1)}, u32[]{:S(2)}, u32[]{:S(2)}) collective-permute-start(bf16[256,128]{1,0:T(8,128)(2,1)S(1)} %add_convert_fusion.11), channel_id=1, source_target_pairs={{0,24},{4,28},{8,16},{12,20},{16,8},{20,12},{24,0},{28,4},{1,25},{... | collective-permute-start | bytes 196616 | tf_op jit(solution)/shard_map/ppermute | solution.py:311
  118.5 6.2 %collective-permute-start.26 = (bf16[256,128]{1,0:T(8,128)(2,1)S(1)}, bf16[256,128]{1,0:T(8,128)(2,1)S(1)}, u32[]{:S(2)}, u32[]{:S(2)}) collective-permute-start(bf16[256,128]{1,0:T(8,128)(2,1)S(1)} %add_convert_fusion.11), channel_id=1, source_target_pairs={{0,16},{4,20},{8,24},{12,28},{16,0},{20,4},{24,8},{28,12},{1,17},{... | collective-permute-start | bytes 196616 | tf_op jit(solution)/shard_map/ppermute | solution.py:311
  118.8 7.0 %collective-permute-start.25 = (bf16[256,128]{1,0:T(8,128)(2,1)S(1)}, bf16[256,128]{1,0:T(8,128)(2,1)S(1)}, u32[]{:S(2)}, u32[]{:S(2)}) collective-permute-start(bf16[256,128]{1,0:T(8,128)(2,1)S(1)} %add_convert_fusion.11), channel_id=1, source_target_pairs={{0,8},{4,12},{8,0},{12,4},{16,24},{20,28},{24,16},{28,20},{1,9},{5... | collective-permute-start | bytes 196616 | tf_op jit(solution)/shard_map/ppermute | solution.py:311
  125.8 3.6 %collective-permute-start.28 = (bf16[256,128]{1,0:T(8,128)(2,1)S(1)}, bf16[256,128]{1,0:T(8,128)(2,1)S(1)}, u32[]{:S(2)}, u32[]{:S(2)}) collective-permute-start(bf16[256,128]{1,0:T(8,128)(2,1)S(1)} %add_convert_fusion.10), channel_id=1, source_target_pairs={{0,4},{4,0},{8,12},{12,8},{16,20},{20,16},{24,28},{28,24},{1,5},{5... | collective-permute-start | bytes 196616 | tf_op jit(solution)/shard_map/ppermute | solution.py:311
  (3 other events, 18.7 us)

commit v18 on v17

--- a/solution.py
+++ b/solution.py
@@ -472,20 +472,21 @@
     bits = [1 << b for b in range(1, n_row.bit_length() - 1)]
     mid = ((col & 3) == 1) | ((col & 3) == 2)
     even = (row & 1) == 0
+    place = jnp.stack([live_counts.reshape(()), row, col, mid.astype(jnp.int32)])
+    place, even, grad_out, preact = fence(place, even, grad_out, preact)
 
     own0, own1 = [
         jnp.where(preact[:, cut] > 0, grad_out[:, cut], jnp.zeros_like(grad_out[:, cut]))
         for cut in (slice(0, cw), slice(cw, width))
     ]
     first0 = gather_first(own0)
-    place = jnp.stack([live_counts.reshape(()), row, col, mid.astype(jnp.int32)])
     plan0, plan1, slot = make_plans(tile_rows, tile_cols, place, n_row, nodes // SIDE)
     flipped = flip_tiles(slot, tiles.reshape(slots, SIDE, SIDE))
     features, plan0 = fence(features, plan0)
     near = [[features]]
     for bit in bits[:2]:
         near.append([xor_permute(features, "row", bit)])
-    own0, own1, first0, plan0, plan1, flipped, even = fence(own0, own1, first0, plan0, plan1, flipped, even)
+    own0, own1, first0, plan0, plan1, flipped = fence(own0, own1, first0, plan0, plan1, flipped)
 
     second0 = gather_second(own0, first0[1], n_col)
     acc0 = spmm(plan0, [[own0], [first0[0]], [first0[1]]], flipped, None, n_row)

time: 131 us -> 130 us (level)
  blocking collectives: 9.08 us -> 7.56 us
  Pallas kernels: 40.7 us -> 42.2 us
    all_to_all x1, blocking collectives: 9.08 us -> 7.56 us  [swap_cores(): return lax.all_to_all(both, 'row', 0, 0, axis_index_groups=pairs)]
    pallas_call x4, Pallas kernels: 25 us -> 26.5 us  [spmm(): pl.pallas_call(functools.partial(spmm_kernel, [len(p) for p in pieces], l...]
    unnamed x12 -> x10, local copies, waits for them, and re-layouts: 4.01 us -> 4 us
  transfers between devices with their start and end apart: 29 -> 29, of which waited for: 14 -> 13; matrix products, arithmetic and copies ran while one was open for 2% -> 2% of each run, Pallas kernels for 31% -> 33%
where the time goes in v18:
time: 130 us; the launch traced here: 129 us
  Pallas kernels  42.2 us (32%)
  starting transfers between devices  34.9 us (27%)
  waiting for transfers between devices  30 us (23%)
  blocking collectives  7.56 us (6%)
  local copies, waits for them, and re-layouts  4.77 us (4%)
  other arithmetic  4.56 us (4%)
  matrix products  3.56 us (3%)
  between operations  1.79 us (1%)
    ppermute x25, starting transfers between devices, xor_permute(): return lax.ppermute(value, axis, [(i, i ^ mask) for i in range(size)])  31 us
    pallas_call x4, Pallas kernels, spmm(): pl.pallas_call(functools.partial(spmm_kernel, [len(p) for p in pieces], l...  26.5 us
    ppermute x25, waiting for transfers between devices, xor_permute(): return lax.ppermute(value, axis, [(i, i ^ mask) for i in range(size)])  23.1 us
    pallas_call x1, Pallas kernels, flip_tiles(): pl.pallas_call(flip_kernel, out_shape=jax.ShapeDtypeStruct((slots + GROUP...  9.59 us
    all_to_all x1, blocking collectives, swap_cores(): return lax.all_to_all(both, 'row', 0, 0, axis_index_groups=pairs)  7.56 us
    ppermute x2, waiting for transfers between devices, gather_second(): lax.ppermute(by_two, 'col', ends)  6.9 us
    unnamed x10, local copies, waits for them, and re-layouts  4 us
    pallas_call x1, Pallas kernels, weight_term_early(): pl.pallas_call(term_kernel, out_shape=jax.ShapeDtypeStruct(shape, jnp.bfl...  3.79 us
  transfers between devices with their start and end apart: 29, of which 13 were waited for; matrix products, arithmetic and copies ran while one was open for 2% of the time, Pallas kernels for 33%

profile of v18, /device:TPU:1, one launch (start us, length us, event | category | flops | bytes accessed | tf_op | source)
XLA Modules:
  0.0 129.4 jit_solution(16581524400545179274)
XLA Ops:
  1.5 1.6 %compare_select_fusion = (bf16[2048,128]{1,0:T(8,128)(2,1)S(1)}, bf16[2048,128]{1,0:T(8,128)(2,1)S(1)}) fusion(bf16[2048,256]{1,0:T(8,128)(2,1)} %param.8, bf16[2048,256]{1,0:T(8,128)(2,1)} %param.9), kind=kLoop, calls=%fused_computation.16 | loop fusion | flops 1048576 | bytes 3145728 | tf_op jit(solution)/shard_map/jit(_where)/select_n | solution.py:479
  3.1 3.2 %collective-permute-start.1 = (bf16[2048,128]{1,0:T(8,128)(2,1)S(1)}, bf16[2048,128]{1,0:T(8,128)(2,1)S(1)}, u32[]{:S(2)}, u32[]{:S(2)}) collective-permute-start(bf16[2048,128]{1,0:T(8,128)(2,1)S(1)} %get-tuple-element.87.refs_0_), channel_id=1, source_target_pairs={{0,2},{1,3},{2,0},{3,1},{4,6},{5,7},{6,4},{7,5},{8,10},{9,11},{10,... | collective-permute-start | bytes 1572872 | tf_op jit(solution)/shard_map/ppermute | solution.py:311
  6.3 1.3 %collective-permute-start = (bf16[2048,128]{1,0:T(8,128)(2,1)S(1)}, bf16[2048,128]{1,0:T(8,128)(2,1)}, u32[]{:S(2)}, u32[]{:S(2)}) collective-permute-start(bf16[2048,128]{1,0:T(8,128)(2,1)S(1)} %get-tuple-element.87.refs_0_), channel_id=1, source_target_pairs={{0,1},{1,0},{2,3},{3,2},{4,5},{5,4},{6,7},{7,6},{8,9},{9,8},{10,11... | collective-permute-start | bytes 1572872 | tf_op jit(solution)/shard_map/ppermute | solution.py:311
  7.9 2.3 %plan_slots.1 = (s32[8,512]{1,0:T(8,128)S(1)}, s32[8,512]{1,0:T(8,128)S(1)}, s32[1,320]{1,0:T(1,128)S(1)}) custom-call(s32[4]{0:T(128)S(1)} %pad_add_fusion.place_ref, s32[1,320]{1,0:T(1,128)S(1)} %bitcast.42, s32[1,320]{1,0:T(1,128)S(1)} %bitcast.44, s32[320,1]{1,0:T(8,128)S(1)} %copy.10.rows_c, s32[320,1]{1,0:T(8,128)S(1)} %copy.11.cols_c), custom_call_target="tpu_custom_call" | custom-call | bytes 4096 | tf_op jit(solution)/shard_map/plan_slots/pallas_call | solution.py:122
  10.3 1.3 %collective-permute-start.7 = (bf16[2048,256]{1,0:T(8,128)(2,1)S(1)}, bf16[2048,256]{1,0:T(8,128)(2,1)S(1)}, u32[]{:S(2)}, u32[]{:S(2)}) collective-permute-start(bf16[2048,256]{1,0:T(8,128)(2,1)S(1)} %copy-done.2), channel_id=1, source_target_pairs={{0,16},{4,20},{8,24},{12,28},{16,0},{20,4},{24,8},{28,12},{1,17},{... | collective-permute-start | bytes 3145736 | tf_op jit(solution)/shard_map/ppermute | solution.py:311
  12.8 4.0 %copy-done.1 = bf16[1,1,320,128,128]{4,3,2,1,0:T(8,128)(2,1)S(1)} copy-done((bf16[1,1,320,128,128]{4,3,2,1,0:T(8,128)(2,1)S(1)}, bf16[1,1,320,128,128]{4,3,2,1,0:T(8,128)(2,1)}, u32[]{:S(2)}) %copy-start.1) | copy-done | bytes 10485784
  16.8 9.6 %flip_tiles.1.refs_3_.refs_2_ = bf16[352,128,128]{2,1,0:T(8,128)(2,1)S(1)} custom-call(s32[1,320]{1,0:T(1,128)S(1)} %get-tuple-element.83.slot_ref, bf16[320,128,128]{2,1,0:T(8,128)(2,1)S(1)} %bitcast.40), custom_call_target="tpu_custom_call" | custom-call | bytes 4096 | tf_op jit(solution)/shard_map/flip_tiles/pallas_call | solution.py:165
  26.4 2.9 %collective-permute-done.1.refs_2_ = bf16[2048,128]{1,0:T(8,128)(2,1)S(1)} collective-permute-done((bf16[2048,128]{1,0:T(8,128)(2,1)S(1)}, bf16[2048,128]{1,0:T(8,128)(2,1)S(1)}, u32[]{:S(2)}, u32[]{:S(2)}) %collective-permute-start.1) | collective-permute-done | bytes 524320 | tf_op jit(solution)/shard_map/ppermute | solution.py:311
  30.0 1.3 collective-permute-start.5
  31.3 9.7 %spmm_first.2 = (bf16[8192,128]{1,0:T(8,128)(2,1)S(1)}, bf16[8192,128]{1,0:T(8,128)(2,1)S(1)}) custom-call(s32[8,512]{1,0:T(8,128)S(1)} %get-tuple-element.86.plan_ref, bf16[2048,128]{1,0:T(8,128)(2,1)S(1)} %get-tuple-element.87.refs_0_, bf16[2048,128]{1,0:T(8,128)(2,1)} %collective-permute-done.refs_1_, ...), custom_call_target="tpu_custom_call" | custom-call | bytes 4096 | tf_op jit(solution)/shard_map/spmm_first/pallas_call | solution.py:288
  41.0 3.4 %collective-permute-done.5.refs_1_ = bf16[2048,128]{1,0:T(8,128)(2,1)S(1)} collective-permute-done((bf16[2048,128]{1,0:T(8,128)(2,1)S(1)}, bf16[2048,128]{1,0:T(8,128)(2,1)S(1)}, u32[]{:S(2)}, u32[]{:S(2)}) %collective-permute-start.5) | collective-permute-done | bytes 524320 | tf_op jit(solution)/shard_map/ppermute | solution.py:329
  47.0 2.5 %collective-permute-start.3 = (bf16[2048,128]{1,0:T(8,128)(2,1)S(1)}, bf16[2048,128]{1,0:T(8,128)(2,1)S(1)}, u32[]{:S(2)}, u32[]{:S(2)}) collective-permute-start(bf16[2048,128]{1,0:T(8,128)(2,1)S(1)} %get-tuple-element.110.refs_0_), channel_id=1, source_target_pairs={{0,2},{1,3},{2,0},{3,1},{4,6},{5,7},{6,4},{7,5},{8,10},{9,11},{10,... | collective-permute-start | bytes 1572872 | tf_op jit(solution)/shard_map/ppermute | solution.py:311
  49.5 2.2 %collective-permute-start.2 = (bf16[2048,128]{1,0:T(8,128)(2,1)S(1)}, bf16[2048,128]{1,0:T(8,128)(2,1)S(1)}, u32[]{:S(2)}, u32[]{:S(2)}) collective-permute-start(bf16[2048,128]{1,0:T(8,128)(2,1)S(1)} %get-tuple-element.110.refs_0_), channel_id=1, source_target_pairs={{0,1},{1,0},{2,3},{3,2},{4,5},{5,4},{6,7},{7,6},{8,9},{9,8},{10,11... | collective-permute-start | bytes 1572872 | tf_op jit(solution)/shard_map/ppermute | solution.py:311
  51.7 4.1 %spmm_last.2 = bf16[2,8192,128]{2,1,0:T(8,128)(2,1)S(1)} custom-call(s32[8,512]{1,0:T(8,128)S(1)} %get-tuple-element.84.plan_ref, bf16[2048,128]{1,0:T(8,128)(2,1)S(1)} %collective-permute-done.4.refs_0_, bf16[2048,128]{1,0:T(8,128)(2,1)S(1)} %collective-permute-done.5.refs_1_, bf16[352,128,128]{2,1,0:T(8,128)(2,1)S(1)} %flip_tiles.1.refs_3_.refs_2_, ...), custom_call_target="tpu_custom_call" | custom-call | bytes 4096 | tf_op jit(solution)/shard_map/spmm_last/pallas_call | solution.py:288
  55.8 7.6 %all_to_all.5 = bf16[2,8192,128]{2,1,0:T(8,128)(2,1)S(1)} all-to-all(bf16[2,8192,128]{2,1,0:T(8,128)(2,1)S(1)} %spmm_last.2), channel_id=1, replica_groups={{0,4},{8,12},{16,20},{24,28},{1,5},{9,13},{17,21},{25,29},{2,6},{10,14}..., dimensions={0} | all-to-all | bytes 8388608 | tf_op jit(solution)/shard_map/all_to_all | solution.py:343
  64.0 2.1 %collective-permute-start.12 = (bf16[2048,128]{1,0:T(8,128)(2,1)S(1)}, bf16[2048,128]{1,0:T(8,128)(2,1)S(1)}, u32[]{:S(2)}, u32[]{:S(2)}) collective-permute-start(bf16[2048,128]{1,0:T(8,128)(2,1)S(1)} %bitcast.56), channel_id=1, source_target_pairs={{0,8},{4,12},{8,0},{12,4},{16,24},{20,28},{24,16},{28,20},{1,9},{5... | collective-permute-start | bytes 1572872 | tf_op jit(solution)/shard_map/ppermute | solution.py:311
  66.1 3.8 %weight_term.1 = bf16[256,128]{1,0:T(8,128)(2,1)S(1)} custom-call(bf16[2048,256]{1,0:T(8,128)(2,1)S(1)} %copy-done.2, bf16[2048,256]{1,0:T(8,128)(2,1)S(1)} %collective-permute-done.6.refs_1_, bf16[2048,256]{1,0:T(8,128)(2,1)S(1)} %collective-permute-done.7.refs_2_, bf16[1024,256]{1,0:T(8,128)(2,1)S(1)} %collective-permute-done.8.refs_3_, ...), custom_call_target="tpu_custom_call" | custom-call | bytes 4096 | tf_op jit(solution)/shard_map/weight_term/pallas_call | solution.py:448
  73.2 8.6 %spmm_first.3 = (bf16[8192,128]{1,0:T(8,128)(2,1)S(1)}, bf16[8192,128]{1,0:T(8,128)(2,1)S(1)}) custom-call(s32[8,512]{1,0:T(8,128)S(1)} %get-tuple-element.86.plan_ref, bf16[2048,128]{1,0:T(8,128)(2,1)S(1)} %get-tuple-element.110.refs_0_, bf16[2048,128]{1,0:T(8,128)(2,1)S(1)} %collective-permute-done.2.refs_1_, ...), custom_call_target="tpu_custom_call" | custom-call | bytes 4096 | tf_op jit(solution)/shard_map/spmm_first/pallas_call | solution.py:288
  82.8 3.5 %collective-permute-done.11.refs_1_ = bf16[2048,128]{1,0:T(8,128)(2,1)S(1)} collective-permute-done((bf16[2048,128]{1,0:T(8,128)(2,1)S(1)}, bf16[2048,128]{1,0:T(8,128)(2,1)S(1)}, u32[]{:S(2)}, u32[]{:S(2)}) %collective-permute-start.11) | collective-permute-done | bytes 524320 | tf_op jit(solution)/shard_map/ppermute | solution.py:329
  86.3 4.2 %spmm_last.3 = (bf16[8192,128]{1,0:T(8,128)(2,1)S(1)}, bf16[8192,128]{1,0:T(8,128)(2,1)S(1)}) custom-call(s32[8,512]{1,0:T(8,128)S(1)} %get-tuple-element.84.plan_ref, bf16[2048,128]{1,0:T(8,128)(2,1)S(1)} %collective-permute-done.10.refs_0_, bf16[2048,128]{1,0:T(8,128)(2,1)S(1)} %collective-permute-done.11.refs_1_, ...), custom_call_target="tpu_custom_call" | custom-call | bytes 4096 | tf_op jit(solution)/shard_map/spmm_last/pallas_call | solution.py:288
  90.5 1.9 %collective-permute-start.16 = (bf16[8192,128]{1,0:T(8,128)(2,1)S(1)}, bf16[8192,128]{1,0:T(8,128)(2,1)S(1)}, u32[]{:S(2)}, u32[]{:S(2)}) collective-permute-start(bf16[8192,128]{1,0:T(8,128)(2,1)S(1)} %get-tuple-element.128), channel_id=1, source_target_pairs={{0,4},{4,0},{8,12},{12,8},{16,20},{20,16},{24,28},{28,24},{1,5},{5... | collective-permute-start | bytes 6291464 | tf_op jit(solution)/shard_map/ppermute | solution.py:311
  92.4 3.7 %collective-permute-done.16 = bf16[8192,128]{1,0:T(8,128)(2,1)S(1)} collective-permute-done((bf16[8192,128]{1,0:T(8,128)(2,1)S(1)}, bf16[8192,128]{1,0:T(8,128)(2,1)S(1)}, u32[]{:S(2)}, u32[]{:S(2)}) %collective-permute-start.16) | collective-permute-done | bytes 2097184 | tf_op jit(solution)/shard_map/ppermute | solution.py:311
  99.5 2.0 %collective-permute-start.17 = (bf16[2048,128]{1,0:T(8,128)(2,1)S(1)}, bf16[2048,128]{1,0:T(8,128)(2,1)S(1)}, u32[]{:S(2)}, u32[]{:S(2)}) collective-permute-start(bf16[2048,128]{1,0:T(8,128)(2,1)S(1)} %bitcast.54), channel_id=1, source_target_pairs={{0,8},{4,12},{8,0},{12,4},{16,24},{20,28},{24,16},{28,20},{1,9},{5... | collective-permute-start | bytes 1572872 | tf_op jit(solution)/shard_map/ppermute | solution.py:311
  101.6 3.7 %collective-permute-start.22 = (bf16[256,128]{1,0:T(8,128)(2,1)S(1)}, bf16[256,128]{1,0:T(8,128)(2,1)S(1)}, u32[]{:S(2)}, u32[]{:S(2)}) collective-permute-start(bf16[256,128]{1,0:T(8,128)(2,1)S(1)} %add_convert_fusion.12), channel_id=1, source_target_pairs={{0,3},{1,2},{2,1},{3,0},{4,7},{5,6},{6,5},{7,4},{8,11},{9,10},{10,... | collective-permute-start | bytes 196616 | tf_op jit(solution)/shard_map/ppermute | solution.py:311
  105.7 1.7 %collective-permute-done.22 = bf16[256,128]{1,0:T(8,128)(2,1)S(1)} collective-permute-done((bf16[256,128]{1,0:T(8,128)(2,1)S(1)}, bf16[256,128]{1,0:T(8,128)(2,1)S(1)}, u32[]{:S(2)}, u32[]{:S(2)}) %collective-permute-start.22) | collective-permute-done | bytes 65568 | tf_op jit(solution)/shard_map/ppermute | solution.py:311
  107.4 3.5 %collective-permute-done.21 = bf16[256,128]{1,0:T(8,128)(2,1)S(1)} collective-permute-done((bf16[256,128]{1,0:T(8,128)(2,1)S(1)}, bf16[256,128]{1,0:T(8,128)(2,1)S(1)}, u32[]{:S(2)}, u32[]{:S(2)}) %collective-permute-start.21) | collective-permute-done | bytes 65568 | tf_op jit(solution)/shard_map/ppermute | solution.py:311
  110.9 2.8 %collective-permute-done.17 = bf16[2048,128]{1,0:T(8,128)(2,1)S(1)} collective-permute-done((bf16[2048,128]{1,0:T(8,128)(2,1)S(1)}, bf16[2048,128]{1,0:T(8,128)(2,1)S(1)}, u32[]{:S(2)}, u32[]{:S(2)}) %collective-permute-start.17) | collective-permute-done | bytes 524320 | tf_op jit(solution)/shard_map/ppermute | solution.py:311
  115.6 2.1 %collective-permute-start.27 = (bf16[256,128]{1,0:T(8,128)(2,1)S(1)}, bf16[256,128]{1,0:T(8,128)(2,1)S(1)}, u32[]{:S(2)}, u32[]{:S(2)}) collective-permute-start(bf16[256,128]{1,0:T(8,128)(2,1)S(1)} %add_convert_fusion.11), channel_id=1, source_target_pairs={{0,24},{4,28},{8,16},{12,20},{16,8},{20,12},{24,0},{28,4},{1,25},{... | collective-permute-start | bytes 196616 | tf_op jit(solution)/shard_map/ppermute | solution.py:311
  118.3 3.4 %collective-permute-done.23 = bf16[1024,128]{1,0:T(8,128)(2,1)S(1)} collective-permute-done((bf16[1024,128]{1,0:T(8,128)(2,1)S(1)}, bf16[1024,128]{1,0:T(8,128)(2,1)S(1)}, u32[]{:S(2)}, u32[]{:S(2)}) %collective-permute-start.23) | collective-permute-done | bytes 262176 | tf_op jit(solution)/shard_map/ppermute | solution.py:311
  122.1 1.5 %collective-permute-done.27 = bf16[256,128]{1,0:T(8,128)(2,1)S(1)} collective-permute-done((bf16[256,128]{1,0:T(8,128)(2,1)S(1)}, bf16[256,128]{1,0:T(8,128)(2,1)S(1)}, u32[]{:S(2)}, u32[]{:S(2)}) %collective-permute-start.27) | collective-permute-done | bytes 65568 | tf_op jit(solution)/shard_map/ppermute | solution.py:311
  124.8 2.4 %collective-permute-start.28 = (bf16[256,128]{1,0:T(8,128)(2,1)S(1)}, bf16[256,128]{1,0:T(8,128)(2,1)S(1)}, u32[]{:S(2)}, u32[]{:S(2)}) collective-permute-start(bf16[256,128]{1,0:T(8,128)(2,1)S(1)} %add_convert_fusion.10), channel_id=1, source_target_pairs={{0,4},{4,0},{8,12},{12,8},{16,20},{20,16},{24,28},{28,24},{1,5},{5... | collective-permute-start | bytes 196616 | tf_op jit(solution)/shard_map/ppermute | solution.py:311
  127.2 1.4 %convolution_convert_fusion = bf16[2048,256]{1,0:T(8,128)(2,1)} fusion(bf16[256,256]{1,0:T(8,128)(2,1)S(1)} %copy-done, bf16[2048,128]{1,0:T(8,128)(2,1)S(1)} %pad_maximum_fusion.1, bf16[2048,128]{1,0:T(8,128)(2,1)S(1)} %pad_maximum_fusion), kind=kOutput, calls=%fused_computation.2 | convolution fusion | flops 271056896 | bytes 2228224 | tf_op jit(solution)/shard_map/dot_general | solution.py:543
  (81 shorter events, 18.4 us)
Async XLA Ops:
  0.6 126.6 %copy-start = (bf16[256,256]{1,0:T(8,128)(2,1)S(1)}, bf16[256,256]{1,0:T(8,128)(2,1)}, u32[]{:S(2)}) copy-start(bf16[256,256]{1,0:T(8,128)(2,1)} %param.11) | copy-start | bytes 393220
  0.7 7.1 %copy-start.3 = (s32[1,1,320]{2,1,0:T(1,128)S(1)}, s32[1,1,320]{2,1,0:T(1,128)}, u32[]{:S(2)}) copy-start(s32[1,1,320]{2,1,0:T(1,128)} %param.13) | copy-start | bytes 3844
  0.7 9.6 %copy-start.2 = (bf16[2048,256]{1,0:T(8,128)(2,1)S(1)}, bf16[2048,256]{1,0:T(8,128)(2,1)}, u32[]{:S(2)}) copy-start(bf16[2048,256]{1,0:T(8,128)(2,1)} %refs_0_) | copy-start | bytes 3145732
  3.1 26.1 %collective-permute-start.1 = (bf16[2048,128]{1,0:T(8,128)(2,1)S(1)}, bf16[2048,128]{1,0:T(8,128)(2,1)S(1)}, u32[]{:S(2)}, u32[]{:S(2)}) collective-permute-start(bf16[2048,128]{1,0:T(8,128)(2,1)S(1)} %get-tuple-element.87.refs_0_), channel_id=1, source_target_pairs={{0,2},{1,3},{2,0},{3,1},{4,6},{5,7},{6,4},{7,5},{8,10},{9,11},{10,... | collective-permute-start | bytes 1572872 | tf_op jit(solution)/shard_map/ppermute | solution.py:311
  6.3 22.9 %collective-permute-start = (bf16[2048,128]{1,0:T(8,128)(2,1)S(1)}, bf16[2048,128]{1,0:T(8,128)(2,1)}, u32[]{:S(2)}, u32[]{:S(2)}) collective-permute-start(bf16[2048,128]{1,0:T(8,128)(2,1)S(1)} %get-tuple-element.87.refs_0_), channel_id=1, source_target_pairs={{0,1},{1,0},{2,3},{3,2},{4,5},{5,4},{6,7},{7,6},{8,9},{9,8},{10,11... | collective-permute-start | bytes 1572872 | tf_op jit(solution)/shard_map/ppermute | solution.py:311
  10.3 30.6 %collective-permute-start.7 = (bf16[2048,256]{1,0:T(8,128)(2,1)S(1)}, bf16[2048,256]{1,0:T(8,128)(2,1)S(1)}, u32[]{:S(2)}, u32[]{:S(2)}) collective-permute-start(bf16[2048,256]{1,0:T(8,128)(2,1)S(1)} %copy-done.2), channel_id=1, source_target_pairs={{0,16},{4,20},{8,24},{12,28},{16,0},{20,4},{24,8},{28,12},{1,17},{... | collective-permute-start | bytes 3145736 | tf_op jit(solution)/shard_map/ppermute | solution.py:311
  11.6 29.4 %collective-permute-start.6 = (bf16[2048,256]{1,0:T(8,128)(2,1)S(1)}, bf16[2048,256]{1,0:T(8,128)(2,1)S(1)}, u32[]{:S(2)}, u32[]{:S(2)}) collective-permute-start(bf16[2048,256]{1,0:T(8,128)(2,1)S(1)} %copy-done.2), channel_id=1, source_target_pairs={{0,8},{4,12},{8,0},{12,4},{16,24},{20,28},{24,16},{28,20},{1,9},{5... | collective-permute-start | bytes 3145736 | tf_op jit(solution)/shard_map/ppermute | solution.py:311
  29.3 11.7 %collective-permute-start.4 = (bf16[2048,128]{1,0:T(8,128)(2,1)S(1)}, bf16[2048,128]{1,0:T(8,128)(2,1)S(1)}, u32[]{:S(2)}, u32[]{:S(2)}) collective-permute-start(bf16[2048,128]{1,0:T(8,128)(2,1)S(1)} %get-tuple-element.87.refs_0_), channel_id=1, source_target_pairs={{1,2},{2,1},{5,6},{6,5},{9,10},{10,9},{13,14},{14,13},{17,18},{18,... | collective-permute-start | bytes 1572872 | tf_op jit(solution)/shard_map/ppermute | solution.py:329
  30.0 14.4 %collective-permute-start.5 = (bf16[2048,128]{1,0:T(8,128)(2,1)S(1)}, bf16[2048,128]{1,0:T(8,128)(2,1)S(1)}, u32[]{:S(2)}, u32[]{:S(2)}) collective-permute-start(bf16[2048,128]{1,0:T(8,128)(2,1)S(1)} %collective-permute-done.1.refs_2_), channel_id=1, source_target_pairs={{1,0},{2,3},{5,4},{6,7},{9,8},{10,11},{13,12},{14,15},{17,16},{18,... | collective-permute-start | bytes 1572872 | tf_op jit(solution)/shard_map/ppermute | solution.py:329
  44.4 18.9 %collective-permute-start.9 = (bf16[1024,256]{1,0:T(8,128)(2,1)S(1)}, bf16[1024,256]{1,0:T(8,128)(2,1)S(1)}, u32[]{:S(2)}, u32[]{:S(2)}) collective-permute-start(bf16[1024,256]{1,0:T(8,128)(2,1)S(1)} %slice.96), channel_id=1, source_target_pairs={{0,8},{4,12},{8,0},{12,4},{16,24},{20,28},{24,16},{28,20},{1,9},{5... | collective-permute-start | bytes 1572872 | tf_op jit(solution)/shard_map/ppermute | solution.py:311
  45.7 17.6 %collective-permute-start.8 = (bf16[1024,256]{1,0:T(8,128)(2,1)S(1)}, bf16[1024,256]{1,0:T(8,128)(2,1)S(1)}, u32[]{:S(2)}, u32[]{:S(2)}) collective-permute-start(bf16[1024,256]{1,0:T(8,128)(2,1)S(1)} %slice.95), channel_id=1, source_target_pairs={{0,16},{4,20},{8,24},{12,28},{16,0},{20,4},{24,8},{28,12},{1,17},{... | collective-permute-start | bytes 1572872 | tf_op jit(solution)/shard_map/ppermute | solution.py:311
  47.0 24.2 %collective-permute-start.3 = (bf16[2048,128]{1,0:T(8,128)(2,1)S(1)}, bf16[2048,128]{1,0:T(8,128)(2,1)S(1)}, u32[]{:S(2)}, u32[]{:S(2)}) collective-permute-start(bf16[2048,128]{1,0:T(8,128)(2,1)S(1)} %get-tuple-element.110.refs_0_), channel_id=1, source_target_pairs={{0,2},{1,3},{2,0},{3,1},{4,6},{5,7},{6,4},{7,5},{8,10},{9,11},{10,... | collective-permute-start | bytes 1572872 | tf_op jit(solution)/shard_map/ppermute | solution.py:311
  49.5 21.7 %collective-permute-start.2 = (bf16[2048,128]{1,0:T(8,128)(2,1)S(1)}, bf16[2048,128]{1,0:T(8,128)(2,1)S(1)}, u32[]{:S(2)}, u32[]{:S(2)}) collective-permute-start(bf16[2048,128]{1,0:T(8,128)(2,1)S(1)} %get-tuple-element.110.refs_0_), channel_id=1, source_target_pairs={{0,1},{1,0},{2,3},{3,2},{4,5},{5,4},{6,7},{7,6},{8,9},{9,8},{10,11... | collective-permute-start | bytes 1572872 | tf_op jit(solution)/shard_map/ppermute | solution.py:311
  64.0 17.8 %collective-permute-start.12 = (bf16[2048,128]{1,0:T(8,128)(2,1)S(1)}, bf16[2048,128]{1,0:T(8,128)(2,1)S(1)}, u32[]{:S(2)}, u32[]{:S(2)}) collective-permute-start(bf16[2048,128]{1,0:T(8,128)(2,1)S(1)} %bitcast.56), channel_id=1, source_target_pairs={{0,8},{4,12},{8,0},{12,4},{16,24},{20,28},{24,16},{28,20},{1,9},{5... | collective-permute-start | bytes 1572872 | tf_op jit(solution)/shard_map/ppermute | solution.py:311
  66.1 15.7 %collective-permute-start.13 = (bf16[2048,128]{1,0:T(8,128)(2,1)S(1)}, bf16[2048,128]{1,0:T(8,128)(2,1)S(1)}, u32[]{:S(2)}, u32[]{:S(2)}) collective-permute-start(bf16[2048,128]{1,0:T(8,128)(2,1)S(1)} %bitcast.55), channel_id=1, source_target_pairs={{0,16},{4,20},{8,24},{12,28},{16,0},{20,4},{24,8},{28,12},{1,17},{... | collective-permute-start | bytes 1572872 | tf_op jit(solution)/shard_map/ppermute | solution.py:311
  71.2 11.6 %collective-permute-start.10 = (bf16[2048,128]{1,0:T(8,128)(2,1)S(1)}, bf16[2048,128]{1,0:T(8,128)(2,1)S(1)}, u32[]{:S(2)}, u32[]{:S(2)}) collective-permute-start(bf16[2048,128]{1,0:T(8,128)(2,1)S(1)} %get-tuple-element.110.refs_0_), channel_id=1, source_target_pairs={{1,2},{2,1},{5,6},{6,5},{9,10},{10,9},{13,14},{14,13},{17,18},{18,... | collective-permute-start | bytes 1572872 | tf_op jit(solution)/shard_map/ppermute | solution.py:329
  71.9 14.4 %collective-permute-start.11 = (bf16[2048,128]{1,0:T(8,128)(2,1)S(1)}, bf16[2048,128]{1,0:T(8,128)(2,1)S(1)}, u32[]{:S(2)}, u32[]{:S(2)}) collective-permute-start(bf16[2048,128]{1,0:T(8,128)(2,1)S(1)} %collective-permute-done.3.refs_2_), channel_id=1, source_target_pairs={{1,0},{2,3},{5,4},{6,7},{9,8},{10,11},{13,12},{14,15},{17,16},{18,... | collective-permute-start | bytes 1572872 | tf_op jit(solution)/shard_map/ppermute | solution.py:329
  82.1 8.4 %collective-permute-start.15 = (bf16[1024,128]{1,0:T(8,128)(2,1)S(1)}, bf16[1024,128]{1,0:T(8,128)(2,1)S(1)}, u32[]{:S(2)}, u32[]{:S(2)}) collective-permute-start(bf16[1024,128]{1,0:T(8,128)(2,1)S(1)} %get-tuple-element.166), channel_id=1, source_target_pairs={{0,8},{4,12},{8,0},{12,4},{16,24},{20,28},{24,16},{28,20},{1,9},{5... | collective-permute-start | bytes 786440 | tf_op jit(solution)/shard_map/ppermute | solution.py:311
  82.3 8.2 %collective-permute-start.14 = (bf16[1024,128]{1,0:T(8,128)(2,1)S(1)}, bf16[1024,128]{1,0:T(8,128)(2,1)S(1)}, u32[]{:S(2)}, u32[]{:S(2)}) collective-permute-start(bf16[1024,128]{1,0:T(8,128)(2,1)S(1)} %get-tuple-element.168), channel_id=1, source_target_pairs={{0,16},{4,20},{8,24},{12,28},{16,0},{20,4},{24,8},{28,12},{1,17},{... | collective-permute-start | bytes 786440 | tf_op jit(solution)/shard_map/ppermute | solution.py:311
  90.5 5.6 %collective-permute-start.16 = (bf16[8192,128]{1,0:T(8,128)(2,1)S(1)}, bf16[8192,128]{1,0:T(8,128)(2,1)S(1)}, u32[]{:S(2)}, u32[]{:S(2)}) collective-permute-start(bf16[8192,128]{1,0:T(8,128)(2,1)S(1)} %get-tuple-element.128), channel_id=1, source_target_pairs={{0,4},{4,0},{8,12},{12,8},{16,20},{20,16},{24,28},{28,24},{1,5},{5... | collective-permute-start | bytes 6291464 | tf_op jit(solution)/shard_map/ppermute | solution.py:311
  99.0 2.6 %collective-permute-start.19 = (bf16[256,128]{1,0:T(8,128)(2,1)S(1)}, bf16[256,128]{1,0:T(8,128)(2,1)S(1)}, u32[]{:S(2)}, u32[]{:S(2)}) collective-permute-start(bf16[256,128]{1,0:T(8,128)(2,1)S(1)} %broadcast_select_fusion.2), channel_id=1, source_target_pairs={{0,4},{4,0},{8,12},{12,8},{16,20},{20,16},{24,28},{28,24},{1,5},{5... | collective-permute-start | bytes 196616 | tf_op jit(solution)/shard_map/ppermute | solution.py:311
  99.5 14.2 %collective-permute-start.17 = (bf16[2048,128]{1,0:T(8,128)(2,1)S(1)}, bf16[2048,128]{1,0:T(8,128)(2,1)S(1)}, u32[]{:S(2)}, u32[]{:S(2)}) collective-permute-start(bf16[2048,128]{1,0:T(8,128)(2,1)S(1)} %bitcast.54), channel_id=1, source_target_pairs={{0,8},{4,12},{8,0},{12,4},{16,24},{20,28},{24,16},{28,20},{1,9},{5... | collective-permute-start | bytes 1572872 | tf_op jit(solution)/shard_map/ppermute | solution.py:311
  101.6 13.1 %collective-permute-start.18 = (bf16[2048,128]{1,0:T(8,128)(2,1)S(1)}, bf16[2048,128]{1,0:T(8,128)(2,1)S(1)}, u32[]{:S(2)}, u32[]{:S(2)}) collective-permute-start(bf16[2048,128]{1,0:T(8,128)(2,1)S(1)} %bitcast.53), channel_id=1, source_target_pairs={{0,16},{4,20},{8,24},{12,28},{16,0},{20,4},{24,8},{28,12},{1,17},{... | collective-permute-start | bytes 1572872 | tf_op jit(solution)/shard_map/ppermute | solution.py:311
  101.6 5.8 %collective-permute-start.22 = (bf16[256,128]{1,0:T(8,128)(2,1)S(1)}, bf16[256,128]{1,0:T(8,128)(2,1)S(1)}, u32[]{:S(2)}, u32[]{:S(2)}) collective-permute-start(bf16[256,128]{1,0:T(8,128)(2,1)S(1)} %add_convert_fusion.12), channel_id=1, source_target_pairs={{0,3},{1,2},{2,1},{3,0},{4,7},{5,6},{6,5},{7,4},{8,11},{9,10},{10,... | collective-permute-start | bytes 196616 | tf_op jit(solution)/shard_map/ppermute | solution.py:311
  105.3 5.6 %collective-permute-start.21 = (bf16[256,128]{1,0:T(8,128)(2,1)S(1)}, bf16[256,128]{1,0:T(8,128)(2,1)S(1)}, u32[]{:S(2)}, u32[]{:S(2)}) collective-permute-start(bf16[256,128]{1,0:T(8,128)(2,1)S(1)} %add_convert_fusion.12), channel_id=1, source_target_pairs={{0,2},{1,3},{2,0},{3,1},{4,6},{5,7},{6,4},{7,5},{8,10},{9,11},{10,... | collective-permute-start | bytes 196616 | tf_op jit(solution)/shard_map/ppermute | solution.py:311
  105.3 5.6 %collective-permute-start.20 = (bf16[256,128]{1,0:T(8,128)(2,1)S(1)}, bf16[256,128]{1,0:T(8,128)(2,1)S(1)}, u32[]{:S(2)}, u32[]{:S(2)}) collective-permute-start(bf16[256,128]{1,0:T(8,128)(2,1)S(1)} %add_convert_fusion.12), channel_id=1, source_target_pairs={{0,1},{1,0},{2,3},{3,2},{4,5},{5,4},{6,7},{7,6},{8,9},{9,8},{10,11... | collective-permute-start | bytes 196616 | tf_op jit(solution)/shard_map/ppermute | solution.py:311
  115.0 6.6 %collective-permute-start.23 = (bf16[1024,128]{1,0:T(8,128)(2,1)S(1)}, bf16[1024,128]{1,0:T(8,128)(2,1)S(1)}, u32[]{:S(2)}, u32[]{:S(2)}) collective-permute-start(bf16[1024,128]{1,0:T(8,128)(2,1)S(1)} %get-tuple-element.146), channel_id=1, source_target_pairs={{0,16},{4,20},{8,24},{12,28},{16,0},{20,4},{24,8},{28,12},{1,17},{... | collective-permute-start | bytes 786440 | tf_op jit(solution)/shard_map/ppermute | solution.py:311
  115.4 6.6 %collective-permute-start.24 = (bf16[1024,128]{1,0:T(8,128)(2,1)S(1)}, bf16[1024,128]{1,0:T(8,128)(2,1)S(1)}, u32[]{:S(2)}, u32[]{:S(2)}) collective-permute-start(bf16[1024,128]{1,0:T(8,128)(2,1)S(1)} %get-tuple-element.148), channel_id=1, source_target_pairs={{0,8},{4,12},{8,0},{12,4},{16,24},{20,28},{24,16},{28,20},{1,9},{5... | collective-permute-start | bytes 786440 | tf_op jit(solution)/shard_map/ppermute | solution.py:311
  115.6 8.0 %collective-permute-start.27 = (bf16[256,128]{1,0:T(8,128)(2,1)S(1)}, bf16[256,128]{1,0:T(8,128)(2,1)S(1)}, u32[]{:S(2)}, u32[]{:S(2)}) collective-permute-start(bf16[256,128]{1,0:T(8,128)(2,1)S(1)} %add_convert_fusion.11), channel_id=1, source_target_pairs={{0,24},{4,28},{8,16},{12,20},{16,8},{20,12},{24,0},{28,4},{1,25},{... | collective-permute-start | bytes 196616 | tf_op jit(solution)/shard_map/ppermute | solution.py:311
  117.7 5.9 %collective-permute-start.26 = (bf16[256,128]{1,0:T(8,128)(2,1)S(1)}, bf16[256,128]{1,0:T(8,128)(2,1)S(1)}, u32[]{:S(2)}, u32[]{:S(2)}) collective-permute-start(bf16[256,128]{1,0:T(8,128)(2,1)S(1)} %add_convert_fusion.11), channel_id=1, source_target_pairs={{0,16},{4,20},{8,24},{12,28},{16,0},{20,4},{24,8},{28,12},{1,17},{... | collective-permute-start | bytes 196616 | tf_op jit(solution)/shard_map/ppermute | solution.py:311
  118.1 6.7 %collective-permute-start.25 = (bf16[256,128]{1,0:T(8,128)(2,1)S(1)}, bf16[256,128]{1,0:T(8,128)(2,1)S(1)}, u32[]{:S(2)}, u32[]{:S(2)}) collective-permute-start(bf16[256,128]{1,0:T(8,128)(2,1)S(1)} %add_convert_fusion.11), channel_id=1, source_target_pairs={{0,8},{4,12},{8,0},{12,4},{16,24},{20,28},{24,16},{28,20},{1,9},{5... | collective-permute-start | bytes 196616 | tf_op jit(solution)/shard_map/ppermute | solution.py:311
  124.8 3.8 %collective-permute-start.28 = (bf16[256,128]{1,0:T(8,128)(2,1)S(1)}, bf16[256,128]{1,0:T(8,128)(2,1)S(1)}, u32[]{:S(2)}, u32[]{:S(2)}) collective-permute-start(bf16[256,128]{1,0:T(8,128)(2,1)S(1)} %add_convert_fusion.10), channel_id=1, source_target_pairs={{0,4},{4,0},{8,12},{12,8},{16,20},{20,16},{24,28},{28,24},{1,5},{5... | collective-permute-start | bytes 196616 | tf_op jit(solution)/shard_map/ppermute | solution.py:311
  (2 other events, 11.0 us)

commit v19 on v18

--- a/solution.py
+++ b/solution.py
@@ -8,7 +8,7 @@
 from jax.sharding import PartitionSpec as P
 
 SIDE = 128
-UNROLL = 8
+UNROLL = 16
 GROUP = 32
 RING = 4
 FIRST_PIECES = 3

time: 130 us -> 129 us (level)
  Pallas kernels: 42.2 us -> 29.4 us
  waiting for transfers between devices: 30 us -> 37.1 us
  starting transfers between devices: 34.9 us -> 38.4 us
  blocking collectives: 7.56 us -> 9.19 us
    pallas_call x4, Pallas kernels: 26.5 us -> 13.7 us  [spmm(): pl.pallas_call(functools.partial(spmm_kernel, [len(p) for p in pieces], l...]
    ppermute x2, waiting for transfers between devices: 6.9 us -> 13.4 us  [gather_second(): lax.ppermute(by_two, 'col', ends)]
    ppermute x25, starting transfers between devices: 31 us -> 34.5 us  [xor_permute(): return lax.ppermute(value, axis, [(i, i ^ mask) for i in range(size)])]
    all_to_all x1, blocking collectives: 7.56 us -> 9.19 us  [swap_cores(): return lax.all_to_all(both, 'row', 0, 0, axis_index_groups=pairs)]
  transfers between devices with their start and end apart: 29 -> 29, of which waited for: 13 -> 15; matrix products, arithmetic and copies ran while one was open for 2% -> 2% of each run, Pallas kernels for 33% -> 23%
where the time goes in v19:
time: 129 us
  starting transfers between devices  38.4 us (30%)
  waiting for transfers between devices  37.1 us (29%)
  Pallas kernels  29.4 us (23%)
  blocking collectives  9.19 us (7%)
  local copies, waits for them, and re-layouts  4.77 us (4%)
  other arithmetic  4.56 us (4%)
  matrix products  3.55 us (3%)
  between operations  1.76 us (1%)
    ppermute x25, starting transfers between devices, xor_permute(): return lax.ppermute(value, axis, [(i, i ^ mask) for i in range(size)])  34.5 us
    ppermute x25, waiting for transfers between devices, xor_permute(): return lax.ppermute(value, axis, [(i, i ^ mask) for i in range(size)])  23.8 us
    pallas_call x4, Pallas kernels, spmm(): pl.pallas_call(functools.partial(spmm_kernel, [len(p) for p in pieces], l...  13.7 us
    ppermute x2, waiting for transfers between devices, gather_second(): lax.ppermute(by_two, 'col', ends)  13.4 us
    pallas_call x1, Pallas kernels, flip_tiles(): pl.pallas_call(flip_kernel, out_shape=jax.ShapeDtypeStruct((slots + GROUP...  9.59 us
    all_to_all x1, blocking collectives, swap_cores(): return lax.all_to_all(both, 'row', 0, 0, axis_index_groups=pairs)  9.19 us
    unnamed x10, local copies, waits for them, and re-layouts  4 us
    pallas_call x1, Pallas kernels, weight_term_early(): pl.pallas_call(term_kernel, out_shape=jax.ShapeDtypeStruct(shape, jnp.bfl...  3.8 us
  transfers between devices with their start and end apart: 29, of which 15 were waited for; matrix products, arithmetic and copies ran while one was open for 2% of the time, Pallas kernels for 23%

profile of v19, /device:TPU:1, one launch (start us, length us, event | category | flops | bytes accessed | tf_op | source)
XLA Modules:
  0.0 128.8 jit_solution(16524482639085517997)
XLA Ops:
  1.5 1.6 %compare_select_fusion = (bf16[2048,128]{1,0:T(8,128)(2,1)S(1)}, bf16[2048,128]{1,0:T(8,128)(2,1)S(1)}) fusion(bf16[2048,256]{1,0:T(8,128)(2,1)} %param.8, bf16[2048,256]{1,0:T(8,128)(2,1)} %param.9), kind=kLoop, calls=%fused_computation.16 | loop fusion | flops 1048576 | bytes 3145728 | tf_op jit(solution)/shard_map/jit(_where)/select_n | solution.py:479
  3.1 3.2 %collective-permute-start.1 = (bf16[2048,128]{1,0:T(8,128)(2,1)S(1)}, bf16[2048,128]{1,0:T(8,128)(2,1)S(1)}, u32[]{:S(2)}, u32[]{:S(2)}) collective-permute-start(bf16[2048,128]{1,0:T(8,128)(2,1)S(1)} %get-tuple-element.87.refs_0_), channel_id=1, source_target_pairs={{0,2},{1,3},{2,0},{3,1},{4,6},{5,7},{6,4},{7,5},{8,10},{9,11},{10,... | collective-permute-start | bytes 1572872 | tf_op jit(solution)/shard_map/ppermute | solution.py:311
  7.9 2.3 %plan_slots.1 = (s32[8,512]{1,0:T(8,128)S(1)}, s32[8,512]{1,0:T(8,128)S(1)}, s32[1,320]{1,0:T(1,128)S(1)}) custom-call(s32[4]{0:T(128)S(1)} %pad_add_fusion.place_ref, s32[1,320]{1,0:T(1,128)S(1)} %bitcast.42, s32[1,320]{1,0:T(1,128)S(1)} %bitcast.44, s32[320,1]{1,0:T(8,128)S(1)} %copy.10.rows_c, s32[320,1]{1,0:T(8,128)S(1)} %copy.11.cols_c), custom_call_target="tpu_custom_call" | custom-call | bytes 4096 | tf_op jit(solution)/shard_map/plan_slots/pallas_call | solution.py:122
  10.3 1.3 %collective-permute-start.7 = (bf16[2048,256]{1,0:T(8,128)(2,1)S(1)}, bf16[2048,256]{1,0:T(8,128)(2,1)S(1)}, u32[]{:S(2)}, u32[]{:S(2)}) collective-permute-start(bf16[2048,256]{1,0:T(8,128)(2,1)S(1)} %copy-done.2), channel_id=1, source_target_pairs={{0,16},{4,20},{8,24},{12,28},{16,0},{20,4},{24,8},{28,12},{1,17},{... | collective-permute-start | bytes 3145736 | tf_op jit(solution)/shard_map/ppermute | solution.py:311
  12.8 4.0 %copy-done.1 = bf16[1,1,320,128,128]{4,3,2,1,0:T(8,128)(2,1)S(1)} copy-done((bf16[1,1,320,128,128]{4,3,2,1,0:T(8,128)(2,1)S(1)}, bf16[1,1,320,128,128]{4,3,2,1,0:T(8,128)(2,1)}, u32[]{:S(2)}) %copy-start.1) | copy-done | bytes 10485784
  16.8 9.6 %flip_tiles.1.refs_3_.refs_2_ = bf16[352,128,128]{2,1,0:T(8,128)(2,1)S(1)} custom-call(s32[1,320]{1,0:T(1,128)S(1)} %get-tuple-element.83.slot_ref, bf16[320,128,128]{2,1,0:T(8,128)(2,1)S(1)} %bitcast.40), custom_call_target="tpu_custom_call" | custom-call | bytes 4096 | tf_op jit(solution)/shard_map/flip_tiles/pallas_call | solution.py:165
  26.4 2.9 %collective-permute-done.1.refs_2_ = bf16[2048,128]{1,0:T(8,128)(2,1)S(1)} collective-permute-done((bf16[2048,128]{1,0:T(8,128)(2,1)S(1)}, bf16[2048,128]{1,0:T(8,128)(2,1)S(1)}, u32[]{:S(2)}, u32[]{:S(2)}) %collective-permute-start.1) | collective-permute-done | bytes 524320 | tf_op jit(solution)/shard_map/ppermute | solution.py:311
  31.3 4.9 %spmm_first.2 = (bf16[8192,128]{1,0:T(8,128)(2,1)S(1)}, bf16[8192,128]{1,0:T(8,128)(2,1)S(1)}) custom-call(s32[8,512]{1,0:T(8,128)S(1)} %get-tuple-element.86.plan_ref, bf16[2048,128]{1,0:T(8,128)(2,1)S(1)} %get-tuple-element.87.refs_0_, bf16[2048,128]{1,0:T(8,128)(2,1)} %collective-permute-done.refs_1_, ...), custom_call_target="tpu_custom_call" | custom-call | bytes 4096 | tf_op jit(solution)/shard_map/spmm_first/pallas_call | solution.py:288
  36.2 8.2 %collective-permute-done.5.refs_1_ = bf16[2048,128]{1,0:T(8,128)(2,1)S(1)} collective-permute-done((bf16[2048,128]{1,0:T(8,128)(2,1)S(1)}, bf16[2048,128]{1,0:T(8,128)(2,1)S(1)}, u32[]{:S(2)}, u32[]{:S(2)}) %collective-permute-start.5) | collective-permute-done | bytes 524320 | tf_op jit(solution)/shard_map/ppermute | solution.py:329
  47.0 2.5 %collective-permute-start.3 = (bf16[2048,128]{1,0:T(8,128)(2,1)S(1)}, bf16[2048,128]{1,0:T(8,128)(2,1)S(1)}, u32[]{:S(2)}, u32[]{:S(2)}) collective-permute-start(bf16[2048,128]{1,0:T(8,128)(2,1)S(1)} %get-tuple-element.110.refs_0_), channel_id=1, source_target_pairs={{0,2},{1,3},{2,0},{3,1},{4,6},{5,7},{6,4},{7,5},{8,10},{9,11},{10,... | collective-permute-start | bytes 1572872 | tf_op jit(solution)/shard_map/ppermute | solution.py:311
  49.5 2.2 %collective-permute-start.2 = (bf16[2048,128]{1,0:T(8,128)(2,1)S(1)}, bf16[2048,128]{1,0:T(8,128)(2,1)S(1)}, u32[]{:S(2)}, u32[]{:S(2)}) collective-permute-start(bf16[2048,128]{1,0:T(8,128)(2,1)S(1)} %get-tuple-element.110.refs_0_), channel_id=1, source_target_pairs={{0,1},{1,0},{2,3},{3,2},{4,5},{5,4},{6,7},{7,6},{8,9},{9,8},{10,11... | collective-permute-start | bytes 1572872 | tf_op jit(solution)/shard_map/ppermute | solution.py:311
  51.7 2.4 %spmm_last.2 = bf16[2,8192,128]{2,1,0:T(8,128)(2,1)S(1)} custom-call(s32[8,512]{1,0:T(8,128)S(1)} %get-tuple-element.84.plan_ref, bf16[2048,128]{1,0:T(8,128)(2,1)S(1)} %collective-permute-done.4.refs_0_, bf16[2048,128]{1,0:T(8,128)(2,1)S(1)} %collective-permute-done.5.refs_1_, bf16[352,128,128]{2,1,0:T(8,128)(2,1)S(1)} %flip_tiles.1.refs_3_.refs_2_, ...), custom_call_target="tpu_custom_call" | custom-call | bytes 4096 | tf_op jit(solution)/shard_map/spmm_last/pallas_call | solution.py:288
  54.1 9.2 %all_to_all.5 = bf16[2,8192,128]{2,1,0:T(8,128)(2,1)S(1)} all-to-all(bf16[2,8192,128]{2,1,0:T(8,128)(2,1)S(1)} %spmm_last.2), channel_id=1, replica_groups={{0,4},{8,12},{16,20},{24,28},{1,5},{9,13},{17,21},{25,29},{2,6},{10,14}..., dimensions={0} | all-to-all | bytes 8388608 | tf_op jit(solution)/shard_map/all_to_all | solution.py:343
  64.0 1.4 %collective-permute-start.12 = (bf16[2048,128]{1,0:T(8,128)(2,1)S(1)}, bf16[2048,128]{1,0:T(8,128)(2,1)S(1)}, u32[]{:S(2)}, u32[]{:S(2)}) collective-permute-start(bf16[2048,128]{1,0:T(8,128)(2,1)S(1)} %bitcast.56), channel_id=1, source_target_pairs={{0,8},{4,12},{8,0},{12,4},{16,24},{20,28},{24,16},{28,20},{1,9},{5... | collective-permute-start | bytes 1572872 | tf_op jit(solution)/shard_map/ppermute | solution.py:311
  65.4 3.8 %weight_term.1 = bf16[256,128]{1,0:T(8,128)(2,1)S(1)} custom-call(bf16[2048,256]{1,0:T(8,128)(2,1)S(1)} %copy-done.2, bf16[2048,256]{1,0:T(8,128)(2,1)S(1)} %collective-permute-done.6.refs_1_, bf16[2048,256]{1,0:T(8,128)(2,1)S(1)} %collective-permute-done.7.refs_2_, bf16[1024,256]{1,0:T(8,128)(2,1)S(1)} %collective-permute-done.8.refs_3_, ...), custom_call_target="tpu_custom_call" | custom-call | bytes 4096 | tf_op jit(solution)/shard_map/weight_term/pallas_call | solution.py:448
  69.2 1.9 %collective-permute-done.3.refs_2_ = bf16[2048,128]{1,0:T(8,128)(2,1)S(1)} collective-permute-done((bf16[2048,128]{1,0:T(8,128)(2,1)S(1)}, bf16[2048,128]{1,0:T(8,128)(2,1)S(1)}, u32[]{:S(2)}, u32[]{:S(2)}) %collective-permute-start.3) | collective-permute-done | bytes 524320 | tf_op jit(solution)/shard_map/ppermute | solution.py:311
  73.2 3.8 %spmm_first.3 = (bf16[8192,128]{1,0:T(8,128)(2,1)S(1)}, bf16[8192,128]{1,0:T(8,128)(2,1)S(1)}) custom-call(s32[8,512]{1,0:T(8,128)S(1)} %get-tuple-element.86.plan_ref, bf16[2048,128]{1,0:T(8,128)(2,1)S(1)} %get-tuple-element.110.refs_0_, bf16[2048,128]{1,0:T(8,128)(2,1)S(1)} %collective-permute-done.2.refs_1_, ...), custom_call_target="tpu_custom_call" | custom-call | bytes 4096 | tf_op jit(solution)/shard_map/spmm_first/pallas_call | solution.py:288
  79.0 2.1 %collective-permute-start.14 = (bf16[1024,128]{1,0:T(8,128)(2,1)S(1)}, bf16[1024,128]{1,0:T(8,128)(2,1)S(1)}, u32[]{:S(2)}, u32[]{:S(2)}) collective-permute-start(bf16[1024,128]{1,0:T(8,128)(2,1)S(1)} %get-tuple-element.168), channel_id=1, source_target_pairs={{0,16},{4,20},{8,24},{12,28},{16,0},{20,4},{24,8},{28,12},{1,17},{... | collective-permute-start | bytes 786440 | tf_op jit(solution)/shard_map/ppermute | solution.py:311
  81.1 5.2 %collective-permute-done.11.refs_1_ = bf16[2048,128]{1,0:T(8,128)(2,1)S(1)} collective-permute-done((bf16[2048,128]{1,0:T(8,128)(2,1)S(1)}, bf16[2048,128]{1,0:T(8,128)(2,1)S(1)}, u32[]{:S(2)}, u32[]{:S(2)}) %collective-permute-start.11) | collective-permute-done | bytes 524320 | tf_op jit(solution)/shard_map/ppermute | solution.py:329
  86.3 2.6 %spmm_last.3 = (bf16[8192,128]{1,0:T(8,128)(2,1)S(1)}, bf16[8192,128]{1,0:T(8,128)(2,1)S(1)}) custom-call(s32[8,512]{1,0:T(8,128)S(1)} %get-tuple-element.84.plan_ref, bf16[2048,128]{1,0:T(8,128)(2,1)S(1)} %collective-permute-done.10.refs_0_, bf16[2048,128]{1,0:T(8,128)(2,1)S(1)} %collective-permute-done.11.refs_1_, ...), custom_call_target="tpu_custom_call" | custom-call | bytes 4096 | tf_op jit(solution)/shard_map/spmm_last/pallas_call | solution.py:288
  88.9 3.5 %collective-permute-start.16 = (bf16[8192,128]{1,0:T(8,128)(2,1)S(1)}, bf16[8192,128]{1,0:T(8,128)(2,1)S(1)}, u32[]{:S(2)}, u32[]{:S(2)}) collective-permute-start(bf16[8192,128]{1,0:T(8,128)(2,1)S(1)} %get-tuple-element.128), channel_id=1, source_target_pairs={{0,4},{4,0},{8,12},{12,8},{16,20},{20,16},{24,28},{28,24},{1,5},{5... | collective-permute-start | bytes 6291464 | tf_op jit(solution)/shard_map/ppermute | solution.py:311
  92.4 3.7 %collective-permute-done.16 = bf16[8192,128]{1,0:T(8,128)(2,1)S(1)} collective-permute-done((bf16[8192,128]{1,0:T(8,128)(2,1)S(1)}, bf16[8192,128]{1,0:T(8,128)(2,1)S(1)}, u32[]{:S(2)}, u32[]{:S(2)}) %collective-permute-start.16) | collective-permute-done | bytes 2097184 | tf_op jit(solution)/shard_map/ppermute | solution.py:311
  99.5 1.4 %collective-permute-start.17 = (bf16[2048,128]{1,0:T(8,128)(2,1)S(1)}, bf16[2048,128]{1,0:T(8,128)(2,1)S(1)}, u32[]{:S(2)}, u32[]{:S(2)}) collective-permute-start(bf16[2048,128]{1,0:T(8,128)(2,1)S(1)} %bitcast.54), channel_id=1, source_target_pairs={{0,8},{4,12},{8,0},{12,4},{16,24},{20,28},{24,16},{28,20},{1,9},{5... | collective-permute-start | bytes 1572872 | tf_op jit(solution)/shard_map/ppermute | solution.py:311
  101.0 4.1 %collective-permute-start.22 = (bf16[256,128]{1,0:T(8,128)(2,1)S(1)}, bf16[256,128]{1,0:T(8,128)(2,1)S(1)}, u32[]{:S(2)}, u32[]{:S(2)}) collective-permute-start(bf16[256,128]{1,0:T(8,128)(2,1)S(1)} %add_convert_fusion.12), channel_id=1, source_target_pairs={{0,3},{1,2},{2,1},{3,0},{4,7},{5,6},{6,5},{7,4},{8,11},{9,10},{10,... | collective-permute-start | bytes 196616 | tf_op jit(solution)/shard_map/ppermute | solution.py:311
  105.5 1.8 %collective-permute-done.22 = bf16[256,128]{1,0:T(8,128)(2,1)S(1)} collective-permute-done((bf16[256,128]{1,0:T(8,128)(2,1)S(1)}, bf16[256,128]{1,0:T(8,128)(2,1)S(1)}, u32[]{:S(2)}, u32[]{:S(2)}) %collective-permute-start.22) | collective-permute-done | bytes 65568 | tf_op jit(solution)/shard_map/ppermute | solution.py:311
  107.3 3.5 %collective-permute-done.21 = bf16[256,128]{1,0:T(8,128)(2,1)S(1)} collective-permute-done((bf16[256,128]{1,0:T(8,128)(2,1)S(1)}, bf16[256,128]{1,0:T(8,128)(2,1)S(1)}, u32[]{:S(2)}, u32[]{:S(2)}) %collective-permute-start.21) | collective-permute-done | bytes 65568 | tf_op jit(solution)/shard_map/ppermute | solution.py:311
  110.9 2.1 %collective-permute-done.17 = bf16[2048,128]{1,0:T(8,128)(2,1)S(1)} collective-permute-done((bf16[2048,128]{1,0:T(8,128)(2,1)S(1)}, bf16[2048,128]{1,0:T(8,128)(2,1)S(1)}, u32[]{:S(2)}, u32[]{:S(2)}) %collective-permute-start.17) | collective-permute-done | bytes 524320 | tf_op jit(solution)/shard_map/ppermute | solution.py:311
  115.8 1.3 %collective-permute-start.27 = (bf16[256,128]{1,0:T(8,128)(2,1)S(1)}, bf16[256,128]{1,0:T(8,128)(2,1)S(1)}, u32[]{:S(2)}, u32[]{:S(2)}) collective-permute-start(bf16[256,128]{1,0:T(8,128)(2,1)S(1)} %add_convert_fusion.11), channel_id=1, source_target_pairs={{0,24},{4,28},{8,16},{12,20},{16,8},{20,12},{24,0},{28,4},{1,25},{... | collective-permute-start | bytes 196616 | tf_op jit(solution)/shard_map/ppermute | solution.py:311
  118.5 2.5 %collective-permute-done.23 = bf16[1024,128]{1,0:T(8,128)(2,1)S(1)} collective-permute-done((bf16[1024,128]{1,0:T(8,128)(2,1)S(1)}, bf16[1024,128]{1,0:T(8,128)(2,1)S(1)}, u32[]{:S(2)}, u32[]{:S(2)}) %collective-permute-start.23) | collective-permute-done | bytes 262176 | tf_op jit(solution)/shard_map/ppermute | solution.py:311
  121.5 1.5 %collective-permute-done.27 = bf16[256,128]{1,0:T(8,128)(2,1)S(1)} collective-permute-done((bf16[256,128]{1,0:T(8,128)(2,1)S(1)}, bf16[256,128]{1,0:T(8,128)(2,1)S(1)}, u32[]{:S(2)}, u32[]{:S(2)}) %collective-permute-start.27) | collective-permute-done | bytes 65568 | tf_op jit(solution)/shard_map/ppermute | solution.py:311
  124.2 2.4 %collective-permute-start.28 = (bf16[256,128]{1,0:T(8,128)(2,1)S(1)}, bf16[256,128]{1,0:T(8,128)(2,1)S(1)}, u32[]{:S(2)}, u32[]{:S(2)}) collective-permute-start(bf16[256,128]{1,0:T(8,128)(2,1)S(1)} %add_convert_fusion.10), channel_id=1, source_target_pairs={{0,4},{4,0},{8,12},{12,8},{16,20},{20,16},{24,28},{28,24},{1,5},{5... | collective-permute-start | bytes 196616 | tf_op jit(solution)/shard_map/ppermute | solution.py:311
  126.6 1.4 %convolution_convert_fusion = bf16[2048,256]{1,0:T(8,128)(2,1)} fusion(bf16[256,256]{1,0:T(8,128)(2,1)S(1)} %copy-done, bf16[2048,128]{1,0:T(8,128)(2,1)S(1)} %pad_maximum_fusion.1, bf16[2048,128]{1,0:T(8,128)(2,1)S(1)} %pad_maximum_fusion), kind=kOutput, calls=%fused_computation.2 | convolution fusion | flops 271056896 | bytes 2228224 | tf_op jit(solution)/shard_map/dot_general | solution.py:543
  (81 shorter events, 22.5 us)
Async XLA Ops:
  0.6 126.0 %copy-start = (bf16[256,256]{1,0:T(8,128)(2,1)S(1)}, bf16[256,256]{1,0:T(8,128)(2,1)}, u32[]{:S(2)}) copy-start(bf16[256,256]{1,0:T(8,128)(2,1)} %param.11) | copy-start | bytes 393220
  0.7 7.1 %copy-start.3 = (s32[1,1,320]{2,1,0:T(1,128)S(1)}, s32[1,1,320]{2,1,0:T(1,128)}, u32[]{:S(2)}) copy-start(s32[1,1,320]{2,1,0:T(1,128)} %param.13) | copy-start | bytes 3844
  0.7 9.6 %copy-start.2 = (bf16[2048,256]{1,0:T(8,128)(2,1)S(1)}, bf16[2048,256]{1,0:T(8,128)(2,1)}, u32[]{:S(2)}) copy-start(bf16[2048,256]{1,0:T(8,128)(2,1)} %refs_0_) | copy-start | bytes 3145732
  3.1 26.1 %collective-permute-start.1 = (bf16[2048,128]{1,0:T(8,128)(2,1)S(1)}, bf16[2048,128]{1,0:T(8,128)(2,1)S(1)}, u32[]{:S(2)}, u32[]{:S(2)}) collective-permute-start(bf16[2048,128]{1,0:T(8,128)(2,1)S(1)} %get-tuple-element.87.refs_0_), channel_id=1, source_target_pairs={{0,2},{1,3},{2,0},{3,1},{4,6},{5,7},{6,4},{7,5},{8,10},{9,11},{10,... | collective-permute-start | bytes 1572872 | tf_op jit(solution)/shard_map/ppermute | solution.py:311
  6.3 22.9 %collective-permute-start = (bf16[2048,128]{1,0:T(8,128)(2,1)S(1)}, bf16[2048,128]{1,0:T(8,128)(2,1)}, u32[]{:S(2)}, u32[]{:S(2)}) collective-permute-start(bf16[2048,128]{1,0:T(8,128)(2,1)S(1)} %get-tuple-element.87.refs_0_), channel_id=1, source_target_pairs={{0,1},{1,0},{2,3},{3,2},{4,5},{5,4},{6,7},{7,6},{8,9},{9,8},{10,11... | collective-permute-start | bytes 1572872 | tf_op jit(solution)/shard_map/ppermute | solution.py:311
  10.3 25.8 %collective-permute-start.7 = (bf16[2048,256]{1,0:T(8,128)(2,1)S(1)}, bf16[2048,256]{1,0:T(8,128)(2,1)S(1)}, u32[]{:S(2)}, u32[]{:S(2)}) collective-permute-start(bf16[2048,256]{1,0:T(8,128)(2,1)S(1)} %copy-done.2), channel_id=1, source_target_pairs={{0,16},{4,20},{8,24},{12,28},{16,0},{20,4},{24,8},{28,12},{1,17},{... | collective-permute-start | bytes 3145736 | tf_op jit(solution)/shard_map/ppermute | solution.py:311
  11.6 24.6 %collective-permute-start.6 = (bf16[2048,256]{1,0:T(8,128)(2,1)S(1)}, bf16[2048,256]{1,0:T(8,128)(2,1)S(1)}, u32[]{:S(2)}, u32[]{:S(2)}) collective-permute-start(bf16[2048,256]{1,0:T(8,128)(2,1)S(1)} %copy-done.2), channel_id=1, source_target_pairs={{0,8},{4,12},{8,0},{12,4},{16,24},{20,28},{24,16},{28,20},{1,9},{5... | collective-permute-start | bytes 3145736 | tf_op jit(solution)/shard_map/ppermute | solution.py:311
  29.3 6.9 %collective-permute-start.4 = (bf16[2048,128]{1,0:T(8,128)(2,1)S(1)}, bf16[2048,128]{1,0:T(8,128)(2,1)S(1)}, u32[]{:S(2)}, u32[]{:S(2)}) collective-permute-start(bf16[2048,128]{1,0:T(8,128)(2,1)S(1)} %get-tuple-element.87.refs_0_), channel_id=1, source_target_pairs={{1,2},{2,1},{5,6},{6,5},{9,10},{10,9},{13,14},{14,13},{17,18},{18,... | collective-permute-start | bytes 1572872 | tf_op jit(solution)/shard_map/ppermute | solution.py:329
  30.0 14.4 %collective-permute-start.5 = (bf16[2048,128]{1,0:T(8,128)(2,1)S(1)}, bf16[2048,128]{1,0:T(8,128)(2,1)S(1)}, u32[]{:S(2)}, u32[]{:S(2)}) collective-permute-start(bf16[2048,128]{1,0:T(8,128)(2,1)S(1)} %collective-permute-done.1.refs_2_), channel_id=1, source_target_pairs={{1,0},{2,3},{5,4},{6,7},{9,8},{10,11},{13,12},{14,15},{17,16},{18,... | collective-permute-start | bytes 1572872 | tf_op jit(solution)/shard_map/ppermute | solution.py:329
  44.4 18.9 %collective-permute-start.9 = (bf16[1024,256]{1,0:T(8,128)(2,1)S(1)}, bf16[1024,256]{1,0:T(8,128)(2,1)S(1)}, u32[]{:S(2)}, u32[]{:S(2)}) collective-permute-start(bf16[1024,256]{1,0:T(8,128)(2,1)S(1)} %slice.96), channel_id=1, source_target_pairs={{0,8},{4,12},{8,0},{12,4},{16,24},{20,28},{24,16},{28,20},{1,9},{5... | collective-permute-start | bytes 1572872 | tf_op jit(solution)/shard_map/ppermute | solution.py:311
  45.7 17.6 %collective-permute-start.8 = (bf16[1024,256]{1,0:T(8,128)(2,1)S(1)}, bf16[1024,256]{1,0:T(8,128)(2,1)S(1)}, u32[]{:S(2)}, u32[]{:S(2)}) collective-permute-start(bf16[1024,256]{1,0:T(8,128)(2,1)S(1)} %slice.95), channel_id=1, source_target_pairs={{0,16},{4,20},{8,24},{12,28},{16,0},{20,4},{24,8},{28,12},{1,17},{... | collective-permute-start | bytes 1572872 | tf_op jit(solution)/shard_map/ppermute | solution.py:311
  47.0 24.2 %collective-permute-start.3 = (bf16[2048,128]{1,0:T(8,128)(2,1)S(1)}, bf16[2048,128]{1,0:T(8,128)(2,1)S(1)}, u32[]{:S(2)}, u32[]{:S(2)}) collective-permute-start(bf16[2048,128]{1,0:T(8,128)(2,1)S(1)} %get-tuple-element.110.refs_0_), channel_id=1, source_target_pairs={{0,2},{1,3},{2,0},{3,1},{4,6},{5,7},{6,4},{7,5},{8,10},{9,11},{10,... | collective-permute-start | bytes 1572872 | tf_op jit(solution)/shard_map/ppermute | solution.py:311
  49.5 21.7 %collective-permute-start.2 = (bf16[2048,128]{1,0:T(8,128)(2,1)S(1)}, bf16[2048,128]{1,0:T(8,128)(2,1)S(1)}, u32[]{:S(2)}, u32[]{:S(2)}) collective-permute-start(bf16[2048,128]{1,0:T(8,128)(2,1)S(1)} %get-tuple-element.110.refs_0_), channel_id=1, source_target_pairs={{0,1},{1,0},{2,3},{3,2},{4,5},{5,4},{6,7},{7,6},{8,9},{9,8},{10,11... | collective-permute-start | bytes 1572872 | tf_op jit(solution)/shard_map/ppermute | solution.py:311
  64.0 13.2 %collective-permute-start.12 = (bf16[2048,128]{1,0:T(8,128)(2,1)S(1)}, bf16[2048,128]{1,0:T(8,128)(2,1)S(1)}, u32[]{:S(2)}, u32[]{:S(2)}) collective-permute-start(bf16[2048,128]{1,0:T(8,128)(2,1)S(1)} %bitcast.56), channel_id=1, source_target_pairs={{0,8},{4,12},{8,0},{12,4},{16,24},{20,28},{24,16},{28,20},{1,9},{5... | collective-permute-start | bytes 1572872 | tf_op jit(solution)/shard_map/ppermute | solution.py:311
  65.4 12.8 %collective-permute-start.13 = (bf16[2048,128]{1,0:T(8,128)(2,1)S(1)}, bf16[2048,128]{1,0:T(8,128)(2,1)S(1)}, u32[]{:S(2)}, u32[]{:S(2)}) collective-permute-start(bf16[2048,128]{1,0:T(8,128)(2,1)S(1)} %bitcast.55), channel_id=1, source_target_pairs={{0,16},{4,20},{8,24},{12,28},{16,0},{20,4},{24,8},{28,12},{1,17},{... | collective-permute-start | bytes 1572872 | tf_op jit(solution)/shard_map/ppermute | solution.py:311
  71.2 10.0 %collective-permute-start.10 = (bf16[2048,128]{1,0:T(8,128)(2,1)S(1)}, bf16[2048,128]{1,0:T(8,128)(2,1)S(1)}, u32[]{:S(2)}, u32[]{:S(2)}) collective-permute-start(bf16[2048,128]{1,0:T(8,128)(2,1)S(1)} %get-tuple-element.110.refs_0_), channel_id=1, source_target_pairs={{1,2},{2,1},{5,6},{6,5},{9,10},{10,9},{13,14},{14,13},{17,18},{18,... | collective-permute-start | bytes 1572872 | tf_op jit(solution)/shard_map/ppermute | solution.py:329
  71.9 14.4 %collective-permute-start.11 = (bf16[2048,128]{1,0:T(8,128)(2,1)S(1)}, bf16[2048,128]{1,0:T(8,128)(2,1)S(1)}, u32[]{:S(2)}, u32[]{:S(2)}) collective-permute-start(bf16[2048,128]{1,0:T(8,128)(2,1)S(1)} %collective-permute-done.3.refs_2_), channel_id=1, source_target_pairs={{1,0},{2,3},{5,4},{6,7},{9,8},{10,11},{13,12},{14,15},{17,16},{18,... | collective-permute-start | bytes 1572872 | tf_op jit(solution)/shard_map/ppermute | solution.py:329
  78.6 10.3 %collective-permute-start.15 = (bf16[1024,128]{1,0:T(8,128)(2,1)S(1)}, bf16[1024,128]{1,0:T(8,128)(2,1)S(1)}, u32[]{:S(2)}, u32[]{:S(2)}) collective-permute-start(bf16[1024,128]{1,0:T(8,128)(2,1)S(1)} %get-tuple-element.166), channel_id=1, source_target_pairs={{0,8},{4,12},{8,0},{12,4},{16,24},{20,28},{24,16},{28,20},{1,9},{5... | collective-permute-start | bytes 786440 | tf_op jit(solution)/shard_map/ppermute | solution.py:311
  79.0 9.9 %collective-permute-start.14 = (bf16[1024,128]{1,0:T(8,128)(2,1)S(1)}, bf16[1024,128]{1,0:T(8,128)(2,1)S(1)}, u32[]{:S(2)}, u32[]{:S(2)}) collective-permute-start(bf16[1024,128]{1,0:T(8,128)(2,1)S(1)} %get-tuple-element.168), channel_id=1, source_target_pairs={{0,16},{4,20},{8,24},{12,28},{16,0},{20,4},{24,8},{28,12},{1,17},{... | collective-permute-start | bytes 786440 | tf_op jit(solution)/shard_map/ppermute | solution.py:311
  88.9 7.3 %collective-permute-start.16 = (bf16[8192,128]{1,0:T(8,128)(2,1)S(1)}, bf16[8192,128]{1,0:T(8,128)(2,1)S(1)}, u32[]{:S(2)}, u32[]{:S(2)}) collective-permute-start(bf16[8192,128]{1,0:T(8,128)(2,1)S(1)} %get-tuple-element.128), channel_id=1, source_target_pairs={{0,4},{4,0},{8,12},{12,8},{16,20},{20,16},{24,28},{28,24},{1,5},{5... | collective-permute-start | bytes 6291464 | tf_op jit(solution)/shard_map/ppermute | solution.py:311
  99.0 2.0 %collective-permute-start.19 = (bf16[256,128]{1,0:T(8,128)(2,1)S(1)}, bf16[256,128]{1,0:T(8,128)(2,1)S(1)}, u32[]{:S(2)}, u32[]{:S(2)}) collective-permute-start(bf16[256,128]{1,0:T(8,128)(2,1)S(1)} %broadcast_select_fusion.2), channel_id=1, source_target_pairs={{0,4},{4,0},{8,12},{12,8},{16,20},{20,16},{24,28},{28,24},{1,5},{5... | collective-permute-start | bytes 196616 | tf_op jit(solution)/shard_map/ppermute | solution.py:311
  99.5 13.4 %collective-permute-start.17 = (bf16[2048,128]{1,0:T(8,128)(2,1)S(1)}, bf16[2048,128]{1,0:T(8,128)(2,1)S(1)}, u32[]{:S(2)}, u32[]{:S(2)}) collective-permute-start(bf16[2048,128]{1,0:T(8,128)(2,1)S(1)} %bitcast.54), channel_id=1, source_target_pairs={{0,8},{4,12},{8,0},{12,4},{16,24},{20,28},{24,16},{28,20},{1,9},{5... | collective-permute-start | bytes 1572872 | tf_op jit(solution)/shard_map/ppermute | solution.py:311
  101.0 13.1 %collective-permute-start.18 = (bf16[2048,128]{1,0:T(8,128)(2,1)S(1)}, bf16[2048,128]{1,0:T(8,128)(2,1)S(1)}, u32[]{:S(2)}, u32[]{:S(2)}) collective-permute-start(bf16[2048,128]{1,0:T(8,128)(2,1)S(1)} %bitcast.53), channel_id=1, source_target_pairs={{0,16},{4,20},{8,24},{12,28},{16,0},{20,4},{24,8},{28,12},{1,17},{... | collective-permute-start | bytes 1572872 | tf_op jit(solution)/shard_map/ppermute | solution.py:311
  101.0 6.3 %collective-permute-start.22 = (bf16[256,128]{1,0:T(8,128)(2,1)S(1)}, bf16[256,128]{1,0:T(8,128)(2,1)S(1)}, u32[]{:S(2)}, u32[]{:S(2)}) collective-permute-start(bf16[256,128]{1,0:T(8,128)(2,1)S(1)} %add_convert_fusion.12), channel_id=1, source_target_pairs={{0,3},{1,2},{2,1},{3,0},{4,7},{5,6},{6,5},{7,4},{8,11},{9,10},{10,... | collective-permute-start | bytes 196616 | tf_op jit(solution)/shard_map/ppermute | solution.py:311
  105.1 5.7 %collective-permute-start.21 = (bf16[256,128]{1,0:T(8,128)(2,1)S(1)}, bf16[256,128]{1,0:T(8,128)(2,1)S(1)}, u32[]{:S(2)}, u32[]{:S(2)}) collective-permute-start(bf16[256,128]{1,0:T(8,128)(2,1)S(1)} %add_convert_fusion.12), channel_id=1, source_target_pairs={{0,2},{1,3},{2,0},{3,1},{4,6},{5,7},{6,4},{7,5},{8,10},{9,11},{10,... | collective-permute-start | bytes 196616 | tf_op jit(solution)/shard_map/ppermute | solution.py:311
  105.1 5.7 %collective-permute-start.20 = (bf16[256,128]{1,0:T(8,128)(2,1)S(1)}, bf16[256,128]{1,0:T(8,128)(2,1)S(1)}, u32[]{:S(2)}, u32[]{:S(2)}) collective-permute-start(bf16[256,128]{1,0:T(8,128)(2,1)S(1)} %add_convert_fusion.12), channel_id=1, source_target_pairs={{0,1},{1,0},{2,3},{3,2},{4,5},{5,4},{6,7},{7,6},{8,9},{9,8},{10,11... | collective-permute-start | bytes 196616 | tf_op jit(solution)/shard_map/ppermute | solution.py:311
  114.4 6.6 %collective-permute-start.23 = (bf16[1024,128]{1,0:T(8,128)(2,1)S(1)}, bf16[1024,128]{1,0:T(8,128)(2,1)S(1)}, u32[]{:S(2)}, u32[]{:S(2)}) collective-permute-start(bf16[1024,128]{1,0:T(8,128)(2,1)S(1)} %get-tuple-element.146), channel_id=1, source_target_pairs={{0,16},{4,20},{8,24},{12,28},{16,0},{20,4},{24,8},{28,12},{1,17},{... | collective-permute-start | bytes 786440 | tf_op jit(solution)/shard_map/ppermute | solution.py:311
  114.8 6.6 %collective-permute-start.24 = (bf16[1024,128]{1,0:T(8,128)(2,1)S(1)}, bf16[1024,128]{1,0:T(8,128)(2,1)S(1)}, u32[]{:S(2)}, u32[]{:S(2)}) collective-permute-start(bf16[1024,128]{1,0:T(8,128)(2,1)S(1)} %get-tuple-element.148), channel_id=1, source_target_pairs={{0,8},{4,12},{8,0},{12,4},{16,24},{20,28},{24,16},{28,20},{1,9},{5... | collective-permute-start | bytes 786440 | tf_op jit(solution)/shard_map/ppermute | solution.py:311
  115.8 7.2 %collective-permute-start.27 = (bf16[256,128]{1,0:T(8,128)(2,1)S(1)}, bf16[256,128]{1,0:T(8,128)(2,1)S(1)}, u32[]{:S(2)}, u32[]{:S(2)}) collective-permute-start(bf16[256,128]{1,0:T(8,128)(2,1)S(1)} %add_convert_fusion.11), channel_id=1, source_target_pairs={{0,24},{4,28},{8,16},{12,20},{16,8},{20,12},{24,0},{28,4},{1,25},{... | collective-permute-start | bytes 196616 | tf_op jit(solution)/shard_map/ppermute | solution.py:311
  117.1 5.9 %collective-permute-start.26 = (bf16[256,128]{1,0:T(8,128)(2,1)S(1)}, bf16[256,128]{1,0:T(8,128)(2,1)S(1)}, u32[]{:S(2)}, u32[]{:S(2)}) collective-permute-start(bf16[256,128]{1,0:T(8,128)(2,1)S(1)} %add_convert_fusion.11), channel_id=1, source_target_pairs={{0,16},{4,20},{8,24},{12,28},{16,0},{20,4},{24,8},{28,12},{1,17},{... | collective-permute-start | bytes 196616 | tf_op jit(solution)/shard_map/ppermute | solution.py:311
  117.4 6.7 %collective-permute-start.25 = (bf16[256,128]{1,0:T(8,128)(2,1)S(1)}, bf16[256,128]{1,0:T(8,128)(2,1)S(1)}, u32[]{:S(2)}, u32[]{:S(2)}) collective-permute-start(bf16[256,128]{1,0:T(8,128)(2,1)S(1)} %add_convert_fusion.11), channel_id=1, source_target_pairs={{0,8},{4,12},{8,0},{12,4},{16,24},{20,28},{24,16},{28,20},{1,9},{5... | collective-permute-start | bytes 196616 | tf_op jit(solution)/shard_map/ppermute | solution.py:311
  124.2 3.8 %collective-permute-start.28 = (bf16[256,128]{1,0:T(8,128)(2,1)S(1)}, bf16[256,128]{1,0:T(8,128)(2,1)S(1)}, u32[]{:S(2)}, u32[]{:S(2)}) collective-permute-start(bf16[256,128]{1,0:T(8,128)(2,1)S(1)} %add_convert_fusion.10), channel_id=1, source_target_pairs={{0,4},{4,0},{8,12},{12,8},{16,20},{20,16},{24,28},{28,24},{1,5},{5... | collective-permute-start | bytes 196616 | tf_op jit(solution)/shard_map/ppermute | solution.py:311
  (2 other events, 11.0 us)
